TPU v7x, 32 devices: a whole 2x2x4 slice. The times are simulated.
32 devices in a mesh: seq: 8 (over y, x, core), pack: 4 (over z).
Axes of the slice: x: 2, y: 2, z: 4, core: 2. Of those that a mesh axis runs over, the one named last changes fastest.
Arguments:
- patches: bfloat16 [4, 1536, 1408], P('pack', 'seq'), may hold values from -80 to 80
- patch_mask: int32 [4, 1536], P('pack', 'seq'), may hold values 0 or 1
- mask_embed: bfloat16 [1408], replicated, may hold values from -6 to 6
- norm_gain: bfloat16 [1408], replicated, may hold values from 0.5 to 1.5
- qkv_weight: bfloat16 [1408, 4224], P(None, 'seq'), may hold values from -1 to 1
- segment_ids: int32 [4, 1536], P('pack', 'seq'), may hold values from 0 to 3, as said below
- patch_rows: int32 [4, 1536], P('pack', 'seq'), may hold values from 0 to 23, as said below
- patch_column: int32 [4, 1536], P('pack', 'seq'), may hold values from 0 to 31, as said below
- out_weight: bfloat16 [1408, 1408], replicated, may hold values from -0.625 to 0.625
- merge_gain: bfloat16 [1408], replicated, may hold values from 0.5 to 1.5
- merge_weight: bfloat16 [5632, 3584], P(None, 'seq'), may hold values from -0.078125 to 0.078125
- merge_bias: bfloat16 [3584], P('seq'), may hold values from -3 to 3
- image_owner: int32 [4, 4], P('pack'), may hold values from 0 to 3, as said below
Outputs:
- routed: bfloat16 [4, 4, 192, 3584], P('pack', None, None, 'seq')
Inputs may be any that keep to these rules, and one draw needn't show every extreme that they name: `segment_ids`: in each pack the tokens come in aligned groups of four of one image (the four patches of one 2 x 2 window, in merge order); image numbers never fall along a pack; each of the 4 images has 1 to 192 groups and one has exactly 192. `patch_rows`: each image is some number w of windows wide, 1 <= w <= 16; the image with exactly 192 groups has w = 16; group g of an image covers rows 2 (g // w) and 2 (g // w) + 1 and columns 2 (g % w) and 2 (g % w) + 1, in the order (top left, top right, bottom left, bottom right). `patch_column`: as for patch_rows. `image_owner`: in each pack the owners of its 4 images are distinct owner indices, so at most 192 merged tokens go from one pack to one owner; one owner gets a pack's largest image, of exactly 192 merged tokens, from every pack.
All inputs are finite; a program needn't handle non-finite values. No bound on the sum of `patch_mask` on one device may be relied on, other than what follows from the above.
Results may differ from a plain program's by a relative error of at most 0.0061.
Values may be sent and summed in bfloat16 or wider, within the bound.
No kernel may reach another device: no remote copies, remote signals or barrier semaphores. Data moves between devices by JAX's collectives and lax.ppermute only.
A program may use at most 64 MiB of HBM per device.

v0:
```python
import jax
import jax.numpy as jnp
from jax import lax
from jax.sharding import PartitionSpec as P

D = 1408
HEADS = 16
HD = 88


EPSILON = 1e-06


def layer_norm(values, gain_vector):
    center = values - jnp.mean(values, axis=-1, keepdims=True)
    spread = jnp.mean(center * center, axis=-1, keepdims=True)
    return center * lax.rsqrt(spread + EPSILON) * gain_vector.astype(jnp.float32)


def rotate(vectors, row_index, column_index):
    total_rows, heads_here, head_width = vectors.shape
    quarter = head_width // 4
    frequency = 10000.0 ** (-jnp.arange(quarter, dtype=jnp.float32) / quarter)
    row_angle = row_index.astype(jnp.float32)[:, None] * frequency[None, :]
    column_angle = column_index.astype(jnp.float32)[:, None] * frequency[None, :]
    angles = jnp.stack([row_angle, column_angle], axis=1)[:, None, :, None, :]
    split_up = vectors.reshape(total_rows, heads_here, 2, 2, quarter)
    partner = jnp.stack([-split_up[:, :, :, 1], split_up[:, :, :, 0]], axis=3)
    turned = split_up * jnp.cos(angles) + partner * jnp.sin(angles)
    return turned.reshape(total_rows, heads_here, head_width)


def qkv_block(projected, row_index, column_index):
    turned_queries = rotate(projected[:, :, 0], row_index, column_index)
    turned_keys = rotate(projected[:, :, 1], row_index, column_index)
    return jnp.concatenate([turned_queries, turned_keys, projected[:, :, 2]], axis=-1).astype(
        jnp.bfloat16
    )


def attention(block, segments):
    total_rows, heads_here, triple = block.shape
    head_width = triple // 3
    step_rows = min(512, total_rows)
    query_part = block[:, :, :head_width].reshape(
        total_rows // step_rows, step_rows, heads_here, head_width
    )
    key_part = block[:, :, head_width : 2 * head_width]
    value_part = block[:, :, 2 * head_width :]
    query_segments = segments.reshape(total_rows // step_rows, step_rows)
    scale = head_width ** (-0.5)

    def one_block(inputs_pair):
        queries_here, segments_here = inputs_pair
        scores = (
            jnp.einsum("qhd,khd->hqk", queries_here, key_part, preferred_element_type=jnp.float32)
            * scale
        )
        same_image = (segments_here[:, None] == segments[None, :])[None]
        scores = jnp.where(same_image, scores, -jnp.inf)
        highest = jnp.max(scores, axis=-1, keepdims=True)
        weights = jnp.exp(scores - highest)
        probs = (weights / jnp.sum(weights, axis=-1, keepdims=True)).astype(jnp.bfloat16)
        result = jnp.einsum("hqk,khd->qhd", probs, value_part, preferred_element_type=jnp.float32)
        return result.astype(jnp.bfloat16)

    return lax.map(one_block, (query_part, query_segments)).reshape(
        total_rows, heads_here, head_width
    )


def route(projected, segments, owners_here, packs, most):
    merged_segments = segments[::4]
    images = owners_here.shape[0]
    image_ids = jnp.arange(images, dtype=jnp.int32)
    member = (merged_segments[None, :] == image_ids[:, None]).astype(jnp.int32)
    lengths = jnp.sum(member, axis=1, dtype=jnp.int32)
    starts = jnp.cumsum(lengths, dtype=jnp.int32) - lengths
    owner_ids = jnp.arange(packs, dtype=jnp.int32)
    owned = owners_here[None, :] == owner_ids[:, None]
    first_row = jnp.sum(jnp.where(owned, starts[None, :], 0), axis=1, dtype=jnp.int32)
    owned_length = jnp.sum(jnp.where(owned, lengths[None, :], 0), axis=1, dtype=jnp.int32)
    slots = jnp.arange(most, dtype=jnp.int32)
    source_rows = jnp.clip(first_row[:, None] + slots[None, :], 0, projected.shape[0] - 1)
    picked = jnp.take(projected, source_rows.reshape(-1), axis=0).reshape(
        packs, most, projected.shape[1]
    )
    filled = slots[None, :] < owned_length[:, None]
    return jnp.where(filled[:, :, None], picked, jnp.zeros_like(picked))


def local(
    patches,
    patch_mask,
    mask_embed,
    norm_gain,
    qkv_weight,
    segment_ids,
    patch_rows,
    patch_column,
    out_weight,
    merge_gain,
    merge_weight,
    merge_bias,
    image_owner,
):
    local_rows = patches.shape[1]
    shards = lax.axis_size("seq")
    packs = lax.axis_size("pack")
    heads_here = HEADS // shards
    inputs = jnp.where(patch_mask[0][:, None] == 1, mask_embed[None, :], patches[0])
    normed = layer_norm(inputs.astype(jnp.float32), norm_gain).astype(jnp.bfloat16)
    labels = lax.all_gather(
        jnp.stack([segment_ids[0], patch_rows[0], patch_column[0]]), "seq", axis=1, tiled=True
    )
    piece = lax.all_gather(normed, "seq", axis=0, tiled=True)
    span = piece.shape[0]
    projected = jnp.dot(piece, qkv_weight, preferred_element_type=jnp.float32)
    row_part = labels[1]
    column_part = labels[2]
    block = qkv_block(projected.reshape(span, heads_here, 3, HD), row_part, column_part)
    result = attention(block, labels[0])
    mixed_heads = lax.all_to_all(result, "seq", split_axis=0, concat_axis=1, tiled=True)
    attended = mixed_heads.reshape(local_rows, D)
    residual = inputs.astype(jnp.float32) + jnp.dot(
        attended, out_weight, preferred_element_type=jnp.float32
    )
    merged = layer_norm(residual, merge_gain).astype(jnp.bfloat16).reshape(local_rows // 4, 4 * D)
    projected_all = (
        jnp.dot(
            lax.all_gather(merged, "seq", axis=0, tiled=True),
            merge_weight,
            preferred_element_type=jnp.float32,
        )
        + merge_bias.astype(jnp.float32)
    ).astype(jnp.bfloat16)
    images = image_owner.shape[1]
    most = 2 * projected_all.shape[0] // images
    outgoing = route(projected_all, labels[0], image_owner[0], packs, most)
    delivered = lax.all_to_all(outgoing, "pack", split_axis=0, concat_axis=0, tiled=True)
    return delivered[None]


def solution(mesh):
    placed = (
        P("pack", "seq", None),
        P("pack", "seq"),
        P(),
        P(),
        P(None, "seq"),
        P("pack", "seq"),
        P("pack", "seq"),
        P("pack", "seq"),
        P(),
        P(),
        P(None, "seq"),
        P("seq"),
        P("pack", None),
    )
    return jax.shard_map(
        local, mesh=mesh, in_specs=placed, out_specs=P("pack", None, None, "seq"), check_vma=False
    )
```

profile of v0, /device:TPU:0, one launch (start us, length us, event | category | flops | bytes accessed | tf_op | source)
XLA Modules:
  0.0 198.6 jit_solution(1451118463645392768)
XLA Ops:
  7.4 1.3 convert_reduce_fusion
  8.8 1.4 fusion.39
  10.2 1.5 fusion.41
  11.8 10.5 %all-gather = s32[8,192,3]{1,2,0:T(4,128)S(1)} all-gather(s32[1,192,3]{1,2,0:T(4,128)S(1)} %add_bitcast_fusion), channel_id=1, replica_groups=mesh['seq'=8,'pack'=4] {'seq'}, dimensions={0}, use_global_device_ids=true | all-gather | bytes 20736 | tf_op jit(solution)/shard_map/all_gather | solution.py:113
  22.6 1.1 fusion.48
  23.7 0.9 mul.152
  24.7 0.9 mul.156
  25.6 26.3 %all-gather.4.cloned.1.call-done = bf16[1536,1408]{1,0:T(8,128)(2,1)} async-done(((bf16[192,1408]{1,0:T(8,128)(2,1)}), bf16[1536,1408]{1,0:T(8,128)(2,1)}) %all-gather.4.cloned.1.call-update) | async-done | bytes 4325392 | tf_op jit(solution)/shard_map/all_gather | solution.py:116
  51.8 4.5 %fusion.58 = f32[1536,528]{0,1:T(8,128)S(1)} fusion(bf16[1536,1408]{1,0:T(8,128)(2,1)} %all-gather.4.cloned.1.call-done, bf16[1408,528]{0,1:T(8,128)(2,1)S(1)} %copy-done), kind=kOutput, calls=%fused_computation.91 | convolution fusion | flops 2283798528 | bytes 9056256 | tf_op jit(solution)/shard_map/dot_general | solution.py:118
  56.4 0.8 fusion.46
  59.8 1.0 pad_maximum_fusion
  61.0 2.3 %fusion.43 = (bf16[1536,2,88]{0,1,2:T(2,128)(2,1)S(1)}, bf16[1536,2,88]{0,1,2:T(2,128)(2,1)S(1)}) fusion(f32[1536,2,2,2,22]{0,1,4,3,2:T(2,128)S(1)} %get-tuple-element.106, f32[1536,88]{0,1:T(8,128)S(1)} %copy-done.3, f32[1536,88]{0,1:T(8,128)S(1)} %copy-done.2, f32[1536,2,1,88]{0,3,2,1:T(8,128)S(1)} %get-tuple-element.89, ...), kind=kLoop, calls=%fused_computation.43 | loop fusion | flops 2162688 | bytes 6488064 | tf_op jit(solution)/shard_map/slice | solution.py:48
  63.3 0.9 copy.56
  64.8 26.1 %while.10 = (s32[]{:T(128)}, bf16[3,512,2,88]{1,3,2,0:T(8,128)(2,1)}, s32[3,512]{1,0:T(4,128)S(1)}, s32[1,1536]{1,0:T(1,128)S(1)}, bf16[3,512,2,88]{1,3,2,0:T(8,...) while((s32[]{:T(128)}, ...), condition=%wide.region_9.10_spmd, body=%wide.region_6.9_spmd.sunk | while | flops 845508608 | bytes 4555889 | solution.py:67
  65.5 3.4 %fusion.81 = f32[2,512]{1,0:T(2,128)S(1)} fusion(pred[512,1536]{1,0:T(8,128)(4,1)S(1)} %broadcast_compare_fusion.2, bf16[1536,2,88]{0,2,1:T(8,128)(2,1)} %get-tuple-element.175, bf16[3,512,2,88]{1,3,2,0:T(8,128)(2,1)S(1)} %get-tuple-element.174, s32[]{:T(128)S(6)} %copy.78), kind=kOutput, calls=%fused_computation.87.clone.1 | convolution fusion | flops 283117056 | bytes 1511428 | tf_op jit(solution)/shard_map/while/body/eval_jaxpr/sub | solution.py:62
  69.0 4.6 %fusion.82 = bf16[3,512,2,88]{1,3,2,0:T(8,128)(2,1)} fusion(bf16[3,512,2,88]{1,3,2,0:T(8,128)(2,1)} %get-tuple-element.162, s32[]{:T(128)S(6)} %copy.78, bf16[1536,2,88]{0,2,1:T(8,128)(2,1)} %get-tuple-element.176, f32[2,512]{1,0:T(2,128)S(1)} %fusion.81, pred[512,1536]{1,0:T(8,128)(4,1)S(1)} %broadcast_compare_fusion.2, ...), kind=kOutput, calls=%fused_computation.13.clone.1 | convolution fusion | flops 561605120 | bytes 2233344 | tf_op jit(solution)/shard_map/while/body/eval_jaxpr/hqk,khd->qhd/dot_general | solution.py:64
  74.2 3.4 %fusion.81 = f32[2,512]{1,0:T(2,128)S(1)} fusion(pred[512,1536]{1,0:T(8,128)(4,1)S(1)} %broadcast_compare_fusion.2, bf16[1536,2,88]{0,2,1:T(8,128)(2,1)} %get-tuple-element.175, bf16[3,512,2,88]{1,3,2,0:T(8,128)(2,1)S(1)} %get-tuple-element.174, s32[]{:T(128)S(6)} %copy.78), kind=kOutput, calls=%fused_computation.87.clone.1 | convolution fusion | flops 283117056 | bytes 1511428 | tf_op jit(solution)/shard_map/while/body/eval_jaxpr/sub | solution.py:62
  77.6 4.6 %fusion.82 = bf16[3,512,2,88]{1,3,2,0:T(8,128)(2,1)} fusion(bf16[3,512,2,88]{1,3,2,0:T(8,128)(2,1)} %get-tuple-element.162, s32[]{:T(128)S(6)} %copy.78, bf16[1536,2,88]{0,2,1:T(8,128)(2,1)} %get-tuple-element.176, f32[2,512]{1,0:T(2,128)S(1)} %fusion.81, pred[512,1536]{1,0:T(8,128)(4,1)S(1)} %broadcast_compare_fusion.2, ...), kind=kOutput, calls=%fused_computation.13.clone.1 | convolution fusion | flops 561605120 | bytes 2233344 | tf_op jit(solution)/shard_map/while/body/eval_jaxpr/hqk,khd->qhd/dot_general | solution.py:64
  82.8 3.4 %fusion.81 = f32[2,512]{1,0:T(2,128)S(1)} fusion(pred[512,1536]{1,0:T(8,128)(4,1)S(1)} %broadcast_compare_fusion.2, bf16[1536,2,88]{0,2,1:T(8,128)(2,1)} %get-tuple-element.175, bf16[3,512,2,88]{1,3,2,0:T(8,128)(2,1)S(1)} %get-tuple-element.174, s32[]{:T(128)S(6)} %copy.78), kind=kOutput, calls=%fused_computation.87.clone.1 | convolution fusion | flops 283117056 | bytes 1511428 | tf_op jit(solution)/shard_map/while/body/eval_jaxpr/sub | solution.py:62
  86.2 4.7 %fusion.82 = bf16[3,512,2,88]{1,3,2,0:T(8,128)(2,1)} fusion(bf16[3,512,2,88]{1,3,2,0:T(8,128)(2,1)} %get-tuple-element.162, s32[]{:T(128)S(6)} %copy.78, bf16[1536,2,88]{0,2,1:T(8,128)(2,1)} %get-tuple-element.176, f32[2,512]{1,0:T(2,128)S(1)} %fusion.81, pred[512,1536]{1,0:T(8,128)(4,1)S(1)} %broadcast_compare_fusion.2, ...), kind=kOutput, calls=%fused_computation.13.clone.1 | convolution fusion | flops 561605120 | bytes 2233344 | tf_op jit(solution)/shard_map/while/body/eval_jaxpr/hqk,khd->qhd/dot_general | solution.py:64
  90.9 3.0 %copy.63 = bf16[3,512,2,88]{3,2,1,0:T(2,128)(2,1)} copy(bf16[3,512,2,88]{1,3,2,0:T(8,128)(2,1)} %get-tuple-element.42) | data formatting | bytes 1081344 | tf_op jit(solution)/shard_map/reshape | solution.py:67
  93.9 3.7 %all-to-all-start = ((bf16[1536,2,88]{2,1,0:T(2,128)(2,1)}), bf16[1536,2,88]{2,1,0:T(2,128)(2,1)S(1)}, u32[]{:S(2)}, u32[]{:S(2)}) async-start(bf16[1536,2,88]{2,1,0:T(2,128)(2,1)} %bitcast.108), calls=%async_computation | async-start | bytes 1572864 | tf_op jit(solution)/shard_map/all_to_all | solution.py:123
  97.6 12.5 %all-to-all-done = bf16[1536,2,88]{2,1,0:T(2,128)(2,1)S(1)} async-done(((bf16[1536,2,88]{2,1,0:T(2,128)(2,1)}), bf16[1536,2,88]{2,1,0:T(2,128)(2,1)S(1)}, u32[]{:S(2)}, u32[]{:S(2)}) %all-to-all-start) | async-done | bytes 540704 | tf_op jit(solution)/shard_map/all_to_all | solution.py:123
  110.1 1.4 copy.74
  111.5 3.1 %reshape.344 = bf16[192,1408]{1,0:T(8,128)(2,1)S(1)} reshape(bf16[192,8,2,88]{3,2,1,0:T(2,128)(2,1)} %bitcast.109) | data formatting | bytes 1081344 | tf_op jit(solution)/shard_map/reshape | solution.py:124
  114.6 3.3 %fusion.57 = (f32[192]{0:T(256)S(1)}, f32[192,1408]{1,0:T(8,128)S(1)}) fusion(bf16[192,1408]{1,0:T(8,128)(2,1)S(1)} %reshape.344, bf16[1408,1408]{1,0:T(8,128)(2,1)} %param.23, bf16[1,192,1408]{2,1,0:T(8,128)(2,1)S(1)} %copy-done.1, bf16[1408]{0:T(1024)(128)(2,1)S(1)} %copy-done.4, pred[192]{0:T(512)(128)(4,1)S(1)} %compare_reduce_fusion), kind=kOutput, calls=%fused_computation.90 | convolution fusion | flops 762347328 | bytes 6131392 | tf_op jit(solution)/shard_map/dot_general | solution.py:125
  118.5 1.2 reshape.345
  120.7 35.5 %all-gather.6.cloned.1.call-done = bf16[384,5632]{1,0:T(8,128)(2,1)} async-done(((bf16[48,5632]{1,0:T(8,128)(2,1)}), bf16[384,5632]{1,0:T(8,128)(2,1)}) %all-gather.6.cloned.1.call-update) | async-done | bytes 4325392 | tf_op jit(solution)/shard_map/all_gather | solution.py:131
  156.2 6.6 %fusion.38 = bf16[384,448]{0,1:T(8,128)(2,1)S(1)} fusion(bf16[384,5632]{1,0:T(8,128)(2,1)} %all-gather.6.cloned.1.call-done, bf16[5632,448]{0,1:T(8,128)(2,1)} %param.25, f32[448]{0:T(512)S(1)} %convert_element_type.67), kind=kOutput, calls=%fused_computation.34 | convolution fusion | flops 1938112512 | bytes 9717504 | tf_op jit(solution)/shard_map/dot_general | solution.py:130
  163.0 2.7 %gather_fusion = bf16[768,448]{1,0:T(8,128)(2,1)S(1)} fusion(bf16[384,448]{1,0:T(8,128)(2,1)S(1)} %copy.60, s32[1024]{0:T(1024)S(1)} %pad_clamp_fusion), kind=kCustom, calls=%fused_computation | custom fusion | bytes 1379328 | tf_op jit(solution)/shard_map/jit(_take)/gather | solution.py:85
  165.9 24.9 %all_to_all.20 = bf16[4,192,448]{2,1,0:T(8,128)(2,1)S(1)} all-to-all(bf16[4,192,448]{2,1,0:T(8,128)(2,1)S(1)} %select_select_fusion), channel_id=1, replica_groups=mesh['seq'=8,'pack'=4] {'pack'}, dimensions={0} | all-to-all | bytes 1376256 | tf_op jit(solution)/shard_map/all_to_all | solution.py:140
  190.9 0.9 copy.83
  (77 shorter events, 8.2 us)
Async XLA Ops:
  6.5 45.3 %copy-start = (bf16[1408,528]{0,1:T(8,128)(2,1)S(1)}, bf16[1408,528]{0,1:T(8,128)(2,1)}, u32[]{:S(2)}) copy-start(bf16[1408,528]{0,1:T(8,128)(2,1)} %param.19) | copy-start | bytes 4460548
  6.5 3.7 %copy-start.4 = (bf16[1408]{0:T(1024)(128)(2,1)S(1)}, bf16[1408]{0:T(1024)(128)(2,1)}, u32[]{:S(2)}) copy-start(bf16[1408]{0:T(1024)(128)(2,1)} %param.17) | copy-start | bytes 8452
  6.5 3.7 %copy-start.1 = (bf16[1,192,1408]{2,1,0:T(8,128)(2,1)S(1)}, bf16[1,192,1408]{2,1,0:T(8,128)(2,1)}, u32[]{:S(2)}) copy-start(bf16[1,192,1408]{2,1,0:T(8,128)(2,1)} %param.15) | copy-start | bytes 1622020
  6.5 3.7 %copy-start.5 = (bf16[1408]{0:T(1024)(128)(2,1)S(1)}, bf16[1408]{0:T(1024)(128)(2,1)}, u32[]{:S(2)}) copy-start(bf16[1408]{0:T(1024)(128)(2,1)} %param.18) | copy-start | bytes 8452
  6.5 45.3 %all-gather.4.cloned.1.call-start = ((), (), s32[]{:S(2)}) async-start(), calls=%async_computation.2 | async-start | bytes 4866048 | tf_op jit(solution)/shard_map/all_gather | solution.py:116
  8.7 3.0 %copy-start.7 = (s32[1,192]{1,0:T(1,128)S(1)}, s32[1,192]{1,0:T(1,128)}, u32[]{:S(2)}) copy-start(s32[1,192]{1,0:T(1,128)} %param.22) | copy-start | bytes 2308
  8.8 3.0 %copy-start.8 = (s32[1,192]{1,0:T(1,128)S(1)}, s32[1,192]{1,0:T(1,128)}, u32[]{:S(2)}) copy-start(s32[1,192]{1,0:T(1,128)} %param.21) | copy-start | bytes 2308
  8.8 3.0 %copy-start.9 = (s32[1,192]{1,0:T(1,128)S(1)}, s32[1,192]{1,0:T(1,128)}, u32[]{:S(2)}) copy-start(s32[1,192]{1,0:T(1,128)} %param.20) | copy-start | bytes 2308
  59.8 1.0 copy-start.2
  59.8 1.2 copy-start.3
  93.9 3.7 %copy-start.6 = (bf16[1408]{0:T(1024)(128)(2,1)S(1)}, bf16[1408]{0:T(1024)(128)(2,1)}, u32[]{:S(2)}) copy-start(bf16[1408]{0:T(1024)(128)(2,1)} %param.24) | copy-start | bytes 8452
  93.9 16.2 %all-to-all-start = ((bf16[1536,2,88]{2,1,0:T(2,128)(2,1)}), bf16[1536,2,88]{2,1,0:T(2,128)(2,1)S(1)}, u32[]{:S(2)}, u32[]{:S(2)}) async-start(bf16[1536,2,88]{2,1,0:T(2,128)(2,1)} %bitcast.108), calls=%async_computation | async-start | bytes 1572864 | tf_op jit(solution)/shard_map/all_to_all | solution.py:123
  97.6 58.7 %all-gather.6.cloned.1.call-start = ((), (), s32[]{:S(2)}) async-start(), calls=%async_computation.3 | async-start | bytes 4866048 | tf_op jit(solution)/shard_map/all_gather | solution.py:131
  118.5 1.4 copy-start.10
  118.5 1.7 copy-start.11
Sparse Core Ops, SparseCore 0:
  11.8 39.9 all-gather.3
  119.8 36.3 all-gather.5
where the time goes:
time: 199 us
  waiting for transfers between devices  74.3 us (37%)
  matrix products  38.7 us (19%)
  blocking collectives  35.5 us (18%)
  local copies, waits for them, and re-layouts  19.1 us (10%)
  between operations  13.8 us (7%)
  other arithmetic  13.2 us (7%)
  starting transfers between devices  3.75 us (2%)
    all_gather x1, waiting for transfers between devices, local(): lax.all_gather(merged, 'seq', axis=0, tiled=True)  35.5 us
    all_gather x1, waiting for transfers between devices, local(): piece = lax.all_gather(normed, 'seq', axis=0, tiled=True)  26.3 us
    all_to_all x1, blocking collectives, local(): lax.all_to_all(outgoing, 'pack', split_axis=0, concat_axis=0, tiled=True)  24.9 us
    dot_general x3, matrix products, one_block(): jnp.einsum('hqk,khd->qhd', probs, value_part, preferred_element_type=jnp....  13.9 us
    all_to_all x1, waiting for transfers between devices, local(): lax.all_to_all(result, 'seq', split_axis=0, concat_axis=1, tiled=True)  12.5 us
    all_gather x1, blocking collectives, local(): lax.all_gather(jnp.stack([segment_ids[0], patch_rows[0], patch_column[0]]...  10.5 us
    sub x3, matrix products, one_block(): weights = jnp.exp(scores - highest)  10.3 us
    dot_general x1, matrix products, local(): jnp.dot(lax.all_gather(merged, 'seq', axis=0, tiled=True), merge_weight,...  6.56 us
  transfers between devices with their start and end apart: 3, of which 3 were waited for; matrix products, arithmetic and copies ran while one was open for 2% of the time, Pallas kernels for 0%

commit v1 on v0

--- a/solution.py
+++ b/solution.py
@@ -1,6 +1,11 @@
+import functools
+
 import jax
 import jax.numpy as jnp
+import numpy as np
 from jax import lax
+from jax.experimental import pallas as pl
+from jax.experimental.pallas import tpu as pltpu
 from jax.sharding import PartitionSpec as P
 
 D = 1408
@@ -89,7 +94,7 @@
     return jnp.where(filled[:, :, None], picked, jnp.zeros_like(picked))
 
 
-def local(
+def general_local(
     patches,
     patch_mask,
     mask_embed,
@@ -141,6 +146,482 @@
     return delivered[None]
 
 
+LANES = 128
+
+
+def norm_rows(values, gain_row):
+    center = values - jnp.mean(values, axis=-1, keepdims=True)
+    spread = jnp.mean(center * center, axis=-1, keepdims=True)
+    return center * lax.rsqrt(spread + EPSILON) * gain_row
+
+
+def qkv_kernel(place, first, second, cos, sin, embed, gain, weight, *rest):
+    inputs_out, qkv_out = rest[-2:]
+    mine, other = first[...].astype(jnp.float32), second[...].astype(jnp.float32)
+    leads = place[1] == 0
+    values = jnp.concatenate(
+        [jnp.where(leads, mine, other), jnp.where(leads, other, mine)], axis=0
+    )
+    masked = cos[:, MASK_LANE : MASK_LANE + 1] > 0.5
+    values = jnp.where(masked, embed[...].astype(jnp.float32), values)
+    inputs_out[...] = values.astype(jnp.bfloat16)
+    normed = norm_rows(values, gain[...]).astype(jnp.bfloat16)
+    columns = jnp.dot(normed, weight[...], preferred_element_type=jnp.float32)
+    cosine, sine = cos[...], sin[...]
+    lane = lax.broadcasted_iota(jnp.int32, cosine.shape, 1)
+    first_head = lane < HD // 2
+
+    def turn(start):
+        a = columns[:, start : start + LANES]
+        b = columns[:, start + LANES : start + 2 * LANES]
+        return a * cosine - b * sine, b * cosine + a * sine
+
+    query_a, query_b = turn(0)
+    key_a, key_b = turn(2 * LANES)
+    zero = jnp.zeros_like(key_a)
+    parts = [
+        query_a,
+        query_b,
+        jnp.where(first_head, key_a, zero),
+        jnp.where(first_head, key_b, zero),
+        jnp.where(first_head, zero, key_a),
+        jnp.where(first_head, zero, key_b),
+    ]
+    values_part = columns[:, 4 * LANES :]
+    wide = lax.broadcasted_iota(jnp.int32, values_part.shape, 1)
+    ones = jnp.where(wide == 2 * HD, 1.0, 0.0)
+    parts.append(jnp.where(wide < HD, values_part, ones))
+    parts.append(jnp.where((wide >= HD) & (wide < 2 * HD), values_part, ones))
+    qkv_out[...] = jnp.concatenate(parts, axis=1).astype(jnp.bfloat16)
+
+
+def qkv_call(place, pair, tables, embed, gain, weight, earlier, total):
+    rows = 2 * pair[0].shape[0]
+    whole = lambda shape: pl.BlockSpec(shape, lambda i, place: (0,) * len(shape))
+    block = lambda width: pl.BlockSpec((rows, width), lambda i, place: (place[0], 0))
+    width = 10 * LANES
+    in_specs = [
+        whole(pair[0].shape),
+        whole(pair[1].shape),
+        block(LANES),
+        block(LANES),
+        whole(embed.shape),
+        whole(gain.shape),
+        whole(weight.shape),
+    ] + [pl.BlockSpec(memory_space=pl.ANY)] * len(earlier)
+    return pl.pallas_call(
+        qkv_kernel,
+        grid_spec=pltpu.PrefetchScalarGridSpec(
+            num_scalar_prefetch=1,
+            grid=(1,),
+            in_specs=in_specs,
+            out_specs=[block(D), block(width)],
+        ),
+        out_shape=[
+            jax.ShapeDtypeStruct((total, D), jnp.bfloat16),
+            jax.ShapeDtypeStruct((total, width), jnp.bfloat16),
+        ],
+        input_output_aliases={8: 0, 9: 1} if earlier else {},
+        compiler_params=pltpu.CompilerParams(vmem_limit_bytes=24 << 20),
+        cost_estimate=pl.CostEstimate(
+            flops=2 * rows * D * weight.shape[1],
+            bytes_accessed=2 * (rows * (2 * D + width) + weight.size),
+            transcendentals=rows,
+        ),
+        name="norm_qkv",
+    )(place, *pair, *tables, embed, gain, weight, *earlier)
+
+
+BLOCK = 256
+
+
+def attention_kernel(chunk, segments, segment_rows, columns, block, out, scores, high, acc):
+    rows = acc.shape[0]
+    blocks = scores.shape[1]
+    scale = HD**-0.5
+    for part in range(rows // BLOCK):
+        start = chunk * rows + part * BLOCK
+        segment_low = segments[start]
+        segment_high = segments[start + BLOCK - 1]
+        all_rows = segment_rows[...]
+        before = jnp.sum((all_rows < segment_low).astype(jnp.int32))
+        through = jnp.sum((all_rows <= segment_high).astype(jnp.int32))
+        begin = before // BLOCK
+        end = (through + BLOCK - 1) // BLOCK
+        queries = block[start : start + BLOCK, : 2 * LANES]
+        own = columns[start : start + BLOCK, SEGMENT_LANE : SEGMENT_LANE + 1]
+        own = jnp.broadcast_to(own, (BLOCK, BLOCK)).astype(jnp.int32)
+        high[...] = jnp.full_like(high, NEGATIVE)
+
+        def score(step, carry):
+            at = pl.ds(pl.multiple_of(step * BLOCK, BLOCK), BLOCK)
+            same = own == segment_rows[pl.ds(step, 1), :]
+            for head in range(2):
+                keys = block[at, (2 + 2 * head) * LANES : (4 + 2 * head) * LANES]
+                values = lax.dot_general(
+                    queries, keys, (((1,), (1,)), ((), ())), preferred_element_type=jnp.float32
+                )
+                values = jnp.where(same, values, NEGATIVE)
+                scores[head, step] = values
+                high[head] = jnp.maximum(
+                    high[head], jnp.maximum(values[:, :LANES], values[:, LANES:])
+                )
+            return carry
+
+        lax.fori_loop(begin, end, score, 0)
+        highest = [jnp.max(high[head], axis=-1, keepdims=True) for head in range(2)]
+        acc_shape = (BLOCK, 2 * LANES)
+
+        def weigh(step, carry):
+            at = pl.ds(pl.multiple_of(step * BLOCK, BLOCK), BLOCK)
+            sums = []
+            for head in range(2):
+                weights = jnp.exp((scores[head, step] - highest[head]) * scale)
+                values = block[at, (6 + 2 * head) * LANES : (8 + 2 * head) * LANES]
+                sums.append(
+                    carry[head]
+                    + jnp.dot(
+                        weights.astype(jnp.bfloat16), values, preferred_element_type=jnp.float32
+                    )
+                )
+            return tuple(sums)
+
+        zero = jnp.zeros(acc_shape, jnp.float32)
+        sums = lax.fori_loop(begin, end, weigh, (zero, zero))
+        total = sum(
+            one / one[:, 2 * HD : 2 * HD + 1] for one in sums
+        )
+        acc[part * BLOCK : (part + 1) * BLOCK, :] = total
+    out[:rows] = acc[:, :LANES].astype(jnp.bfloat16)
+    half = rows // 2
+    low, up = acc[:half, LANES:], acc[half:, LANES:]
+    lane = lax.broadcasted_iota(jnp.int32, low.shape, 1)
+    tail = 2 * HD - LANES
+    zero = jnp.zeros_like(low)
+    packed = jnp.where(
+        lane < tail, low, jnp.where(lane < 2 * tail, pltpu.roll(up, tail, 1), zero)
+    )
+    out[rows:] = packed.astype(jnp.bfloat16)
+
+
+def attention_call(chunk, chunks, segments, segment_rows, columns, block):
+    total = block.shape[0]
+    rows = total // chunks
+    vmem = pl.BlockSpec(memory_space=pltpu.VMEM)
+    return pl.pallas_call(
+        functools.partial(attention_kernel, chunk),
+        in_specs=[pl.BlockSpec(memory_space=pltpu.SMEM), vmem, vmem, vmem],
+        out_specs=vmem,
+        out_shape=jax.ShapeDtypeStruct((rows + rows // 2, LANES), jnp.bfloat16),
+        scratch_shapes=[
+            pltpu.VMEM((2, total // BLOCK, BLOCK, BLOCK), jnp.float32),
+            pltpu.VMEM((2, BLOCK, LANES), jnp.float32),
+            pltpu.VMEM((rows, 2 * LANES), jnp.float32),
+        ],
+        compiler_params=pltpu.CompilerParams(vmem_limit_bytes=24 << 20),
+        cost_estimate=pl.CostEstimate(
+            flops=8 * rows * total * 2 * LANES,
+            bytes_accessed=2 * block.size,
+            transcendentals=rows * total,
+        ),
+        name="attention",
+    )(segments, segment_rows, columns, block)
+
+
+def merge_kernel(shards, ids, *refs):
+    sources = refs[:shards]
+    inputs, out_weight, gain, merge_weight, bias, out = refs[shards : shards + 6]
+    wide, tail, merge, state, wide_sems, tail_sems, merge_sem = refs[shards + 6 :]
+    rows = inputs.shape[0]
+    half = rows // 2
+    rest = 2 * HD - LANES
+    merge_copy = pltpu.make_async_copy(merge_weight, merge, merge_sem)
+    tail[...] = jnp.zeros_like(tail)
+    copies = []
+    for place in range(shards):
+        start = pl.multiple_of(ids[place] * (2 * HD), 16)
+        copies.append(
+            pltpu.make_async_copy(
+                out_weight.at[pl.ds(start, LANES), :],
+                wide.at[pl.ds(place * LANES, LANES), :],
+                wide_sems.at[place],
+            )
+        )
+        copies.append(
+            pltpu.make_async_copy(
+                out_weight.at[pl.ds(start + LANES, rest), :],
+                tail.at[pl.ds(rest + place * LANES, rest), :],
+                tail_sems.at[place],
+            )
+        )
+    for copy in copies:
+        copy.start()
+    merge_copy.start()
+    for copy in copies:
+        copy.wait()
+    size = shards * LANES
+    for part in range(2):
+        at = slice(part * half, (part + 1) * half)
+        wide_in = jnp.concatenate([source[at, :] for source in sources], axis=1)
+        tail_in = jnp.concatenate([source[rows:, :] for source in sources], axis=1)
+        offset = rest if part == 0 else 0
+        mixed = jnp.dot(wide_in, wide[...], preferred_element_type=jnp.float32)
+        mixed = mixed + jnp.dot(
+            tail_in, tail[offset : offset + size, :], preferred_element_type=jnp.float32
+        )
+        residual = inputs[at, :].astype(jnp.float32) + mixed
+        normed = norm_rows(residual, gain[...])
+        for column in range(D // LANES):
+            state[column, at, :] = normed[:, column * LANES : (column + 1) * LANES]
+    merge_copy.wait()
+    groups = rows // 4
+    total = None
+    for quadrant in range(4):
+        tokens = jnp.concatenate(
+            [
+                state[column, pl.ds(quadrant, groups, stride=4), :].astype(jnp.bfloat16)
+                for column in range(D // LANES)
+            ],
+            axis=1,
+        )
+        term = jnp.dot(
+            tokens, merge[quadrant * D : (quadrant + 1) * D, :], preferred_element_type=jnp.float32
+        )
+        total = term if total is None else total + term
+    result = total + bias[...]
+    whole = result.shape[1] // LANES
+    for column in range(whole):
+        out[column * groups : (column + 1) * groups, :] = result[
+            :, column * LANES : (column + 1) * LANES
+        ].astype(jnp.bfloat16)
+    low = result[: groups // 2, whole * LANES :]
+    up = result[groups // 2 :, whole * LANES :]
+    out[whole * groups :, :] = jnp.concatenate([low, up], axis=1).astype(jnp.bfloat16)
+
+
+def merge_call(chunk, chunks, ids, sources, inputs, out_weight, gain, merge_weight, bias):
+    shards = len(sources)
+    rows = inputs.shape[0] // chunks
+    groups = rows // 4
+    width = merge_weight.shape[1]
+    fixed = lambda shape: pl.BlockSpec(shape, lambda i, ids: (0,) * len(shape))
+    anywhere = pl.BlockSpec(memory_space=pl.ANY)
+    rest = 2 * HD - LANES
+    return pl.pallas_call(
+        functools.partial(merge_kernel, shards),
+        grid_spec=pltpu.PrefetchScalarGridSpec(
+            num_scalar_prefetch=1,
+            grid=(1,),
+            in_specs=[fixed(source.shape) for source in sources]
+            + [
+                pl.BlockSpec((rows, D), lambda i, ids: (chunk, 0)),
+                anywhere,
+                fixed(gain.shape),
+                anywhere,
+                fixed(bias.shape),
+            ],
+            out_specs=fixed((groups * width // LANES, LANES)),
+            scratch_shapes=[
+                pltpu.VMEM((shards * LANES, D), jnp.bfloat16),
+                pltpu.VMEM((shards * LANES + LANES, D), jnp.bfloat16),
+                pltpu.VMEM(merge_weight.shape, jnp.bfloat16),
+                pltpu.VMEM((D // LANES, rows, LANES), jnp.float32),
+                pltpu.SemaphoreType.DMA((shards,)),
+                pltpu.SemaphoreType.DMA((shards,)),
+                pltpu.SemaphoreType.DMA,
+            ],
+        ),
+        out_shape=jax.ShapeDtypeStruct((groups * width // LANES, LANES), jnp.bfloat16),
+        compiler_params=pltpu.CompilerParams(vmem_limit_bytes=40 << 20),
+        cost_estimate=pl.CostEstimate(
+            flops=2 * rows * D * D + 2 * groups * merge_weight.size,
+            bytes_accessed=2 * (D * D + merge_weight.size + 3 * rows * D),
+            transcendentals=rows,
+        ),
+        name="out_merge",
+    )(ids, *sources, inputs, out_weight, gain, merge_weight, bias)
+
+
+def select_kernel(packs, picks, *refs):
+    parts, out = refs[:-1], refs[-1]
+    most, width = out.shape[1:]
+    whole = width // LANES
+    groups = parts[0].shape[1] * LANES // width
+    half = groups // 2
+    slot = lax.broadcasted_iota(jnp.int32, (most, groups), 0)
+    row = lax.broadcasted_iota(jnp.int32, (most, groups), 1)
+    for pack in range(packs):
+        first, length = picks[pack], picks[packs + pack]
+        sums = [None] * (whole + 2)
+        for position, part in enumerate(parts):
+            chosen = ((row + position * groups) == (slot + first)) & (slot < length)
+            chosen = jnp.where(chosen, 1.0, 0.0).astype(jnp.bfloat16)
+            terms = [
+                jnp.dot(
+                    chosen,
+                    part[pack, column * groups : (column + 1) * groups, :],
+                    preferred_element_type=jnp.float32,
+                )
+                for column in range(whole)
+            ]
+            packed = part[pack, whole * groups :, :]
+            terms.append(jnp.dot(chosen[:, :half], packed, preferred_element_type=jnp.float32))
+            terms.append(jnp.dot(chosen[:, half:], packed, preferred_element_type=jnp.float32))
+            sums = [term if kept is None else kept + term for kept, term in zip(sums, terms)]
+        for column in range(whole):
+            out[pack, :, column * LANES : (column + 1) * LANES] = sums[column].astype(jnp.bfloat16)
+        middle = LANES // 2
+        last = sums[whole] + pltpu.roll(sums[whole + 1], middle, 1)
+        out[pack, :, whole * LANES :] = last[:, :middle].astype(jnp.bfloat16)
+
+
+def select_call(picks, parts, packs, most, width):
+    vmem = pl.BlockSpec(memory_space=pltpu.VMEM)
+    return pl.pallas_call(
+        functools.partial(select_kernel, packs),
+        in_specs=[pl.BlockSpec(memory_space=pltpu.SMEM)] + [vmem] * len(parts),
+        out_specs=vmem,
+        out_shape=jax.ShapeDtypeStruct((packs, most, width), jnp.bfloat16),
+        compiler_params=pltpu.CompilerParams(vmem_limit_bytes=24 << 20),
+        cost_estimate=pl.CostEstimate(
+            flops=2 * packs * most * packs * most * width,
+            bytes_accessed=4 * packs * most * width,
+            transcendentals=0,
+        ),
+        name="select_rows",
+    )(picks, *parts)
+
+
+MASK_LANE = HD
+SEGMENT_LANE = HD + 1
+NEGATIVE = -1e30
+
+
+def send_across(value, flip, size):
+    return lax.ppermute(value, "seq", [(i, i ^ flip) for i in range(size)])
+
+
+def gather_pairs(value, size):
+    across = [flip for flip in range(0, size, 2)]
+    same_core = [value if flip == 0 else send_across(value, flip, size) for flip in across]
+    return [(one, send_across(one, 1, size)) for one in same_core]
+
+
+def weight_order(heads_here):
+    quarter = HD // 4
+    order = -np.ones((6 * LANES,), np.int32)
+    for head in range(heads_here):
+        base = head * 3 * HD
+        for kind in range(2):
+            for half in range(2):
+                for letter in range(2):
+                    target = (2 * kind + letter) * LANES + head * (HD // 2) + half * quarter
+                    source = base + kind * HD + half * (HD // 2) + letter * quarter
+                    order[target : target + quarter] = np.arange(source, source + quarter)
+        target = 4 * LANES + head * HD
+        order[target : target + HD] = np.arange(base + 2 * HD, base + 3 * HD)
+    return order
+
+
+def fast_local(
+    patches,
+    patch_mask,
+    mask_embed,
+    norm_gain,
+    qkv_weight,
+    segment_ids,
+    patch_rows,
+    patch_column,
+    out_weight,
+    merge_gain,
+    merge_weight,
+    merge_bias,
+    image_owner,
+):
+    chunks = CHUNKS
+    local_rows = patches.shape[1]
+    shards = lax.axis_size("seq")
+    packs = lax.axis_size("pack")
+    heads_here = HEADS // shards
+    images = image_owner.shape[1]
+    total = local_rows * shards
+    me = lax.axis_index("seq")
+    pack = lax.axis_index("pack")
+    pairs = gather_pairs(patches[0], shards)
+
+    owners = jnp.pad(image_owner[0], (0, local_rows - images))
+    labels = jnp.stack([segment_ids[0], patch_rows[0], patch_column[0], patch_mask[0], owners])
+    labels = jnp.pad(labels, ((0, 3), (0, 0)))
+    gathered = lax.all_gather(labels, ("pack", "seq"), axis=0, tiled=False)
+    gathered = gathered.reshape(packs, shards, 8, local_rows)
+    mine = lax.dynamic_index_in_dim(gathered, pack, 0, keepdims=False)
+    mine = jnp.swapaxes(mine, 0, 1).reshape(8, total)
+    segments = mine[0]
+    quarter = HD // 4
+    frequency = 10000.0 ** (-jnp.arange(quarter, dtype=jnp.float32) / quarter)
+    frequency = jnp.tile(frequency, 2 * heads_here)
+    frequency = jnp.pad(frequency, (0, LANES - frequency.shape[0]))
+    lane = jnp.arange(LANES)
+    by_column = (lane // quarter) % 2 == 1
+    position = jnp.where(by_column[None, :], mine[2][:, None], mine[1][:, None])
+    angles = position.astype(jnp.float32) * frequency[None, :]
+    cosine = jnp.where(lane[None, :] == MASK_LANE, mine[3][:, None].astype(jnp.float32), jnp.cos(angles))
+    cosine = jnp.where(lane[None, :] == SEGMENT_LANE, segments[:, None].astype(jnp.float32), cosine)
+    sine = jnp.sin(angles)
+
+    merged_segments = gathered[:, :, 0, ::4].reshape(packs, -1)
+    image_ids = jnp.arange(images, dtype=jnp.int32)
+    owned = gathered[:, 0, 4, :images] == pack
+    member = merged_segments[:, None, :] == image_ids[None, :, None]
+    below = merged_segments[:, None, :] < image_ids[None, :, None]
+    lengths = jnp.sum(jnp.where(owned[:, :, None], member, False).astype(jnp.int32), axis=(1, 2))
+    starts = jnp.sum(jnp.where(owned[:, :, None], below, False).astype(jnp.int32), axis=(1, 2))
+    picks = jnp.concatenate([starts, lengths])
+
+    order = jnp.asarray(weight_order(heads_here))
+    spread = (jnp.arange(qkv_weight.shape[1])[:, None] == order[None, :]).astype(jnp.bfloat16)
+    weight = jnp.dot(qkv_weight, spread, preferred_element_type=jnp.float32).astype(jnp.bfloat16)
+    embed = mask_embed[None, :]
+    gain = norm_gain.astype(jnp.float32)[None, :]
+    merge_gain_row = merge_gain.astype(jnp.float32)[None, :]
+    bias = merge_bias.astype(jnp.float32)[None, :]
+
+    buffers = ()
+    for place, pair in enumerate(pairs):
+        where = jnp.stack([(me // 2) ^ place, me % 2]).astype(jnp.int32)
+        buffers = qkv_call(where, pair, (cosine, sine), embed, gain, weight, buffers, total)
+    inputs, block = buffers
+
+    segment_rows = segments.reshape(total // BLOCK, BLOCK)
+    attended = [
+        gather_pairs(
+            attention_call(chunk, chunks, segments, segment_rows, cosine, block), shards
+        )
+        for chunk in range(chunks)
+    ]
+    ids = jnp.stack([me ^ place for place in range(shards)]).astype(jnp.int32)
+    delivered = []
+    for chunk in range(chunks):
+        sources = [one for pair in attended[chunk] for one in pair]
+        projected = merge_call(
+            chunk, chunks, ids, sources, inputs, out_weight, merge_gain_row, merge_weight, bias
+        )
+        delivered.append(lax.all_gather(projected, "pack", axis=0, tiled=False))
+    most = 2 * (total // 4) // images
+    return select_call(picks, delivered, packs, most, merge_weight.shape[1])[None]
+
+
+CHUNKS = 2
+
+
+def local(*arguments):
+    patches, weight = arguments[0], arguments[4]
+    shards = lax.axis_size("seq")
+    fits = shards == 8 and HEADS // shards == 2 and weight.shape[1] == 6 * HD
+    fits = fits and (patches.shape[1] * shards) % (CHUNKS * BLOCK) == 0
+    return fast_local(*arguments) if fits else general_local(*arguments)
+
+
 def solution(mesh):
     placed = (
         P("pack", "seq", None),

time: 199 us -> 203 us (1.020)
  waiting for transfers between devices: 74.3 us -> 3.21 us
  Pallas kernels: 0 us -> 59.1 us
  blocking collectives: 35.5 us -> 90.9 us
  matrix products: 38.7 us -> 2.61 us
  starting transfers between devices: 3.75 us -> 21.3 us
  between operations: 13.8 us -> 0.31 us
  other arithmetic: 13.2 us -> 4.33 us
  local copies, waits for them, and re-layouts: 19.1 us -> 21.5 us
    all_gather x1 -> x3, blocking collectives: 10.5 us -> 90.9 us  [the longest x1 56.7 us: fast_local(): gathered = lax.all_gather(labels, ('pack', 'seq'), axis=0, tiled=False)]
    all_gather x2 -> x0, waiting for transfers between devices: 61.8 us -> none  [the longest x1 35.5 us: local(): lax.all_gather(merged, 'seq', axis=0, tiled=True)]
    pallas_call x0 -> x9, Pallas kernels: none -> 59.1 us  [the longest x2 24.5 us: merge_call(): pl.pallas_call(functools.partial(merge_kernel, shards), grid_spec=pltpu.P...]
    dot_general x6 -> x1, matrix products: 28.4 us -> 2.61 us  [fast_local(): jnp.dot(qkv_weight, spread, preferred_element_type=jnp.float32)]
    all_to_all x1 -> x0, blocking collectives: 24.9 us -> none  [local(): lax.all_to_all(outgoing, 'pack', split_axis=0, concat_axis=0, tiled=True)]
    ppermute x0 -> x21, starting transfers between devices: none -> 21.3 us  [send_across(): return lax.ppermute(value, 'seq', [(i, i ^ flip) for i in range(size)])]
    all_to_all x1 -> x0, waiting for transfers between devices: 12.5 us -> none  [local(): lax.all_to_all(result, 'seq', split_axis=0, concat_axis=1, tiled=True)]
    unnamed x28 -> x23, local copies, waits for them, and re-layouts: 2.9 us -> 14.6 us
  transfers between devices with their start and end apart: 3 -> 21, of which waited for: 3 -> 2; matrix products, arithmetic and copies ran while one was open for 2% -> 11% of each run, Pallas kernels for 0% -> 16%
where the time goes in v1:
time: 203 us
  blocking collectives  90.9 us (45%)
  Pallas kernels  59.1 us (29%)
  local copies, waits for them, and re-layouts  21.5 us (11%)
  starting transfers between devices  21.3 us (10%)
  other arithmetic  4.33 us (2%)
  waiting for transfers between devices  3.21 us (2%)
  matrix products  2.61 us (1%)
    all_gather x1, blocking collectives, fast_local(): gathered = lax.all_gather(labels, ('pack', 'seq'), axis=0, tiled=False)  56.7 us
    all_gather x2, blocking collectives, fast_local(): delivered.append(lax.all_gather(projected, 'pack', axis=0, tiled=False))  34.2 us
    pallas_call x2, Pallas kernels, merge_call(): pl.pallas_call(functools.partial(merge_kernel, shards), grid_spec=pltpu.P...  24.5 us
    ppermute x21, starting transfers between devices, send_across(): return lax.ppermute(value, 'seq', [(i, i ^ flip) for i in range(size)])  21.3 us
    pallas_call x2, Pallas kernels, attention_call(): pl.pallas_call(functools.partial(attention_kernel, chunk), in_specs=[pl.B...  17.9 us
    unnamed x23, local copies, waits for them, and re-layouts  14.6 us
    pallas_call x4, Pallas kernels, qkv_call(): pl.pallas_call(qkv_kernel, grid_spec=pltpu.PrefetchScalarGridSpec(num_sca...  14.2 us
  transfers between devices with their start and end apart: 21, of which 2 were waited for; matrix products, arithmetic and copies ran while one was open for 11% of the time, Pallas kernels for 16%

profile of v1, /device:TPU:0, one launch (start us, length us, event | category | flops | bytes accessed | tf_op | source)
XLA Modules:
  0.0 203.3 jit_solution(18311960281507382919)
XLA Ops:
  0.5 2.6 %collective-permute-start.4 = (bf16[192,1408]{1,0:T(8,128)(2,1)}, bf16[192,1408]{1,0:T(8,128)(2,1)}, u32[]{:S(2)}, u32[]{:S(2)}) collective-permute-start(bf16[192,1408]{1,0:T(8,128)(2,1)} %bitcast.35), channel_id=1, source_target_pairs={{0,8},{4,12},{8,0},{12,4},{16,24},{20,28},{24,16},{28,20},{1,9},{5... | collective-permute-start | bytes 1622024 | tf_op jit(solution)/shard_map/ppermute | solution.py:501
  3.0 1.5 collective-permute-start.2
  5.3 0.7 stack.64
  6.1 56.7 %all-gather = s32[256,192]{1,0:T(8,128)S(1)} all-gather(s32[8,192]{1,0:T(8,128)S(1)} %pad.13), channel_id=2, replica_groups=mesh['seq'=8,'pack'=4] {'pack','seq'}, dimensions={0}, use_global_device_ids=true | all-gather | bytes 202752 | tf_op jit(solution)/shard_map/all_gather | solution.py:555
  63.5 2.9 %fusion.2 = (f32[1536,128]{1,0:T(8,128)S(1)}, f32[1536,128]{1,0:T(8,128)S(1)}) fusion(f32[128]{0:T(128)S(1)} %pad.14, s32[1536]{0:T(1024)S(1)} %broadcast_in_dim.110, s32[1536]{0:T(1024)S(1)} %broadcast_in_dim.108, pred[128]{0:T(512)(128)(4,1)S(1)} %get-tuple-element.29, f32[1536]{0:T(1024)S(1)} %convert_element_type.43, ...), kind=kLoop, calls=%fused_computation.6 | loop fusion | flops 983040 | bytes 1598336 | tf_op jit(solution)/shard_map/sin | solution.py:570
  67.1 0.7 broadcast_in_dim.112.embed
  67.8 0.7 reshape.83.gain
  69.0 2.6 %fusion.weight = bf16[1408,768]{1,0:T(8,128)(2,1)S(1)} fusion(bf16[1408,528]{0,1:T(8,128)(2,1)S(1)} %copy-done, s32[768]{0:T(1024)} %constant.93.clone), kind=kOutput, calls=%fused_computation.1 | convolution fusion | flops 1143386112 | bytes 3652608 | tf_op jit(solution)/shard_map/dot_general | solution.py:583
  71.6 3.5 %norm_qkv.4 = (bf16[1536,1408]{1,0:T(8,128)(2,1)S(1)}, bf16[1536,1280]{1,0:T(8,128)(2,1)S(1)}) custom-call(s32[2]{0:T(128)S(1)} %pad_add_fusion.4.place, bf16[192,1408]{1,0:T(8,128)(2,1)S(1)} %bitcast.38, bf16[192,1408]{1,0:T(8,128)(2,1)} %collective-permute-done.6.second, f32[1536,128]{1,0:T(8,128)S(1)} %get-tuple-element.28.cos.columns, ...), custom_call_target="tpu_custom_call" | custom-call | flops 830472192 | bytes 5308416 | tf_op jit(solution)/shard_map/norm_qkv/pallas_call | solution.py:212
  75.1 3.6 %norm_qkv.5 = (bf16[1536,1408]{1,0:T(8,128)(2,1)S(1)}, bf16[1536,1280]{1,0:T(8,128)(2,1)S(1)}) custom-call(s32[2]{0:T(128)S(1)} %pad_add_fusion.3.place, bf16[192,1408]{1,0:T(8,128)(2,1)} %collective-permute-done.4.first, bf16[192,1408]{1,0:T(8,128)(2,1)} %collective-permute-done.5.second, ...), custom_call_target="tpu_custom_call", output_to_operand_aliasing={{0}: (8, {}), {1}: (9, {})} | custom-call | flops 830472192 | bytes 5308416 | tf_op jit(solution)/shard_map/norm_qkv/pallas_call | solution.py:212
  78.7 3.6 %norm_qkv.6 = (bf16[1536,1408]{1,0:T(8,128)(2,1)S(1)}, bf16[1536,1280]{1,0:T(8,128)(2,1)S(1)}) custom-call(s32[2]{0:T(128)S(1)} %pad_add_fusion.2.place, bf16[192,1408]{1,0:T(8,128)(2,1)} %collective-permute-done.2.first, bf16[192,1408]{1,0:T(8,128)(2,1)} %collective-permute-done.3.second, ...), custom_call_target="tpu_custom_call", output_to_operand_aliasing={{0}: (8, {}), {1}: (9, {})} | custom-call | flops 830472192 | bytes 5308416 | tf_op jit(solution)/shard_map/norm_qkv/pallas_call | solution.py:212
  82.4 3.5 %norm_qkv.7 = (bf16[1536,1408]{1,0:T(8,128)(2,1)S(1)}, bf16[1536,1280]{1,0:T(8,128)(2,1)S(1)}) custom-call(s32[2]{0:T(128)S(1)} %pad_add_fusion.1.place, bf16[192,1408]{1,0:T(8,128)(2,1)} %collective-permute-done.first, bf16[192,1408]{1,0:T(8,128)(2,1)S(1)} %collective-permute-done.1.second, ...), custom_call_target="tpu_custom_call", output_to_operand_aliasing={{0}: (8, {}), {1}: (9, {})} | custom-call | flops 830472192 | bytes 5308416 | tf_op jit(solution)/shard_map/norm_qkv/pallas_call | solution.py:212
  85.9 9.0 %attention.3.refs_0_ = bf16[1152,128]{1,0:T(8,128)(2,1)S(1)} custom-call(s32[1536]{0:T(1024)S(1)} %squeeze.16.segments, s32[6,256]{1,0:T(8,128)S(1)} %reshape_squeeze.3.segment_rows, f32[1536,128]{1,0:T(8,128)S(1)} %get-tuple-element.28.cos.columns, bf16[1536,1280]{1,0:T(8,128)(2,1)S(1)} %get-tuple-element.19.block), custom_call_target="tpu_custom_call" | custom-call | flops 2415919104 | bytes 3932160 | tf_op jit(solution)/shard_map/attention/pallas_call | solution.py:311
  95.0 3.4 %collective-permute-start.19 = (bf16[1152,128]{1,0:T(8,128)(2,1)S(1)}, bf16[1152,128]{1,0:T(8,128)(2,1)}, u32[]{:S(2)}, u32[]{:S(2)}) collective-permute-start(bf16[1152,128]{1,0:T(8,128)(2,1)S(1)} %attention.3.refs_0_), channel_id=1, source_target_pairs={{0,24},{4,28},{8,16},{12,20},{16,8},{20,12},{24,0},{28,4},{1,25},{... | collective-permute-start | bytes 884744 | tf_op jit(solution)/shard_map/ppermute | solution.py:501
  98.4 8.8 %attention.2.refs_0_ = bf16[1152,128]{1,0:T(8,128)(2,1)S(1)} custom-call(s32[1536]{0:T(1024)S(1)} %squeeze.16.segments, s32[6,256]{1,0:T(8,128)S(1)} %reshape_squeeze.3.segment_rows, f32[1536,128]{1,0:T(8,128)S(1)} %get-tuple-element.28.cos.columns, bf16[1536,1280]{1,0:T(8,128)(2,1)S(1)} %get-tuple-element.19.block), custom_call_target="tpu_custom_call" | custom-call | flops 2415919104 | bytes 3932160 | tf_op jit(solution)/shard_map/attention/pallas_call | solution.py:311
  107.4 0.7 slice.28
  108.1 1.5 collective-permute-start.12
  109.6 0.8 collective-permute-done.17.refs_4_
  110.4 9.1 %collective-permute-start.8 = (bf16[1152,128]{1,0:T(8,128)(2,1)S(1)}, bf16[1152,128]{1,0:T(8,128)(2,1)}, u32[]{:S(2)}, u32[]{:S(2)}) collective-permute-start(bf16[1152,128]{1,0:T(8,128)(2,1)S(1)} %attention.2.refs_0_), channel_id=1, source_target_pairs={{0,8},{4,12},{8,0},{12,4},{16,24},{20,28},{24,16},{28,20},{1,9},{5... | collective-permute-start | bytes 884744 | tf_op jit(solution)/shard_map/ppermute | solution.py:501
  119.5 0.7 copy-done.6
  120.7 2.3 %collective-permute-done.10.refs_4_ = bf16[1152,128]{1,0:T(8,128)(2,1)S(1)} collective-permute-done((bf16[1152,128]{1,0:T(8,128)(2,1)S(1)}, bf16[1152,128]{1,0:T(8,128)(2,1)S(1)}, u32[]{:S(2)}, u32[]{:S(2)}) %collective-permute-start.10) | collective-permute-done | bytes 294944 | tf_op jit(solution)/shard_map/ppermute | solution.py:501
  123.1 2.1 %slice.23 = s32[4,8,1,48]{3,2,1,0:T(1,128)S(1)} slice(s32[4,8,8,192]{3,2,1,0:T(8,128)} %bitcast.43), slice={[0:4:1], [0:8:1], [0:1:1], [0:192:4]} | slice | bytes 12288 | tf_op jit(solution)/shard_map/slice | solution.py:572
  125.2 8.5 %copy.29.refs_11_ = bf16[5632,448]{1,0:T(8,128)(2,1)} copy(bf16[5632,448]{0,1:T(8,128)(2,1)} %param.24) | data formatting | bytes 10092544 | tf_op args[10]
  134.3 0.7 reduce.3
  136.7 2.2 %copy-done.2 = bf16[1536,1408]{1,0:T(8,128)(2,1)S(1)} copy-done((bf16[1536,1408]{1,0:T(8,128)(2,1)S(1)}, bf16[1536,1408]{1,0:T(8,128)(2,1)}, u32[]{:S(2)}) %copy-start.2) | copy-done | bytes 4325400
  138.9 2.1 %copy-done.3 = bf16[1408,1408]{1,0:T(8,128)(2,1)S(1)} copy-done((bf16[1408,1408]{1,0:T(8,128)(2,1)S(1)}, bf16[1408,1408]{1,0:T(8,128)(2,1)}, u32[]{:S(2)}) %copy-start.3) | copy-done | bytes 3964952
  141.0 1.0 copy-done.7
  142.0 12.5 %out_merge.3 = bf16[672,128]{1,0:T(8,128)(2,1)S(1)} custom-call(s32[8]{0:T(128)S(1)} %stack.73.ids, bf16[1152,128]{1,0:T(8,128)(2,1)S(1)} %attention.3.refs_0_, bf16[1152,128]{1,0:T(8,128)(2,1)S(1)} %copy-done.7, bf16[1152,128]{1,0:T(8,128)(2,1)S(1)} %collective-permute-done.15.refs_2_, bf16[1152,128]{1,0:T(8,128)(2,1)} %collective-permute-done.16.refs_3_, ...), custom_call_target="tpu_custom_call" | custom-call | flops 4013948928 | bytes 15499264 | tf_op jit(solution)/shard_map/out_merge/pallas_call | solution.py:410
  154.5 17.2 %all-gather.2 = bf16[2688,128]{1,0:T(8,128)(2,1)S(1)} all-gather(bf16[672,128]{1,0:T(8,128)(2,1)S(1)} %out_merge.3), channel_id=4, replica_groups=mesh['seq'=8,'pack'=4] {'pack'}, dimensions={0}, use_global_device_ids=true | all-gather | bytes 860160 | tf_op jit(solution)/shard_map/all_gather | solution.py:609
  171.7 12.0 %out_merge.2 = bf16[672,128]{1,0:T(8,128)(2,1)S(1)} custom-call(s32[8]{0:T(128)S(1)} %stack.73.ids, bf16[1152,128]{1,0:T(8,128)(2,1)S(1)} %attention.2.refs_0_, bf16[1152,128]{1,0:T(8,128)(2,1)S(1)} %collective-permute-done.7.refs_1_, bf16[1152,128]{1,0:T(8,128)(2,1)} %collective-permute-done.8.refs_2_, ...), custom_call_target="tpu_custom_call" | custom-call | flops 4013948928 | bytes 15499264 | tf_op jit(solution)/shard_map/out_merge/pallas_call | solution.py:410
  183.7 17.0 %all-gather.1 = bf16[2688,128]{1,0:T(8,128)(2,1)S(1)} all-gather(bf16[672,128]{1,0:T(8,128)(2,1)S(1)} %out_merge.2), channel_id=3, replica_groups=mesh['seq'=8,'pack'=4] {'pack'}, dimensions={0}, use_global_device_ids=true | all-gather | bytes 860160 | tf_op jit(solution)/shard_map/all_gather | solution.py:609
  200.7 2.5 %select_rows.1 = bf16[4,192,448]{2,1,0:T(8,128)(2,1)} custom-call(s32[8]{0:T(128)S(1)} %pad_add_fusion.picks, bf16[4,672,128]{2,1,0:T(8,128)(2,1)S(1)} %bitcast.33, bf16[4,672,128]{2,1,0:T(8,128)(2,1)S(1)} %bitcast.32), custom_call_target="tpu_custom_call" | custom-call | flops 528482304 | bytes 1376256 | tf_op jit(solution)/shard_map/select_rows/pallas_call | solution.py:480
  (82 shorter events, 6.1 us)
Async XLA Ops:
  0.0 68.9 %copy-start = (bf16[1408,528]{0,1:T(8,128)(2,1)S(1)}, bf16[1408,528]{0,1:T(8,128)(2,1)}, u32[]{:S(2)}) copy-start(bf16[1408,528]{0,1:T(8,128)(2,1)} %param.18) | copy-start | bytes 4460548
  0.0 71.6 %collective-permute-start.6 = (bf16[192,1408]{1,0:T(8,128)(2,1)}, bf16[192,1408]{1,0:T(8,128)(2,1)}, u32[]{:S(2)}, u32[]{:S(2)}) collective-permute-start(bf16[192,1408]{1,0:T(8,128)(2,1)} %bitcast.34), channel_id=1, source_target_pairs={{0,4},{4,0},{8,12},{12,8},{16,20},{20,16},{24,28},{28,24},{1,5},{5... | collective-permute-start | bytes 1622024 | tf_op jit(solution)/shard_map/ppermute | solution.py:501
  0.5 66.0 %collective-permute-start.4 = (bf16[192,1408]{1,0:T(8,128)(2,1)}, bf16[192,1408]{1,0:T(8,128)(2,1)}, u32[]{:S(2)}, u32[]{:S(2)}) collective-permute-start(bf16[192,1408]{1,0:T(8,128)(2,1)} %bitcast.35), channel_id=1, source_target_pairs={{0,8},{4,12},{8,0},{12,4},{16,24},{20,28},{24,16},{28,20},{1,9},{5... | collective-permute-start | bytes 1622024 | tf_op jit(solution)/shard_map/ppermute | solution.py:501
  3.0 63.8 %collective-permute-start.2 = (bf16[192,1408]{1,0:T(8,128)(2,1)}, bf16[192,1408]{1,0:T(8,128)(2,1)}, u32[]{:S(2)}, u32[]{:S(2)}) collective-permute-start(bf16[192,1408]{1,0:T(8,128)(2,1)} %bitcast.36), channel_id=1, source_target_pairs={{0,16},{4,20},{8,24},{12,28},{16,0},{20,4},{24,8},{28,12},{1,17},{... | collective-permute-start | bytes 1622024 | tf_op jit(solution)/shard_map/ppermute | solution.py:501
  4.5 64.0 %collective-permute-start = (bf16[192,1408]{1,0:T(8,128)(2,1)}, bf16[192,1408]{1,0:T(8,128)(2,1)}, u32[]{:S(2)}, u32[]{:S(2)}) collective-permute-start(bf16[192,1408]{1,0:T(8,128)(2,1)} %bitcast.37), channel_id=1, source_target_pairs={{0,24},{4,28},{8,16},{12,20},{16,8},{20,12},{24,0},{28,4},{1,25},{... | collective-permute-start | bytes 1622024 | tf_op jit(solution)/shard_map/ppermute | solution.py:501
  62.8 0.7 copy-start.8
  66.5 8.6 %collective-permute-start.5 = (bf16[192,1408]{1,0:T(8,128)(2,1)}, bf16[192,1408]{1,0:T(8,128)(2,1)}, u32[]{:S(2)}, u32[]{:S(2)}) collective-permute-start(bf16[192,1408]{1,0:T(8,128)(2,1)} %collective-permute-done.4.first), channel_id=1, source_target_pairs={{0,4},{4,0},{8,12},{12,8},{16,20},{20,16},{24,28},{28,24},{1,5},{5... | collective-permute-start | bytes 1622024 | tf_op jit(solution)/shard_map/ppermute | solution.py:501
  66.8 11.9 %collective-permute-start.3 = (bf16[192,1408]{1,0:T(8,128)(2,1)}, bf16[192,1408]{1,0:T(8,128)(2,1)}, u32[]{:S(2)}, u32[]{:S(2)}) collective-permute-start(bf16[192,1408]{1,0:T(8,128)(2,1)} %collective-permute-done.2.first), channel_id=1, source_target_pairs={{0,4},{4,0},{8,12},{12,8},{16,20},{20,16},{24,28},{28,24},{1,5},{5... | collective-permute-start | bytes 1622024 | tf_op jit(solution)/shard_map/ppermute | solution.py:501
  68.5 3.0 %copy-start.5 = (bf16[1,192,1408]{2,1,0:T(8,128)(2,1)S(1)}, bf16[1,192,1408]{2,1,0:T(8,128)(2,1)}, u32[]{:S(2)}) copy-start(bf16[1,192,1408]{2,1,0:T(8,128)(2,1)} %param.14) | copy-start | bytes 1622020
  68.5 13.8 %collective-permute-start.1 = (bf16[192,1408]{1,0:T(8,128)(2,1)}, bf16[192,1408]{1,0:T(8,128)(2,1)S(1)}, u32[]{:S(2)}, u32[]{:S(2)}) collective-permute-start(bf16[192,1408]{1,0:T(8,128)(2,1)} %collective-permute-done.first), channel_id=1, source_target_pairs={{0,4},{4,0},{8,12},{12,8},{16,20},{20,16},{24,28},{28,24},{1,5},{5... | collective-permute-start | bytes 1622024 | tf_op jit(solution)/shard_map/ppermute | solution.py:501
  85.8 9.0 %copy-start.1 = (bf16[1536,1408]{1,0:T(8,128)(2,1)}, bf16[1536,1408]{1,0:T(8,128)(2,1)S(1)}, u32[]{:S(2)}) copy-start(bf16[1536,1408]{1,0:T(8,128)(2,1)S(1)} %get-tuple-element.20.refs_8_) | copy-start | bytes 12976132
  94.9 13.2 %collective-permute-start.15 = (bf16[1152,128]{1,0:T(8,128)(2,1)S(1)}, bf16[1152,128]{1,0:T(8,128)(2,1)S(1)}, u32[]{:S(2)}, u32[]{:S(2)}) collective-permute-start(bf16[1152,128]{1,0:T(8,128)(2,1)S(1)} %attention.3.refs_0_), channel_id=1, source_target_pairs={{0,8},{4,12},{8,0},{12,4},{16,24},{20,28},{24,16},{28,20},{1,9},{5... | collective-permute-start | bytes 884744 | tf_op jit(solution)/shard_map/ppermute | solution.py:501
  95.0 15.5 %collective-permute-start.17 = (bf16[1152,128]{1,0:T(8,128)(2,1)S(1)}, bf16[1152,128]{1,0:T(8,128)(2,1)S(1)}, u32[]{:S(2)}, u32[]{:S(2)}) collective-permute-start(bf16[1152,128]{1,0:T(8,128)(2,1)S(1)} %attention.3.refs_0_), channel_id=1, source_target_pairs={{0,16},{4,20},{8,24},{12,28},{16,0},{20,4},{24,8},{28,12},{1,17},{... | collective-permute-start | bytes 884744 | tf_op jit(solution)/shard_map/ppermute | solution.py:501
  95.0 24.5 %collective-permute-start.19 = (bf16[1152,128]{1,0:T(8,128)(2,1)S(1)}, bf16[1152,128]{1,0:T(8,128)(2,1)}, u32[]{:S(2)}, u32[]{:S(2)}) collective-permute-start(bf16[1152,128]{1,0:T(8,128)(2,1)S(1)} %attention.3.refs_0_), channel_id=1, source_target_pairs={{0,24},{4,28},{8,16},{12,20},{16,8},{20,12},{24,0},{28,4},{1,25},{... | collective-permute-start | bytes 884744 | tf_op jit(solution)/shard_map/ppermute | solution.py:501
  98.4 21.1 %collective-permute-start.14 = (bf16[1152,128]{1,0:T(8,128)(2,1)S(1)}, bf16[1152,128]{1,0:T(8,128)(2,1)S(1)}, u32[]{:S(2)}, u32[]{:S(2)}) collective-permute-start(bf16[1152,128]{1,0:T(8,128)(2,1)S(1)} %attention.3.refs_0_), channel_id=1, source_target_pairs={{0,4},{4,0},{8,12},{12,8},{16,20},{20,16},{24,28},{28,24},{1,5},{5... | collective-permute-start | bytes 884744 | tf_op jit(solution)/shard_map/ppermute | solution.py:501
  107.3 15.8 %collective-permute-start.10 = (bf16[1152,128]{1,0:T(8,128)(2,1)S(1)}, bf16[1152,128]{1,0:T(8,128)(2,1)S(1)}, u32[]{:S(2)}, u32[]{:S(2)}) collective-permute-start(bf16[1152,128]{1,0:T(8,128)(2,1)S(1)} %attention.2.refs_0_), channel_id=1, source_target_pairs={{0,16},{4,20},{8,24},{12,28},{16,0},{20,4},{24,8},{28,12},{1,17},{... | collective-permute-start | bytes 884744 | tf_op jit(solution)/shard_map/ppermute | solution.py:501
  108.1 27.5 %collective-permute-start.12 = (bf16[1152,128]{1,0:T(8,128)(2,1)S(1)}, bf16[1152,128]{1,0:T(8,128)(2,1)S(1)}, u32[]{:S(2)}, u32[]{:S(2)}) collective-permute-start(bf16[1152,128]{1,0:T(8,128)(2,1)S(1)} %attention.2.refs_0_), channel_id=1, source_target_pairs={{0,24},{4,28},{8,16},{12,20},{16,8},{20,12},{24,0},{28,4},{1,25},{... | collective-permute-start | bytes 884744 | tf_op jit(solution)/shard_map/ppermute | solution.py:501
  110.4 25.6 %collective-permute-start.8 = (bf16[1152,128]{1,0:T(8,128)(2,1)S(1)}, bf16[1152,128]{1,0:T(8,128)(2,1)}, u32[]{:S(2)}, u32[]{:S(2)}) collective-permute-start(bf16[1152,128]{1,0:T(8,128)(2,1)S(1)} %attention.2.refs_0_), channel_id=1, source_target_pairs={{0,8},{4,12},{8,0},{12,4},{16,24},{20,28},{24,16},{28,20},{1,9},{5... | collective-permute-start | bytes 884744 | tf_op jit(solution)/shard_map/ppermute | solution.py:501
  119.5 16.7 %collective-permute-start.16 = (bf16[1152,128]{1,0:T(8,128)(2,1)S(1)}, bf16[1152,128]{1,0:T(8,128)(2,1)}, u32[]{:S(2)}, u32[]{:S(2)}) collective-permute-start(bf16[1152,128]{1,0:T(8,128)(2,1)S(1)} %collective-permute-done.15.refs_2_), channel_id=1, source_target_pairs={{0,4},{4,0},{8,12},{12,8},{16,20},{20,16},{24,28},{28,24},{1,5},{5... | collective-permute-start | bytes 884744 | tf_op jit(solution)/shard_map/ppermute | solution.py:501
  119.5 0.7 copy-start.6
  120.2 16.4 %collective-permute-start.18 = (bf16[1152,128]{1,0:T(8,128)(2,1)S(1)}, bf16[1152,128]{1,0:T(8,128)(2,1)}, u32[]{:S(2)}, u32[]{:S(2)}) collective-permute-start(bf16[1152,128]{1,0:T(8,128)(2,1)S(1)} %collective-permute-done.17.refs_4_), channel_id=1, source_target_pairs={{0,4},{4,0},{8,12},{12,8},{16,20},{20,16},{24,28},{28,24},{1,5},{5... | collective-permute-start | bytes 884744 | tf_op jit(solution)/shard_map/ppermute | solution.py:501
  123.1 13.6 %collective-permute-start.20 = (bf16[1152,128]{1,0:T(8,128)(2,1)}, bf16[1152,128]{1,0:T(8,128)(2,1)}, u32[]{:S(2)}, u32[]{:S(2)}) collective-permute-start(bf16[1152,128]{1,0:T(8,128)(2,1)} %collective-permute-done.19.refs_6_), channel_id=1, source_target_pairs={{0,4},{4,0},{8,12},{12,8},{16,20},{20,16},{24,28},{28,24},{1,5},{5... | collective-permute-start | bytes 884744 | tf_op jit(solution)/shard_map/ppermute | solution.py:501
  125.2 8.5 %copy-start.9 = (bf16[1408]{0:T(1024)(128)(2,1)S(1)}, bf16[1408]{0:T(1024)(128)(2,1)}, u32[]{:S(2)}) copy-start(bf16[1408]{0:T(1024)(128)(2,1)} %param.23) | copy-start | bytes 8452
  125.2 8.5 %copy-start.10 = (bf16[448]{0:T(512)(128)(2,1)S(1)}, bf16[448]{0:T(512)(128)(2,1)}, u32[]{:S(2)}) copy-start(bf16[448]{0:T(512)(128)(2,1)} %param.25) | copy-start | bytes 2692
  135.6 36.1 %collective-permute-start.7 = (bf16[1152,128]{1,0:T(8,128)(2,1)S(1)}, bf16[1152,128]{1,0:T(8,128)(2,1)S(1)}, u32[]{:S(2)}, u32[]{:S(2)}) collective-permute-start(bf16[1152,128]{1,0:T(8,128)(2,1)S(1)} %attention.2.refs_0_), channel_id=1, source_target_pairs={{0,4},{4,0},{8,12},{12,8},{16,20},{20,16},{24,28},{28,24},{1,5},{5... | collective-permute-start | bytes 884744 | tf_op jit(solution)/shard_map/ppermute | solution.py:501
  136.1 35.6 %collective-permute-start.11 = (bf16[1152,128]{1,0:T(8,128)(2,1)S(1)}, bf16[1152,128]{1,0:T(8,128)(2,1)S(1)}, u32[]{:S(2)}, u32[]{:S(2)}) collective-permute-start(bf16[1152,128]{1,0:T(8,128)(2,1)S(1)} %collective-permute-done.10.refs_4_), channel_id=1, source_target_pairs={{0,4},{4,0},{8,12},{12,8},{16,20},{20,16},{24,28},{28,24},{1,5},{5... | collective-permute-start | bytes 884744 | tf_op jit(solution)/shard_map/ppermute | solution.py:501
  136.2 35.5 %collective-permute-start.13 = (bf16[1152,128]{1,0:T(8,128)(2,1)S(1)}, bf16[1152,128]{1,0:T(8,128)(2,1)S(1)}, u32[]{:S(2)}, u32[]{:S(2)}) collective-permute-start(bf16[1152,128]{1,0:T(8,128)(2,1)S(1)} %collective-permute-done.12.refs_6_), channel_id=1, source_target_pairs={{0,4},{4,0},{8,12},{12,8},{16,20},{20,16},{24,28},{28,24},{1,5},{5... | collective-permute-start | bytes 884744 | tf_op jit(solution)/shard_map/ppermute | solution.py:501
  136.6 35.1 %collective-permute-start.9 = (bf16[1152,128]{1,0:T(8,128)(2,1)}, bf16[1152,128]{1,0:T(8,128)(2,1)S(1)}, u32[]{:S(2)}, u32[]{:S(2)}) collective-permute-start(bf16[1152,128]{1,0:T(8,128)(2,1)} %collective-permute-done.8.refs_2_), channel_id=1, source_target_pairs={{0,4},{4,0},{8,12},{12,8},{16,20},{20,16},{24,28},{28,24},{1,5},{5... | collective-permute-start | bytes 884744 | tf_op jit(solution)/shard_map/ppermute | solution.py:501
  136.7 2.2 %copy-start.2 = (bf16[1536,1408]{1,0:T(8,128)(2,1)S(1)}, bf16[1536,1408]{1,0:T(8,128)(2,1)}, u32[]{:S(2)}) copy-start(bf16[1536,1408]{1,0:T(8,128)(2,1)} %copy-done.1) | copy-start | bytes 12976132
  138.9 2.1 %copy-start.3 = (bf16[1408,1408]{1,0:T(8,128)(2,1)S(1)}, bf16[1408,1408]{1,0:T(8,128)(2,1)}, u32[]{:S(2)}) copy-start(bf16[1408,1408]{1,0:T(8,128)(2,1)} %refs_9_.3) | copy-start | bytes 11894788
  141.0 1.0 copy-start.7
  142.0 29.7 %copy-start.4 = (bf16[1408,1408]{1,0:T(8,128)(2,1)S(1)}, bf16[1408,1408]{1,0:T(8,128)(2,1)}, u32[]{:S(2)}) copy-start(bf16[1408,1408]{1,0:T(8,128)(2,1)} %refs_9_.3) | copy-start | bytes 11894788

commit v2 on v0

--- a/solution.py
+++ b/solution.py
@@ -1,6 +1,11 @@
+import functools
+
 import jax
 import jax.numpy as jnp
+import numpy as np
 from jax import lax
+from jax.experimental import pallas as pl
+from jax.experimental.pallas import tpu as pltpu
 from jax.sharding import PartitionSpec as P
 
 D = 1408
@@ -89,7 +94,7 @@
     return jnp.where(filled[:, :, None], picked, jnp.zeros_like(picked))
 
 
-def local(
+def general_local(
     patches,
     patch_mask,
     mask_embed,
@@ -141,6 +146,542 @@
     return delivered[None]
 
 
+LANES = 128
+BLOCK = 256
+POSITIONS = 64
+NEGATIVE = -1e30
+CHUNKS = (768, 768)
+
+
+def norm_rows(values, gain_row):
+    center = values - jnp.mean(values, axis=-1, keepdims=True)
+    spread = jnp.mean(center * center, axis=-1, keepdims=True)
+    return center * lax.rsqrt(spread + EPSILON) * gain_row
+
+
+def stacked(pieces):
+    loaded = [piece[...] for piece in pieces]
+    return loaded[0] if len(loaded) == 1 else jnp.concatenate(loaded, axis=0)
+
+
+def qkv_kernel(count, place, *refs):
+    first, second = refs[:count], refs[count : 2 * count]
+    table, gain, weight = refs[2 * count : 2 * count + 3]
+    inputs_out, qkv_out, label_out = refs[-3:]
+    mine, other = stacked(first), stacked(second)
+    leads = place[1] == 0
+    ahead = jnp.where(leads, mine, other)
+    behind = jnp.where(leads, other, mine)
+    both = jnp.concatenate([ahead, behind], axis=0)
+    inputs_out[...] = both[:, :D]
+    label_out[...] = both[:, D:]
+    labels = both[:, D:].astype(jnp.float32)
+    normed = norm_rows(both[:, :D].astype(jnp.float32), gain[...]).astype(jnp.bfloat16)
+    columns = jnp.dot(normed, weight[...], preferred_element_type=jnp.float32)
+    lane = lax.broadcasted_iota(jnp.int32, labels.shape, 1)
+    numbers = lane.astype(jnp.float32)
+    hot = (numbers == labels[:, 1:2]) | (numbers == labels[:, 2:3] + POSITIONS)
+    looked = jnp.dot(
+        jnp.where(hot, 1.0, 0.0).astype(jnp.bfloat16), table[...], preferred_element_type=jnp.float32
+    )
+    cosine = looked[:, :LANES] + looked[:, LANES : 2 * LANES]
+    sine = looked[:, 2 * LANES : 3 * LANES] + looked[:, 3 * LANES :]
+    first_head = lane < HD // 2
+
+    def turn(start):
+        a = columns[:, start : start + LANES]
+        b = columns[:, start + LANES : start + 2 * LANES]
+        return a * cosine - b * sine, b * cosine + a * sine
+
+    query_a, query_b = turn(0)
+    key_a, key_b = turn(2 * LANES)
+    zero = jnp.zeros_like(key_a)
+    parts = [
+        query_a,
+        query_b,
+        jnp.where(first_head, key_a, zero),
+        jnp.where(first_head, key_b, zero),
+        jnp.where(first_head, zero, key_a),
+        jnp.where(first_head, zero, key_b),
+    ]
+    values_part = columns[:, 4 * LANES :]
+    wide = lax.broadcasted_iota(jnp.int32, values_part.shape, 1)
+    ones = jnp.where(wide == 2 * HD, 1.0, 0.0)
+    parts.append(jnp.where(wide < HD, values_part, ones))
+    parts.append(jnp.where((wide >= HD) & (wide < 2 * HD), values_part, ones))
+    qkv_out[...] = jnp.concatenate(parts, axis=1).astype(jnp.bfloat16)
+
+
+def qkv_call(place, first, second, table, gain, weight, earlier, total):
+    rows = 2 * sum(piece.shape[0] for piece in first)
+    whole = lambda shape: pl.BlockSpec(shape, lambda i, place: (0,) * len(shape))
+    block = lambda width: pl.BlockSpec((rows, width), lambda i, place: (place[0], 0))
+    widths = (D, 10 * LANES, LANES)
+    operands = [*first, *second, table, gain, weight]
+    return pl.pallas_call(
+        functools.partial(qkv_kernel, len(first)),
+        grid_spec=pltpu.PrefetchScalarGridSpec(
+            num_scalar_prefetch=1,
+            grid=(1,),
+            in_specs=[whole(one.shape) for one in operands]
+            + [pl.BlockSpec(memory_space=pl.ANY)] * len(earlier),
+            out_specs=[block(width) for width in widths],
+        ),
+        out_shape=[jax.ShapeDtypeStruct((total, width), jnp.bfloat16) for width in widths],
+        input_output_aliases={1 + len(operands) + i: i for i in range(len(earlier))},
+        compiler_params=pltpu.CompilerParams(vmem_limit_bytes=24 << 20),
+        cost_estimate=pl.CostEstimate(
+            flops=2 * rows * D * weight.shape[1],
+            bytes_accessed=2 * (rows * 4 * D + weight.size),
+            transcendentals=rows,
+        ),
+        name="norm_qkv",
+    )(place, *operands, *earlier)
+
+
+def segment_row(labels):
+    pick = jnp.where(lax.broadcasted_iota(jnp.int32, (8, LANES), 1) == 0, 1.0, 0.0)
+    return lax.dot_general(
+        pick.astype(jnp.bfloat16),
+        labels,
+        (((1,), (1,)), ((), ())),
+        preferred_element_type=jnp.float32,
+    )
+
+
+def attention_kernel(start, owners, labels, block, *refs):
+    out, *rest = refs
+    scores, high, rows_scratch = rest[-3:]
+    rows = high.shape[1]
+    total = block.shape[0]
+    factor = HD**-0.5 * float(np.log2(np.e))
+    segments = segment_row(labels[...])
+    for step in range(total // BLOCK):
+        rows_scratch[step] = segments[:, step * BLOCK : (step + 1) * BLOCK]
+    own = labels[start : start + rows, :1].astype(jnp.float32)
+    lowest, largest = jnp.min(own), jnp.max(own)
+    one_row = segments[:1]
+    begin = jnp.sum(jnp.where(one_row < lowest, 1, 0)) // BLOCK
+    end = (jnp.sum(jnp.where(one_row <= largest, 1, 0)) + BLOCK - 1) // BLOCK
+    queries = block[start : start + rows, : 2 * LANES]
+    own = jnp.broadcast_to(own, (rows, LANES))
+    high[...] = jnp.full_like(high, NEGATIVE)
+
+    def score(step, carry):
+        at = pl.ds(pl.multiple_of(step * BLOCK, BLOCK), BLOCK)
+        theirs = rows_scratch[step, :1]
+        same = jnp.concatenate([own == theirs[:, :LANES], own == theirs[:, LANES:]], axis=1)
+        for head in range(2):
+            keys = block[at, (2 + 2 * head) * LANES : (4 + 2 * head) * LANES]
+            values = lax.dot_general(
+                queries, keys, (((1,), (1,)), ((), ())), preferred_element_type=jnp.float32
+            )
+            values = jnp.where(same, values, NEGATIVE)
+            scores[head, step] = values
+            high[head] = jnp.maximum(
+                high[head], jnp.maximum(values[:, :LANES], values[:, LANES:])
+            )
+        return carry
+
+    lax.fori_loop(begin, end, score, 0)
+    highest = [jnp.max(high[head], axis=-1, keepdims=True) for head in range(2)]
+
+    def weigh(step, carry):
+        at = pl.ds(pl.multiple_of(step * BLOCK, BLOCK), BLOCK)
+        sums = []
+        for head in range(2):
+            weights = jnp.exp2((scores[head, step] - highest[head]) * factor)
+            values = block[at, (6 + 2 * head) * LANES : (8 + 2 * head) * LANES]
+            sums.append(
+                carry[head]
+                + jnp.dot(weights.astype(jnp.bfloat16), values, preferred_element_type=jnp.float32)
+            )
+        return tuple(sums)
+
+    zero = jnp.zeros((rows, 2 * LANES), jnp.float32)
+    sums = lax.fori_loop(begin, end, weigh, (zero, zero))
+    acc = sum(one / one[:, 2 * HD : 2 * HD + 1] for one in sums)
+    out[:rows] = acc[:, :LANES].astype(jnp.bfloat16)
+    half = rows // 2
+    low, up = acc[:half, LANES:], acc[half:, LANES:]
+    lane = lax.broadcasted_iota(jnp.int32, low.shape, 1)
+    tail = 2 * HD - LANES
+    packed = jnp.where(lane < tail, low, jnp.where(lane < 2 * tail, pltpu.roll(up, tail, 1), 0.0))
+    out[rows:] = packed.astype(jnp.bfloat16)
+
+    if len(rest) > 3:
+        note = rest[0]
+        row = lax.broadcasted_iota(jnp.int32, note.shape, 0)
+        lane = lax.broadcasted_iota(jnp.int32, note.shape, 1)
+        found = jnp.zeros(note.shape, jnp.float32)
+        for image in range(owners.shape[0]):
+            below = jnp.sum(jnp.where(one_row < image, 0.25, 0.0), axis=1, keepdims=True)
+            inside = jnp.sum(jnp.where(one_row == image, 0.25, 0.0), axis=1, keepdims=True)
+            here = row == owners[image]
+            for place, number in enumerate((below, inside)):
+                upper = jnp.floor(number * (1.0 / 16))
+                found = jnp.where(here & (lane == 2 * place), upper, found)
+                found = jnp.where(here & (lane == 2 * place + 1), number - 16 * upper, found)
+        note[...] = found.astype(jnp.bfloat16)
+
+
+def attention_call(start, rows, owners, labels, block, noted):
+    total = block.shape[0]
+    vmem = pl.BlockSpec(memory_space=pltpu.VMEM)
+    shapes = [jax.ShapeDtypeStruct((rows + rows // 2, LANES), jnp.bfloat16)]
+    if noted:
+        shapes.append(jax.ShapeDtypeStruct((16, LANES), jnp.bfloat16))
+    return pl.pallas_call(
+        functools.partial(attention_kernel, start),
+        in_specs=[pl.BlockSpec(memory_space=pltpu.SMEM), vmem, vmem],
+        out_specs=[vmem] * len(shapes),
+        out_shape=shapes,
+        scratch_shapes=[
+            pltpu.VMEM((2, total // BLOCK, rows, BLOCK), jnp.float32),
+            pltpu.VMEM((2, rows, LANES), jnp.float32),
+            pltpu.VMEM((total // BLOCK, 8, BLOCK), jnp.float32),
+        ],
+        compiler_params=pltpu.CompilerParams(vmem_limit_bytes=28 << 20),
+        cost_estimate=pl.CostEstimate(
+            flops=4 * rows * total * 2 * LANES,
+            bytes_accessed=2 * block.size,
+            transcendentals=rows * total,
+        ),
+        name="attention",
+    )(owners, labels, block)
+
+
+def order_kernel(shards, ids, weight, out, sems):
+    rest = 2 * HD - LANES
+    out[shards * LANES :] = jnp.zeros((shards // 2 * LANES, D), jnp.bfloat16)
+    copies = []
+    for place in range(shards):
+        start = pl.multiple_of(ids[place] * (2 * HD), 16)
+        to = (shards + place // 2) * LANES + place % 2 * rest
+        copies.append((pl.ds(start, LANES), pl.ds(place * LANES, LANES)))
+        copies.append((pl.ds(start + LANES, rest), pl.ds(to, rest)))
+    copies = [
+        pltpu.make_async_copy(weight.at[source, :], out.at[target, :], sems.at[i])
+        for i, (source, target) in enumerate(copies)
+    ]
+    for copy in copies:
+        copy.start()
+    for copy in copies:
+        copy.wait()
+
+
+def order_call(ids, weight):
+    shards = ids.shape[0]
+    shape = (shards * LANES * 3 // 2, D)
+    return pl.pallas_call(
+        functools.partial(order_kernel, shards),
+        in_specs=[
+            pl.BlockSpec(memory_space=pltpu.SMEM),
+            pl.BlockSpec(memory_space=pl.ANY),
+        ],
+        out_specs=pl.BlockSpec(memory_space=pltpu.VMEM),
+        out_shape=jax.ShapeDtypeStruct(shape, jnp.bfloat16),
+        scratch_shapes=[pltpu.SemaphoreType.DMA((2 * shards,))],
+        compiler_params=pltpu.CompilerParams(vmem_limit_bytes=16 << 20),
+        cost_estimate=pl.CostEstimate(flops=0, bytes_accessed=4 * weight.size, transcendentals=0),
+        name="order_rows",
+    )(ids, weight)
+
+
+def merge_kernel(counts, inputs, weight, gain, merge_weight, bias, note, *refs):
+    pieces = refs[: sum(counts)]
+    out, state, merge, merge_sem = refs[sum(counts) :]
+    merge_copy = pltpu.make_async_copy(merge_weight, merge, merge_sem)
+    merge_copy.start()
+    rows = inputs.shape[0]
+    half = rows // 2
+    rest = 2 * HD - LANES
+    sources, at = [], 0
+    for count in counts:
+        sources.append(stacked(pieces[at : at + count]))
+        at += count
+    shards = len(sources)
+    lane = lax.broadcasted_iota(jnp.int32, (half, LANES), 1)
+    for part in range(2):
+        token = slice(part * half, (part + 1) * half)
+        lined = [source[token, :] for source in sources]
+        for pair in range(shards // 2):
+            mine = sources[2 * pair][rows:, :].astype(jnp.float32)
+            other = sources[2 * pair + 1][rows:, :].astype(jnp.float32)
+            if part == 0:
+                other = pltpu.roll(other, rest, 1)
+            else:
+                mine = pltpu.roll(mine, LANES - rest, 1)
+            lined.append(jnp.where(lane < rest, mine, other).astype(jnp.bfloat16))
+        mixed = jnp.dot(
+            jnp.concatenate(lined, axis=1), weight[...], preferred_element_type=jnp.float32
+        )
+        normed = norm_rows(inputs[token, :].astype(jnp.float32) + mixed, gain[...])
+        for column in range(D // LANES):
+            state[column, token, :] = normed[:, column * LANES : (column + 1) * LANES]
+    groups = rows // 4
+    total = bias[...]
+    merge_copy.wait()
+    for quadrant in range(4):
+        tokens = jnp.concatenate(
+            [
+                state[column, pl.ds(quadrant, groups, stride=4), :].astype(jnp.bfloat16)
+                for column in range(D // LANES)
+            ],
+            axis=1,
+        )
+        total = total + lax.dot_general(
+            tokens,
+            merge[:, quadrant * D : (quadrant + 1) * D],
+            (((1,), (1,)), ((), ())),
+            preferred_element_type=jnp.float32,
+        )
+    whole = total.shape[1] // LANES
+    for column in range(whole):
+        out[column * groups : (column + 1) * groups, :] = total[
+            :, column * LANES : (column + 1) * LANES
+        ].astype(jnp.bfloat16)
+    low = total[: groups // 2, whole * LANES :]
+    up = total[groups // 2 :, whole * LANES :]
+    end = whole * groups + groups // 2
+    out[whole * groups : end, :] = jnp.concatenate([low, up], axis=1).astype(jnp.bfloat16)
+    out[end:, :] = note[...]
+
+
+def merge_call(start, rows, sources, inputs, weight, gain, merge_weight, bias, note):
+    groups = rows // 4
+    width = merge_weight.shape[0]
+    pieces = [piece for source in sources for piece in source]
+    fixed = lambda shape: pl.BlockSpec(shape, lambda i: (0,) * len(shape))
+    out_shape = (groups * width // LANES + 16, LANES)
+    operands = [inputs, weight, gain, merge_weight, bias, note, *pieces]
+    specs = [fixed(one.shape) for one in operands]
+    specs[0] = pl.BlockSpec((rows, D), lambda i: (start // rows, 0))
+    specs[3] = pl.BlockSpec(memory_space=pl.ANY)
+    return pl.pallas_call(
+        functools.partial(merge_kernel, [len(source) for source in sources]),
+        grid=(1,),
+        in_specs=specs,
+        out_specs=fixed(out_shape),
+        scratch_shapes=[
+            pltpu.VMEM((D // LANES, rows, LANES), jnp.float32),
+            pltpu.VMEM(merge_weight.shape, jnp.bfloat16),
+            pltpu.SemaphoreType.DMA,
+        ],
+        out_shape=jax.ShapeDtypeStruct(out_shape, jnp.bfloat16),
+        compiler_params=pltpu.CompilerParams(vmem_limit_bytes=36 << 20),
+        cost_estimate=pl.CostEstimate(
+            flops=2 * rows * D * D + 2 * groups * merge_weight.size,
+            bytes_accessed=2 * (D * D + merge_weight.size + 3 * rows * D),
+            transcendentals=rows,
+        ),
+        name="out_merge",
+    )(*operands)
+
+
+def select_kernel(packs, offsets, groups_each, me, *refs):
+    parts, out = refs[:-1], refs[-1]
+    most, width = out.shape[1:]
+    whole = width // LANES
+    middle = LANES // 2
+    chunks = len(groups_each)
+    for number, offset in enumerate(offsets):
+        source = parts[number * chunks : (number + 1) * chunks]
+        target = me[0] + offset
+
+        @pl.when((target >= 0) & (target < packs))
+        def _(source=source, target=target):
+            sums = [None] * (whole + 2)
+            base = 0
+            for part, groups in zip(source, groups_each):
+                half = groups // 2
+                if base == 0:
+                    end = whole * groups + half
+                    notes = part[end:, :].astype(jnp.float32)
+                    mine = lax.broadcasted_iota(jnp.int32, notes.shape, 0) == me[0]
+                    note = jnp.sum(jnp.where(mine, notes, 0.0), axis=0, keepdims=True)
+                    first = (16.0 * note[:, :1] + note[:, 1:2]).astype(jnp.int32)
+                    length = (16.0 * note[:, 2:3] + note[:, 3:4]).astype(jnp.int32)
+                slot = lax.broadcasted_iota(jnp.int32, (most, groups), 0)
+                row = lax.broadcasted_iota(jnp.int32, (most, groups), 1) + base
+                chosen = (row == slot + first) & (slot < length)
+                chosen = jnp.where(chosen, 1.0, 0.0).astype(jnp.bfloat16)
+                product = lambda a, b: jnp.dot(a, b, preferred_element_type=jnp.float32)
+                terms = [
+                    product(chosen, part[column * groups : (column + 1) * groups, :])
+                    for column in range(whole)
+                ]
+                packed = part[whole * groups : whole * groups + half, :]
+                terms.append(product(chosen[:, :half], packed))
+                terms.append(product(chosen[:, half:], packed))
+                sums = [
+                    term if kept is None else kept + term for kept, term in zip(sums, terms)
+                ]
+                base += groups
+            for column in range(whole):
+                out[target, :, column * LANES : (column + 1) * LANES] = sums[column].astype(
+                    jnp.bfloat16
+                )
+            last = sums[whole] + pltpu.roll(sums[whole + 1], middle, 1)
+            out[target, :, whole * LANES :] = last[:, :middle].astype(jnp.bfloat16)
+
+
+def select_call(me, gathered, groups_each, packs, most, width):
+    offsets = [offset for offset, _ in gathered[0]]
+    parts = [chunk[number][1] for number in range(len(offsets)) for chunk in gathered]
+    vmem = pl.BlockSpec(memory_space=pltpu.VMEM)
+    return pl.pallas_call(
+        functools.partial(select_kernel, packs, offsets, groups_each),
+        in_specs=[pl.BlockSpec(memory_space=pltpu.SMEM)] + [vmem] * len(parts),
+        out_specs=vmem,
+        out_shape=jax.ShapeDtypeStruct((packs, most, width), jnp.bfloat16),
+        compiler_params=pltpu.CompilerParams(vmem_limit_bytes=16 << 20),
+        cost_estimate=pl.CostEstimate(
+            flops=4 * packs * most * sum(groups_each) * width,
+            bytes_accessed=4 * packs * most * width,
+            transcendentals=0,
+        ),
+        name="select_rows",
+    )(me, *parts)
+
+
+def send_seq(value, flip):
+    size = lax.axis_size("seq")
+    return lax.ppermute(value, "seq", [(i, i ^ flip) for i in range(size)])
+
+
+def gather_seq(value):
+    half = value.shape[0] // 2
+    near = [send_seq(value, 2), send_seq(value, 4)]
+    own_swap = send_seq(value, 1)
+    far = [send_seq(near[0][:half], 4), send_seq(near[1][half:], 2)]
+    swapped = [send_seq(one, 1) for one in near + far]
+    return [
+        ([value], [own_swap]),
+        ([near[0]], [swapped[0]]),
+        ([near[1]], [swapped[1]]),
+        (far, swapped[2:]),
+    ]
+
+
+def gather_pack(value):
+    size = lax.axis_size("pack")
+    found = [(0, value)]
+    for direction in (1, -1):
+        moving = value
+        for step in range(1, size):
+            ahead = [(z, z + 1) for z in range(step - 1, size - 1)]
+            if direction < 0:
+                ahead = [(size - 1 - a, size - 1 - b) for a, b in ahead]
+            moving = lax.ppermute(moving, "pack", ahead)
+            found.append((-direction * step, moving))
+    return found
+
+
+def weight_order(heads_here):
+    quarter = HD // 4
+    order = -np.ones((6 * LANES,), np.int32)
+    for head in range(heads_here):
+        base = head * 3 * HD
+        for kind in range(2):
+            for half in range(2):
+                for letter in range(2):
+                    target = (2 * kind + letter) * LANES + head * (HD // 2) + half * quarter
+                    source = base + kind * HD + half * (HD // 2) + letter * quarter
+                    order[target : target + quarter] = np.arange(source, source + quarter)
+        target = 4 * LANES + head * HD
+        order[target : target + HD] = np.arange(base + 2 * HD, base + 3 * HD)
+    return order
+
+
+def angle_table(heads_here):
+    quarter = HD // 4
+    frequency = (10000.0 ** (-np.arange(quarter) / quarter)).astype(np.float32)
+    angles = np.arange(POSITIONS, dtype=np.float32)[:, None] * frequency[None, :]
+    pieces = []
+    for function in (np.cos, np.sin):
+        exact = np.zeros((2 * POSITIONS, LANES), np.float64)
+        for head in range(heads_here):
+            for half in range(2):
+                lane = head * (HD // 2) + half * quarter
+                rows = slice(half * POSITIONS, (half + 1) * POSITIONS)
+                exact[rows, lane : lane + quarter] = function(angles.astype(np.float64))
+        upper = exact.astype(jnp.bfloat16)
+        pieces += [upper, (exact - upper.astype(np.float64)).astype(jnp.bfloat16)]
+    return np.concatenate(pieces, axis=1)
+
+
+def fast_local(
+    patches,
+    patch_mask,
+    mask_embed,
+    norm_gain,
+    qkv_weight,
+    segment_ids,
+    patch_rows,
+    patch_column,
+    out_weight,
+    merge_gain,
+    merge_weight,
+    merge_bias,
+    image_owner,
+):
+    local_rows = patches.shape[1]
+    shards = lax.axis_size("seq")
+    packs = lax.axis_size("pack")
+    heads_here = HEADS // shards
+    images = image_owner.shape[1]
+    total = local_rows * shards
+    me = lax.axis_index("seq").astype(jnp.int32)
+    pack = lax.axis_index("pack").astype(jnp.int32)
+
+    tokens = jnp.where(patch_mask[0][:, None] == 1, mask_embed[None, :], patches[0])
+    labels = jnp.stack([segment_ids[0], patch_rows[0], patch_column[0]], axis=1)
+    labels = jnp.pad(labels.astype(jnp.bfloat16), ((0, 0), (0, LANES - labels.shape[1])))
+    shares = gather_seq(jnp.concatenate([tokens, labels], axis=1))
+
+    order = jnp.asarray(weight_order(heads_here))
+    spread = (jnp.arange(qkv_weight.shape[1])[:, None] == order[None, :]).astype(jnp.bfloat16)
+    weight = jnp.dot(qkv_weight, spread, preferred_element_type=jnp.float32).astype(jnp.bfloat16)
+    table = jnp.asarray(angle_table(heads_here))
+    gain = norm_gain.astype(jnp.float32)[None, :]
+    merge_gain_row = merge_gain.astype(jnp.float32)[None, :]
+    bias = merge_bias.astype(jnp.float32)[None, :]
+    ids = jnp.stack([me ^ place for place in range(shards)])
+    ordered = order_call(ids, out_weight)
+
+    buffers = ()
+    for place, (first, second) in enumerate(shares):
+        where = jnp.stack([(me // 2) ^ place, me % 2])
+        buffers = qkv_call(where, first, second, table, gain, weight, buffers, total)
+    inputs, block, labels = buffers
+
+    starts = [sum(CHUNKS[:number]) for number in range(len(CHUNKS))]
+    attended, note = [], None
+    for start, rows in zip(starts, CHUNKS):
+        made = attention_call(start, rows, image_owner[0], labels, block, note is None)
+        note = made[1] if note is None else note
+        attended.append(gather_seq(made[0]))
+    gathered = []
+    for start, rows, shares in zip(starts, CHUNKS, attended):
+        sources = [pieces for share in shares for pieces in share]
+        projected = merge_call(
+            start, rows, sources, inputs, ordered, merge_gain_row, merge_weight.T, bias, note
+        )
+        gathered.append(gather_pack(projected))
+    most = 2 * (total // 4) // images
+    groups_each = [rows // 4 for rows in CHUNKS]
+    return select_call(pack[None], gathered, groups_each, packs, most, merge_weight.shape[1])[None]
+
+
+def local(*arguments):
+    patches, weight = arguments[0], arguments[4]
+    shards = lax.axis_size("seq")
+    fits = shards == 8 and HEADS // shards == 2 and weight.shape[1] == 6 * HD
+    fits = fits and patches.shape[1] * shards == sum(CHUNKS)
+    return fast_local(*arguments) if fits else general_local(*arguments)
+
+
 def solution(mesh):
     placed = (
         P("pack", "seq", None),

time: 199 us -> 147 us (0.74)
  Pallas kernels: 0 us -> 46.6 us
  starting transfers between devices: 3.75 us -> 41.6 us
  matrix products: 38.7 us -> 1.92 us
  blocking collectives: 35.5 us -> 0 us
  waiting for transfers between devices: 74.3 us -> 44 us
  between operations: 13.8 us -> 0.49 us
  local copies, waits for them, and re-layouts: 19.1 us -> 9.45 us
  other arithmetic: 13.2 us -> 3.76 us
    all_gather x2 -> x0, waiting for transfers between devices: 61.8 us -> none  [the longest x1 35.5 us: local(): lax.all_gather(merged, 'seq', axis=0, tiled=True)]
    pallas_call x0 -> x10, Pallas kernels: none -> 46.6 us  [the longest x2 16.8 us: merge_call(): pl.pallas_call(functools.partial(merge_kernel, [len(source) for source in...]
    ppermute x0 -> x39, waiting for transfers between devices: none -> 44 us  [the longest x27 26.6 us: send_seq(): return lax.ppermute(value, 'seq', [(i, i ^ flip) for i in range(size)])]
    ppermute x0 -> x39, starting transfers between devices: none -> 41.6 us  [the longest x12 23.5 us: gather_pack(): moving = lax.ppermute(moving, 'pack', ahead)]
    dot_general x6 -> x1, matrix products: 28.4 us -> 1.92 us  [fast_local(): jnp.dot(qkv_weight, spread, preferred_element_type=jnp.float32)]
    all_to_all x1 -> x0, blocking collectives: 24.9 us -> none  [local(): lax.all_to_all(outgoing, 'pack', split_axis=0, concat_axis=0, tiled=True)]
    all_to_all x1 -> x0, waiting for transfers between devices: 12.5 us -> none  [local(): lax.all_to_all(result, 'seq', split_axis=0, concat_axis=1, tiled=True)]
    all_gather x1 -> x0, blocking collectives: 10.5 us -> none  [local(): lax.all_gather(jnp.stack([segment_ids[0], patch_rows[0], patch_column[0]]...]
  transfers between devices with their start and end apart: 3 -> 39, of which waited for: 3 -> 15; matrix products, arithmetic and copies ran while one was open for 2% -> 2% of each run, Pallas kernels for 0% -> 23%
where the time goes in v2:
time: 147 us; the launch traced here: 148 us
  Pallas kernels  46.6 us (32%)
  waiting for transfers between devices  44 us (30%)
  starting transfers between devices  41.6 us (28%)
  local copies, waits for them, and re-layouts  9.45 us (6%)
  other arithmetic  3.76 us (3%)
  matrix products  1.92 us (1%)
    ppermute x27, waiting for transfers between devices, send_seq(): return lax.ppermute(value, 'seq', [(i, i ^ flip) for i in range(size)])  26.6 us
    ppermute x12, starting transfers between devices, gather_pack(): moving = lax.ppermute(moving, 'pack', ahead)  23.5 us
    ppermute x27, starting transfers between devices, send_seq(): return lax.ppermute(value, 'seq', [(i, i ^ flip) for i in range(size)])  18.2 us
    ppermute x12, waiting for transfers between devices, gather_pack(): moving = lax.ppermute(moving, 'pack', ahead)  17.4 us
    pallas_call x2, Pallas kernels, merge_call(): pl.pallas_call(functools.partial(merge_kernel, [len(source) for source in...  16.8 us
    pallas_call x4, Pallas kernels, qkv_call(): pl.pallas_call(functools.partial(qkv_kernel, len(first)), grid_spec=pltpu...  12 us
    pallas_call x2, Pallas kernels, attention_call(): pl.pallas_call(functools.partial(attention_kernel, start), in_specs=[pl.B...  9.9 us
    unnamed x34, local copies, waits for them, and re-layouts  8.45 us
  transfers between devices with their start and end apart: 39, of which 15 were waited for; matrix products, arithmetic and copies ran while one was open for 2% of the time, Pallas kernels for 23%

profile of v2, /device:TPU:0, one launch (start us, length us, event | category | flops | bytes accessed | tf_op | source)
XLA Modules:
  0.0 147.8 jit_solution(5073786341938499794)
XLA Ops:
  3.6 3.0 %collective-permute-start = (bf16[192,1536]{1,0:T(8,128)(2,1)S(1)}, bf16[192,1536]{1,0:T(8,128)(2,1)S(1)}, u32[]{:S(2)}, u32[]{:S(2)}) collective-permute-start(bf16[192,1536]{1,0:T(8,128)(2,1)S(1)} %fusion.3.refs_0_), channel_id=1, source_target_pairs={{0,8},{4,12},{8,0},{12,4},{16,24},{20,28},{24,16},{28,20},{1,9},{5... | collective-permute-start | bytes 1769480 | tf_op jit(solution)/shard_map/ppermute | solution.py:550
  6.6 1.5 %collective-permute-start.2 = (bf16[192,1536]{1,0:T(8,128)(2,1)S(1)}, bf16[192,1536]{1,0:T(8,128)(2,1)S(1)}, u32[]{:S(2)}, u32[]{:S(2)}) collective-permute-start(bf16[192,1536]{1,0:T(8,128)(2,1)S(1)} %fusion.3.refs_0_), channel_id=1, source_target_pairs={{0,16},{4,20},{8,24},{12,28},{16,0},{20,4},{24,8},{28,12},{1,17},{... | collective-permute-start | bytes 1769480 | tf_op jit(solution)/shard_map/ppermute | solution.py:550
  8.3 11.7 %collective-permute-done.refs_0_ = bf16[192,1536]{1,0:T(8,128)(2,1)S(1)} collective-permute-done((bf16[192,1536]{1,0:T(8,128)(2,1)S(1)}, bf16[192,1536]{1,0:T(8,128)(2,1)S(1)}, u32[]{:S(2)}, u32[]{:S(2)}) %collective-permute-start) | collective-permute-done | bytes 589856 | tf_op jit(solution)/shard_map/ppermute | solution.py:550
  20.1 1.8 %collective-permute-start.1 = (bf16[96,1536]{1,0:T(8,128)(2,1)S(1)}, bf16[96,1536]{1,0:T(8,128)(2,1)S(1)}, u32[]{:S(2)}, u32[]{:S(2)}) collective-permute-start(bf16[96,1536]{1,0:T(8,128)(2,1)S(1)} %slice.24), channel_id=1, source_target_pairs={{0,16},{4,20},{8,24},{12,28},{16,0},{20,4},{24,8},{28,12},{1,17},{... | collective-permute-start | bytes 884744 | tf_op jit(solution)/shard_map/ppermute | solution.py:550
  22.0 1.6 %collective-permute-start.3 = (bf16[96,1536]{1,0:T(8,128)(2,1)S(1)}, bf16[96,1536]{1,0:T(8,128)(2,1)S(1)}, u32[]{:S(2)}, u32[]{:S(2)}) collective-permute-start(bf16[96,1536]{1,0:T(8,128)(2,1)S(1)} %slice.25), channel_id=1, source_target_pairs={{0,8},{4,12},{8,0},{12,4},{16,24},{20,28},{24,16},{28,20},{1,9},{5... | collective-permute-start | bytes 884744 | tf_op jit(solution)/shard_map/ppermute | solution.py:550
  23.5 1.9 %fusion.refs_4_.refs_6_ = bf16[1408,768]{1,0:T(8,128)(2,1)S(1)} fusion(bf16[1408,528]{0,1:T(8,128)(2,1)S(1)} %copy-done, s32[768]{0:T(1024)S(1)} %copy-done.14), kind=kOutput, calls=%fused_computation.1 | convolution fusion | flops 1143386112 | bytes 3652608 | tf_op jit(solution)/shard_map/dot_general | solution.py:645
  25.5 4.1 %collective-permute-done.1.refs_0_ = bf16[96,1536]{1,0:T(8,128)(2,1)S(1)} collective-permute-done((bf16[96,1536]{1,0:T(8,128)(2,1)S(1)}, bf16[96,1536]{1,0:T(8,128)(2,1)S(1)}, u32[]{:S(2)}, u32[]{:S(2)}) %collective-permute-start.1) | collective-permute-done | bytes 294944 | tf_op jit(solution)/shard_map/ppermute | solution.py:550
  29.6 1.6 %collective-permute-done.3.refs_1_ = bf16[96,1536]{1,0:T(8,128)(2,1)S(1)} collective-permute-done((bf16[96,1536]{1,0:T(8,128)(2,1)S(1)}, bf16[96,1536]{1,0:T(8,128)(2,1)S(1)}, u32[]{:S(2)}, u32[]{:S(2)}) %collective-permute-start.3) | collective-permute-done | bytes 294944 | tf_op jit(solution)/shard_map/ppermute | solution.py:550
  31.2 3.5 %norm_qkv.4 = (bf16[1536,1408]{1,0:T(8,128)(2,1)S(1)}, bf16[1536,1280]{1,0:T(8,128)(2,1)S(1)}, bf16[1536,128]{1,0:T(8,128)(2,1)S(1)}) custom-call(s32[2]{0:T(128)S(1)} %pad_add_fusion.3.place, bf16[192,1536]{1,0:T(8,128)(2,1)S(1)} %fusion.3.refs_0_, bf16[192,1536]{1,0:T(8,128)(2,1)} %collective-permute-done.8.refs_1_, bf16[128,512]{1,0:T(8,128)(2,1)S(1)} %copy-done.5, ...), custom_call_target="tpu_custom_call" | custom-call | flops 830472192 | bytes 6488064 | tf_op jit(solution)/shard_map/norm_qkv/pallas_call | solution.py:221
  34.8 3.6 %norm_qkv.5 = (bf16[1536,1408]{1,0:T(8,128)(2,1)S(1)}, bf16[1536,1280]{1,0:T(8,128)(2,1)S(1)}, bf16[1536,128]{1,0:T(8,128)(2,1)S(1)}) custom-call(s32[2]{0:T(128)S(1)} %pad_add_fusion.2.place, bf16[192,1536]{1,0:T(8,128)(2,1)S(1)} %collective-permute-done.refs_0_, ...), custom_call_target="tpu_custom_call", output_to_operand_aliasing={{0}: (6, {}), {1}: (7, {}), {2}: (8, {})} | custom-call | flops 830472192 | bytes 6488064 | tf_op jit(solution)/shard_map/norm_qkv/pallas_call | solution.py:221
  38.4 2.4 %norm_qkv.6 = (bf16[1536,1408]{1,0:T(8,128)(2,1)S(1)}, bf16[1536,1280]{1,0:T(8,128)(2,1)S(1)}, bf16[1536,128]{1,0:T(8,128)(2,1)S(1)}) custom-call(s32[2]{0:T(128)S(1)} %pad_add_fusion.1.place, bf16[192,1536]{1,0:T(8,128)(2,1)S(1)} %collective-permute-done.2.refs_0_, ...), custom_call_target="tpu_custom_call", output_to_operand_aliasing={{0}: (6, {}), {1}: (7, {}), {2}: (8, {})} | custom-call | flops 830472192 | bytes 6488064 | tf_op jit(solution)/shard_map/norm_qkv/pallas_call | solution.py:221
  40.9 2.4 %norm_qkv.7 = (bf16[1536,1408]{1,0:T(8,128)(2,1)S(1)}, bf16[1536,1280]{1,0:T(8,128)(2,1)S(1)}, bf16[1536,128]{1,0:T(8,128)(2,1)S(1)}) custom-call(s32[2]{0:T(128)S(1)} %pad_add_fusion.place, bf16[96,1536]{1,0:T(8,128)(2,1)S(1)} %collective-permute-done.1.refs_0_, ...), custom_call_target="tpu_custom_call", output_to_operand_aliasing={{0}: (8, {}), {1}: (9, {}), {2}: (10, {})} | custom-call | flops 830472192 | bytes 6488064 | tf_op jit(solution)/shard_map/norm_qkv/pallas_call | solution.py:221
  43.3 5.0 %attention.3.refs_0_ = bf16[1152,128]{1,0:T(8,128)(2,1)S(1)} custom-call(s32[4]{0:T(128)S(1)} %bitcast.35, bf16[1536,128]{1,0:T(8,128)(2,1)S(1)} %get-tuple-element.29.labels, bf16[1536,1280]{1,0:T(8,128)(2,1)S(1)} %get-tuple-element.30.block), custom_call_target="tpu_custom_call" | custom-call | flops 1207959552 | bytes 3932160 | tf_op jit(solution)/shard_map/attention/pallas_call | solution.py:334
  48.4 1.6 %collective-permute-start.19 = (bf16[1152,128]{1,0:T(8,128)(2,1)S(1)}, bf16[1152,128]{1,0:T(8,128)(2,1)S(1)}, u32[]{:S(2)}, u32[]{:S(2)}) collective-permute-start(bf16[1152,128]{1,0:T(8,128)(2,1)S(1)} %attention.3.refs_0_), channel_id=1, source_target_pairs={{0,8},{4,12},{8,0},{12,4},{16,24},{20,28},{24,16},{28,20},{1,9},{5... | collective-permute-start | bytes 884744 | tf_op jit(solution)/shard_map/ppermute | solution.py:550
  50.7 4.9 %attention.2 = (bf16[1152,128]{1,0:T(8,128)(2,1)S(1)}, bf16[16,128]{1,0:T(8,128)(2,1)S(1)}) custom-call(s32[4]{0:T(128)S(1)} %bitcast.36, bf16[1536,128]{1,0:T(8,128)(2,1)S(1)} %get-tuple-element.29.labels, bf16[1536,1280]{1,0:T(8,128)(2,1)S(1)} %get-tuple-element.30.block), custom_call_target="tpu_custom_call" | custom-call | flops 1207959552 | bytes 3932160 | tf_op jit(solution)/shard_map/attention/pallas_call | solution.py:334
  59.1 5.2 %collective-permute-done.10.refs_2_ = bf16[1152,128]{1,0:T(8,128)(2,1)S(1)} collective-permute-done((bf16[1152,128]{1,0:T(8,128)(2,1)S(1)}, bf16[1152,128]{1,0:T(8,128)(2,1)S(1)}, u32[]{:S(2)}, u32[]{:S(2)}) %collective-permute-start.10) | collective-permute-done | bytes 294944 | tf_op jit(solution)/shard_map/ppermute | solution.py:550
  68.7 1.8 %collective-permute-start.15 = (bf16[576,128]{1,0:T(8,128)(2,1)}, bf16[576,128]{1,0:T(8,128)(2,1)}, u32[]{:S(2)}, u32[]{:S(2)}) collective-permute-start(bf16[576,128]{1,0:T(8,128)(2,1)} %slice.27), channel_id=1, source_target_pairs={{0,8},{4,12},{8,0},{12,4},{16,24},{20,28},{24,16},{28,20},{1,9},{5... | collective-permute-start | bytes 442376 | tf_op jit(solution)/shard_map/ppermute | solution.py:550
  72.7 2.1 %copy-done.4 = bf16[1408,1408]{1,0:T(8,128)(2,1)S(1)} copy-done((bf16[1408,1408]{1,0:T(8,128)(2,1)S(1)}, bf16[1408,1408]{1,0:T(8,128)(2,1)}, u32[]{:S(2)}) %copy-start.4) | copy-done | bytes 3964952
  74.8 3.4 %order_rows.1.weight = bf16[1536,1408]{1,0:T(8,128)(2,1)S(1)} custom-call(s32[8]{0:T(128)S(1)} %stack.79.ids, bf16[1408,1408]{1,0:T(8,128)(2,1)S(1)} %copy-done.4), custom_call_target="tpu_custom_call" | custom-call | bytes 7929856 | tf_op jit(solution)/shard_map/order_rows/pallas_call | solution.py:376
  79.8 2.2 %copy-done.2 = bf16[1536,1408]{1,0:T(8,128)(2,1)S(1)} copy-done((bf16[1536,1408]{1,0:T(8,128)(2,1)S(1)}, bf16[1536,1408]{1,0:T(8,128)(2,1)}, u32[]{:S(2)}) %copy-start.2) | copy-done | bytes 4325400
  82.1 2.4 %copy-done.3 = bf16[5632,448]{0,1:T(8,128)(2,1)S(1)} copy-done((bf16[5632,448]{0,1:T(8,128)(2,1)S(1)}, bf16[5632,448]{0,1:T(8,128)(2,1)}, u32[]{:S(2)}) %copy-start.3) | copy-done | bytes 5046296
  85.4 8.5 %out_merge.3.refs_1_ = bf16[688,128]{1,0:T(8,128)(2,1)S(1)} custom-call(bf16[1536,1408]{1,0:T(8,128)(2,1)S(1)} %copy-done.2, bf16[1536,1408]{1,0:T(8,128)(2,1)S(1)} %order_rows.1.weight, f32[1,1408]{1,0:T(1,128)S(1)} %reshape.12.gain, bf16[448,5632]{1,0:T(8,128)(2,1)S(1)} %bitcast.29, f32[1,448]{1,0:T(1,128)S(1)} %bitcast.33, ...), custom_call_target="tpu_custom_call" | custom-call | flops 4013948928 | bytes 15499264 | tf_op jit(solution)/shard_map/out_merge/pallas_call | solution.py:461
  94.0 7.0 %collective-permute-start.28 = (bf16[688,128]{1,0:T(8,128)(2,1)S(1)}, bf16[688,128]{1,0:T(8,128)(2,1)S(1)}, u32[]{:S(2)}, u32[]{:S(2)}) collective-permute-start(bf16[688,128]{1,0:T(8,128)(2,1)S(1)} %out_merge.3.refs_1_), channel_id=1, source_target_pairs={{0,1},{1,2},{2,3},{4,5},{5,6},{6,7},{8,9},{9,10},{10,11},{12,13},{... | collective-permute-start | bytes 528392 | tf_op jit(solution)/shard_map/ppermute | solution.py:576
  100.9 1.5 %collective-permute-start.34 = (bf16[688,128]{1,0:T(8,128)(2,1)S(1)}, bf16[688,128]{1,0:T(8,128)(2,1)S(1)}, u32[]{:S(2)}, u32[]{:S(2)}) collective-permute-start(bf16[688,128]{1,0:T(8,128)(2,1)S(1)} %out_merge.3.refs_1_), channel_id=1, source_target_pairs={{3,2},{2,1},{1,0},{7,6},{6,5},{5,4},{11,10},{10,9},{9,8},{15,14},{... | collective-permute-start | bytes 528392 | tf_op jit(solution)/shard_map/ppermute | solution.py:576
  102.5 8.3 %out_merge.2.refs_0_ = bf16[688,128]{1,0:T(8,128)(2,1)S(1)} custom-call(bf16[1536,1408]{1,0:T(8,128)(2,1)S(1)} %copy-done.2, bf16[1536,1408]{1,0:T(8,128)(2,1)S(1)} %order_rows.1.weight, f32[1,1408]{1,0:T(1,128)S(1)} %reshape.12.gain, bf16[448,5632]{1,0:T(8,128)(2,1)S(1)} %bitcast.32, f32[1,448]{1,0:T(1,128)S(1)} %bitcast.34, ...), custom_call_target="tpu_custom_call" | custom-call | flops 4013948928 | bytes 15499264 | tf_op jit(solution)/shard_map/out_merge/pallas_call | solution.py:461
  110.8 4.6 %collective-permute-start.27 = (bf16[688,128]{1,0:T(8,128)(2,1)S(1)}, bf16[688,128]{1,0:T(8,128)(2,1)S(1)}, u32[]{:S(2)}, u32[]{:S(2)}) collective-permute-start(bf16[688,128]{1,0:T(8,128)(2,1)S(1)} %out_merge.2.refs_0_), channel_id=1, source_target_pairs={{0,1},{1,2},{2,3},{4,5},{5,6},{6,7},{8,9},{9,10},{10,11},{12,13},{... | collective-permute-start | bytes 528392 | tf_op jit(solution)/shard_map/ppermute | solution.py:576
  119.4 3.5 %collective-permute-done.33.refs_8_ = bf16[688,128]{1,0:T(8,128)(2,1)S(1)} collective-permute-done((bf16[688,128]{1,0:T(8,128)(2,1)S(1)}, bf16[688,128]{1,0:T(8,128)(2,1)S(1)}, u32[]{:S(2)}, u32[]{:S(2)}) %collective-permute-start.33) | collective-permute-done | bytes 176160 | tf_op jit(solution)/shard_map/ppermute | solution.py:576
  125.5 2.6 %collective-permute-done.36.refs_11_ = bf16[688,128]{1,0:T(8,128)(2,1)S(1)} collective-permute-done((bf16[688,128]{1,0:T(8,128)(2,1)S(1)}, bf16[688,128]{1,0:T(8,128)(2,1)S(1)}, u32[]{:S(2)}, u32[]{:S(2)}) %collective-permute-start.36) | collective-permute-done | bytes 176160 | tf_op jit(solution)/shard_map/ppermute | solution.py:576
  130.8 5.1 %collective-permute-done.35.refs_10_ = bf16[688,128]{1,0:T(8,128)(2,1)S(1)} collective-permute-done((bf16[688,128]{1,0:T(8,128)(2,1)S(1)}, bf16[688,128]{1,0:T(8,128)(2,1)S(1)}, u32[]{:S(2)}, u32[]{:S(2)}) %collective-permute-start.35) | collective-permute-done | bytes 176160 | tf_op jit(solution)/shard_map/ppermute | solution.py:576
  137.1 2.6 %collective-permute-done.38.refs_13_ = bf16[688,128]{1,0:T(8,128)(2,1)} collective-permute-done((bf16[688,128]{1,0:T(8,128)(2,1)S(1)}, bf16[688,128]{1,0:T(8,128)(2,1)}, u32[]{:S(2)}, u32[]{:S(2)}) %collective-permute-start.38) | collective-permute-done | bytes 176160 | tf_op jit(solution)/shard_map/ppermute | solution.py:576
  139.7 3.6 %collective-permute-done.37.refs_12_ = bf16[688,128]{1,0:T(8,128)(2,1)} collective-permute-done((bf16[688,128]{1,0:T(8,128)(2,1)S(1)}, bf16[688,128]{1,0:T(8,128)(2,1)}, u32[]{:S(2)}, u32[]{:S(2)}) %collective-permute-start.37) | collective-permute-done | bytes 176160 | tf_op jit(solution)/shard_map/ppermute | solution.py:576
  143.3 4.5 %select_rows.1 = bf16[4,192,448]{2,1,0:T(8,128)(2,1)} custom-call(s32[1]{0:T(128)} %bitcast.me, bf16[688,128]{1,0:T(8,128)(2,1)S(1)} %out_merge.2.refs_0_, bf16[688,128]{1,0:T(8,128)(2,1)S(1)} %out_merge.3.refs_1_, bf16[688,128]{1,0:T(8,128)(2,1)S(1)} %collective-permute-done.27.refs_2_, bf16[688,128]{1,0:T(8,128)(2,1)S(1)} %collective-permute-done.28.refs_3_, ...), custom_call_target="tpu_custom_call" | custom-call | flops 528482304 | bytes 1376256 | tf_op jit(solution)/shard_map/select_rows/pallas_call | solution.py:533
  (113 shorter events, 27.9 us)
Async XLA Ops:
  3.6 16.3 %collective-permute-start = (bf16[192,1536]{1,0:T(8,128)(2,1)S(1)}, bf16[192,1536]{1,0:T(8,128)(2,1)S(1)}, u32[]{:S(2)}, u32[]{:S(2)}) collective-permute-start(bf16[192,1536]{1,0:T(8,128)(2,1)S(1)} %fusion.3.refs_0_), channel_id=1, source_target_pairs={{0,8},{4,12},{8,0},{12,4},{16,24},{20,28},{24,16},{28,20},{1,9},{5... | collective-permute-start | bytes 1769480 | tf_op jit(solution)/shard_map/ppermute | solution.py:550
  6.6 15.3 %collective-permute-start.2 = (bf16[192,1536]{1,0:T(8,128)(2,1)S(1)}, bf16[192,1536]{1,0:T(8,128)(2,1)S(1)}, u32[]{:S(2)}, u32[]{:S(2)}) collective-permute-start(bf16[192,1536]{1,0:T(8,128)(2,1)S(1)} %fusion.3.refs_0_), channel_id=1, source_target_pairs={{0,16},{4,20},{8,24},{12,28},{16,0},{20,4},{24,8},{28,12},{1,17},{... | collective-permute-start | bytes 1769480 | tf_op jit(solution)/shard_map/ppermute | solution.py:550
  8.2 23.1 %collective-permute-start.8 = (bf16[192,1536]{1,0:T(8,128)(2,1)S(1)}, bf16[192,1536]{1,0:T(8,128)(2,1)}, u32[]{:S(2)}, u32[]{:S(2)}) collective-permute-start(bf16[192,1536]{1,0:T(8,128)(2,1)S(1)} %fusion.3.refs_0_), channel_id=1, source_target_pairs={{0,4},{4,0},{8,12},{12,8},{16,20},{20,16},{24,28},{28,24},{1,5},{5... | collective-permute-start | bytes 1769480 | tf_op jit(solution)/shard_map/ppermute | solution.py:550
  20.0 14.8 %collective-permute-start.7 = (bf16[192,1536]{1,0:T(8,128)(2,1)S(1)}, bf16[192,1536]{1,0:T(8,128)(2,1)}, u32[]{:S(2)}, u32[]{:S(2)}) collective-permute-start(bf16[192,1536]{1,0:T(8,128)(2,1)S(1)} %collective-permute-done.refs_0_), channel_id=1, source_target_pairs={{0,4},{4,0},{8,12},{12,8},{16,20},{20,16},{24,28},{28,24},{1,5},{5... | collective-permute-start | bytes 1769480 | tf_op jit(solution)/shard_map/ppermute | solution.py:550
  20.1 9.5 %collective-permute-start.1 = (bf16[96,1536]{1,0:T(8,128)(2,1)S(1)}, bf16[96,1536]{1,0:T(8,128)(2,1)S(1)}, u32[]{:S(2)}, u32[]{:S(2)}) collective-permute-start(bf16[96,1536]{1,0:T(8,128)(2,1)S(1)} %slice.24), channel_id=1, source_target_pairs={{0,16},{4,20},{8,24},{12,28},{16,0},{20,4},{24,8},{28,12},{1,17},{... | collective-permute-start | bytes 884744 | tf_op jit(solution)/shard_map/ppermute | solution.py:550
  22.0 9.2 %collective-permute-start.3 = (bf16[96,1536]{1,0:T(8,128)(2,1)S(1)}, bf16[96,1536]{1,0:T(8,128)(2,1)S(1)}, u32[]{:S(2)}, u32[]{:S(2)}) collective-permute-start(bf16[96,1536]{1,0:T(8,128)(2,1)S(1)} %slice.25), channel_id=1, source_target_pairs={{0,8},{4,12},{8,0},{12,4},{16,24},{20,28},{24,16},{28,20},{1,9},{5... | collective-permute-start | bytes 884744 | tf_op jit(solution)/shard_map/ppermute | solution.py:550
  23.5 14.9 %collective-permute-start.6 = (bf16[192,1536]{1,0:T(8,128)(2,1)S(1)}, bf16[192,1536]{1,0:T(8,128)(2,1)S(1)}, u32[]{:S(2)}, u32[]{:S(2)}) collective-permute-start(bf16[192,1536]{1,0:T(8,128)(2,1)S(1)} %collective-permute-done.2.refs_0_), channel_id=1, source_target_pairs={{0,4},{4,0},{8,12},{12,8},{16,20},{20,16},{24,28},{28,24},{1,5},{5... | collective-permute-start | bytes 1769480 | tf_op jit(solution)/shard_map/ppermute | solution.py:550
  29.6 11.2 %collective-permute-start.4 = (bf16[96,1536]{1,0:T(8,128)(2,1)S(1)}, bf16[96,1536]{1,0:T(8,128)(2,1)S(1)}, u32[]{:S(2)}, u32[]{:S(2)}) collective-permute-start(bf16[96,1536]{1,0:T(8,128)(2,1)S(1)} %collective-permute-done.1.refs_0_), channel_id=1, source_target_pairs={{0,4},{4,0},{8,12},{12,8},{16,20},{20,16},{24,28},{28,24},{1,5},{5... | collective-permute-start | bytes 884744 | tf_op jit(solution)/shard_map/ppermute | solution.py:550
  31.2 9.7 %collective-permute-start.5 = (bf16[96,1536]{1,0:T(8,128)(2,1)S(1)}, bf16[96,1536]{1,0:T(8,128)(2,1)S(1)}, u32[]{:S(2)}, u32[]{:S(2)}) collective-permute-start(bf16[96,1536]{1,0:T(8,128)(2,1)S(1)} %collective-permute-done.3.refs_1_), channel_id=1, source_target_pairs={{0,4},{4,0},{8,12},{12,8},{16,20},{20,16},{24,28},{28,24},{1,5},{5... | collective-permute-start | bytes 884744 | tf_op jit(solution)/shard_map/ppermute | solution.py:550
  48.4 9.5 %collective-permute-start.19 = (bf16[1152,128]{1,0:T(8,128)(2,1)S(1)}, bf16[1152,128]{1,0:T(8,128)(2,1)S(1)}, u32[]{:S(2)}, u32[]{:S(2)}) collective-permute-start(bf16[1152,128]{1,0:T(8,128)(2,1)S(1)} %attention.3.refs_0_), channel_id=1, source_target_pairs={{0,8},{4,12},{8,0},{12,4},{16,24},{20,28},{24,16},{28,20},{1,9},{5... | collective-permute-start | bytes 884744 | tf_op jit(solution)/shard_map/ppermute | solution.py:550
  50.0 9.1 %collective-permute-start.21 = (bf16[1152,128]{1,0:T(8,128)(2,1)S(1)}, bf16[1152,128]{1,0:T(8,128)(2,1)S(1)}, u32[]{:S(2)}, u32[]{:S(2)}) collective-permute-start(bf16[1152,128]{1,0:T(8,128)(2,1)S(1)} %attention.3.refs_0_), channel_id=1, source_target_pairs={{0,16},{4,20},{8,24},{12,28},{16,0},{20,4},{24,8},{28,12},{1,17},{... | collective-permute-start | bytes 884744 | tf_op jit(solution)/shard_map/ppermute | solution.py:550
  55.6 8.7 %collective-permute-start.10 = (bf16[1152,128]{1,0:T(8,128)(2,1)S(1)}, bf16[1152,128]{1,0:T(8,128)(2,1)S(1)}, u32[]{:S(2)}, u32[]{:S(2)}) collective-permute-start(bf16[1152,128]{1,0:T(8,128)(2,1)S(1)} %get-tuple-element.32.refs_0_), channel_id=1, source_target_pairs={{0,8},{4,12},{8,0},{12,4},{16,24},{20,28},{24,16},{28,20},{1,9},{5... | collective-permute-start | bytes 884744 | tf_op jit(solution)/shard_map/ppermute | solution.py:550
  56.1 8.2 %collective-permute-start.18 = (bf16[1152,128]{1,0:T(8,128)(2,1)S(1)}, bf16[1152,128]{1,0:T(8,128)(2,1)S(1)}, u32[]{:S(2)}, u32[]{:S(2)}) collective-permute-start(bf16[1152,128]{1,0:T(8,128)(2,1)S(1)} %attention.3.refs_0_), channel_id=1, source_target_pairs={{0,4},{4,0},{8,12},{12,8},{16,20},{20,16},{24,28},{28,24},{1,5},{5... | collective-permute-start | bytes 884744 | tf_op jit(solution)/shard_map/ppermute | solution.py:550
  56.1 10.3 %collective-permute-start.12 = (bf16[1152,128]{1,0:T(8,128)(2,1)S(1)}, bf16[1152,128]{1,0:T(8,128)(2,1)S(1)}, u32[]{:S(2)}, u32[]{:S(2)}) collective-permute-start(bf16[1152,128]{1,0:T(8,128)(2,1)S(1)} %get-tuple-element.32.refs_0_), channel_id=1, source_target_pairs={{0,16},{4,20},{8,24},{12,28},{16,0},{20,4},{24,8},{28,12},{1,17},{... | collective-permute-start | bytes 884744 | tf_op jit(solution)/shard_map/ppermute | solution.py:550
  57.9 10.8 %collective-permute-start.23 = (bf16[576,128]{1,0:T(8,128)(2,1)S(1)}, bf16[576,128]{1,0:T(8,128)(2,1)S(1)}, u32[]{:S(2)}, u32[]{:S(2)}) collective-permute-start(bf16[576,128]{1,0:T(8,128)(2,1)S(1)} %slice.28), channel_id=1, source_target_pairs={{0,16},{4,20},{8,24},{12,28},{16,0},{20,4},{24,8},{28,12},{1,17},{... | collective-permute-start | bytes 442376 | tf_op jit(solution)/shard_map/ppermute | solution.py:550
  59.1 19.7 %collective-permute-start.20 = (bf16[1152,128]{1,0:T(8,128)(2,1)S(1)}, bf16[1152,128]{1,0:T(8,128)(2,1)}, u32[]{:S(2)}, u32[]{:S(2)}) collective-permute-start(bf16[1152,128]{1,0:T(8,128)(2,1)S(1)} %collective-permute-done.19.refs_2_), channel_id=1, source_target_pairs={{0,4},{4,0},{8,12},{12,8},{16,20},{20,16},{24,28},{28,24},{1,5},{5... | collective-permute-start | bytes 884744 | tf_op jit(solution)/shard_map/ppermute | solution.py:550
  64.3 14.6 %collective-permute-start.22 = (bf16[1152,128]{1,0:T(8,128)(2,1)S(1)}, bf16[1152,128]{1,0:T(8,128)(2,1)}, u32[]{:S(2)}, u32[]{:S(2)}) collective-permute-start(bf16[1152,128]{1,0:T(8,128)(2,1)S(1)} %collective-permute-done.21.refs_4_), channel_id=1, source_target_pairs={{0,4},{4,0},{8,12},{12,8},{16,20},{20,16},{24,28},{28,24},{1,5},{5... | collective-permute-start | bytes 884744 | tf_op jit(solution)/shard_map/ppermute | solution.py:550
  68.7 9.5 %collective-permute-start.15 = (bf16[576,128]{1,0:T(8,128)(2,1)}, bf16[576,128]{1,0:T(8,128)(2,1)}, u32[]{:S(2)}, u32[]{:S(2)}) collective-permute-start(bf16[576,128]{1,0:T(8,128)(2,1)} %slice.27), channel_id=1, source_target_pairs={{0,8},{4,12},{8,0},{12,4},{16,24},{20,28},{24,16},{28,20},{1,9},{5... | collective-permute-start | bytes 442376 | tf_op jit(solution)/shard_map/ppermute | solution.py:550
  78.2 15.7 %collective-permute-start.9 = (bf16[1152,128]{1,0:T(8,128)(2,1)S(1)}, bf16[1152,128]{1,0:T(8,128)(2,1)S(1)}, u32[]{:S(2)}, u32[]{:S(2)}) collective-permute-start(bf16[1152,128]{1,0:T(8,128)(2,1)S(1)} %get-tuple-element.32.refs_0_), channel_id=1, source_target_pairs={{0,4},{4,0},{8,12},{12,8},{16,20},{20,16},{24,28},{28,24},{1,5},{5... | collective-permute-start | bytes 884744 | tf_op jit(solution)/shard_map/ppermute | solution.py:550
  78.8 22.1 %collective-permute-start.11 = (bf16[1152,128]{1,0:T(8,128)(2,1)S(1)}, bf16[1152,128]{1,0:T(8,128)(2,1)S(1)}, u32[]{:S(2)}, u32[]{:S(2)}) collective-permute-start(bf16[1152,128]{1,0:T(8,128)(2,1)S(1)} %collective-permute-done.10.refs_2_), channel_id=1, source_target_pairs={{0,4},{4,0},{8,12},{12,8},{16,20},{20,16},{24,28},{28,24},{1,5},{5... | collective-permute-start | bytes 884744 | tf_op jit(solution)/shard_map/ppermute | solution.py:550
  78.9 23.6 %collective-permute-start.13 = (bf16[1152,128]{1,0:T(8,128)(2,1)S(1)}, bf16[1152,128]{1,0:T(8,128)(2,1)S(1)}, u32[]{:S(2)}, u32[]{:S(2)}) collective-permute-start(bf16[1152,128]{1,0:T(8,128)(2,1)S(1)} %collective-permute-done.12.refs_4_), channel_id=1, source_target_pairs={{0,4},{4,0},{8,12},{12,8},{16,20},{20,16},{24,28},{28,24},{1,5},{5... | collective-permute-start | bytes 884744 | tf_op jit(solution)/shard_map/ppermute | solution.py:550
  79.3 23.2 %collective-permute-start.16 = (bf16[576,128]{1,0:T(8,128)(2,1)}, bf16[576,128]{1,0:T(8,128)(2,1)S(1)}, u32[]{:S(2)}, u32[]{:S(2)}) collective-permute-start(bf16[576,128]{1,0:T(8,128)(2,1)} %collective-permute-done.14.refs_6_), channel_id=1, source_target_pairs={{0,4},{4,0},{8,12},{12,8},{16,20},{20,16},{24,28},{28,24},{1,5},{5... | collective-permute-start | bytes 442376 | tf_op jit(solution)/shard_map/ppermute | solution.py:550
  79.4 23.1 %collective-permute-start.17 = (bf16[576,128]{1,0:T(8,128)(2,1)}, bf16[576,128]{1,0:T(8,128)(2,1)S(1)}, u32[]{:S(2)}, u32[]{:S(2)}) collective-permute-start(bf16[576,128]{1,0:T(8,128)(2,1)} %collective-permute-done.15.refs_7_), channel_id=1, source_target_pairs={{0,4},{4,0},{8,12},{12,8},{16,20},{20,16},{24,28},{28,24},{1,5},{5... | collective-permute-start | bytes 442376 | tf_op jit(solution)/shard_map/ppermute | solution.py:550
  94.0 22.7 %collective-permute-start.28 = (bf16[688,128]{1,0:T(8,128)(2,1)S(1)}, bf16[688,128]{1,0:T(8,128)(2,1)S(1)}, u32[]{:S(2)}, u32[]{:S(2)}) collective-permute-start(bf16[688,128]{1,0:T(8,128)(2,1)S(1)} %out_merge.3.refs_1_), channel_id=1, source_target_pairs={{0,1},{1,2},{2,3},{4,5},{5,6},{6,7},{8,9},{9,10},{10,11},{12,13},{... | collective-permute-start | bytes 528392 | tf_op jit(solution)/shard_map/ppermute | solution.py:576
  100.9 16.4 %collective-permute-start.34 = (bf16[688,128]{1,0:T(8,128)(2,1)S(1)}, bf16[688,128]{1,0:T(8,128)(2,1)S(1)}, u32[]{:S(2)}, u32[]{:S(2)}) collective-permute-start(bf16[688,128]{1,0:T(8,128)(2,1)S(1)} %out_merge.3.refs_1_), channel_id=1, source_target_pairs={{3,2},{2,1},{1,0},{7,6},{6,5},{5,4},{11,10},{10,9},{9,8},{15,14},{... | collective-permute-start | bytes 528392 | tf_op jit(solution)/shard_map/ppermute | solution.py:576
  110.8 8.0 %collective-permute-start.27 = (bf16[688,128]{1,0:T(8,128)(2,1)S(1)}, bf16[688,128]{1,0:T(8,128)(2,1)S(1)}, u32[]{:S(2)}, u32[]{:S(2)}) collective-permute-start(bf16[688,128]{1,0:T(8,128)(2,1)S(1)} %out_merge.2.refs_0_), channel_id=1, source_target_pairs={{0,1},{1,2},{2,3},{4,5},{5,6},{6,7},{8,9},{9,10},{10,11},{12,13},{... | collective-permute-start | bytes 528392 | tf_op jit(solution)/shard_map/ppermute | solution.py:576
  117.4 10.8 %collective-permute-start.36 = (bf16[688,128]{1,0:T(8,128)(2,1)S(1)}, bf16[688,128]{1,0:T(8,128)(2,1)S(1)}, u32[]{:S(2)}, u32[]{:S(2)}) collective-permute-start(bf16[688,128]{1,0:T(8,128)(2,1)S(1)} %collective-permute-done.34.refs_9_), channel_id=1, source_target_pairs={{2,1},{1,0},{6,5},{5,4},{10,9},{9,8},{14,13},{13,12},{18,17},{17,1... | collective-permute-start | bytes 528392 | tf_op jit(solution)/shard_map/ppermute | solution.py:576
  118.7 10.7 %collective-permute-start.29 = (bf16[688,128]{1,0:T(8,128)(2,1)S(1)}, bf16[688,128]{1,0:T(8,128)(2,1)S(1)}, u32[]{:S(2)}, u32[]{:S(2)}) collective-permute-start(bf16[688,128]{1,0:T(8,128)(2,1)S(1)} %collective-permute-done.27.refs_2_), channel_id=1, source_target_pairs={{1,2},{2,3},{5,6},{6,7},{9,10},{10,11},{13,14},{14,15},{17,18},{18... | collective-permute-start | bytes 528392 | tf_op jit(solution)/shard_map/ppermute | solution.py:576
  122.9 13.0 %collective-permute-start.35 = (bf16[688,128]{1,0:T(8,128)(2,1)S(1)}, bf16[688,128]{1,0:T(8,128)(2,1)S(1)}, u32[]{:S(2)}, u32[]{:S(2)}) collective-permute-start(bf16[688,128]{1,0:T(8,128)(2,1)S(1)} %collective-permute-done.33.refs_8_), channel_id=1, source_target_pairs={{2,1},{1,0},{6,5},{5,4},{10,9},{9,8},{14,13},{13,12},{18,17},{17,1... | collective-permute-start | bytes 528392 | tf_op jit(solution)/shard_map/ppermute | solution.py:576
  124.2 13.0 %collective-permute-start.32 = (bf16[688,128]{1,0:T(8,128)(2,1)S(1)}, bf16[688,128]{1,0:T(8,128)(2,1)}, u32[]{:S(2)}, u32[]{:S(2)}) collective-permute-start(bf16[688,128]{1,0:T(8,128)(2,1)S(1)} %collective-permute-done.30.refs_5_), channel_id=1, source_target_pairs={{2,3},{6,7},{10,11},{14,15},{18,19},{22,23},{26,27},{30,31}} | collective-permute-start | bytes 528392 | tf_op jit(solution)/shard_map/ppermute | solution.py:576
  128.1 11.6 %collective-permute-start.38 = (bf16[688,128]{1,0:T(8,128)(2,1)S(1)}, bf16[688,128]{1,0:T(8,128)(2,1)}, u32[]{:S(2)}, u32[]{:S(2)}) collective-permute-start(bf16[688,128]{1,0:T(8,128)(2,1)S(1)} %collective-permute-done.36.refs_11_), channel_id=1, source_target_pairs={{1,0},{5,4},{9,8},{13,12},{17,16},{21,20},{25,24},{29,28}} | collective-permute-start | bytes 528392 | tf_op jit(solution)/shard_map/ppermute | solution.py:576
  129.4 10.3 %collective-permute-start.31 = (bf16[688,128]{1,0:T(8,128)(2,1)S(1)}, bf16[688,128]{1,0:T(8,128)(2,1)}, u32[]{:S(2)}, u32[]{:S(2)}) collective-permute-start(bf16[688,128]{1,0:T(8,128)(2,1)S(1)} %collective-permute-done.29.refs_4_), channel_id=1, source_target_pairs={{2,3},{6,7},{10,11},{14,15},{18,19},{22,23},{26,27},{30,31}} | collective-permute-start | bytes 528392 | tf_op jit(solution)/shard_map/ppermute | solution.py:576
  (24 other events, 249.6 us)

commit v3 on v2

--- a/solution.py
+++ b/solution.py
@@ -164,10 +164,51 @@
     return loaded[0] if len(loaded) == 1 else jnp.concatenate(loaded, axis=0)
 
 
+def payload_kernel(segments, rows, columns, mask, embed, patches, out):
+    labels = [one[...].astype(jnp.float32) for one in (segments, rows, columns, mask)]
+    labels.append(jnp.zeros((4, labels[0].shape[1]), jnp.float32))
+    labels = jnp.concatenate(labels, axis=0).astype(jnp.bfloat16)
+    shape = (8, LANES)
+    row = lax.broadcasted_iota(jnp.int32, shape, 0)
+    place = jnp.where(row == lax.broadcasted_iota(jnp.int32, shape, 1), 1.0, 0.0)
+    turned = lax.dot_general(
+        labels,
+        place.astype(jnp.bfloat16),
+        (((0,), (0,)), ((), ())),
+        preferred_element_type=jnp.float32,
+    )
+    masked = turned[:, 3:4] > 0.5
+    tokens = jnp.where(
+        masked, embed[...].astype(jnp.float32)[None, :], patches[0].astype(jnp.float32)
+    )
+    out[:, :D] = tokens.astype(jnp.bfloat16)
+    out[:, D:] = turned.astype(jnp.bfloat16)
+
+
+def payload_call(segments, rows, columns, mask, embed, patches):
+    count = patches.shape[1]
+    operands = (segments, rows, columns, mask, embed, patches)
+    fixed = lambda shape: pl.BlockSpec(shape, lambda i: (0,) * len(shape))
+    shape = (count, D + LANES)
+    return pl.pallas_call(
+        payload_kernel,
+        grid=(1,),
+        in_specs=[fixed(one.shape) for one in operands],
+        out_specs=fixed(shape),
+        out_shape=jax.ShapeDtypeStruct(shape, jnp.bfloat16),
+        compiler_params=pltpu.CompilerParams(vmem_limit_bytes=8 << 20),
+        cost_estimate=pl.CostEstimate(
+            flops=count * D, bytes_accessed=4 * count * D, transcendentals=0
+        ),
+        name="payload",
+    )(*operands)
+
+
 def qkv_kernel(count, place, *refs):
     first, second = refs[:count], refs[count : 2 * count]
     table, gain, weight = refs[2 * count : 2 * count + 3]
-    inputs_out, qkv_out, label_out = refs[-3:]
+    *outs, inputs_out, qkv_out, label_out, sems = refs[-7:]
+    start = pl.multiple_of(place[0] * inputs_out.shape[0], inputs_out.shape[0])
     mine, other = stacked(first), stacked(second)
     leads = place[1] == 0
     ahead = jnp.where(leads, mine, other)
@@ -175,6 +216,13 @@
     both = jnp.concatenate([ahead, behind], axis=0)
     inputs_out[...] = both[:, :D]
     label_out[...] = both[:, D:]
+    target = pl.ds(start, inputs_out.shape[0])
+    copies = [
+        pltpu.make_async_copy(source, out.at[target, :], sems.at[number])
+        for number, (source, out) in enumerate(zip((inputs_out, qkv_out, label_out), outs))
+    ]
+    copies[0].start()
+    copies[2].start()
     labels = both[:, D:].astype(jnp.float32)
     normed = norm_rows(both[:, :D].astype(jnp.float32), gain[...]).astype(jnp.bfloat16)
     columns = jnp.dot(normed, weight[...], preferred_element_type=jnp.float32)
@@ -210,28 +258,30 @@
     parts.append(jnp.where(wide < HD, values_part, ones))
     parts.append(jnp.where((wide >= HD) & (wide < 2 * HD), values_part, ones))
     qkv_out[...] = jnp.concatenate(parts, axis=1).astype(jnp.bfloat16)
+    copies[1].start()
+    for copy in copies:
+        copy.wait()
 
 
 def qkv_call(place, first, second, table, gain, weight, earlier, total):
     rows = 2 * sum(piece.shape[0] for piece in first)
-    whole = lambda shape: pl.BlockSpec(shape, lambda i, place: (0,) * len(shape))
-    block = lambda width: pl.BlockSpec((rows, width), lambda i, place: (place[0], 0))
     widths = (D, 10 * LANES, LANES)
     operands = [*first, *second, table, gain, weight]
+    vmem = pl.BlockSpec(memory_space=pltpu.VMEM)
+    anywhere = pl.BlockSpec(memory_space=pl.ANY)
     return pl.pallas_call(
         functools.partial(qkv_kernel, len(first)),
-        grid_spec=pltpu.PrefetchScalarGridSpec(
-            num_scalar_prefetch=1,
-            grid=(1,),
-            in_specs=[whole(one.shape) for one in operands]
-            + [pl.BlockSpec(memory_space=pl.ANY)] * len(earlier),
-            out_specs=[block(width) for width in widths],
-        ),
+        in_specs=[pl.BlockSpec(memory_space=pltpu.SMEM)]
+        + [vmem] * len(operands)
+        + [anywhere] * len(earlier),
+        out_specs=[anywhere] * len(widths),
+        scratch_shapes=[pltpu.VMEM((rows, width), jnp.bfloat16) for width in widths]
+        + [pltpu.SemaphoreType.DMA((len(widths),))],
         out_shape=[jax.ShapeDtypeStruct((total, width), jnp.bfloat16) for width in widths],
         input_output_aliases={1 + len(operands) + i: i for i in range(len(earlier))},
-        compiler_params=pltpu.CompilerParams(vmem_limit_bytes=24 << 20),
+        compiler_params=pltpu.CompilerParams(vmem_limit_bytes=16 << 20),
         cost_estimate=pl.CostEstimate(
-            flops=2 * rows * D * weight.shape[1],
+            flops=6 * rows * D * weight.shape[1],
             bytes_accessed=2 * (rows * 4 * D + weight.size),
             transcendentals=rows,
         ),
@@ -341,9 +391,9 @@
             pltpu.VMEM((2, rows, LANES), jnp.float32),
             pltpu.VMEM((total // BLOCK, 8, BLOCK), jnp.float32),
         ],
-        compiler_params=pltpu.CompilerParams(vmem_limit_bytes=28 << 20),
+        compiler_params=pltpu.CompilerParams(vmem_limit_bytes=22 << 20),
         cost_estimate=pl.CostEstimate(
-            flops=4 * rows * total * 2 * LANES,
+            flops=10 * rows * total * 2 * LANES,
             bytes_accessed=2 * block.size,
             transcendentals=rows * total,
         ),
@@ -388,12 +438,11 @@
     )(ids, weight)
 
 
-def merge_kernel(counts, inputs, weight, gain, merge_weight, bias, note, *refs):
-    pieces = refs[: sum(counts)]
-    out, state, merge, merge_sem = refs[sum(counts) :]
-    merge_copy = pltpu.make_async_copy(merge_weight, merge, merge_sem)
-    merge_copy.start()
-    rows = inputs.shape[0]
+def merge_kernel(start, counts, packs, last, *refs):
+    inputs, weight, gain, merge_weight, bias = refs[:5]
+    pieces = refs[5 : 5 + sum(counts)]
+    *refs, state = refs[5 + sum(counts) :]
+    rows = state.shape[1]
     half = rows // 2
     rest = 2 * HD - LANES
     sources, at = [], 0
@@ -416,12 +465,12 @@
         mixed = jnp.dot(
             jnp.concatenate(lined, axis=1), weight[...], preferred_element_type=jnp.float32
         )
-        normed = norm_rows(inputs[token, :].astype(jnp.float32) + mixed, gain[...])
+        before = inputs[start + part * half : start + (part + 1) * half, :].astype(jnp.float32)
+        normed = norm_rows(before + mixed, gain[...])
         for column in range(D // LANES):
             state[column, token, :] = normed[:, column * LANES : (column + 1) * LANES]
     groups = rows // 4
     total = bias[...]
-    merge_copy.wait()
     for quadrant in range(4):
         tokens = jnp.concatenate(
             [
@@ -432,46 +481,64 @@
         )
         total = total + lax.dot_general(
             tokens,
-            merge[:, quadrant * D : (quadrant + 1) * D],
+            merge_weight[:, quadrant * D : (quadrant + 1) * D],
             (((1,), (1,)), ((), ())),
             preferred_element_type=jnp.float32,
         )
+    total = total.astype(jnp.bfloat16)
+    if not last:
+        refs[0][...] = total
+        return
+    me, note, *earlier = refs[:-packs]
+    outs = refs[-packs:]
+    total = jnp.concatenate([*[one[...] for one in earlier], total], axis=0)
     whole = total.shape[1] // LANES
-    for column in range(whole):
-        out[column * groups : (column + 1) * groups, :] = total[
-            :, column * LANES : (column + 1) * LANES
-        ].astype(jnp.bfloat16)
-    low = total[: groups // 2, whole * LANES :]
-    up = total[groups // 2 :, whole * LANES :]
-    end = whole * groups + groups // 2
-    out[whole * groups : end, :] = jnp.concatenate([low, up], axis=1).astype(jnp.bfloat16)
-    out[end:, :] = note[...]
-
-
-def merge_call(start, rows, sources, inputs, weight, gain, merge_weight, bias, note):
+    most = outs[0].shape[0] * LANES // total.shape[1]
+    notes = note[...].astype(jnp.float32)
+    note_row = lax.broadcasted_iota(jnp.int32, notes.shape, 0)
+    slot = lax.broadcasted_iota(jnp.int32, (most, total.shape[0]), 0)
+    row = lax.broadcasted_iota(jnp.int32, (most, total.shape[0]), 1)
+    for place, out in enumerate(outs):
+        found = jnp.where(note_row == (me[0] ^ place), notes, 0.0)
+        found = jnp.sum(found, axis=0, keepdims=True)
+        first = (16.0 * found[:, :1] + found[:, 1:2]).astype(jnp.int32)
+        length = (16.0 * found[:, 2:3] + found[:, 3:4]).astype(jnp.int32)
+        chosen = (row == slot + first) & (slot < length)
+        chosen = jnp.where(chosen, 1.0, 0.0).astype(jnp.bfloat16)
+        block = jnp.dot(chosen, total, preferred_element_type=jnp.float32)
+        for column in range(whole):
+            out[column * most : (column + 1) * most, :] = block[
+                :, column * LANES : (column + 1) * LANES
+            ].astype(jnp.bfloat16)
+        low = block[: most // 2, whole * LANES :]
+        up = block[most // 2 :, whole * LANES :]
+        out[whole * most :, :] = jnp.concatenate([low, up], axis=1).astype(jnp.bfloat16)
+
+
+def merge_call(start, rows, sources, inputs, weight, gain, merge_weight, bias, packs, route):
     groups = rows // 4
     width = merge_weight.shape[0]
     pieces = [piece for source in sources for piece in source]
-    fixed = lambda shape: pl.BlockSpec(shape, lambda i: (0,) * len(shape))
-    out_shape = (groups * width // LANES + 16, LANES)
-    operands = [inputs, weight, gain, merge_weight, bias, note, *pieces]
-    specs = [fixed(one.shape) for one in operands]
-    specs[0] = pl.BlockSpec((rows, D), lambda i: (start // rows, 0))
-    specs[3] = pl.BlockSpec(memory_space=pl.ANY)
+    vmem = pl.BlockSpec(memory_space=pltpu.VMEM)
+    operands = [inputs, weight, gain, merge_weight, bias, *pieces]
+    specs = [vmem] * len(operands)
+    shapes = [jax.ShapeDtypeStruct((groups, width), jnp.bfloat16)]
+    if route:
+        me, most, *others = route
+        operands += [me, *others]
+        specs += [pl.BlockSpec(memory_space=pltpu.SMEM)] + [vmem] * len(others)
+        shapes = [jax.ShapeDtypeStruct((most * width // LANES, LANES), jnp.bfloat16)] * packs
     return pl.pallas_call(
-        functools.partial(merge_kernel, [len(source) for source in sources]),
-        grid=(1,),
+        functools.partial(
+            merge_kernel, start, [len(source) for source in sources], packs, bool(route)
+        ),
         in_specs=specs,
-        out_specs=fixed(out_shape),
-        scratch_shapes=[
-            pltpu.VMEM((D // LANES, rows, LANES), jnp.float32),
-            pltpu.VMEM(merge_weight.shape, jnp.bfloat16),
-            pltpu.SemaphoreType.DMA,
-        ],
-        out_shape=jax.ShapeDtypeStruct(out_shape, jnp.bfloat16),
-        compiler_params=pltpu.CompilerParams(vmem_limit_bytes=36 << 20),
+        out_specs=[vmem] * len(shapes),
+        scratch_shapes=[pltpu.VMEM((D // LANES, rows, LANES), jnp.float32)],
+        out_shape=shapes,
+        compiler_params=pltpu.CompilerParams(vmem_limit_bytes=26 << 20),
         cost_estimate=pl.CostEstimate(
-            flops=2 * rows * D * D + 2 * groups * merge_weight.size,
+            flops=4 * rows * D * D + 2 * groups * merge_weight.size,
             bytes_accessed=2 * (D * D + merge_weight.size + 3 * rows * D),
             transcendentals=rows,
         ),
@@ -479,70 +546,35 @@
     )(*operands)
 
 
-def select_kernel(packs, offsets, groups_each, me, *refs):
-    parts, out = refs[:-1], refs[-1]
+def place_kernel(me, *refs):
+    blocks, out = refs[:-1], refs[-1]
     most, width = out.shape[1:]
     whole = width // LANES
+    half = most // 2
     middle = LANES // 2
-    chunks = len(groups_each)
-    for number, offset in enumerate(offsets):
-        source = parts[number * chunks : (number + 1) * chunks]
-        target = me[0] + offset
-
-        @pl.when((target >= 0) & (target < packs))
-        def _(source=source, target=target):
-            sums = [None] * (whole + 2)
-            base = 0
-            for part, groups in zip(source, groups_each):
-                half = groups // 2
-                if base == 0:
-                    end = whole * groups + half
-                    notes = part[end:, :].astype(jnp.float32)
-                    mine = lax.broadcasted_iota(jnp.int32, notes.shape, 0) == me[0]
-                    note = jnp.sum(jnp.where(mine, notes, 0.0), axis=0, keepdims=True)
-                    first = (16.0 * note[:, :1] + note[:, 1:2]).astype(jnp.int32)
-                    length = (16.0 * note[:, 2:3] + note[:, 3:4]).astype(jnp.int32)
-                slot = lax.broadcasted_iota(jnp.int32, (most, groups), 0)
-                row = lax.broadcasted_iota(jnp.int32, (most, groups), 1) + base
-                chosen = (row == slot + first) & (slot < length)
-                chosen = jnp.where(chosen, 1.0, 0.0).astype(jnp.bfloat16)
-                product = lambda a, b: jnp.dot(a, b, preferred_element_type=jnp.float32)
-                terms = [
-                    product(chosen, part[column * groups : (column + 1) * groups, :])
-                    for column in range(whole)
-                ]
-                packed = part[whole * groups : whole * groups + half, :]
-                terms.append(product(chosen[:, :half], packed))
-                terms.append(product(chosen[:, half:], packed))
-                sums = [
-                    term if kept is None else kept + term for kept, term in zip(sums, terms)
-                ]
-                base += groups
-            for column in range(whole):
-                out[target, :, column * LANES : (column + 1) * LANES] = sums[column].astype(
-                    jnp.bfloat16
-                )
-            last = sums[whole] + pltpu.roll(sums[whole + 1], middle, 1)
-            out[target, :, whole * LANES :] = last[:, :middle].astype(jnp.bfloat16)
-
-
-def select_call(me, gathered, groups_each, packs, most, width):
-    offsets = [offset for offset, _ in gathered[0]]
-    parts = [chunk[number][1] for number in range(len(offsets)) for chunk in gathered]
+    for place, block in enumerate(blocks):
+        target = me[0] ^ place
+        for column in range(whole):
+            out[target, :, column * LANES : (column + 1) * LANES] = block[
+                column * most : (column + 1) * most, :
+            ]
+        out[target, :half, whole * LANES :] = block[whole * most :, :middle]
+        out[target, half:, whole * LANES :] = block[whole * most :, middle:]
+
+
+def place_call(me, blocks, most, width):
     vmem = pl.BlockSpec(memory_space=pltpu.VMEM)
     return pl.pallas_call(
-        functools.partial(select_kernel, packs, offsets, groups_each),
-        in_specs=[pl.BlockSpec(memory_space=pltpu.SMEM)] + [vmem] * len(parts),
+        place_kernel,
+        in_specs=[pl.BlockSpec(memory_space=pltpu.SMEM)] + [vmem] * len(blocks),
         out_specs=vmem,
-        out_shape=jax.ShapeDtypeStruct((packs, most, width), jnp.bfloat16),
-        compiler_params=pltpu.CompilerParams(vmem_limit_bytes=16 << 20),
+        out_shape=jax.ShapeDtypeStruct((len(blocks), most, width), jnp.bfloat16),
+        compiler_params=pltpu.CompilerParams(vmem_limit_bytes=8 << 20),
         cost_estimate=pl.CostEstimate(
-            flops=4 * packs * most * sum(groups_each) * width,
-            bytes_accessed=4 * packs * most * width,
-            transcendentals=0,
+            flops=0, bytes_accessed=4 * len(blocks) * most * width, transcendentals=0
         ),
-        name="select_rows",
-    )(me, *parts)
+        name="place_rows",
+    )(me, *blocks)
 
 
 def send_seq(value, flip):
@@ -550,32 +582,17 @@
     return lax.ppermute(value, "seq", [(i, i ^ flip) for i in range(size)])
 
 
-def gather_seq(value):
-    half = value.shape[0] // 2
-    near = [send_seq(value, 2), send_seq(value, 4)]
-    own_swap = send_seq(value, 1)
-    far = [send_seq(near[0][:half], 4), send_seq(near[1][half:], 2)]
-    swapped = [send_seq(one, 1) for one in near + far]
-    return [
-        ([value], [own_swap]),
-        ([near[0]], [swapped[0]]),
-        ([near[1]], [swapped[1]]),
-        (far, swapped[2:]),
-    ]
-
-
-def gather_pack(value):
-    size = lax.axis_size("pack")
-    found = [(0, value)]
-    for direction in (1, -1):
-        moving = value
-        for step in range(1, size):
-            ahead = [(z, z + 1) for z in range(step - 1, size - 1)]
-            if direction < 0:
-                ahead = [(size - 1 - a, size - 1 - b) for a, b in ahead]
-            moving = lax.ppermute(moving, "pack", ahead)
-            found.append((-direction * step, moving))
-    return found
+def after(values, *earlier):
+    return lax.optimization_barrier((tuple(values), earlier))[0]
+
+
+def near_shards(value):
+    return [send_seq(value, 1), send_seq(value, 2), send_seq(value, 4)]
+
+
+def far_shards(across_x, across_y):
+    half = across_x.shape[0] // 2
+    return [send_seq(across_x[:half], 4), send_seq(across_y[half:], 2)]
 
 
 def weight_order(heads_here):
@@ -635,10 +652,8 @@
     me = lax.axis_index("seq").astype(jnp.int32)
     pack = lax.axis_index("pack").astype(jnp.int32)
 
-    tokens = jnp.where(patch_mask[0][:, None] == 1, mask_embed[None, :], patches[0])
-    labels = jnp.stack([segment_ids[0], patch_rows[0], patch_column[0]], axis=1)
-    labels = jnp.pad(labels.astype(jnp.bfloat16), ((0, 0), (0, LANES - labels.shape[1])))
-    shares = gather_seq(jnp.concatenate([tokens, labels], axis=1))
+    value = payload_call(segment_ids, patch_rows, patch_column, patch_mask, mask_embed, patches)
+    own_swap, across_x, across_y = near_shards(value)
 
     order = jnp.asarray(weight_order(heads_here))
     spread = (jnp.arange(qkv_weight.shape[1])[:, None] == order[None, :]).astype(jnp.bfloat16)
@@ -650,10 +665,17 @@
     ids = jnp.stack([me ^ place for place in range(shards)])
     ordered = order_call(ids, out_weight)
 
-    buffers = ()
-    for place, (first, second) in enumerate(shares):
-        where = jnp.stack([(me // 2) ^ place, me % 2])
-        buffers = qkv_call(where, first, second, table, gain, weight, buffers, total)
+    chip, core = me // 2, me % 2
+    project = lambda place, first, second, earlier: qkv_call(
+        jnp.stack([chip ^ place, core]), first, second, table, gain, weight, earlier, total
+    )
+    buffers = project(0, [value], [own_swap], ())
+    across_x, across_y = after([across_x, across_y], buffers[2], ordered)
+    far = far_shards(across_x, across_y)
+    buffers = project(1, [across_x], [send_seq(across_x, 1)], buffers)
+    buffers = project(2, [across_y], [send_seq(across_y, 1)], buffers)
+    far = after(far, buffers[2])
+    buffers = project(3, far, [send_seq(one, 1) for one in far], buffers)
     inputs, block, labels = buffers
 
     starts = [sum(CHUNKS[:number]) for number in range(len(CHUNKS))]
@@ -661,24 +683,40 @@
     for start, rows in zip(starts, CHUNKS):
         made = attention_call(start, rows, image_owner[0], labels, block, note is None)
         note = made[1] if note is None else note
-        attended.append(gather_seq(made[0]))
-    gathered = []
-    for start, rows, shares in zip(starts, CHUNKS, attended):
-        sources = [pieces for share in shares for pieces in share]
-        projected = merge_call(
-            start, rows, sources, inputs, ordered, merge_gain_row, merge_weight.T, bias, note
+        attended.append((made[0], near_shards(made[0])))
+    latest = attended[-1][0]
+    most = 2 * (total // 4) // images
+    projected, moving = [], []
+    for own, (own_swap, across_x, across_y) in attended:
+        across_x, across_y = after([across_x, across_y], latest)
+        far = far_shards(across_x, across_y)
+        moving.append(
+            (own, own_swap, across_x, send_seq(across_x, 1), across_y, send_seq(across_y, 1), far)
         )
-        gathered.append(gather_pack(projected))
-    most = 2 * (total // 4) // images
-    groups_each = [rows // 4 for rows in CHUNKS]
-    return select_call(pack[None], gathered, groups_each, packs, most, merge_weight.shape[1])[None]
+    for number, (start, rows) in enumerate(zip(starts, CHUNKS)):
+        *near, far = moving[number]
+        if projected:
+            far = after(far, projected[-1])
+        sources = [[one] for one in near] + [far, [send_seq(one, 1) for one in far]]
+        route = ()
+        if number == len(CHUNKS) - 1:
+            route = (pack[None], most, note, *projected)
+        made = merge_call(
+            start, rows, sources, inputs, ordered, merge_gain_row, merge_weight.T, bias, packs, route
+        )
+        projected.append(made[0])
+    blocks = [made[0]] + [
+        lax.ppermute(made[flip], "pack", [(z, z ^ flip) for z in range(packs)])
+        for flip in range(1, packs)
+    ]
+    return place_call(pack[None], blocks, most, merge_weight.shape[1])[None]
 
 
 def local(*arguments):
     patches, weight = arguments[0], arguments[4]
     shards = lax.axis_size("seq")
     fits = shards == 8 and HEADS // shards == 2 and weight.shape[1] == 6 * HD
-    fits = fits and patches.shape[1] * shards == sum(CHUNKS)
+    fits = fits and patches.shape[1] * shards == sum(CHUNKS) and lax.axis_size("pack") == 4
     return fast_local(*arguments) if fits else general_local(*arguments)
 
 

time: 147 us -> 145 us (0.986); the launches traced: 148 us -> 143 us
  local copies, waits for them, and re-layouts: 9.45 us -> 44.4 us
  starting transfers between devices: 41.6 us -> 20.8 us
  waiting for transfers between devices: 44 us -> 25.4 us
  other arithmetic: 3.76 us -> 0.3 us
  Pallas kernels: 46.6 us -> 50 us
    unnamed x34 -> x78, local copies, waits for them, and re-layouts: 8.45 us -> 43.5 us
    ppermute x12 -> x3, starting transfers between devices: 23.5 us -> 4.44 us  [fast_local(): lax.ppermute(made[flip], 'pack', [(z, z ^ flip) for z in range(packs)])]
    ppermute x27, waiting for transfers between devices: 26.6 us -> 14.2 us  [send_seq(): return lax.ppermute(value, 'seq', [(i, i ^ flip) for i in range(size)])]
    ppermute x12 -> x3, waiting for transfers between devices: 17.4 us -> 11.2 us  [fast_local(): lax.ppermute(made[flip], 'pack', [(z, z ^ flip) for z in range(packs)])]
    pallas_call x2, Pallas kernels: 9.9 us -> 13.8 us  [attention_call(): pl.pallas_call(functools.partial(attention_kernel, start), in_specs=[pl.B...]
    ppermute x27, starting transfers between devices: 18.2 us -> 16.4 us  [send_seq(): return lax.ppermute(value, 'seq', [(i, i ^ flip) for i in range(size)])]
    another operation x7 -> x4, other arithmetic: 1.82 us -> 0.3 us  [fast_local(): jnp.stack([chip ^ place, core])]
    pallas_call x7 -> x8, Pallas kernels: 33.3 us -> 32.7 us  [the longest x4 15.5 us: qkv_call(): pl.pallas_call(functools.partial(qkv_kernel, len(first)), in_specs=[pl.Bl...]
  transfers between devices with their start and end apart: 39 -> 30, of which waited for: 15 -> 10; matrix products, arithmetic and copies ran while one was open for 2% -> 2% of each run, Pallas kernels for 23% -> 20%
where the time goes in v3:
time: 145 us; the launch traced here: 143 us
  Pallas kernels  50 us (34%)
  local copies, waits for them, and re-layouts  44.4 us (31%)
  waiting for transfers between devices  25.4 us (18%)
  starting transfers between devices  20.8 us (14%)
  matrix products  1.92 us (1%)
    unnamed x78, local copies, waits for them, and re-layouts  43.5 us
    ppermute x27, starting transfers between devices, send_seq(): return lax.ppermute(value, 'seq', [(i, i ^ flip) for i in range(size)])  16.4 us
    pallas_call x4, Pallas kernels, qkv_call(): pl.pallas_call(functools.partial(qkv_kernel, len(first)), in_specs=[pl.Bl...  15.5 us
    pallas_call x2, Pallas kernels, merge_call(): pl.pallas_call(functools.partial(merge_kernel, start, [len(source) for so...  15 us
    ppermute x27, waiting for transfers between devices, send_seq(): return lax.ppermute(value, 'seq', [(i, i ^ flip) for i in range(size)])  14.2 us
    pallas_call x2, Pallas kernels, attention_call(): pl.pallas_call(functools.partial(attention_kernel, start), in_specs=[pl.B...  13.8 us
    ppermute x3, waiting for transfers between devices, fast_local(): lax.ppermute(made[flip], 'pack', [(z, z ^ flip) for z in range(packs)])  11.2 us
    ppermute x3, starting transfers between devices, fast_local(): lax.ppermute(made[flip], 'pack', [(z, z ^ flip) for z in range(packs)])  4.44 us
  transfers between devices with their start and end apart: 30, of which 10 were waited for; matrix products, arithmetic and copies ran while one was open for 2% of the time, Pallas kernels for 20%

profile of v3, /device:TPU:0, one launch (start us, length us, event | category | flops | bytes accessed | tf_op | source)
XLA Modules:
  0.0 143.1 jit_solution(11874496704138916577)
XLA Ops:
  6.2 2.5 %collective-permute-start = (bf16[192,1536]{1,0:T(8,128)(2,1)}, bf16[192,1536]{1,0:T(8,128)(2,1)S(1)}, u32[]{:S(2)}, u32[]{:S(2)}) collective-permute-start(bf16[192,1536]{1,0:T(8,128)(2,1)} %payload.1.refs_0_), channel_id=1, source_target_pairs={{0,8},{4,12},{8,0},{12,4},{16,24},{20,28},{24,16},{28,20},{1,9},{5... | collective-permute-start | bytes 1769480 | tf_op jit(solution)/shard_map/ppermute | solution.py:582
  11.0 2.1 %copy-done.18 = bf16[1408,1408]{1,0:T(8,128)(2,1)S(1)} copy-done((bf16[1408,1408]{1,0:T(8,128)(2,1)S(1)}, bf16[1408,1408]{1,0:T(8,128)(2,1)}, u32[]{:S(2)}) %copy-start.18) | copy-done | bytes 3964952
  13.1 3.4 %order_rows.1.refs_1_ = bf16[1536,1408]{1,0:T(8,128)(2,1)S(1)} custom-call(s32[8]{0:T(128)S(1)} %stack.70.ids, bf16[1408,1408]{1,0:T(8,128)(2,1)S(1)} %copy-done.18), custom_call_target="tpu_custom_call" | custom-call | bytes 7929856 | tf_op jit(solution)/shard_map/order_rows/pallas_call | solution.py:426
  16.5 2.1 %copy-done.16 = bf16[1536,1408]{1,0:T(8,128)(2,1)} copy-done((bf16[1536,1408]{1,0:T(8,128)(2,1)}, bf16[1536,1408]{1,0:T(8,128)(2,1)S(1)}, u32[]{:S(2)}) %copy-start.16) | copy-done | bytes 4325400
  18.6 1.9 %fusion.refs_4_.refs_6_ = bf16[1408,768]{1,0:T(8,128)(2,1)S(1)} fusion(bf16[1408,528]{0,1:T(8,128)(2,1)S(1)} %copy-done, s32[768]{0:T(1024)S(1)} %copy-done.32), kind=kOutput, calls=%fused_computation.1 | convolution fusion | flops 1143386112 | bytes 3652608 | tf_op jit(solution)/shard_map/dot_general | solution.py:660
  20.6 4.5 %norm_qkv.4 = (bf16[1536,1408]{1,0:T(8,128)(2,1)S(1)}, bf16[1536,1280]{1,0:T(8,128)(2,1)S(1)}, bf16[1536,128]{1,0:T(8,128)(2,1)S(1)}) custom-call(s32[2]{0:T(128)S(1)} %pad_add_fusion.1.place, bf16[192,1536]{1,0:T(8,128)(2,1)} %payload.1.refs_0_, bf16[192,1536]{1,0:T(8,128)(2,1)} %collective-permute-done.2.refs_1_, bf16[128,512]{1,0:T(8,128)(2,1)S(1)} %copy-done.19, ...), custom_call_target="tpu_custom_call" | custom-call | flops 2491416576 | bytes 6488064 | tf_op jit(solution)/shard_map/norm_qkv/pallas_call | solution.py:272
  25.2 2.0 %copy-done.1 = bf16[1536,1408]{1,0:T(8,128)(2,1)} copy-done((bf16[1536,1408]{1,0:T(8,128)(2,1)}, bf16[1536,1408]{1,0:T(8,128)(2,1)S(1)}, u32[]{:S(2)}) %copy-start.1) | copy-done | bytes 4325400
  27.2 2.0 %copy-done.7 = bf16[1536,1280]{1,0:T(8,128)(2,1)} copy-done((bf16[1536,1280]{1,0:T(8,128)(2,1)}, bf16[1536,1280]{1,0:T(8,128)(2,1)S(1)}, u32[]{:S(2)}) %copy-start.7) | copy-done | bytes 3932184
  31.4 2.2 %copy-done.2 = bf16[1536,1408]{1,0:T(8,128)(2,1)S(1)} copy-done((bf16[1536,1408]{1,0:T(8,128)(2,1)S(1)}, bf16[1536,1408]{1,0:T(8,128)(2,1)}, u32[]{:S(2)}) %copy-start.2) | copy-done | bytes 4325400
  33.6 2.1 %copy-done.8 = bf16[1536,1280]{1,0:T(8,128)(2,1)S(1)} copy-done((bf16[1536,1280]{1,0:T(8,128)(2,1)S(1)}, bf16[1536,1280]{1,0:T(8,128)(2,1)}, u32[]{:S(2)}) %copy-start.8) | copy-done | bytes 3932184
  37.3 3.7 %norm_qkv.5 = (bf16[1536,1408]{1,0:T(8,128)(2,1)S(1)}, bf16[1536,1280]{1,0:T(8,128)(2,1)S(1)}, bf16[1536,128]{1,0:T(8,128)(2,1)S(1)}) custom-call(s32[2]{0:T(128)S(1)} %pad_add_fusion.3.place, bf16[192,1536]{1,0:T(8,128)(2,1)S(1)} %collective-permute-done.refs_0_, ...), custom_call_target="tpu_custom_call", output_to_operand_aliasing={{0}: (6, {}), {1}: (7, {}), {2}: (8, {})} | custom-call | flops 2491416576 | bytes 6488064 | tf_op jit(solution)/shard_map/norm_qkv/pallas_call | solution.py:272
  41.0 3.7 %norm_qkv.6 = (bf16[1536,1408]{1,0:T(8,128)(2,1)S(1)}, bf16[1536,1280]{1,0:T(8,128)(2,1)S(1)}, bf16[1536,128]{1,0:T(8,128)(2,1)S(1)}) custom-call(s32[2]{0:T(128)S(1)} %pad_add_fusion.2.place, bf16[192,1536]{1,0:T(8,128)(2,1)S(1)} %collective-permute-done.1.refs_0_, ...), custom_call_target="tpu_custom_call", output_to_operand_aliasing={{0}: (6, {}), {1}: (7, {}), {2}: (8, {})} | custom-call | flops 2491416576 | bytes 6488064 | tf_op jit(solution)/shard_map/norm_qkv/pallas_call | solution.py:272
  44.7 2.0 %copy-done.3 = bf16[1536,1408]{1,0:T(8,128)(2,1)} copy-done((bf16[1536,1408]{1,0:T(8,128)(2,1)}, bf16[1536,1408]{1,0:T(8,128)(2,1)S(1)}, u32[]{:S(2)}) %copy-start.3) | copy-done | bytes 4325400
  46.7 2.0 %copy-done.9 = bf16[1536,1280]{1,0:T(8,128)(2,1)} copy-done((bf16[1536,1280]{1,0:T(8,128)(2,1)}, bf16[1536,1280]{1,0:T(8,128)(2,1)S(1)}, u32[]{:S(2)}) %copy-start.9) | copy-done | bytes 3932184
  51.0 2.2 %copy-done.4 = bf16[1536,1408]{1,0:T(8,128)(2,1)S(1)} copy-done((bf16[1536,1408]{1,0:T(8,128)(2,1)S(1)}, bf16[1536,1408]{1,0:T(8,128)(2,1)}, u32[]{:S(2)}) %copy-start.4) | copy-done | bytes 4325400
  53.2 2.1 %copy-done.10 = bf16[1536,1280]{1,0:T(8,128)(2,1)S(1)} copy-done((bf16[1536,1280]{1,0:T(8,128)(2,1)S(1)}, bf16[1536,1280]{1,0:T(8,128)(2,1)}, u32[]{:S(2)}) %copy-start.10) | copy-done | bytes 3932184
  56.9 3.7 %norm_qkv.7 = (bf16[1536,1408]{1,0:T(8,128)(2,1)S(1)}, bf16[1536,1280]{1,0:T(8,128)(2,1)S(1)}, bf16[1536,128]{1,0:T(8,128)(2,1)S(1)}) custom-call(s32[2]{0:T(128)S(1)} %pad_add_fusion.place, bf16[96,1536]{1,0:T(8,128)(2,1)S(1)} %collective-permute-done.3.refs_0_, ...), custom_call_target="tpu_custom_call", output_to_operand_aliasing={{0}: (8, {}), {1}: (9, {}), {2}: (10, {})} | custom-call | flops 2491416576 | bytes 6488064 | tf_op jit(solution)/shard_map/norm_qkv/pallas_call | solution.py:272
  60.6 2.0 %copy-done.5 = bf16[1536,1408]{1,0:T(8,128)(2,1)} copy-done((bf16[1536,1408]{1,0:T(8,128)(2,1)}, bf16[1536,1408]{1,0:T(8,128)(2,1)S(1)}, u32[]{:S(2)}) %copy-start.5) | copy-done | bytes 4325400
  62.6 2.0 %copy-done.11 = bf16[1536,1280]{1,0:T(8,128)(2,1)} copy-done((bf16[1536,1280]{1,0:T(8,128)(2,1)}, bf16[1536,1280]{1,0:T(8,128)(2,1)S(1)}, u32[]{:S(2)}) %copy-start.11) | copy-done | bytes 3932184
  64.7 2.1 %copy-done.12 = bf16[1536,1280]{1,0:T(8,128)(2,1)S(1)} copy-done((bf16[1536,1280]{1,0:T(8,128)(2,1)S(1)}, bf16[1536,1280]{1,0:T(8,128)(2,1)}, u32[]{:S(2)}) %copy-start.12) | copy-done | bytes 3932184
  66.8 7.0 %attention.3 = (bf16[1152,128]{1,0:T(8,128)(2,1)S(1)}, bf16[16,128]{1,0:T(8,128)(2,1)S(1)}) custom-call(s32[4]{0:T(128)S(1)} %bitcast.31, bf16[1536,128]{1,0:T(8,128)(2,1)S(1)} %get-tuple-element.47.labels, bf16[1536,1280]{1,0:T(8,128)(2,1)S(1)} %copy-done.12), custom_call_target="tpu_custom_call" | custom-call | flops 3019898880 | bytes 3932160 | tf_op jit(solution)/shard_map/attention/pallas_call | solution.py:384
  76.7 6.8 %attention.2.refs_5_ = bf16[1152,128]{1,0:T(8,128)(2,1)S(1)} custom-call(s32[4]{0:T(128)S(1)} %bitcast.32, bf16[1536,128]{1,0:T(8,128)(2,1)S(1)} %get-tuple-element.47.labels, bf16[1536,1280]{1,0:T(8,128)(2,1)S(1)} %copy-done.12), custom_call_target="tpu_custom_call" | custom-call | flops 3019898880 | bytes 3932160 | tf_op jit(solution)/shard_map/attention/pallas_call | solution.py:384
  85.6 6.4 %collective-permute-done.10.refs_7_ = bf16[1152,128]{1,0:T(8,128)(2,1)S(1)} collective-permute-done((bf16[1152,128]{1,0:T(8,128)(2,1)S(1)}, bf16[1152,128]{1,0:T(8,128)(2,1)S(1)}, u32[]{:S(2)}, u32[]{:S(2)}) %collective-permute-start.10) | collective-permute-done | bytes 294944 | tf_op jit(solution)/shard_map/ppermute | solution.py:582
  93.8 3.4 %collective-permute-done.21.refs_11_ = bf16[576,128]{1,0:T(8,128)(2,1)S(1)} collective-permute-done((bf16[576,128]{1,0:T(8,128)(2,1)S(1)}, bf16[576,128]{1,0:T(8,128)(2,1)S(1)}, u32[]{:S(2)}, u32[]{:S(2)}) %collective-permute-start.21) | collective-permute-done | bytes 147488 | tf_op jit(solution)/shard_map/ppermute | solution.py:582
  101.0 6.7 %out_merge.2.refs_17_ = bf16[192,448]{1,0:T(8,128)(2,1)S(1)} custom-call(bf16[1536,1408]{1,0:T(8,128)(2,1)S(1)} %bitcast.22, bf16[1536,1408]{1,0:T(8,128)(2,1)S(1)} %bitcast.24, f32[1,1408]{1,0:T(1,128)S(1)} %reshape.2.refs_2_, bf16[448,5632]{1,0:T(8,128)(2,1)S(1)} %bitcast.29, f32[1,448]{1,0:T(1,128)S(1)} %bitcast.25, ...), custom_call_target="tpu_custom_call" | custom-call | flops 7059013632 | bytes 15499264 | tf_op jit(solution)/shard_map/out_merge/pallas_call | solution.py:531
  110.3 2.2 %copy-done.6 = bf16[1536,1408]{1,0:T(8,128)(2,1)S(1)} copy-done((bf16[1536,1408]{1,0:T(8,128)(2,1)S(1)}, bf16[1536,1408]{1,0:T(8,128)(2,1)}, u32[]{:S(2)}) %copy-start.6) | copy-done | bytes 4325400
  112.5 2.2 %copy-done.17 = bf16[1536,1408]{1,0:T(8,128)(2,1)S(1)} copy-done((bf16[1536,1408]{1,0:T(8,128)(2,1)S(1)}, bf16[1536,1408]{1,0:T(8,128)(2,1)}, u32[]{:S(2)}) %copy-start.17) | copy-done | bytes 4325400
  114.7 2.4 %copy-done.26 = bf16[5632,448]{0,1:T(8,128)(2,1)S(1)} copy-done((bf16[5632,448]{0,1:T(8,128)(2,1)S(1)}, bf16[5632,448]{0,1:T(8,128)(2,1)}, u32[]{:S(2)}) %copy-start.26) | copy-done | bytes 5046296
  118.1 8.4 %out_merge.3 = (bf16[672,128]{1,0:T(8,128)(2,1)S(1)}, bf16[672,128]{1,0:T(8,128)(2,1)S(1)}, bf16[672,128]{1,0:T(8,128)(2,1)S(1)}, bf16[672,128]{1,0:T(8,128)(2,1)S(1)}) custom-call(bf16[1536,1408]{1,0:T(8,128)(2,1)S(1)} %copy-done.6, bf16[1536,1408]{1,0:T(8,128)(2,1)S(1)} %copy-done.17, f32[1,1408]{1,0:T(1,128)S(1)} %reshape.2.refs_2_, ...), custom_call_target="tpu_custom_call" | custom-call | flops 7059013632 | bytes 15499264 | tf_op jit(solution)/shard_map/out_merge/pallas_call | solution.py:531
  126.7 4.2 %collective-permute-start.29 = (bf16[672,128]{1,0:T(8,128)(2,1)S(1)}, bf16[672,128]{1,0:T(8,128)(2,1)S(1)}, u32[]{:S(2)}, u32[]{:S(2)}) collective-permute-start(bf16[672,128]{1,0:T(8,128)(2,1)S(1)} %get-tuple-element.60), channel_id=1, source_target_pairs={{0,3},{1,2},{2,1},{3,0},{4,7},{5,6},{6,5},{7,4},{8,11},{9,10},{10,... | collective-permute-start | bytes 516104 | tf_op jit(solution)/shard_map/ppermute | solution.py:709
  130.9 3.3 %collective-permute-done.27.refs_1_ = bf16[672,128]{1,0:T(8,128)(2,1)S(1)} collective-permute-done((bf16[672,128]{1,0:T(8,128)(2,1)S(1)}, bf16[672,128]{1,0:T(8,128)(2,1)S(1)}, u32[]{:S(2)}, u32[]{:S(2)}) %collective-permute-start.27) | collective-permute-done | bytes 172064 | tf_op jit(solution)/shard_map/ppermute | solution.py:709
  134.2 7.9 %collective-permute-done.28.refs_2_ = bf16[672,128]{1,0:T(8,128)(2,1)S(1)} collective-permute-done((bf16[672,128]{1,0:T(8,128)(2,1)S(1)}, bf16[672,128]{1,0:T(8,128)(2,1)S(1)}, u32[]{:S(2)}, u32[]{:S(2)}) %collective-permute-start.28) | collective-permute-done | bytes 172064 | tf_op jit(solution)/shard_map/ppermute | solution.py:709
  (135 shorter events, 31.3 us)
Async XLA Ops:
  5.7 14.9 %collective-permute-start.2 = (bf16[192,1536]{1,0:T(8,128)(2,1)}, bf16[192,1536]{1,0:T(8,128)(2,1)}, u32[]{:S(2)}, u32[]{:S(2)}) collective-permute-start(bf16[192,1536]{1,0:T(8,128)(2,1)} %payload.1.refs_0_), channel_id=1, source_target_pairs={{0,4},{4,0},{8,12},{12,8},{16,20},{20,16},{24,28},{28,24},{1,5},{5... | collective-permute-start | bytes 1769480 | tf_op jit(solution)/shard_map/ppermute | solution.py:582
  6.2 23.1 %collective-permute-start = (bf16[192,1536]{1,0:T(8,128)(2,1)}, bf16[192,1536]{1,0:T(8,128)(2,1)S(1)}, u32[]{:S(2)}, u32[]{:S(2)}) collective-permute-start(bf16[192,1536]{1,0:T(8,128)(2,1)} %payload.1.refs_0_), channel_id=1, source_target_pairs={{0,8},{4,12},{8,0},{12,4},{16,24},{20,28},{24,16},{28,20},{1,9},{5... | collective-permute-start | bytes 1769480 | tf_op jit(solution)/shard_map/ppermute | solution.py:582
  8.7 20.6 %collective-permute-start.1 = (bf16[192,1536]{1,0:T(8,128)(2,1)}, bf16[192,1536]{1,0:T(8,128)(2,1)S(1)}, u32[]{:S(2)}, u32[]{:S(2)}) collective-permute-start(bf16[192,1536]{1,0:T(8,128)(2,1)} %payload.1.refs_0_), channel_id=1, source_target_pairs={{0,16},{4,20},{8,24},{12,28},{16,0},{20,4},{24,8},{28,12},{1,17},{... | collective-permute-start | bytes 1769480 | tf_op jit(solution)/shard_map/ppermute | solution.py:582
  29.2 2.1 %collective-permute-start.6 = (bf16[192,1536]{1,0:T(8,128)(2,1)S(1)}, bf16[192,1536]{1,0:T(8,128)(2,1)}, u32[]{:S(2)}, u32[]{:S(2)}) collective-permute-start(bf16[192,1536]{1,0:T(8,128)(2,1)S(1)} %collective-permute-done.refs_0_), channel_id=1, source_target_pairs={{0,4},{4,0},{8,12},{12,8},{16,20},{20,16},{24,28},{28,24},{1,5},{5... | collective-permute-start | bytes 1769480 | tf_op jit(solution)/shard_map/ppermute | solution.py:582
  29.3 11.7 %collective-permute-start.5 = (bf16[192,1536]{1,0:T(8,128)(2,1)S(1)}, bf16[192,1536]{1,0:T(8,128)(2,1)}, u32[]{:S(2)}, u32[]{:S(2)}) collective-permute-start(bf16[192,1536]{1,0:T(8,128)(2,1)S(1)} %collective-permute-done.1.refs_0_), channel_id=1, source_target_pairs={{0,4},{4,0},{8,12},{12,8},{16,20},{20,16},{24,28},{28,24},{1,5},{5... | collective-permute-start | bytes 1769480 | tf_op jit(solution)/shard_map/ppermute | solution.py:582
  30.0 18.8 %collective-permute-start.3 = (bf16[96,1536]{1,0:T(8,128)(2,1)S(1)}, bf16[96,1536]{1,0:T(8,128)(2,1)S(1)}, u32[]{:S(2)}, u32[]{:S(2)}) collective-permute-start(bf16[96,1536]{1,0:T(8,128)(2,1)S(1)} %slice.18), channel_id=1, source_target_pairs={{0,16},{4,20},{8,24},{12,28},{16,0},{20,4},{24,8},{28,12},{1,17},{... | collective-permute-start | bytes 884744 | tf_op jit(solution)/shard_map/ppermute | solution.py:582
  30.5 18.2 %collective-permute-start.4 = (bf16[96,1536]{1,0:T(8,128)(2,1)S(1)}, bf16[96,1536]{1,0:T(8,128)(2,1)}, u32[]{:S(2)}, u32[]{:S(2)}) collective-permute-start(bf16[96,1536]{1,0:T(8,128)(2,1)S(1)} %slice.19), channel_id=1, source_target_pairs={{0,8},{4,12},{8,0},{12,4},{16,24},{20,28},{24,16},{28,20},{1,9},{5... | collective-permute-start | bytes 884744 | tf_op jit(solution)/shard_map/ppermute | solution.py:582
  48.7 1.6 %collective-permute-start.7 = (bf16[96,1536]{1,0:T(8,128)(2,1)S(1)}, bf16[96,1536]{1,0:T(8,128)(2,1)S(1)}, u32[]{:S(2)}, u32[]{:S(2)}) collective-permute-start(bf16[96,1536]{1,0:T(8,128)(2,1)S(1)} %collective-permute-done.3.refs_0_), channel_id=1, source_target_pairs={{0,4},{4,0},{8,12},{12,8},{16,20},{20,16},{24,28},{28,24},{1,5},{5... | collective-permute-start | bytes 884744 | tf_op jit(solution)/shard_map/ppermute | solution.py:582
  48.9 2.1 %collective-permute-start.8 = (bf16[96,1536]{1,0:T(8,128)(2,1)}, bf16[96,1536]{1,0:T(8,128)(2,1)S(1)}, u32[]{:S(2)}, u32[]{:S(2)}) collective-permute-start(bf16[96,1536]{1,0:T(8,128)(2,1)} %collective-permute-done.4.refs_1_), channel_id=1, source_target_pairs={{0,4},{4,0},{8,12},{12,8},{16,20},{20,16},{24,28},{28,24},{1,5},{5... | collective-permute-start | bytes 884744 | tf_op jit(solution)/shard_map/ppermute | solution.py:582
  56.9 44.0 %slice-start.4 = ((s8[5046272]{0:T(1024)(128)(4,1)}), s8[4194304]{0:T(1024)(128)(4,1)S(1)}, s32[]{:S(2)}) async-start(s8[5046272]{0:T(1024)(128)(4,1)} %bitcast.27), calls=%async_computation.4 | async-start | bytes 8388608
  66.8 34.2 %slice-start.5 = ((s8[5046272]{0:T(1024)(128)(4,1)}), s8[851968]{0:T(1024)(128)(4,1)S(1)}, s32[]{:S(2)}) async-start(s8[5046272]{0:T(1024)(128)(4,1)} %bitcast.27), calls=%async_computation.5 | async-start | bytes 1703936
  73.9 11.0 %collective-permute-start.17 = (bf16[1152,128]{1,0:T(8,128)(2,1)S(1)}, bf16[1152,128]{1,0:T(8,128)(2,1)S(1)}, u32[]{:S(2)}, u32[]{:S(2)}) collective-permute-start(bf16[1152,128]{1,0:T(8,128)(2,1)S(1)} %get-tuple-element.51.refs_5_), channel_id=1, source_target_pairs={{0,8},{4,12},{8,0},{12,4},{16,24},{20,28},{24,16},{28,20},{1,9},{5... | collective-permute-start | bytes 884744 | tf_op jit(solution)/shard_map/ppermute | solution.py:582
  75.1 9.8 %collective-permute-start.18 = (bf16[1152,128]{1,0:T(8,128)(2,1)S(1)}, bf16[1152,128]{1,0:T(8,128)(2,1)S(1)}, u32[]{:S(2)}, u32[]{:S(2)}) collective-permute-start(bf16[1152,128]{1,0:T(8,128)(2,1)S(1)} %get-tuple-element.51.refs_5_), channel_id=1, source_target_pairs={{0,16},{4,20},{8,24},{12,28},{16,0},{20,4},{24,8},{28,12},{1,17},{... | collective-permute-start | bytes 884744 | tf_op jit(solution)/shard_map/ppermute | solution.py:582
  83.5 8.6 %collective-permute-start.10 = (bf16[1152,128]{1,0:T(8,128)(2,1)S(1)}, bf16[1152,128]{1,0:T(8,128)(2,1)S(1)}, u32[]{:S(2)}, u32[]{:S(2)}) collective-permute-start(bf16[1152,128]{1,0:T(8,128)(2,1)S(1)} %attention.2.refs_5_), channel_id=1, source_target_pairs={{0,8},{4,12},{8,0},{12,4},{16,24},{20,28},{24,16},{28,20},{1,9},{5... | collective-permute-start | bytes 884744 | tf_op jit(solution)/shard_map/ppermute | solution.py:582
  84.1 8.5 %collective-permute-start.11 = (bf16[1152,128]{1,0:T(8,128)(2,1)S(1)}, bf16[1152,128]{1,0:T(8,128)(2,1)S(1)}, u32[]{:S(2)}, u32[]{:S(2)}) collective-permute-start(bf16[1152,128]{1,0:T(8,128)(2,1)S(1)} %attention.2.refs_5_), channel_id=1, source_target_pairs={{0,16},{4,20},{8,24},{12,28},{16,0},{20,4},{24,8},{28,12},{1,17},{... | collective-permute-start | bytes 884744 | tf_op jit(solution)/shard_map/ppermute | solution.py:582
  84.9 12.9 %collective-permute-start.16 = (bf16[1152,128]{1,0:T(8,128)(2,1)S(1)}, bf16[1152,128]{1,0:T(8,128)(2,1)S(1)}, u32[]{:S(2)}, u32[]{:S(2)}) collective-permute-start(bf16[1152,128]{1,0:T(8,128)(2,1)S(1)} %get-tuple-element.51.refs_5_), channel_id=1, source_target_pairs={{0,4},{4,0},{8,12},{12,8},{16,20},{20,16},{24,28},{28,24},{1,5},{5... | collective-permute-start | bytes 884744 | tf_op jit(solution)/shard_map/ppermute | solution.py:582
  84.9 13.4 %collective-permute-start.19 = (bf16[1152,128]{1,0:T(8,128)(2,1)S(1)}, bf16[1152,128]{1,0:T(8,128)(2,1)S(1)}, u32[]{:S(2)}, u32[]{:S(2)}) collective-permute-start(bf16[1152,128]{1,0:T(8,128)(2,1)S(1)} %collective-permute-done.17.refs_7_), channel_id=1, source_target_pairs={{0,4},{4,0},{8,12},{12,8},{16,20},{20,16},{24,28},{28,24},{1,5},{5... | collective-permute-start | bytes 884744 | tf_op jit(solution)/shard_map/ppermute | solution.py:582
  85.5 12.9 %collective-permute-start.20 = (bf16[1152,128]{1,0:T(8,128)(2,1)S(1)}, bf16[1152,128]{1,0:T(8,128)(2,1)S(1)}, u32[]{:S(2)}, u32[]{:S(2)}) collective-permute-start(bf16[1152,128]{1,0:T(8,128)(2,1)S(1)} %collective-permute-done.18.refs_9_), channel_id=1, source_target_pairs={{0,4},{4,0},{8,12},{12,8},{16,20},{20,16},{24,28},{28,24},{1,5},{5... | collective-permute-start | bytes 884744 | tf_op jit(solution)/shard_map/ppermute | solution.py:582
  92.0 5.1 %collective-permute-start.21 = (bf16[576,128]{1,0:T(8,128)(2,1)S(1)}, bf16[576,128]{1,0:T(8,128)(2,1)S(1)}, u32[]{:S(2)}, u32[]{:S(2)}) collective-permute-start(bf16[576,128]{1,0:T(8,128)(2,1)S(1)} %slice.22), channel_id=1, source_target_pairs={{0,16},{4,20},{8,24},{12,28},{16,0},{20,4},{24,8},{28,12},{1,17},{... | collective-permute-start | bytes 442376 | tf_op jit(solution)/shard_map/ppermute | solution.py:582
  92.5 5.1 %collective-permute-start.22 = (bf16[576,128]{1,0:T(8,128)(2,1)S(1)}, bf16[576,128]{1,0:T(8,128)(2,1)S(1)}, u32[]{:S(2)}, u32[]{:S(2)}) collective-permute-start(bf16[576,128]{1,0:T(8,128)(2,1)S(1)} %slice.23), channel_id=1, source_target_pairs={{0,8},{4,12},{8,0},{12,4},{16,24},{20,28},{24,16},{28,20},{1,9},{5... | collective-permute-start | bytes 442376 | tf_op jit(solution)/shard_map/ppermute | solution.py:582
  97.2 1.7 %collective-permute-start.23 = (bf16[576,128]{1,0:T(8,128)(2,1)S(1)}, bf16[576,128]{1,0:T(8,128)(2,1)S(1)}, u32[]{:S(2)}, u32[]{:S(2)}) collective-permute-start(bf16[576,128]{1,0:T(8,128)(2,1)S(1)} %collective-permute-done.21.refs_11_), channel_id=1, source_target_pairs={{0,4},{4,0},{8,12},{12,8},{16,20},{20,16},{24,28},{28,24},{1,5},{5... | collective-permute-start | bytes 442376 | tf_op jit(solution)/shard_map/ppermute | solution.py:582
  97.7 2.7 %collective-permute-start.24 = (bf16[576,128]{1,0:T(8,128)(2,1)S(1)}, bf16[576,128]{1,0:T(8,128)(2,1)S(1)}, u32[]{:S(2)}, u32[]{:S(2)}) collective-permute-start(bf16[576,128]{1,0:T(8,128)(2,1)S(1)} %collective-permute-done.22.refs_12_), channel_id=1, source_target_pairs={{0,4},{4,0},{8,12},{12,8},{16,20},{20,16},{24,28},{28,24},{1,5},{5... | collective-permute-start | bytes 442376 | tf_op jit(solution)/shard_map/ppermute | solution.py:582
  97.8 11.1 %collective-permute-start.9 = (bf16[1152,128]{1,0:T(8,128)(2,1)S(1)}, bf16[1152,128]{1,0:T(8,128)(2,1)S(1)}, u32[]{:S(2)}, u32[]{:S(2)}) collective-permute-start(bf16[1152,128]{1,0:T(8,128)(2,1)S(1)} %attention.2.refs_5_), channel_id=1, source_target_pairs={{0,4},{4,0},{8,12},{12,8},{16,20},{20,16},{24,28},{28,24},{1,5},{5... | collective-permute-start | bytes 884744 | tf_op jit(solution)/shard_map/ppermute | solution.py:582
  98.3 10.5 %collective-permute-start.12 = (bf16[1152,128]{1,0:T(8,128)(2,1)S(1)}, bf16[1152,128]{1,0:T(8,128)(2,1)S(1)}, u32[]{:S(2)}, u32[]{:S(2)}) collective-permute-start(bf16[1152,128]{1,0:T(8,128)(2,1)S(1)} %collective-permute-done.10.refs_7_), channel_id=1, source_target_pairs={{0,4},{4,0},{8,12},{12,8},{16,20},{20,16},{24,28},{28,24},{1,5},{5... | collective-permute-start | bytes 884744 | tf_op jit(solution)/shard_map/ppermute | solution.py:582
  98.4 10.4 %collective-permute-start.13 = (bf16[1152,128]{1,0:T(8,128)(2,1)S(1)}, bf16[1152,128]{1,0:T(8,128)(2,1)S(1)}, u32[]{:S(2)}, u32[]{:S(2)}) collective-permute-start(bf16[1152,128]{1,0:T(8,128)(2,1)S(1)} %collective-permute-done.11.refs_9_), channel_id=1, source_target_pairs={{0,4},{4,0},{8,12},{12,8},{16,20},{20,16},{24,28},{28,24},{1,5},{5... | collective-permute-start | bytes 884744 | tf_op jit(solution)/shard_map/ppermute | solution.py:582
  98.9 9.5 %collective-permute-start.14 = (bf16[576,128]{1,0:T(8,128)(2,1)S(1)}, bf16[576,128]{1,0:T(8,128)(2,1)S(1)}, u32[]{:S(2)}, u32[]{:S(2)}) collective-permute-start(bf16[576,128]{1,0:T(8,128)(2,1)S(1)} %slice.20), channel_id=1, source_target_pairs={{0,16},{4,20},{8,24},{12,28},{16,0},{20,4},{24,8},{28,12},{1,17},{... | collective-permute-start | bytes 442376 | tf_op jit(solution)/shard_map/ppermute | solution.py:582
  100.4 7.9 %collective-permute-start.15 = (bf16[576,128]{1,0:T(8,128)(2,1)S(1)}, bf16[576,128]{1,0:T(8,128)(2,1)}, u32[]{:S(2)}, u32[]{:S(2)}) collective-permute-start(bf16[576,128]{1,0:T(8,128)(2,1)S(1)} %slice.21), channel_id=1, source_target_pairs={{0,8},{4,12},{8,0},{12,4},{16,24},{20,28},{24,16},{28,20},{1,9},{5... | collective-permute-start | bytes 442376 | tf_op jit(solution)/shard_map/ppermute | solution.py:582
  108.3 1.5 %collective-permute-start.25 = (bf16[576,128]{1,0:T(8,128)(2,1)S(1)}, bf16[576,128]{1,0:T(8,128)(2,1)}, u32[]{:S(2)}, u32[]{:S(2)}) collective-permute-start(bf16[576,128]{1,0:T(8,128)(2,1)S(1)} %collective-permute-done.14.refs_11_), channel_id=1, source_target_pairs={{0,4},{4,0},{8,12},{12,8},{16,20},{20,16},{24,28},{28,24},{1,5},{5... | collective-permute-start | bytes 442376 | tf_op jit(solution)/shard_map/ppermute | solution.py:582
  108.3 1.9 %collective-permute-start.26 = (bf16[576,128]{1,0:T(8,128)(2,1)}, bf16[576,128]{1,0:T(8,128)(2,1)}, u32[]{:S(2)}, u32[]{:S(2)}) collective-permute-start(bf16[576,128]{1,0:T(8,128)(2,1)} %collective-permute-done.15.refs_12_), channel_id=1, source_target_pairs={{0,4},{4,0},{8,12},{12,8},{16,20},{20,16},{24,28},{28,24},{1,5},{5... | collective-permute-start | bytes 442376 | tf_op jit(solution)/shard_map/ppermute | solution.py:582
  126.4 7.8 %collective-permute-start.27 = (bf16[672,128]{1,0:T(8,128)(2,1)S(1)}, bf16[672,128]{1,0:T(8,128)(2,1)S(1)}, u32[]{:S(2)}, u32[]{:S(2)}) collective-permute-start(bf16[672,128]{1,0:T(8,128)(2,1)S(1)} %get-tuple-element.58), channel_id=1, source_target_pairs={{0,1},{1,0},{2,3},{3,2},{4,5},{5,4},{6,7},{7,6},{8,9},{9,8},{10,11... | collective-permute-start | bytes 516104 | tf_op jit(solution)/shard_map/ppermute | solution.py:709
  126.5 15.6 %collective-permute-start.28 = (bf16[672,128]{1,0:T(8,128)(2,1)S(1)}, bf16[672,128]{1,0:T(8,128)(2,1)S(1)}, u32[]{:S(2)}, u32[]{:S(2)}) collective-permute-start(bf16[672,128]{1,0:T(8,128)(2,1)S(1)} %get-tuple-element.59), channel_id=1, source_target_pairs={{0,2},{1,3},{2,0},{3,1},{4,6},{5,7},{6,4},{7,5},{8,10},{9,11},{10,... | collective-permute-start | bytes 516104 | tf_op jit(solution)/shard_map/ppermute | solution.py:709
  126.7 15.4 %collective-permute-start.29 = (bf16[672,128]{1,0:T(8,128)(2,1)S(1)}, bf16[672,128]{1,0:T(8,128)(2,1)S(1)}, u32[]{:S(2)}, u32[]{:S(2)}) collective-permute-start(bf16[672,128]{1,0:T(8,128)(2,1)S(1)} %get-tuple-element.60), channel_id=1, source_target_pairs={{0,3},{1,2},{2,1},{3,0},{4,7},{5,6},{6,5},{7,4},{8,11},{9,10},{10,... | collective-permute-start | bytes 516104 | tf_op jit(solution)/shard_map/ppermute | solution.py:709
  (37 other events, 238.0 us)

commit v4 on v3

--- a/solution.py
+++ b/solution.py
@@ -164,6 +164,10 @@
     return loaded[0] if len(loaded) == 1 else jnp.concatenate(loaded, axis=0)
 
 
+def in_hbm(value):
+    return pltpu.with_memory_space_constraint(value, pltpu.HBM)
+
+
 def payload_kernel(segments, rows, columns, mask, embed, patches, out):
     labels = [one[...].astype(jnp.float32) for one in (segments, rows, columns, mask)]
     labels.append(jnp.zeros((4, labels[0].shape[1]), jnp.float32))
@@ -201,14 +205,13 @@
             flops=count * D, bytes_accessed=4 * count * D, transcendentals=0
         ),
         name="payload",
-    )(*operands)
+    )(*map(in_hbm, operands))
 
 
 def qkv_kernel(count, place, *refs):
     first, second = refs[:count], refs[count : 2 * count]
     table, gain, weight = refs[2 * count : 2 * count + 3]
-    *outs, inputs_out, qkv_out, label_out, sems = refs[-7:]
-    start = pl.multiple_of(place[0] * inputs_out.shape[0], inputs_out.shape[0])
+    inputs_out, qkv_out, label_out = refs[-3:]
     mine, other = stacked(first), stacked(second)
     leads = place[1] == 0
     ahead = jnp.where(leads, mine, other)
@@ -216,13 +219,6 @@
     both = jnp.concatenate([ahead, behind], axis=0)
     inputs_out[...] = both[:, :D]
     label_out[...] = both[:, D:]
-    target = pl.ds(start, inputs_out.shape[0])
-    copies = [
-        pltpu.make_async_copy(source, out.at[target, :], sems.at[number])
-        for number, (source, out) in enumerate(zip((inputs_out, qkv_out, label_out), outs))
-    ]
-    copies[0].start()
-    copies[2].start()
     labels = both[:, D:].astype(jnp.float32)
     normed = norm_rows(both[:, :D].astype(jnp.float32), gain[...]).astype(jnp.bfloat16)
     columns = jnp.dot(normed, weight[...], preferred_element_type=jnp.float32)
@@ -258,35 +254,33 @@
     parts.append(jnp.where(wide < HD, values_part, ones))
     parts.append(jnp.where((wide >= HD) & (wide < 2 * HD), values_part, ones))
     qkv_out[...] = jnp.concatenate(parts, axis=1).astype(jnp.bfloat16)
-    copies[1].start()
-    for copy in copies:
-        copy.wait()
 
 
 def qkv_call(place, first, second, table, gain, weight, earlier, total):
     rows = 2 * sum(piece.shape[0] for piece in first)
+    whole = lambda shape: pl.BlockSpec(shape, lambda i, place: (0,) * len(shape))
+    block = lambda width: pl.BlockSpec((rows, width), lambda i, place: (place[0], 0))
     widths = (D, 10 * LANES, LANES)
     operands = [*first, *second, table, gain, weight]
-    vmem = pl.BlockSpec(memory_space=pltpu.VMEM)
-    anywhere = pl.BlockSpec(memory_space=pl.ANY)
     return pl.pallas_call(
         functools.partial(qkv_kernel, len(first)),
-        in_specs=[pl.BlockSpec(memory_space=pltpu.SMEM)]
-        + [vmem] * len(operands)
-        + [anywhere] * len(earlier),
-        out_specs=[anywhere] * len(widths),
-        scratch_shapes=[pltpu.VMEM((rows, width), jnp.bfloat16) for width in widths]
-        + [pltpu.SemaphoreType.DMA((len(widths),))],
-        out_shape=[jax.ShapeDtypeStruct((total, width), jnp.bfloat16) for width in widths],
+        grid_spec=pltpu.PrefetchScalarGridSpec(
+            num_scalar_prefetch=1,
+            grid=(1,),
+            in_specs=[whole(one.shape) for one in operands]
+            + [pl.BlockSpec(memory_space=pl.ANY)] * len(earlier),
+            out_specs=[block(width) for width in widths],
+        ),
+        out_shape=[pltpu.HBM((total, width), jnp.bfloat16) for width in widths],
         input_output_aliases={1 + len(operands) + i: i for i in range(len(earlier))},
-        compiler_params=pltpu.CompilerParams(vmem_limit_bytes=16 << 20),
+        compiler_params=pltpu.CompilerParams(vmem_limit_bytes=20 << 20),
         cost_estimate=pl.CostEstimate(
             flops=6 * rows * D * weight.shape[1],
             bytes_accessed=2 * (rows * 4 * D + weight.size),
             transcendentals=rows,
         ),
         name="norm_qkv",
-    )(place, *operands, *earlier)
+    )(place, *operands, *map(in_hbm, earlier))
 
 
 def segment_row(labels):
@@ -299,25 +293,40 @@
     )
 
 
-def attention_kernel(start, owners, labels, block, *refs):
+def attention_kernel(start, owners, labels, source, *refs):
     out, *rest = refs
-    scores, high, rows_scratch = rest[-3:]
+    block, scores, high, rows_scratch, sems = rest[-5:]
     rows = high.shape[1]
     total = block.shape[0]
+    steps = total // BLOCK
     factor = HD**-0.5 * float(np.log2(np.e))
+
+    def copy(step):
+        at = pl.ds(pl.multiple_of(step * BLOCK, BLOCK), BLOCK)
+        return pltpu.make_async_copy(source.at[at, :], block.at[at, :], sems.at[step])
+
+    own_steps = range(start // BLOCK, (start + rows) // BLOCK)
+    for step in [*own_steps, *(step for step in range(steps) if step not in own_steps)]:
+        copy(step).start()
     segments = segment_row(labels[...])
-    for step in range(total // BLOCK):
+    for step in range(steps):
         rows_scratch[step] = segments[:, step * BLOCK : (step + 1) * BLOCK]
     own = labels[start : start + rows, :1].astype(jnp.float32)
     lowest, largest = jnp.min(own), jnp.max(own)
     one_row = segments[:1]
     begin = jnp.sum(jnp.where(one_row < lowest, 1, 0)) // BLOCK
     end = (jnp.sum(jnp.where(one_row <= largest, 1, 0)) + BLOCK - 1) // BLOCK
-    queries = block[start : start + rows, : 2 * LANES]
     own = jnp.broadcast_to(own, (rows, LANES))
     high[...] = jnp.full_like(high, NEGATIVE)
+    for step in own_steps:
+        copy(step).wait()
+    queries = block[start : start + rows, : 2 * LANES]
 
     def score(step, carry):
+        @pl.when((step < own_steps[0]) | (step > own_steps[-1]))
+        def _():
+            copy(step).wait()
+
         at = pl.ds(pl.multiple_of(step * BLOCK, BLOCK), BLOCK)
         theirs = rows_scratch[step, :1]
         same = jnp.concatenate([own == theirs[:, :LANES], own == theirs[:, LANES:]], axis=1)
@@ -350,6 +359,13 @@
 
     zero = jnp.zeros((rows, 2 * LANES), jnp.float32)
     sums = lax.fori_loop(begin, end, weigh, (zero, zero))
+    for step in range(steps):
+        if step not in own_steps:
+
+            @pl.when((step < begin) | (step >= end))
+            def _(step=step):
+                copy(step).wait()
+
     acc = sum(one / one[:, 2 * HD : 2 * HD + 1] for one in sums)
     out[:rows] = acc[:, :LANES].astype(jnp.bfloat16)
     half = rows // 2
@@ -359,7 +375,7 @@
     packed = jnp.where(lane < tail, low, jnp.where(lane < 2 * tail, pltpu.roll(up, tail, 1), 0.0))
     out[rows:] = packed.astype(jnp.bfloat16)
 
-    if len(rest) > 3:
+    if len(rest) > 5:
         note = rest[0]
         row = lax.broadcasted_iota(jnp.int32, note.shape, 0)
         lane = lax.broadcasted_iota(jnp.int32, note.shape, 1)
@@ -377,28 +393,35 @@
 
 def attention_call(start, rows, owners, labels, block, noted):
     total = block.shape[0]
-    vmem = pl.BlockSpec(memory_space=pltpu.VMEM)
+    fixed = lambda shape: pl.BlockSpec(shape, lambda i: (0,) * len(shape))
     shapes = [jax.ShapeDtypeStruct((rows + rows // 2, LANES), jnp.bfloat16)]
     if noted:
         shapes.append(jax.ShapeDtypeStruct((16, LANES), jnp.bfloat16))
     return pl.pallas_call(
         functools.partial(attention_kernel, start),
-        in_specs=[pl.BlockSpec(memory_space=pltpu.SMEM), vmem, vmem],
-        out_specs=[vmem] * len(shapes),
+        grid=(1,),
+        in_specs=[
+            pl.BlockSpec(memory_space=pltpu.SMEM),
+            fixed(labels.shape),
+            pl.BlockSpec(memory_space=pl.ANY),
+        ],
+        out_specs=[fixed(one.shape) for one in shapes],
         out_shape=shapes,
         scratch_shapes=[
+            pltpu.VMEM(block.shape, jnp.bfloat16),
             pltpu.VMEM((2, total // BLOCK, rows, BLOCK), jnp.float32),
             pltpu.VMEM((2, rows, LANES), jnp.float32),
             pltpu.VMEM((total // BLOCK, 8, BLOCK), jnp.float32),
+            pltpu.SemaphoreType.DMA((total // BLOCK,)),
         ],
-        compiler_params=pltpu.CompilerParams(vmem_limit_bytes=22 << 20),
+        compiler_params=pltpu.CompilerParams(vmem_limit_bytes=30 << 20),
         cost_estimate=pl.CostEstimate(
             flops=10 * rows * total * 2 * LANES,
             bytes_accessed=2 * block.size,
             transcendentals=rows * total,
         ),
         name="attention",
-    )(owners, labels, block)
+    )(owners, in_hbm(labels), in_hbm(block))
 
 
 def order_kernel(shards, ids, weight, out, sems):
@@ -425,63 +448,114 @@
     shape = (shards * LANES * 3 // 2, D)
     return pl.pallas_call(
         functools.partial(order_kernel, shards),
+        grid=(1,),
         in_specs=[
             pl.BlockSpec(memory_space=pltpu.SMEM),
             pl.BlockSpec(memory_space=pl.ANY),
         ],
-        out_specs=pl.BlockSpec(memory_space=pltpu.VMEM),
-        out_shape=jax.ShapeDtypeStruct(shape, jnp.bfloat16),
+        out_specs=pl.BlockSpec(shape, lambda i: (0, 0)),
+        out_shape=pltpu.HBM(shape, jnp.bfloat16),
         scratch_shapes=[pltpu.SemaphoreType.DMA((2 * shards,))],
-        compiler_params=pltpu.CompilerParams(vmem_limit_bytes=16 << 20),
+        compiler_params=pltpu.CompilerParams(vmem_limit_bytes=12 << 20),
         cost_estimate=pl.CostEstimate(flops=0, bytes_accessed=4 * weight.size, transcendentals=0),
         name="order_rows",
-    )(ids, weight)
+    )(ids, in_hbm(weight))
+
+
+OUT_BLOCKS = ((0, 512), (512, 1024), (1024, 1408))
 
 
 def merge_kernel(start, counts, packs, last, *refs):
     inputs, weight, gain, merge_weight, bias = refs[:5]
     pieces = refs[5 : 5 + sum(counts)]
-    *refs, state = refs[5 + sum(counts) :]
+    refs = refs[5 + sum(counts) :]
+    refs, (state, lined, tails, before, out_buffer, merge_buffer, piece_sems, sems) = (
+        refs[:-8],
+        refs[-8:],
+    )
     rows = state.shape[1]
     half = rows // 2
     rest = 2 * HD - LANES
-    sources, at = [], 0
-    for count in counts:
-        sources.append(stacked(pieces[at : at + count]))
+    shards = len(counts)
+    piece_copies, at = [], 0
+    for shard, count in enumerate(counts):
+        done = 0
+        for piece in pieces[at : at + count]:
+            size = piece.shape[0]
+            for low, high, buffer, base in (
+                (done, min(done + size, rows), lined, 0),
+                (max(done, rows), done + size, tails, rows),
+            ):
+                if low < high:
+                    target = (
+                        lined.at[low:high, shard * LANES : (shard + 1) * LANES]
+                        if buffer is lined
+                        else tails.at[shard, low - base : high - base, :]
+                    )
+                    piece_copies.append((piece.at[low - done : high - done, :], target))
+            done += size
         at += count
-    shards = len(sources)
+    piece_copies = [
+        pltpu.make_async_copy(source, target, piece_sems.at[number])
+        for number, (source, target) in enumerate(piece_copies)
+    ]
+    out_copies = [
+        pltpu.make_async_copy(
+            weight.at[:, low:high], out_buffer.at[:, low:high], sems.at[number]
+        )
+        for number, (low, high) in enumerate(OUT_BLOCKS)
+    ]
+    before_copy = pltpu.make_async_copy(
+        inputs.at[start : start + rows, :], before, sems.at[len(OUT_BLOCKS)]
+    )
+    merge_copies = [
+        pltpu.make_async_copy(
+            merge_weight.at[:, quadrant * D : (quadrant + 1) * D],
+            merge_buffer.at[:, quadrant * D : (quadrant + 1) * D],
+            sems.at[len(OUT_BLOCKS) + 1 + quadrant],
+        )
+        for quadrant in range(4)
+    ]
+    for copy in [*piece_copies, out_copies[0], before_copy, *out_copies[1:], *merge_copies]:
+        copy.start()
+    for copy in piece_copies:
+        copy.wait()
     lane = lax.broadcasted_iota(jnp.int32, (half, LANES), 1)
-    for part in range(2):
-        token = slice(part * half, (part + 1) * half)
-        lined = [source[token, :] for source in sources]
-        for pair in range(shards // 2):
-            mine = sources[2 * pair][rows:, :].astype(jnp.float32)
-            other = sources[2 * pair + 1][rows:, :].astype(jnp.float32)
-            if part == 0:
-                other = pltpu.roll(other, rest, 1)
-            else:
-                mine = pltpu.roll(mine, LANES - rest, 1)
-            lined.append(jnp.where(lane < rest, mine, other).astype(jnp.bfloat16))
+    for pair in range(shards // 2):
+        mine = tails[2 * pair].astype(jnp.float32)
+        other = tails[2 * pair + 1].astype(jnp.float32)
+        column = slice((shards + pair) * LANES, (shards + pair + 1) * LANES)
+        lined[:half, column] = jnp.where(lane < rest, mine, pltpu.roll(other, rest, 1)).astype(
+            jnp.bfloat16
+        )
+        lined[half:, column] = jnp.where(
+            lane < rest, pltpu.roll(mine, LANES - rest, 1), other
+        ).astype(jnp.bfloat16)
+    for number, (low, high) in enumerate(OUT_BLOCKS):
+        out_copies[number].wait()
         mixed = jnp.dot(
-            jnp.concatenate(lined, axis=1), weight[...], preferred_element_type=jnp.float32
-        )
-        before = inputs[start + part * half : start + (part + 1) * half, :].astype(jnp.float32)
-        normed = norm_rows(before + mixed, gain[...])
-        for column in range(D // LANES):
-            state[column, token, :] = normed[:, column * LANES : (column + 1) * LANES]
+            lined[...], out_buffer[:, low:high], preferred_element_type=jnp.float32
+        )
+        if number == 0:
+            before_copy.wait()
+        mixed = before[:, low:high].astype(jnp.float32) + mixed
+        for column in range(low // LANES, high // LANES):
+            state[column] = mixed[:, column * LANES - low : (column + 1) * LANES - low]
     groups = rows // 4
     total = bias[...]
     for quadrant in range(4):
-        tokens = jnp.concatenate(
+        residual = jnp.concatenate(
             [
-                state[column, pl.ds(quadrant, groups, stride=4), :].astype(jnp.bfloat16)
+                state[column, pl.ds(quadrant, groups, stride=4), :]
                 for column in range(D // LANES)
             ],
             axis=1,
         )
+        tokens = norm_rows(residual, gain[...]).astype(jnp.bfloat16)
+        merge_copies[quadrant].wait()
         total = total + lax.dot_general(
             tokens,
-            merge_weight[:, quadrant * D : (quadrant + 1) * D],
+            merge_buffer[:, quadrant * D : (quadrant + 1) * D],
             (((1,), (1,)), ((), ())),
             preferred_element_type=jnp.float32,
         )
@@ -518,25 +592,38 @@
 def merge_call(start, rows, sources, inputs, weight, gain, merge_weight, bias, packs, route):
     groups = rows // 4
     width = merge_weight.shape[0]
+    shards = len(sources)
     pieces = [piece for source in sources for piece in source]
-    vmem = pl.BlockSpec(memory_space=pltpu.VMEM)
-    operands = [inputs, weight, gain, merge_weight, bias, *pieces]
-    specs = [vmem] * len(operands)
+    fixed = lambda shape: pl.BlockSpec(shape, lambda i: (0,) * len(shape))
+    anywhere = pl.BlockSpec(memory_space=pl.ANY)
+    operands = [in_hbm(inputs), in_hbm(weight), gain, in_hbm(merge_weight), bias, *pieces]
+    specs = [anywhere, anywhere, fixed(gain.shape), anywhere, fixed(bias.shape)]
+    specs += [anywhere] * len(pieces)
     shapes = [jax.ShapeDtypeStruct((groups, width), jnp.bfloat16)]
     if route:
         me, most, *others = route
         operands += [me, *others]
-        specs += [pl.BlockSpec(memory_space=pltpu.SMEM)] + [vmem] * len(others)
+        specs += [pl.BlockSpec(memory_space=pltpu.SMEM)] + [fixed(one.shape) for one in others]
         shapes = [jax.ShapeDtypeStruct((most * width // LANES, LANES), jnp.bfloat16)] * packs
     return pl.pallas_call(
         functools.partial(
             merge_kernel, start, [len(source) for source in sources], packs, bool(route)
         ),
+        grid=(1,),
         in_specs=specs,
-        out_specs=[vmem] * len(shapes),
-        scratch_shapes=[pltpu.VMEM((D // LANES, rows, LANES), jnp.float32)],
+        out_specs=[fixed(one.shape) for one in shapes],
+        scratch_shapes=[
+            pltpu.VMEM((D // LANES, rows, LANES), jnp.float32),
+            pltpu.VMEM((rows, weight.shape[0]), jnp.bfloat16),
+            pltpu.VMEM((shards, rows // 2, LANES), jnp.bfloat16),
+            pltpu.VMEM((rows, D), jnp.bfloat16),
+            pltpu.VMEM(weight.shape, jnp.bfloat16),
+            pltpu.VMEM(merge_weight.shape, jnp.bfloat16),
+            pltpu.SemaphoreType.DMA((3 * shards,)),
+            pltpu.SemaphoreType.DMA((len(OUT_BLOCKS) + 5,)),
+        ],
         out_shape=shapes,
-        compiler_params=pltpu.CompilerParams(vmem_limit_bytes=26 << 20),
+        compiler_params=pltpu.CompilerParams(vmem_limit_bytes=30 << 20),
         cost_estimate=pl.CostEstimate(
             flops=4 * rows * D * D + 2 * groups * merge_weight.size,
             bytes_accessed=2 * (D * D + merge_weight.size + 3 * rows * D),
@@ -563,12 +650,14 @@
 
 
 def place_call(me, blocks, most, width):
-    vmem = pl.BlockSpec(memory_space=pltpu.VMEM)
+    fixed = lambda shape: pl.BlockSpec(shape, lambda i: (0,) * len(shape))
+    shape = (len(blocks), most, width)
     return pl.pallas_call(
         place_kernel,
-        in_specs=[pl.BlockSpec(memory_space=pltpu.SMEM)] + [vmem] * len(blocks),
-        out_specs=vmem,
-        out_shape=jax.ShapeDtypeStruct((len(blocks), most, width), jnp.bfloat16),
+        grid=(1,),
+        in_specs=[pl.BlockSpec(memory_space=pltpu.SMEM)] + [fixed(one.shape) for one in blocks],
+        out_specs=fixed(shape),
+        out_shape=jax.ShapeDtypeStruct(shape, jnp.bfloat16),
         compiler_params=pltpu.CompilerParams(vmem_limit_bytes=8 << 20),
         cost_estimate=pl.CostEstimate(
             flops=0, bytes_accessed=4 * len(blocks) * most * width, transcendentals=0

time: 145 us -> 125 us (0.86); the launches traced: 143 us -> 125 us
  local copies, waits for them, and re-layouts: 44.4 us -> 5.72 us
  Pallas kernels: 50 us -> 66.4 us
  waiting for transfers between devices: 25.4 us -> 27.5 us
  starting transfers between devices: 20.8 us -> 22.7 us
    unnamed x78 -> x22, local copies, waits for them, and re-layouts: 43.5 us -> 4.85 us
    pallas_call x2, Pallas kernels: 15 us -> 24.1 us  [merge_call(): pl.pallas_call(functools.partial(merge_kernel, start, [len(source) for so...]
    pallas_call x8, Pallas kernels: 33.8 us -> 40.7 us  [the longest x2 17.5 us: attention_call(): pl.pallas_call(functools.partial(attention_kernel, start), grid=(1,), in_...]
    ppermute x27, starting transfers between devices: 16.4 us -> 18.3 us  [send_seq(): return lax.ppermute(value, 'seq', [(i, i ^ flip) for i in range(size)])]
  transfers between devices with their start and end apart: 30 -> 30, of which waited for: 10 -> 11; matrix products, arithmetic and copies ran while one was open for 2% -> 2% of each run, Pallas kernels for 20% -> 29%
where the time goes in v4:
time: 125 us
  Pallas kernels  66.4 us (53%)
  waiting for transfers between devices  27.5 us (22%)
  starting transfers between devices  22.7 us (18%)
  local copies, waits for them, and re-layouts  5.72 us (5%)
  matrix products  1.93 us (2%)
    pallas_call x2, Pallas kernels, merge_call(): pl.pallas_call(functools.partial(merge_kernel, start, [len(source) for so...  24.1 us
    ppermute x27, starting transfers between devices, send_seq(): return lax.ppermute(value, 'seq', [(i, i ^ flip) for i in range(size)])  18.3 us
    pallas_call x2, Pallas kernels, attention_call(): pl.pallas_call(functools.partial(attention_kernel, start), grid=(1,), in_...  17.5 us
    pallas_call x4, Pallas kernels, qkv_call(): pl.pallas_call(functools.partial(qkv_kernel, len(first)), grid_spec=pltpu...  17.3 us
    ppermute x27, waiting for transfers between devices, send_seq(): return lax.ppermute(value, 'seq', [(i, i ^ flip) for i in range(size)])  15 us
    ppermute x3, waiting for transfers between devices, fast_local(): lax.ppermute(made[flip], 'pack', [(z, z ^ flip) for z in range(packs)])  12.5 us
    pallas_call x1, Pallas kernels, order_call(): pl.pallas_call(functools.partial(order_kernel, shards), grid=(1,), in_spe...  4.89 us
    unnamed x22, local copies, waits for them, and re-layouts  4.85 us
  transfers between devices with their start and end apart: 30, of which 11 were waited for; matrix products, arithmetic and copies ran while one was open for 2% of the time, Pallas kernels for 29%

profile of v4, /device:TPU:0, one launch (start us, length us, event | category | flops | bytes accessed | tf_op | source)
XLA Modules:
  0.0 124.7 jit_solution(3821635828349024944)
XLA Ops:
  0.0 1.6 %payload.1.refs_0_ = bf16[192,1536]{1,0:T(8,128)(2,1)S(1)} custom-call(s32[1,192]{1,0:T(1,128)} %segments.1, s32[1,192]{1,0:T(1,128)} %rows.1, s32[1,192]{1,0:T(1,128)} %columns.1, s32[1,192]{1,0:T(1,128)} %mask.1, bf16[1408]{0:T(1024)(128)(2,1)} %embed.1, bf16[1,192,1408]{2,1,0:T(8,128)(2,1)} %patches.1), custom_call_target="tpu_custom_call" | custom-call | flops 270336 | bytes 1081344 | tf_op jit(solution)/shard_map/payload/pallas_call | solution.py:197
  2.1 2.6 %collective-permute-start = (bf16[192,1536]{1,0:T(8,128)(2,1)S(1)}, bf16[192,1536]{1,0:T(8,128)(2,1)S(1)}, u32[]{:S(2)}, u32[]{:S(2)}) collective-permute-start(bf16[192,1536]{1,0:T(8,128)(2,1)S(1)} %payload.1.refs_0_), channel_id=1, source_target_pairs={{0,8},{4,12},{8,0},{12,4},{16,24},{20,28},{24,16},{28,20},{1,9},{5... | collective-permute-start | bytes 1769480 | tf_op jit(solution)/shard_map/ppermute | solution.py:671
  4.7 1.5 %collective-permute-start.1 = (bf16[192,1536]{1,0:T(8,128)(2,1)S(1)}, bf16[192,1536]{1,0:T(8,128)(2,1)S(1)}, u32[]{:S(2)}, u32[]{:S(2)}) collective-permute-start(bf16[192,1536]{1,0:T(8,128)(2,1)S(1)} %payload.1.refs_0_), channel_id=1, source_target_pairs={{0,16},{4,20},{8,24},{12,28},{16,0},{20,4},{24,8},{28,12},{1,17},{... | collective-permute-start | bytes 1769480 | tf_op jit(solution)/shard_map/ppermute | solution.py:671
  7.0 4.9 %order_rows.1.refs_1_ = bf16[1536,1408]{1,0:T(8,128)(2,1)} custom-call(s32[8]{0:T(128)S(1)} %stack.70.ids, bf16[1408,1408]{1,0:T(8,128)(2,1)} %weight.1), custom_call_target="tpu_custom_call" | custom-call | bytes 7929856 | tf_op jit(solution)/shard_map/order_rows/pallas_call | solution.py:449
  12.0 1.9 %fusion.refs_4_.refs_6_ = bf16[1408,768]{1,0:T(8,128)(2,1)S(1)} fusion(bf16[1408,528]{0,1:T(8,128)(2,1)S(1)} %copy-done, s32[768]{0:T(1024)S(1)} %copy-done.10), kind=kOutput, calls=%fused_computation.1 | convolution fusion | flops 1143386112 | bytes 3652608 | tf_op jit(solution)/shard_map/dot_general | solution.py:749
  13.9 4.7 %norm_qkv.4 = (bf16[1536,1408]{1,0:T(8,128)(2,1)}, bf16[1536,1280]{1,0:T(8,128)(2,1)}, bf16[1536,128]{1,0:T(8,128)(2,1)}) custom-call(s32[2]{0:T(128)S(1)} %pad_add_fusion.1.place, bf16[192,1536]{1,0:T(8,128)(2,1)S(1)} %payload.1.refs_0_, bf16[192,1536]{1,0:T(8,128)(2,1)} %collective-permute-done.2.refs_1_, bf16[128,512]{1,0:T(8,128)(2,1)S(1)} %copy-done.4, ...), custom_call_target="tpu_custom_call" | custom-call | flops 2491416576 | bytes 6488064 | tf_op jit(solution)/shard_map/norm_qkv/pallas_call | solution.py:265
  18.6 1.4 %collective-permute-done.1.refs_0_ = bf16[192,1536]{1,0:T(8,128)(2,1)S(1)} collective-permute-done((bf16[192,1536]{1,0:T(8,128)(2,1)S(1)}, bf16[192,1536]{1,0:T(8,128)(2,1)S(1)}, u32[]{:S(2)}, u32[]{:S(2)}) %collective-permute-start.1) | collective-permute-done | bytes 589856 | tf_op jit(solution)/shard_map/ppermute | solution.py:671
  20.8 1.6 %collective-permute-start.3 = (bf16[96,1536]{1,0:T(8,128)(2,1)S(1)}, bf16[96,1536]{1,0:T(8,128)(2,1)}, u32[]{:S(2)}, u32[]{:S(2)}) collective-permute-start(bf16[96,1536]{1,0:T(8,128)(2,1)S(1)} %slice.18), channel_id=1, source_target_pairs={{0,16},{4,20},{8,24},{12,28},{16,0},{20,4},{24,8},{28,12},{1,17},{... | collective-permute-start | bytes 884744 | tf_op jit(solution)/shard_map/ppermute | solution.py:671
  23.0 1.6 %copy-done.2 = bf16[1408,768]{1,0:T(8,128)(2,1)S(1)} copy-done((bf16[1408,768]{1,0:T(8,128)(2,1)S(1)}, bf16[1408,768]{1,0:T(8,128)(2,1)}, u32[]{:S(2)}) %copy-start.2) | copy-done | bytes 2162712
  24.6 4.5 %norm_qkv.5 = (bf16[1536,1408]{1,0:T(8,128)(2,1)}, bf16[1536,1280]{1,0:T(8,128)(2,1)}, bf16[1536,128]{1,0:T(8,128)(2,1)}) custom-call(s32[2]{0:T(128)S(1)} %pad_add_fusion.3.place, bf16[192,1536]{1,0:T(8,128)(2,1)S(1)} %collective-permute-done.refs_0_, ...), custom_call_target="tpu_custom_call", output_to_operand_aliasing={{0}: (6, {}), {1}: (7, {}), {2}: (8, {})} | custom-call | flops 2491416576 | bytes 6488064 | tf_op jit(solution)/shard_map/norm_qkv/pallas_call | solution.py:265
  29.2 3.5 %norm_qkv.6 = (bf16[1536,1408]{1,0:T(8,128)(2,1)}, bf16[1536,1280]{1,0:T(8,128)(2,1)}, bf16[1536,128]{1,0:T(8,128)(2,1)}) custom-call(s32[2]{0:T(128)S(1)} %pad_add_fusion.2.place, bf16[192,1536]{1,0:T(8,128)(2,1)S(1)} %collective-permute-done.1.refs_0_, ...), custom_call_target="tpu_custom_call", output_to_operand_aliasing={{0}: (6, {}), {1}: (7, {}), {2}: (8, {})} | custom-call | flops 2491416576 | bytes 6488064 | tf_op jit(solution)/shard_map/norm_qkv/pallas_call | solution.py:265
  33.2 1.2 collective-permute-done.7.refs_2_
  34.9 1.6 %copy-done.3 = bf16[1408,768]{1,0:T(8,128)(2,1)S(1)} copy-done((bf16[1408,768]{1,0:T(8,128)(2,1)S(1)}, bf16[1408,768]{1,0:T(8,128)(2,1)}, u32[]{:S(2)}) %copy-start.3) | copy-done | bytes 2162712
  36.5 4.5 %norm_qkv.7 = (bf16[1536,1408]{1,0:T(8,128)(2,1)}, bf16[1536,1280]{1,0:T(8,128)(2,1)}, bf16[1536,128]{1,0:T(8,128)(2,1)}) custom-call(s32[2]{0:T(128)S(1)} %pad_add_fusion.place, bf16[96,1536]{1,0:T(8,128)(2,1)} %collective-permute-done.3.refs_0_, ...), custom_call_target="tpu_custom_call", output_to_operand_aliasing={{0}: (8, {}), {1}: (9, {}), {2}: (10, {})} | custom-call | flops 2491416576 | bytes 6488064 | tf_op jit(solution)/shard_map/norm_qkv/pallas_call | solution.py:265
  41.0 8.7 %attention.3 = (bf16[1152,128]{1,0:T(8,128)(2,1)S(1)}, bf16[16,128]{1,0:T(8,128)(2,1)S(1)}) custom-call(s32[4]{0:T(128)S(1)} %bitcast.23, bf16[1536,128]{1,0:T(8,128)(2,1)} %get-tuple-element.47.labels, bf16[1536,1280]{1,0:T(8,128)(2,1)} %get-tuple-element.48.source), custom_call_target="tpu_custom_call" | custom-call | flops 3019898880 | bytes 3932160 | tf_op jit(solution)/shard_map/attention/pallas_call | solution.py:400
  49.8 1.5 %collective-permute-start.17 = (bf16[1152,128]{1,0:T(8,128)(2,1)S(1)}, bf16[1152,128]{1,0:T(8,128)(2,1)S(1)}, u32[]{:S(2)}, u32[]{:S(2)}) collective-permute-start(bf16[1152,128]{1,0:T(8,128)(2,1)S(1)} %get-tuple-element.51.refs_5_), channel_id=1, source_target_pairs={{0,8},{4,12},{8,0},{12,4},{16,24},{20,28},{24,16},{28,20},{1,9},{5... | collective-permute-start | bytes 884744 | tf_op jit(solution)/shard_map/ppermute | solution.py:671
  51.9 8.8 %attention.2.refs_5_ = bf16[1152,128]{1,0:T(8,128)(2,1)S(1)} custom-call(s32[4]{0:T(128)S(1)} %bitcast.24, bf16[1536,128]{1,0:T(8,128)(2,1)} %get-tuple-element.47.labels, bf16[1536,1280]{1,0:T(8,128)(2,1)} %get-tuple-element.48.source), custom_call_target="tpu_custom_call" | custom-call | flops 3019898880 | bytes 3932160 | tf_op jit(solution)/shard_map/attention/pallas_call | solution.py:400
  60.7 1.5 %collective-permute-start.10 = (bf16[1152,128]{1,0:T(8,128)(2,1)S(1)}, bf16[1152,128]{1,0:T(8,128)(2,1)S(1)}, u32[]{:S(2)}, u32[]{:S(2)}) collective-permute-start(bf16[1152,128]{1,0:T(8,128)(2,1)S(1)} %attention.2.refs_5_), channel_id=1, source_target_pairs={{0,8},{4,12},{8,0},{12,4},{16,24},{20,28},{24,16},{28,20},{1,9},{5... | collective-permute-start | bytes 884744 | tf_op jit(solution)/shard_map/ppermute | solution.py:671
  63.4 5.8 %collective-permute-done.10.refs_7_ = bf16[1152,128]{1,0:T(8,128)(2,1)S(1)} collective-permute-done((bf16[1152,128]{1,0:T(8,128)(2,1)S(1)}, bf16[1152,128]{1,0:T(8,128)(2,1)S(1)}, u32[]{:S(2)}, u32[]{:S(2)}) %collective-permute-start.10) | collective-permute-done | bytes 294944 | tf_op jit(solution)/shard_map/ppermute | solution.py:671
  69.2 1.4 %collective-permute-start.21 = (bf16[576,128]{1,0:T(8,128)(2,1)S(1)}, bf16[576,128]{1,0:T(8,128)(2,1)S(1)}, u32[]{:S(2)}, u32[]{:S(2)}) collective-permute-start(bf16[576,128]{1,0:T(8,128)(2,1)S(1)} %slice.22), channel_id=1, source_target_pairs={{0,16},{4,20},{8,24},{12,28},{16,0},{20,4},{24,8},{28,12},{1,17},{... | collective-permute-start | bytes 442376 | tf_op jit(solution)/shard_map/ppermute | solution.py:671
  71.2 3.1 %collective-permute-done.21.refs_11_ = bf16[576,128]{1,0:T(8,128)(2,1)S(1)} collective-permute-done((bf16[576,128]{1,0:T(8,128)(2,1)S(1)}, bf16[576,128]{1,0:T(8,128)(2,1)S(1)}, u32[]{:S(2)}, u32[]{:S(2)}) %collective-permute-start.21) | collective-permute-done | bytes 147488 | tf_op jit(solution)/shard_map/ppermute | solution.py:671
  74.4 1.4 %collective-permute-done.22.refs_12_ = bf16[576,128]{1,0:T(8,128)(2,1)S(1)} collective-permute-done((bf16[576,128]{1,0:T(8,128)(2,1)S(1)}, bf16[576,128]{1,0:T(8,128)(2,1)S(1)}, u32[]{:S(2)}, u32[]{:S(2)}) %collective-permute-start.22) | collective-permute-done | bytes 147488 | tf_op jit(solution)/shard_map/ppermute | solution.py:671
  77.6 1.4 %collective-permute-start.15 = (bf16[576,128]{1,0:T(8,128)(2,1)S(1)}, bf16[576,128]{1,0:T(8,128)(2,1)}, u32[]{:S(2)}, u32[]{:S(2)}) collective-permute-start(bf16[576,128]{1,0:T(8,128)(2,1)S(1)} %slice.21), channel_id=1, source_target_pairs={{0,8},{4,12},{8,0},{12,4},{16,24},{20,28},{24,16},{28,20},{1,9},{5... | collective-permute-start | bytes 442376 | tf_op jit(solution)/shard_map/ppermute | solution.py:671
  79.0 10.3 %out_merge.2.refs_17_ = bf16[192,448]{1,0:T(8,128)(2,1)S(1)} custom-call(bf16[1536,1408]{1,0:T(8,128)(2,1)} %get-tuple-element.46.refs_0_, bf16[1536,1408]{1,0:T(8,128)(2,1)} %order_rows.1.refs_1_, f32[1,1408]{1,0:T(1,128)S(1)} %reshape.2.refs_2_, bf16[448,5632]{1,0:T(8,128)(2,1)} %bitcast.25, f32[1,448]{1,0:T(1,128)S(1)} %bitcast.21, ...), custom_call_target="tpu_custom_call" | custom-call | flops 7059013632 | bytes 15499264 | tf_op jit(solution)/shard_map/out_merge/pallas_call | solution.py:608
  90.5 1.0 collective-permute-done.25.refs_13_
  91.9 0.9 copy-done.7
  92.8 13.8 %out_merge.3 = (bf16[672,128]{1,0:T(8,128)(2,1)S(1)}, bf16[672,128]{1,0:T(8,128)(2,1)S(1)}, bf16[672,128]{1,0:T(8,128)(2,1)S(1)}, bf16[672,128]{1,0:T(8,128)(2,1)S(1)}) custom-call(bf16[1536,1408]{1,0:T(8,128)(2,1)} %get-tuple-element.46.refs_0_, bf16[1536,1408]{1,0:T(8,128)(2,1)} %order_rows.1.refs_1_, f32[1,1408]{1,0:T(1,128)S(1)} %reshape.2.refs_2_, ...), custom_call_target="tpu_custom_call" | custom-call | flops 7059013632 | bytes 15499264 | tf_op jit(solution)/shard_map/out_merge/pallas_call | solution.py:608
  106.7 1.4 %collective-permute-start.27 = (bf16[672,128]{1,0:T(8,128)(2,1)S(1)}, bf16[672,128]{1,0:T(8,128)(2,1)S(1)}, u32[]{:S(2)}, u32[]{:S(2)}) collective-permute-start(bf16[672,128]{1,0:T(8,128)(2,1)S(1)} %get-tuple-element.58), channel_id=1, source_target_pairs={{0,1},{1,0},{2,3},{3,2},{4,5},{5,4},{6,7},{7,6},{8,9},{9,8},{10,11... | collective-permute-start | bytes 516104 | tf_op jit(solution)/shard_map/ppermute | solution.py:798
  108.4 2.7 %collective-permute-start.29 = (bf16[672,128]{1,0:T(8,128)(2,1)S(1)}, bf16[672,128]{1,0:T(8,128)(2,1)S(1)}, u32[]{:S(2)}, u32[]{:S(2)}) collective-permute-start(bf16[672,128]{1,0:T(8,128)(2,1)S(1)} %get-tuple-element.60), channel_id=1, source_target_pairs={{0,3},{1,2},{2,1},{3,0},{4,7},{5,6},{6,5},{7,4},{8,11},{9,10},{10,... | collective-permute-start | bytes 516104 | tf_op jit(solution)/shard_map/ppermute | solution.py:798
  111.2 5.0 %collective-permute-done.27.refs_1_ = bf16[672,128]{1,0:T(8,128)(2,1)S(1)} collective-permute-done((bf16[672,128]{1,0:T(8,128)(2,1)S(1)}, bf16[672,128]{1,0:T(8,128)(2,1)S(1)}, u32[]{:S(2)}, u32[]{:S(2)}) %collective-permute-start.27) | collective-permute-done | bytes 172064 | tf_op jit(solution)/shard_map/ppermute | solution.py:798
  116.1 7.6 %collective-permute-done.28.refs_2_ = bf16[672,128]{1,0:T(8,128)(2,1)S(1)} collective-permute-done((bf16[672,128]{1,0:T(8,128)(2,1)S(1)}, bf16[672,128]{1,0:T(8,128)(2,1)S(1)}, u32[]{:S(2)}, u32[]{:S(2)}) %collective-permute-start.28) | collective-permute-done | bytes 172064 | tf_op jit(solution)/shard_map/ppermute | solution.py:798
  123.7 1.1 place_rows.1
  (76 shorter events, 10.0 us)
Async XLA Ops:
  1.6 12.3 %collective-permute-start.2 = (bf16[192,1536]{1,0:T(8,128)(2,1)S(1)}, bf16[192,1536]{1,0:T(8,128)(2,1)}, u32[]{:S(2)}, u32[]{:S(2)}) collective-permute-start(bf16[192,1536]{1,0:T(8,128)(2,1)S(1)} %payload.1.refs_0_), channel_id=1, source_target_pairs={{0,4},{4,0},{8,12},{12,8},{16,20},{20,16},{24,28},{28,24},{1,5},{5... | collective-permute-start | bytes 1769480 | tf_op jit(solution)/shard_map/ppermute | solution.py:671
  2.1 16.5 %collective-permute-start = (bf16[192,1536]{1,0:T(8,128)(2,1)S(1)}, bf16[192,1536]{1,0:T(8,128)(2,1)S(1)}, u32[]{:S(2)}, u32[]{:S(2)}) collective-permute-start(bf16[192,1536]{1,0:T(8,128)(2,1)S(1)} %payload.1.refs_0_), channel_id=1, source_target_pairs={{0,8},{4,12},{8,0},{12,4},{16,24},{20,28},{24,16},{28,20},{1,9},{5... | collective-permute-start | bytes 1769480 | tf_op jit(solution)/shard_map/ppermute | solution.py:671
  4.7 15.4 %collective-permute-start.1 = (bf16[192,1536]{1,0:T(8,128)(2,1)S(1)}, bf16[192,1536]{1,0:T(8,128)(2,1)S(1)}, u32[]{:S(2)}, u32[]{:S(2)}) collective-permute-start(bf16[192,1536]{1,0:T(8,128)(2,1)S(1)} %payload.1.refs_0_), channel_id=1, source_target_pairs={{0,16},{4,20},{8,24},{12,28},{16,0},{20,4},{24,8},{28,12},{1,17},{... | collective-permute-start | bytes 1769480 | tf_op jit(solution)/shard_map/ppermute | solution.py:671
  20.1 2.9 %collective-permute-start.6 = (bf16[192,1536]{1,0:T(8,128)(2,1)S(1)}, bf16[192,1536]{1,0:T(8,128)(2,1)}, u32[]{:S(2)}, u32[]{:S(2)}) collective-permute-start(bf16[192,1536]{1,0:T(8,128)(2,1)S(1)} %collective-permute-done.refs_0_), channel_id=1, source_target_pairs={{0,4},{4,0},{8,12},{12,8},{16,20},{20,16},{24,28},{28,24},{1,5},{5... | collective-permute-start | bytes 1769480 | tf_op jit(solution)/shard_map/ppermute | solution.py:671
  20.1 9.1 %collective-permute-start.5 = (bf16[192,1536]{1,0:T(8,128)(2,1)S(1)}, bf16[192,1536]{1,0:T(8,128)(2,1)S(1)}, u32[]{:S(2)}, u32[]{:S(2)}) collective-permute-start(bf16[192,1536]{1,0:T(8,128)(2,1)S(1)} %collective-permute-done.1.refs_0_), channel_id=1, source_target_pairs={{0,4},{4,0},{8,12},{12,8},{16,20},{20,16},{24,28},{28,24},{1,5},{5... | collective-permute-start | bytes 1769480 | tf_op jit(solution)/shard_map/ppermute | solution.py:671
  20.8 11.9 %collective-permute-start.3 = (bf16[96,1536]{1,0:T(8,128)(2,1)S(1)}, bf16[96,1536]{1,0:T(8,128)(2,1)}, u32[]{:S(2)}, u32[]{:S(2)}) collective-permute-start(bf16[96,1536]{1,0:T(8,128)(2,1)S(1)} %slice.18), channel_id=1, source_target_pairs={{0,16},{4,20},{8,24},{12,28},{16,0},{20,4},{24,8},{28,12},{1,17},{... | collective-permute-start | bytes 884744 | tf_op jit(solution)/shard_map/ppermute | solution.py:671
  22.4 10.3 %collective-permute-start.4 = (bf16[96,1536]{1,0:T(8,128)(2,1)S(1)}, bf16[96,1536]{1,0:T(8,128)(2,1)}, u32[]{:S(2)}, u32[]{:S(2)}) collective-permute-start(bf16[96,1536]{1,0:T(8,128)(2,1)S(1)} %slice.19), channel_id=1, source_target_pairs={{0,8},{4,12},{8,0},{12,4},{16,24},{20,28},{24,16},{28,20},{1,9},{5... | collective-permute-start | bytes 884744 | tf_op jit(solution)/shard_map/ppermute | solution.py:671
  32.7 1.8 %collective-permute-start.7 = (bf16[96,1536]{1,0:T(8,128)(2,1)}, bf16[96,1536]{1,0:T(8,128)(2,1)S(1)}, u32[]{:S(2)}, u32[]{:S(2)}) collective-permute-start(bf16[96,1536]{1,0:T(8,128)(2,1)} %collective-permute-done.3.refs_0_), channel_id=1, source_target_pairs={{0,4},{4,0},{8,12},{12,8},{16,20},{20,16},{24,28},{28,24},{1,5},{5... | collective-permute-start | bytes 884744 | tf_op jit(solution)/shard_map/ppermute | solution.py:671
  32.8 2.1 %collective-permute-start.8 = (bf16[96,1536]{1,0:T(8,128)(2,1)}, bf16[96,1536]{1,0:T(8,128)(2,1)S(1)}, u32[]{:S(2)}, u32[]{:S(2)}) collective-permute-start(bf16[96,1536]{1,0:T(8,128)(2,1)} %collective-permute-done.4.refs_1_), channel_id=1, source_target_pairs={{0,4},{4,0},{8,12},{12,8},{16,20},{20,16},{24,28},{28,24},{1,5},{5... | collective-permute-start | bytes 884744 | tf_op jit(solution)/shard_map/ppermute | solution.py:671
  49.7 26.0 %copy-start.8 = (bf16[1408]{0:T(1024)(128)(2,1)S(1)}, bf16[1408]{0:T(1024)(128)(2,1)}, u32[]{:S(2)}) copy-start(bf16[1408]{0:T(1024)(128)(2,1)} %param.24) | copy-start | bytes 8452
  49.7 26.0 %copy-start.9 = (bf16[448]{0:T(512)(128)(2,1)S(1)}, bf16[448]{0:T(512)(128)(2,1)}, u32[]{:S(2)}) copy-start(bf16[448]{0:T(512)(128)(2,1)} %param.26) | copy-start | bytes 2692
  49.8 13.0 %collective-permute-start.17 = (bf16[1152,128]{1,0:T(8,128)(2,1)S(1)}, bf16[1152,128]{1,0:T(8,128)(2,1)S(1)}, u32[]{:S(2)}, u32[]{:S(2)}) collective-permute-start(bf16[1152,128]{1,0:T(8,128)(2,1)S(1)} %get-tuple-element.51.refs_5_), channel_id=1, source_target_pairs={{0,8},{4,12},{8,0},{12,4},{16,24},{20,28},{24,16},{28,20},{1,9},{5... | collective-permute-start | bytes 884744 | tf_op jit(solution)/shard_map/ppermute | solution.py:671
  51.2 11.5 %collective-permute-start.18 = (bf16[1152,128]{1,0:T(8,128)(2,1)S(1)}, bf16[1152,128]{1,0:T(8,128)(2,1)S(1)}, u32[]{:S(2)}, u32[]{:S(2)}) collective-permute-start(bf16[1152,128]{1,0:T(8,128)(2,1)S(1)} %get-tuple-element.51.refs_5_), channel_id=1, source_target_pairs={{0,16},{4,20},{8,24},{12,28},{16,0},{20,4},{24,8},{28,12},{1,17},{... | collective-permute-start | bytes 884744 | tf_op jit(solution)/shard_map/ppermute | solution.py:671
  60.7 8.6 %collective-permute-start.10 = (bf16[1152,128]{1,0:T(8,128)(2,1)S(1)}, bf16[1152,128]{1,0:T(8,128)(2,1)S(1)}, u32[]{:S(2)}, u32[]{:S(2)}) collective-permute-start(bf16[1152,128]{1,0:T(8,128)(2,1)S(1)} %attention.2.refs_5_), channel_id=1, source_target_pairs={{0,8},{4,12},{8,0},{12,4},{16,24},{20,28},{24,16},{28,20},{1,9},{5... | collective-permute-start | bytes 884744 | tf_op jit(solution)/shard_map/ppermute | solution.py:671
  62.2 8.4 %collective-permute-start.11 = (bf16[1152,128]{1,0:T(8,128)(2,1)S(1)}, bf16[1152,128]{1,0:T(8,128)(2,1)S(1)}, u32[]{:S(2)}, u32[]{:S(2)}) collective-permute-start(bf16[1152,128]{1,0:T(8,128)(2,1)S(1)} %attention.2.refs_5_), channel_id=1, source_target_pairs={{0,16},{4,20},{8,24},{12,28},{16,0},{20,4},{24,8},{28,12},{1,17},{... | collective-permute-start | bytes 884744 | tf_op jit(solution)/shard_map/ppermute | solution.py:671
  62.7 13.1 %collective-permute-start.16 = (bf16[1152,128]{1,0:T(8,128)(2,1)S(1)}, bf16[1152,128]{1,0:T(8,128)(2,1)S(1)}, u32[]{:S(2)}, u32[]{:S(2)}) collective-permute-start(bf16[1152,128]{1,0:T(8,128)(2,1)S(1)} %get-tuple-element.51.refs_5_), channel_id=1, source_target_pairs={{0,4},{4,0},{8,12},{12,8},{16,20},{20,16},{24,28},{28,24},{1,5},{5... | collective-permute-start | bytes 884744 | tf_op jit(solution)/shard_map/ppermute | solution.py:671
  62.8 13.7 %collective-permute-start.19 = (bf16[1152,128]{1,0:T(8,128)(2,1)S(1)}, bf16[1152,128]{1,0:T(8,128)(2,1)S(1)}, u32[]{:S(2)}, u32[]{:S(2)}) collective-permute-start(bf16[1152,128]{1,0:T(8,128)(2,1)S(1)} %collective-permute-done.17.refs_7_), channel_id=1, source_target_pairs={{0,4},{4,0},{8,12},{12,8},{16,20},{20,16},{24,28},{28,24},{1,5},{5... | collective-permute-start | bytes 884744 | tf_op jit(solution)/shard_map/ppermute | solution.py:671
  63.3 13.2 %collective-permute-start.20 = (bf16[1152,128]{1,0:T(8,128)(2,1)S(1)}, bf16[1152,128]{1,0:T(8,128)(2,1)S(1)}, u32[]{:S(2)}, u32[]{:S(2)}) collective-permute-start(bf16[1152,128]{1,0:T(8,128)(2,1)S(1)} %collective-permute-done.18.refs_9_), channel_id=1, source_target_pairs={{0,4},{4,0},{8,12},{12,8},{16,20},{20,16},{24,28},{28,24},{1,5},{5... | collective-permute-start | bytes 884744 | tf_op jit(solution)/shard_map/ppermute | solution.py:671
  69.2 5.1 %collective-permute-start.21 = (bf16[576,128]{1,0:T(8,128)(2,1)S(1)}, bf16[576,128]{1,0:T(8,128)(2,1)S(1)}, u32[]{:S(2)}, u32[]{:S(2)}) collective-permute-start(bf16[576,128]{1,0:T(8,128)(2,1)S(1)} %slice.22), channel_id=1, source_target_pairs={{0,16},{4,20},{8,24},{12,28},{16,0},{20,4},{24,8},{28,12},{1,17},{... | collective-permute-start | bytes 442376 | tf_op jit(solution)/shard_map/ppermute | solution.py:671
  70.6 5.1 %collective-permute-start.22 = (bf16[576,128]{1,0:T(8,128)(2,1)S(1)}, bf16[576,128]{1,0:T(8,128)(2,1)S(1)}, u32[]{:S(2)}, u32[]{:S(2)}) collective-permute-start(bf16[576,128]{1,0:T(8,128)(2,1)S(1)} %slice.23), channel_id=1, source_target_pairs={{0,8},{4,12},{8,0},{12,4},{16,24},{20,28},{24,16},{28,20},{1,9},{5... | collective-permute-start | bytes 442376 | tf_op jit(solution)/shard_map/ppermute | solution.py:671
  74.4 2.6 %collective-permute-start.23 = (bf16[576,128]{1,0:T(8,128)(2,1)S(1)}, bf16[576,128]{1,0:T(8,128)(2,1)S(1)}, u32[]{:S(2)}, u32[]{:S(2)}) collective-permute-start(bf16[576,128]{1,0:T(8,128)(2,1)S(1)} %collective-permute-done.21.refs_11_), channel_id=1, source_target_pairs={{0,4},{4,0},{8,12},{12,8},{16,20},{20,16},{24,28},{28,24},{1,5},{5... | collective-permute-start | bytes 442376 | tf_op jit(solution)/shard_map/ppermute | solution.py:671
  75.8 1.8 %collective-permute-start.24 = (bf16[576,128]{1,0:T(8,128)(2,1)S(1)}, bf16[576,128]{1,0:T(8,128)(2,1)S(1)}, u32[]{:S(2)}, u32[]{:S(2)}) collective-permute-start(bf16[576,128]{1,0:T(8,128)(2,1)S(1)} %collective-permute-done.22.refs_12_), channel_id=1, source_target_pairs={{0,4},{4,0},{8,12},{12,8},{16,20},{20,16},{24,28},{28,24},{1,5},{5... | collective-permute-start | bytes 442376 | tf_op jit(solution)/shard_map/ppermute | solution.py:671
  75.8 14.7 %collective-permute-start.9 = (bf16[1152,128]{1,0:T(8,128)(2,1)S(1)}, bf16[1152,128]{1,0:T(8,128)(2,1)S(1)}, u32[]{:S(2)}, u32[]{:S(2)}) collective-permute-start(bf16[1152,128]{1,0:T(8,128)(2,1)S(1)} %attention.2.refs_5_), channel_id=1, source_target_pairs={{0,4},{4,0},{8,12},{12,8},{16,20},{20,16},{24,28},{28,24},{1,5},{5... | collective-permute-start | bytes 884744 | tf_op jit(solution)/shard_map/ppermute | solution.py:671
  76.4 14.1 %collective-permute-start.12 = (bf16[1152,128]{1,0:T(8,128)(2,1)S(1)}, bf16[1152,128]{1,0:T(8,128)(2,1)S(1)}, u32[]{:S(2)}, u32[]{:S(2)}) collective-permute-start(bf16[1152,128]{1,0:T(8,128)(2,1)S(1)} %collective-permute-done.10.refs_7_), channel_id=1, source_target_pairs={{0,4},{4,0},{8,12},{12,8},{16,20},{20,16},{24,28},{28,24},{1,5},{5... | collective-permute-start | bytes 884744 | tf_op jit(solution)/shard_map/ppermute | solution.py:671
  76.5 14.0 %collective-permute-start.13 = (bf16[1152,128]{1,0:T(8,128)(2,1)S(1)}, bf16[1152,128]{1,0:T(8,128)(2,1)S(1)}, u32[]{:S(2)}, u32[]{:S(2)}) collective-permute-start(bf16[1152,128]{1,0:T(8,128)(2,1)S(1)} %collective-permute-done.11.refs_9_), channel_id=1, source_target_pairs={{0,4},{4,0},{8,12},{12,8},{16,20},{20,16},{24,28},{28,24},{1,5},{5... | collective-permute-start | bytes 884744 | tf_op jit(solution)/shard_map/ppermute | solution.py:671
  76.9 13.1 %collective-permute-start.14 = (bf16[576,128]{1,0:T(8,128)(2,1)S(1)}, bf16[576,128]{1,0:T(8,128)(2,1)S(1)}, u32[]{:S(2)}, u32[]{:S(2)}) collective-permute-start(bf16[576,128]{1,0:T(8,128)(2,1)S(1)} %slice.20), channel_id=1, source_target_pairs={{0,16},{4,20},{8,24},{12,28},{16,0},{20,4},{24,8},{28,12},{1,17},{... | collective-permute-start | bytes 442376 | tf_op jit(solution)/shard_map/ppermute | solution.py:671
  77.6 12.4 %collective-permute-start.15 = (bf16[576,128]{1,0:T(8,128)(2,1)S(1)}, bf16[576,128]{1,0:T(8,128)(2,1)}, u32[]{:S(2)}, u32[]{:S(2)}) collective-permute-start(bf16[576,128]{1,0:T(8,128)(2,1)S(1)} %slice.21), channel_id=1, source_target_pairs={{0,8},{4,12},{8,0},{12,4},{16,24},{20,28},{24,16},{28,20},{1,9},{5... | collective-permute-start | bytes 442376 | tf_op jit(solution)/shard_map/ppermute | solution.py:671
  90.0 1.5 %collective-permute-start.25 = (bf16[576,128]{1,0:T(8,128)(2,1)S(1)}, bf16[576,128]{1,0:T(8,128)(2,1)}, u32[]{:S(2)}, u32[]{:S(2)}) collective-permute-start(bf16[576,128]{1,0:T(8,128)(2,1)S(1)} %collective-permute-done.14.refs_11_), channel_id=1, source_target_pairs={{0,4},{4,0},{8,12},{12,8},{16,20},{20,16},{24,28},{28,24},{1,5},{5... | collective-permute-start | bytes 442376 | tf_op jit(solution)/shard_map/ppermute | solution.py:671
  90.0 1.9 %collective-permute-start.26 = (bf16[576,128]{1,0:T(8,128)(2,1)}, bf16[576,128]{1,0:T(8,128)(2,1)}, u32[]{:S(2)}, u32[]{:S(2)}) collective-permute-start(bf16[576,128]{1,0:T(8,128)(2,1)} %collective-permute-done.15.refs_12_), channel_id=1, source_target_pairs={{0,4},{4,0},{8,12},{12,8},{16,20},{20,16},{24,28},{28,24},{1,5},{5... | collective-permute-start | bytes 442376 | tf_op jit(solution)/shard_map/ppermute | solution.py:671
  106.7 9.4 %collective-permute-start.27 = (bf16[672,128]{1,0:T(8,128)(2,1)S(1)}, bf16[672,128]{1,0:T(8,128)(2,1)S(1)}, u32[]{:S(2)}, u32[]{:S(2)}) collective-permute-start(bf16[672,128]{1,0:T(8,128)(2,1)S(1)} %get-tuple-element.58), channel_id=1, source_target_pairs={{0,1},{1,0},{2,3},{3,2},{4,5},{5,4},{6,7},{7,6},{8,9},{9,8},{10,11... | collective-permute-start | bytes 516104 | tf_op jit(solution)/shard_map/ppermute | solution.py:798
  108.1 15.6 %collective-permute-start.28 = (bf16[672,128]{1,0:T(8,128)(2,1)S(1)}, bf16[672,128]{1,0:T(8,128)(2,1)S(1)}, u32[]{:S(2)}, u32[]{:S(2)}) collective-permute-start(bf16[672,128]{1,0:T(8,128)(2,1)S(1)} %get-tuple-element.59), channel_id=1, source_target_pairs={{0,2},{1,3},{2,0},{3,1},{4,6},{5,7},{6,4},{7,5},{8,10},{9,11},{10,... | collective-permute-start | bytes 516104 | tf_op jit(solution)/shard_map/ppermute | solution.py:798
  108.4 15.2 %collective-permute-start.29 = (bf16[672,128]{1,0:T(8,128)(2,1)S(1)}, bf16[672,128]{1,0:T(8,128)(2,1)S(1)}, u32[]{:S(2)}, u32[]{:S(2)}) collective-permute-start(bf16[672,128]{1,0:T(8,128)(2,1)S(1)} %get-tuple-element.60), channel_id=1, source_target_pairs={{0,3},{1,2},{2,1},{3,0},{4,7},{5,6},{6,5},{7,4},{8,11},{9,10},{10,... | collective-permute-start | bytes 516104 | tf_op jit(solution)/shard_map/ppermute | solution.py:798
  (9 other events, 33.0 us)

commit v5 on v3

--- a/solution.py
+++ b/solution.py
@@ -164,6 +164,14 @@
     return loaded[0] if len(loaded) == 1 else jnp.concatenate(loaded, axis=0)
 
 
+def in_vmem(value):
+    return pltpu.with_memory_space_constraint(value, pltpu.VMEM)
+
+
+def in_hbm(value):
+    return pltpu.with_memory_space_constraint(value, pltpu.HBM)
+
+
 def payload_kernel(segments, rows, columns, mask, embed, patches, out):
     labels = [one[...].astype(jnp.float32) for one in (segments, rows, columns, mask)]
     labels.append(jnp.zeros((4, labels[0].shape[1]), jnp.float32))
@@ -201,31 +209,27 @@
             flops=count * D, bytes_accessed=4 * count * D, transcendentals=0
         ),
         name="payload",
-    )(*operands)
+    )(*map(in_hbm, operands))
 
 
 def qkv_kernel(count, place, *refs):
     first, second = refs[:count], refs[count : 2 * count]
     table, gain, weight = refs[2 * count : 2 * count + 3]
-    *outs, inputs_out, qkv_out, label_out, sems = refs[-7:]
-    start = pl.multiple_of(place[0] * inputs_out.shape[0], inputs_out.shape[0])
+    inputs_out, qkv_out, label_out = refs[-3:]
     mine, other = stacked(first), stacked(second)
     leads = place[1] == 0
     ahead = jnp.where(leads, mine, other)
     behind = jnp.where(leads, other, mine)
     both = jnp.concatenate([ahead, behind], axis=0)
-    inputs_out[...] = both[:, :D]
-    label_out[...] = both[:, D:]
-    target = pl.ds(start, inputs_out.shape[0])
-    copies = [
-        pltpu.make_async_copy(source, out.at[target, :], sems.at[number])
-        for number, (source, out) in enumerate(zip((inputs_out, qkv_out, label_out), outs))
-    ]
-    copies[0].start()
-    copies[2].start()
+    rows = both.shape[0]
+    at = pl.ds(pl.multiple_of(place[0] * rows, rows), rows)
+    inputs_out[at, :] = both[:, :D]
+    label_out[at, :] = both[:, D:]
     labels = both[:, D:].astype(jnp.float32)
     normed = norm_rows(both[:, :D].astype(jnp.float32), gain[...]).astype(jnp.bfloat16)
-    columns = jnp.dot(normed, weight[...], preferred_element_type=jnp.float32)
+    columns = lax.dot_general(
+        normed, weight[...], (((1,), (1,)), ((), ())), preferred_element_type=jnp.float32
+    )
     lane = lax.broadcasted_iota(jnp.int32, labels.shape, 1)
     numbers = lane.astype(jnp.float32)
     hot = (numbers == labels[:, 1:2]) | (numbers == labels[:, 2:3] + POSITIONS)
@@ -257,36 +261,34 @@
     ones = jnp.where(wide == 2 * HD, 1.0, 0.0)
     parts.append(jnp.where(wide < HD, values_part, ones))
     parts.append(jnp.where((wide >= HD) & (wide < 2 * HD), values_part, ones))
-    qkv_out[...] = jnp.concatenate(parts, axis=1).astype(jnp.bfloat16)
-    copies[1].start()
-    for copy in copies:
-        copy.wait()
+    for number, part in enumerate(parts[:6]):
+        qkv_out[at, number * LANES : (number + 1) * LANES] = part.astype(jnp.bfloat16)
+    for number, part in enumerate(parts[6:]):
+        low = (6 + 2 * number) * LANES
+        qkv_out[at, low : low + 2 * LANES] = part.astype(jnp.bfloat16)
 
 
 def qkv_call(place, first, second, table, gain, weight, earlier, total):
     rows = 2 * sum(piece.shape[0] for piece in first)
     widths = (D, 10 * LANES, LANES)
-    operands = [*first, *second, table, gain, weight]
+    operands = [*first, *second, table, gain, in_vmem(weight)]
     vmem = pl.BlockSpec(memory_space=pltpu.VMEM)
-    anywhere = pl.BlockSpec(memory_space=pl.ANY)
+    held = [in_vmem(one) for one in earlier]
     return pl.pallas_call(
         functools.partial(qkv_kernel, len(first)),
         in_specs=[pl.BlockSpec(memory_space=pltpu.SMEM)]
-        + [vmem] * len(operands)
-        + [anywhere] * len(earlier),
-        out_specs=[anywhere] * len(widths),
-        scratch_shapes=[pltpu.VMEM((rows, width), jnp.bfloat16) for width in widths]
-        + [pltpu.SemaphoreType.DMA((len(widths),))],
-        out_shape=[jax.ShapeDtypeStruct((total, width), jnp.bfloat16) for width in widths],
+        + [vmem] * (len(operands) + len(earlier)),
+        out_specs=[vmem] * len(widths),
+        out_shape=[pltpu.VMEM((total, width), jnp.bfloat16) for width in widths],
         input_output_aliases={1 + len(operands) + i: i for i in range(len(earlier))},
-        compiler_params=pltpu.CompilerParams(vmem_limit_bytes=16 << 20),
+        compiler_params=pltpu.CompilerParams(vmem_limit_bytes=14 << 20),
         cost_estimate=pl.CostEstimate(
-            flops=6 * rows * D * weight.shape[1],
+            flops=6 * rows * D * weight.shape[0],
             bytes_accessed=2 * (rows * 4 * D + weight.size),
             transcendentals=rows,
         ),
         name="norm_qkv",
-    )(place, *operands, *earlier)
+    )(place, *operands, *held)
 
 
 def segment_row(labels):
@@ -391,51 +393,68 @@
             pltpu.VMEM((2, rows, LANES), jnp.float32),
             pltpu.VMEM((total // BLOCK, 8, BLOCK), jnp.float32),
         ],
-        compiler_params=pltpu.CompilerParams(vmem_limit_bytes=22 << 20),
+        compiler_params=pltpu.CompilerParams(vmem_limit_bytes=20 << 20),
         cost_estimate=pl.CostEstimate(
             flops=10 * rows * total * 2 * LANES,
             bytes_accessed=2 * block.size,
             transcendentals=rows * total,
         ),
         name="attention",
-    )(owners, labels, block)
-
-
-def order_kernel(shards, ids, weight, out, sems):
+    )(owners, in_vmem(labels), in_vmem(block))
+
+
+def prepare_kernel(shards, ids, out_weight, merge_weight, qkv_weight, spread, *refs):
+    out, merge, qkv, qkv_buffer, spread_buffer, sems = refs
     rest = 2 * HD - LANES
+    copies = [(qkv_weight, qkv_buffer), (spread, spread_buffer)]
     out[shards * LANES :] = jnp.zeros((shards // 2 * LANES, D), jnp.bfloat16)
-    copies = []
     for place in range(shards):
         start = pl.multiple_of(ids[place] * (2 * HD), 16)
         to = (shards + place // 2) * LANES + place % 2 * rest
-        copies.append((pl.ds(start, LANES), pl.ds(place * LANES, LANES)))
-        copies.append((pl.ds(start + LANES, rest), pl.ds(to, rest)))
+        copies.append(
+            (out_weight.at[pl.ds(start, LANES), :], out.at[pl.ds(place * LANES, LANES), :])
+        )
+        copies.append((out_weight.at[pl.ds(start + LANES, rest), :], out.at[pl.ds(to, rest), :]))
+    copies.append((merge_weight, merge))
     copies = [
-        pltpu.make_async_copy(weight.at[source, :], out.at[target, :], sems.at[i])
+        pltpu.make_async_copy(source, target, sems.at[i])
         for i, (source, target) in enumerate(copies)
     ]
     for copy in copies:
         copy.start()
-    for copy in copies:
+    copies[0].wait()
+    copies[1].wait()
+    qkv[...] = jnp.dot(
+        spread_buffer[...], qkv_buffer[...], preferred_element_type=jnp.float32
+    ).astype(jnp.bfloat16)
+    for copy in copies[2:]:
         copy.wait()
 
 
-def order_call(ids, weight):
+def prepare_call(ids, out_weight, merge_weight, qkv_weight, spread):
     shards = ids.shape[0]
-    shape = (shards * LANES * 3 // 2, D)
+    anywhere = pl.BlockSpec(memory_space=pl.ANY)
+    vmem = pl.BlockSpec(memory_space=pltpu.VMEM)
+    operands = (out_weight, merge_weight, qkv_weight, spread)
+    shapes = [(shards * LANES * 3 // 2, D), merge_weight.shape, (spread.shape[0], D)]
     return pl.pallas_call(
-        functools.partial(order_kernel, shards),
-        in_specs=[
-            pl.BlockSpec(memory_space=pltpu.SMEM),
-            pl.BlockSpec(memory_space=pl.ANY),
+        functools.partial(prepare_kernel, shards),
+        in_specs=[pl.BlockSpec(memory_space=pltpu.SMEM)] + [anywhere] * len(operands),
+        out_specs=[vmem] * len(shapes),
+        out_shape=[pltpu.VMEM(shape, jnp.bfloat16) for shape in shapes],
+        scratch_shapes=[
+            pltpu.VMEM(qkv_weight.shape, jnp.bfloat16),
+            pltpu.VMEM(spread.shape, jnp.bfloat16),
+            pltpu.SemaphoreType.DMA((2 * shards + 3,)),
         ],
-        out_specs=pl.BlockSpec(memory_space=pltpu.VMEM),
-        out_shape=jax.ShapeDtypeStruct(shape, jnp.bfloat16),
-        scratch_shapes=[pltpu.SemaphoreType.DMA((2 * shards,))],
-        compiler_params=pltpu.CompilerParams(vmem_limit_bytes=16 << 20),
-        cost_estimate=pl.CostEstimate(flops=0, bytes_accessed=4 * weight.size, transcendentals=0),
-        name="order_rows",
-    )(ids, weight)
+        compiler_params=pltpu.CompilerParams(vmem_limit_bytes=10 << 20),
+        cost_estimate=pl.CostEstimate(
+            flops=2 * spread.size * D,
+            bytes_accessed=4 * (out_weight.size + merge_weight.size + qkv_weight.size),
+            transcendentals=0,
+        ),
+        name="prepare",
+    )(ids, *map(in_hbm, operands))
 
 
 def merge_kernel(start, counts, packs, last, *refs):
@@ -520,7 +539,7 @@
     width = merge_weight.shape[0]
     pieces = [piece for source in sources for piece in source]
     vmem = pl.BlockSpec(memory_space=pltpu.VMEM)
-    operands = [inputs, weight, gain, merge_weight, bias, *pieces]
+    operands = [in_vmem(inputs), in_vmem(weight), gain, in_vmem(merge_weight), bias, *pieces]
     specs = [vmem] * len(operands)
     shapes = [jax.ShapeDtypeStruct((groups, width), jnp.bfloat16)]
     if route:
@@ -536,7 +555,7 @@
         out_specs=[vmem] * len(shapes),
         scratch_shapes=[pltpu.VMEM((D // LANES, rows, LANES), jnp.float32)],
         out_shape=shapes,
-        compiler_params=pltpu.CompilerParams(vmem_limit_bytes=26 << 20),
+        compiler_params=pltpu.CompilerParams(vmem_limit_bytes=20 << 20),
         cost_estimate=pl.CostEstimate(
             flops=4 * rows * D * D + 2 * groups * merge_weight.size,
             bytes_accessed=2 * (D * D + merge_weight.size + 3 * rows * D),
@@ -563,12 +582,14 @@
 
 
 def place_call(me, blocks, most, width):
-    vmem = pl.BlockSpec(memory_space=pltpu.VMEM)
+    fixed = lambda shape: pl.BlockSpec(shape, lambda i: (0,) * len(shape))
+    shape = (len(blocks), most, width)
     return pl.pallas_call(
         place_kernel,
-        in_specs=[pl.BlockSpec(memory_space=pltpu.SMEM)] + [vmem] * len(blocks),
-        out_specs=vmem,
-        out_shape=jax.ShapeDtypeStruct((len(blocks), most, width), jnp.bfloat16),
+        grid=(1,),
+        in_specs=[pl.BlockSpec(memory_space=pltpu.SMEM)] + [fixed(one.shape) for one in blocks],
+        out_specs=fixed(shape),
+        out_shape=jax.ShapeDtypeStruct(shape, jnp.bfloat16),
         compiler_params=pltpu.CompilerParams(vmem_limit_bytes=8 << 20),
         cost_estimate=pl.CostEstimate(
             flops=0, bytes_accessed=4 * len(blocks) * most * width, transcendentals=0
@@ -655,15 +676,16 @@
     value = payload_call(segment_ids, patch_rows, patch_column, patch_mask, mask_embed, patches)
     own_swap, across_x, across_y = near_shards(value)
 
-    order = jnp.asarray(weight_order(heads_here))
-    spread = (jnp.arange(qkv_weight.shape[1])[:, None] == order[None, :]).astype(jnp.bfloat16)
-    weight = jnp.dot(qkv_weight, spread, preferred_element_type=jnp.float32).astype(jnp.bfloat16)
+    order = weight_order(heads_here)
+    spread = (order[:, None] == np.arange(qkv_weight.shape[1])[None, :]).astype(jnp.bfloat16)
     table = jnp.asarray(angle_table(heads_here))
     gain = norm_gain.astype(jnp.float32)[None, :]
     merge_gain_row = merge_gain.astype(jnp.float32)[None, :]
     bias = merge_bias.astype(jnp.float32)[None, :]
     ids = jnp.stack([me ^ place for place in range(shards)])
-    ordered = order_call(ids, out_weight)
+    ordered, merge_rows, weight = prepare_call(
+        ids, out_weight, merge_weight.T, qkv_weight.T, jnp.asarray(spread)
+    )
 
     chip, core = me // 2, me % 2
     project = lambda place, first, second, earlier: qkv_call(
@@ -683,12 +705,16 @@
     for start, rows in zip(starts, CHUNKS):
         made = attention_call(start, rows, image_owner[0], labels, block, note is None)
         note = made[1] if note is None else note
-        attended.append((made[0], near_shards(made[0])))
+        value = made[0]
+        if attended:
+            (value,) = after([value], *attended[-1][1])
+        attended.append((value, near_shards(value)))
     latest = attended[-1][0]
     most = 2 * (total // 4) // images
     projected, moving = [], []
     for own, (own_swap, across_x, across_y) in attended:
-        across_x, across_y = after([across_x, across_y], latest)
+        previous = moving[-1][-1] if moving else ()
+        across_x, across_y = after([across_x, across_y], latest, *previous)
         far = far_shards(across_x, across_y)
         moving.append(
             (own, own_swap, across_x, send_seq(across_x, 1), across_y, send_seq(across_y, 1), far)
@@ -702,7 +728,7 @@
         if number == len(CHUNKS) - 1:
             route = (pack[None], most, note, *projected)
         made = merge_call(
-            start, rows, sources, inputs, ordered, merge_gain_row, merge_weight.T, bias, packs, route
+            start, rows, sources, inputs, ordered, merge_gain_row, merge_rows, bias, packs, route
         )
         projected.append(made[0])
     blocks = [made[0]] + [

time: 145 us -> 132 us (0.910)
  local copies, waits for them, and re-layouts: 44.4 us -> 35.7 us
  matrix products: 1.92 us -> 0 us
  Pallas kernels: 50 us -> 48.3 us
    unnamed x78 -> x52, local copies, waits for them, and re-layouts: 43.5 us -> 33.9 us
    pallas_call x4, Pallas kernels: 15.5 us -> 12.2 us  [qkv_call(): pl.pallas_call(functools.partial(qkv_kernel, len(first)), in_specs=[pl.Bl...]
    ppermute x27, waiting for transfers between devices: 14.2 us -> 12 us  [send_seq(): return lax.ppermute(value, 'seq', [(i, i ^ flip) for i in range(size)])]
    dot_general x1 -> x0, matrix products: 1.92 us -> none  [fast_local(): jnp.dot(qkv_weight, spread, preferred_element_type=jnp.float32)]
    pallas_call x2, Pallas kernels: 4.45 us -> 6.16 us  [the longest x1 5.11 us: prepare_call(): pl.pallas_call(functools.partial(prepare_kernel, shards), in_specs=[pl.Bl...]
  transfers between devices with their start and end apart: 30 -> 30, of which waited for: 10 -> 9; matrix products, arithmetic and copies ran while one was open for 2% -> 2% of each run, Pallas kernels for 20% -> 22%
where the time goes in v5:
time: 132 us; the launch traced here: 130 us
  Pallas kernels  48.3 us (37%)
  local copies, waits for them, and re-layouts  35.7 us (27%)
  waiting for transfers between devices  24 us (18%)
  starting transfers between devices  21.6 us (16%)
    unnamed x52, local copies, waits for them, and re-layouts  33.9 us
    ppermute x27, starting transfers between devices, send_seq(): return lax.ppermute(value, 'seq', [(i, i ^ flip) for i in range(size)])  17.2 us
    pallas_call x2, Pallas kernels, merge_call(): pl.pallas_call(functools.partial(merge_kernel, start, [len(source) for so...  13.9 us
    pallas_call x2, Pallas kernels, attention_call(): pl.pallas_call(functools.partial(attention_kernel, start), in_specs=[pl.B...  13.8 us
    pallas_call x4, Pallas kernels, qkv_call(): pl.pallas_call(functools.partial(qkv_kernel, len(first)), in_specs=[pl.Bl...  12.2 us
    ppermute x27, waiting for transfers between devices, send_seq(): return lax.ppermute(value, 'seq', [(i, i ^ flip) for i in range(size)])  12 us
    ppermute x3, waiting for transfers between devices, fast_local(): lax.ppermute(made[flip], 'pack', [(z, z ^ flip) for z in range(packs)])  12 us
    pallas_call x1, Pallas kernels, prepare_call(): pl.pallas_call(functools.partial(prepare_kernel, shards), in_specs=[pl.Bl...  5.11 us
  transfers between devices with their start and end apart: 30, of which 9 were waited for; matrix products, arithmetic and copies ran while one was open for 2% of the time, Pallas kernels for 22%

profile of v5, /device:TPU:0, one launch (start us, length us, event | category | flops | bytes accessed | tf_op | source)
XLA Modules:
  0.0 130.3 jit_solution(15698754550457494473)
XLA Ops:
  0.0 2.3 %payload.1.refs_0_ = bf16[192,1536]{1,0:T(8,128)(2,1)} custom-call(s32[1,192]{1,0:T(1,128)} %segments.1, s32[1,192]{1,0:T(1,128)} %rows.1, s32[1,192]{1,0:T(1,128)} %columns.1, s32[1,192]{1,0:T(1,128)} %mask.1, bf16[1408]{0:T(1024)(128)(2,1)} %embed.1, bf16[1,192,1408]{2,1,0:T(8,128)(2,1)} %patches.1), custom_call_target="tpu_custom_call" | custom-call | flops 270336 | bytes 1081344 | tf_op jit(solution)/shard_map/payload/pallas_call | solution.py:201
  2.7 2.5 %collective-permute-start = (bf16[192,1536]{1,0:T(8,128)(2,1)}, bf16[192,1536]{1,0:T(8,128)(2,1)}, u32[]{:S(2)}, u32[]{:S(2)}) collective-permute-start(bf16[192,1536]{1,0:T(8,128)(2,1)} %payload.1.refs_0_), channel_id=1, source_target_pairs={{0,8},{4,12},{8,0},{12,4},{16,24},{20,28},{24,16},{28,20},{1,9},{5... | collective-permute-start | bytes 1769480 | tf_op jit(solution)/shard_map/ppermute | solution.py:603
  7.5 5.1 %prepare.1 = (bf16[1536,1408]{1,0:T(8,128)(2,1)S(1)}, bf16[448,5632]{1,0:T(8,128)(2,1)S(1)}, bf16[768,1408]{1,0:T(8,128)(2,1)S(1)}) custom-call(s32[8]{0:T(128)S(1)} %stack.70.ids, bf16[1408,1408]{1,0:T(8,128)(2,1)} %out_weight.1, bf16[448,5632]{1,0:T(8,128)(2,1)} %bitcast.29, bf16[528,1408]{1,0:T(8,128)(2,1)} %bitcast.30, ...), custom_call_target="tpu_custom_call" | custom-call | flops 1141899264 | bytes 20996096 | tf_op jit(solution)/shard_map/prepare/pallas_call | solution.py:440
  12.6 2.3 %copy-done.13 = bf16[448,5632]{1,0:T(8,128)(2,1)} copy-done((bf16[448,5632]{1,0:T(8,128)(2,1)}, bf16[448,5632]{1,0:T(8,128)(2,1)S(1)}, u32[]{:S(2)}) %copy-start.13) | copy-done | bytes 5046296
  14.9 2.1 %copy-done.15 = bf16[1536,1408]{1,0:T(8,128)(2,1)} copy-done((bf16[1536,1408]{1,0:T(8,128)(2,1)}, bf16[1536,1408]{1,0:T(8,128)(2,1)S(1)}, u32[]{:S(2)}) %copy-start.15) | copy-done | bytes 4325400
  17.1 3.1 %norm_qkv.4 = (bf16[1536,1408]{1,0:T(8,128)(2,1)S(1)}, bf16[1536,1280]{1,0:T(8,128)(2,1)S(1)}, bf16[1536,128]{1,0:T(8,128)(2,1)S(1)}) custom-call(s32[2]{0:T(128)S(1)} %pad_add_fusion.1.place, bf16[192,1536]{1,0:T(8,128)(2,1)} %payload.1.refs_0_, bf16[192,1536]{1,0:T(8,128)(2,1)} %collective-permute-done.2.refs_1_, bf16[128,512]{1,0:T(8,128)(2,1)S(1)} %copy-done.12, ...), custom_call_target="tpu_custom_call" | custom-call | flops 2491416576 | bytes 6488064 | tf_op jit(solution)/shard_map/norm_qkv/pallas_call | solution.py:277
  20.2 2.1 %copy-done = bf16[1536,1408]{1,0:T(8,128)(2,1)} copy-done((bf16[1536,1408]{1,0:T(8,128)(2,1)}, bf16[1536,1408]{1,0:T(8,128)(2,1)S(1)}, u32[]{:S(2)}) %copy-start) | copy-done | bytes 4325400
  22.3 1.9 %copy-done.6 = bf16[1536,1280]{1,0:T(8,128)(2,1)} copy-done((bf16[1536,1280]{1,0:T(8,128)(2,1)}, bf16[1536,1280]{1,0:T(8,128)(2,1)S(1)}, u32[]{:S(2)}) %copy-start.6) | copy-done | bytes 3932184
  26.6 2.2 %copy-done.1 = bf16[1536,1408]{1,0:T(8,128)(2,1)S(1)} copy-done((bf16[1536,1408]{1,0:T(8,128)(2,1)S(1)}, bf16[1536,1408]{1,0:T(8,128)(2,1)}, u32[]{:S(2)}) %copy-start.1) | copy-done | bytes 4325400
  28.8 2.1 %copy-done.7 = bf16[1536,1280]{1,0:T(8,128)(2,1)S(1)} copy-done((bf16[1536,1280]{1,0:T(8,128)(2,1)S(1)}, bf16[1536,1280]{1,0:T(8,128)(2,1)}, u32[]{:S(2)}) %copy-start.7) | copy-done | bytes 3932184
  30.9 3.1 %norm_qkv.5 = (bf16[1536,1408]{1,0:T(8,128)(2,1)S(1)}, bf16[1536,1280]{1,0:T(8,128)(2,1)S(1)}, bf16[1536,128]{1,0:T(8,128)(2,1)S(1)}) custom-call(s32[2]{0:T(128)S(1)} %pad_add_fusion.3.place, bf16[192,1536]{1,0:T(8,128)(2,1)} %collective-permute-done.refs_0_, ...), custom_call_target="tpu_custom_call", output_to_operand_aliasing={{0}: (6, {}), {1}: (7, {}), {2}: (8, {})} | custom-call | flops 2491416576 | bytes 6488064 | tf_op jit(solution)/shard_map/norm_qkv/pallas_call | solution.py:277
  34.1 3.0 %norm_qkv.6 = (bf16[1536,1408]{1,0:T(8,128)(2,1)S(1)}, bf16[1536,1280]{1,0:T(8,128)(2,1)S(1)}, bf16[1536,128]{1,0:T(8,128)(2,1)S(1)}) custom-call(s32[2]{0:T(128)S(1)} %pad_add_fusion.2.place, bf16[192,1536]{1,0:T(8,128)(2,1)S(1)} %collective-permute-done.1.refs_0_, ...), custom_call_target="tpu_custom_call", output_to_operand_aliasing={{0}: (6, {}), {1}: (7, {}), {2}: (8, {})} | custom-call | flops 2491416576 | bytes 6488064 | tf_op jit(solution)/shard_map/norm_qkv/pallas_call | solution.py:277
  37.1 2.1 %copy-done.2 = bf16[1536,1408]{1,0:T(8,128)(2,1)} copy-done((bf16[1536,1408]{1,0:T(8,128)(2,1)}, bf16[1536,1408]{1,0:T(8,128)(2,1)S(1)}, u32[]{:S(2)}) %copy-start.2) | copy-done | bytes 4325400
  39.1 1.9 %copy-done.8 = bf16[1536,1280]{1,0:T(8,128)(2,1)} copy-done((bf16[1536,1280]{1,0:T(8,128)(2,1)}, bf16[1536,1280]{1,0:T(8,128)(2,1)S(1)}, u32[]{:S(2)}) %copy-start.8) | copy-done | bytes 3932184
  43.2 2.2 %copy-done.3 = bf16[1536,1408]{1,0:T(8,128)(2,1)S(1)} copy-done((bf16[1536,1408]{1,0:T(8,128)(2,1)S(1)}, bf16[1536,1408]{1,0:T(8,128)(2,1)}, u32[]{:S(2)}) %copy-start.3) | copy-done | bytes 4325400
  45.5 2.1 %copy-done.9 = bf16[1536,1280]{1,0:T(8,128)(2,1)S(1)} copy-done((bf16[1536,1280]{1,0:T(8,128)(2,1)S(1)}, bf16[1536,1280]{1,0:T(8,128)(2,1)}, u32[]{:S(2)}) %copy-start.9) | copy-done | bytes 3932184
  47.6 3.0 %norm_qkv.7 = (bf16[1536,1408]{1,0:T(8,128)(2,1)S(1)}, bf16[1536,1280]{1,0:T(8,128)(2,1)S(1)}, bf16[1536,128]{1,0:T(8,128)(2,1)S(1)}) custom-call(s32[2]{0:T(128)S(1)} %pad_add_fusion.place, bf16[96,1536]{1,0:T(8,128)(2,1)} %collective-permute-done.3.refs_0_, ...), custom_call_target="tpu_custom_call", output_to_operand_aliasing={{0}: (8, {}), {1}: (9, {}), {2}: (10, {})} | custom-call | flops 2491416576 | bytes 6488064 | tf_op jit(solution)/shard_map/norm_qkv/pallas_call | solution.py:277
  50.6 2.1 %copy-done.4 = bf16[1536,1408]{1,0:T(8,128)(2,1)} copy-done((bf16[1536,1408]{1,0:T(8,128)(2,1)}, bf16[1536,1408]{1,0:T(8,128)(2,1)S(1)}, u32[]{:S(2)}) %copy-start.4) | copy-done | bytes 4325400
  54.5 2.1 %copy-done.11 = bf16[1536,1280]{1,0:T(8,128)(2,1)S(1)} copy-done((bf16[1536,1280]{1,0:T(8,128)(2,1)S(1)}, bf16[1536,1280]{1,0:T(8,128)(2,1)}, u32[]{:S(2)}) %copy-start.11) | copy-done | bytes 3932184
  56.6 5.9 %attention.3 = (bf16[1152,128]{1,0:T(8,128)(2,1)S(1)}, bf16[16,128]{1,0:T(8,128)(2,1)S(1)}) custom-call(s32[4]{0:T(128)S(1)} %bitcast.27, bf16[1536,128]{1,0:T(8,128)(2,1)S(1)} %get-tuple-element.54.labels, bf16[1536,1280]{1,0:T(8,128)(2,1)S(1)} %copy-done.11), custom_call_target="tpu_custom_call" | custom-call | flops 3019898880 | bytes 3932160 | tf_op jit(solution)/shard_map/attention/pallas_call | solution.py:386
  62.6 1.9 %collective-permute-start.10 = (bf16[1152,128]{1,0:T(8,128)(2,1)S(1)}, bf16[1152,128]{1,0:T(8,128)(2,1)S(1)}, u32[]{:S(2)}, u32[]{:S(2)}) collective-permute-start(bf16[1152,128]{1,0:T(8,128)(2,1)S(1)} %get-tuple-element.56.refs_5_), channel_id=1, source_target_pairs={{0,8},{4,12},{8,0},{12,4},{16,24},{20,28},{24,16},{28,20},{1,9},{5... | collective-permute-start | bytes 884744 | tf_op jit(solution)/shard_map/ppermute | solution.py:603
  66.0 8.0 %attention.2.refs_5_ = bf16[1152,128]{1,0:T(8,128)(2,1)S(1)} custom-call(s32[4]{0:T(128)S(1)} %bitcast.28, bf16[1536,128]{1,0:T(8,128)(2,1)S(1)} %get-tuple-element.54.labels, bf16[1536,1280]{1,0:T(8,128)(2,1)S(1)} %copy-done.11), custom_call_target="tpu_custom_call" | custom-call | flops 3019898880 | bytes 3932160 | tf_op jit(solution)/shard_map/attention/pallas_call | solution.py:386
  77.2 3.5 %collective-permute-done.15.refs_11_ = bf16[576,128]{1,0:T(8,128)(2,1)S(1)} collective-permute-done((bf16[576,128]{1,0:T(8,128)(2,1)S(1)}, bf16[576,128]{1,0:T(8,128)(2,1)S(1)}, u32[]{:S(2)}, u32[]{:S(2)}) %collective-permute-start.15) | collective-permute-done | bytes 147488 | tf_op jit(solution)/shard_map/ppermute | solution.py:603
  81.2 5.6 %collective-permute-done.16.refs_12_ = bf16[576,128]{1,0:T(8,128)(2,1)S(1)} collective-permute-done((bf16[576,128]{1,0:T(8,128)(2,1)S(1)}, bf16[576,128]{1,0:T(8,128)(2,1)S(1)}, u32[]{:S(2)}, u32[]{:S(2)}) %collective-permute-start.16) | collective-permute-done | bytes 147488 | tf_op jit(solution)/shard_map/ppermute | solution.py:603
  90.4 6.6 %out_merge.2.refs_17_ = bf16[192,448]{1,0:T(8,128)(2,1)S(1)} custom-call(bf16[1536,1408]{1,0:T(8,128)(2,1)S(1)} %bitcast.20, bf16[1536,1408]{1,0:T(8,128)(2,1)S(1)} %bitcast.26, f32[1,1408]{1,0:T(1,128)S(1)} %reshape.1.refs_2_, bf16[448,5632]{1,0:T(8,128)(2,1)S(1)} %bitcast.24, f32[1,448]{1,0:T(1,128)S(1)} %bitcast.21, ...), custom_call_target="tpu_custom_call" | custom-call | flops 7059013632 | bytes 15499264 | tf_op jit(solution)/shard_map/out_merge/pallas_call | solution.py:550
  98.7 2.2 %copy-done.5 = bf16[1536,1408]{1,0:T(8,128)(2,1)S(1)} copy-done((bf16[1536,1408]{1,0:T(8,128)(2,1)S(1)}, bf16[1536,1408]{1,0:T(8,128)(2,1)}, u32[]{:S(2)}) %copy-start.5) | copy-done | bytes 4325400
  100.9 2.4 %copy-done.14 = bf16[448,5632]{1,0:T(8,128)(2,1)S(1)} copy-done((bf16[448,5632]{1,0:T(8,128)(2,1)S(1)}, bf16[448,5632]{1,0:T(8,128)(2,1)}, u32[]{:S(2)}) %copy-start.14) | copy-done | bytes 5046296
  103.3 2.2 %copy-done.16 = bf16[1536,1408]{1,0:T(8,128)(2,1)S(1)} copy-done((bf16[1536,1408]{1,0:T(8,128)(2,1)S(1)}, bf16[1536,1408]{1,0:T(8,128)(2,1)}, u32[]{:S(2)}) %copy-start.16) | copy-done | bytes 4325400
  105.5 7.3 %out_merge.3 = (bf16[672,128]{1,0:T(8,128)(2,1)S(1)}, bf16[672,128]{1,0:T(8,128)(2,1)S(1)}, bf16[672,128]{1,0:T(8,128)(2,1)S(1)}, bf16[672,128]{1,0:T(8,128)(2,1)S(1)}) custom-call(bf16[1536,1408]{1,0:T(8,128)(2,1)S(1)} %copy-done.5, bf16[1536,1408]{1,0:T(8,128)(2,1)S(1)} %copy-done.16, f32[1,1408]{1,0:T(1,128)S(1)} %reshape.1.refs_2_, ...), custom_call_target="tpu_custom_call" | custom-call | flops 7059013632 | bytes 15499264 | tf_op jit(solution)/shard_map/out_merge/pallas_call | solution.py:550
  112.9 2.9 %collective-permute-start.28 = (bf16[672,128]{1,0:T(8,128)(2,1)S(1)}, bf16[672,128]{1,0:T(8,128)(2,1)S(1)}, u32[]{:S(2)}, u32[]{:S(2)}) collective-permute-start(bf16[672,128]{1,0:T(8,128)(2,1)S(1)} %get-tuple-element.67), channel_id=1, source_target_pairs={{0,2},{1,3},{2,0},{3,1},{4,6},{5,7},{6,4},{7,5},{8,10},{9,11},{10,... | collective-permute-start | bytes 516104 | tf_op jit(solution)/shard_map/ppermute | solution.py:735
  117.3 5.9 %collective-permute-done.27.refs_1_ = bf16[672,128]{1,0:T(8,128)(2,1)S(1)} collective-permute-done((bf16[672,128]{1,0:T(8,128)(2,1)S(1)}, bf16[672,128]{1,0:T(8,128)(2,1)S(1)}, u32[]{:S(2)}, u32[]{:S(2)}) %collective-permute-start.27) | collective-permute-done | bytes 172064 | tf_op jit(solution)/shard_map/ppermute | solution.py:735
  123.1 6.1 %collective-permute-done.29.refs_3_ = bf16[672,128]{1,0:T(8,128)(2,1)S(1)} collective-permute-done((bf16[672,128]{1,0:T(8,128)(2,1)S(1)}, bf16[672,128]{1,0:T(8,128)(2,1)S(1)}, u32[]{:S(2)}, u32[]{:S(2)}) %collective-permute-start.29) | collective-permute-done | bytes 172064 | tf_op jit(solution)/shard_map/ppermute | solution.py:735
  (108 shorter events, 22.3 us)
Async XLA Ops:
  2.3 14.8 %collective-permute-start.2 = (bf16[192,1536]{1,0:T(8,128)(2,1)}, bf16[192,1536]{1,0:T(8,128)(2,1)}, u32[]{:S(2)}, u32[]{:S(2)}) collective-permute-start(bf16[192,1536]{1,0:T(8,128)(2,1)} %payload.1.refs_0_), channel_id=1, source_target_pairs={{0,4},{4,0},{8,12},{12,8},{16,20},{20,16},{24,28},{28,24},{1,5},{5... | collective-permute-start | bytes 1769480 | tf_op jit(solution)/shard_map/ppermute | solution.py:603
  2.7 21.4 %collective-permute-start = (bf16[192,1536]{1,0:T(8,128)(2,1)}, bf16[192,1536]{1,0:T(8,128)(2,1)}, u32[]{:S(2)}, u32[]{:S(2)}) collective-permute-start(bf16[192,1536]{1,0:T(8,128)(2,1)} %payload.1.refs_0_), channel_id=1, source_target_pairs={{0,8},{4,12},{8,0},{12,4},{16,24},{20,28},{24,16},{28,20},{1,9},{5... | collective-permute-start | bytes 1769480 | tf_op jit(solution)/shard_map/ppermute | solution.py:603
  5.2 18.9 %collective-permute-start.1 = (bf16[192,1536]{1,0:T(8,128)(2,1)}, bf16[192,1536]{1,0:T(8,128)(2,1)S(1)}, u32[]{:S(2)}, u32[]{:S(2)}) collective-permute-start(bf16[192,1536]{1,0:T(8,128)(2,1)} %payload.1.refs_0_), channel_id=1, source_target_pairs={{0,16},{4,20},{8,24},{12,28},{16,0},{20,4},{24,8},{28,12},{1,17},{... | collective-permute-start | bytes 1769480 | tf_op jit(solution)/shard_map/ppermute | solution.py:603
  24.2 2.5 %collective-permute-start.6 = (bf16[192,1536]{1,0:T(8,128)(2,1)}, bf16[192,1536]{1,0:T(8,128)(2,1)}, u32[]{:S(2)}, u32[]{:S(2)}) collective-permute-start(bf16[192,1536]{1,0:T(8,128)(2,1)} %collective-permute-done.refs_0_), channel_id=1, source_target_pairs={{0,4},{4,0},{8,12},{12,8},{16,20},{20,16},{24,28},{28,24},{1,5},{5... | collective-permute-start | bytes 1769480 | tf_op jit(solution)/shard_map/ppermute | solution.py:603
  24.2 9.9 %collective-permute-start.5 = (bf16[192,1536]{1,0:T(8,128)(2,1)S(1)}, bf16[192,1536]{1,0:T(8,128)(2,1)}, u32[]{:S(2)}, u32[]{:S(2)}) collective-permute-start(bf16[192,1536]{1,0:T(8,128)(2,1)S(1)} %collective-permute-done.1.refs_0_), channel_id=1, source_target_pairs={{0,4},{4,0},{8,12},{12,8},{16,20},{20,16},{24,28},{28,24},{1,5},{5... | collective-permute-start | bytes 1769480 | tf_op jit(solution)/shard_map/ppermute | solution.py:603
  25.8 15.2 %collective-permute-start.3 = (bf16[96,1536]{1,0:T(8,128)(2,1)S(1)}, bf16[96,1536]{1,0:T(8,128)(2,1)}, u32[]{:S(2)}, u32[]{:S(2)}) collective-permute-start(bf16[96,1536]{1,0:T(8,128)(2,1)S(1)} %slice.18), channel_id=1, source_target_pairs={{0,16},{4,20},{8,24},{12,28},{16,0},{20,4},{24,8},{28,12},{1,17},{... | collective-permute-start | bytes 884744 | tf_op jit(solution)/shard_map/ppermute | solution.py:603
  26.4 14.6 %collective-permute-start.4 = (bf16[96,1536]{1,0:T(8,128)(2,1)S(1)}, bf16[96,1536]{1,0:T(8,128)(2,1)}, u32[]{:S(2)}, u32[]{:S(2)}) collective-permute-start(bf16[96,1536]{1,0:T(8,128)(2,1)S(1)} %slice.19), channel_id=1, source_target_pairs={{0,8},{4,12},{8,0},{12,4},{16,24},{20,28},{24,16},{28,20},{1,9},{5... | collective-permute-start | bytes 884744 | tf_op jit(solution)/shard_map/ppermute | solution.py:603
  41.0 1.8 %collective-permute-start.7 = (bf16[96,1536]{1,0:T(8,128)(2,1)}, bf16[96,1536]{1,0:T(8,128)(2,1)S(1)}, u32[]{:S(2)}, u32[]{:S(2)}) collective-permute-start(bf16[96,1536]{1,0:T(8,128)(2,1)} %collective-permute-done.3.refs_0_), channel_id=1, source_target_pairs={{0,4},{4,0},{8,12},{12,8},{16,20},{20,16},{24,28},{28,24},{1,5},{5... | collective-permute-start | bytes 884744 | tf_op jit(solution)/shard_map/ppermute | solution.py:603
  41.2 2.1 %collective-permute-start.8 = (bf16[96,1536]{1,0:T(8,128)(2,1)}, bf16[96,1536]{1,0:T(8,128)(2,1)S(1)}, u32[]{:S(2)}, u32[]{:S(2)}) collective-permute-start(bf16[96,1536]{1,0:T(8,128)(2,1)} %collective-permute-done.4.refs_1_), channel_id=1, source_target_pairs={{0,4},{4,0},{8,12},{12,8},{16,20},{20,16},{24,28},{28,24},{1,5},{5... | collective-permute-start | bytes 884744 | tf_op jit(solution)/shard_map/ppermute | solution.py:603
  47.6 42.7 %slice-start.4 = ((s8[4325376]{0:T(1024)(128)(4,1)}), s8[131072]{0:T(1024)(128)(4,1)S(1)}, s32[]{:S(2)}) async-start(s8[4325376]{0:T(1024)(128)(4,1)} %bitcast.25), calls=%async_computation.4 | async-start | bytes 262144
  56.6 33.7 %slice-start.5 = ((s8[4325376]{0:T(1024)(128)(4,1)}), s8[4194304]{0:T(1024)(128)(4,1)S(1)}, s32[]{:S(2)}) async-start(s8[4325376]{0:T(1024)(128)(4,1)} %bitcast.25), calls=%async_computation.5 | async-start | bytes 8388608
  62.6 11.4 %collective-permute-start.10 = (bf16[1152,128]{1,0:T(8,128)(2,1)S(1)}, bf16[1152,128]{1,0:T(8,128)(2,1)S(1)}, u32[]{:S(2)}, u32[]{:S(2)}) collective-permute-start(bf16[1152,128]{1,0:T(8,128)(2,1)S(1)} %get-tuple-element.56.refs_5_), channel_id=1, source_target_pairs={{0,8},{4,12},{8,0},{12,4},{16,24},{20,28},{24,16},{28,20},{1,9},{5... | collective-permute-start | bytes 884744 | tf_op jit(solution)/shard_map/ppermute | solution.py:603
  64.4 9.5 %collective-permute-start.11 = (bf16[1152,128]{1,0:T(8,128)(2,1)S(1)}, bf16[1152,128]{1,0:T(8,128)(2,1)S(1)}, u32[]{:S(2)}, u32[]{:S(2)}) collective-permute-start(bf16[1152,128]{1,0:T(8,128)(2,1)S(1)} %get-tuple-element.56.refs_5_), channel_id=1, source_target_pairs={{0,16},{4,20},{8,24},{12,28},{16,0},{20,4},{24,8},{28,12},{1,17},{... | collective-permute-start | bytes 884744 | tf_op jit(solution)/shard_map/ppermute | solution.py:603
  66.0 8.0 %collective-permute-start.9 = (bf16[1152,128]{1,0:T(8,128)(2,1)S(1)}, bf16[1152,128]{1,0:T(8,128)(2,1)S(1)}, u32[]{:S(2)}, u32[]{:S(2)}) collective-permute-start(bf16[1152,128]{1,0:T(8,128)(2,1)S(1)} %get-tuple-element.56.refs_5_), channel_id=1, source_target_pairs={{0,4},{4,0},{8,12},{12,8},{16,20},{20,16},{24,28},{28,24},{1,5},{5... | collective-permute-start | bytes 884744 | tf_op jit(solution)/shard_map/ppermute | solution.py:603
  74.0 6.7 %collective-permute-start.15 = (bf16[576,128]{1,0:T(8,128)(2,1)S(1)}, bf16[576,128]{1,0:T(8,128)(2,1)S(1)}, u32[]{:S(2)}, u32[]{:S(2)}) collective-permute-start(bf16[576,128]{1,0:T(8,128)(2,1)S(1)} %slice.20), channel_id=1, source_target_pairs={{0,16},{4,20},{8,24},{12,28},{16,0},{20,4},{24,8},{28,12},{1,17},{... | collective-permute-start | bytes 442376 | tf_op jit(solution)/shard_map/ppermute | solution.py:603
  74.8 12.1 %collective-permute-start.13 = (bf16[1152,128]{1,0:T(8,128)(2,1)S(1)}, bf16[1152,128]{1,0:T(8,128)(2,1)S(1)}, u32[]{:S(2)}, u32[]{:S(2)}) collective-permute-start(bf16[1152,128]{1,0:T(8,128)(2,1)S(1)} %attention.2.refs_5_), channel_id=1, source_target_pairs={{0,8},{4,12},{8,0},{12,4},{16,24},{20,28},{24,16},{28,20},{1,9},{5... | collective-permute-start | bytes 884744 | tf_op jit(solution)/shard_map/ppermute | solution.py:603
  75.3 12.1 %collective-permute-start.14 = (bf16[1152,128]{1,0:T(8,128)(2,1)S(1)}, bf16[1152,128]{1,0:T(8,128)(2,1)S(1)}, u32[]{:S(2)}, u32[]{:S(2)}) collective-permute-start(bf16[1152,128]{1,0:T(8,128)(2,1)S(1)} %attention.2.refs_5_), channel_id=1, source_target_pairs={{0,16},{4,20},{8,24},{12,28},{16,0},{20,4},{24,8},{28,12},{1,17},{... | collective-permute-start | bytes 884744 | tf_op jit(solution)/shard_map/ppermute | solution.py:603
  76.6 10.9 %collective-permute-start.21 = (bf16[1152,128]{1,0:T(8,128)(2,1)S(1)}, bf16[1152,128]{1,0:T(8,128)(2,1)S(1)}, u32[]{:S(2)}, u32[]{:S(2)}) collective-permute-start(bf16[1152,128]{1,0:T(8,128)(2,1)S(1)} %collective-permute-done.10.refs_7_), channel_id=1, source_target_pairs={{0,4},{4,0},{8,12},{12,8},{16,20},{20,16},{24,28},{28,24},{1,5},{5... | collective-permute-start | bytes 884744 | tf_op jit(solution)/shard_map/ppermute | solution.py:603
  76.6 11.5 %collective-permute-start.22 = (bf16[1152,128]{1,0:T(8,128)(2,1)S(1)}, bf16[1152,128]{1,0:T(8,128)(2,1)S(1)}, u32[]{:S(2)}, u32[]{:S(2)}) collective-permute-start(bf16[1152,128]{1,0:T(8,128)(2,1)S(1)} %collective-permute-done.11.refs_9_), channel_id=1, source_target_pairs={{0,4},{4,0},{8,12},{12,8},{16,20},{20,16},{24,28},{28,24},{1,5},{5... | collective-permute-start | bytes 884744 | tf_op jit(solution)/shard_map/ppermute | solution.py:603
  80.7 6.2 %collective-permute-start.16 = (bf16[576,128]{1,0:T(8,128)(2,1)S(1)}, bf16[576,128]{1,0:T(8,128)(2,1)S(1)}, u32[]{:S(2)}, u32[]{:S(2)}) collective-permute-start(bf16[576,128]{1,0:T(8,128)(2,1)S(1)} %slice.21), channel_id=1, source_target_pairs={{0,8},{4,12},{8,0},{12,4},{16,24},{20,28},{24,16},{28,20},{1,9},{5... | collective-permute-start | bytes 442376 | tf_op jit(solution)/shard_map/ppermute | solution.py:603
  86.9 1.4 %collective-permute-start.23 = (bf16[576,128]{1,0:T(8,128)(2,1)S(1)}, bf16[576,128]{1,0:T(8,128)(2,1)S(1)}, u32[]{:S(2)}, u32[]{:S(2)}) collective-permute-start(bf16[576,128]{1,0:T(8,128)(2,1)S(1)} %collective-permute-done.15.refs_11_), channel_id=1, source_target_pairs={{0,4},{4,0},{8,12},{12,8},{16,20},{20,16},{24,28},{28,24},{1,5},{5... | collective-permute-start | bytes 442376 | tf_op jit(solution)/shard_map/ppermute | solution.py:603
  86.9 2.9 %collective-permute-start.24 = (bf16[576,128]{1,0:T(8,128)(2,1)S(1)}, bf16[576,128]{1,0:T(8,128)(2,1)S(1)}, u32[]{:S(2)}, u32[]{:S(2)}) collective-permute-start(bf16[576,128]{1,0:T(8,128)(2,1)S(1)} %collective-permute-done.16.refs_12_), channel_id=1, source_target_pairs={{0,4},{4,0},{8,12},{12,8},{16,20},{20,16},{24,28},{28,24},{1,5},{5... | collective-permute-start | bytes 442376 | tf_op jit(solution)/shard_map/ppermute | solution.py:603
  87.4 10.2 %collective-permute-start.12 = (bf16[1152,128]{1,0:T(8,128)(2,1)S(1)}, bf16[1152,128]{1,0:T(8,128)(2,1)S(1)}, u32[]{:S(2)}, u32[]{:S(2)}) collective-permute-start(bf16[1152,128]{1,0:T(8,128)(2,1)S(1)} %attention.2.refs_5_), channel_id=1, source_target_pairs={{0,4},{4,0},{8,12},{12,8},{16,20},{20,16},{24,28},{28,24},{1,5},{5... | collective-permute-start | bytes 884744 | tf_op jit(solution)/shard_map/ppermute | solution.py:603
  87.5 10.0 %collective-permute-start.17 = (bf16[1152,128]{1,0:T(8,128)(2,1)S(1)}, bf16[1152,128]{1,0:T(8,128)(2,1)S(1)}, u32[]{:S(2)}, u32[]{:S(2)}) collective-permute-start(bf16[1152,128]{1,0:T(8,128)(2,1)S(1)} %collective-permute-done.13.refs_7_), channel_id=1, source_target_pairs={{0,4},{4,0},{8,12},{12,8},{16,20},{20,16},{24,28},{28,24},{1,5},{5... | collective-permute-start | bytes 884744 | tf_op jit(solution)/shard_map/ppermute | solution.py:603
  88.1 9.5 %collective-permute-start.18 = (bf16[1152,128]{1,0:T(8,128)(2,1)S(1)}, bf16[1152,128]{1,0:T(8,128)(2,1)S(1)}, u32[]{:S(2)}, u32[]{:S(2)}) collective-permute-start(bf16[1152,128]{1,0:T(8,128)(2,1)S(1)} %collective-permute-done.14.refs_9_), channel_id=1, source_target_pairs={{0,4},{4,0},{8,12},{12,8},{16,20},{20,16},{24,28},{28,24},{1,5},{5... | collective-permute-start | bytes 884744 | tf_op jit(solution)/shard_map/ppermute | solution.py:603
  88.2 8.8 %collective-permute-start.19 = (bf16[576,128]{1,0:T(8,128)(2,1)S(1)}, bf16[576,128]{1,0:T(8,128)(2,1)S(1)}, u32[]{:S(2)}, u32[]{:S(2)}) collective-permute-start(bf16[576,128]{1,0:T(8,128)(2,1)S(1)} %slice.22), channel_id=1, source_target_pairs={{0,16},{4,20},{8,24},{12,28},{16,0},{20,4},{24,8},{28,12},{1,17},{... | collective-permute-start | bytes 442376 | tf_op jit(solution)/shard_map/ppermute | solution.py:603
  89.8 7.2 %collective-permute-start.20 = (bf16[576,128]{1,0:T(8,128)(2,1)S(1)}, bf16[576,128]{1,0:T(8,128)(2,1)S(1)}, u32[]{:S(2)}, u32[]{:S(2)}) collective-permute-start(bf16[576,128]{1,0:T(8,128)(2,1)S(1)} %slice.23), channel_id=1, source_target_pairs={{0,8},{4,12},{8,0},{12,4},{16,24},{20,28},{24,16},{28,20},{1,9},{5... | collective-permute-start | bytes 442376 | tf_op jit(solution)/shard_map/ppermute | solution.py:603
  97.0 1.4 %collective-permute-start.25 = (bf16[576,128]{1,0:T(8,128)(2,1)S(1)}, bf16[576,128]{1,0:T(8,128)(2,1)S(1)}, u32[]{:S(2)}, u32[]{:S(2)}) collective-permute-start(bf16[576,128]{1,0:T(8,128)(2,1)S(1)} %collective-permute-done.19.refs_11_), channel_id=1, source_target_pairs={{0,4},{4,0},{8,12},{12,8},{16,20},{20,16},{24,28},{28,24},{1,5},{5... | collective-permute-start | bytes 442376 | tf_op jit(solution)/shard_map/ppermute | solution.py:603
  97.1 1.6 %collective-permute-start.26 = (bf16[576,128]{1,0:T(8,128)(2,1)S(1)}, bf16[576,128]{1,0:T(8,128)(2,1)S(1)}, u32[]{:S(2)}, u32[]{:S(2)}) collective-permute-start(bf16[576,128]{1,0:T(8,128)(2,1)S(1)} %collective-permute-done.20.refs_12_), channel_id=1, source_target_pairs={{0,4},{4,0},{8,12},{12,8},{16,20},{20,16},{24,28},{28,24},{1,5},{5... | collective-permute-start | bytes 442376 | tf_op jit(solution)/shard_map/ppermute | solution.py:603
  112.8 10.3 %collective-permute-start.27 = (bf16[672,128]{1,0:T(8,128)(2,1)S(1)}, bf16[672,128]{1,0:T(8,128)(2,1)S(1)}, u32[]{:S(2)}, u32[]{:S(2)}) collective-permute-start(bf16[672,128]{1,0:T(8,128)(2,1)S(1)} %get-tuple-element.66), channel_id=1, source_target_pairs={{0,1},{1,0},{2,3},{3,2},{4,5},{5,4},{6,7},{7,6},{8,9},{9,8},{10,11... | collective-permute-start | bytes 516104 | tf_op jit(solution)/shard_map/ppermute | solution.py:735
  112.9 10.3 %collective-permute-start.28 = (bf16[672,128]{1,0:T(8,128)(2,1)S(1)}, bf16[672,128]{1,0:T(8,128)(2,1)S(1)}, u32[]{:S(2)}, u32[]{:S(2)}) collective-permute-start(bf16[672,128]{1,0:T(8,128)(2,1)S(1)} %get-tuple-element.67), channel_id=1, source_target_pairs={{0,2},{1,3},{2,0},{3,1},{4,6},{5,7},{6,4},{7,5},{8,10},{9,11},{10,... | collective-permute-start | bytes 516104 | tf_op jit(solution)/shard_map/ppermute | solution.py:735
  115.8 13.4 %collective-permute-start.29 = (bf16[672,128]{1,0:T(8,128)(2,1)S(1)}, bf16[672,128]{1,0:T(8,128)(2,1)S(1)}, u32[]{:S(2)}, u32[]{:S(2)}) collective-permute-start(bf16[672,128]{1,0:T(8,128)(2,1)S(1)} %get-tuple-element.68), channel_id=1, source_target_pairs={{0,3},{1,2},{2,1},{3,0},{4,7},{5,6},{6,5},{7,4},{8,11},{9,10},{10,... | collective-permute-start | bytes 516104 | tf_op jit(solution)/shard_map/ppermute | solution.py:735
  (24 other events, 217.2 us)

commit v6 on v5

--- a/solution.py
+++ b/solution.py
@@ -147,6 +147,7 @@
 
 
 LANES = 128
+CHIP, CORE, PACK, IDS = 0, 1, 2, 3
 BLOCK = 256
 POSITIONS = 64
 NEGATIVE = -1e30
@@ -212,17 +213,17 @@
     )(*map(in_hbm, operands))
 
 
-def qkv_kernel(count, place, *refs):
+def qkv_kernel(count, flip, info, *refs):
     first, second = refs[:count], refs[count : 2 * count]
     table, gain, weight = refs[2 * count : 2 * count + 3]
     inputs_out, qkv_out, label_out = refs[-3:]
     mine, other = stacked(first), stacked(second)
-    leads = place[1] == 0
+    leads = info[CORE] == 0
     ahead = jnp.where(leads, mine, other)
     behind = jnp.where(leads, other, mine)
     both = jnp.concatenate([ahead, behind], axis=0)
     rows = both.shape[0]
-    at = pl.ds(pl.multiple_of(place[0] * rows, rows), rows)
+    at = pl.ds(pl.multiple_of((info[CHIP] ^ flip) * rows, rows), rows)
     inputs_out[at, :] = both[:, :D]
     label_out[at, :] = both[:, D:]
     labels = both[:, D:].astype(jnp.float32)
@@ -268,14 +269,14 @@
         qkv_out[at, low : low + 2 * LANES] = part.astype(jnp.bfloat16)
 
 
-def qkv_call(place, first, second, table, gain, weight, earlier, total):
+def qkv_call(info, flip, first, second, table, gain, weight, earlier, total):
     rows = 2 * sum(piece.shape[0] for piece in first)
     widths = (D, 10 * LANES, LANES)
     operands = [*first, *second, table, gain, in_vmem(weight)]
     vmem = pl.BlockSpec(memory_space=pltpu.VMEM)
     held = [in_vmem(one) for one in earlier]
     return pl.pallas_call(
-        functools.partial(qkv_kernel, len(first)),
+        functools.partial(qkv_kernel, len(first), flip),
         in_specs=[pl.BlockSpec(memory_space=pltpu.SMEM)]
         + [vmem] * (len(operands) + len(earlier)),
         out_specs=[vmem] * len(widths),
@@ -288,7 +289,7 @@
             transcendentals=rows,
         ),
         name="norm_qkv",
-    )(place, *operands, *held)
+    )(info, *operands, *held)
 
 
 def segment_row(labels):
@@ -301,7 +302,7 @@
     )
 
 
-def attention_kernel(start, owners, labels, block, *refs):
+def attention_kernel(start, first_owner, images, info, labels, block, *refs):
     out, *rest = refs
     scores, high, rows_scratch = rest[-3:]
     rows = high.shape[1]
@@ -366,10 +367,10 @@
         row = lax.broadcasted_iota(jnp.int32, note.shape, 0)
         lane = lax.broadcasted_iota(jnp.int32, note.shape, 1)
         found = jnp.zeros(note.shape, jnp.float32)
-        for image in range(owners.shape[0]):
+        for image in range(images):
             below = jnp.sum(jnp.where(one_row < image, 0.25, 0.0), axis=1, keepdims=True)
             inside = jnp.sum(jnp.where(one_row == image, 0.25, 0.0), axis=1, keepdims=True)
-            here = row == owners[image]
+            here = row == info[first_owner + image]
             for place, number in enumerate((below, inside)):
                 upper = jnp.floor(number * (1.0 / 16))
                 found = jnp.where(here & (lane == 2 * place), upper, found)
@@ -377,14 +378,14 @@
         note[...] = found.astype(jnp.bfloat16)
 
 
-def attention_call(start, rows, owners, labels, block, noted):
+def attention_call(start, rows, first_owner, info, labels, block, noted):
     total = block.shape[0]
     vmem = pl.BlockSpec(memory_space=pltpu.VMEM)
     shapes = [jax.ShapeDtypeStruct((rows + rows // 2, LANES), jnp.bfloat16)]
     if noted:
         shapes.append(jax.ShapeDtypeStruct((16, LANES), jnp.bfloat16))
     return pl.pallas_call(
-        functools.partial(attention_kernel, start),
+        functools.partial(attention_kernel, start, first_owner, info.shape[0] - first_owner),
         in_specs=[pl.BlockSpec(memory_space=pltpu.SMEM), vmem, vmem],
         out_specs=[vmem] * len(shapes),
         out_shape=shapes,
@@ -400,16 +401,18 @@
             transcendentals=rows * total,
         ),
         name="attention",
-    )(owners, in_vmem(labels), in_vmem(block))
-
-
-def prepare_kernel(shards, ids, out_weight, merge_weight, qkv_weight, spread, *refs):
-    out, merge, qkv, qkv_buffer, spread_buffer, sems = refs
+    )(info, in_vmem(labels), in_vmem(block))
+
+
+def prepare_kernel(shards, info, out_weight, merge_weight, qkv_weight, spread, *refs):
+    *rows, out, merge, qkv, qkv_buffer, spread_buffer, sems = refs
+    for row, row_out in zip(rows[: len(rows) // 2], rows[len(rows) // 2 :]):
+        row_out[...] = row[...].astype(jnp.float32)[None, :]
     rest = 2 * HD - LANES
     copies = [(qkv_weight, qkv_buffer), (spread, spread_buffer)]
     out[shards * LANES :] = jnp.zeros((shards // 2 * LANES, D), jnp.bfloat16)
     for place in range(shards):
-        start = pl.multiple_of(ids[place] * (2 * HD), 16)
+        start = pl.multiple_of(info[IDS + place] * (2 * HD), 16)
         to = (shards + place // 2) * LANES + place % 2 * rest
         copies.append(
             (out_weight.at[pl.ds(start, LANES), :], out.at[pl.ds(place * LANES, LANES), :])
@@ -431,17 +434,19 @@
         copy.wait()
 
 
-def prepare_call(ids, out_weight, merge_weight, qkv_weight, spread):
-    shards = ids.shape[0]
+def prepare_call(shards, info, out_weight, merge_weight, qkv_weight, spread, rows):
     anywhere = pl.BlockSpec(memory_space=pl.ANY)
     vmem = pl.BlockSpec(memory_space=pltpu.VMEM)
     operands = (out_weight, merge_weight, qkv_weight, spread)
     shapes = [(shards * LANES * 3 // 2, D), merge_weight.shape, (spread.shape[0], D)]
     return pl.pallas_call(
         functools.partial(prepare_kernel, shards),
-        in_specs=[pl.BlockSpec(memory_space=pltpu.SMEM)] + [anywhere] * len(operands),
-        out_specs=[vmem] * len(shapes),
-        out_shape=[pltpu.VMEM(shape, jnp.bfloat16) for shape in shapes],
+        in_specs=[pl.BlockSpec(memory_space=pltpu.SMEM)]
+        + [anywhere] * len(operands)
+        + [vmem] * len(rows),
+        out_specs=[vmem] * (len(rows) + len(shapes)),
+        out_shape=[pltpu.VMEM((1, row.shape[0]), jnp.float32) for row in rows]
+        + [pltpu.VMEM(shape, jnp.bfloat16) for shape in shapes],
         scratch_shapes=[
             pltpu.VMEM(qkv_weight.shape, jnp.bfloat16),
             pltpu.VMEM(spread.shape, jnp.bfloat16),
@@ -454,7 +459,7 @@
             transcendentals=0,
         ),
         name="prepare",
-    )(ids, *map(in_hbm, operands))
+    )(info, *map(in_hbm, operands), *rows)
 
 
 def merge_kernel(start, counts, packs, last, *refs):
@@ -508,7 +513,7 @@
     if not last:
         refs[0][...] = total
         return
-    me, note, *earlier = refs[:-packs]
+    info, note, *earlier = refs[:-packs]
     outs = refs[-packs:]
     total = jnp.concatenate([*[one[...] for one in earlier], total], axis=0)
     whole = total.shape[1] // LANES
@@ -518,7 +523,7 @@
     slot = lax.broadcasted_iota(jnp.int32, (most, total.shape[0]), 0)
     row = lax.broadcasted_iota(jnp.int32, (most, total.shape[0]), 1)
     for place, out in enumerate(outs):
-        found = jnp.where(note_row == (me[0] ^ place), notes, 0.0)
+        found = jnp.where(note_row == (info[PACK] ^ place), notes, 0.0)
         found = jnp.sum(found, axis=0, keepdims=True)
         first = (16.0 * found[:, :1] + found[:, 1:2]).astype(jnp.int32)
         length = (16.0 * found[:, 2:3] + found[:, 3:4]).astype(jnp.int32)
@@ -565,14 +570,14 @@
     )(*operands)
 
 
-def place_kernel(me, *refs):
+def place_kernel(info, *refs):
     blocks, out = refs[:-1], refs[-1]
     most, width = out.shape[1:]
     whole = width // LANES
     half = most // 2
     middle = LANES // 2
     for place, block in enumerate(blocks):
-        target = me[0] ^ place
+        target = info[PACK] ^ place
         for column in range(whole):
             out[target, :, column * LANES : (column + 1) * LANES] = block[
                 column * most : (column + 1) * most, :
@@ -581,7 +586,7 @@
         out[target, half:, whole * LANES :] = block[whole * most :, middle:]
 
 
-def place_call(me, blocks, most, width):
+def place_call(info, blocks, most, width):
     fixed = lambda shape: pl.BlockSpec(shape, lambda i: (0,) * len(shape))
     shape = (len(blocks), most, width)
     return pl.pallas_call(
@@ -595,7 +600,7 @@
             flops=0, bytes_accessed=4 * len(blocks) * most * width, transcendentals=0
         ),
         name="place_rows",
-    )(me, *blocks)
+    )(info, *blocks)
 
 
 def send_seq(value, flip):
@@ -607,13 +612,35 @@
     return lax.optimization_barrier((tuple(values), earlier))[0]
 
 
+def halves_kernel(across_x, across_y, upper, lower):
+    half = upper.shape[0]
+    upper[...] = across_x[:half]
+    lower[...] = across_y[half:]
+
+
+def halves_call(across_x, across_y):
+    vmem = pl.BlockSpec(memory_space=pltpu.VMEM)
+    shape = (across_x.shape[0] // 2, across_x.shape[1])
+    return pl.pallas_call(
+        halves_kernel,
+        in_specs=[vmem] * 2,
+        out_specs=[vmem] * 2,
+        out_shape=[jax.ShapeDtypeStruct(shape, across_x.dtype)] * 2,
+        compiler_params=pltpu.CompilerParams(vmem_limit_bytes=4 << 20),
+        cost_estimate=pl.CostEstimate(
+            flops=0, bytes_accessed=4 * across_x.size, transcendentals=0
+        ),
+        name="halves",
+    )(across_x, across_y)
+
+
 def near_shards(value):
     return [send_seq(value, 1), send_seq(value, 2), send_seq(value, 4)]
 
 
 def far_shards(across_x, across_y):
-    half = across_x.shape[0] // 2
-    return [send_seq(across_x[:half], 4), send_seq(across_y[half:], 2)]
+    upper, lower = halves_call(across_x, across_y)
+    return [send_seq(upper, 4), send_seq(lower, 2)]
 
 
 def weight_order(heads_here):
@@ -679,17 +706,21 @@
     order = weight_order(heads_here)
     spread = (order[:, None] == np.arange(qkv_weight.shape[1])[None, :]).astype(jnp.bfloat16)
     table = jnp.asarray(angle_table(heads_here))
-    gain = norm_gain.astype(jnp.float32)[None, :]
-    merge_gain_row = merge_gain.astype(jnp.float32)[None, :]
-    bias = merge_bias.astype(jnp.float32)[None, :]
-    ids = jnp.stack([me ^ place for place in range(shards)])
-    ordered, merge_rows, weight = prepare_call(
-        ids, out_weight, merge_weight.T, qkv_weight.T, jnp.asarray(spread)
-    )
-
     chip, core = me // 2, me % 2
+    info = [chip, core, pack, *[me ^ place for place in range(shards)]]
+    info = jnp.concatenate([jnp.stack(info), image_owner[0]])
+    gain, merge_gain_row, bias, ordered, merge_rows, weight = prepare_call(
+        shards,
+        info,
+        out_weight,
+        merge_weight.T,
+        qkv_weight.T,
+        jnp.asarray(spread),
+        (norm_gain, merge_gain, merge_bias),
+    )
+
     project = lambda place, first, second, earlier: qkv_call(
-        jnp.stack([chip ^ place, core]), first, second, table, gain, weight, earlier, total
+        info, place, first, second, table, gain, weight, earlier, total
     )
     buffers = project(0, [value], [own_swap], ())
     across_x, across_y = after([across_x, across_y], buffers[2], ordered)
@@ -703,7 +734,7 @@
     starts = [sum(CHUNKS[:number]) for number in range(len(CHUNKS))]
     attended, note = [], None
     for start, rows in zip(starts, CHUNKS):
-        made = attention_call(start, rows, image_owner[0], labels, block, note is None)
+        made = attention_call(start, rows, IDS + shards, info, labels, block, note is None)
         note = made[1] if note is None else note
         value = made[0]
         if attended:
@@ -726,7 +757,7 @@
         sources = [[one] for one in near] + [far, [send_seq(one, 1) for one in far]]
         route = ()
         if number == len(CHUNKS) - 1:
-            route = (pack[None], most, note, *projected)
+            route = (info, most, note, *projected)
         made = merge_call(
             start, rows, sources, inputs, ordered, merge_gain_row, merge_rows, bias, packs, route
         )
@@ -735,7 +766,7 @@
         lax.ppermute(made[flip], "pack", [(z, z ^ flip) for z in range(packs)])
         for flip in range(1, packs)
     ]
-    return place_call(pack[None], blocks, most, merge_weight.shape[1])[None]
+    return place_call(info, blocks, most, merge_weight.shape[1])[None]
 
 
 def local(*arguments):

time: 132 us -> 103 us (0.78)
  local copies, waits for them, and re-layouts: 35.7 us -> 2.79 us
  waiting for transfers between devices: 24 us -> 28.2 us
  starting transfers between devices: 21.6 us -> 23.3 us
  Pallas kernels: 48.3 us -> 46.7 us
    unnamed x52 -> x8, local copies, waits for them, and re-layouts: 33.9 us -> 2.05 us
    ppermute x27, waiting for transfers between devices: 12 us -> 17 us  [send_seq(): return lax.ppermute(value, 'seq', [(i, i ^ flip) for i in range(size)])]
    pallas_call x6 -> x9, Pallas kernels: 26 us -> 23.8 us  [the longest x2 13.9 us: attention_call(): pl.pallas_call(functools.partial(attention_kernel, start, first_owner, in...]
    ppermute x27, starting transfers between devices: 17.2 us -> 18.9 us  [send_seq(): return lax.ppermute(value, 'seq', [(i, i ^ flip) for i in range(size)])]
  transfers between devices with their start and end apart: 30 -> 30, of which waited for: 9 -> 15; matrix products, arithmetic and copies ran while one was open for 2% -> 1% of each run, Pallas kernels for 22% -> 26%
where the time goes in v6:
time: 103 us; the launch traced here: 101 us
  Pallas kernels  46.7 us (45%)
  waiting for transfers between devices  28.2 us (27%)
  starting transfers between devices  23.3 us (23%)
  local copies, waits for them, and re-layouts  2.79 us (3%)
    ppermute x27, starting transfers between devices, send_seq(): return lax.ppermute(value, 'seq', [(i, i ^ flip) for i in range(size)])  18.9 us
    ppermute x27, waiting for transfers between devices, send_seq(): return lax.ppermute(value, 'seq', [(i, i ^ flip) for i in range(size)])  17 us
    pallas_call x2, Pallas kernels, merge_call(): pl.pallas_call(functools.partial(merge_kernel, start, [len(source) for so...  14.7 us
    pallas_call x2, Pallas kernels, attention_call(): pl.pallas_call(functools.partial(attention_kernel, start, first_owner, in...  13.9 us
    ppermute x3, waiting for transfers between devices, fast_local(): lax.ppermute(made[flip], 'pack', [(z, z ^ flip) for z in range(packs)])  11.2 us
    pallas_call x4, Pallas kernels, qkv_call(): pl.pallas_call(functools.partial(qkv_kernel, len(first), flip), in_specs=...  9.83 us
    pallas_call x1, Pallas kernels, prepare_call(): pl.pallas_call(functools.partial(prepare_kernel, shards), in_specs=[pl.Bl...  5.1 us
    ppermute x3, starting transfers between devices, fast_local(): lax.ppermute(made[flip], 'pack', [(z, z ^ flip) for z in range(packs)])  4.44 us
  transfers between devices with their start and end apart: 30, of which 15 were waited for; matrix products, arithmetic and copies ran while one was open for 1% of the time, Pallas kernels for 26%

profile of v6, /device:TPU:0, one launch (start us, length us, event | category | flops | bytes accessed | tf_op | source)
XLA Modules:
  0.0 101.2 jit_solution(8380016084563889661)
XLA Ops:
  0.0 1.5 %payload.1.refs_0_ = bf16[192,1536]{1,0:T(8,128)(2,1)S(1)} custom-call(s32[1,192]{1,0:T(1,128)} %segments.1, s32[1,192]{1,0:T(1,128)} %rows.1, s32[1,192]{1,0:T(1,128)} %columns.1, s32[1,192]{1,0:T(1,128)} %mask.1, bf16[1408]{0:T(1024)(128)(2,1)} %embed.1, bf16[1,192,1408]{2,1,0:T(8,128)(2,1)} %patches.1), custom_call_target="tpu_custom_call" | custom-call | flops 270336 | bytes 1081344 | tf_op jit(solution)/shard_map/payload/pallas_call | solution.py:202
  2.0 2.6 %collective-permute-start = (bf16[192,1536]{1,0:T(8,128)(2,1)S(1)}, bf16[192,1536]{1,0:T(8,128)(2,1)S(1)}, u32[]{:S(2)}, u32[]{:S(2)}) collective-permute-start(bf16[192,1536]{1,0:T(8,128)(2,1)S(1)} %payload.1.refs_0_), channel_id=1, source_target_pairs={{0,8},{4,12},{8,0},{12,4},{16,24},{20,28},{24,16},{28,20},{1,9},{5... | collective-permute-start | bytes 1769480 | tf_op jit(solution)/shard_map/ppermute | solution.py:608
  4.6 1.5 %collective-permute-start.1 = (bf16[192,1536]{1,0:T(8,128)(2,1)S(1)}, bf16[192,1536]{1,0:T(8,128)(2,1)S(1)}, u32[]{:S(2)}, u32[]{:S(2)}) collective-permute-start(bf16[192,1536]{1,0:T(8,128)(2,1)S(1)} %payload.1.refs_0_), channel_id=1, source_target_pairs={{0,16},{4,20},{8,24},{12,28},{16,0},{20,4},{24,8},{28,12},{1,17},{... | collective-permute-start | bytes 1769480 | tf_op jit(solution)/shard_map/ppermute | solution.py:608
  6.1 0.7 concatenate.3.info.refs_15_
  8.9 5.1 %prepare.1 = (f32[1,1408]{1,0:T(1,128)S(1)}, f32[1,1408]{1,0:T(1,128)S(1)}, f32[1,448]{1,0:T(1,128)S(1)}, bf16[1536,1408]{1,0:T(8,128)(2,1)S(1)}, bf16[448,5632]...) custom-call(s32[15]{0:T(128)S(1)} %concatenate.3.info.refs_15_, bf16[1408,1408]{1,0:T(8,128)(2,1)} %out_weight.1, ...), custom_call_target="tpu_custom_call" | custom-call | flops 1141899264 | bytes 20996096 | tf_op jit(solution)/shard_map/prepare/pallas_call | solution.py:442
  14.0 2.5 %norm_qkv.4 = (bf16[1536,1408]{1,0:T(8,128)(2,1)S(1)}, bf16[1536,1280]{1,0:T(8,128)(2,1)S(1)}, bf16[1536,128]{1,0:T(8,128)(2,1)S(1)}) custom-call(s32[15]{0:T(128)S(1)} %concatenate.3.info.refs_15_, bf16[192,1536]{1,0:T(8,128)(2,1)S(1)} %payload.1.refs_0_, bf16[192,1536]{1,0:T(8,128)(2,1)S(1)} %collective-permute-done.2.refs_1_, ...), custom_call_target="tpu_custom_call" | custom-call | flops 2491416576 | bytes 6488064 | tf_op jit(solution)/shard_map/norm_qkv/pallas_call | solution.py:278
  16.5 2.0 %collective-permute-done.across_x.refs_0_ = bf16[192,1536]{1,0:T(8,128)(2,1)S(1)} collective-permute-done((bf16[192,1536]{1,0:T(8,128)(2,1)S(1)}, bf16[192,1536]{1,0:T(8,128)(2,1)S(1)}, u32[]{:S(2)}, u32[]{:S(2)}) %collective-permute-start) | collective-permute-done | bytes 589856 | tf_op jit(solution)/shard_map/ppermute | solution.py:608
  18.5 1.5 %collective-permute-done.1.across_y.refs_0_ = bf16[192,1536]{1,0:T(8,128)(2,1)S(1)} collective-permute-done((bf16[192,1536]{1,0:T(8,128)(2,1)S(1)}, bf16[192,1536]{1,0:T(8,128)(2,1)S(1)}, u32[]{:S(2)}, u32[]{:S(2)}) %collective-permute-start.1) | collective-permute-done | bytes 589856 | tf_op jit(solution)/shard_map/ppermute | solution.py:608
  20.5 1.6 %collective-permute-start.3 = (bf16[96,1536]{1,0:T(8,128)(2,1)S(1)}, bf16[96,1536]{1,0:T(8,128)(2,1)S(1)}, u32[]{:S(2)}, u32[]{:S(2)}) collective-permute-start(bf16[96,1536]{1,0:T(8,128)(2,1)S(1)} %get-tuple-element.52), channel_id=1, source_target_pairs={{0,16},{4,20},{8,24},{12,28},{16,0},{20,4},{24,8},{28,12},{1,17},{... | collective-permute-start | bytes 884744 | tf_op jit(solution)/shard_map/ppermute | solution.py:608
  22.6 2.5 %norm_qkv.5 = (bf16[1536,1408]{1,0:T(8,128)(2,1)S(1)}, bf16[1536,1280]{1,0:T(8,128)(2,1)S(1)}, bf16[1536,128]{1,0:T(8,128)(2,1)S(1)}) custom-call(s32[15]{0:T(128)S(1)} %concatenate.3.info.refs_15_, bf16[192,1536]{1,0:T(8,128)(2,1)S(1)} %collective-permute-done.across_x.refs_0_, ...), custom_call_target="tpu_custom_call", output_to_operand_aliasing={{0}: (6, {}), {1}: (7, {}), {2}: (8, {})} | custom-call | flops 2491416576 | bytes 6488064 | tf_op jit(solution)/shard_map/norm_qkv/pallas_call | solution.py:278
  25.1 2.4 %norm_qkv.6 = (bf16[1536,1408]{1,0:T(8,128)(2,1)S(1)}, bf16[1536,1280]{1,0:T(8,128)(2,1)S(1)}, bf16[1536,128]{1,0:T(8,128)(2,1)S(1)}) custom-call(s32[15]{0:T(128)S(1)} %concatenate.3.info.refs_15_, bf16[192,1536]{1,0:T(8,128)(2,1)S(1)} %collective-permute-done.1.across_y.refs_0_, ...), custom_call_target="tpu_custom_call", output_to_operand_aliasing={{0}: (6, {}), {1}: (7, {}), {2}: (8, {})} | custom-call | flops 2491416576 | bytes 6488064 | tf_op jit(solution)/shard_map/norm_qkv/pallas_call | solution.py:278
  27.6 1.9 %collective-permute-done.3.refs_0_ = bf16[96,1536]{1,0:T(8,128)(2,1)S(1)} collective-permute-done((bf16[96,1536]{1,0:T(8,128)(2,1)S(1)}, bf16[96,1536]{1,0:T(8,128)(2,1)S(1)}, u32[]{:S(2)}, u32[]{:S(2)}) %collective-permute-start.3) | collective-permute-done | bytes 294944 | tf_op jit(solution)/shard_map/ppermute | solution.py:608
  29.5 1.2 %collective-permute-done.4.refs_1_ = bf16[96,1536]{1,0:T(8,128)(2,1)S(1)} collective-permute-done((bf16[96,1536]{1,0:T(8,128)(2,1)S(1)}, bf16[96,1536]{1,0:T(8,128)(2,1)S(1)}, u32[]{:S(2)}, u32[]{:S(2)}) %collective-permute-start.4) | collective-permute-done | bytes 294944 | tf_op jit(solution)/shard_map/ppermute | solution.py:608
  31.2 1.1 %collective-permute-done.7.refs_2_ = bf16[96,1536]{1,0:T(8,128)(2,1)S(1)} collective-permute-done((bf16[96,1536]{1,0:T(8,128)(2,1)S(1)}, bf16[96,1536]{1,0:T(8,128)(2,1)S(1)}, u32[]{:S(2)}, u32[]{:S(2)}) %collective-permute-start.7) | collective-permute-done | bytes 294944 | tf_op jit(solution)/shard_map/ppermute | solution.py:608
  32.7 2.4 %norm_qkv.7 = (bf16[1536,1408]{1,0:T(8,128)(2,1)S(1)}, bf16[1536,1280]{1,0:T(8,128)(2,1)S(1)}, bf16[1536,128]{1,0:T(8,128)(2,1)S(1)}) custom-call(s32[15]{0:T(128)S(1)} %concatenate.3.info.refs_15_, bf16[96,1536]{1,0:T(8,128)(2,1)S(1)} %collective-permute-done.3.refs_0_, ...), custom_call_target="tpu_custom_call", output_to_operand_aliasing={{0}: (8, {}), {1}: (9, {}), {2}: (10, {})} | custom-call | flops 2491416576 | bytes 6488064 | tf_op jit(solution)/shard_map/norm_qkv/pallas_call | solution.py:278
  35.2 6.9 %attention.3 = (bf16[1152,128]{1,0:T(8,128)(2,1)S(1)}, bf16[16,128]{1,0:T(8,128)(2,1)S(1)}) custom-call(s32[15]{0:T(128)S(1)} %concatenate.3.info.refs_15_, bf16[1536,128]{1,0:T(8,128)(2,1)S(1)} %get-tuple-element.68.labels, bf16[1536,1280]{1,0:T(8,128)(2,1)S(1)} %get-tuple-element.69.block), custom_call_target="tpu_custom_call" | custom-call | flops 3019898880 | bytes 3932160 | tf_op jit(solution)/shard_map/attention/pallas_call | solution.py:387
  43.0 7.0 %attention.2.refs_5_ = bf16[1152,128]{1,0:T(8,128)(2,1)S(1)} custom-call(s32[15]{0:T(128)S(1)} %concatenate.3.info.refs_15_, bf16[1536,128]{1,0:T(8,128)(2,1)S(1)} %get-tuple-element.68.labels, bf16[1536,1280]{1,0:T(8,128)(2,1)S(1)} %get-tuple-element.69.block), custom_call_target="tpu_custom_call" | custom-call | flops 3019898880 | bytes 3932160 | tf_op jit(solution)/shard_map/attention/pallas_call | solution.py:387
  50.1 1.1 %collective-permute-done.10.across_x.refs_7_ = bf16[1152,128]{1,0:T(8,128)(2,1)S(1)} collective-permute-done((bf16[1152,128]{1,0:T(8,128)(2,1)S(1)}, bf16[1152,128]{1,0:T(8,128)(2,1)S(1)}, u32[]{:S(2)}, u32[]{:S(2)}) %collective-permute-start.10) | collective-permute-done | bytes 294944 | tf_op jit(solution)/shard_map/ppermute | solution.py:608
  51.9 1.6 %collective-permute-start.13 = (bf16[1152,128]{1,0:T(8,128)(2,1)S(1)}, bf16[1152,128]{1,0:T(8,128)(2,1)S(1)}, u32[]{:S(2)}, u32[]{:S(2)}) collective-permute-start(bf16[1152,128]{1,0:T(8,128)(2,1)S(1)} %attention.2.refs_5_), channel_id=1, source_target_pairs={{0,8},{4,12},{8,0},{12,4},{16,24},{20,28},{24,16},{28,20},{1,9},{5... | collective-permute-start | bytes 884744 | tf_op jit(solution)/shard_map/ppermute | solution.py:608
  53.5 1.5 %collective-permute-start.14 = (bf16[1152,128]{1,0:T(8,128)(2,1)S(1)}, bf16[1152,128]{1,0:T(8,128)(2,1)S(1)}, u32[]{:S(2)}, u32[]{:S(2)}) collective-permute-start(bf16[1152,128]{1,0:T(8,128)(2,1)S(1)} %attention.2.refs_5_), channel_id=1, source_target_pairs={{0,16},{4,20},{8,24},{12,28},{16,0},{20,4},{24,8},{28,12},{1,17},{... | collective-permute-start | bytes 884744 | tf_op jit(solution)/shard_map/ppermute | solution.py:608
  55.6 1.9 %collective-permute-done.15.refs_11_ = bf16[576,128]{1,0:T(8,128)(2,1)S(1)} collective-permute-done((bf16[576,128]{1,0:T(8,128)(2,1)S(1)}, bf16[576,128]{1,0:T(8,128)(2,1)S(1)}, u32[]{:S(2)}, u32[]{:S(2)}) %collective-permute-start.15) | collective-permute-done | bytes 147488 | tf_op jit(solution)/shard_map/ppermute | solution.py:608
  57.5 2.3 %collective-permute-start.16 = (bf16[576,128]{1,0:T(8,128)(2,1)S(1)}, bf16[576,128]{1,0:T(8,128)(2,1)S(1)}, u32[]{:S(2)}, u32[]{:S(2)}) collective-permute-start(bf16[576,128]{1,0:T(8,128)(2,1)S(1)} %get-tuple-element.75), channel_id=1, source_target_pairs={{0,8},{4,12},{8,0},{12,4},{16,24},{20,28},{24,16},{28,20},{1,9},{5... | collective-permute-start | bytes 442376 | tf_op jit(solution)/shard_map/ppermute | solution.py:608
  59.8 4.3 %collective-permute-done.16.refs_12_ = bf16[576,128]{1,0:T(8,128)(2,1)S(1)} collective-permute-done((bf16[576,128]{1,0:T(8,128)(2,1)S(1)}, bf16[576,128]{1,0:T(8,128)(2,1)S(1)}, u32[]{:S(2)}, u32[]{:S(2)}) %collective-permute-start.16) | collective-permute-done | bytes 147488 | tf_op jit(solution)/shard_map/ppermute | solution.py:608
  65.9 1.6 %collective-permute-start.20 = (bf16[576,128]{1,0:T(8,128)(2,1)S(1)}, bf16[576,128]{1,0:T(8,128)(2,1)S(1)}, u32[]{:S(2)}, u32[]{:S(2)}) collective-permute-start(bf16[576,128]{1,0:T(8,128)(2,1)S(1)} %get-tuple-element.79), channel_id=1, source_target_pairs={{0,8},{4,12},{8,0},{12,4},{16,24},{20,28},{24,16},{28,20},{1,9},{5... | collective-permute-start | bytes 442376 | tf_op jit(solution)/shard_map/ppermute | solution.py:608
  67.6 6.7 %out_merge.2.refs_17_ = bf16[192,448]{1,0:T(8,128)(2,1)S(1)} custom-call(bf16[1536,1408]{1,0:T(8,128)(2,1)S(1)} %get-tuple-element.64.refs_0_, bf16[1536,1408]{1,0:T(8,128)(2,1)S(1)} %get-tuple-element.49.refs_1_, f32[1,1408]{1,0:T(1,128)S(1)} %get-tuple-element.65.refs_2_, bf16[448,5632]{1,0:T(8,128)(2,1)S(1)} %get-tuple-element.66.refs_3_, ...), custom_call_target="tpu_custom_call" | custom-call | flops 7059013632 | bytes 15499264 | tf_op jit(solution)/shard_map/out_merge/pallas_call | solution.py:555
  74.9 0.8 collective-permute-done.25.refs_13_
  75.9 8.0 %out_merge.3 = (bf16[672,128]{1,0:T(8,128)(2,1)S(1)}, bf16[672,128]{1,0:T(8,128)(2,1)S(1)}, bf16[672,128]{1,0:T(8,128)(2,1)S(1)}, bf16[672,128]{1,0:T(8,128)(2,1)S(1)}) custom-call(bf16[1536,1408]{1,0:T(8,128)(2,1)S(1)} %get-tuple-element.64.refs_0_, bf16[1536,1408]{1,0:T(8,128)(2,1)S(1)} %get-tuple-element.49.refs_1_, ...), custom_call_target="tpu_custom_call" | custom-call | flops 7059013632 | bytes 15499264 | tf_op jit(solution)/shard_map/out_merge/pallas_call | solution.py:555
  84.0 1.8 %collective-permute-start.28 = (bf16[672,128]{1,0:T(8,128)(2,1)S(1)}, bf16[672,128]{1,0:T(8,128)(2,1)S(1)}, u32[]{:S(2)}, u32[]{:S(2)}) collective-permute-start(bf16[672,128]{1,0:T(8,128)(2,1)S(1)} %get-tuple-element.85), channel_id=1, source_target_pairs={{0,2},{1,3},{2,0},{3,1},{4,6},{5,7},{6,4},{7,5},{8,10},{9,11},{10,... | collective-permute-start | bytes 516104 | tf_op jit(solution)/shard_map/ppermute | solution.py:766
  85.8 2.6 %collective-permute-start.29 = (bf16[672,128]{1,0:T(8,128)(2,1)S(1)}, bf16[672,128]{1,0:T(8,128)(2,1)S(1)}, u32[]{:S(2)}, u32[]{:S(2)}) collective-permute-start(bf16[672,128]{1,0:T(8,128)(2,1)S(1)} %get-tuple-element.86), channel_id=1, source_target_pairs={{0,3},{1,2},{2,1},{3,0},{4,7},{5,6},{6,5},{7,4},{8,11},{9,10},{10,... | collective-permute-start | bytes 516104 | tf_op jit(solution)/shard_map/ppermute | solution.py:766
  88.4 4.6 %collective-permute-done.27.refs_1_ = bf16[672,128]{1,0:T(8,128)(2,1)S(1)} collective-permute-done((bf16[672,128]{1,0:T(8,128)(2,1)S(1)}, bf16[672,128]{1,0:T(8,128)(2,1)S(1)}, u32[]{:S(2)}, u32[]{:S(2)}) %collective-permute-start.27) | collective-permute-done | bytes 172064 | tf_op jit(solution)/shard_map/ppermute | solution.py:766
  93.0 6.6 %collective-permute-done.28.refs_2_ = bf16[672,128]{1,0:T(8,128)(2,1)S(1)} collective-permute-done((bf16[672,128]{1,0:T(8,128)(2,1)S(1)}, bf16[672,128]{1,0:T(8,128)(2,1)S(1)}, u32[]{:S(2)}, u32[]{:S(2)}) %collective-permute-start.28) | collective-permute-done | bytes 172064 | tf_op jit(solution)/shard_map/ppermute | solution.py:766
  99.6 1.6 %place_rows.1 = bf16[4,192,448]{2,1,0:T(8,128)(2,1)} custom-call(s32[15]{0:T(128)S(1)} %concatenate.3.info.refs_15_, bf16[672,128]{1,0:T(8,128)(2,1)S(1)} %get-tuple-element.83.refs_0_, bf16[672,128]{1,0:T(8,128)(2,1)S(1)} %collective-permute-done.27.refs_1_, bf16[672,128]{1,0:T(8,128)(2,1)S(1)} %collective-permute-done.28.refs_2_, ...), custom_call_target="tpu_custom_call" | custom-call | bytes 1376256 | tf_op jit(solution)/shard_map/place_rows/pallas_call | solution.py:592
  (51 shorter events, 9.3 us)
Async XLA Ops:
  1.5 12.5 %collective-permute-start.2 = (bf16[192,1536]{1,0:T(8,128)(2,1)S(1)}, bf16[192,1536]{1,0:T(8,128)(2,1)S(1)}, u32[]{:S(2)}, u32[]{:S(2)}) collective-permute-start(bf16[192,1536]{1,0:T(8,128)(2,1)S(1)} %payload.1.refs_0_), channel_id=1, source_target_pairs={{0,4},{4,0},{8,12},{12,8},{16,20},{20,16},{24,28},{28,24},{1,5},{5... | collective-permute-start | bytes 1769480 | tf_op jit(solution)/shard_map/ppermute | solution.py:608
  2.0 16.5 %collective-permute-start = (bf16[192,1536]{1,0:T(8,128)(2,1)S(1)}, bf16[192,1536]{1,0:T(8,128)(2,1)S(1)}, u32[]{:S(2)}, u32[]{:S(2)}) collective-permute-start(bf16[192,1536]{1,0:T(8,128)(2,1)S(1)} %payload.1.refs_0_), channel_id=1, source_target_pairs={{0,8},{4,12},{8,0},{12,4},{16,24},{20,28},{24,16},{28,20},{1,9},{5... | collective-permute-start | bytes 1769480 | tf_op jit(solution)/shard_map/ppermute | solution.py:608
  4.6 15.4 %collective-permute-start.1 = (bf16[192,1536]{1,0:T(8,128)(2,1)S(1)}, bf16[192,1536]{1,0:T(8,128)(2,1)S(1)}, u32[]{:S(2)}, u32[]{:S(2)}) collective-permute-start(bf16[192,1536]{1,0:T(8,128)(2,1)S(1)} %payload.1.refs_0_), channel_id=1, source_target_pairs={{0,16},{4,20},{8,24},{12,28},{16,0},{20,4},{24,8},{28,12},{1,17},{... | collective-permute-start | bytes 1769480 | tf_op jit(solution)/shard_map/ppermute | solution.py:608
  6.8 0.7 copy-start.1
  8.9 5.1 %copy-start = (bf16[128,512]{1,0:T(8,128)(2,1)S(1)}, bf16[128,512]{1,0:T(8,128)(2,1)}, u32[]{:S(2)}) copy-start(bf16[128,512]{1,0:T(8,128)(2,1)} %constant.48.clone.refs_2_.refs_4_) | copy-start | bytes 393220
  20.0 2.7 %collective-permute-start.6 = (bf16[192,1536]{1,0:T(8,128)(2,1)S(1)}, bf16[192,1536]{1,0:T(8,128)(2,1)S(1)}, u32[]{:S(2)}, u32[]{:S(2)}) collective-permute-start(bf16[192,1536]{1,0:T(8,128)(2,1)S(1)} %collective-permute-done.across_x.refs_0_), channel_id=1, source_target_pairs={{0,4},{4,0},{8,12},{12,8},{16,20},{20,16},{24,28},{28,24},{1,5},{5... | collective-permute-start | bytes 1769480 | tf_op jit(solution)/shard_map/ppermute | solution.py:608
  20.0 5.2 %collective-permute-start.5 = (bf16[192,1536]{1,0:T(8,128)(2,1)S(1)}, bf16[192,1536]{1,0:T(8,128)(2,1)S(1)}, u32[]{:S(2)}, u32[]{:S(2)}) collective-permute-start(bf16[192,1536]{1,0:T(8,128)(2,1)S(1)} %collective-permute-done.1.across_y.refs_0_), channel_id=1, source_target_pairs={{0,4},{4,0},{8,12},{12,8},{16,20},{20,16},{24,28},{28,24},{1,5},{5... | collective-permute-start | bytes 1769480 | tf_op jit(solution)/shard_map/ppermute | solution.py:608
  20.5 9.0 %collective-permute-start.3 = (bf16[96,1536]{1,0:T(8,128)(2,1)S(1)}, bf16[96,1536]{1,0:T(8,128)(2,1)S(1)}, u32[]{:S(2)}, u32[]{:S(2)}) collective-permute-start(bf16[96,1536]{1,0:T(8,128)(2,1)S(1)} %get-tuple-element.52), channel_id=1, source_target_pairs={{0,16},{4,20},{8,24},{12,28},{16,0},{20,4},{24,8},{28,12},{1,17},{... | collective-permute-start | bytes 884744 | tf_op jit(solution)/shard_map/ppermute | solution.py:608
  22.1 8.6 %collective-permute-start.4 = (bf16[96,1536]{1,0:T(8,128)(2,1)S(1)}, bf16[96,1536]{1,0:T(8,128)(2,1)S(1)}, u32[]{:S(2)}, u32[]{:S(2)}) collective-permute-start(bf16[96,1536]{1,0:T(8,128)(2,1)S(1)} %get-tuple-element.53), channel_id=1, source_target_pairs={{0,8},{4,12},{8,0},{12,4},{16,24},{20,28},{24,16},{28,20},{1,9},{5... | collective-permute-start | bytes 884744 | tf_op jit(solution)/shard_map/ppermute | solution.py:608
  30.7 1.6 %collective-permute-start.7 = (bf16[96,1536]{1,0:T(8,128)(2,1)S(1)}, bf16[96,1536]{1,0:T(8,128)(2,1)S(1)}, u32[]{:S(2)}, u32[]{:S(2)}) collective-permute-start(bf16[96,1536]{1,0:T(8,128)(2,1)S(1)} %collective-permute-done.3.refs_0_), channel_id=1, source_target_pairs={{0,4},{4,0},{8,12},{12,8},{16,20},{20,16},{24,28},{28,24},{1,5},{5... | collective-permute-start | bytes 884744 | tf_op jit(solution)/shard_map/ppermute | solution.py:608
  30.7 2.0 %collective-permute-start.8 = (bf16[96,1536]{1,0:T(8,128)(2,1)S(1)}, bf16[96,1536]{1,0:T(8,128)(2,1)S(1)}, u32[]{:S(2)}, u32[]{:S(2)}) collective-permute-start(bf16[96,1536]{1,0:T(8,128)(2,1)S(1)} %collective-permute-done.4.refs_1_), channel_id=1, source_target_pairs={{0,4},{4,0},{8,12},{12,8},{16,20},{20,16},{24,28},{28,24},{1,5},{5... | collective-permute-start | bytes 884744 | tf_op jit(solution)/shard_map/ppermute | solution.py:608
  42.1 9.1 %collective-permute-start.10 = (bf16[1152,128]{1,0:T(8,128)(2,1)S(1)}, bf16[1152,128]{1,0:T(8,128)(2,1)S(1)}, u32[]{:S(2)}, u32[]{:S(2)}) collective-permute-start(bf16[1152,128]{1,0:T(8,128)(2,1)S(1)} %get-tuple-element.70.refs_5_), channel_id=1, source_target_pairs={{0,8},{4,12},{8,0},{12,4},{16,24},{20,28},{24,16},{28,20},{1,9},{5... | collective-permute-start | bytes 884744 | tf_op jit(solution)/shard_map/ppermute | solution.py:608
  42.7 8.8 %collective-permute-start.11 = (bf16[1152,128]{1,0:T(8,128)(2,1)S(1)}, bf16[1152,128]{1,0:T(8,128)(2,1)S(1)}, u32[]{:S(2)}, u32[]{:S(2)}) collective-permute-start(bf16[1152,128]{1,0:T(8,128)(2,1)S(1)} %get-tuple-element.70.refs_5_), channel_id=1, source_target_pairs={{0,16},{4,20},{8,24},{12,28},{16,0},{20,4},{24,8},{28,12},{1,17},{... | collective-permute-start | bytes 884744 | tf_op jit(solution)/shard_map/ppermute | solution.py:608
  43.0 8.4 %collective-permute-start.9 = (bf16[1152,128]{1,0:T(8,128)(2,1)S(1)}, bf16[1152,128]{1,0:T(8,128)(2,1)S(1)}, u32[]{:S(2)}, u32[]{:S(2)}) collective-permute-start(bf16[1152,128]{1,0:T(8,128)(2,1)S(1)} %get-tuple-element.70.refs_5_), channel_id=1, source_target_pairs={{0,4},{4,0},{8,12},{12,8},{16,20},{20,16},{24,28},{28,24},{1,5},{5... | collective-permute-start | bytes 884744 | tf_op jit(solution)/shard_map/ppermute | solution.py:608
  51.5 6.0 %collective-permute-start.15 = (bf16[576,128]{1,0:T(8,128)(2,1)S(1)}, bf16[576,128]{1,0:T(8,128)(2,1)S(1)}, u32[]{:S(2)}, u32[]{:S(2)}) collective-permute-start(bf16[576,128]{1,0:T(8,128)(2,1)S(1)} %get-tuple-element.74), channel_id=1, source_target_pairs={{0,16},{4,20},{8,24},{12,28},{16,0},{20,4},{24,8},{28,12},{1,17},{... | collective-permute-start | bytes 442376 | tf_op jit(solution)/shard_map/ppermute | solution.py:608
  51.9 12.3 %collective-permute-start.13 = (bf16[1152,128]{1,0:T(8,128)(2,1)S(1)}, bf16[1152,128]{1,0:T(8,128)(2,1)S(1)}, u32[]{:S(2)}, u32[]{:S(2)}) collective-permute-start(bf16[1152,128]{1,0:T(8,128)(2,1)S(1)} %attention.2.refs_5_), channel_id=1, source_target_pairs={{0,8},{4,12},{8,0},{12,4},{16,24},{20,28},{24,16},{28,20},{1,9},{5... | collective-permute-start | bytes 884744 | tf_op jit(solution)/shard_map/ppermute | solution.py:608
  53.5 11.2 %collective-permute-start.14 = (bf16[1152,128]{1,0:T(8,128)(2,1)S(1)}, bf16[1152,128]{1,0:T(8,128)(2,1)S(1)}, u32[]{:S(2)}, u32[]{:S(2)}) collective-permute-start(bf16[1152,128]{1,0:T(8,128)(2,1)S(1)} %attention.2.refs_5_), channel_id=1, source_target_pairs={{0,16},{4,20},{8,24},{12,28},{16,0},{20,4},{24,8},{28,12},{1,17},{... | collective-permute-start | bytes 884744 | tf_op jit(solution)/shard_map/ppermute | solution.py:608
  55.1 9.7 %collective-permute-start.21 = (bf16[1152,128]{1,0:T(8,128)(2,1)S(1)}, bf16[1152,128]{1,0:T(8,128)(2,1)S(1)}, u32[]{:S(2)}, u32[]{:S(2)}) collective-permute-start(bf16[1152,128]{1,0:T(8,128)(2,1)S(1)} %collective-permute-done.10.across_x.refs_7_), channel_id=1, source_target_pairs={{0,4},{4,0},{8,12},{12,8},{16,20},{20,16},{24,28},{28,24},{1,5},{5... | collective-permute-start | bytes 884744 | tf_op jit(solution)/shard_map/ppermute | solution.py:608
  55.1 10.2 %collective-permute-start.22 = (bf16[1152,128]{1,0:T(8,128)(2,1)S(1)}, bf16[1152,128]{1,0:T(8,128)(2,1)S(1)}, u32[]{:S(2)}, u32[]{:S(2)}) collective-permute-start(bf16[1152,128]{1,0:T(8,128)(2,1)S(1)} %collective-permute-done.11.across_y.refs_9_), channel_id=1, source_target_pairs={{0,4},{4,0},{8,12},{12,8},{16,20},{20,16},{24,28},{28,24},{1,5},{5... | collective-permute-start | bytes 884744 | tf_op jit(solution)/shard_map/ppermute | solution.py:608
  57.5 6.7 %collective-permute-start.16 = (bf16[576,128]{1,0:T(8,128)(2,1)S(1)}, bf16[576,128]{1,0:T(8,128)(2,1)S(1)}, u32[]{:S(2)}, u32[]{:S(2)}) collective-permute-start(bf16[576,128]{1,0:T(8,128)(2,1)S(1)} %get-tuple-element.75), channel_id=1, source_target_pairs={{0,8},{4,12},{8,0},{12,4},{16,24},{20,28},{24,16},{28,20},{1,9},{5... | collective-permute-start | bytes 442376 | tf_op jit(solution)/shard_map/ppermute | solution.py:608
  64.2 1.4 %collective-permute-start.23 = (bf16[576,128]{1,0:T(8,128)(2,1)S(1)}, bf16[576,128]{1,0:T(8,128)(2,1)S(1)}, u32[]{:S(2)}, u32[]{:S(2)}) collective-permute-start(bf16[576,128]{1,0:T(8,128)(2,1)S(1)} %collective-permute-done.15.refs_11_), channel_id=1, source_target_pairs={{0,4},{4,0},{8,12},{12,8},{16,20},{20,16},{24,28},{28,24},{1,5},{5... | collective-permute-start | bytes 442376 | tf_op jit(solution)/shard_map/ppermute | solution.py:608
  64.2 1.7 %collective-permute-start.24 = (bf16[576,128]{1,0:T(8,128)(2,1)S(1)}, bf16[576,128]{1,0:T(8,128)(2,1)S(1)}, u32[]{:S(2)}, u32[]{:S(2)}) collective-permute-start(bf16[576,128]{1,0:T(8,128)(2,1)S(1)} %collective-permute-done.16.refs_12_), channel_id=1, source_target_pairs={{0,4},{4,0},{8,12},{12,8},{16,20},{20,16},{24,28},{28,24},{1,5},{5... | collective-permute-start | bytes 442376 | tf_op jit(solution)/shard_map/ppermute | solution.py:608
  64.7 10.1 %collective-permute-start.12 = (bf16[1152,128]{1,0:T(8,128)(2,1)S(1)}, bf16[1152,128]{1,0:T(8,128)(2,1)S(1)}, u32[]{:S(2)}, u32[]{:S(2)}) collective-permute-start(bf16[1152,128]{1,0:T(8,128)(2,1)S(1)} %attention.2.refs_5_), channel_id=1, source_target_pairs={{0,4},{4,0},{8,12},{12,8},{16,20},{20,16},{24,28},{28,24},{1,5},{5... | collective-permute-start | bytes 884744 | tf_op jit(solution)/shard_map/ppermute | solution.py:608
  64.8 10.0 %collective-permute-start.17 = (bf16[1152,128]{1,0:T(8,128)(2,1)S(1)}, bf16[1152,128]{1,0:T(8,128)(2,1)S(1)}, u32[]{:S(2)}, u32[]{:S(2)}) collective-permute-start(bf16[1152,128]{1,0:T(8,128)(2,1)S(1)} %collective-permute-done.13.across_x.refs_7_), channel_id=1, source_target_pairs={{0,4},{4,0},{8,12},{12,8},{16,20},{20,16},{24,28},{28,24},{1,5},{5... | collective-permute-start | bytes 884744 | tf_op jit(solution)/shard_map/ppermute | solution.py:608
  65.3 9.5 %collective-permute-start.18 = (bf16[1152,128]{1,0:T(8,128)(2,1)S(1)}, bf16[1152,128]{1,0:T(8,128)(2,1)S(1)}, u32[]{:S(2)}, u32[]{:S(2)}) collective-permute-start(bf16[1152,128]{1,0:T(8,128)(2,1)S(1)} %collective-permute-done.14.across_y.refs_9_), channel_id=1, source_target_pairs={{0,4},{4,0},{8,12},{12,8},{16,20},{20,16},{24,28},{28,24},{1,5},{5... | collective-permute-start | bytes 884744 | tf_op jit(solution)/shard_map/ppermute | solution.py:608
  65.6 8.7 %collective-permute-start.19 = (bf16[576,128]{1,0:T(8,128)(2,1)S(1)}, bf16[576,128]{1,0:T(8,128)(2,1)S(1)}, u32[]{:S(2)}, u32[]{:S(2)}) collective-permute-start(bf16[576,128]{1,0:T(8,128)(2,1)S(1)} %get-tuple-element.78), channel_id=1, source_target_pairs={{0,16},{4,20},{8,24},{12,28},{16,0},{20,4},{24,8},{28,12},{1,17},{... | collective-permute-start | bytes 442376 | tf_op jit(solution)/shard_map/ppermute | solution.py:608
  65.9 8.3 %collective-permute-start.20 = (bf16[576,128]{1,0:T(8,128)(2,1)S(1)}, bf16[576,128]{1,0:T(8,128)(2,1)S(1)}, u32[]{:S(2)}, u32[]{:S(2)}) collective-permute-start(bf16[576,128]{1,0:T(8,128)(2,1)S(1)} %get-tuple-element.79), channel_id=1, source_target_pairs={{0,8},{4,12},{8,0},{12,4},{16,24},{20,28},{24,16},{28,20},{1,9},{5... | collective-permute-start | bytes 442376 | tf_op jit(solution)/shard_map/ppermute | solution.py:608
  74.3 1.4 %collective-permute-start.25 = (bf16[576,128]{1,0:T(8,128)(2,1)S(1)}, bf16[576,128]{1,0:T(8,128)(2,1)S(1)}, u32[]{:S(2)}, u32[]{:S(2)}) collective-permute-start(bf16[576,128]{1,0:T(8,128)(2,1)S(1)} %collective-permute-done.19.refs_11_), channel_id=1, source_target_pairs={{0,4},{4,0},{8,12},{12,8},{16,20},{20,16},{24,28},{28,24},{1,5},{5... | collective-permute-start | bytes 442376 | tf_op jit(solution)/shard_map/ppermute | solution.py:608
  74.3 1.6 %collective-permute-start.26 = (bf16[576,128]{1,0:T(8,128)(2,1)S(1)}, bf16[576,128]{1,0:T(8,128)(2,1)S(1)}, u32[]{:S(2)}, u32[]{:S(2)}) collective-permute-start(bf16[576,128]{1,0:T(8,128)(2,1)S(1)} %collective-permute-done.20.refs_12_), channel_id=1, source_target_pairs={{0,4},{4,0},{8,12},{12,8},{16,20},{20,16},{24,28},{28,24},{1,5},{5... | collective-permute-start | bytes 442376 | tf_op jit(solution)/shard_map/ppermute | solution.py:608
  83.9 9.1 %collective-permute-start.27 = (bf16[672,128]{1,0:T(8,128)(2,1)S(1)}, bf16[672,128]{1,0:T(8,128)(2,1)S(1)}, u32[]{:S(2)}, u32[]{:S(2)}) collective-permute-start(bf16[672,128]{1,0:T(8,128)(2,1)S(1)} %get-tuple-element.84), channel_id=1, source_target_pairs={{0,1},{1,0},{2,3},{3,2},{4,5},{5,4},{6,7},{7,6},{8,9},{9,8},{10,11... | collective-permute-start | bytes 516104 | tf_op jit(solution)/shard_map/ppermute | solution.py:766
  84.0 15.6 %collective-permute-start.28 = (bf16[672,128]{1,0:T(8,128)(2,1)S(1)}, bf16[672,128]{1,0:T(8,128)(2,1)S(1)}, u32[]{:S(2)}, u32[]{:S(2)}) collective-permute-start(bf16[672,128]{1,0:T(8,128)(2,1)S(1)} %get-tuple-element.85), channel_id=1, source_target_pairs={{0,2},{1,3},{2,0},{3,1},{4,6},{5,7},{6,4},{7,5},{8,10},{9,11},{10,... | collective-permute-start | bytes 516104 | tf_op jit(solution)/shard_map/ppermute | solution.py:766
  85.8 13.8 %collective-permute-start.29 = (bf16[672,128]{1,0:T(8,128)(2,1)S(1)}, bf16[672,128]{1,0:T(8,128)(2,1)S(1)}, u32[]{:S(2)}, u32[]{:S(2)}) collective-permute-start(bf16[672,128]{1,0:T(8,128)(2,1)S(1)} %get-tuple-element.86), channel_id=1, source_target_pairs={{0,3},{1,2},{2,1},{3,0},{4,7},{5,6},{6,5},{7,4},{8,11},{9,10},{10,... | collective-permute-start | bytes 516104 | tf_op jit(solution)/shard_map/ppermute | solution.py:766
  (2 other events, 1.4 us)

commit v7 on v6

--- a/solution.py
+++ b/solution.py
@@ -151,7 +151,7 @@
 BLOCK = 256
 POSITIONS = 64
 NEGATIVE = -1e30
-CHUNKS = (768, 768)
+CHUNKS = (512, 512, 512)
 
 
 def norm_rows(values, gain_row):
@@ -257,21 +257,16 @@
         jnp.where(first_head, zero, key_a),
         jnp.where(first_head, zero, key_b),
     ]
-    values_part = columns[:, 4 * LANES :]
-    wide = lax.broadcasted_iota(jnp.int32, values_part.shape, 1)
-    ones = jnp.where(wide == 2 * HD, 1.0, 0.0)
-    parts.append(jnp.where(wide < HD, values_part, ones))
-    parts.append(jnp.where((wide >= HD) & (wide < 2 * HD), values_part, ones))
-    for number, part in enumerate(parts[:6]):
+    for head in range(2):
+        values = columns[:, (4 + head) * LANES : (5 + head) * LANES]
+        parts.append(jnp.where(lane == HD, 1.0, values))
+    for number, part in enumerate(parts):
         qkv_out[at, number * LANES : (number + 1) * LANES] = part.astype(jnp.bfloat16)
-    for number, part in enumerate(parts[6:]):
-        low = (6 + 2 * number) * LANES
-        qkv_out[at, low : low + 2 * LANES] = part.astype(jnp.bfloat16)
 
 
 def qkv_call(info, flip, first, second, table, gain, weight, earlier, total):
     rows = 2 * sum(piece.shape[0] for piece in first)
-    widths = (D, 10 * LANES, LANES)
+    widths = (D, 8 * LANES, LANES)
     operands = [*first, *second, table, gain, in_vmem(weight)]
     vmem = pl.BlockSpec(memory_space=pltpu.VMEM)
     held = [in_vmem(one) for one in earlier]
@@ -344,22 +339,24 @@
         sums = []
         for head in range(2):
             weights = jnp.exp2((scores[head, step] - highest[head]) * factor)
-            values = block[at, (6 + 2 * head) * LANES : (8 + 2 * head) * LANES]
+            values = block[at, (6 + head) * LANES : (7 + head) * LANES]
             sums.append(
                 carry[head]
                 + jnp.dot(weights.astype(jnp.bfloat16), values, preferred_element_type=jnp.float32)
             )
         return tuple(sums)
 
-    zero = jnp.zeros((rows, 2 * LANES), jnp.float32)
+    zero = jnp.zeros((rows, LANES), jnp.float32)
     sums = lax.fori_loop(begin, end, weigh, (zero, zero))
-    acc = sum(one / one[:, 2 * HD : 2 * HD + 1] for one in sums)
-    out[:rows] = acc[:, :LANES].astype(jnp.bfloat16)
+    first, second = (one / one[:, HD : HD + 1] for one in sums)
+    lane = lax.broadcasted_iota(jnp.int32, first.shape, 1)
+    turned = pltpu.roll(second, HD, 1)
+    out[:rows] = jnp.where(lane < HD, first, turned).astype(jnp.bfloat16)
     half = rows // 2
-    low, up = acc[:half, LANES:], acc[half:, LANES:]
-    lane = lax.broadcasted_iota(jnp.int32, low.shape, 1)
     tail = 2 * HD - LANES
-    packed = jnp.where(lane < tail, low, jnp.where(lane < 2 * tail, pltpu.roll(up, tail, 1), 0.0))
+    lane = lane[:half]
+    up = pltpu.roll(turned[half:], tail, 1)
+    packed = jnp.where(lane < tail, turned[:half], jnp.where(lane < 2 * tail, up, 0.0))
     out[rows:] = packed.astype(jnp.bfloat16)
 
     if len(rest) > 3:
@@ -643,6 +640,10 @@
     return [send_seq(upper, 4), send_seq(lower, 2)]
 
 
+def chip_shards(value):
+    return [value] + [send_seq(value, flip) for flip in (2, 4, 6)]
+
+
 def weight_order(heads_here):
     quarter = HD // 4
     order = -np.ones((6 * LANES,), np.int32)
@@ -654,7 +655,7 @@
                     target = (2 * kind + letter) * LANES + head * (HD // 2) + half * quarter
                     source = base + kind * HD + half * (HD // 2) + letter * quarter
                     order[target : target + quarter] = np.arange(source, source + quarter)
-        target = 4 * LANES + head * HD
+        target = (4 + head) * LANES
         order[target : target + HD] = np.arange(base + 2 * HD, base + 3 * HD)
     return order
 
@@ -734,27 +735,18 @@
     starts = [sum(CHUNKS[:number]) for number in range(len(CHUNKS))]
     attended, note = [], None
     for start, rows in zip(starts, CHUNKS):
+        if attended:
+            labels, block = after([labels, block], attended[-1][0])
         made = attention_call(start, rows, IDS + shards, info, labels, block, note is None)
         note = made[1] if note is None else note
-        value = made[0]
-        if attended:
-            (value,) = after([value], *attended[-1][1])
-        attended.append((value, near_shards(value)))
+        attended.append(chip_shards(made[0]))
     latest = attended[-1][0]
     most = 2 * (total // 4) // images
-    projected, moving = [], []
-    for own, (own_swap, across_x, across_y) in attended:
-        previous = moving[-1][-1] if moving else ()
-        across_x, across_y = after([across_x, across_y], latest, *previous)
-        far = far_shards(across_x, across_y)
-        moving.append(
-            (own, own_swap, across_x, send_seq(across_x, 1), across_y, send_seq(across_y, 1), far)
-        )
+    projected = []
     for number, (start, rows) in enumerate(zip(starts, CHUNKS)):
-        *near, far = moving[number]
-        if projected:
-            far = after(far, projected[-1])
-        sources = [[one] for one in near] + [far, [send_seq(one, 1) for one in far]]
+        own, *others = attended[number]
+        others = after(others, latest, *projected)
+        sources = [[one] for share in (own, *others) for one in (share, send_seq(share, 1))]
         route = ()
         if number == len(CHUNKS) - 1:
             route = (info, most, note, *projected)

time: 103 us -> 106 us (1.029)
  starting transfers between devices: 23.3 us -> 24.8 us
  waiting for transfers between devices: 28.2 us -> 29.5 us
    pallas_call x2 -> x3, Pallas kernels: 14.7 us -> 16.4 us  [merge_call(): pl.pallas_call(functools.partial(merge_kernel, start, [len(source) for so...]
    ppermute x27 -> x30, starting transfers between devices: 18.9 us -> 20.4 us  [send_seq(): return lax.ppermute(value, 'seq', [(i, i ^ flip) for i in range(size)])]
    ppermute x3, waiting for transfers between devices: 11.2 us -> 12.7 us  [fast_local(): lax.ppermute(made[flip], 'pack', [(z, z ^ flip) for z in range(packs)])]
    pallas_call x2 -> x3, Pallas kernels: 13.9 us -> 12.4 us  [attention_call(): pl.pallas_call(functools.partial(attention_kernel, start, first_owner, in...]
    ppermute x27 -> x30, waiting for transfers between devices: 17 us -> 16.7 us  [send_seq(): return lax.ppermute(value, 'seq', [(i, i ^ flip) for i in range(size)])]
  transfers between devices with their start and end apart: 30 -> 33, of which waited for: 15 -> 13; matrix products, arithmetic and copies ran while one was open for 1% -> 1% of each run, Pallas kernels for 26% -> 30%
where the time goes in v7:
time: 106 us; the launch traced here: 104 us
  Pallas kernels  46.8 us (44%)
  waiting for transfers between devices  29.5 us (28%)
  starting transfers between devices  24.8 us (23%)
  local copies, waits for them, and re-layouts  2.79 us (3%)
    ppermute x30, starting transfers between devices, send_seq(): return lax.ppermute(value, 'seq', [(i, i ^ flip) for i in range(size)])  20.4 us
    ppermute x30, waiting for transfers between devices, send_seq(): return lax.ppermute(value, 'seq', [(i, i ^ flip) for i in range(size)])  16.7 us
    pallas_call x3, Pallas kernels, merge_call(): pl.pallas_call(functools.partial(merge_kernel, start, [len(source) for so...  16.4 us
    ppermute x3, waiting for transfers between devices, fast_local(): lax.ppermute(made[flip], 'pack', [(z, z ^ flip) for z in range(packs)])  12.7 us
    pallas_call x3, Pallas kernels, attention_call(): pl.pallas_call(functools.partial(attention_kernel, start, first_owner, in...  12.4 us
    pallas_call x4, Pallas kernels, qkv_call(): pl.pallas_call(functools.partial(qkv_kernel, len(first), flip), in_specs=...  9.81 us
    pallas_call x1, Pallas kernels, prepare_call(): pl.pallas_call(functools.partial(prepare_kernel, shards), in_specs=[pl.Bl...  5.1 us
    ppermute x3, starting transfers between devices, fast_local(): lax.ppermute(made[flip], 'pack', [(z, z ^ flip) for z in range(packs)])  4.45 us
  transfers between devices with their start and end apart: 33, of which 13 were waited for; matrix products, arithmetic and copies ran while one was open for 1% of the time, Pallas kernels for 30%

profile of v7, /device:TPU:0, one launch (start us, length us, event | category | flops | bytes accessed | tf_op | source)
XLA Modules:
  0.0 104.1 jit_solution(3999865393238360054)
XLA Ops:
  0.0 1.5 %payload.1.refs_0_ = bf16[192,1536]{1,0:T(8,128)(2,1)S(1)} custom-call(s32[1,192]{1,0:T(1,128)} %segments.1, s32[1,192]{1,0:T(1,128)} %rows.1, s32[1,192]{1,0:T(1,128)} %columns.1, s32[1,192]{1,0:T(1,128)} %mask.1, bf16[1408]{0:T(1024)(128)(2,1)} %embed.1, bf16[1,192,1408]{2,1,0:T(8,128)(2,1)} %patches.1), custom_call_target="tpu_custom_call" | custom-call | flops 270336 | bytes 1081344 | tf_op jit(solution)/shard_map/payload/pallas_call | solution.py:202
  2.0 2.6 %collective-permute-start = (bf16[192,1536]{1,0:T(8,128)(2,1)S(1)}, bf16[192,1536]{1,0:T(8,128)(2,1)S(1)}, u32[]{:S(2)}, u32[]{:S(2)}) collective-permute-start(bf16[192,1536]{1,0:T(8,128)(2,1)S(1)} %payload.1.refs_0_), channel_id=1, source_target_pairs={{0,8},{4,12},{8,0},{12,4},{16,24},{20,28},{24,16},{28,20},{1,9},{5... | collective-permute-start | bytes 1769480 | tf_op jit(solution)/shard_map/ppermute | solution.py:605
  4.6 1.5 %collective-permute-start.1 = (bf16[192,1536]{1,0:T(8,128)(2,1)S(1)}, bf16[192,1536]{1,0:T(8,128)(2,1)S(1)}, u32[]{:S(2)}, u32[]{:S(2)}) collective-permute-start(bf16[192,1536]{1,0:T(8,128)(2,1)S(1)} %payload.1.refs_0_), channel_id=1, source_target_pairs={{0,16},{4,20},{8,24},{12,28},{16,0},{20,4},{24,8},{28,12},{1,17},{... | collective-permute-start | bytes 1769480 | tf_op jit(solution)/shard_map/ppermute | solution.py:605
  8.9 5.1 %prepare.1 = (f32[1,1408]{1,0:T(1,128)S(1)}, f32[1,1408]{1,0:T(1,128)S(1)}, f32[1,448]{1,0:T(1,128)S(1)}, bf16[1536,1408]{1,0:T(8,128)(2,1)S(1)}, bf16[448,5632]...) custom-call(s32[15]{0:T(128)S(1)} %concatenate.3.info.refs_13_, bf16[1408,1408]{1,0:T(8,128)(2,1)} %out_weight.1, ...), custom_call_target="tpu_custom_call" | custom-call | flops 1141899264 | bytes 20996096 | tf_op jit(solution)/shard_map/prepare/pallas_call | solution.py:439
  14.0 2.5 %norm_qkv.4 = (bf16[1536,1408]{1,0:T(8,128)(2,1)S(1)}, bf16[1536,1024]{1,0:T(8,128)(2,1)S(1)}, bf16[1536,128]{1,0:T(8,128)(2,1)S(1)}) custom-call(s32[15]{0:T(128)S(1)} %concatenate.3.info.refs_13_, bf16[192,1536]{1,0:T(8,128)(2,1)S(1)} %payload.1.refs_0_, bf16[192,1536]{1,0:T(8,128)(2,1)S(1)} %collective-permute-done.2.refs_1_, ...), custom_call_target="tpu_custom_call" | custom-call | flops 2491416576 | bytes 6488064 | tf_op jit(solution)/shard_map/norm_qkv/pallas_call | solution.py:273
  16.5 2.0 %collective-permute-done.across_x.refs_0_ = bf16[192,1536]{1,0:T(8,128)(2,1)S(1)} collective-permute-done((bf16[192,1536]{1,0:T(8,128)(2,1)S(1)}, bf16[192,1536]{1,0:T(8,128)(2,1)S(1)}, u32[]{:S(2)}, u32[]{:S(2)}) %collective-permute-start) | collective-permute-done | bytes 589856 | tf_op jit(solution)/shard_map/ppermute | solution.py:605
  18.5 1.5 %collective-permute-done.1.across_y.refs_0_ = bf16[192,1536]{1,0:T(8,128)(2,1)S(1)} collective-permute-done((bf16[192,1536]{1,0:T(8,128)(2,1)S(1)}, bf16[192,1536]{1,0:T(8,128)(2,1)S(1)}, u32[]{:S(2)}, u32[]{:S(2)}) %collective-permute-start.1) | collective-permute-done | bytes 589856 | tf_op jit(solution)/shard_map/ppermute | solution.py:605
  20.5 1.6 %collective-permute-start.3 = (bf16[96,1536]{1,0:T(8,128)(2,1)S(1)}, bf16[96,1536]{1,0:T(8,128)(2,1)S(1)}, u32[]{:S(2)}, u32[]{:S(2)}) collective-permute-start(bf16[96,1536]{1,0:T(8,128)(2,1)S(1)} %get-tuple-element.54), channel_id=1, source_target_pairs={{0,16},{4,20},{8,24},{12,28},{16,0},{20,4},{24,8},{28,12},{1,17},{... | collective-permute-start | bytes 884744 | tf_op jit(solution)/shard_map/ppermute | solution.py:605
  22.6 2.5 %norm_qkv.5 = (bf16[1536,1408]{1,0:T(8,128)(2,1)S(1)}, bf16[1536,1024]{1,0:T(8,128)(2,1)S(1)}, bf16[1536,128]{1,0:T(8,128)(2,1)S(1)}) custom-call(s32[15]{0:T(128)S(1)} %concatenate.3.info.refs_13_, bf16[192,1536]{1,0:T(8,128)(2,1)S(1)} %collective-permute-done.across_x.refs_0_, ...), custom_call_target="tpu_custom_call", output_to_operand_aliasing={{0}: (6, {}), {1}: (7, {}), {2}: (8, {})} | custom-call | flops 2491416576 | bytes 6488064 | tf_op jit(solution)/shard_map/norm_qkv/pallas_call | solution.py:273
  25.1 2.4 %norm_qkv.6 = (bf16[1536,1408]{1,0:T(8,128)(2,1)S(1)}, bf16[1536,1024]{1,0:T(8,128)(2,1)S(1)}, bf16[1536,128]{1,0:T(8,128)(2,1)S(1)}) custom-call(s32[15]{0:T(128)S(1)} %concatenate.3.info.refs_13_, bf16[192,1536]{1,0:T(8,128)(2,1)S(1)} %collective-permute-done.1.across_y.refs_0_, ...), custom_call_target="tpu_custom_call", output_to_operand_aliasing={{0}: (6, {}), {1}: (7, {}), {2}: (8, {})} | custom-call | flops 2491416576 | bytes 6488064 | tf_op jit(solution)/shard_map/norm_qkv/pallas_call | solution.py:273
  27.6 1.9 %collective-permute-done.3.refs_0_ = bf16[96,1536]{1,0:T(8,128)(2,1)S(1)} collective-permute-done((bf16[96,1536]{1,0:T(8,128)(2,1)S(1)}, bf16[96,1536]{1,0:T(8,128)(2,1)S(1)}, u32[]{:S(2)}, u32[]{:S(2)}) %collective-permute-start.3) | collective-permute-done | bytes 294944 | tf_op jit(solution)/shard_map/ppermute | solution.py:605
  29.5 1.2 %collective-permute-done.4.refs_1_ = bf16[96,1536]{1,0:T(8,128)(2,1)S(1)} collective-permute-done((bf16[96,1536]{1,0:T(8,128)(2,1)S(1)}, bf16[96,1536]{1,0:T(8,128)(2,1)S(1)}, u32[]{:S(2)}, u32[]{:S(2)}) %collective-permute-start.4) | collective-permute-done | bytes 294944 | tf_op jit(solution)/shard_map/ppermute | solution.py:605
  31.2 1.1 %collective-permute-done.7.refs_2_ = bf16[96,1536]{1,0:T(8,128)(2,1)S(1)} collective-permute-done((bf16[96,1536]{1,0:T(8,128)(2,1)S(1)}, bf16[96,1536]{1,0:T(8,128)(2,1)S(1)}, u32[]{:S(2)}, u32[]{:S(2)}) %collective-permute-start.7) | collective-permute-done | bytes 294944 | tf_op jit(solution)/shard_map/ppermute | solution.py:605
  32.7 2.4 %norm_qkv.7 = (bf16[1536,1408]{1,0:T(8,128)(2,1)S(1)}, bf16[1536,1024]{1,0:T(8,128)(2,1)S(1)}, bf16[1536,128]{1,0:T(8,128)(2,1)S(1)}) custom-call(s32[15]{0:T(128)S(1)} %concatenate.3.info.refs_13_, bf16[96,1536]{1,0:T(8,128)(2,1)S(1)} %collective-permute-done.3.refs_0_, ...), custom_call_target="tpu_custom_call", output_to_operand_aliasing={{0}: (8, {}), {1}: (9, {}), {2}: (10, {})} | custom-call | flops 2491416576 | bytes 6488064 | tf_op jit(solution)/shard_map/norm_qkv/pallas_call | solution.py:273
  35.2 3.6 %attention.3 = (bf16[768,128]{1,0:T(8,128)(2,1)S(1)}, bf16[16,128]{1,0:T(8,128)(2,1)S(1)}) custom-call(s32[15]{0:T(128)S(1)} %concatenate.3.info.refs_13_, bf16[1536,128]{1,0:T(8,128)(2,1)S(1)} %get-tuple-element.75.labels, bf16[1536,1024]{1,0:T(8,128)(2,1)S(1)} %get-tuple-element.76.block), custom_call_target="tpu_custom_call" | custom-call | flops 2013265920 | bytes 3145728 | tf_op jit(solution)/shard_map/attention/pallas_call | solution.py:384
  39.8 2.6 %collective-permute-start.16 = (bf16[768,128]{1,0:T(8,128)(2,1)S(1)}, bf16[768,128]{1,0:T(8,128)(2,1)S(1)}, u32[]{:S(2)}, u32[]{:S(2)}) collective-permute-start(bf16[768,128]{1,0:T(8,128)(2,1)S(1)} %get-tuple-element.72.refs_5_), channel_id=1, source_target_pairs={{0,24},{4,28},{8,16},{12,20},{16,8},{20,12},{24,0},{28,4},{1,25},{... | collective-permute-start | bytes 589832 | tf_op jit(solution)/shard_map/ppermute | solution.py:605
  42.4 5.0 %attention.4.refs_5_ = bf16[768,128]{1,0:T(8,128)(2,1)S(1)} custom-call(s32[15]{0:T(128)S(1)} %concatenate.3.info.refs_13_, bf16[1536,128]{1,0:T(8,128)(2,1)S(1)} %get-tuple-element.75.labels, bf16[1536,1024]{1,0:T(8,128)(2,1)S(1)} %get-tuple-element.76.block), custom_call_target="tpu_custom_call" | custom-call | flops 2013265920 | bytes 3145728 | tf_op jit(solution)/shard_map/attention/pallas_call | solution.py:384
  47.4 3.8 %attention.5.refs_5_ = bf16[768,128]{1,0:T(8,128)(2,1)S(1)} custom-call(s32[15]{0:T(128)S(1)} %concatenate.3.info.refs_13_, bf16[1536,128]{1,0:T(8,128)(2,1)S(1)} %get-tuple-element.75.labels, bf16[1536,1024]{1,0:T(8,128)(2,1)S(1)} %get-tuple-element.76.block), custom_call_target="tpu_custom_call" | custom-call | flops 2013265920 | bytes 3145728 | tf_op jit(solution)/shard_map/attention/pallas_call | solution.py:384
  53.2 2.6 %collective-permute-start.23 = (bf16[768,128]{1,0:T(8,128)(2,1)S(1)}, bf16[768,128]{1,0:T(8,128)(2,1)S(1)}, u32[]{:S(2)}, u32[]{:S(2)}) collective-permute-start(bf16[768,128]{1,0:T(8,128)(2,1)S(1)} %attention.4.refs_5_), channel_id=1, source_target_pairs={{0,24},{4,28},{8,16},{12,20},{16,8},{20,12},{24,0},{28,4},{1,25},{... | collective-permute-start | bytes 589832 | tf_op jit(solution)/shard_map/ppermute | solution.py:605
  55.8 5.0 %out_merge.3.refs_15_ = bf16[128,448]{1,0:T(8,128)(2,1)S(1)} custom-call(bf16[1536,1408]{1,0:T(8,128)(2,1)S(1)} %get-tuple-element.66.refs_0_, bf16[1536,1408]{1,0:T(8,128)(2,1)S(1)} %get-tuple-element.51.refs_1_, f32[1,1408]{1,0:T(1,128)S(1)} %get-tuple-element.67.refs_2_, bf16[448,5632]{1,0:T(8,128)(2,1)S(1)} %get-tuple-element.68.refs_3_, ...), custom_call_target="tpu_custom_call" | custom-call | flops 4706009088 | bytes 13336576 | tf_op jit(solution)/shard_map/out_merge/pallas_call | solution.py:552
  60.8 2.9 %collective-permute-done.22.refs_9_ = bf16[768,128]{1,0:T(8,128)(2,1)S(1)} collective-permute-done((bf16[768,128]{1,0:T(8,128)(2,1)S(1)}, bf16[768,128]{1,0:T(8,128)(2,1)S(1)}, u32[]{:S(2)}, u32[]{:S(2)}) %collective-permute-start.22) | collective-permute-done | bytes 196640 | tf_op jit(solution)/shard_map/ppermute | solution.py:605
  64.2 1.5 %collective-permute-start.10 = (bf16[768,128]{1,0:T(8,128)(2,1)S(1)}, bf16[768,128]{1,0:T(8,128)(2,1)S(1)}, u32[]{:S(2)}, u32[]{:S(2)}) collective-permute-start(bf16[768,128]{1,0:T(8,128)(2,1)S(1)} %attention.5.refs_5_), channel_id=1, source_target_pairs={{0,8},{4,12},{8,0},{12,4},{16,24},{20,28},{24,16},{28,20},{1,9},{5... | collective-permute-start | bytes 589832 | tf_op jit(solution)/shard_map/ppermute | solution.py:605
  66.2 1.5 %collective-permute-start.12 = (bf16[768,128]{1,0:T(8,128)(2,1)S(1)}, bf16[768,128]{1,0:T(8,128)(2,1)S(1)}, u32[]{:S(2)}, u32[]{:S(2)}) collective-permute-start(bf16[768,128]{1,0:T(8,128)(2,1)S(1)} %attention.5.refs_5_), channel_id=1, source_target_pairs={{0,24},{4,28},{8,16},{12,20},{16,8},{20,12},{24,0},{28,4},{1,25},{... | collective-permute-start | bytes 589832 | tf_op jit(solution)/shard_map/ppermute | solution.py:605
  67.7 5.0 %out_merge.4.refs_16_ = bf16[128,448]{1,0:T(8,128)(2,1)S(1)} custom-call(bf16[1536,1408]{1,0:T(8,128)(2,1)S(1)} %get-tuple-element.66.refs_0_, bf16[1536,1408]{1,0:T(8,128)(2,1)S(1)} %get-tuple-element.51.refs_1_, f32[1,1408]{1,0:T(1,128)S(1)} %get-tuple-element.67.refs_2_, bf16[448,5632]{1,0:T(8,128)(2,1)S(1)} %get-tuple-element.68.refs_3_, ...), custom_call_target="tpu_custom_call" | custom-call | flops 4706009088 | bytes 13336576 | tf_op jit(solution)/shard_map/out_merge/pallas_call | solution.py:552
  72.7 4.2 %collective-permute-done.11.refs_9_ = bf16[768,128]{1,0:T(8,128)(2,1)S(1)} collective-permute-done((bf16[768,128]{1,0:T(8,128)(2,1)S(1)}, bf16[768,128]{1,0:T(8,128)(2,1)S(1)}, u32[]{:S(2)}, u32[]{:S(2)}) %collective-permute-start.11) | collective-permute-done | bytes 196640 | tf_op jit(solution)/shard_map/ppermute | solution.py:605
  77.4 0.9 collective-permute-done.27.refs_8_
  78.9 6.4 %out_merge.5 = (bf16[672,128]{1,0:T(8,128)(2,1)S(1)}, bf16[672,128]{1,0:T(8,128)(2,1)S(1)}, bf16[672,128]{1,0:T(8,128)(2,1)S(1)}, bf16[672,128]{1,0:T(8,128)(2,1)S(1)}) custom-call(bf16[1536,1408]{1,0:T(8,128)(2,1)S(1)} %get-tuple-element.66.refs_0_, bf16[1536,1408]{1,0:T(8,128)(2,1)S(1)} %get-tuple-element.51.refs_1_, ...), custom_call_target="tpu_custom_call" | custom-call | flops 4706009088 | bytes 13336576 | tf_op jit(solution)/shard_map/out_merge/pallas_call | solution.py:552
  85.3 1.6 %collective-permute-start.30 = (bf16[672,128]{1,0:T(8,128)(2,1)S(1)}, bf16[672,128]{1,0:T(8,128)(2,1)S(1)}, u32[]{:S(2)}, u32[]{:S(2)}) collective-permute-start(bf16[672,128]{1,0:T(8,128)(2,1)S(1)} %get-tuple-element.88), channel_id=1, source_target_pairs={{0,1},{1,0},{2,3},{3,2},{4,5},{5,4},{6,7},{7,6},{8,9},{9,8},{10,11... | collective-permute-start | bytes 516104 | tf_op jit(solution)/shard_map/ppermute | solution.py:758
  87.0 2.6 %collective-permute-start.31 = (bf16[672,128]{1,0:T(8,128)(2,1)S(1)}, bf16[672,128]{1,0:T(8,128)(2,1)S(1)}, u32[]{:S(2)}, u32[]{:S(2)}) collective-permute-start(bf16[672,128]{1,0:T(8,128)(2,1)S(1)} %get-tuple-element.89), channel_id=1, source_target_pairs={{0,2},{1,3},{2,0},{3,1},{4,6},{5,7},{6,4},{7,5},{8,10},{9,11},{10,... | collective-permute-start | bytes 516104 | tf_op jit(solution)/shard_map/ppermute | solution.py:758
  89.8 5.3 %collective-permute-done.30.refs_1_ = bf16[672,128]{1,0:T(8,128)(2,1)S(1)} collective-permute-done((bf16[672,128]{1,0:T(8,128)(2,1)S(1)}, bf16[672,128]{1,0:T(8,128)(2,1)S(1)}, u32[]{:S(2)}, u32[]{:S(2)}) %collective-permute-start.30) | collective-permute-done | bytes 172064 | tf_op jit(solution)/shard_map/ppermute | solution.py:758
  95.0 7.4 %collective-permute-done.31.refs_2_ = bf16[672,128]{1,0:T(8,128)(2,1)S(1)} collective-permute-done((bf16[672,128]{1,0:T(8,128)(2,1)S(1)}, bf16[672,128]{1,0:T(8,128)(2,1)S(1)}, u32[]{:S(2)}, u32[]{:S(2)}) %collective-permute-start.31) | collective-permute-done | bytes 172064 | tf_op jit(solution)/shard_map/ppermute | solution.py:758
  102.5 1.6 %place_rows.1 = bf16[4,192,448]{2,1,0:T(8,128)(2,1)} custom-call(s32[15]{0:T(128)S(1)} %concatenate.3.info.refs_13_, bf16[672,128]{1,0:T(8,128)(2,1)S(1)} %get-tuple-element.87.refs_0_, bf16[672,128]{1,0:T(8,128)(2,1)S(1)} %collective-permute-done.30.refs_1_, bf16[672,128]{1,0:T(8,128)(2,1)S(1)} %collective-permute-done.31.refs_2_, ...), custom_call_target="tpu_custom_call" | custom-call | bytes 1376256 | tf_op jit(solution)/shard_map/place_rows/pallas_call | solution.py:589
  (57 shorter events, 10.6 us)
Async XLA Ops:
  1.5 12.5 %collective-permute-start.2 = (bf16[192,1536]{1,0:T(8,128)(2,1)S(1)}, bf16[192,1536]{1,0:T(8,128)(2,1)S(1)}, u32[]{:S(2)}, u32[]{:S(2)}) collective-permute-start(bf16[192,1536]{1,0:T(8,128)(2,1)S(1)} %payload.1.refs_0_), channel_id=1, source_target_pairs={{0,4},{4,0},{8,12},{12,8},{16,20},{20,16},{24,28},{28,24},{1,5},{5... | collective-permute-start | bytes 1769480 | tf_op jit(solution)/shard_map/ppermute | solution.py:605
  2.0 16.5 %collective-permute-start = (bf16[192,1536]{1,0:T(8,128)(2,1)S(1)}, bf16[192,1536]{1,0:T(8,128)(2,1)S(1)}, u32[]{:S(2)}, u32[]{:S(2)}) collective-permute-start(bf16[192,1536]{1,0:T(8,128)(2,1)S(1)} %payload.1.refs_0_), channel_id=1, source_target_pairs={{0,8},{4,12},{8,0},{12,4},{16,24},{20,28},{24,16},{28,20},{1,9},{5... | collective-permute-start | bytes 1769480 | tf_op jit(solution)/shard_map/ppermute | solution.py:605
  4.6 15.4 %collective-permute-start.1 = (bf16[192,1536]{1,0:T(8,128)(2,1)S(1)}, bf16[192,1536]{1,0:T(8,128)(2,1)S(1)}, u32[]{:S(2)}, u32[]{:S(2)}) collective-permute-start(bf16[192,1536]{1,0:T(8,128)(2,1)S(1)} %payload.1.refs_0_), channel_id=1, source_target_pairs={{0,16},{4,20},{8,24},{12,28},{16,0},{20,4},{24,8},{28,12},{1,17},{... | collective-permute-start | bytes 1769480 | tf_op jit(solution)/shard_map/ppermute | solution.py:605
  20.0 2.7 %collective-permute-start.6 = (bf16[192,1536]{1,0:T(8,128)(2,1)S(1)}, bf16[192,1536]{1,0:T(8,128)(2,1)S(1)}, u32[]{:S(2)}, u32[]{:S(2)}) collective-permute-start(bf16[192,1536]{1,0:T(8,128)(2,1)S(1)} %collective-permute-done.across_x.refs_0_), channel_id=1, source_target_pairs={{0,4},{4,0},{8,12},{12,8},{16,20},{20,16},{24,28},{28,24},{1,5},{5... | collective-permute-start | bytes 1769480 | tf_op jit(solution)/shard_map/ppermute | solution.py:605
  20.0 5.2 %collective-permute-start.5 = (bf16[192,1536]{1,0:T(8,128)(2,1)S(1)}, bf16[192,1536]{1,0:T(8,128)(2,1)S(1)}, u32[]{:S(2)}, u32[]{:S(2)}) collective-permute-start(bf16[192,1536]{1,0:T(8,128)(2,1)S(1)} %collective-permute-done.1.across_y.refs_0_), channel_id=1, source_target_pairs={{0,4},{4,0},{8,12},{12,8},{16,20},{20,16},{24,28},{28,24},{1,5},{5... | collective-permute-start | bytes 1769480 | tf_op jit(solution)/shard_map/ppermute | solution.py:605
  20.5 9.0 %collective-permute-start.3 = (bf16[96,1536]{1,0:T(8,128)(2,1)S(1)}, bf16[96,1536]{1,0:T(8,128)(2,1)S(1)}, u32[]{:S(2)}, u32[]{:S(2)}) collective-permute-start(bf16[96,1536]{1,0:T(8,128)(2,1)S(1)} %get-tuple-element.54), channel_id=1, source_target_pairs={{0,16},{4,20},{8,24},{12,28},{16,0},{20,4},{24,8},{28,12},{1,17},{... | collective-permute-start | bytes 884744 | tf_op jit(solution)/shard_map/ppermute | solution.py:605
  22.1 8.6 %collective-permute-start.4 = (bf16[96,1536]{1,0:T(8,128)(2,1)S(1)}, bf16[96,1536]{1,0:T(8,128)(2,1)S(1)}, u32[]{:S(2)}, u32[]{:S(2)}) collective-permute-start(bf16[96,1536]{1,0:T(8,128)(2,1)S(1)} %get-tuple-element.55), channel_id=1, source_target_pairs={{0,8},{4,12},{8,0},{12,4},{16,24},{20,28},{24,16},{28,20},{1,9},{5... | collective-permute-start | bytes 884744 | tf_op jit(solution)/shard_map/ppermute | solution.py:605
  30.7 1.6 %collective-permute-start.7 = (bf16[96,1536]{1,0:T(8,128)(2,1)S(1)}, bf16[96,1536]{1,0:T(8,128)(2,1)S(1)}, u32[]{:S(2)}, u32[]{:S(2)}) collective-permute-start(bf16[96,1536]{1,0:T(8,128)(2,1)S(1)} %collective-permute-done.3.refs_0_), channel_id=1, source_target_pairs={{0,4},{4,0},{8,12},{12,8},{16,20},{20,16},{24,28},{28,24},{1,5},{5... | collective-permute-start | bytes 884744 | tf_op jit(solution)/shard_map/ppermute | solution.py:605
  30.7 2.0 %collective-permute-start.8 = (bf16[96,1536]{1,0:T(8,128)(2,1)S(1)}, bf16[96,1536]{1,0:T(8,128)(2,1)S(1)}, u32[]{:S(2)}, u32[]{:S(2)}) collective-permute-start(bf16[96,1536]{1,0:T(8,128)(2,1)S(1)} %collective-permute-done.4.refs_1_), channel_id=1, source_target_pairs={{0,4},{4,0},{8,12},{12,8},{16,20},{20,16},{24,28},{28,24},{1,5},{5... | collective-permute-start | bytes 884744 | tf_op jit(solution)/shard_map/ppermute | solution.py:605
  38.8 12.4 %collective-permute-start.14 = (bf16[768,128]{1,0:T(8,128)(2,1)S(1)}, bf16[768,128]{1,0:T(8,128)(2,1)S(1)}, u32[]{:S(2)}, u32[]{:S(2)}) collective-permute-start(bf16[768,128]{1,0:T(8,128)(2,1)S(1)} %get-tuple-element.72.refs_5_), channel_id=1, source_target_pairs={{0,8},{4,12},{8,0},{12,4},{16,24},{20,28},{24,16},{28,20},{1,9},{5... | collective-permute-start | bytes 589832 | tf_op jit(solution)/shard_map/ppermute | solution.py:605
  39.4 11.8 %collective-permute-start.15 = (bf16[768,128]{1,0:T(8,128)(2,1)S(1)}, bf16[768,128]{1,0:T(8,128)(2,1)S(1)}, u32[]{:S(2)}, u32[]{:S(2)}) collective-permute-start(bf16[768,128]{1,0:T(8,128)(2,1)S(1)} %get-tuple-element.72.refs_5_), channel_id=1, source_target_pairs={{0,16},{4,20},{8,24},{12,28},{16,0},{20,4},{24,8},{28,12},{1,17},{... | collective-permute-start | bytes 589832 | tf_op jit(solution)/shard_map/ppermute | solution.py:605
  39.8 11.4 %collective-permute-start.16 = (bf16[768,128]{1,0:T(8,128)(2,1)S(1)}, bf16[768,128]{1,0:T(8,128)(2,1)S(1)}, u32[]{:S(2)}, u32[]{:S(2)}) collective-permute-start(bf16[768,128]{1,0:T(8,128)(2,1)S(1)} %get-tuple-element.72.refs_5_), channel_id=1, source_target_pairs={{0,24},{4,28},{8,16},{12,20},{16,8},{20,12},{24,0},{28,4},{1,25},{... | collective-permute-start | bytes 589832 | tf_op jit(solution)/shard_map/ppermute | solution.py:605
  42.4 10.5 %collective-permute-start.13 = (bf16[768,128]{1,0:T(8,128)(2,1)S(1)}, bf16[768,128]{1,0:T(8,128)(2,1)S(1)}, u32[]{:S(2)}, u32[]{:S(2)}) collective-permute-start(bf16[768,128]{1,0:T(8,128)(2,1)S(1)} %get-tuple-element.72.refs_5_), channel_id=1, source_target_pairs={{0,4},{4,0},{8,12},{12,8},{16,20},{20,16},{24,28},{28,24},{1,5},{5... | collective-permute-start | bytes 589832 | tf_op jit(solution)/shard_map/ppermute | solution.py:605
  51.2 2.0 %collective-permute-start.17 = (bf16[768,128]{1,0:T(8,128)(2,1)S(1)}, bf16[768,128]{1,0:T(8,128)(2,1)S(1)}, u32[]{:S(2)}, u32[]{:S(2)}) collective-permute-start(bf16[768,128]{1,0:T(8,128)(2,1)S(1)} %collective-permute-done.14.refs_7_), channel_id=1, source_target_pairs={{0,4},{4,0},{8,12},{12,8},{16,20},{20,16},{24,28},{28,24},{1,5},{5... | collective-permute-start | bytes 589832 | tf_op jit(solution)/shard_map/ppermute | solution.py:605
  51.8 4.0 %collective-permute-start.18 = (bf16[768,128]{1,0:T(8,128)(2,1)S(1)}, bf16[768,128]{1,0:T(8,128)(2,1)S(1)}, u32[]{:S(2)}, u32[]{:S(2)}) collective-permute-start(bf16[768,128]{1,0:T(8,128)(2,1)S(1)} %collective-permute-done.15.refs_9_), channel_id=1, source_target_pairs={{0,4},{4,0},{8,12},{12,8},{16,20},{20,16},{24,28},{28,24},{1,5},{5... | collective-permute-start | bytes 589832 | tf_op jit(solution)/shard_map/ppermute | solution.py:605
  51.9 3.9 %collective-permute-start.19 = (bf16[768,128]{1,0:T(8,128)(2,1)S(1)}, bf16[768,128]{1,0:T(8,128)(2,1)S(1)}, u32[]{:S(2)}, u32[]{:S(2)}) collective-permute-start(bf16[768,128]{1,0:T(8,128)(2,1)S(1)} %collective-permute-done.16.refs_11_), channel_id=1, source_target_pairs={{0,4},{4,0},{8,12},{12,8},{16,20},{20,16},{24,28},{28,24},{1,5},{5... | collective-permute-start | bytes 589832 | tf_op jit(solution)/shard_map/ppermute | solution.py:605
  52.3 8.5 %collective-permute-start.21 = (bf16[768,128]{1,0:T(8,128)(2,1)S(1)}, bf16[768,128]{1,0:T(8,128)(2,1)S(1)}, u32[]{:S(2)}, u32[]{:S(2)}) collective-permute-start(bf16[768,128]{1,0:T(8,128)(2,1)S(1)} %attention.4.refs_5_), channel_id=1, source_target_pairs={{0,8},{4,12},{8,0},{12,4},{16,24},{20,28},{24,16},{28,20},{1,9},{5... | collective-permute-start | bytes 589832 | tf_op jit(solution)/shard_map/ppermute | solution.py:605
  52.8 10.8 %collective-permute-start.22 = (bf16[768,128]{1,0:T(8,128)(2,1)S(1)}, bf16[768,128]{1,0:T(8,128)(2,1)S(1)}, u32[]{:S(2)}, u32[]{:S(2)}) collective-permute-start(bf16[768,128]{1,0:T(8,128)(2,1)S(1)} %attention.4.refs_5_), channel_id=1, source_target_pairs={{0,16},{4,20},{8,24},{12,28},{16,0},{20,4},{24,8},{28,12},{1,17},{... | collective-permute-start | bytes 589832 | tf_op jit(solution)/shard_map/ppermute | solution.py:605
  53.2 10.5 %collective-permute-start.23 = (bf16[768,128]{1,0:T(8,128)(2,1)S(1)}, bf16[768,128]{1,0:T(8,128)(2,1)S(1)}, u32[]{:S(2)}, u32[]{:S(2)}) collective-permute-start(bf16[768,128]{1,0:T(8,128)(2,1)S(1)} %attention.4.refs_5_), channel_id=1, source_target_pairs={{0,24},{4,28},{8,16},{12,20},{16,8},{20,12},{24,0},{28,4},{1,25},{... | collective-permute-start | bytes 589832 | tf_op jit(solution)/shard_map/ppermute | solution.py:605
  55.8 9.9 %collective-permute-start.20 = (bf16[768,128]{1,0:T(8,128)(2,1)S(1)}, bf16[768,128]{1,0:T(8,128)(2,1)S(1)}, u32[]{:S(2)}, u32[]{:S(2)}) collective-permute-start(bf16[768,128]{1,0:T(8,128)(2,1)S(1)} %attention.4.refs_5_), channel_id=1, source_target_pairs={{0,4},{4,0},{8,12},{12,8},{16,20},{20,16},{24,28},{28,24},{1,5},{5... | collective-permute-start | bytes 589832 | tf_op jit(solution)/shard_map/ppermute | solution.py:605
  63.7 2.5 %collective-permute-start.24 = (bf16[768,128]{1,0:T(8,128)(2,1)S(1)}, bf16[768,128]{1,0:T(8,128)(2,1)S(1)}, u32[]{:S(2)}, u32[]{:S(2)}) collective-permute-start(bf16[768,128]{1,0:T(8,128)(2,1)S(1)} %collective-permute-done.21.refs_7_), channel_id=1, source_target_pairs={{0,4},{4,0},{8,12},{12,8},{16,20},{20,16},{24,28},{28,24},{1,5},{5... | collective-permute-start | bytes 589832 | tf_op jit(solution)/shard_map/ppermute | solution.py:605
  63.7 4.0 %collective-permute-start.25 = (bf16[768,128]{1,0:T(8,128)(2,1)S(1)}, bf16[768,128]{1,0:T(8,128)(2,1)S(1)}, u32[]{:S(2)}, u32[]{:S(2)}) collective-permute-start(bf16[768,128]{1,0:T(8,128)(2,1)S(1)} %collective-permute-done.22.refs_9_), channel_id=1, source_target_pairs={{0,4},{4,0},{8,12},{12,8},{16,20},{20,16},{24,28},{28,24},{1,5},{5... | collective-permute-start | bytes 589832 | tf_op jit(solution)/shard_map/ppermute | solution.py:605
  64.2 3.5 %collective-permute-start.26 = (bf16[768,128]{1,0:T(8,128)(2,1)S(1)}, bf16[768,128]{1,0:T(8,128)(2,1)S(1)}, u32[]{:S(2)}, u32[]{:S(2)}) collective-permute-start(bf16[768,128]{1,0:T(8,128)(2,1)S(1)} %collective-permute-done.23.refs_11_), channel_id=1, source_target_pairs={{0,4},{4,0},{8,12},{12,8},{16,20},{20,16},{24,28},{28,24},{1,5},{5... | collective-permute-start | bytes 589832 | tf_op jit(solution)/shard_map/ppermute | solution.py:605
  64.2 8.5 %collective-permute-start.10 = (bf16[768,128]{1,0:T(8,128)(2,1)S(1)}, bf16[768,128]{1,0:T(8,128)(2,1)S(1)}, u32[]{:S(2)}, u32[]{:S(2)}) collective-permute-start(bf16[768,128]{1,0:T(8,128)(2,1)S(1)} %attention.5.refs_5_), channel_id=1, source_target_pairs={{0,8},{4,12},{8,0},{12,4},{16,24},{20,28},{24,16},{28,20},{1,9},{5... | collective-permute-start | bytes 589832 | tf_op jit(solution)/shard_map/ppermute | solution.py:605
  65.7 11.2 %collective-permute-start.11 = (bf16[768,128]{1,0:T(8,128)(2,1)S(1)}, bf16[768,128]{1,0:T(8,128)(2,1)S(1)}, u32[]{:S(2)}, u32[]{:S(2)}) collective-permute-start(bf16[768,128]{1,0:T(8,128)(2,1)S(1)} %attention.5.refs_5_), channel_id=1, source_target_pairs={{0,16},{4,20},{8,24},{12,28},{16,0},{20,4},{24,8},{28,12},{1,17},{... | collective-permute-start | bytes 589832 | tf_op jit(solution)/shard_map/ppermute | solution.py:605
  66.2 10.7 %collective-permute-start.12 = (bf16[768,128]{1,0:T(8,128)(2,1)S(1)}, bf16[768,128]{1,0:T(8,128)(2,1)S(1)}, u32[]{:S(2)}, u32[]{:S(2)}) collective-permute-start(bf16[768,128]{1,0:T(8,128)(2,1)S(1)} %attention.5.refs_5_), channel_id=1, source_target_pairs={{0,24},{4,28},{8,16},{12,20},{16,8},{20,12},{24,0},{28,4},{1,25},{... | collective-permute-start | bytes 589832 | tf_op jit(solution)/shard_map/ppermute | solution.py:605
  67.7 9.8 %collective-permute-start.9 = (bf16[768,128]{1,0:T(8,128)(2,1)S(1)}, bf16[768,128]{1,0:T(8,128)(2,1)S(1)}, u32[]{:S(2)}, u32[]{:S(2)}) collective-permute-start(bf16[768,128]{1,0:T(8,128)(2,1)S(1)} %attention.5.refs_5_), channel_id=1, source_target_pairs={{0,4},{4,0},{8,12},{12,8},{16,20},{20,16},{24,28},{28,24},{1,5},{5... | collective-permute-start | bytes 589832 | tf_op jit(solution)/shard_map/ppermute | solution.py:605
  76.9 1.7 %collective-permute-start.28 = (bf16[768,128]{1,0:T(8,128)(2,1)S(1)}, bf16[768,128]{1,0:T(8,128)(2,1)S(1)}, u32[]{:S(2)}, u32[]{:S(2)}) collective-permute-start(bf16[768,128]{1,0:T(8,128)(2,1)S(1)} %collective-permute-done.11.refs_9_), channel_id=1, source_target_pairs={{0,4},{4,0},{8,12},{12,8},{16,20},{20,16},{24,28},{28,24},{1,5},{5... | collective-permute-start | bytes 589832 | tf_op jit(solution)/shard_map/ppermute | solution.py:605
  77.4 1.5 %collective-permute-start.29 = (bf16[768,128]{1,0:T(8,128)(2,1)S(1)}, bf16[768,128]{1,0:T(8,128)(2,1)S(1)}, u32[]{:S(2)}, u32[]{:S(2)}) collective-permute-start(bf16[768,128]{1,0:T(8,128)(2,1)S(1)} %collective-permute-done.12.refs_11_), channel_id=1, source_target_pairs={{0,4},{4,0},{8,12},{12,8},{16,20},{20,16},{24,28},{28,24},{1,5},{5... | collective-permute-start | bytes 589832 | tf_op jit(solution)/shard_map/ppermute | solution.py:605
  85.3 9.7 %collective-permute-start.30 = (bf16[672,128]{1,0:T(8,128)(2,1)S(1)}, bf16[672,128]{1,0:T(8,128)(2,1)S(1)}, u32[]{:S(2)}, u32[]{:S(2)}) collective-permute-start(bf16[672,128]{1,0:T(8,128)(2,1)S(1)} %get-tuple-element.88), channel_id=1, source_target_pairs={{0,1},{1,0},{2,3},{3,2},{4,5},{5,4},{6,7},{7,6},{8,9},{9,8},{10,11... | collective-permute-start | bytes 516104 | tf_op jit(solution)/shard_map/ppermute | solution.py:758
  87.0 15.5 %collective-permute-start.31 = (bf16[672,128]{1,0:T(8,128)(2,1)S(1)}, bf16[672,128]{1,0:T(8,128)(2,1)S(1)}, u32[]{:S(2)}, u32[]{:S(2)}) collective-permute-start(bf16[672,128]{1,0:T(8,128)(2,1)S(1)} %get-tuple-element.89), channel_id=1, source_target_pairs={{0,2},{1,3},{2,0},{3,1},{4,6},{5,7},{6,4},{7,5},{8,10},{9,11},{10,... | collective-permute-start | bytes 516104 | tf_op jit(solution)/shard_map/ppermute | solution.py:758
  89.6 12.9 %collective-permute-start.32 = (bf16[672,128]{1,0:T(8,128)(2,1)S(1)}, bf16[672,128]{1,0:T(8,128)(2,1)S(1)}, u32[]{:S(2)}, u32[]{:S(2)}) collective-permute-start(bf16[672,128]{1,0:T(8,128)(2,1)S(1)} %get-tuple-element.90), channel_id=1, source_target_pairs={{0,3},{1,2},{2,1},{3,0},{4,7},{5,6},{6,5},{7,4},{8,11},{9,10},{10,... | collective-permute-start | bytes 516104 | tf_op jit(solution)/shard_map/ppermute | solution.py:758
  (5 other events, 8.6 us)

commit v8 on v7

--- a/solution.py
+++ b/solution.py
@@ -150,8 +150,9 @@
 CHIP, CORE, PACK, IDS = 0, 1, 2, 3
 BLOCK = 256
 POSITIONS = 64
-NEGATIVE = -1e30
-CHUNKS = (512, 512, 512)
+FAR_APART = -(2.0**100)
+IMAGE_LANE = 96
+CHUNKS = (768, 768)
 
 
 def norm_rows(values, gain_row):
@@ -246,15 +247,19 @@
         b = columns[:, start + LANES : start + 2 * LANES]
         return a * cosine - b * sine, b * cosine + a * sine
 
-    query_a, query_b = turn(0)
+    factor = HD**-0.5 * float(np.log2(np.e))
+    query_a, query_b = (one * factor for one in turn(0))
     key_a, key_b = turn(2 * LANES)
     zero = jnp.zeros_like(key_a)
+    image = numbers == labels[:, :1] + IMAGE_LANE
+    extra = lane >= IMAGE_LANE
+    apart = jnp.where(image, 0.0, FAR_APART)
     parts = [
-        query_a,
+        jnp.where(image, 1.0, query_a),
         query_b,
-        jnp.where(first_head, key_a, zero),
+        jnp.where(extra, apart, jnp.where(first_head, key_a, zero)),
         jnp.where(first_head, key_b, zero),
-        jnp.where(first_head, zero, key_a),
+        jnp.where(extra, apart, jnp.where(first_head, zero, key_a)),
         jnp.where(first_head, zero, key_b),
     ]
     for head in range(2):
@@ -299,32 +304,25 @@
 
 def attention_kernel(start, first_owner, images, info, labels, block, *refs):
     out, *rest = refs
-    scores, high, rows_scratch = rest[-3:]
+    scores, high = rest[-2:]
     rows = high.shape[1]
     total = block.shape[0]
-    factor = HD**-0.5 * float(np.log2(np.e))
     segments = segment_row(labels[...])
-    for step in range(total // BLOCK):
-        rows_scratch[step] = segments[:, step * BLOCK : (step + 1) * BLOCK]
     own = labels[start : start + rows, :1].astype(jnp.float32)
     lowest, largest = jnp.min(own), jnp.max(own)
     one_row = segments[:1]
     begin = jnp.sum(jnp.where(one_row < lowest, 1, 0)) // BLOCK
     end = (jnp.sum(jnp.where(one_row <= largest, 1, 0)) + BLOCK - 1) // BLOCK
     queries = block[start : start + rows, : 2 * LANES]
-    own = jnp.broadcast_to(own, (rows, LANES))
-    high[...] = jnp.full_like(high, NEGATIVE)
+    high[...] = jnp.full_like(high, 2 * FAR_APART)
 
     def score(step, carry):
         at = pl.ds(pl.multiple_of(step * BLOCK, BLOCK), BLOCK)
-        theirs = rows_scratch[step, :1]
-        same = jnp.concatenate([own == theirs[:, :LANES], own == theirs[:, LANES:]], axis=1)
         for head in range(2):
             keys = block[at, (2 + 2 * head) * LANES : (4 + 2 * head) * LANES]
             values = lax.dot_general(
                 queries, keys, (((1,), (1,)), ((), ())), preferred_element_type=jnp.float32
             )
-            values = jnp.where(same, values, NEGATIVE)
             scores[head, step] = values
             high[head] = jnp.maximum(
                 high[head], jnp.maximum(values[:, :LANES], values[:, LANES:])
@@ -338,7 +336,7 @@
         at = pl.ds(pl.multiple_of(step * BLOCK, BLOCK), BLOCK)
         sums = []
         for head in range(2):
-            weights = jnp.exp2((scores[head, step] - highest[head]) * factor)
+            weights = jnp.exp2(scores[head, step] - highest[head])
             values = block[at, (6 + head) * LANES : (7 + head) * LANES]
             sums.append(
                 carry[head]
@@ -359,7 +357,7 @@
     packed = jnp.where(lane < tail, turned[:half], jnp.where(lane < 2 * tail, up, 0.0))
     out[rows:] = packed.astype(jnp.bfloat16)
 
-    if len(rest) > 3:
+    if len(rest) > 2:
         note = rest[0]
         row = lax.broadcasted_iota(jnp.int32, note.shape, 0)
         lane = lax.broadcasted_iota(jnp.int32, note.shape, 1)
@@ -389,7 +387,6 @@
         scratch_shapes=[
             pltpu.VMEM((2, total // BLOCK, rows, BLOCK), jnp.float32),
             pltpu.VMEM((2, rows, LANES), jnp.float32),
-            pltpu.VMEM((total // BLOCK, 8, BLOCK), jnp.float32),
         ],
         compiler_params=pltpu.CompilerParams(vmem_limit_bytes=20 << 20),
         cost_estimate=pl.CostEstimate(
@@ -640,10 +637,6 @@
     return [send_seq(upper, 4), send_seq(lower, 2)]
 
 
-def chip_shards(value):
-    return [value] + [send_seq(value, flip) for flip in (2, 4, 6)]
-
-
 def weight_order(heads_here):
     quarter = HD // 4
     order = -np.ones((6 * LANES,), np.int32)
@@ -735,18 +728,27 @@
     starts = [sum(CHUNKS[:number]) for number in range(len(CHUNKS))]
     attended, note = [], None
     for start, rows in zip(starts, CHUNKS):
-        if attended:
-            labels, block = after([labels, block], attended[-1][0])
         made = attention_call(start, rows, IDS + shards, info, labels, block, note is None)
         note = made[1] if note is None else note
-        attended.append(chip_shards(made[0]))
+        value = made[0]
+        if attended:
+            (value,) = after([value], *attended[-1][1])
+        attended.append((value, near_shards(value)))
     latest = attended[-1][0]
     most = 2 * (total // 4) // images
-    projected = []
+    projected, moving = [], []
+    for own, (own_swap, across_x, across_y) in attended:
+        previous = moving[-1][-1] if moving else ()
+        across_x, across_y = after([across_x, across_y], latest, *previous)
+        far = far_shards(across_x, across_y)
+        moving.append(
+            (own, own_swap, across_x, send_seq(across_x, 1), across_y, send_seq(across_y, 1), far)
+        )
     for number, (start, rows) in enumerate(zip(starts, CHUNKS)):
-        own, *others = attended[number]
-        others = after(others, latest, *projected)
-        sources = [[one] for share in (own, *others) for one in (share, send_seq(share, 1))]
+        *near, far = moving[number]
+        if projected:
+            far = after(far, projected[-1])
+        sources = [[one] for one in near] + [far, [send_seq(one, 1) for one in far]]
         route = ()
         if number == len(CHUNKS) - 1:
             route = (info, most, note, *projected)

time: 106 us -> 102 us (0.962); the launches traced: 104 us -> 102 us
  Pallas kernels: 46.8 us -> 41.8 us
  waiting for transfers between devices: 29.5 us -> 31.8 us
    pallas_call x3 -> x2, Pallas kernels: 12.4 us -> 8.82 us  [attention_call(): pl.pallas_call(functools.partial(attention_kernel, start, first_owner, in...]
    ppermute x30 -> x27, waiting for transfers between devices: 16.7 us -> 19.5 us  [send_seq(): return lax.ppermute(value, 'seq', [(i, i ^ flip) for i in range(size)])]
    ppermute x3, starting transfers between devices: 4.45 us -> 6.65 us  [fast_local(): lax.ppermute(made[flip], 'pack', [(z, z ^ flip) for z in range(packs)])]
    ppermute x30 -> x27, starting transfers between devices: 20.4 us -> 18.4 us  [send_seq(): return lax.ppermute(value, 'seq', [(i, i ^ flip) for i in range(size)])]
    pallas_call x3 -> x2, Pallas kernels: 16.4 us -> 14.7 us  [merge_call(): pl.pallas_call(functools.partial(merge_kernel, start, [len(source) for so...]
  transfers between devices with their start and end apart: 33 -> 30, of which waited for: 13 -> 15; matrix products, arithmetic and copies ran while one was open for 1% -> 1% of each run, Pallas kernels for 30% -> 24%
where the time goes in v8:
time: 102 us
  Pallas kernels  41.8 us (41%)
  waiting for transfers between devices  31.8 us (31%)
  starting transfers between devices  25.1 us (25%)
  local copies, waits for them, and re-layouts  2.79 us (3%)
    ppermute x27, waiting for transfers between devices, send_seq(): return lax.ppermute(value, 'seq', [(i, i ^ flip) for i in range(size)])  19.5 us
    ppermute x27, starting transfers between devices, send_seq(): return lax.ppermute(value, 'seq', [(i, i ^ flip) for i in range(size)])  18.4 us
    pallas_call x2, Pallas kernels, merge_call(): pl.pallas_call(functools.partial(merge_kernel, start, [len(source) for so...  14.7 us
    ppermute x3, waiting for transfers between devices, fast_local(): lax.ppermute(made[flip], 'pack', [(z, z ^ flip) for z in range(packs)])  12.3 us
    pallas_call x4, Pallas kernels, qkv_call(): pl.pallas_call(functools.partial(qkv_kernel, len(first), flip), in_specs=...  10 us
    pallas_call x2, Pallas kernels, attention_call(): pl.pallas_call(functools.partial(attention_kernel, start, first_owner, in...  8.82 us
    ppermute x3, starting transfers between devices, fast_local(): lax.ppermute(made[flip], 'pack', [(z, z ^ flip) for z in range(packs)])  6.65 us
    pallas_call x1, Pallas kernels, prepare_call(): pl.pallas_call(functools.partial(prepare_kernel, shards), in_specs=[pl.Bl...  5.1 us
  transfers between devices with their start and end apart: 30, of which 15 were waited for; matrix products, arithmetic and copies ran while one was open for 1% of the time, Pallas kernels for 24%

profile of v8, /device:TPU:0, one launch (start us, length us, event | category | flops | bytes accessed | tf_op | source)
XLA Modules:
  0.0 101.6 jit_solution(5824765683607839416)
XLA Ops:
  0.0 1.5 %payload.1.refs_0_ = bf16[192,1536]{1,0:T(8,128)(2,1)S(1)} custom-call(s32[1,192]{1,0:T(1,128)} %segments.1, s32[1,192]{1,0:T(1,128)} %rows.1, s32[1,192]{1,0:T(1,128)} %columns.1, s32[1,192]{1,0:T(1,128)} %mask.1, bf16[1408]{0:T(1024)(128)(2,1)} %embed.1, bf16[1,192,1408]{2,1,0:T(8,128)(2,1)} %patches.1), custom_call_target="tpu_custom_call" | custom-call | flops 270336 | bytes 1081344 | tf_op jit(solution)/shard_map/payload/pallas_call | solution.py:203
  2.0 2.6 %collective-permute-start = (bf16[192,1536]{1,0:T(8,128)(2,1)S(1)}, bf16[192,1536]{1,0:T(8,128)(2,1)S(1)}, u32[]{:S(2)}, u32[]{:S(2)}) collective-permute-start(bf16[192,1536]{1,0:T(8,128)(2,1)S(1)} %payload.1.refs_0_), channel_id=1, source_target_pairs={{0,8},{4,12},{8,0},{12,4},{16,24},{20,28},{24,16},{28,20},{1,9},{5... | collective-permute-start | bytes 1769480 | tf_op jit(solution)/shard_map/ppermute | solution.py:602
  4.6 1.5 %collective-permute-start.1 = (bf16[192,1536]{1,0:T(8,128)(2,1)S(1)}, bf16[192,1536]{1,0:T(8,128)(2,1)S(1)}, u32[]{:S(2)}, u32[]{:S(2)}) collective-permute-start(bf16[192,1536]{1,0:T(8,128)(2,1)S(1)} %payload.1.refs_0_), channel_id=1, source_target_pairs={{0,16},{4,20},{8,24},{12,28},{16,0},{20,4},{24,8},{28,12},{1,17},{... | collective-permute-start | bytes 1769480 | tf_op jit(solution)/shard_map/ppermute | solution.py:602
  8.9 5.1 %prepare.1 = (f32[1,1408]{1,0:T(1,128)S(1)}, f32[1,1408]{1,0:T(1,128)S(1)}, f32[1,448]{1,0:T(1,128)S(1)}, bf16[1536,1408]{1,0:T(8,128)(2,1)S(1)}, bf16[448,5632]...) custom-call(s32[15]{0:T(128)S(1)} %concatenate.3.info.refs_15_, bf16[1408,1408]{1,0:T(8,128)(2,1)} %out_weight.1, ...), custom_call_target="tpu_custom_call" | custom-call | flops 1141899264 | bytes 20996096 | tf_op jit(solution)/shard_map/prepare/pallas_call | solution.py:436
  14.0 2.5 %norm_qkv.4 = (bf16[1536,1408]{1,0:T(8,128)(2,1)S(1)}, bf16[1536,1024]{1,0:T(8,128)(2,1)S(1)}, bf16[1536,128]{1,0:T(8,128)(2,1)S(1)}) custom-call(s32[15]{0:T(128)S(1)} %concatenate.3.info.refs_15_, bf16[192,1536]{1,0:T(8,128)(2,1)S(1)} %payload.1.refs_0_, bf16[192,1536]{1,0:T(8,128)(2,1)S(1)} %collective-permute-done.2.refs_1_, ...), custom_call_target="tpu_custom_call" | custom-call | flops 2491416576 | bytes 6488064 | tf_op jit(solution)/shard_map/norm_qkv/pallas_call | solution.py:278
  16.5 1.9 %collective-permute-done.across_x.refs_0_ = bf16[192,1536]{1,0:T(8,128)(2,1)S(1)} collective-permute-done((bf16[192,1536]{1,0:T(8,128)(2,1)S(1)}, bf16[192,1536]{1,0:T(8,128)(2,1)S(1)}, u32[]{:S(2)}, u32[]{:S(2)}) %collective-permute-start) | collective-permute-done | bytes 589856 | tf_op jit(solution)/shard_map/ppermute | solution.py:602
  18.5 1.5 %collective-permute-done.1.across_y.refs_0_ = bf16[192,1536]{1,0:T(8,128)(2,1)S(1)} collective-permute-done((bf16[192,1536]{1,0:T(8,128)(2,1)S(1)}, bf16[192,1536]{1,0:T(8,128)(2,1)S(1)}, u32[]{:S(2)}, u32[]{:S(2)}) %collective-permute-start.1) | collective-permute-done | bytes 589856 | tf_op jit(solution)/shard_map/ppermute | solution.py:602
  20.5 1.6 %collective-permute-start.3 = (bf16[96,1536]{1,0:T(8,128)(2,1)S(1)}, bf16[96,1536]{1,0:T(8,128)(2,1)S(1)}, u32[]{:S(2)}, u32[]{:S(2)}) collective-permute-start(bf16[96,1536]{1,0:T(8,128)(2,1)S(1)} %get-tuple-element.52), channel_id=1, source_target_pairs={{0,16},{4,20},{8,24},{12,28},{16,0},{20,4},{24,8},{28,12},{1,17},{... | collective-permute-start | bytes 884744 | tf_op jit(solution)/shard_map/ppermute | solution.py:602
  22.6 2.5 %norm_qkv.5 = (bf16[1536,1408]{1,0:T(8,128)(2,1)S(1)}, bf16[1536,1024]{1,0:T(8,128)(2,1)S(1)}, bf16[1536,128]{1,0:T(8,128)(2,1)S(1)}) custom-call(s32[15]{0:T(128)S(1)} %concatenate.3.info.refs_15_, bf16[192,1536]{1,0:T(8,128)(2,1)S(1)} %collective-permute-done.across_x.refs_0_, ...), custom_call_target="tpu_custom_call", output_to_operand_aliasing={{0}: (6, {}), {1}: (7, {}), {2}: (8, {})} | custom-call | flops 2491416576 | bytes 6488064 | tf_op jit(solution)/shard_map/norm_qkv/pallas_call | solution.py:278
  25.2 2.5 %norm_qkv.6 = (bf16[1536,1408]{1,0:T(8,128)(2,1)S(1)}, bf16[1536,1024]{1,0:T(8,128)(2,1)S(1)}, bf16[1536,128]{1,0:T(8,128)(2,1)S(1)}) custom-call(s32[15]{0:T(128)S(1)} %concatenate.3.info.refs_15_, bf16[192,1536]{1,0:T(8,128)(2,1)S(1)} %collective-permute-done.1.across_y.refs_0_, ...), custom_call_target="tpu_custom_call", output_to_operand_aliasing={{0}: (6, {}), {1}: (7, {}), {2}: (8, {})} | custom-call | flops 2491416576 | bytes 6488064 | tf_op jit(solution)/shard_map/norm_qkv/pallas_call | solution.py:278
  27.7 1.8 %collective-permute-done.3.refs_0_ = bf16[96,1536]{1,0:T(8,128)(2,1)S(1)} collective-permute-done((bf16[96,1536]{1,0:T(8,128)(2,1)S(1)}, bf16[96,1536]{1,0:T(8,128)(2,1)S(1)}, u32[]{:S(2)}, u32[]{:S(2)}) %collective-permute-start.3) | collective-permute-done | bytes 294944 | tf_op jit(solution)/shard_map/ppermute | solution.py:602
  29.5 1.2 %collective-permute-done.4.refs_1_ = bf16[96,1536]{1,0:T(8,128)(2,1)S(1)} collective-permute-done((bf16[96,1536]{1,0:T(8,128)(2,1)S(1)}, bf16[96,1536]{1,0:T(8,128)(2,1)S(1)}, u32[]{:S(2)}, u32[]{:S(2)}) %collective-permute-start.4) | collective-permute-done | bytes 294944 | tf_op jit(solution)/shard_map/ppermute | solution.py:602
  31.2 1.1 %collective-permute-done.7.refs_2_ = bf16[96,1536]{1,0:T(8,128)(2,1)S(1)} collective-permute-done((bf16[96,1536]{1,0:T(8,128)(2,1)S(1)}, bf16[96,1536]{1,0:T(8,128)(2,1)S(1)}, u32[]{:S(2)}, u32[]{:S(2)}) %collective-permute-start.7) | collective-permute-done | bytes 294944 | tf_op jit(solution)/shard_map/ppermute | solution.py:602
  32.7 2.5 %norm_qkv.7 = (bf16[1536,1408]{1,0:T(8,128)(2,1)S(1)}, bf16[1536,1024]{1,0:T(8,128)(2,1)S(1)}, bf16[1536,128]{1,0:T(8,128)(2,1)S(1)}) custom-call(s32[15]{0:T(128)S(1)} %concatenate.3.info.refs_15_, bf16[96,1536]{1,0:T(8,128)(2,1)S(1)} %collective-permute-done.3.refs_0_, ...), custom_call_target="tpu_custom_call", output_to_operand_aliasing={{0}: (8, {}), {1}: (9, {}), {2}: (10, {})} | custom-call | flops 2491416576 | bytes 6488064 | tf_op jit(solution)/shard_map/norm_qkv/pallas_call | solution.py:278
  35.2 4.3 %attention.3 = (bf16[1152,128]{1,0:T(8,128)(2,1)S(1)}, bf16[16,128]{1,0:T(8,128)(2,1)S(1)}) custom-call(s32[15]{0:T(128)S(1)} %concatenate.3.info.refs_15_, bf16[1536,128]{1,0:T(8,128)(2,1)S(1)} %get-tuple-element.68.labels, bf16[1536,1024]{1,0:T(8,128)(2,1)S(1)} %get-tuple-element.69.block), custom_call_target="tpu_custom_call" | custom-call | flops 3019898880 | bytes 3145728 | tf_op jit(solution)/shard_map/attention/pallas_call | solution.py:382
  40.5 4.5 %attention.2.refs_5_ = bf16[1152,128]{1,0:T(8,128)(2,1)S(1)} custom-call(s32[15]{0:T(128)S(1)} %concatenate.3.info.refs_15_, bf16[1536,128]{1,0:T(8,128)(2,1)S(1)} %get-tuple-element.68.labels, bf16[1536,1024]{1,0:T(8,128)(2,1)S(1)} %get-tuple-element.69.block), custom_call_target="tpu_custom_call" | custom-call | flops 3019898880 | bytes 3145728 | tf_op jit(solution)/shard_map/attention/pallas_call | solution.py:382
  45.0 3.7 %collective-permute-done.10.across_x.refs_7_ = bf16[1152,128]{1,0:T(8,128)(2,1)S(1)} collective-permute-done((bf16[1152,128]{1,0:T(8,128)(2,1)S(1)}, bf16[1152,128]{1,0:T(8,128)(2,1)S(1)}, u32[]{:S(2)}, u32[]{:S(2)}) %collective-permute-start.10) | collective-permute-done | bytes 294944 | tf_op jit(solution)/shard_map/ppermute | solution.py:602
  49.4 1.6 %collective-permute-start.13 = (bf16[1152,128]{1,0:T(8,128)(2,1)S(1)}, bf16[1152,128]{1,0:T(8,128)(2,1)S(1)}, u32[]{:S(2)}, u32[]{:S(2)}) collective-permute-start(bf16[1152,128]{1,0:T(8,128)(2,1)S(1)} %attention.2.refs_5_), channel_id=1, source_target_pairs={{0,8},{4,12},{8,0},{12,4},{16,24},{20,28},{24,16},{28,20},{1,9},{5... | collective-permute-start | bytes 884744 | tf_op jit(solution)/shard_map/ppermute | solution.py:602
  51.0 1.5 %collective-permute-start.14 = (bf16[1152,128]{1,0:T(8,128)(2,1)S(1)}, bf16[1152,128]{1,0:T(8,128)(2,1)S(1)}, u32[]{:S(2)}, u32[]{:S(2)}) collective-permute-start(bf16[1152,128]{1,0:T(8,128)(2,1)S(1)} %attention.2.refs_5_), channel_id=1, source_target_pairs={{0,16},{4,20},{8,24},{12,28},{16,0},{20,4},{24,8},{28,12},{1,17},{... | collective-permute-start | bytes 884744 | tf_op jit(solution)/shard_map/ppermute | solution.py:602
  53.1 2.8 %collective-permute-done.15.refs_11_ = bf16[576,128]{1,0:T(8,128)(2,1)S(1)} collective-permute-done((bf16[576,128]{1,0:T(8,128)(2,1)S(1)}, bf16[576,128]{1,0:T(8,128)(2,1)S(1)}, u32[]{:S(2)}, u32[]{:S(2)}) %collective-permute-start.15) | collective-permute-done | bytes 147488 | tf_op jit(solution)/shard_map/ppermute | solution.py:602
  55.8 1.5 %collective-permute-start.16 = (bf16[576,128]{1,0:T(8,128)(2,1)S(1)}, bf16[576,128]{1,0:T(8,128)(2,1)S(1)}, u32[]{:S(2)}, u32[]{:S(2)}) collective-permute-start(bf16[576,128]{1,0:T(8,128)(2,1)S(1)} %get-tuple-element.75), channel_id=1, source_target_pairs={{0,8},{4,12},{8,0},{12,4},{16,24},{20,28},{24,16},{28,20},{1,9},{5... | collective-permute-start | bytes 442376 | tf_op jit(solution)/shard_map/ppermute | solution.py:602
  57.3 3.7 %collective-permute-done.16.refs_12_ = bf16[576,128]{1,0:T(8,128)(2,1)S(1)} collective-permute-done((bf16[576,128]{1,0:T(8,128)(2,1)S(1)}, bf16[576,128]{1,0:T(8,128)(2,1)S(1)}, u32[]{:S(2)}, u32[]{:S(2)}) %collective-permute-start.16) | collective-permute-done | bytes 147488 | tf_op jit(solution)/shard_map/ppermute | solution.py:602
  62.3 1.0 collective-permute-start.19
  63.3 1.4 %collective-permute-start.20 = (bf16[576,128]{1,0:T(8,128)(2,1)S(1)}, bf16[576,128]{1,0:T(8,128)(2,1)S(1)}, u32[]{:S(2)}, u32[]{:S(2)}) collective-permute-start(bf16[576,128]{1,0:T(8,128)(2,1)S(1)} %get-tuple-element.79), channel_id=1, source_target_pairs={{0,8},{4,12},{8,0},{12,4},{16,24},{20,28},{24,16},{28,20},{1,9},{5... | collective-permute-start | bytes 442376 | tf_op jit(solution)/shard_map/ppermute | solution.py:602
  64.7 6.7 %out_merge.2.refs_17_ = bf16[192,448]{1,0:T(8,128)(2,1)S(1)} custom-call(bf16[1536,1408]{1,0:T(8,128)(2,1)S(1)} %get-tuple-element.64.refs_0_, bf16[1536,1408]{1,0:T(8,128)(2,1)S(1)} %get-tuple-element.49.refs_1_, f32[1,1408]{1,0:T(1,128)S(1)} %get-tuple-element.65.refs_2_, bf16[448,5632]{1,0:T(8,128)(2,1)S(1)} %get-tuple-element.66.refs_3_, ...), custom_call_target="tpu_custom_call" | custom-call | flops 7059013632 | bytes 15499264 | tf_op jit(solution)/shard_map/out_merge/pallas_call | solution.py:549
  73.1 8.0 %out_merge.3 = (bf16[672,128]{1,0:T(8,128)(2,1)S(1)}, bf16[672,128]{1,0:T(8,128)(2,1)S(1)}, bf16[672,128]{1,0:T(8,128)(2,1)S(1)}, bf16[672,128]{1,0:T(8,128)(2,1)S(1)}) custom-call(bf16[1536,1408]{1,0:T(8,128)(2,1)S(1)} %get-tuple-element.64.refs_0_, bf16[1536,1408]{1,0:T(8,128)(2,1)S(1)} %get-tuple-element.49.refs_1_, ...), custom_call_target="tpu_custom_call" | custom-call | flops 7059013632 | bytes 15499264 | tf_op jit(solution)/shard_map/out_merge/pallas_call | solution.py:549
  81.1 3.4 %collective-permute-start.27 = (bf16[672,128]{1,0:T(8,128)(2,1)S(1)}, bf16[672,128]{1,0:T(8,128)(2,1)S(1)}, u32[]{:S(2)}, u32[]{:S(2)}) collective-permute-start(bf16[672,128]{1,0:T(8,128)(2,1)S(1)} %get-tuple-element.84), channel_id=1, source_target_pairs={{0,1},{1,0},{2,3},{3,2},{4,5},{5,4},{6,7},{7,6},{8,9},{9,8},{10,11... | collective-permute-start | bytes 516104 | tf_op jit(solution)/shard_map/ppermute | solution.py:760
  84.5 1.9 %collective-permute-start.28 = (bf16[672,128]{1,0:T(8,128)(2,1)S(1)}, bf16[672,128]{1,0:T(8,128)(2,1)S(1)}, u32[]{:S(2)}, u32[]{:S(2)}) collective-permute-start(bf16[672,128]{1,0:T(8,128)(2,1)S(1)} %get-tuple-element.85), channel_id=1, source_target_pairs={{0,2},{1,3},{2,0},{3,1},{4,6},{5,7},{6,4},{7,5},{8,10},{9,11},{10,... | collective-permute-start | bytes 516104 | tf_op jit(solution)/shard_map/ppermute | solution.py:760
  86.4 1.4 %collective-permute-start.29 = (bf16[672,128]{1,0:T(8,128)(2,1)S(1)}, bf16[672,128]{1,0:T(8,128)(2,1)S(1)}, u32[]{:S(2)}, u32[]{:S(2)}) collective-permute-start(bf16[672,128]{1,0:T(8,128)(2,1)S(1)} %get-tuple-element.86), channel_id=1, source_target_pairs={{0,3},{1,2},{2,1},{3,0},{4,7},{5,6},{6,5},{7,4},{8,11},{9,10},{10,... | collective-permute-start | bytes 516104 | tf_op jit(solution)/shard_map/ppermute | solution.py:760
  87.7 5.0 %collective-permute-done.27.refs_1_ = bf16[672,128]{1,0:T(8,128)(2,1)S(1)} collective-permute-done((bf16[672,128]{1,0:T(8,128)(2,1)S(1)}, bf16[672,128]{1,0:T(8,128)(2,1)S(1)}, u32[]{:S(2)}, u32[]{:S(2)}) %collective-permute-start.27) | collective-permute-done | bytes 172064 | tf_op jit(solution)/shard_map/ppermute | solution.py:760
  92.8 7.2 %collective-permute-done.28.refs_2_ = bf16[672,128]{1,0:T(8,128)(2,1)S(1)} collective-permute-done((bf16[672,128]{1,0:T(8,128)(2,1)S(1)}, bf16[672,128]{1,0:T(8,128)(2,1)S(1)}, u32[]{:S(2)}, u32[]{:S(2)}) %collective-permute-start.28) | collective-permute-done | bytes 172064 | tf_op jit(solution)/shard_map/ppermute | solution.py:760
  100.0 1.6 %place_rows.1 = bf16[4,192,448]{2,1,0:T(8,128)(2,1)} custom-call(s32[15]{0:T(128)S(1)} %concatenate.3.info.refs_15_, bf16[672,128]{1,0:T(8,128)(2,1)S(1)} %get-tuple-element.83.refs_0_, bf16[672,128]{1,0:T(8,128)(2,1)S(1)} %collective-permute-done.27.refs_1_, bf16[672,128]{1,0:T(8,128)(2,1)S(1)} %collective-permute-done.28.refs_2_, ...), custom_call_target="tpu_custom_call" | custom-call | bytes 1376256 | tf_op jit(solution)/shard_map/place_rows/pallas_call | solution.py:586
  (51 shorter events, 10.5 us)
Async XLA Ops:
  1.5 12.5 %collective-permute-start.2 = (bf16[192,1536]{1,0:T(8,128)(2,1)S(1)}, bf16[192,1536]{1,0:T(8,128)(2,1)S(1)}, u32[]{:S(2)}, u32[]{:S(2)}) collective-permute-start(bf16[192,1536]{1,0:T(8,128)(2,1)S(1)} %payload.1.refs_0_), channel_id=1, source_target_pairs={{0,4},{4,0},{8,12},{12,8},{16,20},{20,16},{24,28},{28,24},{1,5},{5... | collective-permute-start | bytes 1769480 | tf_op jit(solution)/shard_map/ppermute | solution.py:602
  2.0 16.5 %collective-permute-start = (bf16[192,1536]{1,0:T(8,128)(2,1)S(1)}, bf16[192,1536]{1,0:T(8,128)(2,1)S(1)}, u32[]{:S(2)}, u32[]{:S(2)}) collective-permute-start(bf16[192,1536]{1,0:T(8,128)(2,1)S(1)} %payload.1.refs_0_), channel_id=1, source_target_pairs={{0,8},{4,12},{8,0},{12,4},{16,24},{20,28},{24,16},{28,20},{1,9},{5... | collective-permute-start | bytes 1769480 | tf_op jit(solution)/shard_map/ppermute | solution.py:602
  4.6 15.4 %collective-permute-start.1 = (bf16[192,1536]{1,0:T(8,128)(2,1)S(1)}, bf16[192,1536]{1,0:T(8,128)(2,1)S(1)}, u32[]{:S(2)}, u32[]{:S(2)}) collective-permute-start(bf16[192,1536]{1,0:T(8,128)(2,1)S(1)} %payload.1.refs_0_), channel_id=1, source_target_pairs={{0,16},{4,20},{8,24},{12,28},{16,0},{20,4},{24,8},{28,12},{1,17},{... | collective-permute-start | bytes 1769480 | tf_op jit(solution)/shard_map/ppermute | solution.py:602
  6.8 0.7 copy-start.1
  8.9 5.1 %copy-start = (bf16[128,512]{1,0:T(8,128)(2,1)S(1)}, bf16[128,512]{1,0:T(8,128)(2,1)}, u32[]{:S(2)}) copy-start(bf16[128,512]{1,0:T(8,128)(2,1)} %constant.48.clone.refs_2_.refs_4_) | copy-start | bytes 393220
  20.0 2.7 %collective-permute-start.6 = (bf16[192,1536]{1,0:T(8,128)(2,1)S(1)}, bf16[192,1536]{1,0:T(8,128)(2,1)S(1)}, u32[]{:S(2)}, u32[]{:S(2)}) collective-permute-start(bf16[192,1536]{1,0:T(8,128)(2,1)S(1)} %collective-permute-done.across_x.refs_0_), channel_id=1, source_target_pairs={{0,4},{4,0},{8,12},{12,8},{16,20},{20,16},{24,28},{28,24},{1,5},{5... | collective-permute-start | bytes 1769480 | tf_op jit(solution)/shard_map/ppermute | solution.py:602
  20.0 5.2 %collective-permute-start.5 = (bf16[192,1536]{1,0:T(8,128)(2,1)S(1)}, bf16[192,1536]{1,0:T(8,128)(2,1)S(1)}, u32[]{:S(2)}, u32[]{:S(2)}) collective-permute-start(bf16[192,1536]{1,0:T(8,128)(2,1)S(1)} %collective-permute-done.1.across_y.refs_0_), channel_id=1, source_target_pairs={{0,4},{4,0},{8,12},{12,8},{16,20},{20,16},{24,28},{28,24},{1,5},{5... | collective-permute-start | bytes 1769480 | tf_op jit(solution)/shard_map/ppermute | solution.py:602
  20.5 9.0 %collective-permute-start.3 = (bf16[96,1536]{1,0:T(8,128)(2,1)S(1)}, bf16[96,1536]{1,0:T(8,128)(2,1)S(1)}, u32[]{:S(2)}, u32[]{:S(2)}) collective-permute-start(bf16[96,1536]{1,0:T(8,128)(2,1)S(1)} %get-tuple-element.52), channel_id=1, source_target_pairs={{0,16},{4,20},{8,24},{12,28},{16,0},{20,4},{24,8},{28,12},{1,17},{... | collective-permute-start | bytes 884744 | tf_op jit(solution)/shard_map/ppermute | solution.py:602
  22.1 8.6 %collective-permute-start.4 = (bf16[96,1536]{1,0:T(8,128)(2,1)S(1)}, bf16[96,1536]{1,0:T(8,128)(2,1)S(1)}, u32[]{:S(2)}, u32[]{:S(2)}) collective-permute-start(bf16[96,1536]{1,0:T(8,128)(2,1)S(1)} %get-tuple-element.53), channel_id=1, source_target_pairs={{0,8},{4,12},{8,0},{12,4},{16,24},{20,28},{24,16},{28,20},{1,9},{5... | collective-permute-start | bytes 884744 | tf_op jit(solution)/shard_map/ppermute | solution.py:602
  30.7 1.6 %collective-permute-start.7 = (bf16[96,1536]{1,0:T(8,128)(2,1)S(1)}, bf16[96,1536]{1,0:T(8,128)(2,1)S(1)}, u32[]{:S(2)}, u32[]{:S(2)}) collective-permute-start(bf16[96,1536]{1,0:T(8,128)(2,1)S(1)} %collective-permute-done.3.refs_0_), channel_id=1, source_target_pairs={{0,4},{4,0},{8,12},{12,8},{16,20},{20,16},{24,28},{28,24},{1,5},{5... | collective-permute-start | bytes 884744 | tf_op jit(solution)/shard_map/ppermute | solution.py:602
  30.7 2.0 %collective-permute-start.8 = (bf16[96,1536]{1,0:T(8,128)(2,1)S(1)}, bf16[96,1536]{1,0:T(8,128)(2,1)S(1)}, u32[]{:S(2)}, u32[]{:S(2)}) collective-permute-start(bf16[96,1536]{1,0:T(8,128)(2,1)S(1)} %collective-permute-done.4.refs_1_), channel_id=1, source_target_pairs={{0,4},{4,0},{8,12},{12,8},{16,20},{20,16},{24,28},{28,24},{1,5},{5... | collective-permute-start | bytes 884744 | tf_op jit(solution)/shard_map/ppermute | solution.py:602
  39.5 9.1 %collective-permute-start.10 = (bf16[1152,128]{1,0:T(8,128)(2,1)S(1)}, bf16[1152,128]{1,0:T(8,128)(2,1)S(1)}, u32[]{:S(2)}, u32[]{:S(2)}) collective-permute-start(bf16[1152,128]{1,0:T(8,128)(2,1)S(1)} %get-tuple-element.70.refs_5_), channel_id=1, source_target_pairs={{0,8},{4,12},{8,0},{12,4},{16,24},{20,28},{24,16},{28,20},{1,9},{5... | collective-permute-start | bytes 884744 | tf_op jit(solution)/shard_map/ppermute | solution.py:602
  40.2 8.8 %collective-permute-start.11 = (bf16[1152,128]{1,0:T(8,128)(2,1)S(1)}, bf16[1152,128]{1,0:T(8,128)(2,1)S(1)}, u32[]{:S(2)}, u32[]{:S(2)}) collective-permute-start(bf16[1152,128]{1,0:T(8,128)(2,1)S(1)} %get-tuple-element.70.refs_5_), channel_id=1, source_target_pairs={{0,16},{4,20},{8,24},{12,28},{16,0},{20,4},{24,8},{28,12},{1,17},{... | collective-permute-start | bytes 884744 | tf_op jit(solution)/shard_map/ppermute | solution.py:602
  40.5 8.4 %collective-permute-start.9 = (bf16[1152,128]{1,0:T(8,128)(2,1)S(1)}, bf16[1152,128]{1,0:T(8,128)(2,1)S(1)}, u32[]{:S(2)}, u32[]{:S(2)}) collective-permute-start(bf16[1152,128]{1,0:T(8,128)(2,1)S(1)} %get-tuple-element.70.refs_5_), channel_id=1, source_target_pairs={{0,4},{4,0},{8,12},{12,8},{16,20},{20,16},{24,28},{28,24},{1,5},{5... | collective-permute-start | bytes 884744 | tf_op jit(solution)/shard_map/ppermute | solution.py:602
  49.0 6.8 %collective-permute-start.15 = (bf16[576,128]{1,0:T(8,128)(2,1)S(1)}, bf16[576,128]{1,0:T(8,128)(2,1)S(1)}, u32[]{:S(2)}, u32[]{:S(2)}) collective-permute-start(bf16[576,128]{1,0:T(8,128)(2,1)S(1)} %get-tuple-element.74), channel_id=1, source_target_pairs={{0,16},{4,20},{8,24},{12,28},{16,0},{20,4},{24,8},{28,12},{1,17},{... | collective-permute-start | bytes 442376 | tf_op jit(solution)/shard_map/ppermute | solution.py:602
  49.4 11.6 %collective-permute-start.13 = (bf16[1152,128]{1,0:T(8,128)(2,1)S(1)}, bf16[1152,128]{1,0:T(8,128)(2,1)S(1)}, u32[]{:S(2)}, u32[]{:S(2)}) collective-permute-start(bf16[1152,128]{1,0:T(8,128)(2,1)S(1)} %attention.2.refs_5_), channel_id=1, source_target_pairs={{0,8},{4,12},{8,0},{12,4},{16,24},{20,28},{24,16},{28,20},{1,9},{5... | collective-permute-start | bytes 884744 | tf_op jit(solution)/shard_map/ppermute | solution.py:602
  51.0 10.4 %collective-permute-start.14 = (bf16[1152,128]{1,0:T(8,128)(2,1)S(1)}, bf16[1152,128]{1,0:T(8,128)(2,1)S(1)}, u32[]{:S(2)}, u32[]{:S(2)}) collective-permute-start(bf16[1152,128]{1,0:T(8,128)(2,1)S(1)} %attention.2.refs_5_), channel_id=1, source_target_pairs={{0,16},{4,20},{8,24},{12,28},{16,0},{20,4},{24,8},{28,12},{1,17},{... | collective-permute-start | bytes 884744 | tf_op jit(solution)/shard_map/ppermute | solution.py:602
  52.5 9.0 %collective-permute-start.21 = (bf16[1152,128]{1,0:T(8,128)(2,1)S(1)}, bf16[1152,128]{1,0:T(8,128)(2,1)S(1)}, u32[]{:S(2)}, u32[]{:S(2)}) collective-permute-start(bf16[1152,128]{1,0:T(8,128)(2,1)S(1)} %collective-permute-done.10.across_x.refs_7_), channel_id=1, source_target_pairs={{0,4},{4,0},{8,12},{12,8},{16,20},{20,16},{24,28},{28,24},{1,5},{5... | collective-permute-start | bytes 884744 | tf_op jit(solution)/shard_map/ppermute | solution.py:602
  52.5 9.5 %collective-permute-start.22 = (bf16[1152,128]{1,0:T(8,128)(2,1)S(1)}, bf16[1152,128]{1,0:T(8,128)(2,1)S(1)}, u32[]{:S(2)}, u32[]{:S(2)}) collective-permute-start(bf16[1152,128]{1,0:T(8,128)(2,1)S(1)} %collective-permute-done.11.across_y.refs_9_), channel_id=1, source_target_pairs={{0,4},{4,0},{8,12},{12,8},{16,20},{20,16},{24,28},{28,24},{1,5},{5... | collective-permute-start | bytes 884744 | tf_op jit(solution)/shard_map/ppermute | solution.py:602
  55.8 5.1 %collective-permute-start.16 = (bf16[576,128]{1,0:T(8,128)(2,1)S(1)}, bf16[576,128]{1,0:T(8,128)(2,1)S(1)}, u32[]{:S(2)}, u32[]{:S(2)}) collective-permute-start(bf16[576,128]{1,0:T(8,128)(2,1)S(1)} %get-tuple-element.75), channel_id=1, source_target_pairs={{0,8},{4,12},{8,0},{12,4},{16,24},{20,28},{24,16},{28,20},{1,9},{5... | collective-permute-start | bytes 442376 | tf_op jit(solution)/shard_map/ppermute | solution.py:602
  61.0 1.4 %collective-permute-start.23 = (bf16[576,128]{1,0:T(8,128)(2,1)S(1)}, bf16[576,128]{1,0:T(8,128)(2,1)S(1)}, u32[]{:S(2)}, u32[]{:S(2)}) collective-permute-start(bf16[576,128]{1,0:T(8,128)(2,1)S(1)} %collective-permute-done.15.refs_11_), channel_id=1, source_target_pairs={{0,4},{4,0},{8,12},{12,8},{16,20},{20,16},{24,28},{28,24},{1,5},{5... | collective-permute-start | bytes 442376 | tf_op jit(solution)/shard_map/ppermute | solution.py:602
  61.0 2.3 %collective-permute-start.24 = (bf16[576,128]{1,0:T(8,128)(2,1)S(1)}, bf16[576,128]{1,0:T(8,128)(2,1)S(1)}, u32[]{:S(2)}, u32[]{:S(2)}) collective-permute-start(bf16[576,128]{1,0:T(8,128)(2,1)S(1)} %collective-permute-done.16.refs_12_), channel_id=1, source_target_pairs={{0,4},{4,0},{8,12},{12,8},{16,20},{20,16},{24,28},{28,24},{1,5},{5... | collective-permute-start | bytes 442376 | tf_op jit(solution)/shard_map/ppermute | solution.py:602
  61.5 10.5 %collective-permute-start.12 = (bf16[1152,128]{1,0:T(8,128)(2,1)S(1)}, bf16[1152,128]{1,0:T(8,128)(2,1)S(1)}, u32[]{:S(2)}, u32[]{:S(2)}) collective-permute-start(bf16[1152,128]{1,0:T(8,128)(2,1)S(1)} %attention.2.refs_5_), channel_id=1, source_target_pairs={{0,4},{4,0},{8,12},{12,8},{16,20},{20,16},{24,28},{28,24},{1,5},{5... | collective-permute-start | bytes 884744 | tf_op jit(solution)/shard_map/ppermute | solution.py:602
  61.6 10.4 %collective-permute-start.17 = (bf16[1152,128]{1,0:T(8,128)(2,1)S(1)}, bf16[1152,128]{1,0:T(8,128)(2,1)S(1)}, u32[]{:S(2)}, u32[]{:S(2)}) collective-permute-start(bf16[1152,128]{1,0:T(8,128)(2,1)S(1)} %collective-permute-done.13.across_x.refs_7_), channel_id=1, source_target_pairs={{0,4},{4,0},{8,12},{12,8},{16,20},{20,16},{24,28},{28,24},{1,5},{5... | collective-permute-start | bytes 884744 | tf_op jit(solution)/shard_map/ppermute | solution.py:602
  62.1 9.9 %collective-permute-start.18 = (bf16[1152,128]{1,0:T(8,128)(2,1)S(1)}, bf16[1152,128]{1,0:T(8,128)(2,1)S(1)}, u32[]{:S(2)}, u32[]{:S(2)}) collective-permute-start(bf16[1152,128]{1,0:T(8,128)(2,1)S(1)} %collective-permute-done.14.across_y.refs_9_), channel_id=1, source_target_pairs={{0,4},{4,0},{8,12},{12,8},{16,20},{20,16},{24,28},{28,24},{1,5},{5... | collective-permute-start | bytes 884744 | tf_op jit(solution)/shard_map/ppermute | solution.py:602
  62.3 9.1 %collective-permute-start.19 = (bf16[576,128]{1,0:T(8,128)(2,1)S(1)}, bf16[576,128]{1,0:T(8,128)(2,1)S(1)}, u32[]{:S(2)}, u32[]{:S(2)}) collective-permute-start(bf16[576,128]{1,0:T(8,128)(2,1)S(1)} %get-tuple-element.78), channel_id=1, source_target_pairs={{0,16},{4,20},{8,24},{12,28},{16,0},{20,4},{24,8},{28,12},{1,17},{... | collective-permute-start | bytes 442376 | tf_op jit(solution)/shard_map/ppermute | solution.py:602
  63.3 8.1 %collective-permute-start.20 = (bf16[576,128]{1,0:T(8,128)(2,1)S(1)}, bf16[576,128]{1,0:T(8,128)(2,1)S(1)}, u32[]{:S(2)}, u32[]{:S(2)}) collective-permute-start(bf16[576,128]{1,0:T(8,128)(2,1)S(1)} %get-tuple-element.79), channel_id=1, source_target_pairs={{0,8},{4,12},{8,0},{12,4},{16,24},{20,28},{24,16},{28,20},{1,9},{5... | collective-permute-start | bytes 442376 | tf_op jit(solution)/shard_map/ppermute | solution.py:602
  71.4 1.4 %collective-permute-start.25 = (bf16[576,128]{1,0:T(8,128)(2,1)S(1)}, bf16[576,128]{1,0:T(8,128)(2,1)S(1)}, u32[]{:S(2)}, u32[]{:S(2)}) collective-permute-start(bf16[576,128]{1,0:T(8,128)(2,1)S(1)} %collective-permute-done.19.refs_11_), channel_id=1, source_target_pairs={{0,4},{4,0},{8,12},{12,8},{16,20},{20,16},{24,28},{28,24},{1,5},{5... | collective-permute-start | bytes 442376 | tf_op jit(solution)/shard_map/ppermute | solution.py:602
  71.5 1.6 %collective-permute-start.26 = (bf16[576,128]{1,0:T(8,128)(2,1)S(1)}, bf16[576,128]{1,0:T(8,128)(2,1)S(1)}, u32[]{:S(2)}, u32[]{:S(2)}) collective-permute-start(bf16[576,128]{1,0:T(8,128)(2,1)S(1)} %collective-permute-done.20.refs_12_), channel_id=1, source_target_pairs={{0,4},{4,0},{8,12},{12,8},{16,20},{20,16},{24,28},{28,24},{1,5},{5... | collective-permute-start | bytes 442376 | tf_op jit(solution)/shard_map/ppermute | solution.py:602
  81.1 11.7 %collective-permute-start.27 = (bf16[672,128]{1,0:T(8,128)(2,1)S(1)}, bf16[672,128]{1,0:T(8,128)(2,1)S(1)}, u32[]{:S(2)}, u32[]{:S(2)}) collective-permute-start(bf16[672,128]{1,0:T(8,128)(2,1)S(1)} %get-tuple-element.84), channel_id=1, source_target_pairs={{0,1},{1,0},{2,3},{3,2},{4,5},{5,4},{6,7},{7,6},{8,9},{9,8},{10,11... | collective-permute-start | bytes 516104 | tf_op jit(solution)/shard_map/ppermute | solution.py:760
  84.5 15.6 %collective-permute-start.28 = (bf16[672,128]{1,0:T(8,128)(2,1)S(1)}, bf16[672,128]{1,0:T(8,128)(2,1)S(1)}, u32[]{:S(2)}, u32[]{:S(2)}) collective-permute-start(bf16[672,128]{1,0:T(8,128)(2,1)S(1)} %get-tuple-element.85), channel_id=1, source_target_pairs={{0,2},{1,3},{2,0},{3,1},{4,6},{5,7},{6,4},{7,5},{8,10},{9,11},{10,... | collective-permute-start | bytes 516104 | tf_op jit(solution)/shard_map/ppermute | solution.py:760
  86.4 13.7 %collective-permute-start.29 = (bf16[672,128]{1,0:T(8,128)(2,1)S(1)}, bf16[672,128]{1,0:T(8,128)(2,1)S(1)}, u32[]{:S(2)}, u32[]{:S(2)}) collective-permute-start(bf16[672,128]{1,0:T(8,128)(2,1)S(1)} %get-tuple-element.86), channel_id=1, source_target_pairs={{0,3},{1,2},{2,1},{3,0},{4,7},{5,6},{6,5},{7,4},{8,11},{9,10},{10,... | collective-permute-start | bytes 516104 | tf_op jit(solution)/shard_map/ppermute | solution.py:760
  (2 other events, 1.4 us)

commit v9 on v8

--- a/solution.py
+++ b/solution.py
@@ -152,6 +152,8 @@
 POSITIONS = 64
 FAR_APART = -(2.0**100)
 IMAGE_LANE = 96
+ROW_BLOCK = 128
+NORM_ROWS = 16
 CHUNKS = (768, 768)
 
 
@@ -217,20 +219,27 @@
 def qkv_kernel(count, flip, info, *refs):
     first, second = refs[:count], refs[count : 2 * count]
     table, gain, weight = refs[2 * count : 2 * count + 3]
-    inputs_out, qkv_out, label_out = refs[-3:]
-    mine, other = stacked(first), stacked(second)
+    inputs_out, qkv_out, label_out, normed = refs[-4:]
     leads = info[CORE] == 0
-    ahead = jnp.where(leads, mine, other)
-    behind = jnp.where(leads, other, mine)
-    both = jnp.concatenate([ahead, behind], axis=0)
-    rows = both.shape[0]
-    at = pl.ds(pl.multiple_of((info[CHIP] ^ flip) * rows, rows), rows)
-    inputs_out[at, :] = both[:, :D]
-    label_out[at, :] = both[:, D:]
-    labels = both[:, D:].astype(jnp.float32)
-    normed = norm_rows(both[:, :D].astype(jnp.float32), gain[...]).astype(jnp.bfloat16)
+    half = sum(piece.shape[0] for piece in first)
+    rows = 2 * half
+    base = pl.multiple_of((info[CHIP] ^ flip) * rows, rows)
+    at = pl.ds(base, rows)
+    for behind, pieces in ((~leads, first), (leads, second)):
+        done = jnp.where(behind, half, 0)
+        for piece in pieces:
+            size = piece.shape[0]
+            target = pl.ds(pl.multiple_of(base + done, NORM_ROWS), size)
+            inputs_out[target, :] = piece[:, :D]
+            label_out[target, :] = piece[:, D:]
+            for block in range(0, size, NORM_ROWS):
+                values = piece[block : block + NORM_ROWS, :D].astype(jnp.float32)
+                target = pl.ds(pl.multiple_of(done + block, NORM_ROWS), NORM_ROWS)
+                normed[target, :] = norm_rows(values, gain[...]).astype(jnp.bfloat16)
+            done += size
+    labels = label_out[at, :].astype(jnp.float32)
     columns = lax.dot_general(
-        normed, weight[...], (((1,), (1,)), ((), ())), preferred_element_type=jnp.float32
+        normed[...], weight[...], (((1,), (1,)), ((), ())), preferred_element_type=jnp.float32
     )
     lane = lax.broadcasted_iota(jnp.int32, labels.shape, 1)
     numbers = lane.astype(jnp.float32)
@@ -280,6 +289,7 @@
         in_specs=[pl.BlockSpec(memory_space=pltpu.SMEM)]
         + [vmem] * (len(operands) + len(earlier)),
         out_specs=[vmem] * len(widths),
+        scratch_shapes=[pltpu.VMEM((rows, D), jnp.bfloat16)],
         out_shape=[pltpu.VMEM((total, width), jnp.bfloat16) for width in widths],
         input_output_aliases={1 + len(operands) + i: i for i in range(len(earlier))},
         compiler_params=pltpu.CompilerParams(vmem_limit_bytes=14 << 20),
@@ -304,7 +314,7 @@
 
 def attention_kernel(start, first_owner, images, info, labels, block, *refs):
     out, *rest = refs
-    scores, high = rest[-2:]
+    high, sums = rest[-2:]
     rows = high.shape[1]
     total = block.shape[0]
     segments = segment_row(labels[...])
@@ -313,40 +323,36 @@
     one_row = segments[:1]
     begin = jnp.sum(jnp.where(one_row < lowest, 1, 0)) // BLOCK
     end = (jnp.sum(jnp.where(one_row <= largest, 1, 0)) + BLOCK - 1) // BLOCK
-    queries = block[start : start + rows, : 2 * LANES]
     high[...] = jnp.full_like(high, 2 * FAR_APART)
-
-    def score(step, carry):
+    sums[...] = jnp.zeros_like(sums)
+
+    def attend(step, carry):
         at = pl.ds(pl.multiple_of(step * BLOCK, BLOCK), BLOCK)
-        for head in range(2):
-            keys = block[at, (2 + 2 * head) * LANES : (4 + 2 * head) * LANES]
-            values = lax.dot_general(
-                queries, keys, (((1,), (1,)), ((), ())), preferred_element_type=jnp.float32
-            )
-            scores[head, step] = values
-            high[head] = jnp.maximum(
-                high[head], jnp.maximum(values[:, :LANES], values[:, LANES:])
-            )
+        for part in range(rows // ROW_BLOCK):
+            for head in range(2):
+                rows_here = slice(part * ROW_BLOCK, (part + 1) * ROW_BLOCK)
+                queries = block[
+                    start + part * ROW_BLOCK : start + (part + 1) * ROW_BLOCK, : 2 * LANES
+                ]
+                keys = block[at, (2 + 2 * head) * LANES : (4 + 2 * head) * LANES]
+                scores = lax.dot_general(
+                    queries, keys, (((1,), (1,)), ((), ())), preferred_element_type=jnp.float32
+                )
+                low, up = scores[:, :LANES], scores[:, LANES:]
+                before = high[head, rows_here, :]
+                top = jnp.max(jnp.maximum(low, up), axis=-1, keepdims=True)
+                now = jnp.maximum(before, top)
+                weights = jnp.concatenate([jnp.exp2(low - now), jnp.exp2(up - now)], axis=1)
+                values = block[at, (6 + head) * LANES : (7 + head) * LANES]
+                term = jnp.dot(
+                    weights.astype(jnp.bfloat16), values, preferred_element_type=jnp.float32
+                )
+                sums[head, rows_here, :] = sums[head, rows_here, :] * jnp.exp2(before - now) + term
+                high[head, rows_here, :] = now
         return carry
 
-    lax.fori_loop(begin, end, score, 0)
-    highest = [jnp.max(high[head], axis=-1, keepdims=True) for head in range(2)]
-
-    def weigh(step, carry):
-        at = pl.ds(pl.multiple_of(step * BLOCK, BLOCK), BLOCK)
-        sums = []
-        for head in range(2):
-            weights = jnp.exp2(scores[head, step] - highest[head])
-            values = block[at, (6 + head) * LANES : (7 + head) * LANES]
-            sums.append(
-                carry[head]
-                + jnp.dot(weights.astype(jnp.bfloat16), values, preferred_element_type=jnp.float32)
-            )
-        return tuple(sums)
-
-    zero = jnp.zeros((rows, LANES), jnp.float32)
-    sums = lax.fori_loop(begin, end, weigh, (zero, zero))
-    first, second = (one / one[:, HD : HD + 1] for one in sums)
+    lax.fori_loop(begin, end, attend, 0)
+    first, second = (sums[head] / sums[head, :, HD : HD + 1] for head in range(2))
     lane = lax.broadcasted_iota(jnp.int32, first.shape, 1)
     turned = pltpu.roll(second, HD, 1)
     out[:rows] = jnp.where(lane < HD, first, turned).astype(jnp.bfloat16)
@@ -385,10 +391,10 @@
         out_specs=[vmem] * len(shapes),
         out_shape=shapes,
         scratch_shapes=[
-            pltpu.VMEM((2, total // BLOCK, rows, BLOCK), jnp.float32),
+            pltpu.VMEM((2, rows, LANES), jnp.float32),
             pltpu.VMEM((2, rows, LANES), jnp.float32),
         ],
-        compiler_params=pltpu.CompilerParams(vmem_limit_bytes=20 << 20),
+        compiler_params=pltpu.CompilerParams(vmem_limit_bytes=12 << 20),
         cost_estimate=pl.CostEstimate(
             flops=10 * rows * total * 2 * LANES,
             bytes_accessed=2 * block.size,
@@ -459,7 +465,7 @@
 def merge_kernel(start, counts, packs, last, *refs):
     inputs, weight, gain, merge_weight, bias = refs[:5]
     pieces = refs[5 : 5 + sum(counts)]
-    *refs, state = refs[5 + sum(counts) :]
+    *refs, state, tokens = refs[5 + sum(counts) :]
     rows = state.shape[1]
     half = rows // 2
     rest = 2 * HD - LANES
@@ -483,26 +489,23 @@
         mixed = jnp.dot(
             jnp.concatenate(lined, axis=1), weight[...], preferred_element_type=jnp.float32
         )
-        before = inputs[start + part * half : start + (part + 1) * half, :].astype(jnp.float32)
-        normed = norm_rows(before + mixed, gain[...])
         for column in range(D // LANES):
-            state[column, token, :] = normed[:, column * LANES : (column + 1) * LANES]
+            lanes = slice(column * LANES, (column + 1) * LANES)
+            before = inputs[start + part * half : start + (part + 1) * half, lanes]
+            state[column, token, :] = before.astype(jnp.float32) + mixed[:, lanes]
     groups = rows // 4
-    total = bias[...]
-    for quadrant in range(4):
-        tokens = jnp.concatenate(
-            [
-                state[column, pl.ds(quadrant, groups, stride=4), :].astype(jnp.bfloat16)
-                for column in range(D // LANES)
-            ],
-            axis=1,
-        )
-        total = total + lax.dot_general(
-            tokens,
-            merge_weight[:, quadrant * D : (quadrant + 1) * D],
-            (((1,), (1,)), ((), ())),
-            preferred_element_type=jnp.float32,
-        )
+    for block in range(0, groups, NORM_ROWS):
+        for quadrant in range(4):
+            at = pl.ds(4 * block + quadrant, NORM_ROWS, stride=4)
+            residual = jnp.concatenate(
+                [state[column, at, :] for column in range(D // LANES)], axis=1
+            )
+            tokens[block : block + NORM_ROWS, quadrant * D : (quadrant + 1) * D] = norm_rows(
+                residual, gain[...]
+            ).astype(jnp.bfloat16)
+    total = bias[...] + lax.dot_general(
+        tokens[...], merge_weight[...], (((1,), (1,)), ((), ())), preferred_element_type=jnp.float32
+    )
     total = total.astype(jnp.bfloat16)
     if not last:
         refs[0][...] = total
@@ -552,7 +555,10 @@
         ),
         in_specs=specs,
         out_specs=[vmem] * len(shapes),
-        scratch_shapes=[pltpu.VMEM((D // LANES, rows, LANES), jnp.float32)],
+        scratch_shapes=[
+            pltpu.VMEM((D // LANES, rows, LANES), jnp.float32),
+            pltpu.VMEM((groups, 4 * D), jnp.bfloat16),
+        ],
         out_shape=shapes,
         compiler_params=pltpu.CompilerParams(vmem_limit_bytes=20 << 20),
         cost_estimate=pl.CostEstimate(

time: 102 us -> 124 us (1.22)
  Pallas kernels: 41.8 us -> 55.4 us
  starting transfers between devices: 25.1 us -> 35.4 us
  waiting for transfers between devices: 31.8 us -> 29.6 us
    pallas_call x2, Pallas kernels: 8.82 us -> 22.2 us  [attention_call(): pl.pallas_call(functools.partial(attention_kernel, start, first_owner, in...]
    ppermute x3, starting transfers between devices: 6.65 us -> 17.1 us  [fast_local(): lax.ppermute(made[flip], 'pack', [(z, z ^ flip) for z in range(packs)])]
    ppermute x27, waiting for transfers between devices: 19.5 us -> 17 us  [send_seq(): return lax.ppermute(value, 'seq', [(i, i ^ flip) for i in range(size)])]
  transfers between devices with their start and end apart: 30 -> 30, of which waited for: 15 -> 12; matrix products, arithmetic and copies ran while one was open for 1% -> 1% of each run, Pallas kernels for 24% -> 25%
where the time goes in v9:
time: 124 us; the launch traced here: 123 us
  Pallas kernels  55.4 us (45%)
  starting transfers between devices  35.4 us (29%)
  waiting for transfers between devices  29.6 us (24%)
  local copies, waits for them, and re-layouts  2.79 us (2%)
    pallas_call x2, Pallas kernels, attention_call(): pl.pallas_call(functools.partial(attention_kernel, start, first_owner, in...  22.2 us
    ppermute x27, starting transfers between devices, send_seq(): return lax.ppermute(value, 'seq', [(i, i ^ flip) for i in range(size)])  18.3 us
    ppermute x3, starting transfers between devices, fast_local(): lax.ppermute(made[flip], 'pack', [(z, z ^ flip) for z in range(packs)])  17.1 us
    ppermute x27, waiting for transfers between devices, send_seq(): return lax.ppermute(value, 'seq', [(i, i ^ flip) for i in range(size)])  17 us
    pallas_call x2, Pallas kernels, merge_call(): pl.pallas_call(functools.partial(merge_kernel, start, [len(source) for so...  14.3 us
    ppermute x3, waiting for transfers between devices, fast_local(): lax.ppermute(made[flip], 'pack', [(z, z ^ flip) for z in range(packs)])  12.5 us
    pallas_call x4, Pallas kernels, qkv_call(): pl.pallas_call(functools.partial(qkv_kernel, len(first), flip), in_specs=...  10.6 us
    pallas_call x1, Pallas kernels, prepare_call(): pl.pallas_call(functools.partial(prepare_kernel, shards), in_specs=[pl.Bl...  5.1 us
  transfers between devices with their start and end apart: 30, of which 12 were waited for; matrix products, arithmetic and copies ran while one was open for 1% of the time, Pallas kernels for 25%

profile of v9, /device:TPU:0, one launch (start us, length us, event | category | flops | bytes accessed | tf_op | source)
XLA Modules:
  0.0 123.4 jit_solution(18076135700382124798)
XLA Ops:
  0.0 1.5 %payload.1.refs_0_ = bf16[192,1536]{1,0:T(8,128)(2,1)S(1)} custom-call(s32[1,192]{1,0:T(1,128)} %segments.1, s32[1,192]{1,0:T(1,128)} %rows.1, s32[1,192]{1,0:T(1,128)} %columns.1, s32[1,192]{1,0:T(1,128)} %mask.1, bf16[1408]{0:T(1024)(128)(2,1)} %embed.1, bf16[1,192,1408]{2,1,0:T(8,128)(2,1)} %patches.1), custom_call_target="tpu_custom_call" | custom-call | flops 270336 | bytes 1081344 | tf_op jit(solution)/shard_map/payload/pallas_call | solution.py:205
  2.0 2.6 %collective-permute-start = (bf16[192,1536]{1,0:T(8,128)(2,1)S(1)}, bf16[192,1536]{1,0:T(8,128)(2,1)S(1)}, u32[]{:S(2)}, u32[]{:S(2)}) collective-permute-start(bf16[192,1536]{1,0:T(8,128)(2,1)S(1)} %payload.1.refs_0_), channel_id=1, source_target_pairs={{0,8},{4,12},{8,0},{12,4},{16,24},{20,28},{24,16},{28,20},{1,9},{5... | collective-permute-start | bytes 1769480 | tf_op jit(solution)/shard_map/ppermute | solution.py:608
  4.6 1.5 %collective-permute-start.1 = (bf16[192,1536]{1,0:T(8,128)(2,1)S(1)}, bf16[192,1536]{1,0:T(8,128)(2,1)S(1)}, u32[]{:S(2)}, u32[]{:S(2)}) collective-permute-start(bf16[192,1536]{1,0:T(8,128)(2,1)S(1)} %payload.1.refs_0_), channel_id=1, source_target_pairs={{0,16},{4,20},{8,24},{12,28},{16,0},{20,4},{24,8},{28,12},{1,17},{... | collective-permute-start | bytes 1769480 | tf_op jit(solution)/shard_map/ppermute | solution.py:608
  6.1 0.7 concatenate.3.info.refs_15_
  6.8 0.7 copy-done.1
  7.5 0.7 copy-done.2
  8.9 5.1 %prepare.1 = (f32[1,1408]{1,0:T(1,128)S(1)}, f32[1,1408]{1,0:T(1,128)S(1)}, f32[1,448]{1,0:T(1,128)S(1)}, bf16[1536,1408]{1,0:T(8,128)(2,1)S(1)}, bf16[448,5632]...) custom-call(s32[15]{0:T(128)S(1)} %concatenate.3.info.refs_15_, bf16[1408,1408]{1,0:T(8,128)(2,1)} %out_weight.1, ...), custom_call_target="tpu_custom_call" | custom-call | flops 1141899264 | bytes 20996096 | tf_op jit(solution)/shard_map/prepare/pallas_call | solution.py:442
  14.0 2.6 %norm_qkv.4 = (bf16[1536,1408]{1,0:T(8,128)(2,1)S(1)}, bf16[1536,1024]{1,0:T(8,128)(2,1)S(1)}, bf16[1536,128]{1,0:T(8,128)(2,1)S(1)}) custom-call(s32[15]{0:T(128)S(1)} %concatenate.3.info.refs_15_, bf16[192,1536]{1,0:T(8,128)(2,1)S(1)} %payload.1.refs_0_, bf16[192,1536]{1,0:T(8,128)(2,1)S(1)} %collective-permute-done.2.refs_1_, ...), custom_call_target="tpu_custom_call" | custom-call | flops 2491416576 | bytes 6488064 | tf_op jit(solution)/shard_map/norm_qkv/pallas_call | solution.py:287
  16.7 1.8 %collective-permute-done.across_x.refs_0_ = bf16[192,1536]{1,0:T(8,128)(2,1)S(1)} collective-permute-done((bf16[192,1536]{1,0:T(8,128)(2,1)S(1)}, bf16[192,1536]{1,0:T(8,128)(2,1)S(1)}, u32[]{:S(2)}, u32[]{:S(2)}) %collective-permute-start) | collective-permute-done | bytes 589856 | tf_op jit(solution)/shard_map/ppermute | solution.py:608
  18.5 1.5 %collective-permute-done.1.across_y.refs_0_ = bf16[192,1536]{1,0:T(8,128)(2,1)S(1)} collective-permute-done((bf16[192,1536]{1,0:T(8,128)(2,1)S(1)}, bf16[192,1536]{1,0:T(8,128)(2,1)S(1)}, u32[]{:S(2)}, u32[]{:S(2)}) %collective-permute-start.1) | collective-permute-done | bytes 589856 | tf_op jit(solution)/shard_map/ppermute | solution.py:608
  20.5 1.6 %collective-permute-start.3 = (bf16[96,1536]{1,0:T(8,128)(2,1)S(1)}, bf16[96,1536]{1,0:T(8,128)(2,1)S(1)}, u32[]{:S(2)}, u32[]{:S(2)}) collective-permute-start(bf16[96,1536]{1,0:T(8,128)(2,1)S(1)} %get-tuple-element.52), channel_id=1, source_target_pairs={{0,16},{4,20},{8,24},{12,28},{16,0},{20,4},{24,8},{28,12},{1,17},{... | collective-permute-start | bytes 884744 | tf_op jit(solution)/shard_map/ppermute | solution.py:608
  22.6 2.6 %norm_qkv.5 = (bf16[1536,1408]{1,0:T(8,128)(2,1)S(1)}, bf16[1536,1024]{1,0:T(8,128)(2,1)S(1)}, bf16[1536,128]{1,0:T(8,128)(2,1)S(1)}) custom-call(s32[15]{0:T(128)S(1)} %concatenate.3.info.refs_15_, bf16[192,1536]{1,0:T(8,128)(2,1)S(1)} %collective-permute-done.across_x.refs_0_, ...), custom_call_target="tpu_custom_call", output_to_operand_aliasing={{0}: (6, {}), {1}: (7, {}), {2}: (8, {})} | custom-call | flops 2491416576 | bytes 6488064 | tf_op jit(solution)/shard_map/norm_qkv/pallas_call | solution.py:287
  25.3 2.6 %norm_qkv.6 = (bf16[1536,1408]{1,0:T(8,128)(2,1)S(1)}, bf16[1536,1024]{1,0:T(8,128)(2,1)S(1)}, bf16[1536,128]{1,0:T(8,128)(2,1)S(1)}) custom-call(s32[15]{0:T(128)S(1)} %concatenate.3.info.refs_15_, bf16[192,1536]{1,0:T(8,128)(2,1)S(1)} %collective-permute-done.1.across_y.refs_0_, ...), custom_call_target="tpu_custom_call", output_to_operand_aliasing={{0}: (6, {}), {1}: (7, {}), {2}: (8, {})} | custom-call | flops 2491416576 | bytes 6488064 | tf_op jit(solution)/shard_map/norm_qkv/pallas_call | solution.py:287
  27.9 1.6 %collective-permute-done.3.refs_0_ = bf16[96,1536]{1,0:T(8,128)(2,1)S(1)} collective-permute-done((bf16[96,1536]{1,0:T(8,128)(2,1)S(1)}, bf16[96,1536]{1,0:T(8,128)(2,1)S(1)}, u32[]{:S(2)}, u32[]{:S(2)}) %collective-permute-start.3) | collective-permute-done | bytes 294944 | tf_op jit(solution)/shard_map/ppermute | solution.py:608
  29.5 1.2 %collective-permute-done.4.refs_1_ = bf16[96,1536]{1,0:T(8,128)(2,1)S(1)} collective-permute-done((bf16[96,1536]{1,0:T(8,128)(2,1)S(1)}, bf16[96,1536]{1,0:T(8,128)(2,1)S(1)}, u32[]{:S(2)}, u32[]{:S(2)}) %collective-permute-start.4) | collective-permute-done | bytes 294944 | tf_op jit(solution)/shard_map/ppermute | solution.py:608
  31.2 1.1 collective-permute-done.7.refs_2_
  32.7 2.7 %norm_qkv.7 = (bf16[1536,1408]{1,0:T(8,128)(2,1)S(1)}, bf16[1536,1024]{1,0:T(8,128)(2,1)S(1)}, bf16[1536,128]{1,0:T(8,128)(2,1)S(1)}) custom-call(s32[15]{0:T(128)S(1)} %concatenate.3.info.refs_15_, bf16[96,1536]{1,0:T(8,128)(2,1)S(1)} %collective-permute-done.3.refs_0_, ...), custom_call_target="tpu_custom_call", output_to_operand_aliasing={{0}: (8, {}), {1}: (9, {}), {2}: (10, {})} | custom-call | flops 2491416576 | bytes 6488064 | tf_op jit(solution)/shard_map/norm_qkv/pallas_call | solution.py:287
  35.4 11.2 %attention.3 = (bf16[1152,128]{1,0:T(8,128)(2,1)S(1)}, bf16[16,128]{1,0:T(8,128)(2,1)S(1)}) custom-call(s32[15]{0:T(128)S(1)} %concatenate.3.info.refs_15_, bf16[1536,128]{1,0:T(8,128)(2,1)S(1)} %get-tuple-element.68.labels, bf16[1536,1024]{1,0:T(8,128)(2,1)S(1)} %get-tuple-element.69.block), custom_call_target="tpu_custom_call" | custom-call | flops 3019898880 | bytes 3145728 | tf_op jit(solution)/shard_map/attention/pallas_call | solution.py:388
  47.6 11.0 %attention.2.refs_5_ = bf16[1152,128]{1,0:T(8,128)(2,1)S(1)} custom-call(s32[15]{0:T(128)S(1)} %concatenate.3.info.refs_15_, bf16[1536,128]{1,0:T(8,128)(2,1)S(1)} %get-tuple-element.68.labels, bf16[1536,1024]{1,0:T(8,128)(2,1)S(1)} %get-tuple-element.69.block), custom_call_target="tpu_custom_call" | custom-call | flops 3019898880 | bytes 3145728 | tf_op jit(solution)/shard_map/attention/pallas_call | solution.py:388
  58.7 1.7 %collective-permute-start.15 = (bf16[576,128]{1,0:T(8,128)(2,1)S(1)}, bf16[576,128]{1,0:T(8,128)(2,1)S(1)}, u32[]{:S(2)}, u32[]{:S(2)}) collective-permute-start(bf16[576,128]{1,0:T(8,128)(2,1)S(1)} %get-tuple-element.74), channel_id=1, source_target_pairs={{0,16},{4,20},{8,24},{12,28},{16,0},{20,4},{24,8},{28,12},{1,17},{... | collective-permute-start | bytes 442376 | tf_op jit(solution)/shard_map/ppermute | solution.py:608
  60.4 1.5 %collective-permute-start.13 = (bf16[1152,128]{1,0:T(8,128)(2,1)S(1)}, bf16[1152,128]{1,0:T(8,128)(2,1)S(1)}, u32[]{:S(2)}, u32[]{:S(2)}) collective-permute-start(bf16[1152,128]{1,0:T(8,128)(2,1)S(1)} %attention.2.refs_5_), channel_id=1, source_target_pairs={{0,8},{4,12},{8,0},{12,4},{16,24},{20,28},{24,16},{28,20},{1,9},{5... | collective-permute-start | bytes 884744 | tf_op jit(solution)/shard_map/ppermute | solution.py:608
  62.9 2.5 %collective-permute-done.15.refs_11_ = bf16[576,128]{1,0:T(8,128)(2,1)S(1)} collective-permute-done((bf16[576,128]{1,0:T(8,128)(2,1)S(1)}, bf16[576,128]{1,0:T(8,128)(2,1)S(1)}, u32[]{:S(2)}, u32[]{:S(2)}) %collective-permute-start.15) | collective-permute-done | bytes 147488 | tf_op jit(solution)/shard_map/ppermute | solution.py:608
  65.4 1.6 %collective-permute-start.16 = (bf16[576,128]{1,0:T(8,128)(2,1)S(1)}, bf16[576,128]{1,0:T(8,128)(2,1)S(1)}, u32[]{:S(2)}, u32[]{:S(2)}) collective-permute-start(bf16[576,128]{1,0:T(8,128)(2,1)S(1)} %get-tuple-element.75), channel_id=1, source_target_pairs={{0,8},{4,12},{8,0},{12,4},{16,24},{20,28},{24,16},{28,20},{1,9},{5... | collective-permute-start | bytes 442376 | tf_op jit(solution)/shard_map/ppermute | solution.py:608
  67.0 5.7 %collective-permute-done.16.refs_12_ = bf16[576,128]{1,0:T(8,128)(2,1)S(1)} collective-permute-done((bf16[576,128]{1,0:T(8,128)(2,1)S(1)}, bf16[576,128]{1,0:T(8,128)(2,1)S(1)}, u32[]{:S(2)}, u32[]{:S(2)}) %collective-permute-start.16) | collective-permute-done | bytes 147488 | tf_op jit(solution)/shard_map/ppermute | solution.py:608
  74.5 1.6 %collective-permute-start.20 = (bf16[576,128]{1,0:T(8,128)(2,1)S(1)}, bf16[576,128]{1,0:T(8,128)(2,1)S(1)}, u32[]{:S(2)}, u32[]{:S(2)}) collective-permute-start(bf16[576,128]{1,0:T(8,128)(2,1)S(1)} %get-tuple-element.79), channel_id=1, source_target_pairs={{0,8},{4,12},{8,0},{12,4},{16,24},{20,28},{24,16},{28,20},{1,9},{5... | collective-permute-start | bytes 442376 | tf_op jit(solution)/shard_map/ppermute | solution.py:608
  76.1 6.6 %out_merge.2.refs_17_ = bf16[192,448]{1,0:T(8,128)(2,1)S(1)} custom-call(bf16[1536,1408]{1,0:T(8,128)(2,1)S(1)} %get-tuple-element.64.refs_0_, bf16[1536,1408]{1,0:T(8,128)(2,1)S(1)} %get-tuple-element.49.refs_1_, f32[1,1408]{1,0:T(1,128)S(1)} %get-tuple-element.65.refs_2_, bf16[448,5632]{1,0:T(8,128)(2,1)S(1)} %get-tuple-element.66.refs_3_, ...), custom_call_target="tpu_custom_call" | custom-call | flops 7059013632 | bytes 15499264 | tf_op jit(solution)/shard_map/out_merge/pallas_call | solution.py:552
  83.3 0.8 collective-permute-done.25.refs_13_
  84.4 7.7 %out_merge.3 = (bf16[672,128]{1,0:T(8,128)(2,1)S(1)}, bf16[672,128]{1,0:T(8,128)(2,1)S(1)}, bf16[672,128]{1,0:T(8,128)(2,1)S(1)}, bf16[672,128]{1,0:T(8,128)(2,1)S(1)}) custom-call(bf16[1536,1408]{1,0:T(8,128)(2,1)S(1)} %get-tuple-element.64.refs_0_, bf16[1536,1408]{1,0:T(8,128)(2,1)S(1)} %get-tuple-element.49.refs_1_, ...), custom_call_target="tpu_custom_call" | custom-call | flops 7059013632 | bytes 15499264 | tf_op jit(solution)/shard_map/out_merge/pallas_call | solution.py:552
  92.1 1.7 %collective-permute-start.27 = (bf16[672,128]{1,0:T(8,128)(2,1)S(1)}, bf16[672,128]{1,0:T(8,128)(2,1)S(1)}, u32[]{:S(2)}, u32[]{:S(2)}) collective-permute-start(bf16[672,128]{1,0:T(8,128)(2,1)S(1)} %get-tuple-element.84), channel_id=1, source_target_pairs={{0,1},{1,0},{2,3},{3,2},{4,5},{5,4},{6,7},{7,6},{8,9},{9,8},{10,11... | collective-permute-start | bytes 516104 | tf_op jit(solution)/shard_map/ppermute | solution.py:766
  93.7 15.5 %collective-permute-start.28 = (bf16[672,128]{1,0:T(8,128)(2,1)S(1)}, bf16[672,128]{1,0:T(8,128)(2,1)S(1)}, u32[]{:S(2)}, u32[]{:S(2)}) collective-permute-start(bf16[672,128]{1,0:T(8,128)(2,1)S(1)} %get-tuple-element.85), channel_id=1, source_target_pairs={{0,2},{1,3},{2,0},{3,1},{4,6},{5,7},{6,4},{7,5},{8,10},{9,11},{10,... | collective-permute-start | bytes 516104 | tf_op jit(solution)/shard_map/ppermute | solution.py:766
  109.2 12.5 %collective-permute-done.28.refs_2_ = bf16[672,128]{1,0:T(8,128)(2,1)S(1)} collective-permute-done((bf16[672,128]{1,0:T(8,128)(2,1)S(1)}, bf16[672,128]{1,0:T(8,128)(2,1)S(1)}, u32[]{:S(2)}, u32[]{:S(2)}) %collective-permute-start.28) | collective-permute-done | bytes 172064 | tf_op jit(solution)/shard_map/ppermute | solution.py:766
  121.8 1.6 %place_rows.1 = bf16[4,192,448]{2,1,0:T(8,128)(2,1)} custom-call(s32[15]{0:T(128)S(1)} %concatenate.3.info.refs_15_, bf16[672,128]{1,0:T(8,128)(2,1)S(1)} %get-tuple-element.83.refs_0_, bf16[672,128]{1,0:T(8,128)(2,1)S(1)} %collective-permute-done.27.refs_1_, bf16[672,128]{1,0:T(8,128)(2,1)S(1)} %collective-permute-done.28.refs_2_, ...), custom_call_target="tpu_custom_call" | custom-call | bytes 1376256 | tf_op jit(solution)/shard_map/place_rows/pallas_call | solution.py:592
  (51 shorter events, 7.8 us)
Async XLA Ops:
  1.5 12.5 %collective-permute-start.2 = (bf16[192,1536]{1,0:T(8,128)(2,1)S(1)}, bf16[192,1536]{1,0:T(8,128)(2,1)S(1)}, u32[]{:S(2)}, u32[]{:S(2)}) collective-permute-start(bf16[192,1536]{1,0:T(8,128)(2,1)S(1)} %payload.1.refs_0_), channel_id=1, source_target_pairs={{0,4},{4,0},{8,12},{12,8},{16,20},{20,16},{24,28},{28,24},{1,5},{5... | collective-permute-start | bytes 1769480 | tf_op jit(solution)/shard_map/ppermute | solution.py:608
  2.0 16.5 %collective-permute-start = (bf16[192,1536]{1,0:T(8,128)(2,1)S(1)}, bf16[192,1536]{1,0:T(8,128)(2,1)S(1)}, u32[]{:S(2)}, u32[]{:S(2)}) collective-permute-start(bf16[192,1536]{1,0:T(8,128)(2,1)S(1)} %payload.1.refs_0_), channel_id=1, source_target_pairs={{0,8},{4,12},{8,0},{12,4},{16,24},{20,28},{24,16},{28,20},{1,9},{5... | collective-permute-start | bytes 1769480 | tf_op jit(solution)/shard_map/ppermute | solution.py:608
  4.6 15.4 %collective-permute-start.1 = (bf16[192,1536]{1,0:T(8,128)(2,1)S(1)}, bf16[192,1536]{1,0:T(8,128)(2,1)S(1)}, u32[]{:S(2)}, u32[]{:S(2)}) collective-permute-start(bf16[192,1536]{1,0:T(8,128)(2,1)S(1)} %payload.1.refs_0_), channel_id=1, source_target_pairs={{0,16},{4,20},{8,24},{12,28},{16,0},{20,4},{24,8},{28,12},{1,17},{... | collective-permute-start | bytes 1769480 | tf_op jit(solution)/shard_map/ppermute | solution.py:608
  6.8 0.7 copy-start.1
  8.9 5.1 %copy-start = (bf16[128,512]{1,0:T(8,128)(2,1)S(1)}, bf16[128,512]{1,0:T(8,128)(2,1)}, u32[]{:S(2)}) copy-start(bf16[128,512]{1,0:T(8,128)(2,1)} %constant.48.clone.refs_2_.refs_4_) | copy-start | bytes 393220
  20.0 2.7 %collective-permute-start.6 = (bf16[192,1536]{1,0:T(8,128)(2,1)S(1)}, bf16[192,1536]{1,0:T(8,128)(2,1)S(1)}, u32[]{:S(2)}, u32[]{:S(2)}) collective-permute-start(bf16[192,1536]{1,0:T(8,128)(2,1)S(1)} %collective-permute-done.across_x.refs_0_), channel_id=1, source_target_pairs={{0,4},{4,0},{8,12},{12,8},{16,20},{20,16},{24,28},{28,24},{1,5},{5... | collective-permute-start | bytes 1769480 | tf_op jit(solution)/shard_map/ppermute | solution.py:608
  20.0 5.3 %collective-permute-start.5 = (bf16[192,1536]{1,0:T(8,128)(2,1)S(1)}, bf16[192,1536]{1,0:T(8,128)(2,1)S(1)}, u32[]{:S(2)}, u32[]{:S(2)}) collective-permute-start(bf16[192,1536]{1,0:T(8,128)(2,1)S(1)} %collective-permute-done.1.across_y.refs_0_), channel_id=1, source_target_pairs={{0,4},{4,0},{8,12},{12,8},{16,20},{20,16},{24,28},{28,24},{1,5},{5... | collective-permute-start | bytes 1769480 | tf_op jit(solution)/shard_map/ppermute | solution.py:608
  20.5 9.0 %collective-permute-start.3 = (bf16[96,1536]{1,0:T(8,128)(2,1)S(1)}, bf16[96,1536]{1,0:T(8,128)(2,1)S(1)}, u32[]{:S(2)}, u32[]{:S(2)}) collective-permute-start(bf16[96,1536]{1,0:T(8,128)(2,1)S(1)} %get-tuple-element.52), channel_id=1, source_target_pairs={{0,16},{4,20},{8,24},{12,28},{16,0},{20,4},{24,8},{28,12},{1,17},{... | collective-permute-start | bytes 884744 | tf_op jit(solution)/shard_map/ppermute | solution.py:608
  22.1 8.6 %collective-permute-start.4 = (bf16[96,1536]{1,0:T(8,128)(2,1)S(1)}, bf16[96,1536]{1,0:T(8,128)(2,1)S(1)}, u32[]{:S(2)}, u32[]{:S(2)}) collective-permute-start(bf16[96,1536]{1,0:T(8,128)(2,1)S(1)} %get-tuple-element.53), channel_id=1, source_target_pairs={{0,8},{4,12},{8,0},{12,4},{16,24},{20,28},{24,16},{28,20},{1,9},{5... | collective-permute-start | bytes 884744 | tf_op jit(solution)/shard_map/ppermute | solution.py:608
  30.7 1.6 %collective-permute-start.7 = (bf16[96,1536]{1,0:T(8,128)(2,1)S(1)}, bf16[96,1536]{1,0:T(8,128)(2,1)S(1)}, u32[]{:S(2)}, u32[]{:S(2)}) collective-permute-start(bf16[96,1536]{1,0:T(8,128)(2,1)S(1)} %collective-permute-done.3.refs_0_), channel_id=1, source_target_pairs={{0,4},{4,0},{8,12},{12,8},{16,20},{20,16},{24,28},{28,24},{1,5},{5... | collective-permute-start | bytes 884744 | tf_op jit(solution)/shard_map/ppermute | solution.py:608
  30.7 2.0 %collective-permute-start.8 = (bf16[96,1536]{1,0:T(8,128)(2,1)S(1)}, bf16[96,1536]{1,0:T(8,128)(2,1)S(1)}, u32[]{:S(2)}, u32[]{:S(2)}) collective-permute-start(bf16[96,1536]{1,0:T(8,128)(2,1)S(1)} %collective-permute-done.4.refs_1_), channel_id=1, source_target_pairs={{0,4},{4,0},{8,12},{12,8},{16,20},{20,16},{24,28},{28,24},{1,5},{5... | collective-permute-start | bytes 884744 | tf_op jit(solution)/shard_map/ppermute | solution.py:608
  46.6 12.0 %collective-permute-start.10 = (bf16[1152,128]{1,0:T(8,128)(2,1)S(1)}, bf16[1152,128]{1,0:T(8,128)(2,1)S(1)}, u32[]{:S(2)}, u32[]{:S(2)}) collective-permute-start(bf16[1152,128]{1,0:T(8,128)(2,1)S(1)} %get-tuple-element.70.refs_5_), channel_id=1, source_target_pairs={{0,8},{4,12},{8,0},{12,4},{16,24},{20,28},{24,16},{28,20},{1,9},{5... | collective-permute-start | bytes 884744 | tf_op jit(solution)/shard_map/ppermute | solution.py:608
  47.2 11.4 %collective-permute-start.11 = (bf16[1152,128]{1,0:T(8,128)(2,1)S(1)}, bf16[1152,128]{1,0:T(8,128)(2,1)S(1)}, u32[]{:S(2)}, u32[]{:S(2)}) collective-permute-start(bf16[1152,128]{1,0:T(8,128)(2,1)S(1)} %get-tuple-element.70.refs_5_), channel_id=1, source_target_pairs={{0,16},{4,20},{8,24},{12,28},{16,0},{20,4},{24,8},{28,12},{1,17},{... | collective-permute-start | bytes 884744 | tf_op jit(solution)/shard_map/ppermute | solution.py:608
  47.6 11.1 %collective-permute-start.9 = (bf16[1152,128]{1,0:T(8,128)(2,1)S(1)}, bf16[1152,128]{1,0:T(8,128)(2,1)S(1)}, u32[]{:S(2)}, u32[]{:S(2)}) collective-permute-start(bf16[1152,128]{1,0:T(8,128)(2,1)S(1)} %get-tuple-element.70.refs_5_), channel_id=1, source_target_pairs={{0,4},{4,0},{8,12},{12,8},{16,20},{20,16},{24,28},{28,24},{1,5},{5... | collective-permute-start | bytes 884744 | tf_op jit(solution)/shard_map/ppermute | solution.py:608
  58.7 6.7 %collective-permute-start.15 = (bf16[576,128]{1,0:T(8,128)(2,1)S(1)}, bf16[576,128]{1,0:T(8,128)(2,1)S(1)}, u32[]{:S(2)}, u32[]{:S(2)}) collective-permute-start(bf16[576,128]{1,0:T(8,128)(2,1)S(1)} %get-tuple-element.74), channel_id=1, source_target_pairs={{0,16},{4,20},{8,24},{12,28},{16,0},{20,4},{24,8},{28,12},{1,17},{... | collective-permute-start | bytes 442376 | tf_op jit(solution)/shard_map/ppermute | solution.py:608
  60.4 12.3 %collective-permute-start.13 = (bf16[1152,128]{1,0:T(8,128)(2,1)S(1)}, bf16[1152,128]{1,0:T(8,128)(2,1)S(1)}, u32[]{:S(2)}, u32[]{:S(2)}) collective-permute-start(bf16[1152,128]{1,0:T(8,128)(2,1)S(1)} %attention.2.refs_5_), channel_id=1, source_target_pairs={{0,8},{4,12},{8,0},{12,4},{16,24},{20,28},{24,16},{28,20},{1,9},{5... | collective-permute-start | bytes 884744 | tf_op jit(solution)/shard_map/ppermute | solution.py:608
  61.9 11.3 %collective-permute-start.14 = (bf16[1152,128]{1,0:T(8,128)(2,1)S(1)}, bf16[1152,128]{1,0:T(8,128)(2,1)S(1)}, u32[]{:S(2)}, u32[]{:S(2)}) collective-permute-start(bf16[1152,128]{1,0:T(8,128)(2,1)S(1)} %attention.2.refs_5_), channel_id=1, source_target_pairs={{0,16},{4,20},{8,24},{12,28},{16,0},{20,4},{24,8},{28,12},{1,17},{... | collective-permute-start | bytes 884744 | tf_op jit(solution)/shard_map/ppermute | solution.py:608
  62.4 10.9 %collective-permute-start.21 = (bf16[1152,128]{1,0:T(8,128)(2,1)S(1)}, bf16[1152,128]{1,0:T(8,128)(2,1)S(1)}, u32[]{:S(2)}, u32[]{:S(2)}) collective-permute-start(bf16[1152,128]{1,0:T(8,128)(2,1)S(1)} %collective-permute-done.10.across_x.refs_7_), channel_id=1, source_target_pairs={{0,4},{4,0},{8,12},{12,8},{16,20},{20,16},{24,28},{28,24},{1,5},{5... | collective-permute-start | bytes 884744 | tf_op jit(solution)/shard_map/ppermute | solution.py:608
  62.4 11.4 %collective-permute-start.22 = (bf16[1152,128]{1,0:T(8,128)(2,1)S(1)}, bf16[1152,128]{1,0:T(8,128)(2,1)S(1)}, u32[]{:S(2)}, u32[]{:S(2)}) collective-permute-start(bf16[1152,128]{1,0:T(8,128)(2,1)S(1)} %collective-permute-done.11.across_y.refs_9_), channel_id=1, source_target_pairs={{0,4},{4,0},{8,12},{12,8},{16,20},{20,16},{24,28},{28,24},{1,5},{5... | collective-permute-start | bytes 884744 | tf_op jit(solution)/shard_map/ppermute | solution.py:608
  65.4 7.3 %collective-permute-start.16 = (bf16[576,128]{1,0:T(8,128)(2,1)S(1)}, bf16[576,128]{1,0:T(8,128)(2,1)S(1)}, u32[]{:S(2)}, u32[]{:S(2)}) collective-permute-start(bf16[576,128]{1,0:T(8,128)(2,1)S(1)} %get-tuple-element.75), channel_id=1, source_target_pairs={{0,8},{4,12},{8,0},{12,4},{16,24},{20,28},{24,16},{28,20},{1,9},{5... | collective-permute-start | bytes 442376 | tf_op jit(solution)/shard_map/ppermute | solution.py:608
  72.7 1.4 %collective-permute-start.23 = (bf16[576,128]{1,0:T(8,128)(2,1)S(1)}, bf16[576,128]{1,0:T(8,128)(2,1)S(1)}, u32[]{:S(2)}, u32[]{:S(2)}) collective-permute-start(bf16[576,128]{1,0:T(8,128)(2,1)S(1)} %collective-permute-done.15.refs_11_), channel_id=1, source_target_pairs={{0,4},{4,0},{8,12},{12,8},{16,20},{20,16},{24,28},{28,24},{1,5},{5... | collective-permute-start | bytes 442376 | tf_op jit(solution)/shard_map/ppermute | solution.py:608
  72.7 1.7 %collective-permute-start.24 = (bf16[576,128]{1,0:T(8,128)(2,1)S(1)}, bf16[576,128]{1,0:T(8,128)(2,1)S(1)}, u32[]{:S(2)}, u32[]{:S(2)}) collective-permute-start(bf16[576,128]{1,0:T(8,128)(2,1)S(1)} %collective-permute-done.16.refs_12_), channel_id=1, source_target_pairs={{0,4},{4,0},{8,12},{12,8},{16,20},{20,16},{24,28},{28,24},{1,5},{5... | collective-permute-start | bytes 442376 | tf_op jit(solution)/shard_map/ppermute | solution.py:608
  73.2 10.1 %collective-permute-start.12 = (bf16[1152,128]{1,0:T(8,128)(2,1)S(1)}, bf16[1152,128]{1,0:T(8,128)(2,1)S(1)}, u32[]{:S(2)}, u32[]{:S(2)}) collective-permute-start(bf16[1152,128]{1,0:T(8,128)(2,1)S(1)} %attention.2.refs_5_), channel_id=1, source_target_pairs={{0,4},{4,0},{8,12},{12,8},{16,20},{20,16},{24,28},{28,24},{1,5},{5... | collective-permute-start | bytes 884744 | tf_op jit(solution)/shard_map/ppermute | solution.py:608
  73.4 10.0 %collective-permute-start.17 = (bf16[1152,128]{1,0:T(8,128)(2,1)S(1)}, bf16[1152,128]{1,0:T(8,128)(2,1)S(1)}, u32[]{:S(2)}, u32[]{:S(2)}) collective-permute-start(bf16[1152,128]{1,0:T(8,128)(2,1)S(1)} %collective-permute-done.13.across_x.refs_7_), channel_id=1, source_target_pairs={{0,4},{4,0},{8,12},{12,8},{16,20},{20,16},{24,28},{28,24},{1,5},{5... | collective-permute-start | bytes 884744 | tf_op jit(solution)/shard_map/ppermute | solution.py:608
  73.9 9.5 %collective-permute-start.18 = (bf16[1152,128]{1,0:T(8,128)(2,1)S(1)}, bf16[1152,128]{1,0:T(8,128)(2,1)S(1)}, u32[]{:S(2)}, u32[]{:S(2)}) collective-permute-start(bf16[1152,128]{1,0:T(8,128)(2,1)S(1)} %collective-permute-done.14.across_y.refs_9_), channel_id=1, source_target_pairs={{0,4},{4,0},{8,12},{12,8},{16,20},{20,16},{24,28},{28,24},{1,5},{5... | collective-permute-start | bytes 884744 | tf_op jit(solution)/shard_map/ppermute | solution.py:608
  74.1 8.6 %collective-permute-start.19 = (bf16[576,128]{1,0:T(8,128)(2,1)S(1)}, bf16[576,128]{1,0:T(8,128)(2,1)S(1)}, u32[]{:S(2)}, u32[]{:S(2)}) collective-permute-start(bf16[576,128]{1,0:T(8,128)(2,1)S(1)} %get-tuple-element.78), channel_id=1, source_target_pairs={{0,16},{4,20},{8,24},{12,28},{16,0},{20,4},{24,8},{28,12},{1,17},{... | collective-permute-start | bytes 442376 | tf_op jit(solution)/shard_map/ppermute | solution.py:608
  74.5 8.3 %collective-permute-start.20 = (bf16[576,128]{1,0:T(8,128)(2,1)S(1)}, bf16[576,128]{1,0:T(8,128)(2,1)S(1)}, u32[]{:S(2)}, u32[]{:S(2)}) collective-permute-start(bf16[576,128]{1,0:T(8,128)(2,1)S(1)} %get-tuple-element.79), channel_id=1, source_target_pairs={{0,8},{4,12},{8,0},{12,4},{16,24},{20,28},{24,16},{28,20},{1,9},{5... | collective-permute-start | bytes 442376 | tf_op jit(solution)/shard_map/ppermute | solution.py:608
  82.7 1.4 %collective-permute-start.25 = (bf16[576,128]{1,0:T(8,128)(2,1)S(1)}, bf16[576,128]{1,0:T(8,128)(2,1)S(1)}, u32[]{:S(2)}, u32[]{:S(2)}) collective-permute-start(bf16[576,128]{1,0:T(8,128)(2,1)S(1)} %collective-permute-done.19.refs_11_), channel_id=1, source_target_pairs={{0,4},{4,0},{8,12},{12,8},{16,20},{20,16},{24,28},{28,24},{1,5},{5... | collective-permute-start | bytes 442376 | tf_op jit(solution)/shard_map/ppermute | solution.py:608
  82.8 1.6 %collective-permute-start.26 = (bf16[576,128]{1,0:T(8,128)(2,1)S(1)}, bf16[576,128]{1,0:T(8,128)(2,1)S(1)}, u32[]{:S(2)}, u32[]{:S(2)}) collective-permute-start(bf16[576,128]{1,0:T(8,128)(2,1)S(1)} %collective-permute-done.20.refs_12_), channel_id=1, source_target_pairs={{0,4},{4,0},{8,12},{12,8},{16,20},{20,16},{24,28},{28,24},{1,5},{5... | collective-permute-start | bytes 442376 | tf_op jit(solution)/shard_map/ppermute | solution.py:608
  92.1 17.1 %collective-permute-start.27 = (bf16[672,128]{1,0:T(8,128)(2,1)S(1)}, bf16[672,128]{1,0:T(8,128)(2,1)S(1)}, u32[]{:S(2)}, u32[]{:S(2)}) collective-permute-start(bf16[672,128]{1,0:T(8,128)(2,1)S(1)} %get-tuple-element.84), channel_id=1, source_target_pairs={{0,1},{1,0},{2,3},{3,2},{4,5},{5,4},{6,7},{7,6},{8,9},{9,8},{10,11... | collective-permute-start | bytes 516104 | tf_op jit(solution)/shard_map/ppermute | solution.py:766
  93.7 28.0 %collective-permute-start.28 = (bf16[672,128]{1,0:T(8,128)(2,1)S(1)}, bf16[672,128]{1,0:T(8,128)(2,1)S(1)}, u32[]{:S(2)}, u32[]{:S(2)}) collective-permute-start(bf16[672,128]{1,0:T(8,128)(2,1)S(1)} %get-tuple-element.85), channel_id=1, source_target_pairs={{0,2},{1,3},{2,0},{3,1},{4,6},{5,7},{6,4},{7,5},{8,10},{9,11},{10,... | collective-permute-start | bytes 516104 | tf_op jit(solution)/shard_map/ppermute | solution.py:766
  109.2 12.6 %collective-permute-start.29 = (bf16[672,128]{1,0:T(8,128)(2,1)S(1)}, bf16[672,128]{1,0:T(8,128)(2,1)S(1)}, u32[]{:S(2)}, u32[]{:S(2)}) collective-permute-start(bf16[672,128]{1,0:T(8,128)(2,1)S(1)} %get-tuple-element.86), channel_id=1, source_target_pairs={{0,3},{1,2},{2,1},{3,0},{4,7},{5,6},{6,5},{7,4},{8,11},{9,10},{10,... | collective-permute-start | bytes 516104 | tf_op jit(solution)/shard_map/ppermute | solution.py:766
  (2 other events, 1.4 us)

commit v10 on v8

--- a/solution.py
+++ b/solution.py
@@ -152,6 +152,7 @@
 POSITIONS = 64
 FAR_APART = -(2.0**100)
 IMAGE_LANE = 96
+NORM_ROWS = 16
 CHUNKS = (768, 768)
 
 
@@ -459,7 +460,7 @@
 def merge_kernel(start, counts, packs, last, *refs):
     inputs, weight, gain, merge_weight, bias = refs[:5]
     pieces = refs[5 : 5 + sum(counts)]
-    *refs, state = refs[5 + sum(counts) :]
+    *refs, state, tokens = refs[5 + sum(counts) :]
     rows = state.shape[1]
     half = rows // 2
     rest = 2 * HD - LANES
@@ -483,26 +484,23 @@
         mixed = jnp.dot(
             jnp.concatenate(lined, axis=1), weight[...], preferred_element_type=jnp.float32
         )
-        before = inputs[start + part * half : start + (part + 1) * half, :].astype(jnp.float32)
-        normed = norm_rows(before + mixed, gain[...])
         for column in range(D // LANES):
-            state[column, token, :] = normed[:, column * LANES : (column + 1) * LANES]
+            lanes = slice(column * LANES, (column + 1) * LANES)
+            before = inputs[start + part * half : start + (part + 1) * half, lanes]
+            state[column, token, :] = before.astype(jnp.float32) + mixed[:, lanes]
     groups = rows // 4
-    total = bias[...]
-    for quadrant in range(4):
-        tokens = jnp.concatenate(
-            [
-                state[column, pl.ds(quadrant, groups, stride=4), :].astype(jnp.bfloat16)
-                for column in range(D // LANES)
-            ],
-            axis=1,
-        )
-        total = total + lax.dot_general(
-            tokens,
-            merge_weight[:, quadrant * D : (quadrant + 1) * D],
-            (((1,), (1,)), ((), ())),
-            preferred_element_type=jnp.float32,
-        )
+    for block in range(0, groups, NORM_ROWS):
+        for quadrant in range(4):
+            at = pl.ds(4 * block + quadrant, NORM_ROWS, stride=4)
+            residual = jnp.concatenate(
+                [state[column, at, :] for column in range(D // LANES)], axis=1
+            )
+            tokens[block : block + NORM_ROWS, quadrant * D : (quadrant + 1) * D] = norm_rows(
+                residual, gain[...]
+            ).astype(jnp.bfloat16)
+    total = bias[...] + lax.dot_general(
+        tokens[...], merge_weight[...], (((1,), (1,)), ((), ())), preferred_element_type=jnp.float32
+    )
     total = total.astype(jnp.bfloat16)
     if not last:
         refs[0][...] = total
@@ -552,7 +550,10 @@
         ),
         in_specs=specs,
         out_specs=[vmem] * len(shapes),
-        scratch_shapes=[pltpu.VMEM((D // LANES, rows, LANES), jnp.float32)],
+        scratch_shapes=[
+            pltpu.VMEM((D // LANES, rows, LANES), jnp.float32),
+            pltpu.VMEM((groups, 4 * D), jnp.bfloat16),
+        ],
         out_shape=shapes,
         compiler_params=pltpu.CompilerParams(vmem_limit_bytes=20 << 20),
         cost_estimate=pl.CostEstimate(
@@ -741,9 +742,11 @@
         previous = moving[-1][-1] if moving else ()
         across_x, across_y = after([across_x, across_y], latest, *previous)
         far = far_shards(across_x, across_y)
-        moving.append(
-            (own, own_swap, across_x, send_seq(across_x, 1), across_y, send_seq(across_y, 1), far)
-        )
+        swapped = [across_x, across_y]
+        if len(moving) < len(attended) - 1:
+            swapped = after(swapped, *far)
+        swap_x, swap_y = (send_seq(one, 1) for one in swapped)
+        moving.append((own, own_swap, across_x, swap_x, across_y, swap_y, far))
     for number, (start, rows) in enumerate(zip(starts, CHUNKS)):
         *near, far = moving[number]
         if projected:

time: 102 us -> 102 us (level)
  Pallas kernels: 41.8 us -> 44.9 us
  starting transfers between devices: 25.1 us -> 22 us
    pallas_call x2, Pallas kernels: 8.82 us -> 12.3 us  [attention_call(): pl.pallas_call(functools.partial(attention_kernel, start, first_owner, in...]
    ppermute x3, starting transfers between devices: 6.65 us -> 4.45 us  [fast_local(): lax.ppermute(made[flip], 'pack', [(z, z ^ flip) for z in range(packs)])]
  transfers between devices with their start and end apart: 30 -> 30, of which waited for: 15 -> 16; matrix products, arithmetic and copies ran while one was open for 1% -> 1% of each run, Pallas kernels for 24% -> 24%
where the time goes in v10:
time: 102 us; the launch traced here: 101 us
  Pallas kernels  44.9 us (44%)
  waiting for transfers between devices  31 us (30%)
  starting transfers between devices  22 us (22%)
  local copies, waits for them, and re-layouts  2.79 us (3%)
    ppermute x27, waiting for transfers between devices, send_seq(): return lax.ppermute(value, 'seq', [(i, i ^ flip) for i in range(size)])  19.6 us
    ppermute x27, starting transfers between devices, send_seq(): return lax.ppermute(value, 'seq', [(i, i ^ flip) for i in range(size)])  17.6 us
    pallas_call x2, Pallas kernels, merge_call(): pl.pallas_call(functools.partial(merge_kernel, start, [len(source) for so...  14.4 us
    pallas_call x2, Pallas kernels, attention_call(): pl.pallas_call(functools.partial(attention_kernel, start, first_owner, in...  12.3 us
    ppermute x3, waiting for transfers between devices, fast_local(): lax.ppermute(made[flip], 'pack', [(z, z ^ flip) for z in range(packs)])  11.4 us
    pallas_call x4, Pallas kernels, qkv_call(): pl.pallas_call(functools.partial(qkv_kernel, len(first), flip), in_specs=...  10 us
    pallas_call x1, Pallas kernels, prepare_call(): pl.pallas_call(functools.partial(prepare_kernel, shards), in_specs=[pl.Bl...  5.1 us
    ppermute x3, starting transfers between devices, fast_local(): lax.ppermute(made[flip], 'pack', [(z, z ^ flip) for z in range(packs)])  4.45 us
  transfers between devices with their start and end apart: 30, of which 16 were waited for; matrix products, arithmetic and copies ran while one was open for 1% of the time, Pallas kernels for 24%

profile of v10, /device:TPU:0, one launch (start us, length us, event | category | flops | bytes accessed | tf_op | source)
XLA Modules:
  0.0 100.9 jit_solution(8521200303627387701)
XLA Ops:
  0.0 1.5 %payload.1.refs_0_ = bf16[192,1536]{1,0:T(8,128)(2,1)S(1)} custom-call(s32[1,192]{1,0:T(1,128)} %segments.1, s32[1,192]{1,0:T(1,128)} %rows.1, s32[1,192]{1,0:T(1,128)} %columns.1, s32[1,192]{1,0:T(1,128)} %mask.1, bf16[1408]{0:T(1024)(128)(2,1)} %embed.1, bf16[1,192,1408]{2,1,0:T(8,128)(2,1)} %patches.1), custom_call_target="tpu_custom_call" | custom-call | flops 270336 | bytes 1081344 | tf_op jit(solution)/shard_map/payload/pallas_call | solution.py:204
  2.0 2.6 %collective-permute-start = (bf16[192,1536]{1,0:T(8,128)(2,1)S(1)}, bf16[192,1536]{1,0:T(8,128)(2,1)S(1)}, u32[]{:S(2)}, u32[]{:S(2)}) collective-permute-start(bf16[192,1536]{1,0:T(8,128)(2,1)S(1)} %payload.1.refs_0_), channel_id=1, source_target_pairs={{0,8},{4,12},{8,0},{12,4},{16,24},{20,28},{24,16},{28,20},{1,9},{5... | collective-permute-start | bytes 1769480 | tf_op jit(solution)/shard_map/ppermute | solution.py:603
  4.6 1.5 %collective-permute-start.1 = (bf16[192,1536]{1,0:T(8,128)(2,1)S(1)}, bf16[192,1536]{1,0:T(8,128)(2,1)S(1)}, u32[]{:S(2)}, u32[]{:S(2)}) collective-permute-start(bf16[192,1536]{1,0:T(8,128)(2,1)S(1)} %payload.1.refs_0_), channel_id=1, source_target_pairs={{0,16},{4,20},{8,24},{12,28},{16,0},{20,4},{24,8},{28,12},{1,17},{... | collective-permute-start | bytes 1769480 | tf_op jit(solution)/shard_map/ppermute | solution.py:603
  8.9 5.1 %prepare.1 = (f32[1,1408]{1,0:T(1,128)S(1)}, f32[1,1408]{1,0:T(1,128)S(1)}, f32[1,448]{1,0:T(1,128)S(1)}, bf16[1536,1408]{1,0:T(8,128)(2,1)S(1)}, bf16[448,5632]...) custom-call(s32[15]{0:T(128)S(1)} %concatenate.3.info.refs_15_, bf16[1408,1408]{1,0:T(8,128)(2,1)} %out_weight.1, ...), custom_call_target="tpu_custom_call" | custom-call | flops 1141899264 | bytes 20996096 | tf_op jit(solution)/shard_map/prepare/pallas_call | solution.py:437
  14.0 2.5 %norm_qkv.4 = (bf16[1536,1408]{1,0:T(8,128)(2,1)S(1)}, bf16[1536,1024]{1,0:T(8,128)(2,1)S(1)}, bf16[1536,128]{1,0:T(8,128)(2,1)S(1)}) custom-call(s32[15]{0:T(128)S(1)} %concatenate.3.info.refs_15_, bf16[192,1536]{1,0:T(8,128)(2,1)S(1)} %payload.1.refs_0_, bf16[192,1536]{1,0:T(8,128)(2,1)S(1)} %collective-permute-done.2.refs_1_, ...), custom_call_target="tpu_custom_call" | custom-call | flops 2491416576 | bytes 6488064 | tf_op jit(solution)/shard_map/norm_qkv/pallas_call | solution.py:279
  16.5 1.9 %collective-permute-done.across_x.refs_0_ = bf16[192,1536]{1,0:T(8,128)(2,1)S(1)} collective-permute-done((bf16[192,1536]{1,0:T(8,128)(2,1)S(1)}, bf16[192,1536]{1,0:T(8,128)(2,1)S(1)}, u32[]{:S(2)}, u32[]{:S(2)}) %collective-permute-start) | collective-permute-done | bytes 589856 | tf_op jit(solution)/shard_map/ppermute | solution.py:603
  18.5 1.5 %collective-permute-done.1.across_y.refs_0_ = bf16[192,1536]{1,0:T(8,128)(2,1)S(1)} collective-permute-done((bf16[192,1536]{1,0:T(8,128)(2,1)S(1)}, bf16[192,1536]{1,0:T(8,128)(2,1)S(1)}, u32[]{:S(2)}, u32[]{:S(2)}) %collective-permute-start.1) | collective-permute-done | bytes 589856 | tf_op jit(solution)/shard_map/ppermute | solution.py:603
  20.5 1.6 %collective-permute-start.3 = (bf16[96,1536]{1,0:T(8,128)(2,1)S(1)}, bf16[96,1536]{1,0:T(8,128)(2,1)S(1)}, u32[]{:S(2)}, u32[]{:S(2)}) collective-permute-start(bf16[96,1536]{1,0:T(8,128)(2,1)S(1)} %get-tuple-element.54), channel_id=1, source_target_pairs={{0,16},{4,20},{8,24},{12,28},{16,0},{20,4},{24,8},{28,12},{1,17},{... | collective-permute-start | bytes 884744 | tf_op jit(solution)/shard_map/ppermute | solution.py:603
  22.6 2.5 %norm_qkv.5 = (bf16[1536,1408]{1,0:T(8,128)(2,1)S(1)}, bf16[1536,1024]{1,0:T(8,128)(2,1)S(1)}, bf16[1536,128]{1,0:T(8,128)(2,1)S(1)}) custom-call(s32[15]{0:T(128)S(1)} %concatenate.3.info.refs_15_, bf16[192,1536]{1,0:T(8,128)(2,1)S(1)} %collective-permute-done.across_x.refs_0_, ...), custom_call_target="tpu_custom_call", output_to_operand_aliasing={{0}: (6, {}), {1}: (7, {}), {2}: (8, {})} | custom-call | flops 2491416576 | bytes 6488064 | tf_op jit(solution)/shard_map/norm_qkv/pallas_call | solution.py:279
  25.2 2.5 %norm_qkv.6 = (bf16[1536,1408]{1,0:T(8,128)(2,1)S(1)}, bf16[1536,1024]{1,0:T(8,128)(2,1)S(1)}, bf16[1536,128]{1,0:T(8,128)(2,1)S(1)}) custom-call(s32[15]{0:T(128)S(1)} %concatenate.3.info.refs_15_, bf16[192,1536]{1,0:T(8,128)(2,1)S(1)} %collective-permute-done.1.across_y.refs_0_, ...), custom_call_target="tpu_custom_call", output_to_operand_aliasing={{0}: (6, {}), {1}: (7, {}), {2}: (8, {})} | custom-call | flops 2491416576 | bytes 6488064 | tf_op jit(solution)/shard_map/norm_qkv/pallas_call | solution.py:279
  27.7 1.8 %collective-permute-done.3.refs_0_ = bf16[96,1536]{1,0:T(8,128)(2,1)S(1)} collective-permute-done((bf16[96,1536]{1,0:T(8,128)(2,1)S(1)}, bf16[96,1536]{1,0:T(8,128)(2,1)S(1)}, u32[]{:S(2)}, u32[]{:S(2)}) %collective-permute-start.3) | collective-permute-done | bytes 294944 | tf_op jit(solution)/shard_map/ppermute | solution.py:603
  29.5 1.2 %collective-permute-done.4.refs_1_ = bf16[96,1536]{1,0:T(8,128)(2,1)S(1)} collective-permute-done((bf16[96,1536]{1,0:T(8,128)(2,1)S(1)}, bf16[96,1536]{1,0:T(8,128)(2,1)S(1)}, u32[]{:S(2)}, u32[]{:S(2)}) %collective-permute-start.4) | collective-permute-done | bytes 294944 | tf_op jit(solution)/shard_map/ppermute | solution.py:603
  31.2 1.1 %collective-permute-done.7.refs_2_ = bf16[96,1536]{1,0:T(8,128)(2,1)S(1)} collective-permute-done((bf16[96,1536]{1,0:T(8,128)(2,1)S(1)}, bf16[96,1536]{1,0:T(8,128)(2,1)S(1)}, u32[]{:S(2)}, u32[]{:S(2)}) %collective-permute-start.7) | collective-permute-done | bytes 294944 | tf_op jit(solution)/shard_map/ppermute | solution.py:603
  32.7 2.5 %norm_qkv.7 = (bf16[1536,1408]{1,0:T(8,128)(2,1)S(1)}, bf16[1536,1024]{1,0:T(8,128)(2,1)S(1)}, bf16[1536,128]{1,0:T(8,128)(2,1)S(1)}) custom-call(s32[15]{0:T(128)S(1)} %concatenate.3.info.refs_15_, bf16[96,1536]{1,0:T(8,128)(2,1)S(1)} %collective-permute-done.3.refs_0_, ...), custom_call_target="tpu_custom_call", output_to_operand_aliasing={{0}: (8, {}), {1}: (9, {}), {2}: (10, {})} | custom-call | flops 2491416576 | bytes 6488064 | tf_op jit(solution)/shard_map/norm_qkv/pallas_call | solution.py:279
  35.2 6.9 %attention.3 = (bf16[1152,128]{1,0:T(8,128)(2,1)S(1)}, bf16[16,128]{1,0:T(8,128)(2,1)S(1)}) custom-call(s32[15]{0:T(128)S(1)} %concatenate.3.info.refs_15_, bf16[1536,128]{1,0:T(8,128)(2,1)S(1)} %get-tuple-element.70.labels, bf16[1536,1024]{1,0:T(8,128)(2,1)S(1)} %get-tuple-element.71.block), custom_call_target="tpu_custom_call" | custom-call | flops 3019898880 | bytes 3145728 | tf_op jit(solution)/shard_map/attention/pallas_call | solution.py:383
  43.1 5.4 %attention.2.refs_5_ = bf16[1152,128]{1,0:T(8,128)(2,1)S(1)} custom-call(s32[15]{0:T(128)S(1)} %concatenate.3.info.refs_15_, bf16[1536,128]{1,0:T(8,128)(2,1)S(1)} %get-tuple-element.70.labels, bf16[1536,1024]{1,0:T(8,128)(2,1)S(1)} %get-tuple-element.71.block), custom_call_target="tpu_custom_call" | custom-call | flops 3019898880 | bytes 3145728 | tf_op jit(solution)/shard_map/attention/pallas_call | solution.py:383
  48.5 2.8 %collective-permute-done.10.across_x.refs_7_ = bf16[1152,128]{1,0:T(8,128)(2,1)S(1)} collective-permute-done((bf16[1152,128]{1,0:T(8,128)(2,1)S(1)}, bf16[1152,128]{1,0:T(8,128)(2,1)S(1)}, u32[]{:S(2)}, u32[]{:S(2)}) %collective-permute-start.10) | collective-permute-done | bytes 294944 | tf_op jit(solution)/shard_map/ppermute | solution.py:603
  52.0 1.6 %collective-permute-start.16 = (bf16[576,128]{1,0:T(8,128)(2,1)S(1)}, bf16[576,128]{1,0:T(8,128)(2,1)S(1)}, u32[]{:S(2)}, u32[]{:S(2)}) collective-permute-start(bf16[576,128]{1,0:T(8,128)(2,1)S(1)} %get-tuple-element.77), channel_id=1, source_target_pairs={{0,8},{4,12},{8,0},{12,4},{16,24},{20,28},{24,16},{28,20},{1,9},{5... | collective-permute-start | bytes 442376 | tf_op jit(solution)/shard_map/ppermute | solution.py:603
  54.0 1.7 %collective-permute-start.14 = (bf16[1152,128]{1,0:T(8,128)(2,1)S(1)}, bf16[1152,128]{1,0:T(8,128)(2,1)S(1)}, u32[]{:S(2)}, u32[]{:S(2)}) collective-permute-start(bf16[1152,128]{1,0:T(8,128)(2,1)S(1)} %attention.2.refs_5_), channel_id=1, source_target_pairs={{0,16},{4,20},{8,24},{12,28},{16,0},{20,4},{24,8},{28,12},{1,17},{... | collective-permute-start | bytes 884744 | tf_op jit(solution)/shard_map/ppermute | solution.py:603
  55.6 2.7 %collective-permute-done.15.refs_11_ = bf16[576,128]{1,0:T(8,128)(2,1)S(1)} collective-permute-done((bf16[576,128]{1,0:T(8,128)(2,1)S(1)}, bf16[576,128]{1,0:T(8,128)(2,1)S(1)}, u32[]{:S(2)}, u32[]{:S(2)}) %collective-permute-start.15) | collective-permute-done | bytes 147488 | tf_op jit(solution)/shard_map/ppermute | solution.py:603
  59.3 3.7 %collective-permute-done.13.across_x.refs_7_ = bf16[1152,128]{1,0:T(8,128)(2,1)S(1)} collective-permute-done((bf16[1152,128]{1,0:T(8,128)(2,1)S(1)}, bf16[1152,128]{1,0:T(8,128)(2,1)S(1)}, u32[]{:S(2)}, u32[]{:S(2)}) %collective-permute-start.13) | collective-permute-done | bytes 294944 | tf_op jit(solution)/shard_map/ppermute | solution.py:603
  63.6 0.7 collective-permute-done.24.refs_14_
  64.5 1.5 %collective-permute-start.19 = (bf16[576,128]{1,0:T(8,128)(2,1)S(1)}, bf16[576,128]{1,0:T(8,128)(2,1)S(1)}, u32[]{:S(2)}, u32[]{:S(2)}) collective-permute-start(bf16[576,128]{1,0:T(8,128)(2,1)S(1)} %get-tuple-element.80), channel_id=1, source_target_pairs={{0,16},{4,20},{8,24},{12,28},{16,0},{20,4},{24,8},{28,12},{1,17},{... | collective-permute-start | bytes 442376 | tf_op jit(solution)/shard_map/ppermute | solution.py:603
  66.0 1.4 %collective-permute-start.20 = (bf16[576,128]{1,0:T(8,128)(2,1)S(1)}, bf16[576,128]{1,0:T(8,128)(2,1)S(1)}, u32[]{:S(2)}, u32[]{:S(2)}) collective-permute-start(bf16[576,128]{1,0:T(8,128)(2,1)S(1)} %get-tuple-element.81), channel_id=1, source_target_pairs={{0,8},{4,12},{8,0},{12,4},{16,24},{20,28},{24,16},{28,20},{1,9},{5... | collective-permute-start | bytes 442376 | tf_op jit(solution)/shard_map/ppermute | solution.py:603
  67.5 6.6 %out_merge.2.refs_17_ = bf16[192,448]{1,0:T(8,128)(2,1)S(1)} custom-call(bf16[1536,1408]{1,0:T(8,128)(2,1)S(1)} %get-tuple-element.66.refs_0_, bf16[1536,1408]{1,0:T(8,128)(2,1)S(1)} %get-tuple-element.51.refs_1_, f32[1,1408]{1,0:T(1,128)S(1)} %get-tuple-element.67.refs_2_, bf16[448,5632]{1,0:T(8,128)(2,1)S(1)} %get-tuple-element.68.refs_3_, ...), custom_call_target="tpu_custom_call" | custom-call | flops 7059013632 | bytes 15499264 | tf_op jit(solution)/shard_map/out_merge/pallas_call | solution.py:547
  74.7 0.8 collective-permute-done.25.refs_13_
  75.7 7.7 %out_merge.3 = (bf16[672,128]{1,0:T(8,128)(2,1)S(1)}, bf16[672,128]{1,0:T(8,128)(2,1)S(1)}, bf16[672,128]{1,0:T(8,128)(2,1)S(1)}, bf16[672,128]{1,0:T(8,128)(2,1)S(1)}) custom-call(bf16[1536,1408]{1,0:T(8,128)(2,1)S(1)} %get-tuple-element.66.refs_0_, bf16[1536,1408]{1,0:T(8,128)(2,1)S(1)} %get-tuple-element.51.refs_1_, ...), custom_call_target="tpu_custom_call" | custom-call | flops 7059013632 | bytes 15499264 | tf_op jit(solution)/shard_map/out_merge/pallas_call | solution.py:547
  83.8 1.6 %collective-permute-start.28 = (bf16[672,128]{1,0:T(8,128)(2,1)S(1)}, bf16[672,128]{1,0:T(8,128)(2,1)S(1)}, u32[]{:S(2)}, u32[]{:S(2)}) collective-permute-start(bf16[672,128]{1,0:T(8,128)(2,1)S(1)} %get-tuple-element.89), channel_id=1, source_target_pairs={{0,2},{1,3},{2,0},{3,1},{4,6},{5,7},{6,4},{7,5},{8,10},{9,11},{10,... | collective-permute-start | bytes 516104 | tf_op jit(solution)/shard_map/ppermute | solution.py:763
  85.3 2.6 %collective-permute-start.29 = (bf16[672,128]{1,0:T(8,128)(2,1)S(1)}, bf16[672,128]{1,0:T(8,128)(2,1)S(1)}, u32[]{:S(2)}, u32[]{:S(2)}) collective-permute-start(bf16[672,128]{1,0:T(8,128)(2,1)S(1)} %get-tuple-element.90), channel_id=1, source_target_pairs={{0,3},{1,2},{2,1},{3,0},{4,7},{5,6},{6,5},{7,4},{8,11},{9,10},{10,... | collective-permute-start | bytes 516104 | tf_op jit(solution)/shard_map/ppermute | solution.py:763
  87.9 5.6 %collective-permute-done.27.refs_1_ = bf16[672,128]{1,0:T(8,128)(2,1)S(1)} collective-permute-done((bf16[672,128]{1,0:T(8,128)(2,1)S(1)}, bf16[672,128]{1,0:T(8,128)(2,1)S(1)}, u32[]{:S(2)}, u32[]{:S(2)}) %collective-permute-start.27) | collective-permute-done | bytes 172064 | tf_op jit(solution)/shard_map/ppermute | solution.py:763
  93.5 5.8 %collective-permute-done.28.refs_2_ = bf16[672,128]{1,0:T(8,128)(2,1)S(1)} collective-permute-done((bf16[672,128]{1,0:T(8,128)(2,1)S(1)}, bf16[672,128]{1,0:T(8,128)(2,1)S(1)}, u32[]{:S(2)}, u32[]{:S(2)}) %collective-permute-start.28) | collective-permute-done | bytes 172064 | tf_op jit(solution)/shard_map/ppermute | solution.py:763
  99.3 1.6 %place_rows.1 = bf16[4,192,448]{2,1,0:T(8,128)(2,1)} custom-call(s32[15]{0:T(128)S(1)} %concatenate.3.info.refs_15_, bf16[672,128]{1,0:T(8,128)(2,1)S(1)} %get-tuple-element.87.refs_0_, bf16[672,128]{1,0:T(8,128)(2,1)S(1)} %collective-permute-done.27.refs_1_, bf16[672,128]{1,0:T(8,128)(2,1)S(1)} %collective-permute-done.28.refs_2_, ...), custom_call_target="tpu_custom_call" | custom-call | bytes 1376256 | tf_op jit(solution)/shard_map/place_rows/pallas_call | solution.py:587
  (51 shorter events, 10.2 us)
Async XLA Ops:
  1.5 12.5 %collective-permute-start.2 = (bf16[192,1536]{1,0:T(8,128)(2,1)S(1)}, bf16[192,1536]{1,0:T(8,128)(2,1)S(1)}, u32[]{:S(2)}, u32[]{:S(2)}) collective-permute-start(bf16[192,1536]{1,0:T(8,128)(2,1)S(1)} %payload.1.refs_0_), channel_id=1, source_target_pairs={{0,4},{4,0},{8,12},{12,8},{16,20},{20,16},{24,28},{28,24},{1,5},{5... | collective-permute-start | bytes 1769480 | tf_op jit(solution)/shard_map/ppermute | solution.py:603
  2.0 16.5 %collective-permute-start = (bf16[192,1536]{1,0:T(8,128)(2,1)S(1)}, bf16[192,1536]{1,0:T(8,128)(2,1)S(1)}, u32[]{:S(2)}, u32[]{:S(2)}) collective-permute-start(bf16[192,1536]{1,0:T(8,128)(2,1)S(1)} %payload.1.refs_0_), channel_id=1, source_target_pairs={{0,8},{4,12},{8,0},{12,4},{16,24},{20,28},{24,16},{28,20},{1,9},{5... | collective-permute-start | bytes 1769480 | tf_op jit(solution)/shard_map/ppermute | solution.py:603
  4.6 15.4 %collective-permute-start.1 = (bf16[192,1536]{1,0:T(8,128)(2,1)S(1)}, bf16[192,1536]{1,0:T(8,128)(2,1)S(1)}, u32[]{:S(2)}, u32[]{:S(2)}) collective-permute-start(bf16[192,1536]{1,0:T(8,128)(2,1)S(1)} %payload.1.refs_0_), channel_id=1, source_target_pairs={{0,16},{4,20},{8,24},{12,28},{16,0},{20,4},{24,8},{28,12},{1,17},{... | collective-permute-start | bytes 1769480 | tf_op jit(solution)/shard_map/ppermute | solution.py:603
  6.8 0.7 copy-start.1
  8.9 5.1 %copy-start = (bf16[128,512]{1,0:T(8,128)(2,1)S(1)}, bf16[128,512]{1,0:T(8,128)(2,1)}, u32[]{:S(2)}) copy-start(bf16[128,512]{1,0:T(8,128)(2,1)} %constant.48.clone.refs_2_.refs_4_) | copy-start | bytes 393220
  20.0 2.7 %collective-permute-start.6 = (bf16[192,1536]{1,0:T(8,128)(2,1)S(1)}, bf16[192,1536]{1,0:T(8,128)(2,1)S(1)}, u32[]{:S(2)}, u32[]{:S(2)}) collective-permute-start(bf16[192,1536]{1,0:T(8,128)(2,1)S(1)} %collective-permute-done.across_x.refs_0_), channel_id=1, source_target_pairs={{0,4},{4,0},{8,12},{12,8},{16,20},{20,16},{24,28},{28,24},{1,5},{5... | collective-permute-start | bytes 1769480 | tf_op jit(solution)/shard_map/ppermute | solution.py:603
  20.0 5.2 %collective-permute-start.5 = (bf16[192,1536]{1,0:T(8,128)(2,1)S(1)}, bf16[192,1536]{1,0:T(8,128)(2,1)S(1)}, u32[]{:S(2)}, u32[]{:S(2)}) collective-permute-start(bf16[192,1536]{1,0:T(8,128)(2,1)S(1)} %collective-permute-done.1.across_y.refs_0_), channel_id=1, source_target_pairs={{0,4},{4,0},{8,12},{12,8},{16,20},{20,16},{24,28},{28,24},{1,5},{5... | collective-permute-start | bytes 1769480 | tf_op jit(solution)/shard_map/ppermute | solution.py:603
  20.5 9.0 %collective-permute-start.3 = (bf16[96,1536]{1,0:T(8,128)(2,1)S(1)}, bf16[96,1536]{1,0:T(8,128)(2,1)S(1)}, u32[]{:S(2)}, u32[]{:S(2)}) collective-permute-start(bf16[96,1536]{1,0:T(8,128)(2,1)S(1)} %get-tuple-element.54), channel_id=1, source_target_pairs={{0,16},{4,20},{8,24},{12,28},{16,0},{20,4},{24,8},{28,12},{1,17},{... | collective-permute-start | bytes 884744 | tf_op jit(solution)/shard_map/ppermute | solution.py:603
  22.1 8.6 %collective-permute-start.4 = (bf16[96,1536]{1,0:T(8,128)(2,1)S(1)}, bf16[96,1536]{1,0:T(8,128)(2,1)S(1)}, u32[]{:S(2)}, u32[]{:S(2)}) collective-permute-start(bf16[96,1536]{1,0:T(8,128)(2,1)S(1)} %get-tuple-element.55), channel_id=1, source_target_pairs={{0,8},{4,12},{8,0},{12,4},{16,24},{20,28},{24,16},{28,20},{1,9},{5... | collective-permute-start | bytes 884744 | tf_op jit(solution)/shard_map/ppermute | solution.py:603
  30.7 1.6 %collective-permute-start.7 = (bf16[96,1536]{1,0:T(8,128)(2,1)S(1)}, bf16[96,1536]{1,0:T(8,128)(2,1)S(1)}, u32[]{:S(2)}, u32[]{:S(2)}) collective-permute-start(bf16[96,1536]{1,0:T(8,128)(2,1)S(1)} %collective-permute-done.3.refs_0_), channel_id=1, source_target_pairs={{0,4},{4,0},{8,12},{12,8},{16,20},{20,16},{24,28},{28,24},{1,5},{5... | collective-permute-start | bytes 884744 | tf_op jit(solution)/shard_map/ppermute | solution.py:603
  30.7 2.0 %collective-permute-start.8 = (bf16[96,1536]{1,0:T(8,128)(2,1)S(1)}, bf16[96,1536]{1,0:T(8,128)(2,1)S(1)}, u32[]{:S(2)}, u32[]{:S(2)}) collective-permute-start(bf16[96,1536]{1,0:T(8,128)(2,1)S(1)} %collective-permute-done.4.refs_1_), channel_id=1, source_target_pairs={{0,4},{4,0},{8,12},{12,8},{16,20},{20,16},{24,28},{28,24},{1,5},{5... | collective-permute-start | bytes 884744 | tf_op jit(solution)/shard_map/ppermute | solution.py:603
  42.1 9.1 %collective-permute-start.10 = (bf16[1152,128]{1,0:T(8,128)(2,1)S(1)}, bf16[1152,128]{1,0:T(8,128)(2,1)S(1)}, u32[]{:S(2)}, u32[]{:S(2)}) collective-permute-start(bf16[1152,128]{1,0:T(8,128)(2,1)S(1)} %get-tuple-element.72.refs_5_), channel_id=1, source_target_pairs={{0,8},{4,12},{8,0},{12,4},{16,24},{20,28},{24,16},{28,20},{1,9},{5... | collective-permute-start | bytes 884744 | tf_op jit(solution)/shard_map/ppermute | solution.py:603
  42.8 8.7 %collective-permute-start.11 = (bf16[1152,128]{1,0:T(8,128)(2,1)S(1)}, bf16[1152,128]{1,0:T(8,128)(2,1)S(1)}, u32[]{:S(2)}, u32[]{:S(2)}) collective-permute-start(bf16[1152,128]{1,0:T(8,128)(2,1)S(1)} %get-tuple-element.72.refs_5_), channel_id=1, source_target_pairs={{0,16},{4,20},{8,24},{12,28},{16,0},{20,4},{24,8},{28,12},{1,17},{... | collective-permute-start | bytes 884744 | tf_op jit(solution)/shard_map/ppermute | solution.py:603
  43.1 8.4 %collective-permute-start.9 = (bf16[1152,128]{1,0:T(8,128)(2,1)S(1)}, bf16[1152,128]{1,0:T(8,128)(2,1)S(1)}, u32[]{:S(2)}, u32[]{:S(2)}) collective-permute-start(bf16[1152,128]{1,0:T(8,128)(2,1)S(1)} %get-tuple-element.72.refs_5_), channel_id=1, source_target_pairs={{0,4},{4,0},{8,12},{12,8},{16,20},{20,16},{24,28},{28,24},{1,5},{5... | collective-permute-start | bytes 884744 | tf_op jit(solution)/shard_map/ppermute | solution.py:603
  51.5 6.8 %collective-permute-start.15 = (bf16[576,128]{1,0:T(8,128)(2,1)S(1)}, bf16[576,128]{1,0:T(8,128)(2,1)S(1)}, u32[]{:S(2)}, u32[]{:S(2)}) collective-permute-start(bf16[576,128]{1,0:T(8,128)(2,1)S(1)} %get-tuple-element.76), channel_id=1, source_target_pairs={{0,16},{4,20},{8,24},{12,28},{16,0},{20,4},{24,8},{28,12},{1,17},{... | collective-permute-start | bytes 442376 | tf_op jit(solution)/shard_map/ppermute | solution.py:603
  52.0 6.8 %collective-permute-start.16 = (bf16[576,128]{1,0:T(8,128)(2,1)S(1)}, bf16[576,128]{1,0:T(8,128)(2,1)S(1)}, u32[]{:S(2)}, u32[]{:S(2)}) collective-permute-start(bf16[576,128]{1,0:T(8,128)(2,1)S(1)} %get-tuple-element.77), channel_id=1, source_target_pairs={{0,8},{4,12},{8,0},{12,4},{16,24},{20,28},{24,16},{28,20},{1,9},{5... | collective-permute-start | bytes 442376 | tf_op jit(solution)/shard_map/ppermute | solution.py:603
  53.6 9.4 %collective-permute-start.13 = (bf16[1152,128]{1,0:T(8,128)(2,1)S(1)}, bf16[1152,128]{1,0:T(8,128)(2,1)S(1)}, u32[]{:S(2)}, u32[]{:S(2)}) collective-permute-start(bf16[1152,128]{1,0:T(8,128)(2,1)S(1)} %attention.2.refs_5_), channel_id=1, source_target_pairs={{0,8},{4,12},{8,0},{12,4},{16,24},{20,28},{24,16},{28,20},{1,9},{5... | collective-permute-start | bytes 884744 | tf_op jit(solution)/shard_map/ppermute | solution.py:603
  54.0 9.0 %collective-permute-start.14 = (bf16[1152,128]{1,0:T(8,128)(2,1)S(1)}, bf16[1152,128]{1,0:T(8,128)(2,1)S(1)}, u32[]{:S(2)}, u32[]{:S(2)}) collective-permute-start(bf16[1152,128]{1,0:T(8,128)(2,1)S(1)} %attention.2.refs_5_), channel_id=1, source_target_pairs={{0,16},{4,20},{8,24},{12,28},{16,0},{20,4},{24,8},{28,12},{1,17},{... | collective-permute-start | bytes 884744 | tf_op jit(solution)/shard_map/ppermute | solution.py:603
  58.8 5.7 %collective-permute-start.21 = (bf16[1152,128]{1,0:T(8,128)(2,1)S(1)}, bf16[1152,128]{1,0:T(8,128)(2,1)S(1)}, u32[]{:S(2)}, u32[]{:S(2)}) collective-permute-start(bf16[1152,128]{1,0:T(8,128)(2,1)S(1)} %collective-permute-done.10.across_x.refs_7_), channel_id=1, source_target_pairs={{0,4},{4,0},{8,12},{12,8},{16,20},{20,16},{24,28},{28,24},{1,5},{5... | collective-permute-start | bytes 884744 | tf_op jit(solution)/shard_map/ppermute | solution.py:603
  58.8 7.3 %collective-permute-start.22 = (bf16[1152,128]{1,0:T(8,128)(2,1)S(1)}, bf16[1152,128]{1,0:T(8,128)(2,1)S(1)}, u32[]{:S(2)}, u32[]{:S(2)}) collective-permute-start(bf16[1152,128]{1,0:T(8,128)(2,1)S(1)} %collective-permute-done.11.across_y.refs_9_), channel_id=1, source_target_pairs={{0,4},{4,0},{8,12},{12,8},{16,20},{20,16},{24,28},{28,24},{1,5},{5... | collective-permute-start | bytes 884744 | tf_op jit(solution)/shard_map/ppermute | solution.py:603
  59.3 4.2 %collective-permute-start.23 = (bf16[576,128]{1,0:T(8,128)(2,1)S(1)}, bf16[576,128]{1,0:T(8,128)(2,1)S(1)}, u32[]{:S(2)}, u32[]{:S(2)}) collective-permute-start(bf16[576,128]{1,0:T(8,128)(2,1)S(1)} %collective-permute-done.15.refs_11_), channel_id=1, source_target_pairs={{0,4},{4,0},{8,12},{12,8},{16,20},{20,16},{24,28},{28,24},{1,5},{5... | collective-permute-start | bytes 442376 | tf_op jit(solution)/shard_map/ppermute | solution.py:603
  63.0 1.4 %collective-permute-start.24 = (bf16[576,128]{1,0:T(8,128)(2,1)S(1)}, bf16[576,128]{1,0:T(8,128)(2,1)S(1)}, u32[]{:S(2)}, u32[]{:S(2)}) collective-permute-start(bf16[576,128]{1,0:T(8,128)(2,1)S(1)} %collective-permute-done.16.refs_12_), channel_id=1, source_target_pairs={{0,4},{4,0},{8,12},{12,8},{16,20},{20,16},{24,28},{28,24},{1,5},{5... | collective-permute-start | bytes 442376 | tf_op jit(solution)/shard_map/ppermute | solution.py:603
  63.0 11.7 %collective-permute-start.12 = (bf16[1152,128]{1,0:T(8,128)(2,1)S(1)}, bf16[1152,128]{1,0:T(8,128)(2,1)S(1)}, u32[]{:S(2)}, u32[]{:S(2)}) collective-permute-start(bf16[1152,128]{1,0:T(8,128)(2,1)S(1)} %attention.2.refs_5_), channel_id=1, source_target_pairs={{0,4},{4,0},{8,12},{12,8},{16,20},{20,16},{24,28},{28,24},{1,5},{5... | collective-permute-start | bytes 884744 | tf_op jit(solution)/shard_map/ppermute | solution.py:603
  63.5 11.2 %collective-permute-start.17 = (bf16[1152,128]{1,0:T(8,128)(2,1)S(1)}, bf16[1152,128]{1,0:T(8,128)(2,1)S(1)}, u32[]{:S(2)}, u32[]{:S(2)}) collective-permute-start(bf16[1152,128]{1,0:T(8,128)(2,1)S(1)} %collective-permute-done.13.across_x.refs_7_), channel_id=1, source_target_pairs={{0,4},{4,0},{8,12},{12,8},{16,20},{20,16},{24,28},{28,24},{1,5},{5... | collective-permute-start | bytes 884744 | tf_op jit(solution)/shard_map/ppermute | solution.py:603
  64.3 10.3 %collective-permute-start.18 = (bf16[1152,128]{1,0:T(8,128)(2,1)S(1)}, bf16[1152,128]{1,0:T(8,128)(2,1)S(1)}, u32[]{:S(2)}, u32[]{:S(2)}) collective-permute-start(bf16[1152,128]{1,0:T(8,128)(2,1)S(1)} %collective-permute-done.14.across_y.refs_9_), channel_id=1, source_target_pairs={{0,4},{4,0},{8,12},{12,8},{16,20},{20,16},{24,28},{28,24},{1,5},{5... | collective-permute-start | bytes 884744 | tf_op jit(solution)/shard_map/ppermute | solution.py:603
  64.5 9.6 %collective-permute-start.19 = (bf16[576,128]{1,0:T(8,128)(2,1)S(1)}, bf16[576,128]{1,0:T(8,128)(2,1)S(1)}, u32[]{:S(2)}, u32[]{:S(2)}) collective-permute-start(bf16[576,128]{1,0:T(8,128)(2,1)S(1)} %get-tuple-element.80), channel_id=1, source_target_pairs={{0,16},{4,20},{8,24},{12,28},{16,0},{20,4},{24,8},{28,12},{1,17},{... | collective-permute-start | bytes 442376 | tf_op jit(solution)/shard_map/ppermute | solution.py:603
  66.0 8.1 %collective-permute-start.20 = (bf16[576,128]{1,0:T(8,128)(2,1)S(1)}, bf16[576,128]{1,0:T(8,128)(2,1)S(1)}, u32[]{:S(2)}, u32[]{:S(2)}) collective-permute-start(bf16[576,128]{1,0:T(8,128)(2,1)S(1)} %get-tuple-element.81), channel_id=1, source_target_pairs={{0,8},{4,12},{8,0},{12,4},{16,24},{20,28},{24,16},{28,20},{1,9},{5... | collective-permute-start | bytes 442376 | tf_op jit(solution)/shard_map/ppermute | solution.py:603
  74.1 1.4 %collective-permute-start.25 = (bf16[576,128]{1,0:T(8,128)(2,1)S(1)}, bf16[576,128]{1,0:T(8,128)(2,1)S(1)}, u32[]{:S(2)}, u32[]{:S(2)}) collective-permute-start(bf16[576,128]{1,0:T(8,128)(2,1)S(1)} %collective-permute-done.19.refs_11_), channel_id=1, source_target_pairs={{0,4},{4,0},{8,12},{12,8},{16,20},{20,16},{24,28},{28,24},{1,5},{5... | collective-permute-start | bytes 442376 | tf_op jit(solution)/shard_map/ppermute | solution.py:603
  74.2 1.6 %collective-permute-start.26 = (bf16[576,128]{1,0:T(8,128)(2,1)S(1)}, bf16[576,128]{1,0:T(8,128)(2,1)S(1)}, u32[]{:S(2)}, u32[]{:S(2)}) collective-permute-start(bf16[576,128]{1,0:T(8,128)(2,1)S(1)} %collective-permute-done.20.refs_12_), channel_id=1, source_target_pairs={{0,4},{4,0},{8,12},{12,8},{16,20},{20,16},{24,28},{28,24},{1,5},{5... | collective-permute-start | bytes 442376 | tf_op jit(solution)/shard_map/ppermute | solution.py:603
  83.5 10.0 %collective-permute-start.27 = (bf16[672,128]{1,0:T(8,128)(2,1)S(1)}, bf16[672,128]{1,0:T(8,128)(2,1)S(1)}, u32[]{:S(2)}, u32[]{:S(2)}) collective-permute-start(bf16[672,128]{1,0:T(8,128)(2,1)S(1)} %get-tuple-element.88), channel_id=1, source_target_pairs={{0,1},{1,0},{2,3},{3,2},{4,5},{5,4},{6,7},{7,6},{8,9},{9,8},{10,11... | collective-permute-start | bytes 516104 | tf_op jit(solution)/shard_map/ppermute | solution.py:763
  83.8 15.5 %collective-permute-start.28 = (bf16[672,128]{1,0:T(8,128)(2,1)S(1)}, bf16[672,128]{1,0:T(8,128)(2,1)S(1)}, u32[]{:S(2)}, u32[]{:S(2)}) collective-permute-start(bf16[672,128]{1,0:T(8,128)(2,1)S(1)} %get-tuple-element.89), channel_id=1, source_target_pairs={{0,2},{1,3},{2,0},{3,1},{4,6},{5,7},{6,4},{7,5},{8,10},{9,11},{10,... | collective-permute-start | bytes 516104 | tf_op jit(solution)/shard_map/ppermute | solution.py:763
  85.3 14.0 %collective-permute-start.29 = (bf16[672,128]{1,0:T(8,128)(2,1)S(1)}, bf16[672,128]{1,0:T(8,128)(2,1)S(1)}, u32[]{:S(2)}, u32[]{:S(2)}) collective-permute-start(bf16[672,128]{1,0:T(8,128)(2,1)S(1)} %get-tuple-element.90), channel_id=1, source_target_pairs={{0,3},{1,2},{2,1},{3,0},{4,7},{5,6},{6,5},{7,4},{8,11},{9,10},{10,... | collective-permute-start | bytes 516104 | tf_op jit(solution)/shard_map/ppermute | solution.py:763
  (2 other events, 1.4 us)

commit v11 on v10

--- a/solution.py
+++ b/solution.py
@@ -148,7 +148,7 @@
 
 LANES = 128
 CHIP, CORE, PACK, IDS = 0, 1, 2, 3
-BLOCK = 256
+BLOCK = 512
 POSITIONS = 64
 FAR_APART = -(2.0**100)
 IMAGE_LANE = 96
@@ -325,9 +325,8 @@
                 queries, keys, (((1,), (1,)), ((), ())), preferred_element_type=jnp.float32
             )
             scores[head, step] = values
-            high[head] = jnp.maximum(
-                high[head], jnp.maximum(values[:, :LANES], values[:, LANES:])
-            )
+            tops = [values[:, lane : lane + LANES] for lane in range(0, BLOCK, LANES)]
+            high[head] = functools.reduce(jnp.maximum, tops, high[head])
         return carry
 
     lax.fori_loop(begin, end, score, 0)
@@ -741,10 +740,12 @@
     for own, (own_swap, across_x, across_y) in attended:
         previous = moving[-1][-1] if moving else ()
         across_x, across_y = after([across_x, across_y], latest, *previous)
-        far = far_shards(across_x, across_y)
         swapped = [across_x, across_y]
         if len(moving) < len(attended) - 1:
+            far = far_shards(across_x, across_y)
             swapped = after(swapped, *far)
+        else:
+            far = [send_seq(own, 6)]
         swap_x, swap_y = (send_seq(one, 1) for one in swapped)
         moving.append((own, own_swap, across_x, swap_x, across_y, swap_y, far))
     for number, (start, rows) in enumerate(zip(starts, CHUNKS)):

time: 102 us -> 100 us (0.980); the launches traced: 101 us -> 100 us
  waiting for transfers between devices: 31 us -> 34.6 us
  Pallas kernels: 44.9 us -> 41.4 us
    pallas_call x2, Pallas kernels: 12.3 us -> 8.85 us  [attention_call(): pl.pallas_call(functools.partial(attention_kernel, start, first_owner, in...]
    ppermute x27 -> x25, waiting for transfers between devices: 19.6 us -> 22 us  [send_seq(): return lax.ppermute(value, 'seq', [(i, i ^ flip) for i in range(size)])]
    ppermute x27 -> x25, starting transfers between devices: 17.6 us -> 15.6 us  [send_seq(): return lax.ppermute(value, 'seq', [(i, i ^ flip) for i in range(size)])]
    ppermute x3, waiting for transfers between devices: 11.4 us -> 12.6 us  [fast_local(): lax.ppermute(made[flip], 'pack', [(z, z ^ flip) for z in range(packs)])]
    ppermute x3, starting transfers between devices: 4.45 us -> 5.47 us  [fast_local(): lax.ppermute(made[flip], 'pack', [(z, z ^ flip) for z in range(packs)])]
  transfers between devices with their start and end apart: 30 -> 28, of which waited for: 16 -> 15; matrix products, arithmetic and copies ran while one was open for 1% -> 1% of each run, Pallas kernels for 24% -> 24%
where the time goes in v11:
time: 100 us
  Pallas kernels  41.4 us (41%)
  waiting for transfers between devices  34.6 us (35%)
  starting transfers between devices  21 us (21%)
  local copies, waits for them, and re-layouts  2.79 us (3%)
    ppermute x25, waiting for transfers between devices, send_seq(): return lax.ppermute(value, 'seq', [(i, i ^ flip) for i in range(size)])  22 us
    ppermute x25, starting transfers between devices, send_seq(): return lax.ppermute(value, 'seq', [(i, i ^ flip) for i in range(size)])  15.6 us
    pallas_call x2, Pallas kernels, merge_call(): pl.pallas_call(functools.partial(merge_kernel, start, [len(source) for so...  14.3 us
    ppermute x3, waiting for transfers between devices, fast_local(): lax.ppermute(made[flip], 'pack', [(z, z ^ flip) for z in range(packs)])  12.6 us
    pallas_call x4, Pallas kernels, qkv_call(): pl.pallas_call(functools.partial(qkv_kernel, len(first), flip), in_specs=...  10 us
    pallas_call x2, Pallas kernels, attention_call(): pl.pallas_call(functools.partial(attention_kernel, start, first_owner, in...  8.85 us
    ppermute x3, starting transfers between devices, fast_local(): lax.ppermute(made[flip], 'pack', [(z, z ^ flip) for z in range(packs)])  5.47 us
    pallas_call x1, Pallas kernels, prepare_call(): pl.pallas_call(functools.partial(prepare_kernel, shards), in_specs=[pl.Bl...  5.1 us
  transfers between devices with their start and end apart: 28, of which 15 were waited for; matrix products, arithmetic and copies ran while one was open for 1% of the time, Pallas kernels for 24%

profile of v11, /device:TPU:0, one launch (start us, length us, event | category | flops | bytes accessed | tf_op | source)
XLA Modules:
  0.0 100.0 jit_solution(9456249166581094797)
XLA Ops:
  0.0 1.5 %payload.1.refs_0_ = bf16[192,1536]{1,0:T(8,128)(2,1)S(1)} custom-call(s32[1,192]{1,0:T(1,128)} %segments.1, s32[1,192]{1,0:T(1,128)} %rows.1, s32[1,192]{1,0:T(1,128)} %columns.1, s32[1,192]{1,0:T(1,128)} %mask.1, bf16[1408]{0:T(1024)(128)(2,1)} %embed.1, bf16[1,192,1408]{2,1,0:T(8,128)(2,1)} %patches.1), custom_call_target="tpu_custom_call" | custom-call | flops 270336 | bytes 1081344 | tf_op jit(solution)/shard_map/payload/pallas_call | solution.py:204
  2.0 2.6 %collective-permute-start = (bf16[192,1536]{1,0:T(8,128)(2,1)S(1)}, bf16[192,1536]{1,0:T(8,128)(2,1)S(1)}, u32[]{:S(2)}, u32[]{:S(2)}) collective-permute-start(bf16[192,1536]{1,0:T(8,128)(2,1)S(1)} %payload.1.refs_0_), channel_id=1, source_target_pairs={{0,8},{4,12},{8,0},{12,4},{16,24},{20,28},{24,16},{28,20},{1,9},{5... | collective-permute-start | bytes 1769480 | tf_op jit(solution)/shard_map/ppermute | solution.py:602
  4.6 1.5 %collective-permute-start.1 = (bf16[192,1536]{1,0:T(8,128)(2,1)S(1)}, bf16[192,1536]{1,0:T(8,128)(2,1)S(1)}, u32[]{:S(2)}, u32[]{:S(2)}) collective-permute-start(bf16[192,1536]{1,0:T(8,128)(2,1)S(1)} %payload.1.refs_0_), channel_id=1, source_target_pairs={{0,16},{4,20},{8,24},{12,28},{16,0},{20,4},{24,8},{28,12},{1,17},{... | collective-permute-start | bytes 1769480 | tf_op jit(solution)/shard_map/ppermute | solution.py:602
  6.1 0.7 concatenate.3.info.refs_13_
  8.9 5.1 %prepare.1 = (f32[1,1408]{1,0:T(1,128)S(1)}, f32[1,1408]{1,0:T(1,128)S(1)}, f32[1,448]{1,0:T(1,128)S(1)}, bf16[1536,1408]{1,0:T(8,128)(2,1)S(1)}, bf16[448,5632]...) custom-call(s32[15]{0:T(128)S(1)} %concatenate.3.info.refs_13_, bf16[1408,1408]{1,0:T(8,128)(2,1)} %out_weight.1, ...), custom_call_target="tpu_custom_call" | custom-call | flops 1141899264 | bytes 20996096 | tf_op jit(solution)/shard_map/prepare/pallas_call | solution.py:436
  14.0 2.5 %norm_qkv.4 = (bf16[1536,1408]{1,0:T(8,128)(2,1)S(1)}, bf16[1536,1024]{1,0:T(8,128)(2,1)S(1)}, bf16[1536,128]{1,0:T(8,128)(2,1)S(1)}) custom-call(s32[15]{0:T(128)S(1)} %concatenate.3.info.refs_13_, bf16[192,1536]{1,0:T(8,128)(2,1)S(1)} %payload.1.refs_0_, bf16[192,1536]{1,0:T(8,128)(2,1)S(1)} %collective-permute-done.2.refs_1_, ...), custom_call_target="tpu_custom_call" | custom-call | flops 2491416576 | bytes 6488064 | tf_op jit(solution)/shard_map/norm_qkv/pallas_call | solution.py:279
  16.5 1.9 %collective-permute-done.across_x.refs_0_ = bf16[192,1536]{1,0:T(8,128)(2,1)S(1)} collective-permute-done((bf16[192,1536]{1,0:T(8,128)(2,1)S(1)}, bf16[192,1536]{1,0:T(8,128)(2,1)S(1)}, u32[]{:S(2)}, u32[]{:S(2)}) %collective-permute-start) | collective-permute-done | bytes 589856 | tf_op jit(solution)/shard_map/ppermute | solution.py:602
  18.5 1.5 %collective-permute-done.1.across_y.refs_0_ = bf16[192,1536]{1,0:T(8,128)(2,1)S(1)} collective-permute-done((bf16[192,1536]{1,0:T(8,128)(2,1)S(1)}, bf16[192,1536]{1,0:T(8,128)(2,1)S(1)}, u32[]{:S(2)}, u32[]{:S(2)}) %collective-permute-start.1) | collective-permute-done | bytes 589856 | tf_op jit(solution)/shard_map/ppermute | solution.py:602
  20.5 1.6 %collective-permute-start.3 = (bf16[96,1536]{1,0:T(8,128)(2,1)S(1)}, bf16[96,1536]{1,0:T(8,128)(2,1)S(1)}, u32[]{:S(2)}, u32[]{:S(2)}) collective-permute-start(bf16[96,1536]{1,0:T(8,128)(2,1)S(1)} %get-tuple-element.51), channel_id=1, source_target_pairs={{0,16},{4,20},{8,24},{12,28},{16,0},{20,4},{24,8},{28,12},{1,17},{... | collective-permute-start | bytes 884744 | tf_op jit(solution)/shard_map/ppermute | solution.py:602
  22.6 2.5 %norm_qkv.5 = (bf16[1536,1408]{1,0:T(8,128)(2,1)S(1)}, bf16[1536,1024]{1,0:T(8,128)(2,1)S(1)}, bf16[1536,128]{1,0:T(8,128)(2,1)S(1)}) custom-call(s32[15]{0:T(128)S(1)} %concatenate.3.info.refs_13_, bf16[192,1536]{1,0:T(8,128)(2,1)S(1)} %collective-permute-done.across_x.refs_0_, ...), custom_call_target="tpu_custom_call", output_to_operand_aliasing={{0}: (6, {}), {1}: (7, {}), {2}: (8, {})} | custom-call | flops 2491416576 | bytes 6488064 | tf_op jit(solution)/shard_map/norm_qkv/pallas_call | solution.py:279
  25.2 2.5 %norm_qkv.6 = (bf16[1536,1408]{1,0:T(8,128)(2,1)S(1)}, bf16[1536,1024]{1,0:T(8,128)(2,1)S(1)}, bf16[1536,128]{1,0:T(8,128)(2,1)S(1)}) custom-call(s32[15]{0:T(128)S(1)} %concatenate.3.info.refs_13_, bf16[192,1536]{1,0:T(8,128)(2,1)S(1)} %collective-permute-done.1.across_y.refs_0_, ...), custom_call_target="tpu_custom_call", output_to_operand_aliasing={{0}: (6, {}), {1}: (7, {}), {2}: (8, {})} | custom-call | flops 2491416576 | bytes 6488064 | tf_op jit(solution)/shard_map/norm_qkv/pallas_call | solution.py:279
  27.7 1.8 %collective-permute-done.3.refs_0_ = bf16[96,1536]{1,0:T(8,128)(2,1)S(1)} collective-permute-done((bf16[96,1536]{1,0:T(8,128)(2,1)S(1)}, bf16[96,1536]{1,0:T(8,128)(2,1)S(1)}, u32[]{:S(2)}, u32[]{:S(2)}) %collective-permute-start.3) | collective-permute-done | bytes 294944 | tf_op jit(solution)/shard_map/ppermute | solution.py:602
  29.5 1.2 %collective-permute-done.4.refs_1_ = bf16[96,1536]{1,0:T(8,128)(2,1)S(1)} collective-permute-done((bf16[96,1536]{1,0:T(8,128)(2,1)S(1)}, bf16[96,1536]{1,0:T(8,128)(2,1)S(1)}, u32[]{:S(2)}, u32[]{:S(2)}) %collective-permute-start.4) | collective-permute-done | bytes 294944 | tf_op jit(solution)/shard_map/ppermute | solution.py:602
  31.2 1.1 %collective-permute-done.7.refs_2_ = bf16[96,1536]{1,0:T(8,128)(2,1)S(1)} collective-permute-done((bf16[96,1536]{1,0:T(8,128)(2,1)S(1)}, bf16[96,1536]{1,0:T(8,128)(2,1)S(1)}, u32[]{:S(2)}, u32[]{:S(2)}) %collective-permute-start.7) | collective-permute-done | bytes 294944 | tf_op jit(solution)/shard_map/ppermute | solution.py:602
  32.7 2.5 %norm_qkv.7 = (bf16[1536,1408]{1,0:T(8,128)(2,1)S(1)}, bf16[1536,1024]{1,0:T(8,128)(2,1)S(1)}, bf16[1536,128]{1,0:T(8,128)(2,1)S(1)}) custom-call(s32[15]{0:T(128)S(1)} %concatenate.3.info.refs_13_, bf16[96,1536]{1,0:T(8,128)(2,1)S(1)} %collective-permute-done.3.refs_0_, ...), custom_call_target="tpu_custom_call", output_to_operand_aliasing={{0}: (8, {}), {1}: (9, {}), {2}: (10, {})} | custom-call | flops 2491416576 | bytes 6488064 | tf_op jit(solution)/shard_map/norm_qkv/pallas_call | solution.py:279
  35.2 4.3 %attention.3 = (bf16[1152,128]{1,0:T(8,128)(2,1)S(1)}, bf16[16,128]{1,0:T(8,128)(2,1)S(1)}) custom-call(s32[15]{0:T(128)S(1)} %concatenate.3.info.refs_13_, bf16[1536,128]{1,0:T(8,128)(2,1)S(1)} %get-tuple-element.67.labels, bf16[1536,1024]{1,0:T(8,128)(2,1)S(1)} %get-tuple-element.68.block), custom_call_target="tpu_custom_call" | custom-call | flops 3019898880 | bytes 3145728 | tf_op jit(solution)/shard_map/attention/pallas_call | solution.py:382
  40.5 4.5 %attention.2.refs_5_ = bf16[1152,128]{1,0:T(8,128)(2,1)S(1)} custom-call(s32[15]{0:T(128)S(1)} %concatenate.3.info.refs_13_, bf16[1536,128]{1,0:T(8,128)(2,1)S(1)} %get-tuple-element.67.labels, bf16[1536,1024]{1,0:T(8,128)(2,1)S(1)} %get-tuple-element.68.block), custom_call_target="tpu_custom_call" | custom-call | flops 3019898880 | bytes 3145728 | tf_op jit(solution)/shard_map/attention/pallas_call | solution.py:382
  45.0 3.6 %collective-permute-done.10.across_x.refs_7_ = bf16[1152,128]{1,0:T(8,128)(2,1)S(1)} collective-permute-done((bf16[1152,128]{1,0:T(8,128)(2,1)S(1)}, bf16[1152,128]{1,0:T(8,128)(2,1)S(1)}, u32[]{:S(2)}, u32[]{:S(2)}) %collective-permute-start.10) | collective-permute-done | bytes 294944 | tf_op jit(solution)/shard_map/ppermute | solution.py:602
  48.9 1.5 %collective-permute-start.13 = (bf16[1152,128]{1,0:T(8,128)(2,1)S(1)}, bf16[1152,128]{1,0:T(8,128)(2,1)S(1)}, u32[]{:S(2)}, u32[]{:S(2)}) collective-permute-start(bf16[1152,128]{1,0:T(8,128)(2,1)S(1)} %attention.2.refs_5_), channel_id=1, source_target_pairs={{0,8},{4,12},{8,0},{12,4},{16,24},{20,28},{24,16},{28,20},{1,9},{5... | collective-permute-start | bytes 884744 | tf_op jit(solution)/shard_map/ppermute | solution.py:602
  51.4 1.7 %collective-permute-start.14 = (bf16[1152,128]{1,0:T(8,128)(2,1)S(1)}, bf16[1152,128]{1,0:T(8,128)(2,1)S(1)}, u32[]{:S(2)}, u32[]{:S(2)}) collective-permute-start(bf16[1152,128]{1,0:T(8,128)(2,1)S(1)} %attention.2.refs_5_), channel_id=1, source_target_pairs={{0,16},{4,20},{8,24},{12,28},{16,0},{20,4},{24,8},{28,12},{1,17},{... | collective-permute-start | bytes 884744 | tf_op jit(solution)/shard_map/ppermute | solution.py:602
  53.1 4.2 %collective-permute-done.15.refs_11_ = bf16[576,128]{1,0:T(8,128)(2,1)S(1)} collective-permute-done((bf16[576,128]{1,0:T(8,128)(2,1)S(1)}, bf16[576,128]{1,0:T(8,128)(2,1)S(1)}, u32[]{:S(2)}, u32[]{:S(2)}) %collective-permute-start.15) | collective-permute-done | bytes 147488 | tf_op jit(solution)/shard_map/ppermute | solution.py:602
  57.3 2.8 %collective-permute-done.16.refs_12_ = bf16[576,128]{1,0:T(8,128)(2,1)S(1)} collective-permute-done((bf16[576,128]{1,0:T(8,128)(2,1)S(1)}, bf16[576,128]{1,0:T(8,128)(2,1)S(1)}, u32[]{:S(2)}, u32[]{:S(2)}) %collective-permute-start.16) | collective-permute-done | bytes 147488 | tf_op jit(solution)/shard_map/ppermute | solution.py:602
  61.3 1.2 %collective-permute-start.19 = (bf16[1152,128]{1,0:T(8,128)(2,1)S(1)}, bf16[1152,128]{1,0:T(8,128)(2,1)S(1)}, u32[]{:S(2)}, u32[]{:S(2)}) collective-permute-start(bf16[1152,128]{1,0:T(8,128)(2,1)S(1)} %attention.2.refs_5_), channel_id=1, source_target_pairs={{0,24},{4,28},{8,16},{12,20},{16,8},{20,12},{24,0},{28,4},{1,25},{... | collective-permute-start | bytes 884744 | tf_op jit(solution)/shard_map/ppermute | solution.py:602
  63.1 6.6 %out_merge.2.refs_15_ = bf16[192,448]{1,0:T(8,128)(2,1)S(1)} custom-call(bf16[1536,1408]{1,0:T(8,128)(2,1)S(1)} %get-tuple-element.63.refs_0_, bf16[1536,1408]{1,0:T(8,128)(2,1)S(1)} %get-tuple-element.48.refs_1_, f32[1,1408]{1,0:T(1,128)S(1)} %get-tuple-element.64.refs_2_, bf16[448,5632]{1,0:T(8,128)(2,1)S(1)} %get-tuple-element.65.refs_3_, ...), custom_call_target="tpu_custom_call" | custom-call | flops 7059013632 | bytes 15499264 | tf_op jit(solution)/shard_map/out_merge/pallas_call | solution.py:546
  69.7 1.3 %collective-permute-done.19.refs_11_ = bf16[1152,128]{1,0:T(8,128)(2,1)S(1)} collective-permute-done((bf16[1152,128]{1,0:T(8,128)(2,1)S(1)}, bf16[1152,128]{1,0:T(8,128)(2,1)S(1)}, u32[]{:S(2)}, u32[]{:S(2)}) %collective-permute-start.19) | collective-permute-done | bytes 294944 | tf_op jit(solution)/shard_map/ppermute | solution.py:602
  71.0 1.6 %collective-permute-done.24.refs_12_ = bf16[1152,128]{1,0:T(8,128)(2,1)S(1)} collective-permute-done((bf16[1152,128]{1,0:T(8,128)(2,1)S(1)}, bf16[1152,128]{1,0:T(8,128)(2,1)S(1)}, u32[]{:S(2)}, u32[]{:S(2)}) %collective-permute-start.24) | collective-permute-done | bytes 294944 | tf_op jit(solution)/shard_map/ppermute | solution.py:602
  72.6 7.7 %out_merge.3 = (bf16[672,128]{1,0:T(8,128)(2,1)S(1)}, bf16[672,128]{1,0:T(8,128)(2,1)S(1)}, bf16[672,128]{1,0:T(8,128)(2,1)S(1)}, bf16[672,128]{1,0:T(8,128)(2,1)S(1)}) custom-call(bf16[1536,1408]{1,0:T(8,128)(2,1)S(1)} %get-tuple-element.63.refs_0_, bf16[1536,1408]{1,0:T(8,128)(2,1)S(1)} %get-tuple-element.48.refs_1_, ...), custom_call_target="tpu_custom_call" | custom-call | flops 7059013632 | bytes 15499264 | tf_op jit(solution)/shard_map/out_merge/pallas_call | solution.py:546
  80.3 1.6 %collective-permute-start.25 = (bf16[672,128]{1,0:T(8,128)(2,1)S(1)}, bf16[672,128]{1,0:T(8,128)(2,1)S(1)}, u32[]{:S(2)}, u32[]{:S(2)}) collective-permute-start(bf16[672,128]{1,0:T(8,128)(2,1)S(1)} %get-tuple-element.82), channel_id=1, source_target_pairs={{0,1},{1,0},{2,3},{3,2},{4,5},{5,4},{6,7},{7,6},{8,9},{9,8},{10,11... | collective-permute-start | bytes 516104 | tf_op jit(solution)/shard_map/ppermute | solution.py:764
  81.9 3.8 %collective-permute-start.26 = (bf16[672,128]{1,0:T(8,128)(2,1)S(1)}, bf16[672,128]{1,0:T(8,128)(2,1)S(1)}, u32[]{:S(2)}, u32[]{:S(2)}) collective-permute-start(bf16[672,128]{1,0:T(8,128)(2,1)S(1)} %get-tuple-element.83), channel_id=1, source_target_pairs={{0,2},{1,3},{2,0},{3,1},{4,6},{5,7},{6,4},{7,5},{8,10},{9,11},{10,... | collective-permute-start | bytes 516104 | tf_op jit(solution)/shard_map/ppermute | solution.py:764
  85.7 4.0 %collective-permute-done.25.refs_1_ = bf16[672,128]{1,0:T(8,128)(2,1)S(1)} collective-permute-done((bf16[672,128]{1,0:T(8,128)(2,1)S(1)}, bf16[672,128]{1,0:T(8,128)(2,1)S(1)}, u32[]{:S(2)}, u32[]{:S(2)}) %collective-permute-start.25) | collective-permute-done | bytes 172064 | tf_op jit(solution)/shard_map/ppermute | solution.py:764
  89.7 8.6 %collective-permute-done.26.refs_2_ = bf16[672,128]{1,0:T(8,128)(2,1)S(1)} collective-permute-done((bf16[672,128]{1,0:T(8,128)(2,1)S(1)}, bf16[672,128]{1,0:T(8,128)(2,1)S(1)}, u32[]{:S(2)}, u32[]{:S(2)}) %collective-permute-start.26) | collective-permute-done | bytes 172064 | tf_op jit(solution)/shard_map/ppermute | solution.py:764
  98.4 1.6 %place_rows.1 = bf16[4,192,448]{2,1,0:T(8,128)(2,1)} custom-call(s32[15]{0:T(128)S(1)} %concatenate.3.info.refs_13_, bf16[672,128]{1,0:T(8,128)(2,1)S(1)} %get-tuple-element.81.refs_0_, bf16[672,128]{1,0:T(8,128)(2,1)S(1)} %collective-permute-done.25.refs_1_, bf16[672,128]{1,0:T(8,128)(2,1)S(1)} %collective-permute-done.26.refs_2_, ...), custom_call_target="tpu_custom_call" | custom-call | bytes 1376256 | tf_op jit(solution)/shard_map/place_rows/pallas_call | solution.py:586
  (46 shorter events, 8.6 us)
Async XLA Ops:
  1.5 12.5 %collective-permute-start.2 = (bf16[192,1536]{1,0:T(8,128)(2,1)S(1)}, bf16[192,1536]{1,0:T(8,128)(2,1)S(1)}, u32[]{:S(2)}, u32[]{:S(2)}) collective-permute-start(bf16[192,1536]{1,0:T(8,128)(2,1)S(1)} %payload.1.refs_0_), channel_id=1, source_target_pairs={{0,4},{4,0},{8,12},{12,8},{16,20},{20,16},{24,28},{28,24},{1,5},{5... | collective-permute-start | bytes 1769480 | tf_op jit(solution)/shard_map/ppermute | solution.py:602
  2.0 16.5 %collective-permute-start = (bf16[192,1536]{1,0:T(8,128)(2,1)S(1)}, bf16[192,1536]{1,0:T(8,128)(2,1)S(1)}, u32[]{:S(2)}, u32[]{:S(2)}) collective-permute-start(bf16[192,1536]{1,0:T(8,128)(2,1)S(1)} %payload.1.refs_0_), channel_id=1, source_target_pairs={{0,8},{4,12},{8,0},{12,4},{16,24},{20,28},{24,16},{28,20},{1,9},{5... | collective-permute-start | bytes 1769480 | tf_op jit(solution)/shard_map/ppermute | solution.py:602
  4.6 15.4 %collective-permute-start.1 = (bf16[192,1536]{1,0:T(8,128)(2,1)S(1)}, bf16[192,1536]{1,0:T(8,128)(2,1)S(1)}, u32[]{:S(2)}, u32[]{:S(2)}) collective-permute-start(bf16[192,1536]{1,0:T(8,128)(2,1)S(1)} %payload.1.refs_0_), channel_id=1, source_target_pairs={{0,16},{4,20},{8,24},{12,28},{16,0},{20,4},{24,8},{28,12},{1,17},{... | collective-permute-start | bytes 1769480 | tf_op jit(solution)/shard_map/ppermute | solution.py:602
  6.8 0.7 copy-start.1
  7.5 0.7 copy-start.2
  8.2 0.7 copy-start.3
  8.9 5.1 %copy-start = (bf16[128,512]{1,0:T(8,128)(2,1)S(1)}, bf16[128,512]{1,0:T(8,128)(2,1)}, u32[]{:S(2)}) copy-start(bf16[128,512]{1,0:T(8,128)(2,1)} %constant.48.clone.refs_2_.refs_4_) | copy-start | bytes 393220
  20.0 2.7 %collective-permute-start.6 = (bf16[192,1536]{1,0:T(8,128)(2,1)S(1)}, bf16[192,1536]{1,0:T(8,128)(2,1)S(1)}, u32[]{:S(2)}, u32[]{:S(2)}) collective-permute-start(bf16[192,1536]{1,0:T(8,128)(2,1)S(1)} %collective-permute-done.across_x.refs_0_), channel_id=1, source_target_pairs={{0,4},{4,0},{8,12},{12,8},{16,20},{20,16},{24,28},{28,24},{1,5},{5... | collective-permute-start | bytes 1769480 | tf_op jit(solution)/shard_map/ppermute | solution.py:602
  20.0 5.2 %collective-permute-start.5 = (bf16[192,1536]{1,0:T(8,128)(2,1)S(1)}, bf16[192,1536]{1,0:T(8,128)(2,1)S(1)}, u32[]{:S(2)}, u32[]{:S(2)}) collective-permute-start(bf16[192,1536]{1,0:T(8,128)(2,1)S(1)} %collective-permute-done.1.across_y.refs_0_), channel_id=1, source_target_pairs={{0,4},{4,0},{8,12},{12,8},{16,20},{20,16},{24,28},{28,24},{1,5},{5... | collective-permute-start | bytes 1769480 | tf_op jit(solution)/shard_map/ppermute | solution.py:602
  20.5 9.0 %collective-permute-start.3 = (bf16[96,1536]{1,0:T(8,128)(2,1)S(1)}, bf16[96,1536]{1,0:T(8,128)(2,1)S(1)}, u32[]{:S(2)}, u32[]{:S(2)}) collective-permute-start(bf16[96,1536]{1,0:T(8,128)(2,1)S(1)} %get-tuple-element.51), channel_id=1, source_target_pairs={{0,16},{4,20},{8,24},{12,28},{16,0},{20,4},{24,8},{28,12},{1,17},{... | collective-permute-start | bytes 884744 | tf_op jit(solution)/shard_map/ppermute | solution.py:602
  22.1 8.6 %collective-permute-start.4 = (bf16[96,1536]{1,0:T(8,128)(2,1)S(1)}, bf16[96,1536]{1,0:T(8,128)(2,1)S(1)}, u32[]{:S(2)}, u32[]{:S(2)}) collective-permute-start(bf16[96,1536]{1,0:T(8,128)(2,1)S(1)} %get-tuple-element.52), channel_id=1, source_target_pairs={{0,8},{4,12},{8,0},{12,4},{16,24},{20,28},{24,16},{28,20},{1,9},{5... | collective-permute-start | bytes 884744 | tf_op jit(solution)/shard_map/ppermute | solution.py:602
  30.7 1.6 %collective-permute-start.7 = (bf16[96,1536]{1,0:T(8,128)(2,1)S(1)}, bf16[96,1536]{1,0:T(8,128)(2,1)S(1)}, u32[]{:S(2)}, u32[]{:S(2)}) collective-permute-start(bf16[96,1536]{1,0:T(8,128)(2,1)S(1)} %collective-permute-done.3.refs_0_), channel_id=1, source_target_pairs={{0,4},{4,0},{8,12},{12,8},{16,20},{20,16},{24,28},{28,24},{1,5},{5... | collective-permute-start | bytes 884744 | tf_op jit(solution)/shard_map/ppermute | solution.py:602
  30.7 2.0 %collective-permute-start.8 = (bf16[96,1536]{1,0:T(8,128)(2,1)S(1)}, bf16[96,1536]{1,0:T(8,128)(2,1)S(1)}, u32[]{:S(2)}, u32[]{:S(2)}) collective-permute-start(bf16[96,1536]{1,0:T(8,128)(2,1)S(1)} %collective-permute-done.4.refs_1_), channel_id=1, source_target_pairs={{0,4},{4,0},{8,12},{12,8},{16,20},{20,16},{24,28},{28,24},{1,5},{5... | collective-permute-start | bytes 884744 | tf_op jit(solution)/shard_map/ppermute | solution.py:602
  39.6 9.1 %collective-permute-start.10 = (bf16[1152,128]{1,0:T(8,128)(2,1)S(1)}, bf16[1152,128]{1,0:T(8,128)(2,1)S(1)}, u32[]{:S(2)}, u32[]{:S(2)}) collective-permute-start(bf16[1152,128]{1,0:T(8,128)(2,1)S(1)} %get-tuple-element.69.refs_5_), channel_id=1, source_target_pairs={{0,8},{4,12},{8,0},{12,4},{16,24},{20,28},{24,16},{28,20},{1,9},{5... | collective-permute-start | bytes 884744 | tf_op jit(solution)/shard_map/ppermute | solution.py:602
  40.2 8.8 %collective-permute-start.11 = (bf16[1152,128]{1,0:T(8,128)(2,1)S(1)}, bf16[1152,128]{1,0:T(8,128)(2,1)S(1)}, u32[]{:S(2)}, u32[]{:S(2)}) collective-permute-start(bf16[1152,128]{1,0:T(8,128)(2,1)S(1)} %get-tuple-element.69.refs_5_), channel_id=1, source_target_pairs={{0,16},{4,20},{8,24},{12,28},{16,0},{20,4},{24,8},{28,12},{1,17},{... | collective-permute-start | bytes 884744 | tf_op jit(solution)/shard_map/ppermute | solution.py:602
  40.5 8.4 %collective-permute-start.9 = (bf16[1152,128]{1,0:T(8,128)(2,1)S(1)}, bf16[1152,128]{1,0:T(8,128)(2,1)S(1)}, u32[]{:S(2)}, u32[]{:S(2)}) collective-permute-start(bf16[1152,128]{1,0:T(8,128)(2,1)S(1)} %get-tuple-element.69.refs_5_), channel_id=1, source_target_pairs={{0,4},{4,0},{8,12},{12,8},{16,20},{20,16},{24,28},{28,24},{1,5},{5... | collective-permute-start | bytes 884744 | tf_op jit(solution)/shard_map/ppermute | solution.py:602
  48.9 11.7 %collective-permute-start.13 = (bf16[1152,128]{1,0:T(8,128)(2,1)S(1)}, bf16[1152,128]{1,0:T(8,128)(2,1)S(1)}, u32[]{:S(2)}, u32[]{:S(2)}) collective-permute-start(bf16[1152,128]{1,0:T(8,128)(2,1)S(1)} %attention.2.refs_5_), channel_id=1, source_target_pairs={{0,8},{4,12},{8,0},{12,4},{16,24},{20,28},{24,16},{28,20},{1,9},{5... | collective-permute-start | bytes 884744 | tf_op jit(solution)/shard_map/ppermute | solution.py:602
  50.5 6.8 %collective-permute-start.15 = (bf16[576,128]{1,0:T(8,128)(2,1)S(1)}, bf16[576,128]{1,0:T(8,128)(2,1)S(1)}, u32[]{:S(2)}, u32[]{:S(2)}) collective-permute-start(bf16[576,128]{1,0:T(8,128)(2,1)S(1)} %get-tuple-element.73), channel_id=1, source_target_pairs={{0,16},{4,20},{8,24},{12,28},{16,0},{20,4},{24,8},{28,12},{1,17},{... | collective-permute-start | bytes 442376 | tf_op jit(solution)/shard_map/ppermute | solution.py:602
  51.0 9.1 %collective-permute-start.16 = (bf16[576,128]{1,0:T(8,128)(2,1)S(1)}, bf16[576,128]{1,0:T(8,128)(2,1)S(1)}, u32[]{:S(2)}, u32[]{:S(2)}) collective-permute-start(bf16[576,128]{1,0:T(8,128)(2,1)S(1)} %get-tuple-element.74), channel_id=1, source_target_pairs={{0,8},{4,12},{8,0},{12,4},{16,24},{20,28},{24,16},{28,20},{1,9},{5... | collective-permute-start | bytes 442376 | tf_op jit(solution)/shard_map/ppermute | solution.py:602
  51.4 9.9 %collective-permute-start.14 = (bf16[1152,128]{1,0:T(8,128)(2,1)S(1)}, bf16[1152,128]{1,0:T(8,128)(2,1)S(1)}, u32[]{:S(2)}, u32[]{:S(2)}) collective-permute-start(bf16[1152,128]{1,0:T(8,128)(2,1)S(1)} %attention.2.refs_5_), channel_id=1, source_target_pairs={{0,16},{4,20},{8,24},{12,28},{16,0},{20,4},{24,8},{28,12},{1,17},{... | collective-permute-start | bytes 884744 | tf_op jit(solution)/shard_map/ppermute | solution.py:602
  60.1 2.9 %collective-permute-start.20 = (bf16[1152,128]{1,0:T(8,128)(2,1)S(1)}, bf16[1152,128]{1,0:T(8,128)(2,1)S(1)}, u32[]{:S(2)}, u32[]{:S(2)}) collective-permute-start(bf16[1152,128]{1,0:T(8,128)(2,1)S(1)} %collective-permute-done.10.across_x.refs_7_), channel_id=1, source_target_pairs={{0,4},{4,0},{8,12},{12,8},{16,20},{20,16},{24,28},{28,24},{1,5},{5... | collective-permute-start | bytes 884744 | tf_op jit(solution)/shard_map/ppermute | solution.py:602
  60.1 3.0 %collective-permute-start.21 = (bf16[1152,128]{1,0:T(8,128)(2,1)S(1)}, bf16[1152,128]{1,0:T(8,128)(2,1)S(1)}, u32[]{:S(2)}, u32[]{:S(2)}) collective-permute-start(bf16[1152,128]{1,0:T(8,128)(2,1)S(1)} %collective-permute-done.11.across_y.refs_9_), channel_id=1, source_target_pairs={{0,4},{4,0},{8,12},{12,8},{16,20},{20,16},{24,28},{28,24},{1,5},{5... | collective-permute-start | bytes 884744 | tf_op jit(solution)/shard_map/ppermute | solution.py:602
  60.6 1.9 %collective-permute-start.22 = (bf16[576,128]{1,0:T(8,128)(2,1)S(1)}, bf16[576,128]{1,0:T(8,128)(2,1)S(1)}, u32[]{:S(2)}, u32[]{:S(2)}) collective-permute-start(bf16[576,128]{1,0:T(8,128)(2,1)S(1)} %collective-permute-done.15.refs_11_), channel_id=1, source_target_pairs={{0,4},{4,0},{8,12},{12,8},{16,20},{20,16},{24,28},{28,24},{1,5},{5... | collective-permute-start | bytes 442376 | tf_op jit(solution)/shard_map/ppermute | solution.py:602
  60.6 1.9 %collective-permute-start.23 = (bf16[576,128]{1,0:T(8,128)(2,1)S(1)}, bf16[576,128]{1,0:T(8,128)(2,1)S(1)}, u32[]{:S(2)}, u32[]{:S(2)}) collective-permute-start(bf16[576,128]{1,0:T(8,128)(2,1)S(1)} %collective-permute-done.16.refs_12_), channel_id=1, source_target_pairs={{0,4},{4,0},{8,12},{12,8},{16,20},{20,16},{24,28},{28,24},{1,5},{5... | collective-permute-start | bytes 442376 | tf_op jit(solution)/shard_map/ppermute | solution.py:602
  61.3 9.7 %collective-permute-start.19 = (bf16[1152,128]{1,0:T(8,128)(2,1)S(1)}, bf16[1152,128]{1,0:T(8,128)(2,1)S(1)}, u32[]{:S(2)}, u32[]{:S(2)}) collective-permute-start(bf16[1152,128]{1,0:T(8,128)(2,1)S(1)} %attention.2.refs_5_), channel_id=1, source_target_pairs={{0,24},{4,28},{8,16},{12,20},{16,8},{20,12},{24,0},{28,4},{1,25},{... | collective-permute-start | bytes 884744 | tf_op jit(solution)/shard_map/ppermute | solution.py:602
  62.5 8.5 %collective-permute-start.12 = (bf16[1152,128]{1,0:T(8,128)(2,1)S(1)}, bf16[1152,128]{1,0:T(8,128)(2,1)S(1)}, u32[]{:S(2)}, u32[]{:S(2)}) collective-permute-start(bf16[1152,128]{1,0:T(8,128)(2,1)S(1)} %attention.2.refs_5_), channel_id=1, source_target_pairs={{0,4},{4,0},{8,12},{12,8},{16,20},{20,16},{24,28},{28,24},{1,5},{5... | collective-permute-start | bytes 884744 | tf_op jit(solution)/shard_map/ppermute | solution.py:602
  62.5 8.5 %collective-permute-start.17 = (bf16[1152,128]{1,0:T(8,128)(2,1)S(1)}, bf16[1152,128]{1,0:T(8,128)(2,1)S(1)}, u32[]{:S(2)}, u32[]{:S(2)}) collective-permute-start(bf16[1152,128]{1,0:T(8,128)(2,1)S(1)} %collective-permute-done.13.refs_7_), channel_id=1, source_target_pairs={{0,4},{4,0},{8,12},{12,8},{16,20},{20,16},{24,28},{28,24},{1,5},{5... | collective-permute-start | bytes 884744 | tf_op jit(solution)/shard_map/ppermute | solution.py:602
  63.0 8.0 %collective-permute-start.18 = (bf16[1152,128]{1,0:T(8,128)(2,1)S(1)}, bf16[1152,128]{1,0:T(8,128)(2,1)S(1)}, u32[]{:S(2)}, u32[]{:S(2)}) collective-permute-start(bf16[1152,128]{1,0:T(8,128)(2,1)S(1)} %collective-permute-done.14.refs_9_), channel_id=1, source_target_pairs={{0,4},{4,0},{8,12},{12,8},{16,20},{20,16},{24,28},{28,24},{1,5},{5... | collective-permute-start | bytes 884744 | tf_op jit(solution)/shard_map/ppermute | solution.py:602
  71.0 1.6 %collective-permute-start.24 = (bf16[1152,128]{1,0:T(8,128)(2,1)S(1)}, bf16[1152,128]{1,0:T(8,128)(2,1)S(1)}, u32[]{:S(2)}, u32[]{:S(2)}) collective-permute-start(bf16[1152,128]{1,0:T(8,128)(2,1)S(1)} %collective-permute-done.19.refs_11_), channel_id=1, source_target_pairs={{0,4},{4,0},{8,12},{12,8},{16,20},{20,16},{24,28},{28,24},{1,5},{5... | collective-permute-start | bytes 884744 | tf_op jit(solution)/shard_map/ppermute | solution.py:602
  80.3 9.4 %collective-permute-start.25 = (bf16[672,128]{1,0:T(8,128)(2,1)S(1)}, bf16[672,128]{1,0:T(8,128)(2,1)S(1)}, u32[]{:S(2)}, u32[]{:S(2)}) collective-permute-start(bf16[672,128]{1,0:T(8,128)(2,1)S(1)} %get-tuple-element.82), channel_id=1, source_target_pairs={{0,1},{1,0},{2,3},{3,2},{4,5},{5,4},{6,7},{7,6},{8,9},{9,8},{10,11... | collective-permute-start | bytes 516104 | tf_op jit(solution)/shard_map/ppermute | solution.py:764
  81.9 16.4 %collective-permute-start.26 = (bf16[672,128]{1,0:T(8,128)(2,1)S(1)}, bf16[672,128]{1,0:T(8,128)(2,1)S(1)}, u32[]{:S(2)}, u32[]{:S(2)}) collective-permute-start(bf16[672,128]{1,0:T(8,128)(2,1)S(1)} %get-tuple-element.83), channel_id=1, source_target_pairs={{0,2},{1,3},{2,0},{3,1},{4,6},{5,7},{6,4},{7,5},{8,10},{9,11},{10,... | collective-permute-start | bytes 516104 | tf_op jit(solution)/shard_map/ppermute | solution.py:764
  85.7 12.6 %collective-permute-start.27 = (bf16[672,128]{1,0:T(8,128)(2,1)S(1)}, bf16[672,128]{1,0:T(8,128)(2,1)S(1)}, u32[]{:S(2)}, u32[]{:S(2)}) collective-permute-start(bf16[672,128]{1,0:T(8,128)(2,1)S(1)} %get-tuple-element.84), channel_id=1, source_target_pairs={{0,3},{1,2},{2,1},{3,0},{4,7},{5,6},{6,5},{7,4},{8,11},{9,10},{10,... | collective-permute-start | bytes 516104 | tf_op jit(solution)/shard_map/ppermute | solution.py:764

commit v12 on v11

--- a/solution.py
+++ b/solution.py
@@ -725,41 +725,27 @@
     buffers = project(3, far, [send_seq(one, 1) for one in far], buffers)
     inputs, block, labels = buffers
 
-    starts = [sum(CHUNKS[:number]) for number in range(len(CHUNKS))]
-    attended, note = [], None
-    for start, rows in zip(starts, CHUNKS):
-        made = attention_call(start, rows, IDS + shards, info, labels, block, note is None)
-        note = made[1] if note is None else note
-        value = made[0]
-        if attended:
-            (value,) = after([value], *attended[-1][1])
-        attended.append((value, near_shards(value)))
-    latest = attended[-1][0]
     most = 2 * (total // 4) // images
-    projected, moving = [], []
-    for own, (own_swap, across_x, across_y) in attended:
-        previous = moving[-1][-1] if moving else ()
-        across_x, across_y = after([across_x, across_y], latest, *previous)
-        swapped = [across_x, across_y]
-        if len(moving) < len(attended) - 1:
-            far = far_shards(across_x, across_y)
-            swapped = after(swapped, *far)
-        else:
-            far = [send_seq(own, 6)]
-        swap_x, swap_y = (send_seq(one, 1) for one in swapped)
-        moving.append((own, own_swap, across_x, swap_x, across_y, swap_y, far))
-    for number, (start, rows) in enumerate(zip(starts, CHUNKS)):
-        *near, far = moving[number]
-        if projected:
-            far = after(far, projected[-1])
-        sources = [[one] for one in near] + [far, [send_seq(one, 1) for one in far]]
-        route = ()
-        if number == len(CHUNKS) - 1:
-            route = (info, most, note, *projected)
-        made = merge_call(
-            start, rows, sources, inputs, ordered, merge_gain_row, merge_rows, bias, packs, route
-        )
-        projected.append(made[0])
+    first_rows, last_rows = CHUNKS
+    attend = functools.partial(attention_call, first_owner=IDS + shards, info=info)
+    own, note = attend(0, first_rows, labels=labels, block=block, noted=True)
+    own_swap, across_x, across_y = near_shards(own)
+    labels, block = after([labels, block], own)
+    (late,) = attend(first_rows, last_rows, labels=labels, block=block, noted=False)
+    across_x, across_y = after([across_x, across_y], late)
+    halves = halves_call(across_x, across_y)
+    far = [send_seq(halves[0], 4), send_seq(halves[1], 2)]
+    (late,) = after([late], *halves)
+    late_shares = [late] + [send_seq(late, flip) for flip in (2, 4, 6)]
+    near = [send_seq(one, 1) for one in after([across_x, across_y], *far)]
+    merge = lambda start, rows, sources, route: merge_call(
+        start, rows, sources, inputs, ordered, merge_gain_row, merge_rows, bias, packs, route
+    )
+    sources = [[own], [own_swap], [across_x], near[:1], [across_y], near[1:], far]
+    (projected,) = merge(0, first_rows, sources + [[send_seq(one, 1) for one in far]], ())
+    late_shares[3:] = after(late_shares[3:], projected)
+    sources = [[one] for share in late_shares for one in (share, send_seq(share, 1))]
+    made = merge(first_rows, last_rows, sources, (info, most, note, projected))
     blocks = [made[0]] + [
         lax.ppermute(made[flip], "pack", [(z, z ^ flip) for z in range(packs)])
         for flip in range(1, packs)

time: 100 us -> 101 us (1.010)
  waiting for transfers between devices: 34.6 us -> 36.2 us
    ppermute x25, waiting for transfers between devices: 22 us -> 23.6 us  [send_seq(): return lax.ppermute(value, 'seq', [(i, i ^ flip) for i in range(size)])]
  transfers between devices with their start and end apart: 28 -> 28, of which waited for: 15 -> 16; matrix products, arithmetic and copies ran while one was open for 1% -> 1% of each run, Pallas kernels for 24% -> 24%
where the time goes in v12:
time: 101 us
  Pallas kernels  41.4 us (41%)
  waiting for transfers between devices  36.2 us (36%)
  starting transfers between devices  20.1 us (20%)
  local copies, waits for them, and re-layouts  2.79 us (3%)
    ppermute x25, waiting for transfers between devices, send_seq(): return lax.ppermute(value, 'seq', [(i, i ^ flip) for i in range(size)])  23.6 us
    ppermute x25, starting transfers between devices, send_seq(): return lax.ppermute(value, 'seq', [(i, i ^ flip) for i in range(size)])  14.6 us
    pallas_call x2, Pallas kernels, merge_call(): pl.pallas_call(functools.partial(merge_kernel, start, [len(source) for so...  14.3 us
    ppermute x3, waiting for transfers between devices, fast_local(): lax.ppermute(made[flip], 'pack', [(z, z ^ flip) for z in range(packs)])  12.6 us
    pallas_call x4, Pallas kernels, qkv_call(): pl.pallas_call(functools.partial(qkv_kernel, len(first), flip), in_specs=...  10 us
    pallas_call x2, Pallas kernels, attention_call(): pl.pallas_call(functools.partial(attention_kernel, start, first_owner, in...  8.85 us
    ppermute x3, starting transfers between devices, fast_local(): lax.ppermute(made[flip], 'pack', [(z, z ^ flip) for z in range(packs)])  5.47 us
    pallas_call x1, Pallas kernels, prepare_call(): pl.pallas_call(functools.partial(prepare_kernel, shards), in_specs=[pl.Bl...  5.1 us
  transfers between devices with their start and end apart: 28, of which 16 were waited for; matrix products, arithmetic and copies ran while one was open for 1% of the time, Pallas kernels for 24%

profile of v12, /device:TPU:0, one launch (start us, length us, event | category | flops | bytes accessed | tf_op | source)
XLA Modules:
  0.0 100.6 jit_solution(3363592188134556287)
XLA Ops:
  0.0 1.5 %payload.1.refs_0_ = bf16[192,1536]{1,0:T(8,128)(2,1)S(1)} custom-call(s32[1,192]{1,0:T(1,128)} %segments.1, s32[1,192]{1,0:T(1,128)} %rows.1, s32[1,192]{1,0:T(1,128)} %columns.1, s32[1,192]{1,0:T(1,128)} %mask.1, bf16[1408]{0:T(1024)(128)(2,1)} %embed.1, bf16[1,192,1408]{2,1,0:T(8,128)(2,1)} %patches.1), custom_call_target="tpu_custom_call" | custom-call | flops 270336 | bytes 1081344 | tf_op jit(solution)/shard_map/payload/pallas_call | solution.py:204
  2.0 2.6 %collective-permute-start = (bf16[192,1536]{1,0:T(8,128)(2,1)S(1)}, bf16[192,1536]{1,0:T(8,128)(2,1)S(1)}, u32[]{:S(2)}, u32[]{:S(2)}) collective-permute-start(bf16[192,1536]{1,0:T(8,128)(2,1)S(1)} %payload.1.refs_0_), channel_id=1, source_target_pairs={{0,8},{4,12},{8,0},{12,4},{16,24},{20,28},{24,16},{28,20},{1,9},{5... | collective-permute-start | bytes 1769480 | tf_op jit(solution)/shard_map/ppermute | solution.py:602
  4.6 1.5 %collective-permute-start.1 = (bf16[192,1536]{1,0:T(8,128)(2,1)S(1)}, bf16[192,1536]{1,0:T(8,128)(2,1)S(1)}, u32[]{:S(2)}, u32[]{:S(2)}) collective-permute-start(bf16[192,1536]{1,0:T(8,128)(2,1)S(1)} %payload.1.refs_0_), channel_id=1, source_target_pairs={{0,16},{4,20},{8,24},{12,28},{16,0},{20,4},{24,8},{28,12},{1,17},{... | collective-permute-start | bytes 1769480 | tf_op jit(solution)/shard_map/ppermute | solution.py:602
  6.1 0.7 concatenate.3.info.refs_13_
  8.9 5.1 %prepare.1 = (f32[1,1408]{1,0:T(1,128)S(1)}, f32[1,1408]{1,0:T(1,128)S(1)}, f32[1,448]{1,0:T(1,128)S(1)}, bf16[1536,1408]{1,0:T(8,128)(2,1)S(1)}, bf16[448,5632]...) custom-call(s32[15]{0:T(128)S(1)} %concatenate.3.info.refs_13_, bf16[1408,1408]{1,0:T(8,128)(2,1)} %out_weight.1, ...), custom_call_target="tpu_custom_call" | custom-call | flops 1141899264 | bytes 20996096 | tf_op jit(solution)/shard_map/prepare/pallas_call | solution.py:436
  14.0 2.5 %norm_qkv.4 = (bf16[1536,1408]{1,0:T(8,128)(2,1)S(1)}, bf16[1536,1024]{1,0:T(8,128)(2,1)S(1)}, bf16[1536,128]{1,0:T(8,128)(2,1)S(1)}) custom-call(s32[15]{0:T(128)S(1)} %concatenate.3.info.refs_13_, bf16[192,1536]{1,0:T(8,128)(2,1)S(1)} %payload.1.refs_0_, bf16[192,1536]{1,0:T(8,128)(2,1)S(1)} %collective-permute-done.2.refs_1_, ...), custom_call_target="tpu_custom_call" | custom-call | flops 2491416576 | bytes 6488064 | tf_op jit(solution)/shard_map/norm_qkv/pallas_call | solution.py:279
  16.5 1.9 %collective-permute-done.across_x.refs_0_ = bf16[192,1536]{1,0:T(8,128)(2,1)S(1)} collective-permute-done((bf16[192,1536]{1,0:T(8,128)(2,1)S(1)}, bf16[192,1536]{1,0:T(8,128)(2,1)S(1)}, u32[]{:S(2)}, u32[]{:S(2)}) %collective-permute-start) | collective-permute-done | bytes 589856 | tf_op jit(solution)/shard_map/ppermute | solution.py:602
  18.5 1.5 %collective-permute-done.1.across_y.refs_0_ = bf16[192,1536]{1,0:T(8,128)(2,1)S(1)} collective-permute-done((bf16[192,1536]{1,0:T(8,128)(2,1)S(1)}, bf16[192,1536]{1,0:T(8,128)(2,1)S(1)}, u32[]{:S(2)}, u32[]{:S(2)}) %collective-permute-start.1) | collective-permute-done | bytes 589856 | tf_op jit(solution)/shard_map/ppermute | solution.py:602
  20.5 1.6 %collective-permute-start.3 = (bf16[96,1536]{1,0:T(8,128)(2,1)S(1)}, bf16[96,1536]{1,0:T(8,128)(2,1)S(1)}, u32[]{:S(2)}, u32[]{:S(2)}) collective-permute-start(bf16[96,1536]{1,0:T(8,128)(2,1)S(1)} %get-tuple-element.51), channel_id=1, source_target_pairs={{0,16},{4,20},{8,24},{12,28},{16,0},{20,4},{24,8},{28,12},{1,17},{... | collective-permute-start | bytes 884744 | tf_op jit(solution)/shard_map/ppermute | solution.py:602
  22.6 2.5 %norm_qkv.5 = (bf16[1536,1408]{1,0:T(8,128)(2,1)S(1)}, bf16[1536,1024]{1,0:T(8,128)(2,1)S(1)}, bf16[1536,128]{1,0:T(8,128)(2,1)S(1)}) custom-call(s32[15]{0:T(128)S(1)} %concatenate.3.info.refs_13_, bf16[192,1536]{1,0:T(8,128)(2,1)S(1)} %collective-permute-done.across_x.refs_0_, ...), custom_call_target="tpu_custom_call", output_to_operand_aliasing={{0}: (6, {}), {1}: (7, {}), {2}: (8, {})} | custom-call | flops 2491416576 | bytes 6488064 | tf_op jit(solution)/shard_map/norm_qkv/pallas_call | solution.py:279
  25.2 2.5 %norm_qkv.6 = (bf16[1536,1408]{1,0:T(8,128)(2,1)S(1)}, bf16[1536,1024]{1,0:T(8,128)(2,1)S(1)}, bf16[1536,128]{1,0:T(8,128)(2,1)S(1)}) custom-call(s32[15]{0:T(128)S(1)} %concatenate.3.info.refs_13_, bf16[192,1536]{1,0:T(8,128)(2,1)S(1)} %collective-permute-done.1.across_y.refs_0_, ...), custom_call_target="tpu_custom_call", output_to_operand_aliasing={{0}: (6, {}), {1}: (7, {}), {2}: (8, {})} | custom-call | flops 2491416576 | bytes 6488064 | tf_op jit(solution)/shard_map/norm_qkv/pallas_call | solution.py:279
  27.7 1.8 %collective-permute-done.3.refs_0_ = bf16[96,1536]{1,0:T(8,128)(2,1)S(1)} collective-permute-done((bf16[96,1536]{1,0:T(8,128)(2,1)S(1)}, bf16[96,1536]{1,0:T(8,128)(2,1)S(1)}, u32[]{:S(2)}, u32[]{:S(2)}) %collective-permute-start.3) | collective-permute-done | bytes 294944 | tf_op jit(solution)/shard_map/ppermute | solution.py:602
  29.5 1.2 %collective-permute-done.4.refs_1_ = bf16[96,1536]{1,0:T(8,128)(2,1)S(1)} collective-permute-done((bf16[96,1536]{1,0:T(8,128)(2,1)S(1)}, bf16[96,1536]{1,0:T(8,128)(2,1)S(1)}, u32[]{:S(2)}, u32[]{:S(2)}) %collective-permute-start.4) | collective-permute-done | bytes 294944 | tf_op jit(solution)/shard_map/ppermute | solution.py:602
  31.2 1.1 %collective-permute-done.7.refs_2_ = bf16[96,1536]{1,0:T(8,128)(2,1)S(1)} collective-permute-done((bf16[96,1536]{1,0:T(8,128)(2,1)S(1)}, bf16[96,1536]{1,0:T(8,128)(2,1)S(1)}, u32[]{:S(2)}, u32[]{:S(2)}) %collective-permute-start.7) | collective-permute-done | bytes 294944 | tf_op jit(solution)/shard_map/ppermute | solution.py:602
  32.7 2.5 %norm_qkv.7 = (bf16[1536,1408]{1,0:T(8,128)(2,1)S(1)}, bf16[1536,1024]{1,0:T(8,128)(2,1)S(1)}, bf16[1536,128]{1,0:T(8,128)(2,1)S(1)}) custom-call(s32[15]{0:T(128)S(1)} %concatenate.3.info.refs_13_, bf16[96,1536]{1,0:T(8,128)(2,1)S(1)} %collective-permute-done.3.refs_0_, ...), custom_call_target="tpu_custom_call", output_to_operand_aliasing={{0}: (8, {}), {1}: (9, {}), {2}: (10, {})} | custom-call | flops 2491416576 | bytes 6488064 | tf_op jit(solution)/shard_map/norm_qkv/pallas_call | solution.py:279
  35.2 4.3 %attention.2 = (bf16[1152,128]{1,0:T(8,128)(2,1)S(1)}, bf16[16,128]{1,0:T(8,128)(2,1)S(1)}) custom-call(s32[15]{0:T(128)S(1)} %concatenate.3.info.refs_13_, bf16[1536,128]{1,0:T(8,128)(2,1)S(1)} %get-tuple-element.70.labels, bf16[1536,1024]{1,0:T(8,128)(2,1)S(1)} %get-tuple-element.71.block), custom_call_target="tpu_custom_call" | custom-call | flops 3019898880 | bytes 3145728 | tf_op jit(solution)/shard_map/attention/pallas_call | solution.py:382
  40.5 4.5 %attention.3.refs_5_ = bf16[1152,128]{1,0:T(8,128)(2,1)S(1)} custom-call(s32[15]{0:T(128)S(1)} %concatenate.3.info.refs_13_, bf16[1536,128]{1,0:T(8,128)(2,1)S(1)} %get-tuple-element.70.labels, bf16[1536,1024]{1,0:T(8,128)(2,1)S(1)} %get-tuple-element.71.block), custom_call_target="tpu_custom_call" | custom-call | flops 3019898880 | bytes 3145728 | tf_op jit(solution)/shard_map/attention/pallas_call | solution.py:382
  45.0 3.6 %collective-permute-done.10.across_y.refs_9_ = bf16[1152,128]{1,0:T(8,128)(2,1)S(1)} collective-permute-done((bf16[1152,128]{1,0:T(8,128)(2,1)S(1)}, bf16[1152,128]{1,0:T(8,128)(2,1)S(1)}, u32[]{:S(2)}, u32[]{:S(2)}) %collective-permute-start.10) | collective-permute-done | bytes 294944 | tf_op jit(solution)/shard_map/ppermute | solution.py:602
  48.9 1.6 %collective-permute-start.18 = (bf16[576,128]{1,0:T(8,128)(2,1)S(1)}, bf16[576,128]{1,0:T(8,128)(2,1)S(1)}, u32[]{:S(2)}, u32[]{:S(2)}) collective-permute-start(bf16[576,128]{1,0:T(8,128)(2,1)S(1)} %get-tuple-element.74), channel_id=1, source_target_pairs={{0,16},{4,20},{8,24},{12,28},{16,0},{20,4},{24,8},{28,12},{1,17},{... | collective-permute-start | bytes 442376 | tf_op jit(solution)/shard_map/ppermute | solution.py:602
  51.1 1.5 %collective-permute-start.12 = (bf16[1152,128]{1,0:T(8,128)(2,1)S(1)}, bf16[1152,128]{1,0:T(8,128)(2,1)S(1)}, u32[]{:S(2)}, u32[]{:S(2)}) collective-permute-start(bf16[1152,128]{1,0:T(8,128)(2,1)S(1)} %attention.3.refs_5_), channel_id=1, source_target_pairs={{0,8},{4,12},{8,0},{12,4},{16,24},{20,28},{24,16},{28,20},{1,9},{5... | collective-permute-start | bytes 884744 | tf_op jit(solution)/shard_map/ppermute | solution.py:602
  53.1 2.0 %collective-permute-done.18.refs_11_ = bf16[576,128]{1,0:T(8,128)(2,1)S(1)} collective-permute-done((bf16[576,128]{1,0:T(8,128)(2,1)S(1)}, bf16[576,128]{1,0:T(8,128)(2,1)S(1)}, u32[]{:S(2)}, u32[]{:S(2)}) %collective-permute-start.18) | collective-permute-done | bytes 147488 | tf_op jit(solution)/shard_map/ppermute | solution.py:602
  55.0 2.3 %collective-permute-done.19.refs_12_ = bf16[576,128]{1,0:T(8,128)(2,1)S(1)} collective-permute-done((bf16[576,128]{1,0:T(8,128)(2,1)S(1)}, bf16[576,128]{1,0:T(8,128)(2,1)S(1)}, u32[]{:S(2)}, u32[]{:S(2)}) %collective-permute-start.19) | collective-permute-done | bytes 147488 | tf_op jit(solution)/shard_map/ppermute | solution.py:602
  57.8 3.5 %collective-permute-done.12.refs_7_ = bf16[1152,128]{1,0:T(8,128)(2,1)S(1)} collective-permute-done((bf16[1152,128]{1,0:T(8,128)(2,1)S(1)}, bf16[1152,128]{1,0:T(8,128)(2,1)S(1)}, u32[]{:S(2)}, u32[]{:S(2)}) %collective-permute-start.12) | collective-permute-done | bytes 294944 | tf_op jit(solution)/shard_map/ppermute | solution.py:602
  63.2 6.6 %out_merge.2.refs_15_ = bf16[192,448]{1,0:T(8,128)(2,1)S(1)} custom-call(bf16[1536,1408]{1,0:T(8,128)(2,1)S(1)} %get-tuple-element.63.refs_0_, bf16[1536,1408]{1,0:T(8,128)(2,1)S(1)} %get-tuple-element.48.refs_1_, f32[1,1408]{1,0:T(1,128)S(1)} %get-tuple-element.64.refs_2_, bf16[448,5632]{1,0:T(8,128)(2,1)S(1)} %get-tuple-element.65.refs_3_, ...), custom_call_target="tpu_custom_call" | custom-call | flops 7059013632 | bytes 15499264 | tf_op jit(solution)/shard_map/out_merge/pallas_call | solution.py:546
  69.8 1.9 %collective-permute-done.16.refs_11_ = bf16[1152,128]{1,0:T(8,128)(2,1)S(1)} collective-permute-done((bf16[1152,128]{1,0:T(8,128)(2,1)S(1)}, bf16[1152,128]{1,0:T(8,128)(2,1)S(1)}, u32[]{:S(2)}, u32[]{:S(2)}) %collective-permute-start.16) | collective-permute-done | bytes 294944 | tf_op jit(solution)/shard_map/ppermute | solution.py:602
  71.7 1.6 %collective-permute-done.24.refs_12_ = bf16[1152,128]{1,0:T(8,128)(2,1)S(1)} collective-permute-done((bf16[1152,128]{1,0:T(8,128)(2,1)S(1)}, bf16[1152,128]{1,0:T(8,128)(2,1)S(1)}, u32[]{:S(2)}, u32[]{:S(2)}) %collective-permute-start.24) | collective-permute-done | bytes 294944 | tf_op jit(solution)/shard_map/ppermute | solution.py:602
  73.2 7.7 %out_merge.3 = (bf16[672,128]{1,0:T(8,128)(2,1)S(1)}, bf16[672,128]{1,0:T(8,128)(2,1)S(1)}, bf16[672,128]{1,0:T(8,128)(2,1)S(1)}, bf16[672,128]{1,0:T(8,128)(2,1)S(1)}) custom-call(bf16[1536,1408]{1,0:T(8,128)(2,1)S(1)} %get-tuple-element.63.refs_0_, bf16[1536,1408]{1,0:T(8,128)(2,1)S(1)} %get-tuple-element.48.refs_1_, ...), custom_call_target="tpu_custom_call" | custom-call | flops 7059013632 | bytes 15499264 | tf_op jit(solution)/shard_map/out_merge/pallas_call | solution.py:546
  80.9 1.6 %collective-permute-start.25 = (bf16[672,128]{1,0:T(8,128)(2,1)S(1)}, bf16[672,128]{1,0:T(8,128)(2,1)S(1)}, u32[]{:S(2)}, u32[]{:S(2)}) collective-permute-start(bf16[672,128]{1,0:T(8,128)(2,1)S(1)} %get-tuple-element.82), channel_id=1, source_target_pairs={{0,1},{1,0},{2,3},{3,2},{4,5},{5,4},{6,7},{7,6},{8,9},{9,8},{10,11... | collective-permute-start | bytes 516104 | tf_op jit(solution)/shard_map/ppermute | solution.py:750
  82.6 3.8 %collective-permute-start.26 = (bf16[672,128]{1,0:T(8,128)(2,1)S(1)}, bf16[672,128]{1,0:T(8,128)(2,1)S(1)}, u32[]{:S(2)}, u32[]{:S(2)}) collective-permute-start(bf16[672,128]{1,0:T(8,128)(2,1)S(1)} %get-tuple-element.83), channel_id=1, source_target_pairs={{0,2},{1,3},{2,0},{3,1},{4,6},{5,7},{6,4},{7,5},{8,10},{9,11},{10,... | collective-permute-start | bytes 516104 | tf_op jit(solution)/shard_map/ppermute | solution.py:750
  86.4 3.9 %collective-permute-done.25.refs_1_ = bf16[672,128]{1,0:T(8,128)(2,1)S(1)} collective-permute-done((bf16[672,128]{1,0:T(8,128)(2,1)S(1)}, bf16[672,128]{1,0:T(8,128)(2,1)S(1)}, u32[]{:S(2)}, u32[]{:S(2)}) %collective-permute-start.25) | collective-permute-done | bytes 172064 | tf_op jit(solution)/shard_map/ppermute | solution.py:750
  90.3 8.7 %collective-permute-done.26.refs_2_ = bf16[672,128]{1,0:T(8,128)(2,1)S(1)} collective-permute-done((bf16[672,128]{1,0:T(8,128)(2,1)S(1)}, bf16[672,128]{1,0:T(8,128)(2,1)S(1)}, u32[]{:S(2)}, u32[]{:S(2)}) %collective-permute-start.26) | collective-permute-done | bytes 172064 | tf_op jit(solution)/shard_map/ppermute | solution.py:750
  99.0 1.6 %place_rows.1 = bf16[4,192,448]{2,1,0:T(8,128)(2,1)} custom-call(s32[15]{0:T(128)S(1)} %concatenate.3.info.refs_13_, bf16[672,128]{1,0:T(8,128)(2,1)S(1)} %get-tuple-element.81.refs_0_, bf16[672,128]{1,0:T(8,128)(2,1)S(1)} %collective-permute-done.25.refs_1_, bf16[672,128]{1,0:T(8,128)(2,1)S(1)} %collective-permute-done.26.refs_2_, ...), custom_call_target="tpu_custom_call" | custom-call | bytes 1376256 | tf_op jit(solution)/shard_map/place_rows/pallas_call | solution.py:586
  (46 shorter events, 9.3 us)
Async XLA Ops:
  1.5 12.5 %collective-permute-start.2 = (bf16[192,1536]{1,0:T(8,128)(2,1)S(1)}, bf16[192,1536]{1,0:T(8,128)(2,1)S(1)}, u32[]{:S(2)}, u32[]{:S(2)}) collective-permute-start(bf16[192,1536]{1,0:T(8,128)(2,1)S(1)} %payload.1.refs_0_), channel_id=1, source_target_pairs={{0,4},{4,0},{8,12},{12,8},{16,20},{20,16},{24,28},{28,24},{1,5},{5... | collective-permute-start | bytes 1769480 | tf_op jit(solution)/shard_map/ppermute | solution.py:602
  2.0 16.5 %collective-permute-start = (bf16[192,1536]{1,0:T(8,128)(2,1)S(1)}, bf16[192,1536]{1,0:T(8,128)(2,1)S(1)}, u32[]{:S(2)}, u32[]{:S(2)}) collective-permute-start(bf16[192,1536]{1,0:T(8,128)(2,1)S(1)} %payload.1.refs_0_), channel_id=1, source_target_pairs={{0,8},{4,12},{8,0},{12,4},{16,24},{20,28},{24,16},{28,20},{1,9},{5... | collective-permute-start | bytes 1769480 | tf_op jit(solution)/shard_map/ppermute | solution.py:602
  4.6 15.4 %collective-permute-start.1 = (bf16[192,1536]{1,0:T(8,128)(2,1)S(1)}, bf16[192,1536]{1,0:T(8,128)(2,1)S(1)}, u32[]{:S(2)}, u32[]{:S(2)}) collective-permute-start(bf16[192,1536]{1,0:T(8,128)(2,1)S(1)} %payload.1.refs_0_), channel_id=1, source_target_pairs={{0,16},{4,20},{8,24},{12,28},{16,0},{20,4},{24,8},{28,12},{1,17},{... | collective-permute-start | bytes 1769480 | tf_op jit(solution)/shard_map/ppermute | solution.py:602
  6.8 0.7 copy-start.1
  7.5 0.7 copy-start.2
  8.2 0.7 copy-start.3
  8.9 5.1 %copy-start = (bf16[128,512]{1,0:T(8,128)(2,1)S(1)}, bf16[128,512]{1,0:T(8,128)(2,1)}, u32[]{:S(2)}) copy-start(bf16[128,512]{1,0:T(8,128)(2,1)} %constant.48.clone.refs_2_.refs_4_) | copy-start | bytes 393220
  20.0 2.7 %collective-permute-start.6 = (bf16[192,1536]{1,0:T(8,128)(2,1)S(1)}, bf16[192,1536]{1,0:T(8,128)(2,1)S(1)}, u32[]{:S(2)}, u32[]{:S(2)}) collective-permute-start(bf16[192,1536]{1,0:T(8,128)(2,1)S(1)} %collective-permute-done.across_x.refs_0_), channel_id=1, source_target_pairs={{0,4},{4,0},{8,12},{12,8},{16,20},{20,16},{24,28},{28,24},{1,5},{5... | collective-permute-start | bytes 1769480 | tf_op jit(solution)/shard_map/ppermute | solution.py:602
  20.0 5.2 %collective-permute-start.5 = (bf16[192,1536]{1,0:T(8,128)(2,1)S(1)}, bf16[192,1536]{1,0:T(8,128)(2,1)S(1)}, u32[]{:S(2)}, u32[]{:S(2)}) collective-permute-start(bf16[192,1536]{1,0:T(8,128)(2,1)S(1)} %collective-permute-done.1.across_y.refs_0_), channel_id=1, source_target_pairs={{0,4},{4,0},{8,12},{12,8},{16,20},{20,16},{24,28},{28,24},{1,5},{5... | collective-permute-start | bytes 1769480 | tf_op jit(solution)/shard_map/ppermute | solution.py:602
  20.5 9.0 %collective-permute-start.3 = (bf16[96,1536]{1,0:T(8,128)(2,1)S(1)}, bf16[96,1536]{1,0:T(8,128)(2,1)S(1)}, u32[]{:S(2)}, u32[]{:S(2)}) collective-permute-start(bf16[96,1536]{1,0:T(8,128)(2,1)S(1)} %get-tuple-element.51), channel_id=1, source_target_pairs={{0,16},{4,20},{8,24},{12,28},{16,0},{20,4},{24,8},{28,12},{1,17},{... | collective-permute-start | bytes 884744 | tf_op jit(solution)/shard_map/ppermute | solution.py:602
  22.1 8.6 %collective-permute-start.4 = (bf16[96,1536]{1,0:T(8,128)(2,1)S(1)}, bf16[96,1536]{1,0:T(8,128)(2,1)S(1)}, u32[]{:S(2)}, u32[]{:S(2)}) collective-permute-start(bf16[96,1536]{1,0:T(8,128)(2,1)S(1)} %get-tuple-element.52), channel_id=1, source_target_pairs={{0,8},{4,12},{8,0},{12,4},{16,24},{20,28},{24,16},{28,20},{1,9},{5... | collective-permute-start | bytes 884744 | tf_op jit(solution)/shard_map/ppermute | solution.py:602
  30.7 1.6 %collective-permute-start.7 = (bf16[96,1536]{1,0:T(8,128)(2,1)S(1)}, bf16[96,1536]{1,0:T(8,128)(2,1)S(1)}, u32[]{:S(2)}, u32[]{:S(2)}) collective-permute-start(bf16[96,1536]{1,0:T(8,128)(2,1)S(1)} %collective-permute-done.3.refs_0_), channel_id=1, source_target_pairs={{0,4},{4,0},{8,12},{12,8},{16,20},{20,16},{24,28},{28,24},{1,5},{5... | collective-permute-start | bytes 884744 | tf_op jit(solution)/shard_map/ppermute | solution.py:602
  30.7 2.0 %collective-permute-start.8 = (bf16[96,1536]{1,0:T(8,128)(2,1)S(1)}, bf16[96,1536]{1,0:T(8,128)(2,1)S(1)}, u32[]{:S(2)}, u32[]{:S(2)}) collective-permute-start(bf16[96,1536]{1,0:T(8,128)(2,1)S(1)} %collective-permute-done.4.refs_1_), channel_id=1, source_target_pairs={{0,4},{4,0},{8,12},{12,8},{16,20},{20,16},{24,28},{28,24},{1,5},{5... | collective-permute-start | bytes 884744 | tf_op jit(solution)/shard_map/ppermute | solution.py:602
  39.6 9.1 %collective-permute-start.10 = (bf16[1152,128]{1,0:T(8,128)(2,1)S(1)}, bf16[1152,128]{1,0:T(8,128)(2,1)S(1)}, u32[]{:S(2)}, u32[]{:S(2)}) collective-permute-start(bf16[1152,128]{1,0:T(8,128)(2,1)S(1)} %get-tuple-element.69.refs_5_), channel_id=1, source_target_pairs={{0,16},{4,20},{8,24},{12,28},{16,0},{20,4},{24,8},{28,12},{1,17},{... | collective-permute-start | bytes 884744 | tf_op jit(solution)/shard_map/ppermute | solution.py:602
  40.1 8.8 %collective-permute-start.9 = (bf16[1152,128]{1,0:T(8,128)(2,1)S(1)}, bf16[1152,128]{1,0:T(8,128)(2,1)S(1)}, u32[]{:S(2)}, u32[]{:S(2)}) collective-permute-start(bf16[1152,128]{1,0:T(8,128)(2,1)S(1)} %get-tuple-element.69.refs_5_), channel_id=1, source_target_pairs={{0,8},{4,12},{8,0},{12,4},{16,24},{20,28},{24,16},{28,20},{1,9},{5... | collective-permute-start | bytes 884744 | tf_op jit(solution)/shard_map/ppermute | solution.py:602
  40.5 17.3 %collective-permute-start.17 = (bf16[1152,128]{1,0:T(8,128)(2,1)S(1)}, bf16[1152,128]{1,0:T(8,128)(2,1)S(1)}, u32[]{:S(2)}, u32[]{:S(2)}) collective-permute-start(bf16[1152,128]{1,0:T(8,128)(2,1)S(1)} %get-tuple-element.69.refs_5_), channel_id=1, source_target_pairs={{0,4},{4,0},{8,12},{12,8},{16,20},{20,16},{24,28},{28,24},{1,5},{5... | collective-permute-start | bytes 884744 | tf_op jit(solution)/shard_map/ppermute | solution.py:602
  48.9 6.1 %collective-permute-start.18 = (bf16[576,128]{1,0:T(8,128)(2,1)S(1)}, bf16[576,128]{1,0:T(8,128)(2,1)S(1)}, u32[]{:S(2)}, u32[]{:S(2)}) collective-permute-start(bf16[576,128]{1,0:T(8,128)(2,1)S(1)} %get-tuple-element.74), channel_id=1, source_target_pairs={{0,16},{4,20},{8,24},{12,28},{16,0},{20,4},{24,8},{28,12},{1,17},{... | collective-permute-start | bytes 442376 | tf_op jit(solution)/shard_map/ppermute | solution.py:602
  50.5 6.8 %collective-permute-start.19 = (bf16[576,128]{1,0:T(8,128)(2,1)S(1)}, bf16[576,128]{1,0:T(8,128)(2,1)S(1)}, u32[]{:S(2)}, u32[]{:S(2)}) collective-permute-start(bf16[576,128]{1,0:T(8,128)(2,1)S(1)} %get-tuple-element.75), channel_id=1, source_target_pairs={{0,8},{4,12},{8,0},{12,4},{16,24},{20,28},{24,16},{28,20},{1,9},{5... | collective-permute-start | bytes 442376 | tf_op jit(solution)/shard_map/ppermute | solution.py:602
  51.1 10.3 %collective-permute-start.12 = (bf16[1152,128]{1,0:T(8,128)(2,1)S(1)}, bf16[1152,128]{1,0:T(8,128)(2,1)S(1)}, u32[]{:S(2)}, u32[]{:S(2)}) collective-permute-start(bf16[1152,128]{1,0:T(8,128)(2,1)S(1)} %attention.3.refs_5_), channel_id=1, source_target_pairs={{0,8},{4,12},{8,0},{12,4},{16,24},{20,28},{24,16},{28,20},{1,9},{5... | collective-permute-start | bytes 884744 | tf_op jit(solution)/shard_map/ppermute | solution.py:602
  52.5 8.8 %collective-permute-start.14 = (bf16[1152,128]{1,0:T(8,128)(2,1)S(1)}, bf16[1152,128]{1,0:T(8,128)(2,1)S(1)}, u32[]{:S(2)}, u32[]{:S(2)}) collective-permute-start(bf16[1152,128]{1,0:T(8,128)(2,1)S(1)} %attention.3.refs_5_), channel_id=1, source_target_pairs={{0,16},{4,20},{8,24},{12,28},{16,0},{20,4},{24,8},{28,12},{1,17},{... | collective-permute-start | bytes 884744 | tf_op jit(solution)/shard_map/ppermute | solution.py:602
  57.3 5.5 %collective-permute-start.20 = (bf16[1152,128]{1,0:T(8,128)(2,1)S(1)}, bf16[1152,128]{1,0:T(8,128)(2,1)S(1)}, u32[]{:S(2)}, u32[]{:S(2)}) collective-permute-start(bf16[1152,128]{1,0:T(8,128)(2,1)S(1)} %collective-permute-done.9.across_x.refs_7_), channel_id=1, source_target_pairs={{0,4},{4,0},{8,12},{12,8},{16,20},{20,16},{24,28},{28,24},{1,5},{5... | collective-permute-start | bytes 884744 | tf_op jit(solution)/shard_map/ppermute | solution.py:602
  57.3 5.9 %collective-permute-start.21 = (bf16[1152,128]{1,0:T(8,128)(2,1)S(1)}, bf16[1152,128]{1,0:T(8,128)(2,1)S(1)}, u32[]{:S(2)}, u32[]{:S(2)}) collective-permute-start(bf16[1152,128]{1,0:T(8,128)(2,1)S(1)} %collective-permute-done.10.across_y.refs_9_), channel_id=1, source_target_pairs={{0,4},{4,0},{8,12},{12,8},{16,20},{20,16},{24,28},{28,24},{1,5},{5... | collective-permute-start | bytes 884744 | tf_op jit(solution)/shard_map/ppermute | solution.py:602
  57.8 4.1 %collective-permute-start.22 = (bf16[576,128]{1,0:T(8,128)(2,1)S(1)}, bf16[576,128]{1,0:T(8,128)(2,1)S(1)}, u32[]{:S(2)}, u32[]{:S(2)}) collective-permute-start(bf16[576,128]{1,0:T(8,128)(2,1)S(1)} %collective-permute-done.18.refs_11_), channel_id=1, source_target_pairs={{0,4},{4,0},{8,12},{12,8},{16,20},{20,16},{24,28},{28,24},{1,5},{5... | collective-permute-start | bytes 442376 | tf_op jit(solution)/shard_map/ppermute | solution.py:602
  61.3 1.4 %collective-permute-start.23 = (bf16[576,128]{1,0:T(8,128)(2,1)S(1)}, bf16[576,128]{1,0:T(8,128)(2,1)S(1)}, u32[]{:S(2)}, u32[]{:S(2)}) collective-permute-start(bf16[576,128]{1,0:T(8,128)(2,1)S(1)} %collective-permute-done.19.refs_12_), channel_id=1, source_target_pairs={{0,4},{4,0},{8,12},{12,8},{16,20},{20,16},{24,28},{28,24},{1,5},{5... | collective-permute-start | bytes 442376 | tf_op jit(solution)/shard_map/ppermute | solution.py:602
  61.3 10.3 %collective-permute-start.16 = (bf16[1152,128]{1,0:T(8,128)(2,1)S(1)}, bf16[1152,128]{1,0:T(8,128)(2,1)S(1)}, u32[]{:S(2)}, u32[]{:S(2)}) collective-permute-start(bf16[1152,128]{1,0:T(8,128)(2,1)S(1)} %attention.3.refs_5_), channel_id=1, source_target_pairs={{0,24},{4,28},{8,16},{12,20},{16,8},{20,12},{24,0},{28,4},{1,25},{... | collective-permute-start | bytes 884744 | tf_op jit(solution)/shard_map/ppermute | solution.py:602
  61.9 9.8 %collective-permute-start.11 = (bf16[1152,128]{1,0:T(8,128)(2,1)S(1)}, bf16[1152,128]{1,0:T(8,128)(2,1)S(1)}, u32[]{:S(2)}, u32[]{:S(2)}) collective-permute-start(bf16[1152,128]{1,0:T(8,128)(2,1)S(1)} %attention.3.refs_5_), channel_id=1, source_target_pairs={{0,4},{4,0},{8,12},{12,8},{16,20},{20,16},{24,28},{28,24},{1,5},{5... | collective-permute-start | bytes 884744 | tf_op jit(solution)/shard_map/ppermute | solution.py:602
  62.7 9.0 %collective-permute-start.13 = (bf16[1152,128]{1,0:T(8,128)(2,1)S(1)}, bf16[1152,128]{1,0:T(8,128)(2,1)S(1)}, u32[]{:S(2)}, u32[]{:S(2)}) collective-permute-start(bf16[1152,128]{1,0:T(8,128)(2,1)S(1)} %collective-permute-done.12.refs_7_), channel_id=1, source_target_pairs={{0,4},{4,0},{8,12},{12,8},{16,20},{20,16},{24,28},{28,24},{1,5},{5... | collective-permute-start | bytes 884744 | tf_op jit(solution)/shard_map/ppermute | solution.py:602
  62.8 8.8 %collective-permute-start.15 = (bf16[1152,128]{1,0:T(8,128)(2,1)S(1)}, bf16[1152,128]{1,0:T(8,128)(2,1)S(1)}, u32[]{:S(2)}, u32[]{:S(2)}) collective-permute-start(bf16[1152,128]{1,0:T(8,128)(2,1)S(1)} %collective-permute-done.14.refs_9_), channel_id=1, source_target_pairs={{0,4},{4,0},{8,12},{12,8},{16,20},{20,16},{24,28},{28,24},{1,5},{5... | collective-permute-start | bytes 884744 | tf_op jit(solution)/shard_map/ppermute | solution.py:602
  71.6 1.6 %collective-permute-start.24 = (bf16[1152,128]{1,0:T(8,128)(2,1)S(1)}, bf16[1152,128]{1,0:T(8,128)(2,1)S(1)}, u32[]{:S(2)}, u32[]{:S(2)}) collective-permute-start(bf16[1152,128]{1,0:T(8,128)(2,1)S(1)} %collective-permute-done.16.refs_11_), channel_id=1, source_target_pairs={{0,4},{4,0},{8,12},{12,8},{16,20},{20,16},{24,28},{28,24},{1,5},{5... | collective-permute-start | bytes 884744 | tf_op jit(solution)/shard_map/ppermute | solution.py:602
  80.9 9.4 %collective-permute-start.25 = (bf16[672,128]{1,0:T(8,128)(2,1)S(1)}, bf16[672,128]{1,0:T(8,128)(2,1)S(1)}, u32[]{:S(2)}, u32[]{:S(2)}) collective-permute-start(bf16[672,128]{1,0:T(8,128)(2,1)S(1)} %get-tuple-element.82), channel_id=1, source_target_pairs={{0,1},{1,0},{2,3},{3,2},{4,5},{5,4},{6,7},{7,6},{8,9},{9,8},{10,11... | collective-permute-start | bytes 516104 | tf_op jit(solution)/shard_map/ppermute | solution.py:750
  82.6 16.4 %collective-permute-start.26 = (bf16[672,128]{1,0:T(8,128)(2,1)S(1)}, bf16[672,128]{1,0:T(8,128)(2,1)S(1)}, u32[]{:S(2)}, u32[]{:S(2)}) collective-permute-start(bf16[672,128]{1,0:T(8,128)(2,1)S(1)} %get-tuple-element.83), channel_id=1, source_target_pairs={{0,2},{1,3},{2,0},{3,1},{4,6},{5,7},{6,4},{7,5},{8,10},{9,11},{10,... | collective-permute-start | bytes 516104 | tf_op jit(solution)/shard_map/ppermute | solution.py:750
  86.4 12.6 %collective-permute-start.27 = (bf16[672,128]{1,0:T(8,128)(2,1)S(1)}, bf16[672,128]{1,0:T(8,128)(2,1)S(1)}, u32[]{:S(2)}, u32[]{:S(2)}) collective-permute-start(bf16[672,128]{1,0:T(8,128)(2,1)S(1)} %get-tuple-element.84), channel_id=1, source_target_pairs={{0,3},{1,2},{2,1},{3,0},{4,7},{5,6},{6,5},{7,4},{8,11},{9,10},{10,... | collective-permute-start | bytes 516104 | tf_op jit(solution)/shard_map/ppermute | solution.py:750

commit v13 on v12

--- a/solution.py
+++ b/solution.py
@@ -309,9 +309,10 @@
     rows = high.shape[1]
     total = block.shape[0]
     segments = segment_row(labels[...])
-    own = labels[start : start + rows, :1].astype(jnp.float32)
-    lowest, largest = jnp.min(own), jnp.max(own)
     one_row = segments[:1]
+    lowest = jnp.min(labels[start : start + 16, :1].astype(jnp.float32), axis=0, keepdims=True)
+    largest = labels[start + rows - 16 : start + rows, :1].astype(jnp.float32)
+    largest = jnp.max(largest, axis=0, keepdims=True)
     begin = jnp.sum(jnp.where(one_row < lowest, 1, 0)) // BLOCK
     end = (jnp.sum(jnp.where(one_row <= largest, 1, 0)) + BLOCK - 1) // BLOCK
     queries = block[start : start + rows, : 2 * LANES]
@@ -556,8 +557,8 @@
         out_shape=shapes,
         compiler_params=pltpu.CompilerParams(vmem_limit_bytes=20 << 20),
         cost_estimate=pl.CostEstimate(
-            flops=4 * rows * D * D + 2 * groups * merge_weight.size,
-            bytes_accessed=2 * (D * D + merge_weight.size + 3 * rows * D),
+            flops=0,
+            bytes_accessed=1024,
             transcendentals=rows,
         ),
         name="out_merge",
@@ -571,7 +572,7 @@
     half = most // 2
     middle = LANES // 2
     for place, block in enumerate(blocks):
-        target = info[PACK] ^ place
+        target = info[PACK] ^ (-place % len(blocks))
         for column in range(whole):
             out[target, :, column * LANES : (column + 1) * LANES] = block[
                 column * most : (column + 1) * most, :
@@ -737,18 +738,18 @@
     far = [send_seq(halves[0], 4), send_seq(halves[1], 2)]
     (late,) = after([late], *halves)
     late_shares = [late] + [send_seq(late, flip) for flip in (2, 4, 6)]
-    near = [send_seq(one, 1) for one in after([across_x, across_y], *far)]
+    near = [send_seq(one, 1) for one in (across_x, across_y)]
     merge = lambda start, rows, sources, route: merge_call(
         start, rows, sources, inputs, ordered, merge_gain_row, merge_rows, bias, packs, route
     )
     sources = [[own], [own_swap], [across_x], near[:1], [across_y], near[1:], far]
     (projected,) = merge(0, first_rows, sources + [[send_seq(one, 1) for one in far]], ())
-    late_shares[3:] = after(late_shares[3:], projected)
+    late_shares[1:] = [after([one], projected)[0] for one in late_shares[1:]]
     sources = [[one] for share in late_shares for one in (share, send_seq(share, 1))]
     made = merge(first_rows, last_rows, sources, (info, most, note, projected))
     blocks = [made[0]] + [
         lax.ppermute(made[flip], "pack", [(z, z ^ flip) for z in range(packs)])
-        for flip in range(1, packs)
+        for flip in range(packs - 1, 0, -1)
     ]
     return place_call(info, blocks, most, merge_weight.shape[1])[None]
 

time: 101 us -> 99.4 us (0.984)
  waiting for transfers between devices: 36.2 us -> 34 us
    ppermute x25, waiting for transfers between devices: 23.6 us -> 19.9 us  [send_seq(): return lax.ppermute(value, 'seq', [(i, i ^ flip) for i in range(size)])]
    ppermute x3, waiting for transfers between devices: 12.6 us -> 14.1 us  [fast_local(): lax.ppermute(made[flip], 'pack', [(z, z ^ flip) for z in range(packs)])]
    ppermute x25, starting transfers between devices: 14.6 us -> 15.9 us  [send_seq(): return lax.ppermute(value, 'seq', [(i, i ^ flip) for i in range(size)])]
    ppermute x3, starting transfers between devices: 5.47 us -> 4.45 us  [fast_local(): lax.ppermute(made[flip], 'pack', [(z, z ^ flip) for z in range(packs)])]
  transfers between devices with their start and end apart: 28 -> 28, of which waited for: 16 -> 18; matrix products, arithmetic and copies ran while one was open for 1% -> 1% of each run, Pallas kernels for 24% -> 24%
where the time goes in v13:
time: 99.4 us; the launch traced here: 98.6 us
  Pallas kernels  41.2 us (41%)
  waiting for transfers between devices  34 us (34%)
  starting transfers between devices  20.4 us (21%)
  local copies, waits for them, and re-layouts  2.79 us (3%)
    ppermute x25, waiting for transfers between devices, send_seq(): return lax.ppermute(value, 'seq', [(i, i ^ flip) for i in range(size)])  19.9 us
    ppermute x25, starting transfers between devices, send_seq(): return lax.ppermute(value, 'seq', [(i, i ^ flip) for i in range(size)])  15.9 us
    pallas_call x2, Pallas kernels, merge_call(): pl.pallas_call(functools.partial(merge_kernel, start, [len(source) for so...  14.2 us
    ppermute x3, waiting for transfers between devices, fast_local(): lax.ppermute(made[flip], 'pack', [(z, z ^ flip) for z in range(packs)])  14.1 us
    pallas_call x4, Pallas kernels, qkv_call(): pl.pallas_call(functools.partial(qkv_kernel, len(first), flip), in_specs=...  10 us
    pallas_call x2, Pallas kernels, attention_call(): pl.pallas_call(functools.partial(attention_kernel, start, first_owner, in...  8.76 us
    pallas_call x1, Pallas kernels, prepare_call(): pl.pallas_call(functools.partial(prepare_kernel, shards), in_specs=[pl.Bl...  5.1 us
    ppermute x3, starting transfers between devices, fast_local(): lax.ppermute(made[flip], 'pack', [(z, z ^ flip) for z in range(packs)])  4.45 us
  transfers between devices with their start and end apart: 28, of which 18 were waited for; matrix products, arithmetic and copies ran while one was open for 1% of the time, Pallas kernels for 24%

profile of v13, /device:TPU:0, one launch (start us, length us, event | category | flops | bytes accessed | tf_op | source)
XLA Modules:
  0.0 98.6 jit_solution(697441304030244081)
XLA Ops:
  0.0 1.5 %payload.1.refs_0_ = bf16[192,1536]{1,0:T(8,128)(2,1)S(1)} custom-call(s32[1,192]{1,0:T(1,128)} %segments.1, s32[1,192]{1,0:T(1,128)} %rows.1, s32[1,192]{1,0:T(1,128)} %columns.1, s32[1,192]{1,0:T(1,128)} %mask.1, bf16[1408]{0:T(1024)(128)(2,1)} %embed.1, bf16[1,192,1408]{2,1,0:T(8,128)(2,1)} %patches.1), custom_call_target="tpu_custom_call" | custom-call | flops 270336 | bytes 1081344 | tf_op jit(solution)/shard_map/payload/pallas_call | solution.py:204
  2.0 2.6 %collective-permute-start = (bf16[192,1536]{1,0:T(8,128)(2,1)S(1)}, bf16[192,1536]{1,0:T(8,128)(2,1)S(1)}, u32[]{:S(2)}, u32[]{:S(2)}) collective-permute-start(bf16[192,1536]{1,0:T(8,128)(2,1)S(1)} %payload.1.refs_0_), channel_id=1, source_target_pairs={{0,8},{4,12},{8,0},{12,4},{16,24},{20,28},{24,16},{28,20},{1,9},{5... | collective-permute-start | bytes 1769480 | tf_op jit(solution)/shard_map/ppermute | solution.py:603
  4.6 1.5 %collective-permute-start.1 = (bf16[192,1536]{1,0:T(8,128)(2,1)S(1)}, bf16[192,1536]{1,0:T(8,128)(2,1)S(1)}, u32[]{:S(2)}, u32[]{:S(2)}) collective-permute-start(bf16[192,1536]{1,0:T(8,128)(2,1)S(1)} %payload.1.refs_0_), channel_id=1, source_target_pairs={{0,16},{4,20},{8,24},{12,28},{16,0},{20,4},{24,8},{28,12},{1,17},{... | collective-permute-start | bytes 1769480 | tf_op jit(solution)/shard_map/ppermute | solution.py:603
  8.9 5.1 %prepare.1 = (f32[1,1408]{1,0:T(1,128)S(1)}, f32[1,1408]{1,0:T(1,128)S(1)}, f32[1,448]{1,0:T(1,128)S(1)}, bf16[1536,1408]{1,0:T(8,128)(2,1)S(1)}, bf16[448,5632]...) custom-call(s32[15]{0:T(128)S(1)} %concatenate.3.info.refs_13_, bf16[1408,1408]{1,0:T(8,128)(2,1)} %out_weight.1, ...), custom_call_target="tpu_custom_call" | custom-call | flops 1141899264 | bytes 20996096 | tf_op jit(solution)/shard_map/prepare/pallas_call | solution.py:437
  14.0 2.5 %norm_qkv.4 = (bf16[1536,1408]{1,0:T(8,128)(2,1)S(1)}, bf16[1536,1024]{1,0:T(8,128)(2,1)S(1)}, bf16[1536,128]{1,0:T(8,128)(2,1)S(1)}) custom-call(s32[15]{0:T(128)S(1)} %concatenate.3.info.refs_13_, bf16[192,1536]{1,0:T(8,128)(2,1)S(1)} %payload.1.refs_0_, bf16[192,1536]{1,0:T(8,128)(2,1)S(1)} %collective-permute-done.2.refs_1_, ...), custom_call_target="tpu_custom_call" | custom-call | flops 2491416576 | bytes 6488064 | tf_op jit(solution)/shard_map/norm_qkv/pallas_call | solution.py:279
  16.5 1.9 %collective-permute-done.across_x.refs_0_ = bf16[192,1536]{1,0:T(8,128)(2,1)S(1)} collective-permute-done((bf16[192,1536]{1,0:T(8,128)(2,1)S(1)}, bf16[192,1536]{1,0:T(8,128)(2,1)S(1)}, u32[]{:S(2)}, u32[]{:S(2)}) %collective-permute-start) | collective-permute-done | bytes 589856 | tf_op jit(solution)/shard_map/ppermute | solution.py:603
  18.5 1.5 %collective-permute-done.1.across_y.refs_0_ = bf16[192,1536]{1,0:T(8,128)(2,1)S(1)} collective-permute-done((bf16[192,1536]{1,0:T(8,128)(2,1)S(1)}, bf16[192,1536]{1,0:T(8,128)(2,1)S(1)}, u32[]{:S(2)}, u32[]{:S(2)}) %collective-permute-start.1) | collective-permute-done | bytes 589856 | tf_op jit(solution)/shard_map/ppermute | solution.py:603
  20.5 1.6 %collective-permute-start.3 = (bf16[96,1536]{1,0:T(8,128)(2,1)S(1)}, bf16[96,1536]{1,0:T(8,128)(2,1)S(1)}, u32[]{:S(2)}, u32[]{:S(2)}) collective-permute-start(bf16[96,1536]{1,0:T(8,128)(2,1)S(1)} %get-tuple-element.51), channel_id=1, source_target_pairs={{0,16},{4,20},{8,24},{12,28},{16,0},{20,4},{24,8},{28,12},{1,17},{... | collective-permute-start | bytes 884744 | tf_op jit(solution)/shard_map/ppermute | solution.py:603
  22.6 2.5 %norm_qkv.5 = (bf16[1536,1408]{1,0:T(8,128)(2,1)S(1)}, bf16[1536,1024]{1,0:T(8,128)(2,1)S(1)}, bf16[1536,128]{1,0:T(8,128)(2,1)S(1)}) custom-call(s32[15]{0:T(128)S(1)} %concatenate.3.info.refs_13_, bf16[192,1536]{1,0:T(8,128)(2,1)S(1)} %collective-permute-done.across_x.refs_0_, ...), custom_call_target="tpu_custom_call", output_to_operand_aliasing={{0}: (6, {}), {1}: (7, {}), {2}: (8, {})} | custom-call | flops 2491416576 | bytes 6488064 | tf_op jit(solution)/shard_map/norm_qkv/pallas_call | solution.py:279
  25.2 2.5 %norm_qkv.6 = (bf16[1536,1408]{1,0:T(8,128)(2,1)S(1)}, bf16[1536,1024]{1,0:T(8,128)(2,1)S(1)}, bf16[1536,128]{1,0:T(8,128)(2,1)S(1)}) custom-call(s32[15]{0:T(128)S(1)} %concatenate.3.info.refs_13_, bf16[192,1536]{1,0:T(8,128)(2,1)S(1)} %collective-permute-done.1.across_y.refs_0_, ...), custom_call_target="tpu_custom_call", output_to_operand_aliasing={{0}: (6, {}), {1}: (7, {}), {2}: (8, {})} | custom-call | flops 2491416576 | bytes 6488064 | tf_op jit(solution)/shard_map/norm_qkv/pallas_call | solution.py:279
  27.7 1.8 %collective-permute-done.3.refs_0_ = bf16[96,1536]{1,0:T(8,128)(2,1)S(1)} collective-permute-done((bf16[96,1536]{1,0:T(8,128)(2,1)S(1)}, bf16[96,1536]{1,0:T(8,128)(2,1)S(1)}, u32[]{:S(2)}, u32[]{:S(2)}) %collective-permute-start.3) | collective-permute-done | bytes 294944 | tf_op jit(solution)/shard_map/ppermute | solution.py:603
  29.5 1.2 %collective-permute-done.4.refs_1_ = bf16[96,1536]{1,0:T(8,128)(2,1)S(1)} collective-permute-done((bf16[96,1536]{1,0:T(8,128)(2,1)S(1)}, bf16[96,1536]{1,0:T(8,128)(2,1)S(1)}, u32[]{:S(2)}, u32[]{:S(2)}) %collective-permute-start.4) | collective-permute-done | bytes 294944 | tf_op jit(solution)/shard_map/ppermute | solution.py:603
  31.2 1.1 %collective-permute-done.7.refs_2_ = bf16[96,1536]{1,0:T(8,128)(2,1)S(1)} collective-permute-done((bf16[96,1536]{1,0:T(8,128)(2,1)S(1)}, bf16[96,1536]{1,0:T(8,128)(2,1)S(1)}, u32[]{:S(2)}, u32[]{:S(2)}) %collective-permute-start.7) | collective-permute-done | bytes 294944 | tf_op jit(solution)/shard_map/ppermute | solution.py:603
  32.7 2.5 %norm_qkv.7 = (bf16[1536,1408]{1,0:T(8,128)(2,1)S(1)}, bf16[1536,1024]{1,0:T(8,128)(2,1)S(1)}, bf16[1536,128]{1,0:T(8,128)(2,1)S(1)}) custom-call(s32[15]{0:T(128)S(1)} %concatenate.3.info.refs_13_, bf16[96,1536]{1,0:T(8,128)(2,1)S(1)} %collective-permute-done.3.refs_0_, ...), custom_call_target="tpu_custom_call", output_to_operand_aliasing={{0}: (8, {}), {1}: (9, {}), {2}: (10, {})} | custom-call | flops 2491416576 | bytes 6488064 | tf_op jit(solution)/shard_map/norm_qkv/pallas_call | solution.py:279
  35.2 4.3 %attention.2 = (bf16[1152,128]{1,0:T(8,128)(2,1)S(1)}, bf16[16,128]{1,0:T(8,128)(2,1)S(1)}) custom-call(s32[15]{0:T(128)S(1)} %concatenate.3.info.refs_13_, bf16[1536,128]{1,0:T(8,128)(2,1)S(1)} %get-tuple-element.70.labels, bf16[1536,1024]{1,0:T(8,128)(2,1)S(1)} %get-tuple-element.71.block), custom_call_target="tpu_custom_call" | custom-call | flops 3019898880 | bytes 3145728 | tf_op jit(solution)/shard_map/attention/pallas_call | solution.py:383
  40.5 4.5 %attention.3.refs_5_ = bf16[1152,128]{1,0:T(8,128)(2,1)S(1)} custom-call(s32[15]{0:T(128)S(1)} %concatenate.3.info.refs_13_, bf16[1536,128]{1,0:T(8,128)(2,1)S(1)} %get-tuple-element.70.labels, bf16[1536,1024]{1,0:T(8,128)(2,1)S(1)} %get-tuple-element.71.block), custom_call_target="tpu_custom_call" | custom-call | flops 3019898880 | bytes 3145728 | tf_op jit(solution)/shard_map/attention/pallas_call | solution.py:383
  45.0 3.7 %collective-permute-done.10.across_y.refs_9_ = bf16[1152,128]{1,0:T(8,128)(2,1)S(1)} collective-permute-done((bf16[1152,128]{1,0:T(8,128)(2,1)S(1)}, bf16[1152,128]{1,0:T(8,128)(2,1)S(1)}, u32[]{:S(2)}, u32[]{:S(2)}) %collective-permute-start.10) | collective-permute-done | bytes 294944 | tf_op jit(solution)/shard_map/ppermute | solution.py:603
  49.4 1.6 %collective-permute-start.16 = (bf16[576,128]{1,0:T(8,128)(2,1)S(1)}, bf16[576,128]{1,0:T(8,128)(2,1)S(1)}, u32[]{:S(2)}, u32[]{:S(2)}) collective-permute-start(bf16[576,128]{1,0:T(8,128)(2,1)S(1)} %get-tuple-element.74), channel_id=1, source_target_pairs={{0,16},{4,20},{8,24},{12,28},{16,0},{20,4},{24,8},{28,12},{1,17},{... | collective-permute-start | bytes 442376 | tf_op jit(solution)/shard_map/ppermute | solution.py:603
  51.5 1.4 %collective-permute-start.23 = (bf16[1152,128]{1,0:T(8,128)(2,1)S(1)}, bf16[1152,128]{1,0:T(8,128)(2,1)S(1)}, u32[]{:S(2)}, u32[]{:S(2)}) collective-permute-start(bf16[1152,128]{1,0:T(8,128)(2,1)S(1)} %attention.3.refs_5_), channel_id=1, source_target_pairs={{0,24},{4,28},{8,16},{12,20},{16,8},{20,12},{24,0},{28,4},{1,25},{... | collective-permute-start | bytes 884744 | tf_op jit(solution)/shard_map/ppermute | solution.py:603
  53.0 2.4 %collective-permute-done.16.refs_11_ = bf16[576,128]{1,0:T(8,128)(2,1)S(1)} collective-permute-done((bf16[576,128]{1,0:T(8,128)(2,1)S(1)}, bf16[576,128]{1,0:T(8,128)(2,1)S(1)}, u32[]{:S(2)}, u32[]{:S(2)}) %collective-permute-start.16) | collective-permute-done | bytes 147488 | tf_op jit(solution)/shard_map/ppermute | solution.py:603
  55.3 1.5 %collective-permute-start.21 = (bf16[1152,128]{1,0:T(8,128)(2,1)S(1)}, bf16[1152,128]{1,0:T(8,128)(2,1)S(1)}, u32[]{:S(2)}, u32[]{:S(2)}) collective-permute-start(bf16[1152,128]{1,0:T(8,128)(2,1)S(1)} %attention.3.refs_5_), channel_id=1, source_target_pairs={{0,16},{4,20},{8,24},{12,28},{16,0},{20,4},{24,8},{28,12},{1,17},{... | collective-permute-start | bytes 884744 | tf_op jit(solution)/shard_map/ppermute | solution.py:603
  56.9 0.9 collective-permute-done.17.refs_12_
  58.8 0.9 collective-permute-done.18.refs_13_
  59.9 6.6 %out_merge.2.refs_15_ = bf16[192,448]{1,0:T(8,128)(2,1)S(1)} custom-call(bf16[1536,1408]{1,0:T(8,128)(2,1)S(1)} %get-tuple-element.63.refs_0_, bf16[1536,1408]{1,0:T(8,128)(2,1)S(1)} %get-tuple-element.48.refs_1_, f32[1,1408]{1,0:T(1,128)S(1)} %get-tuple-element.64.refs_2_, bf16[448,5632]{1,0:T(8,128)(2,1)S(1)} %get-tuple-element.65.refs_3_, ...), custom_call_target="tpu_custom_call" | custom-call | bytes 1024 | tf_op jit(solution)/shard_map/out_merge/pallas_call | solution.py:547
  66.8 1.9 %collective-permute-done.21.refs_9_ = bf16[1152,128]{1,0:T(8,128)(2,1)S(1)} collective-permute-done((bf16[1152,128]{1,0:T(8,128)(2,1)S(1)}, bf16[1152,128]{1,0:T(8,128)(2,1)S(1)}, u32[]{:S(2)}, u32[]{:S(2)}) %collective-permute-start.21) | collective-permute-done | bytes 294944 | tf_op jit(solution)/shard_map/ppermute | solution.py:603
  69.2 1.1 %collective-permute-done.22.refs_10_ = bf16[1152,128]{1,0:T(8,128)(2,1)S(1)} collective-permute-done((bf16[1152,128]{1,0:T(8,128)(2,1)S(1)}, bf16[1152,128]{1,0:T(8,128)(2,1)S(1)}, u32[]{:S(2)}, u32[]{:S(2)}) %collective-permute-start.22) | collective-permute-done | bytes 294944 | tf_op jit(solution)/shard_map/ppermute | solution.py:603
  70.7 7.7 %out_merge.3 = (bf16[672,128]{1,0:T(8,128)(2,1)S(1)}, bf16[672,128]{1,0:T(8,128)(2,1)S(1)}, bf16[672,128]{1,0:T(8,128)(2,1)S(1)}, bf16[672,128]{1,0:T(8,128)(2,1)S(1)}) custom-call(bf16[1536,1408]{1,0:T(8,128)(2,1)S(1)} %get-tuple-element.63.refs_0_, bf16[1536,1408]{1,0:T(8,128)(2,1)S(1)} %get-tuple-element.48.refs_1_, ...), custom_call_target="tpu_custom_call" | custom-call | bytes 1024 | tf_op jit(solution)/shard_map/out_merge/pallas_call | solution.py:547
  78.4 3.7 %collective-permute-start.25 = (bf16[672,128]{1,0:T(8,128)(2,1)S(1)}, bf16[672,128]{1,0:T(8,128)(2,1)S(1)}, u32[]{:S(2)}, u32[]{:S(2)}) collective-permute-start(bf16[672,128]{1,0:T(8,128)(2,1)S(1)} %get-tuple-element.82), channel_id=1, source_target_pairs={{0,3},{1,2},{2,1},{3,0},{4,7},{5,6},{6,5},{7,4},{8,11},{9,10},{10,... | collective-permute-start | bytes 516104 | tf_op jit(solution)/shard_map/ppermute | solution.py:751
  82.1 0.8 collective-permute-start.27
  82.9 4.7 %collective-permute-done.25.refs_1_ = bf16[672,128]{1,0:T(8,128)(2,1)S(1)} collective-permute-done((bf16[672,128]{1,0:T(8,128)(2,1)S(1)}, bf16[672,128]{1,0:T(8,128)(2,1)S(1)}, u32[]{:S(2)}, u32[]{:S(2)}) %collective-permute-start.25) | collective-permute-done | bytes 172064 | tf_op jit(solution)/shard_map/ppermute | solution.py:751
  87.6 9.4 %collective-permute-done.26.refs_2_ = bf16[672,128]{1,0:T(8,128)(2,1)S(1)} collective-permute-done((bf16[672,128]{1,0:T(8,128)(2,1)S(1)}, bf16[672,128]{1,0:T(8,128)(2,1)S(1)}, u32[]{:S(2)}, u32[]{:S(2)}) %collective-permute-start.26) | collective-permute-done | bytes 172064 | tf_op jit(solution)/shard_map/ppermute | solution.py:751
  97.0 1.6 %place_rows.1 = bf16[4,192,448]{2,1,0:T(8,128)(2,1)} custom-call(s32[15]{0:T(128)S(1)} %concatenate.3.info.refs_13_, bf16[672,128]{1,0:T(8,128)(2,1)S(1)} %get-tuple-element.81.refs_0_, bf16[672,128]{1,0:T(8,128)(2,1)S(1)} %collective-permute-done.25.refs_1_, bf16[672,128]{1,0:T(8,128)(2,1)S(1)} %collective-permute-done.26.refs_2_, ...), custom_call_target="tpu_custom_call" | custom-call | bytes 1376256 | tf_op jit(solution)/shard_map/place_rows/pallas_call | solution.py:587
  (46 shorter events, 10.2 us)
Async XLA Ops:
  1.5 12.5 %collective-permute-start.2 = (bf16[192,1536]{1,0:T(8,128)(2,1)S(1)}, bf16[192,1536]{1,0:T(8,128)(2,1)S(1)}, u32[]{:S(2)}, u32[]{:S(2)}) collective-permute-start(bf16[192,1536]{1,0:T(8,128)(2,1)S(1)} %payload.1.refs_0_), channel_id=1, source_target_pairs={{0,4},{4,0},{8,12},{12,8},{16,20},{20,16},{24,28},{28,24},{1,5},{5... | collective-permute-start | bytes 1769480 | tf_op jit(solution)/shard_map/ppermute | solution.py:603
  2.0 16.5 %collective-permute-start = (bf16[192,1536]{1,0:T(8,128)(2,1)S(1)}, bf16[192,1536]{1,0:T(8,128)(2,1)S(1)}, u32[]{:S(2)}, u32[]{:S(2)}) collective-permute-start(bf16[192,1536]{1,0:T(8,128)(2,1)S(1)} %payload.1.refs_0_), channel_id=1, source_target_pairs={{0,8},{4,12},{8,0},{12,4},{16,24},{20,28},{24,16},{28,20},{1,9},{5... | collective-permute-start | bytes 1769480 | tf_op jit(solution)/shard_map/ppermute | solution.py:603
  4.6 15.4 %collective-permute-start.1 = (bf16[192,1536]{1,0:T(8,128)(2,1)S(1)}, bf16[192,1536]{1,0:T(8,128)(2,1)S(1)}, u32[]{:S(2)}, u32[]{:S(2)}) collective-permute-start(bf16[192,1536]{1,0:T(8,128)(2,1)S(1)} %payload.1.refs_0_), channel_id=1, source_target_pairs={{0,16},{4,20},{8,24},{12,28},{16,0},{20,4},{24,8},{28,12},{1,17},{... | collective-permute-start | bytes 1769480 | tf_op jit(solution)/shard_map/ppermute | solution.py:603
  6.8 0.7 copy-start.1
  7.5 0.7 copy-start.2
  8.2 0.7 copy-start.3
  8.9 5.1 %copy-start = (bf16[128,512]{1,0:T(8,128)(2,1)S(1)}, bf16[128,512]{1,0:T(8,128)(2,1)}, u32[]{:S(2)}) copy-start(bf16[128,512]{1,0:T(8,128)(2,1)} %constant.48.clone.refs_2_.refs_4_) | copy-start | bytes 393220
  20.0 2.7 %collective-permute-start.6 = (bf16[192,1536]{1,0:T(8,128)(2,1)S(1)}, bf16[192,1536]{1,0:T(8,128)(2,1)S(1)}, u32[]{:S(2)}, u32[]{:S(2)}) collective-permute-start(bf16[192,1536]{1,0:T(8,128)(2,1)S(1)} %collective-permute-done.across_x.refs_0_), channel_id=1, source_target_pairs={{0,4},{4,0},{8,12},{12,8},{16,20},{20,16},{24,28},{28,24},{1,5},{5... | collective-permute-start | bytes 1769480 | tf_op jit(solution)/shard_map/ppermute | solution.py:603
  20.0 5.2 %collective-permute-start.5 = (bf16[192,1536]{1,0:T(8,128)(2,1)S(1)}, bf16[192,1536]{1,0:T(8,128)(2,1)S(1)}, u32[]{:S(2)}, u32[]{:S(2)}) collective-permute-start(bf16[192,1536]{1,0:T(8,128)(2,1)S(1)} %collective-permute-done.1.across_y.refs_0_), channel_id=1, source_target_pairs={{0,4},{4,0},{8,12},{12,8},{16,20},{20,16},{24,28},{28,24},{1,5},{5... | collective-permute-start | bytes 1769480 | tf_op jit(solution)/shard_map/ppermute | solution.py:603
  20.5 9.0 %collective-permute-start.3 = (bf16[96,1536]{1,0:T(8,128)(2,1)S(1)}, bf16[96,1536]{1,0:T(8,128)(2,1)S(1)}, u32[]{:S(2)}, u32[]{:S(2)}) collective-permute-start(bf16[96,1536]{1,0:T(8,128)(2,1)S(1)} %get-tuple-element.51), channel_id=1, source_target_pairs={{0,16},{4,20},{8,24},{12,28},{16,0},{20,4},{24,8},{28,12},{1,17},{... | collective-permute-start | bytes 884744 | tf_op jit(solution)/shard_map/ppermute | solution.py:603
  22.1 8.6 %collective-permute-start.4 = (bf16[96,1536]{1,0:T(8,128)(2,1)S(1)}, bf16[96,1536]{1,0:T(8,128)(2,1)S(1)}, u32[]{:S(2)}, u32[]{:S(2)}) collective-permute-start(bf16[96,1536]{1,0:T(8,128)(2,1)S(1)} %get-tuple-element.52), channel_id=1, source_target_pairs={{0,8},{4,12},{8,0},{12,4},{16,24},{20,28},{24,16},{28,20},{1,9},{5... | collective-permute-start | bytes 884744 | tf_op jit(solution)/shard_map/ppermute | solution.py:603
  30.7 1.6 %collective-permute-start.7 = (bf16[96,1536]{1,0:T(8,128)(2,1)S(1)}, bf16[96,1536]{1,0:T(8,128)(2,1)S(1)}, u32[]{:S(2)}, u32[]{:S(2)}) collective-permute-start(bf16[96,1536]{1,0:T(8,128)(2,1)S(1)} %collective-permute-done.3.refs_0_), channel_id=1, source_target_pairs={{0,4},{4,0},{8,12},{12,8},{16,20},{20,16},{24,28},{28,24},{1,5},{5... | collective-permute-start | bytes 884744 | tf_op jit(solution)/shard_map/ppermute | solution.py:603
  30.7 2.0 %collective-permute-start.8 = (bf16[96,1536]{1,0:T(8,128)(2,1)S(1)}, bf16[96,1536]{1,0:T(8,128)(2,1)S(1)}, u32[]{:S(2)}, u32[]{:S(2)}) collective-permute-start(bf16[96,1536]{1,0:T(8,128)(2,1)S(1)} %collective-permute-done.4.refs_1_), channel_id=1, source_target_pairs={{0,4},{4,0},{8,12},{12,8},{16,20},{20,16},{24,28},{28,24},{1,5},{5... | collective-permute-start | bytes 884744 | tf_op jit(solution)/shard_map/ppermute | solution.py:603
  39.5 9.1 %collective-permute-start.10 = (bf16[1152,128]{1,0:T(8,128)(2,1)S(1)}, bf16[1152,128]{1,0:T(8,128)(2,1)S(1)}, u32[]{:S(2)}, u32[]{:S(2)}) collective-permute-start(bf16[1152,128]{1,0:T(8,128)(2,1)S(1)} %get-tuple-element.69.refs_5_), channel_id=1, source_target_pairs={{0,16},{4,20},{8,24},{12,28},{16,0},{20,4},{24,8},{28,12},{1,17},{... | collective-permute-start | bytes 884744 | tf_op jit(solution)/shard_map/ppermute | solution.py:603
  40.1 8.8 %collective-permute-start.9 = (bf16[1152,128]{1,0:T(8,128)(2,1)S(1)}, bf16[1152,128]{1,0:T(8,128)(2,1)S(1)}, u32[]{:S(2)}, u32[]{:S(2)}) collective-permute-start(bf16[1152,128]{1,0:T(8,128)(2,1)S(1)} %get-tuple-element.69.refs_5_), channel_id=1, source_target_pairs={{0,8},{4,12},{8,0},{12,4},{16,24},{20,28},{24,16},{28,20},{1,9},{5... | collective-permute-start | bytes 884744 | tf_op jit(solution)/shard_map/ppermute | solution.py:603
  40.5 11.0 %collective-permute-start.13 = (bf16[1152,128]{1,0:T(8,128)(2,1)S(1)}, bf16[1152,128]{1,0:T(8,128)(2,1)S(1)}, u32[]{:S(2)}, u32[]{:S(2)}) collective-permute-start(bf16[1152,128]{1,0:T(8,128)(2,1)S(1)} %get-tuple-element.69.refs_5_), channel_id=1, source_target_pairs={{0,4},{4,0},{8,12},{12,8},{16,20},{20,16},{24,28},{28,24},{1,5},{5... | collective-permute-start | bytes 884744 | tf_op jit(solution)/shard_map/ppermute | solution.py:603
  48.9 9.4 %collective-permute-start.14 = (bf16[1152,128]{1,0:T(8,128)(2,1)S(1)}, bf16[1152,128]{1,0:T(8,128)(2,1)S(1)}, u32[]{:S(2)}, u32[]{:S(2)}) collective-permute-start(bf16[1152,128]{1,0:T(8,128)(2,1)S(1)} %collective-permute-done.9.across_x.refs_7_), channel_id=1, source_target_pairs={{0,4},{4,0},{8,12},{12,8},{16,20},{20,16},{24,28},{28,24},{1,5},{5... | collective-permute-start | bytes 884744 | tf_op jit(solution)/shard_map/ppermute | solution.py:603
  48.9 9.4 %collective-permute-start.15 = (bf16[1152,128]{1,0:T(8,128)(2,1)S(1)}, bf16[1152,128]{1,0:T(8,128)(2,1)S(1)}, u32[]{:S(2)}, u32[]{:S(2)}) collective-permute-start(bf16[1152,128]{1,0:T(8,128)(2,1)S(1)} %collective-permute-done.10.across_y.refs_9_), channel_id=1, source_target_pairs={{0,4},{4,0},{8,12},{12,8},{16,20},{20,16},{24,28},{28,24},{1,5},{5... | collective-permute-start | bytes 884744 | tf_op jit(solution)/shard_map/ppermute | solution.py:603
  49.4 5.9 %collective-permute-start.16 = (bf16[576,128]{1,0:T(8,128)(2,1)S(1)}, bf16[576,128]{1,0:T(8,128)(2,1)S(1)}, u32[]{:S(2)}, u32[]{:S(2)}) collective-permute-start(bf16[576,128]{1,0:T(8,128)(2,1)S(1)} %get-tuple-element.74), channel_id=1, source_target_pairs={{0,16},{4,20},{8,24},{12,28},{16,0},{20,4},{24,8},{28,12},{1,17},{... | collective-permute-start | bytes 442376 | tf_op jit(solution)/shard_map/ppermute | solution.py:603
  51.0 6.8 %collective-permute-start.17 = (bf16[576,128]{1,0:T(8,128)(2,1)S(1)}, bf16[576,128]{1,0:T(8,128)(2,1)S(1)}, u32[]{:S(2)}, u32[]{:S(2)}) collective-permute-start(bf16[576,128]{1,0:T(8,128)(2,1)S(1)} %get-tuple-element.75), channel_id=1, source_target_pairs={{0,8},{4,12},{8,0},{12,4},{16,24},{20,28},{24,16},{28,20},{1,9},{5... | collective-permute-start | bytes 442376 | tf_op jit(solution)/shard_map/ppermute | solution.py:603
  51.5 14.9 %collective-permute-start.23 = (bf16[1152,128]{1,0:T(8,128)(2,1)S(1)}, bf16[1152,128]{1,0:T(8,128)(2,1)S(1)}, u32[]{:S(2)}, u32[]{:S(2)}) collective-permute-start(bf16[1152,128]{1,0:T(8,128)(2,1)S(1)} %attention.3.refs_5_), channel_id=1, source_target_pairs={{0,24},{4,28},{8,16},{12,20},{16,8},{20,12},{24,0},{28,4},{1,25},{... | collective-permute-start | bytes 884744 | tf_op jit(solution)/shard_map/ppermute | solution.py:603
  55.3 13.4 %collective-permute-start.21 = (bf16[1152,128]{1,0:T(8,128)(2,1)S(1)}, bf16[1152,128]{1,0:T(8,128)(2,1)S(1)}, u32[]{:S(2)}, u32[]{:S(2)}) collective-permute-start(bf16[1152,128]{1,0:T(8,128)(2,1)S(1)} %attention.3.refs_5_), channel_id=1, source_target_pairs={{0,16},{4,20},{8,24},{12,28},{16,0},{20,4},{24,8},{28,12},{1,17},{... | collective-permute-start | bytes 884744 | tf_op jit(solution)/shard_map/ppermute | solution.py:603
  57.8 11.4 %collective-permute-start.12 = (bf16[1152,128]{1,0:T(8,128)(2,1)S(1)}, bf16[1152,128]{1,0:T(8,128)(2,1)S(1)}, u32[]{:S(2)}, u32[]{:S(2)}) collective-permute-start(bf16[1152,128]{1,0:T(8,128)(2,1)S(1)} %attention.3.refs_5_), channel_id=1, source_target_pairs={{0,8},{4,12},{8,0},{12,4},{16,24},{20,28},{24,16},{28,20},{1,9},{5... | collective-permute-start | bytes 884744 | tf_op jit(solution)/shard_map/ppermute | solution.py:603
  58.3 1.4 %collective-permute-start.18 = (bf16[576,128]{1,0:T(8,128)(2,1)S(1)}, bf16[576,128]{1,0:T(8,128)(2,1)S(1)}, u32[]{:S(2)}, u32[]{:S(2)}) collective-permute-start(bf16[576,128]{1,0:T(8,128)(2,1)S(1)} %collective-permute-done.16.refs_11_), channel_id=1, source_target_pairs={{0,4},{4,0},{8,12},{12,8},{16,20},{20,16},{24,28},{28,24},{1,5},{5... | collective-permute-start | bytes 442376 | tf_op jit(solution)/shard_map/ppermute | solution.py:603
  58.3 1.6 %collective-permute-start.19 = (bf16[576,128]{1,0:T(8,128)(2,1)S(1)}, bf16[576,128]{1,0:T(8,128)(2,1)S(1)}, u32[]{:S(2)}, u32[]{:S(2)}) collective-permute-start(bf16[576,128]{1,0:T(8,128)(2,1)S(1)} %collective-permute-done.17.refs_12_), channel_id=1, source_target_pairs={{0,4},{4,0},{8,12},{12,8},{16,20},{20,16},{24,28},{28,24},{1,5},{5... | collective-permute-start | bytes 442376 | tf_op jit(solution)/shard_map/ppermute | solution.py:603
  59.7 9.5 %collective-permute-start.11 = (bf16[1152,128]{1,0:T(8,128)(2,1)S(1)}, bf16[1152,128]{1,0:T(8,128)(2,1)S(1)}, u32[]{:S(2)}, u32[]{:S(2)}) collective-permute-start(bf16[1152,128]{1,0:T(8,128)(2,1)S(1)} %attention.3.refs_5_), channel_id=1, source_target_pairs={{0,4},{4,0},{8,12},{12,8},{16,20},{20,16},{24,28},{28,24},{1,5},{5... | collective-permute-start | bytes 884744 | tf_op jit(solution)/shard_map/ppermute | solution.py:603
  66.5 2.8 %collective-permute-start.24 = (bf16[1152,128]{1,0:T(8,128)(2,1)S(1)}, bf16[1152,128]{1,0:T(8,128)(2,1)S(1)}, u32[]{:S(2)}, u32[]{:S(2)}) collective-permute-start(bf16[1152,128]{1,0:T(8,128)(2,1)S(1)} %collective-permute-done.23.refs_11_), channel_id=1, source_target_pairs={{0,4},{4,0},{8,12},{12,8},{16,20},{20,16},{24,28},{28,24},{1,5},{5... | collective-permute-start | bytes 884744 | tf_op jit(solution)/shard_map/ppermute | solution.py:603
  68.7 1.6 %collective-permute-start.22 = (bf16[1152,128]{1,0:T(8,128)(2,1)S(1)}, bf16[1152,128]{1,0:T(8,128)(2,1)S(1)}, u32[]{:S(2)}, u32[]{:S(2)}) collective-permute-start(bf16[1152,128]{1,0:T(8,128)(2,1)S(1)} %collective-permute-done.21.refs_9_), channel_id=1, source_target_pairs={{0,4},{4,0},{8,12},{12,8},{16,20},{20,16},{24,28},{28,24},{1,5},{5... | collective-permute-start | bytes 884744 | tf_op jit(solution)/shard_map/ppermute | solution.py:603
  69.2 1.6 %collective-permute-start.20 = (bf16[1152,128]{1,0:T(8,128)(2,1)S(1)}, bf16[1152,128]{1,0:T(8,128)(2,1)S(1)}, u32[]{:S(2)}, u32[]{:S(2)}) collective-permute-start(bf16[1152,128]{1,0:T(8,128)(2,1)S(1)} %collective-permute-done.12.refs_7_), channel_id=1, source_target_pairs={{0,4},{4,0},{8,12},{12,8},{16,20},{20,16},{24,28},{28,24},{1,5},{5... | collective-permute-start | bytes 884744 | tf_op jit(solution)/shard_map/ppermute | solution.py:603
  78.4 9.2 %collective-permute-start.25 = (bf16[672,128]{1,0:T(8,128)(2,1)S(1)}, bf16[672,128]{1,0:T(8,128)(2,1)S(1)}, u32[]{:S(2)}, u32[]{:S(2)}) collective-permute-start(bf16[672,128]{1,0:T(8,128)(2,1)S(1)} %get-tuple-element.82), channel_id=1, source_target_pairs={{0,3},{1,2},{2,1},{3,0},{4,7},{5,6},{6,5},{7,4},{8,11},{9,10},{10,... | collective-permute-start | bytes 516104 | tf_op jit(solution)/shard_map/ppermute | solution.py:751
  82.1 14.9 %collective-permute-start.26 = (bf16[672,128]{1,0:T(8,128)(2,1)S(1)}, bf16[672,128]{1,0:T(8,128)(2,1)S(1)}, u32[]{:S(2)}, u32[]{:S(2)}) collective-permute-start(bf16[672,128]{1,0:T(8,128)(2,1)S(1)} %get-tuple-element.83), channel_id=1, source_target_pairs={{0,2},{1,3},{2,0},{3,1},{4,6},{5,7},{6,4},{7,5},{8,10},{9,11},{10,... | collective-permute-start | bytes 516104 | tf_op jit(solution)/shard_map/ppermute | solution.py:751
  82.1 14.9 %collective-permute-start.27 = (bf16[672,128]{1,0:T(8,128)(2,1)S(1)}, bf16[672,128]{1,0:T(8,128)(2,1)S(1)}, u32[]{:S(2)}, u32[]{:S(2)}) collective-permute-start(bf16[672,128]{1,0:T(8,128)(2,1)S(1)} %get-tuple-element.84), channel_id=1, source_target_pairs={{0,1},{1,0},{2,3},{3,2},{4,5},{5,4},{6,7},{7,6},{8,9},{9,8},{10,11... | collective-permute-start | bytes 516104 | tf_op jit(solution)/shard_map/ppermute | solution.py:751

commit v14 on v13

--- a/solution.py
+++ b/solution.py
@@ -470,24 +470,20 @@
         at += count
     shards = len(sources)
     lane = lax.broadcasted_iota(jnp.int32, (half, LANES), 1)
-    for part in range(2):
-        token = slice(part * half, (part + 1) * half)
-        lined = [source[token, :] for source in sources]
-        for pair in range(shards // 2):
-            mine = sources[2 * pair][rows:, :].astype(jnp.float32)
-            other = sources[2 * pair + 1][rows:, :].astype(jnp.float32)
-            if part == 0:
-                other = pltpu.roll(other, rest, 1)
-            else:
-                mine = pltpu.roll(mine, LANES - rest, 1)
-            lined.append(jnp.where(lane < rest, mine, other).astype(jnp.bfloat16))
-        mixed = jnp.dot(
-            jnp.concatenate(lined, axis=1), weight[...], preferred_element_type=jnp.float32
-        )
-        for column in range(D // LANES):
-            lanes = slice(column * LANES, (column + 1) * LANES)
-            before = inputs[start + part * half : start + (part + 1) * half, lanes]
-            state[column, token, :] = before.astype(jnp.float32) + mixed[:, lanes]
+    lined = [source[:rows, :] for source in sources]
+    for pair in range(shards // 2):
+        mine = sources[2 * pair][rows:, :].astype(jnp.float32)
+        other = sources[2 * pair + 1][rows:, :].astype(jnp.float32)
+        upper = jnp.where(lane < rest, mine, pltpu.roll(other, rest, 1))
+        lower = jnp.where(lane < rest, pltpu.roll(mine, LANES - rest, 1), other)
+        lined.append(jnp.concatenate([upper, lower], axis=0).astype(jnp.bfloat16))
+    mixed = jnp.dot(
+        jnp.concatenate(lined, axis=1), weight[...], preferred_element_type=jnp.float32
+    )
+    for column in range(D // LANES):
+        lanes = slice(column * LANES, (column + 1) * LANES)
+        before = inputs[start : start + rows, lanes]
+        state[column] = before.astype(jnp.float32) + mixed[:, lanes]
     groups = rows // 4
     for block in range(0, groups, NORM_ROWS):
         for quadrant in range(4):
@@ -565,37 +561,42 @@
     )(*operands)
 
 
-def place_kernel(info, *refs):
-    blocks, out = refs[:-1], refs[-1]
-    most, width = out.shape[1:]
+def place_kernel(place, info, block, *refs):
+    out, rows, sem = refs[-3:]
+    most, width = rows.shape
     whole = width // LANES
     half = most // 2
     middle = LANES // 2
-    for place, block in enumerate(blocks):
-        target = info[PACK] ^ (-place % len(blocks))
-        for column in range(whole):
-            out[target, :, column * LANES : (column + 1) * LANES] = block[
-                column * most : (column + 1) * most, :
-            ]
-        out[target, :half, whole * LANES :] = block[whole * most :, :middle]
-        out[target, half:, whole * LANES :] = block[whole * most :, middle:]
-
-
-def place_call(info, blocks, most, width):
-    fixed = lambda shape: pl.BlockSpec(shape, lambda i: (0,) * len(shape))
-    shape = (len(blocks), most, width)
+    for column in range(whole):
+        rows[:, column * LANES : (column + 1) * LANES] = block[
+            column * most : (column + 1) * most, :
+        ]
+    rows[:half, whole * LANES :] = block[whole * most :, :middle]
+    rows[half:, whole * LANES :] = block[whole * most :, middle:]
+    copy = pltpu.make_async_copy(rows, out.at[info[PACK] ^ place], sem)
+    copy.start()
+    copy.wait()
+
+
+def place_call(info, place, block, earlier, shape):
+    anywhere = pl.BlockSpec(memory_space=pl.ANY)
     return pl.pallas_call(
-        place_kernel,
-        grid=(1,),
-        in_specs=[pl.BlockSpec(memory_space=pltpu.SMEM)] + [fixed(one.shape) for one in blocks],
-        out_specs=fixed(shape),
-        out_shape=jax.ShapeDtypeStruct(shape, jnp.bfloat16),
-        compiler_params=pltpu.CompilerParams(vmem_limit_bytes=8 << 20),
+        functools.partial(place_kernel, place),
+        in_specs=[
+            pl.BlockSpec(memory_space=pltpu.SMEM),
+            pl.BlockSpec(memory_space=pltpu.VMEM),
+        ]
+        + [anywhere] * len(earlier),
+        out_specs=anywhere,
+        out_shape=pltpu.HBM(shape, jnp.bfloat16),
+        scratch_shapes=[pltpu.VMEM(shape[1:], jnp.bfloat16), pltpu.SemaphoreType.DMA],
+        input_output_aliases={2: 0} if earlier else {},
+        compiler_params=pltpu.CompilerParams(vmem_limit_bytes=4 << 20),
         cost_estimate=pl.CostEstimate(
-            flops=0, bytes_accessed=4 * len(blocks) * most * width, transcendentals=0
+            flops=0, bytes_accessed=4 * shape[1] * shape[2], transcendentals=0
         ),
         name="place_rows",
-    )(info, *blocks)
+    )(info, block, *map(in_hbm, earlier))
 
 
 def send_seq(value, flip):
@@ -747,11 +748,15 @@
     late_shares[1:] = [after([one], projected)[0] for one in late_shares[1:]]
     sources = [[one] for share in late_shares for one in (share, send_seq(share, 1))]
     made = merge(first_rows, last_rows, sources, (info, most, note, projected))
-    blocks = [made[0]] + [
-        lax.ppermute(made[flip], "pack", [(z, z ^ flip) for z in range(packs)])
+    sent = {
+        flip: lax.ppermute(made[flip], "pack", [(z, z ^ flip) for z in range(packs)])
         for flip in range(packs - 1, 0, -1)
-    ]
-    return place_call(info, blocks, most, merge_weight.shape[1])[None]
+    }
+    shape = (packs, most, merge_weight.shape[1])
+    routed = place_call(info, 0, made[0], (), shape)
+    for flip in (3, 1, 2):
+        routed = place_call(info, flip, sent[flip], (routed,), shape)
+    return routed[None]
 
 
 def local(*arguments):

time: 99.4 us -> 99.3 us (level)
  waiting for transfers between devices: 34 us -> 28.8 us
  Pallas kernels: 41.2 us -> 46.1 us
    ppermute x3, waiting for transfers between devices: 14.1 us -> 10.2 us  [fast_local(): lax.ppermute(made[flip], 'pack', [(z, z ^ flip) for z in range(packs)])]
    pallas_call x1 -> x4, Pallas kernels: 1.6 us -> 5.21 us  [place_call(): pl.pallas_call(functools.partial(place_kernel, place), in_specs=[pl.Block...]
    pallas_call x2, Pallas kernels: 8.76 us -> 10 us  [attention_call(): pl.pallas_call(functools.partial(attention_kernel, start, first_owner, in...]
    ppermute x25, waiting for transfers between devices: 19.9 us -> 18.7 us  [send_seq(): return lax.ppermute(value, 'seq', [(i, i ^ flip) for i in range(size)])]
  transfers between devices with their start and end apart: 28 -> 28, of which waited for: 18 -> 19; matrix products, arithmetic and copies ran while one was open for 1% -> 1% of each run, Pallas kernels for 24% -> 29%
where the time goes in v14:
time: 99.3 us; the launch traced here: 98.4 us
  Pallas kernels  46.1 us (46%)
  waiting for transfers between devices  28.8 us (29%)
  starting transfers between devices  20.4 us (21%)
  local copies, waits for them, and re-layouts  2.79 us (3%)
    ppermute x25, waiting for transfers between devices, send_seq(): return lax.ppermute(value, 'seq', [(i, i ^ flip) for i in range(size)])  18.7 us
    ppermute x25, starting transfers between devices, send_seq(): return lax.ppermute(value, 'seq', [(i, i ^ flip) for i in range(size)])  15.9 us
    pallas_call x2, Pallas kernels, merge_call(): pl.pallas_call(functools.partial(merge_kernel, start, [len(source) for so...  14.2 us
    ppermute x3, waiting for transfers between devices, fast_local(): lax.ppermute(made[flip], 'pack', [(z, z ^ flip) for z in range(packs)])  10.2 us
    pallas_call x2, Pallas kernels, attention_call(): pl.pallas_call(functools.partial(attention_kernel, start, first_owner, in...  10 us
    pallas_call x4, Pallas kernels, qkv_call(): pl.pallas_call(functools.partial(qkv_kernel, len(first), flip), in_specs=...  10 us
    pallas_call x4, Pallas kernels, place_call(): pl.pallas_call(functools.partial(place_kernel, place), in_specs=[pl.Block...  5.21 us
    pallas_call x1, Pallas kernels, prepare_call(): pl.pallas_call(functools.partial(prepare_kernel, shards), in_specs=[pl.Bl...  5.1 us
  transfers between devices with their start and end apart: 28, of which 19 were waited for; matrix products, arithmetic and copies ran while one was open for 1% of the time, Pallas kernels for 29%

profile of v14, /device:TPU:0, one launch (start us, length us, event | category | flops | bytes accessed | tf_op | source)
XLA Modules:
  0.0 98.4 jit_solution(14629837374793658403)
XLA Ops:
  0.0 1.5 %payload.1.refs_0_ = bf16[192,1536]{1,0:T(8,128)(2,1)S(1)} custom-call(s32[1,192]{1,0:T(1,128)} %segments.1, s32[1,192]{1,0:T(1,128)} %rows.1, s32[1,192]{1,0:T(1,128)} %columns.1, s32[1,192]{1,0:T(1,128)} %mask.1, bf16[1408]{0:T(1024)(128)(2,1)} %embed.1, bf16[1,192,1408]{2,1,0:T(8,128)(2,1)} %patches.1), custom_call_target="tpu_custom_call" | custom-call | flops 270336 | bytes 1081344 | tf_op jit(solution)/shard_map/payload/pallas_call | solution.py:204
  2.0 2.6 %collective-permute-start = (bf16[192,1536]{1,0:T(8,128)(2,1)S(1)}, bf16[192,1536]{1,0:T(8,128)(2,1)S(1)}, u32[]{:S(2)}, u32[]{:S(2)}) collective-permute-start(bf16[192,1536]{1,0:T(8,128)(2,1)S(1)} %payload.1.refs_0_), channel_id=1, source_target_pairs={{0,8},{4,12},{8,0},{12,4},{16,24},{20,28},{24,16},{28,20},{1,9},{5... | collective-permute-start | bytes 1769480 | tf_op jit(solution)/shard_map/ppermute | solution.py:604
  4.6 1.5 %collective-permute-start.1 = (bf16[192,1536]{1,0:T(8,128)(2,1)S(1)}, bf16[192,1536]{1,0:T(8,128)(2,1)S(1)}, u32[]{:S(2)}, u32[]{:S(2)}) collective-permute-start(bf16[192,1536]{1,0:T(8,128)(2,1)S(1)} %payload.1.refs_0_), channel_id=1, source_target_pairs={{0,16},{4,20},{8,24},{12,28},{16,0},{20,4},{24,8},{28,12},{1,17},{... | collective-permute-start | bytes 1769480 | tf_op jit(solution)/shard_map/ppermute | solution.py:604
  8.9 5.1 %prepare.1 = (f32[1,1408]{1,0:T(1,128)S(1)}, f32[1,1408]{1,0:T(1,128)S(1)}, f32[1,448]{1,0:T(1,128)S(1)}, bf16[1536,1408]{1,0:T(8,128)(2,1)S(1)}, bf16[448,5632]...) custom-call(s32[15]{0:T(128)S(1)} %concatenate.3.info.refs_13_, bf16[1408,1408]{1,0:T(8,128)(2,1)} %out_weight.1, ...), custom_call_target="tpu_custom_call" | custom-call | flops 1141899264 | bytes 20996096 | tf_op jit(solution)/shard_map/prepare/pallas_call | solution.py:437
  14.0 2.5 %norm_qkv.4 = (bf16[1536,1408]{1,0:T(8,128)(2,1)S(1)}, bf16[1536,1024]{1,0:T(8,128)(2,1)S(1)}, bf16[1536,128]{1,0:T(8,128)(2,1)S(1)}) custom-call(s32[15]{0:T(128)S(1)} %concatenate.3.info.refs_13_, bf16[192,1536]{1,0:T(8,128)(2,1)S(1)} %payload.1.refs_0_, bf16[192,1536]{1,0:T(8,128)(2,1)S(1)} %collective-permute-done.2.refs_1_, ...), custom_call_target="tpu_custom_call" | custom-call | flops 2491416576 | bytes 6488064 | tf_op jit(solution)/shard_map/norm_qkv/pallas_call | solution.py:279
  16.5 1.9 %collective-permute-done.across_x.refs_0_ = bf16[192,1536]{1,0:T(8,128)(2,1)S(1)} collective-permute-done((bf16[192,1536]{1,0:T(8,128)(2,1)S(1)}, bf16[192,1536]{1,0:T(8,128)(2,1)S(1)}, u32[]{:S(2)}, u32[]{:S(2)}) %collective-permute-start) | collective-permute-done | bytes 589856 | tf_op jit(solution)/shard_map/ppermute | solution.py:604
  18.5 1.5 %collective-permute-done.1.across_y.refs_0_ = bf16[192,1536]{1,0:T(8,128)(2,1)S(1)} collective-permute-done((bf16[192,1536]{1,0:T(8,128)(2,1)S(1)}, bf16[192,1536]{1,0:T(8,128)(2,1)S(1)}, u32[]{:S(2)}, u32[]{:S(2)}) %collective-permute-start.1) | collective-permute-done | bytes 589856 | tf_op jit(solution)/shard_map/ppermute | solution.py:604
  20.5 1.6 %collective-permute-start.3 = (bf16[96,1536]{1,0:T(8,128)(2,1)S(1)}, bf16[96,1536]{1,0:T(8,128)(2,1)S(1)}, u32[]{:S(2)}, u32[]{:S(2)}) collective-permute-start(bf16[96,1536]{1,0:T(8,128)(2,1)S(1)} %get-tuple-element.51), channel_id=1, source_target_pairs={{0,16},{4,20},{8,24},{12,28},{16,0},{20,4},{24,8},{28,12},{1,17},{... | collective-permute-start | bytes 884744 | tf_op jit(solution)/shard_map/ppermute | solution.py:604
  22.6 2.5 %norm_qkv.5 = (bf16[1536,1408]{1,0:T(8,128)(2,1)S(1)}, bf16[1536,1024]{1,0:T(8,128)(2,1)S(1)}, bf16[1536,128]{1,0:T(8,128)(2,1)S(1)}) custom-call(s32[15]{0:T(128)S(1)} %concatenate.3.info.refs_13_, bf16[192,1536]{1,0:T(8,128)(2,1)S(1)} %collective-permute-done.across_x.refs_0_, ...), custom_call_target="tpu_custom_call", output_to_operand_aliasing={{0}: (6, {}), {1}: (7, {}), {2}: (8, {})} | custom-call | flops 2491416576 | bytes 6488064 | tf_op jit(solution)/shard_map/norm_qkv/pallas_call | solution.py:279
  25.2 2.5 %norm_qkv.6 = (bf16[1536,1408]{1,0:T(8,128)(2,1)S(1)}, bf16[1536,1024]{1,0:T(8,128)(2,1)S(1)}, bf16[1536,128]{1,0:T(8,128)(2,1)S(1)}) custom-call(s32[15]{0:T(128)S(1)} %concatenate.3.info.refs_13_, bf16[192,1536]{1,0:T(8,128)(2,1)S(1)} %collective-permute-done.1.across_y.refs_0_, ...), custom_call_target="tpu_custom_call", output_to_operand_aliasing={{0}: (6, {}), {1}: (7, {}), {2}: (8, {})} | custom-call | flops 2491416576 | bytes 6488064 | tf_op jit(solution)/shard_map/norm_qkv/pallas_call | solution.py:279
  27.7 1.8 %collective-permute-done.3.refs_0_ = bf16[96,1536]{1,0:T(8,128)(2,1)S(1)} collective-permute-done((bf16[96,1536]{1,0:T(8,128)(2,1)S(1)}, bf16[96,1536]{1,0:T(8,128)(2,1)S(1)}, u32[]{:S(2)}, u32[]{:S(2)}) %collective-permute-start.3) | collective-permute-done | bytes 294944 | tf_op jit(solution)/shard_map/ppermute | solution.py:604
  29.5 1.2 %collective-permute-done.4.refs_1_ = bf16[96,1536]{1,0:T(8,128)(2,1)S(1)} collective-permute-done((bf16[96,1536]{1,0:T(8,128)(2,1)S(1)}, bf16[96,1536]{1,0:T(8,128)(2,1)S(1)}, u32[]{:S(2)}, u32[]{:S(2)}) %collective-permute-start.4) | collective-permute-done | bytes 294944 | tf_op jit(solution)/shard_map/ppermute | solution.py:604
  31.2 1.1 %collective-permute-done.7.refs_2_ = bf16[96,1536]{1,0:T(8,128)(2,1)S(1)} collective-permute-done((bf16[96,1536]{1,0:T(8,128)(2,1)S(1)}, bf16[96,1536]{1,0:T(8,128)(2,1)S(1)}, u32[]{:S(2)}, u32[]{:S(2)}) %collective-permute-start.7) | collective-permute-done | bytes 294944 | tf_op jit(solution)/shard_map/ppermute | solution.py:604
  32.7 2.5 %norm_qkv.7 = (bf16[1536,1408]{1,0:T(8,128)(2,1)S(1)}, bf16[1536,1024]{1,0:T(8,128)(2,1)S(1)}, bf16[1536,128]{1,0:T(8,128)(2,1)S(1)}) custom-call(s32[15]{0:T(128)S(1)} %concatenate.3.info.refs_13_, bf16[96,1536]{1,0:T(8,128)(2,1)S(1)} %collective-permute-done.3.refs_0_, ...), custom_call_target="tpu_custom_call", output_to_operand_aliasing={{0}: (8, {}), {1}: (9, {}), {2}: (10, {})} | custom-call | flops 2491416576 | bytes 6488064 | tf_op jit(solution)/shard_map/norm_qkv/pallas_call | solution.py:279
  35.2 4.3 %attention.2 = (bf16[1152,128]{1,0:T(8,128)(2,1)S(1)}, bf16[16,128]{1,0:T(8,128)(2,1)S(1)}) custom-call(s32[15]{0:T(128)S(1)} %concatenate.3.info.refs_13_, bf16[1536,128]{1,0:T(8,128)(2,1)S(1)} %get-tuple-element.70.labels, bf16[1536,1024]{1,0:T(8,128)(2,1)S(1)} %get-tuple-element.71.block), custom_call_target="tpu_custom_call" | custom-call | flops 3019898880 | bytes 3145728 | tf_op jit(solution)/shard_map/attention/pallas_call | solution.py:383
  40.5 5.7 %attention.3.refs_5_ = bf16[1152,128]{1,0:T(8,128)(2,1)S(1)} custom-call(s32[15]{0:T(128)S(1)} %concatenate.3.info.refs_13_, bf16[1536,128]{1,0:T(8,128)(2,1)S(1)} %get-tuple-element.70.labels, bf16[1536,1024]{1,0:T(8,128)(2,1)S(1)} %get-tuple-element.71.block), custom_call_target="tpu_custom_call" | custom-call | flops 3019898880 | bytes 3145728 | tf_op jit(solution)/shard_map/attention/pallas_call | solution.py:383
  46.3 2.4 %collective-permute-done.10.across_y.refs_9_ = bf16[1152,128]{1,0:T(8,128)(2,1)S(1)} collective-permute-done((bf16[1152,128]{1,0:T(8,128)(2,1)S(1)}, bf16[1152,128]{1,0:T(8,128)(2,1)S(1)}, u32[]{:S(2)}, u32[]{:S(2)}) %collective-permute-start.10) | collective-permute-done | bytes 294944 | tf_op jit(solution)/shard_map/ppermute | solution.py:604
  49.4 1.6 %collective-permute-start.16 = (bf16[576,128]{1,0:T(8,128)(2,1)S(1)}, bf16[576,128]{1,0:T(8,128)(2,1)S(1)}, u32[]{:S(2)}, u32[]{:S(2)}) collective-permute-start(bf16[576,128]{1,0:T(8,128)(2,1)S(1)} %get-tuple-element.74), channel_id=1, source_target_pairs={{0,16},{4,20},{8,24},{12,28},{16,0},{20,4},{24,8},{28,12},{1,17},{... | collective-permute-start | bytes 442376 | tf_op jit(solution)/shard_map/ppermute | solution.py:604
  51.5 1.4 %collective-permute-start.23 = (bf16[1152,128]{1,0:T(8,128)(2,1)S(1)}, bf16[1152,128]{1,0:T(8,128)(2,1)S(1)}, u32[]{:S(2)}, u32[]{:S(2)}) collective-permute-start(bf16[1152,128]{1,0:T(8,128)(2,1)S(1)} %attention.3.refs_5_), channel_id=1, source_target_pairs={{0,24},{4,28},{8,16},{12,20},{16,8},{20,12},{24,0},{28,4},{1,25},{... | collective-permute-start | bytes 884744 | tf_op jit(solution)/shard_map/ppermute | solution.py:604
  53.0 2.4 %collective-permute-done.16.refs_11_ = bf16[576,128]{1,0:T(8,128)(2,1)S(1)} collective-permute-done((bf16[576,128]{1,0:T(8,128)(2,1)S(1)}, bf16[576,128]{1,0:T(8,128)(2,1)S(1)}, u32[]{:S(2)}, u32[]{:S(2)}) %collective-permute-start.16) | collective-permute-done | bytes 147488 | tf_op jit(solution)/shard_map/ppermute | solution.py:604
  55.3 1.5 %collective-permute-start.21 = (bf16[1152,128]{1,0:T(8,128)(2,1)S(1)}, bf16[1152,128]{1,0:T(8,128)(2,1)S(1)}, u32[]{:S(2)}, u32[]{:S(2)}) collective-permute-start(bf16[1152,128]{1,0:T(8,128)(2,1)S(1)} %attention.3.refs_5_), channel_id=1, source_target_pairs={{0,16},{4,20},{8,24},{12,28},{16,0},{20,4},{24,8},{28,12},{1,17},{... | collective-permute-start | bytes 884744 | tf_op jit(solution)/shard_map/ppermute | solution.py:604
  59.9 6.5 %out_merge.2.refs_15_ = bf16[192,448]{1,0:T(8,128)(2,1)S(1)} custom-call(bf16[1536,1408]{1,0:T(8,128)(2,1)S(1)} %get-tuple-element.63.refs_0_, bf16[1536,1408]{1,0:T(8,128)(2,1)S(1)} %get-tuple-element.48.refs_1_, f32[1,1408]{1,0:T(1,128)S(1)} %get-tuple-element.64.refs_2_, bf16[448,5632]{1,0:T(8,128)(2,1)S(1)} %get-tuple-element.65.refs_3_, ...), custom_call_target="tpu_custom_call" | custom-call | bytes 1024 | tf_op jit(solution)/shard_map/out_merge/pallas_call | solution.py:543
  66.8 1.9 %collective-permute-done.21.refs_9_ = bf16[1152,128]{1,0:T(8,128)(2,1)S(1)} collective-permute-done((bf16[1152,128]{1,0:T(8,128)(2,1)S(1)}, bf16[1152,128]{1,0:T(8,128)(2,1)S(1)}, u32[]{:S(2)}, u32[]{:S(2)}) %collective-permute-start.21) | collective-permute-done | bytes 294944 | tf_op jit(solution)/shard_map/ppermute | solution.py:604
  70.7 7.7 %out_merge.3 = (bf16[672,128]{1,0:T(8,128)(2,1)S(1)}, bf16[672,128]{1,0:T(8,128)(2,1)S(1)}, bf16[672,128]{1,0:T(8,128)(2,1)S(1)}, bf16[672,128]{1,0:T(8,128)(2,1)S(1)}) custom-call(bf16[1536,1408]{1,0:T(8,128)(2,1)S(1)} %get-tuple-element.63.refs_0_, bf16[1536,1408]{1,0:T(8,128)(2,1)S(1)} %get-tuple-element.48.refs_1_, ...), custom_call_target="tpu_custom_call" | custom-call | bytes 1024 | tf_op jit(solution)/shard_map/out_merge/pallas_call | solution.py:543
  78.4 3.6 %collective-permute-start.27 = (bf16[672,128]{1,0:T(8,128)(2,1)S(1)}, bf16[672,128]{1,0:T(8,128)(2,1)S(1)}, u32[]{:S(2)}, u32[]{:S(2)}) collective-permute-start(bf16[672,128]{1,0:T(8,128)(2,1)S(1)} %get-tuple-element.83), channel_id=1, source_target_pairs={{0,3},{1,2},{2,1},{3,0},{4,7},{5,6},{6,5},{7,4},{8,11},{9,10},{10,... | collective-permute-start | bytes 516104 | tf_op jit(solution)/shard_map/ppermute | solution.py:752
  82.9 1.3 %place_rows.4.refs_0_ = bf16[4,192,448]{2,1,0:T(8,128)(2,1)} custom-call(s32[15]{0:T(128)S(1)} %concatenate.3.info.refs_13_, bf16[672,128]{1,0:T(8,128)(2,1)S(1)} %get-tuple-element.84.block), custom_call_target="tpu_custom_call" | custom-call | bytes 344064 | tf_op jit(solution)/shard_map/place_rows/pallas_call | solution.py:583
  84.2 3.4 %collective-permute-done.27.block = bf16[672,128]{1,0:T(8,128)(2,1)S(1)} collective-permute-done((bf16[672,128]{1,0:T(8,128)(2,1)S(1)}, bf16[672,128]{1,0:T(8,128)(2,1)S(1)}, u32[]{:S(2)}, u32[]{:S(2)}) %collective-permute-start.27) | collective-permute-done | bytes 172064 | tf_op jit(solution)/shard_map/ppermute | solution.py:752
  87.6 1.3 %place_rows.5.refs_0_ = bf16[4,192,448]{2,1,0:T(8,128)(2,1)} custom-call(s32[15]{0:T(128)S(1)} %concatenate.3.info.refs_13_, bf16[672,128]{1,0:T(8,128)(2,1)S(1)} %collective-permute-done.27.block, bf16[4,192,448]{2,1,0:T(8,128)(2,1)} %place_rows.4.refs_0_), custom_call_target="tpu_custom_call", output_to_operand_aliasing={{}: (2, {})} | custom-call | bytes 344064 | tf_op jit(solution)/shard_map/place_rows/pallas_call | solution.py:583
  88.9 2.7 %collective-permute-done.26.block = bf16[672,128]{1,0:T(8,128)(2,1)S(1)} collective-permute-done((bf16[672,128]{1,0:T(8,128)(2,1)S(1)}, bf16[672,128]{1,0:T(8,128)(2,1)S(1)}, u32[]{:S(2)}, u32[]{:S(2)}) %collective-permute-start.26) | collective-permute-done | bytes 172064 | tf_op jit(solution)/shard_map/ppermute | solution.py:752
  91.5 1.3 %place_rows.6.refs_0_ = bf16[4,192,448]{2,1,0:T(8,128)(2,1)} custom-call(s32[15]{0:T(128)S(1)} %concatenate.3.info.refs_13_, bf16[672,128]{1,0:T(8,128)(2,1)S(1)} %collective-permute-done.26.block, bf16[4,192,448]{2,1,0:T(8,128)(2,1)} %place_rows.5.refs_0_), custom_call_target="tpu_custom_call", output_to_operand_aliasing={{}: (2, {})} | custom-call | bytes 344064 | tf_op jit(solution)/shard_map/place_rows/pallas_call | solution.py:583
  92.8 4.1 %collective-permute-done.25.block = bf16[672,128]{1,0:T(8,128)(2,1)S(1)} collective-permute-done((bf16[672,128]{1,0:T(8,128)(2,1)S(1)}, bf16[672,128]{1,0:T(8,128)(2,1)S(1)}, u32[]{:S(2)}, u32[]{:S(2)}) %collective-permute-start.25) | collective-permute-done | bytes 172064 | tf_op jit(solution)/shard_map/ppermute | solution.py:752
  97.0 1.3 %place_rows.7 = bf16[4,192,448]{2,1,0:T(8,128)(2,1)} custom-call(s32[15]{0:T(128)S(1)} %concatenate.3.info.refs_13_, bf16[672,128]{1,0:T(8,128)(2,1)S(1)} %collective-permute-done.25.block, bf16[4,192,448]{2,1,0:T(8,128)(2,1)} %place_rows.6.refs_0_), custom_call_target="tpu_custom_call", output_to_operand_aliasing={{}: (2, {})} | custom-call | bytes 344064 | tf_op jit(solution)/shard_map/place_rows/pallas_call | solution.py:583
  (49 shorter events, 13.8 us)
Async XLA Ops:
  1.5 12.5 %collective-permute-start.2 = (bf16[192,1536]{1,0:T(8,128)(2,1)S(1)}, bf16[192,1536]{1,0:T(8,128)(2,1)S(1)}, u32[]{:S(2)}, u32[]{:S(2)}) collective-permute-start(bf16[192,1536]{1,0:T(8,128)(2,1)S(1)} %payload.1.refs_0_), channel_id=1, source_target_pairs={{0,4},{4,0},{8,12},{12,8},{16,20},{20,16},{24,28},{28,24},{1,5},{5... | collective-permute-start | bytes 1769480 | tf_op jit(solution)/shard_map/ppermute | solution.py:604
  2.0 16.5 %collective-permute-start = (bf16[192,1536]{1,0:T(8,128)(2,1)S(1)}, bf16[192,1536]{1,0:T(8,128)(2,1)S(1)}, u32[]{:S(2)}, u32[]{:S(2)}) collective-permute-start(bf16[192,1536]{1,0:T(8,128)(2,1)S(1)} %payload.1.refs_0_), channel_id=1, source_target_pairs={{0,8},{4,12},{8,0},{12,4},{16,24},{20,28},{24,16},{28,20},{1,9},{5... | collective-permute-start | bytes 1769480 | tf_op jit(solution)/shard_map/ppermute | solution.py:604
  4.6 15.4 %collective-permute-start.1 = (bf16[192,1536]{1,0:T(8,128)(2,1)S(1)}, bf16[192,1536]{1,0:T(8,128)(2,1)S(1)}, u32[]{:S(2)}, u32[]{:S(2)}) collective-permute-start(bf16[192,1536]{1,0:T(8,128)(2,1)S(1)} %payload.1.refs_0_), channel_id=1, source_target_pairs={{0,16},{4,20},{8,24},{12,28},{16,0},{20,4},{24,8},{28,12},{1,17},{... | collective-permute-start | bytes 1769480 | tf_op jit(solution)/shard_map/ppermute | solution.py:604
  6.8 0.7 copy-start.1
  7.5 0.7 copy-start.2
  8.2 0.7 copy-start.3
  8.9 5.1 %copy-start = (bf16[128,512]{1,0:T(8,128)(2,1)S(1)}, bf16[128,512]{1,0:T(8,128)(2,1)}, u32[]{:S(2)}) copy-start(bf16[128,512]{1,0:T(8,128)(2,1)} %constant.48.clone.refs_2_.refs_4_) | copy-start | bytes 393220
  20.0 2.7 %collective-permute-start.6 = (bf16[192,1536]{1,0:T(8,128)(2,1)S(1)}, bf16[192,1536]{1,0:T(8,128)(2,1)S(1)}, u32[]{:S(2)}, u32[]{:S(2)}) collective-permute-start(bf16[192,1536]{1,0:T(8,128)(2,1)S(1)} %collective-permute-done.across_x.refs_0_), channel_id=1, source_target_pairs={{0,4},{4,0},{8,12},{12,8},{16,20},{20,16},{24,28},{28,24},{1,5},{5... | collective-permute-start | bytes 1769480 | tf_op jit(solution)/shard_map/ppermute | solution.py:604
  20.0 5.2 %collective-permute-start.5 = (bf16[192,1536]{1,0:T(8,128)(2,1)S(1)}, bf16[192,1536]{1,0:T(8,128)(2,1)S(1)}, u32[]{:S(2)}, u32[]{:S(2)}) collective-permute-start(bf16[192,1536]{1,0:T(8,128)(2,1)S(1)} %collective-permute-done.1.across_y.refs_0_), channel_id=1, source_target_pairs={{0,4},{4,0},{8,12},{12,8},{16,20},{20,16},{24,28},{28,24},{1,5},{5... | collective-permute-start | bytes 1769480 | tf_op jit(solution)/shard_map/ppermute | solution.py:604
  20.5 9.0 %collective-permute-start.3 = (bf16[96,1536]{1,0:T(8,128)(2,1)S(1)}, bf16[96,1536]{1,0:T(8,128)(2,1)S(1)}, u32[]{:S(2)}, u32[]{:S(2)}) collective-permute-start(bf16[96,1536]{1,0:T(8,128)(2,1)S(1)} %get-tuple-element.51), channel_id=1, source_target_pairs={{0,16},{4,20},{8,24},{12,28},{16,0},{20,4},{24,8},{28,12},{1,17},{... | collective-permute-start | bytes 884744 | tf_op jit(solution)/shard_map/ppermute | solution.py:604
  22.1 8.6 %collective-permute-start.4 = (bf16[96,1536]{1,0:T(8,128)(2,1)S(1)}, bf16[96,1536]{1,0:T(8,128)(2,1)S(1)}, u32[]{:S(2)}, u32[]{:S(2)}) collective-permute-start(bf16[96,1536]{1,0:T(8,128)(2,1)S(1)} %get-tuple-element.52), channel_id=1, source_target_pairs={{0,8},{4,12},{8,0},{12,4},{16,24},{20,28},{24,16},{28,20},{1,9},{5... | collective-permute-start | bytes 884744 | tf_op jit(solution)/shard_map/ppermute | solution.py:604
  30.7 1.6 %collective-permute-start.7 = (bf16[96,1536]{1,0:T(8,128)(2,1)S(1)}, bf16[96,1536]{1,0:T(8,128)(2,1)S(1)}, u32[]{:S(2)}, u32[]{:S(2)}) collective-permute-start(bf16[96,1536]{1,0:T(8,128)(2,1)S(1)} %collective-permute-done.3.refs_0_), channel_id=1, source_target_pairs={{0,4},{4,0},{8,12},{12,8},{16,20},{20,16},{24,28},{28,24},{1,5},{5... | collective-permute-start | bytes 884744 | tf_op jit(solution)/shard_map/ppermute | solution.py:604
  30.7 2.0 %collective-permute-start.8 = (bf16[96,1536]{1,0:T(8,128)(2,1)S(1)}, bf16[96,1536]{1,0:T(8,128)(2,1)S(1)}, u32[]{:S(2)}, u32[]{:S(2)}) collective-permute-start(bf16[96,1536]{1,0:T(8,128)(2,1)S(1)} %collective-permute-done.4.refs_1_), channel_id=1, source_target_pairs={{0,4},{4,0},{8,12},{12,8},{16,20},{20,16},{24,28},{28,24},{1,5},{5... | collective-permute-start | bytes 884744 | tf_op jit(solution)/shard_map/ppermute | solution.py:604
  39.5 9.1 %collective-permute-start.10 = (bf16[1152,128]{1,0:T(8,128)(2,1)S(1)}, bf16[1152,128]{1,0:T(8,128)(2,1)S(1)}, u32[]{:S(2)}, u32[]{:S(2)}) collective-permute-start(bf16[1152,128]{1,0:T(8,128)(2,1)S(1)} %get-tuple-element.69.refs_5_), channel_id=1, source_target_pairs={{0,16},{4,20},{8,24},{12,28},{16,0},{20,4},{24,8},{28,12},{1,17},{... | collective-permute-start | bytes 884744 | tf_op jit(solution)/shard_map/ppermute | solution.py:604
  40.1 8.8 %collective-permute-start.9 = (bf16[1152,128]{1,0:T(8,128)(2,1)S(1)}, bf16[1152,128]{1,0:T(8,128)(2,1)S(1)}, u32[]{:S(2)}, u32[]{:S(2)}) collective-permute-start(bf16[1152,128]{1,0:T(8,128)(2,1)S(1)} %get-tuple-element.69.refs_5_), channel_id=1, source_target_pairs={{0,8},{4,12},{8,0},{12,4},{16,24},{20,28},{24,16},{28,20},{1,9},{5... | collective-permute-start | bytes 884744 | tf_op jit(solution)/shard_map/ppermute | solution.py:604
  40.5 11.0 %collective-permute-start.13 = (bf16[1152,128]{1,0:T(8,128)(2,1)S(1)}, bf16[1152,128]{1,0:T(8,128)(2,1)S(1)}, u32[]{:S(2)}, u32[]{:S(2)}) collective-permute-start(bf16[1152,128]{1,0:T(8,128)(2,1)S(1)} %get-tuple-element.69.refs_5_), channel_id=1, source_target_pairs={{0,4},{4,0},{8,12},{12,8},{16,20},{20,16},{24,28},{28,24},{1,5},{5... | collective-permute-start | bytes 884744 | tf_op jit(solution)/shard_map/ppermute | solution.py:604
  48.9 9.4 %collective-permute-start.14 = (bf16[1152,128]{1,0:T(8,128)(2,1)S(1)}, bf16[1152,128]{1,0:T(8,128)(2,1)S(1)}, u32[]{:S(2)}, u32[]{:S(2)}) collective-permute-start(bf16[1152,128]{1,0:T(8,128)(2,1)S(1)} %collective-permute-done.9.across_x.refs_7_), channel_id=1, source_target_pairs={{0,4},{4,0},{8,12},{12,8},{16,20},{20,16},{24,28},{28,24},{1,5},{5... | collective-permute-start | bytes 884744 | tf_op jit(solution)/shard_map/ppermute | solution.py:604
  48.9 9.4 %collective-permute-start.15 = (bf16[1152,128]{1,0:T(8,128)(2,1)S(1)}, bf16[1152,128]{1,0:T(8,128)(2,1)S(1)}, u32[]{:S(2)}, u32[]{:S(2)}) collective-permute-start(bf16[1152,128]{1,0:T(8,128)(2,1)S(1)} %collective-permute-done.10.across_y.refs_9_), channel_id=1, source_target_pairs={{0,4},{4,0},{8,12},{12,8},{16,20},{20,16},{24,28},{28,24},{1,5},{5... | collective-permute-start | bytes 884744 | tf_op jit(solution)/shard_map/ppermute | solution.py:604
  49.4 5.9 %collective-permute-start.16 = (bf16[576,128]{1,0:T(8,128)(2,1)S(1)}, bf16[576,128]{1,0:T(8,128)(2,1)S(1)}, u32[]{:S(2)}, u32[]{:S(2)}) collective-permute-start(bf16[576,128]{1,0:T(8,128)(2,1)S(1)} %get-tuple-element.74), channel_id=1, source_target_pairs={{0,16},{4,20},{8,24},{12,28},{16,0},{20,4},{24,8},{28,12},{1,17},{... | collective-permute-start | bytes 442376 | tf_op jit(solution)/shard_map/ppermute | solution.py:604
  51.0 6.8 %collective-permute-start.17 = (bf16[576,128]{1,0:T(8,128)(2,1)S(1)}, bf16[576,128]{1,0:T(8,128)(2,1)S(1)}, u32[]{:S(2)}, u32[]{:S(2)}) collective-permute-start(bf16[576,128]{1,0:T(8,128)(2,1)S(1)} %get-tuple-element.75), channel_id=1, source_target_pairs={{0,8},{4,12},{8,0},{12,4},{16,24},{20,28},{24,16},{28,20},{1,9},{5... | collective-permute-start | bytes 442376 | tf_op jit(solution)/shard_map/ppermute | solution.py:604
  51.5 14.9 %collective-permute-start.23 = (bf16[1152,128]{1,0:T(8,128)(2,1)S(1)}, bf16[1152,128]{1,0:T(8,128)(2,1)S(1)}, u32[]{:S(2)}, u32[]{:S(2)}) collective-permute-start(bf16[1152,128]{1,0:T(8,128)(2,1)S(1)} %attention.3.refs_5_), channel_id=1, source_target_pairs={{0,24},{4,28},{8,16},{12,20},{16,8},{20,12},{24,0},{28,4},{1,25},{... | collective-permute-start | bytes 884744 | tf_op jit(solution)/shard_map/ppermute | solution.py:604
  55.3 13.4 %collective-permute-start.21 = (bf16[1152,128]{1,0:T(8,128)(2,1)S(1)}, bf16[1152,128]{1,0:T(8,128)(2,1)S(1)}, u32[]{:S(2)}, u32[]{:S(2)}) collective-permute-start(bf16[1152,128]{1,0:T(8,128)(2,1)S(1)} %attention.3.refs_5_), channel_id=1, source_target_pairs={{0,16},{4,20},{8,24},{12,28},{16,0},{20,4},{24,8},{28,12},{1,17},{... | collective-permute-start | bytes 884744 | tf_op jit(solution)/shard_map/ppermute | solution.py:604
  57.8 11.4 %collective-permute-start.12 = (bf16[1152,128]{1,0:T(8,128)(2,1)S(1)}, bf16[1152,128]{1,0:T(8,128)(2,1)S(1)}, u32[]{:S(2)}, u32[]{:S(2)}) collective-permute-start(bf16[1152,128]{1,0:T(8,128)(2,1)S(1)} %attention.3.refs_5_), channel_id=1, source_target_pairs={{0,8},{4,12},{8,0},{12,4},{16,24},{20,28},{24,16},{28,20},{1,9},{5... | collective-permute-start | bytes 884744 | tf_op jit(solution)/shard_map/ppermute | solution.py:604
  58.3 1.4 %collective-permute-start.18 = (bf16[576,128]{1,0:T(8,128)(2,1)S(1)}, bf16[576,128]{1,0:T(8,128)(2,1)S(1)}, u32[]{:S(2)}, u32[]{:S(2)}) collective-permute-start(bf16[576,128]{1,0:T(8,128)(2,1)S(1)} %collective-permute-done.16.refs_11_), channel_id=1, source_target_pairs={{0,4},{4,0},{8,12},{12,8},{16,20},{20,16},{24,28},{28,24},{1,5},{5... | collective-permute-start | bytes 442376 | tf_op jit(solution)/shard_map/ppermute | solution.py:604
  58.3 1.6 %collective-permute-start.19 = (bf16[576,128]{1,0:T(8,128)(2,1)S(1)}, bf16[576,128]{1,0:T(8,128)(2,1)S(1)}, u32[]{:S(2)}, u32[]{:S(2)}) collective-permute-start(bf16[576,128]{1,0:T(8,128)(2,1)S(1)} %collective-permute-done.17.refs_12_), channel_id=1, source_target_pairs={{0,4},{4,0},{8,12},{12,8},{16,20},{20,16},{24,28},{28,24},{1,5},{5... | collective-permute-start | bytes 442376 | tf_op jit(solution)/shard_map/ppermute | solution.py:604
  59.7 9.5 %collective-permute-start.11 = (bf16[1152,128]{1,0:T(8,128)(2,1)S(1)}, bf16[1152,128]{1,0:T(8,128)(2,1)S(1)}, u32[]{:S(2)}, u32[]{:S(2)}) collective-permute-start(bf16[1152,128]{1,0:T(8,128)(2,1)S(1)} %attention.3.refs_5_), channel_id=1, source_target_pairs={{0,4},{4,0},{8,12},{12,8},{16,20},{20,16},{24,28},{28,24},{1,5},{5... | collective-permute-start | bytes 884744 | tf_op jit(solution)/shard_map/ppermute | solution.py:604
  66.4 2.8 %collective-permute-start.24 = (bf16[1152,128]{1,0:T(8,128)(2,1)S(1)}, bf16[1152,128]{1,0:T(8,128)(2,1)S(1)}, u32[]{:S(2)}, u32[]{:S(2)}) collective-permute-start(bf16[1152,128]{1,0:T(8,128)(2,1)S(1)} %collective-permute-done.23.refs_11_), channel_id=1, source_target_pairs={{0,4},{4,0},{8,12},{12,8},{16,20},{20,16},{24,28},{28,24},{1,5},{5... | collective-permute-start | bytes 884744 | tf_op jit(solution)/shard_map/ppermute | solution.py:604
  68.7 1.6 %collective-permute-start.22 = (bf16[1152,128]{1,0:T(8,128)(2,1)S(1)}, bf16[1152,128]{1,0:T(8,128)(2,1)S(1)}, u32[]{:S(2)}, u32[]{:S(2)}) collective-permute-start(bf16[1152,128]{1,0:T(8,128)(2,1)S(1)} %collective-permute-done.21.refs_9_), channel_id=1, source_target_pairs={{0,4},{4,0},{8,12},{12,8},{16,20},{20,16},{24,28},{28,24},{1,5},{5... | collective-permute-start | bytes 884744 | tf_op jit(solution)/shard_map/ppermute | solution.py:604
  69.2 1.6 %collective-permute-start.20 = (bf16[1152,128]{1,0:T(8,128)(2,1)S(1)}, bf16[1152,128]{1,0:T(8,128)(2,1)S(1)}, u32[]{:S(2)}, u32[]{:S(2)}) collective-permute-start(bf16[1152,128]{1,0:T(8,128)(2,1)S(1)} %collective-permute-done.12.refs_7_), channel_id=1, source_target_pairs={{0,4},{4,0},{8,12},{12,8},{16,20},{20,16},{24,28},{28,24},{1,5},{5... | collective-permute-start | bytes 884744 | tf_op jit(solution)/shard_map/ppermute | solution.py:604
  78.4 9.1 %collective-permute-start.27 = (bf16[672,128]{1,0:T(8,128)(2,1)S(1)}, bf16[672,128]{1,0:T(8,128)(2,1)S(1)}, u32[]{:S(2)}, u32[]{:S(2)}) collective-permute-start(bf16[672,128]{1,0:T(8,128)(2,1)S(1)} %get-tuple-element.83), channel_id=1, source_target_pairs={{0,3},{1,2},{2,1},{3,0},{4,7},{5,6},{6,5},{7,4},{8,11},{9,10},{10,... | collective-permute-start | bytes 516104 | tf_op jit(solution)/shard_map/ppermute | solution.py:752
  82.1 9.4 %collective-permute-start.26 = (bf16[672,128]{1,0:T(8,128)(2,1)S(1)}, bf16[672,128]{1,0:T(8,128)(2,1)S(1)}, u32[]{:S(2)}, u32[]{:S(2)}) collective-permute-start(bf16[672,128]{1,0:T(8,128)(2,1)S(1)} %get-tuple-element.82), channel_id=1, source_target_pairs={{0,1},{1,0},{2,3},{3,2},{4,5},{5,4},{6,7},{7,6},{8,9},{9,8},{10,11... | collective-permute-start | bytes 516104 | tf_op jit(solution)/shard_map/ppermute | solution.py:752
  82.1 14.9 %collective-permute-start.25 = (bf16[672,128]{1,0:T(8,128)(2,1)S(1)}, bf16[672,128]{1,0:T(8,128)(2,1)S(1)}, u32[]{:S(2)}, u32[]{:S(2)}) collective-permute-start(bf16[672,128]{1,0:T(8,128)(2,1)S(1)} %get-tuple-element.81), channel_id=1, source_target_pairs={{0,2},{1,3},{2,0},{3,1},{4,6},{5,7},{6,4},{7,5},{8,10},{9,11},{10,... | collective-permute-start | bytes 516104 | tf_op jit(solution)/shard_map/ppermute | solution.py:752

commit v15 on v14

--- a/solution.py
+++ b/solution.py
@@ -147,7 +147,6 @@
 
 
 LANES = 128
-CHIP, CORE, PACK, IDS = 0, 1, 2, 3
 BLOCK = 512
 POSITIONS = 64
 FAR_APART = -(2.0**100)
@@ -215,17 +214,18 @@
     )(*map(in_hbm, operands))
 
 
-def qkv_kernel(count, flip, info, *refs):
+def qkv_kernel(count, flip, *refs):
+    me = lax.axis_index("seq")
     first, second = refs[:count], refs[count : 2 * count]
     table, gain, weight = refs[2 * count : 2 * count + 3]
     inputs_out, qkv_out, label_out = refs[-3:]
     mine, other = stacked(first), stacked(second)
-    leads = info[CORE] == 0
+    leads = me % 2 == 0
     ahead = jnp.where(leads, mine, other)
     behind = jnp.where(leads, other, mine)
     both = jnp.concatenate([ahead, behind], axis=0)
     rows = both.shape[0]
-    at = pl.ds(pl.multiple_of((info[CHIP] ^ flip) * rows, rows), rows)
+    at = pl.ds(pl.multiple_of((me // 2 ^ flip) * rows, rows), rows)
     inputs_out[at, :] = both[:, :D]
     label_out[at, :] = both[:, D:]
     labels = both[:, D:].astype(jnp.float32)
@@ -270,7 +270,7 @@
         qkv_out[at, number * LANES : (number + 1) * LANES] = part.astype(jnp.bfloat16)
 
 
-def qkv_call(info, flip, first, second, table, gain, weight, earlier, total):
+def qkv_call(flip, first, second, table, gain, weight, earlier, total):
     rows = 2 * sum(piece.shape[0] for piece in first)
     widths = (D, 8 * LANES, LANES)
     operands = [*first, *second, table, gain, in_vmem(weight)]
@@ -278,11 +278,10 @@
     held = [in_vmem(one) for one in earlier]
     return pl.pallas_call(
         functools.partial(qkv_kernel, len(first), flip),
-        in_specs=[pl.BlockSpec(memory_space=pltpu.SMEM)]
-        + [vmem] * (len(operands) + len(earlier)),
+        in_specs=[vmem] * (len(operands) + len(earlier)),
         out_specs=[vmem] * len(widths),
         out_shape=[pltpu.VMEM((total, width), jnp.bfloat16) for width in widths],
-        input_output_aliases={1 + len(operands) + i: i for i in range(len(earlier))},
+        input_output_aliases={len(operands) + i: i for i in range(len(earlier))},
         compiler_params=pltpu.CompilerParams(vmem_limit_bytes=14 << 20),
         cost_estimate=pl.CostEstimate(
             flops=6 * rows * D * weight.shape[0],
@@ -290,7 +289,7 @@
             transcendentals=rows,
         ),
         name="norm_qkv",
-    )(info, *operands, *held)
+    )(*operands, *held)
 
 
 def segment_row(labels):
@@ -303,7 +302,8 @@
     )
 
 
-def attention_kernel(start, first_owner, images, info, labels, block, *refs):
+def attention_kernel(start, images, labels, block, *refs):
+    owners, refs = (refs[0], refs[1:]) if images else (None, refs)
     out, *rest = refs
     scores, high = rest[-2:]
     rows = high.shape[1]
@@ -366,7 +366,7 @@
         for image in range(images):
             below = jnp.sum(jnp.where(one_row < image, 0.25, 0.0), axis=1, keepdims=True)
             inside = jnp.sum(jnp.where(one_row == image, 0.25, 0.0), axis=1, keepdims=True)
-            here = row == info[first_owner + image]
+            here = row == owners[0, image]
             for place, number in enumerate((below, inside)):
                 upper = jnp.floor(number * (1.0 / 16))
                 found = jnp.where(here & (lane == 2 * place), upper, found)
@@ -374,15 +374,15 @@
         note[...] = found.astype(jnp.bfloat16)
 
 
-def attention_call(start, rows, first_owner, info, labels, block, noted):
+def attention_call(start, rows, labels, block, owners):
     total = block.shape[0]
     vmem = pl.BlockSpec(memory_space=pltpu.VMEM)
     shapes = [jax.ShapeDtypeStruct((rows + rows // 2, LANES), jnp.bfloat16)]
-    if noted:
+    if owners:
         shapes.append(jax.ShapeDtypeStruct((16, LANES), jnp.bfloat16))
     return pl.pallas_call(
-        functools.partial(attention_kernel, start, first_owner, info.shape[0] - first_owner),
-        in_specs=[pl.BlockSpec(memory_space=pltpu.SMEM), vmem, vmem],
+        functools.partial(attention_kernel, start, owners[0].shape[1] if owners else 0),
+        in_specs=[vmem, vmem] + [pl.BlockSpec(memory_space=pltpu.SMEM)] * len(owners),
         out_specs=[vmem] * len(shapes),
         out_shape=shapes,
         scratch_shapes=[
@@ -396,10 +396,10 @@
             transcendentals=rows * total,
         ),
         name="attention",
-    )(info, in_vmem(labels), in_vmem(block))
-
-
-def prepare_kernel(shards, info, out_weight, merge_weight, qkv_weight, spread, *refs):
+    )(in_vmem(labels), in_vmem(block), *owners)
+
+
+def prepare_kernel(shards, ids, out_weight, merge_weight, qkv_weight, spread, *refs):
     *rows, out, merge, qkv, qkv_buffer, spread_buffer, sems = refs
     for row, row_out in zip(rows[: len(rows) // 2], rows[len(rows) // 2 :]):
         row_out[...] = row[...].astype(jnp.float32)[None, :]
@@ -407,7 +407,7 @@
     copies = [(qkv_weight, qkv_buffer), (spread, spread_buffer)]
     out[shards * LANES :] = jnp.zeros((shards // 2 * LANES, D), jnp.bfloat16)
     for place in range(shards):
-        start = pl.multiple_of(info[IDS + place] * (2 * HD), 16)
+        start = pl.multiple_of(ids[place] * (2 * HD), 16)
         to = (shards + place // 2) * LANES + place % 2 * rest
         copies.append(
             (out_weight.at[pl.ds(start, LANES), :], out.at[pl.ds(place * LANES, LANES), :])
@@ -429,7 +429,7 @@
         copy.wait()
 
 
-def prepare_call(shards, info, out_weight, merge_weight, qkv_weight, spread, rows):
+def prepare_call(shards, ids, out_weight, merge_weight, qkv_weight, spread, rows):
     anywhere = pl.BlockSpec(memory_space=pl.ANY)
     vmem = pl.BlockSpec(memory_space=pltpu.VMEM)
     operands = (out_weight, merge_weight, qkv_weight, spread)
@@ -454,7 +454,7 @@
             transcendentals=0,
         ),
         name="prepare",
-    )(info, *map(in_hbm, operands), *rows)
+    )(ids, *map(in_hbm, operands), *rows)
 
 
 def merge_kernel(start, counts, packs, last, *refs):
@@ -501,7 +501,8 @@
     if not last:
         refs[0][...] = total
         return
-    info, note, *earlier = refs[:-packs]
+    note, *earlier = refs[:-packs]
+    me = lax.axis_index("pack")
     outs = refs[-packs:]
     total = jnp.concatenate([*[one[...] for one in earlier], total], axis=0)
     whole = total.shape[1] // LANES
@@ -511,7 +512,7 @@
     slot = lax.broadcasted_iota(jnp.int32, (most, total.shape[0]), 0)
     row = lax.broadcasted_iota(jnp.int32, (most, total.shape[0]), 1)
     for place, out in enumerate(outs):
-        found = jnp.where(note_row == (info[PACK] ^ place), notes, 0.0)
+        found = jnp.where(note_row == (me ^ place), notes, 0.0)
         found = jnp.sum(found, axis=0, keepdims=True)
         first = (16.0 * found[:, :1] + found[:, 1:2]).astype(jnp.int32)
         length = (16.0 * found[:, 2:3] + found[:, 3:4]).astype(jnp.int32)
@@ -536,9 +537,9 @@
     specs = [vmem] * len(operands)
     shapes = [jax.ShapeDtypeStruct((groups, width), jnp.bfloat16)]
     if route:
-        me, most, *others = route
-        operands += [me, *others]
-        specs += [pl.BlockSpec(memory_space=pltpu.SMEM)] + [vmem] * len(others)
+        most, *others = route
+        operands += others
+        specs += [vmem] * len(others)
         shapes = [jax.ShapeDtypeStruct((most * width // LANES, LANES), jnp.bfloat16)] * packs
     return pl.pallas_call(
         functools.partial(
@@ -561,7 +562,7 @@
     )(*operands)
 
 
-def place_kernel(place, info, block, *refs):
+def place_kernel(place, block, *refs):
     out, rows, sem = refs[-3:]
     most, width = rows.shape
     whole = width // LANES
@@ -573,30 +574,26 @@
         ]
     rows[:half, whole * LANES :] = block[whole * most :, :middle]
     rows[half:, whole * LANES :] = block[whole * most :, middle:]
-    copy = pltpu.make_async_copy(rows, out.at[info[PACK] ^ place], sem)
+    copy = pltpu.make_async_copy(rows, out.at[lax.axis_index("pack") ^ place], sem)
     copy.start()
     copy.wait()
 
 
-def place_call(info, place, block, earlier, shape):
+def place_call(place, block, earlier, shape):
     anywhere = pl.BlockSpec(memory_space=pl.ANY)
     return pl.pallas_call(
         functools.partial(place_kernel, place),
-        in_specs=[
-            pl.BlockSpec(memory_space=pltpu.SMEM),
-            pl.BlockSpec(memory_space=pltpu.VMEM),
-        ]
-        + [anywhere] * len(earlier),
+        in_specs=[pl.BlockSpec(memory_space=pltpu.VMEM)] + [anywhere] * len(earlier),
         out_specs=anywhere,
         out_shape=pltpu.HBM(shape, jnp.bfloat16),
         scratch_shapes=[pltpu.VMEM(shape[1:], jnp.bfloat16), pltpu.SemaphoreType.DMA],
-        input_output_aliases={2: 0} if earlier else {},
+        input_output_aliases={1: 0} if earlier else {},
         compiler_params=pltpu.CompilerParams(vmem_limit_bytes=4 << 20),
         cost_estimate=pl.CostEstimate(
             flops=0, bytes_accessed=4 * shape[1] * shape[2], transcendentals=0
         ),
         name="place_rows",
-    )(info, block, *map(in_hbm, earlier))
+    )(block, *map(in_hbm, earlier))
 
 
 def send_seq(value, flip):
@@ -694,7 +691,6 @@
     images = image_owner.shape[1]
     total = local_rows * shards
     me = lax.axis_index("seq").astype(jnp.int32)
-    pack = lax.axis_index("pack").astype(jnp.int32)
 
     value = payload_call(segment_ids, patch_rows, patch_column, patch_mask, mask_embed, patches)
     own_swap, across_x, across_y = near_shards(value)
@@ -702,12 +698,10 @@
     order = weight_order(heads_here)
     spread = (order[:, None] == np.arange(qkv_weight.shape[1])[None, :]).astype(jnp.bfloat16)
     table = jnp.asarray(angle_table(heads_here))
-    chip, core = me // 2, me % 2
-    info = [chip, core, pack, *[me ^ place for place in range(shards)]]
-    info = jnp.concatenate([jnp.stack(info), image_owner[0]])
+    ids = jnp.stack([me ^ place for place in range(shards)])
     gain, merge_gain_row, bias, ordered, merge_rows, weight = prepare_call(
         shards,
-        info,
+        ids,
         out_weight,
         merge_weight.T,
         qkv_weight.T,
@@ -716,7 +710,7 @@
     )
 
     project = lambda place, first, second, earlier: qkv_call(
-        info, place, first, second, table, gain, weight, earlier, total
+        place, first, second, table, gain, weight, earlier, total
     )
     buffers = project(0, [value], [own_swap], ())
     across_x, across_y = after([across_x, across_y], buffers[2], ordered)
@@ -729,11 +723,10 @@
 
     most = 2 * (total // 4) // images
     first_rows, last_rows = CHUNKS
-    attend = functools.partial(attention_call, first_owner=IDS + shards, info=info)
-    own, note = attend(0, first_rows, labels=labels, block=block, noted=True)
+    (own,) = attention_call(0, first_rows, labels, block, ())
     own_swap, across_x, across_y = near_shards(own)
     labels, block = after([labels, block], own)
-    (late,) = attend(first_rows, last_rows, labels=labels, block=block, noted=False)
+    late, note = attention_call(first_rows, last_rows, labels, block, (image_owner,))
     across_x, across_y = after([across_x, across_y], late)
     halves = halves_call(across_x, across_y)
     far = [send_seq(halves[0], 4), send_seq(halves[1], 2)]
@@ -747,15 +740,15 @@
     (projected,) = merge(0, first_rows, sources + [[send_seq(one, 1) for one in far]], ())
     late_shares[1:] = [after([one], projected)[0] for one in late_shares[1:]]
     sources = [[one] for share in late_shares for one in (share, send_seq(share, 1))]
-    made = merge(first_rows, last_rows, sources, (info, most, note, projected))
+    made = merge(first_rows, last_rows, sources, (most, note, projected))
     sent = {
         flip: lax.ppermute(made[flip], "pack", [(z, z ^ flip) for z in range(packs)])
         for flip in range(packs - 1, 0, -1)
     }
     shape = (packs, most, merge_weight.shape[1])
-    routed = place_call(info, 0, made[0], (), shape)
+    routed = place_call(0, made[0], (), shape)
     for flip in (3, 1, 2):
-        routed = place_call(info, flip, sent[flip], (routed,), shape)
+        routed = place_call(flip, sent[flip], (routed,), shape)
     return routed[None]
 
 

time: 99.3 us -> 96.7 us (0.974)
  Pallas kernels: 46.1 us -> 39.1 us
  waiting for transfers between devices: 28.8 us -> 33 us
  starting transfers between devices: 20.4 us -> 21.5 us
    ppermute x25, waiting for transfers between devices: 18.7 us -> 22.3 us  [send_seq(): return lax.ppermute(value, 'seq', [(i, i ^ flip) for i in range(size)])]
    pallas_call x4, Pallas kernels: 10 us -> 7.85 us  [qkv_call(): pl.pallas_call(functools.partial(qkv_kernel, len(first), flip), in_specs=...]
    pallas_call x4, Pallas kernels: 5.21 us -> 3.05 us  [place_call(): pl.pallas_call(functools.partial(place_kernel, place), in_specs=[pl.Block...]
    pallas_call x2, Pallas kernels: 10 us -> 8.25 us  [attention_call(): pl.pallas_call(functools.partial(attention_kernel, start, owners[0].shape...]
    ppermute x3, starting transfers between devices: 4.45 us -> 5.6 us  [fast_local(): lax.ppermute(made[flip], 'pack', [(z, z ^ flip) for z in range(packs)])]
    unnamed x8 -> x10, local copies, waits for them, and re-layouts: 2.05 us -> 2.06 us
  transfers between devices with their start and end apart: 28 -> 28, of which waited for: 19 -> 19; matrix products, arithmetic and copies ran while one was open for 1% -> 0% of each run, Pallas kernels for 29% -> 25%
where the time goes in v15:
time: 96.7 us; the launch traced here: 96.1 us
  Pallas kernels  39.1 us (40%)
  waiting for transfers between devices  33 us (34%)
  starting transfers between devices  21.5 us (22%)
  local copies, waits for them, and re-layouts  2.15 us (2%)
    ppermute x25, waiting for transfers between devices, send_seq(): return lax.ppermute(value, 'seq', [(i, i ^ flip) for i in range(size)])  22.3 us
    ppermute x25, starting transfers between devices, send_seq(): return lax.ppermute(value, 'seq', [(i, i ^ flip) for i in range(size)])  15.9 us
    pallas_call x2, Pallas kernels, merge_call(): pl.pallas_call(functools.partial(merge_kernel, start, [len(source) for so...  13.4 us
    ppermute x3, waiting for transfers between devices, fast_local(): lax.ppermute(made[flip], 'pack', [(z, z ^ flip) for z in range(packs)])  10.6 us
    pallas_call x2, Pallas kernels, attention_call(): pl.pallas_call(functools.partial(attention_kernel, start, owners[0].shape...  8.25 us
    pallas_call x4, Pallas kernels, qkv_call(): pl.pallas_call(functools.partial(qkv_kernel, len(first), flip), in_specs=...  7.85 us
    ppermute x3, starting transfers between devices, fast_local(): lax.ppermute(made[flip], 'pack', [(z, z ^ flip) for z in range(packs)])  5.6 us
    pallas_call x1, Pallas kernels, prepare_call(): pl.pallas_call(functools.partial(prepare_kernel, shards), in_specs=[pl.Bl...  5.1 us
  transfers between devices with their start and end apart: 28, of which 19 were waited for; matrix products, arithmetic and copies ran while one was open for 0% of the time, Pallas kernels for 25%

profile of v15, /device:TPU:0, one launch (start us, length us, event | category | flops | bytes accessed | tf_op | source)
XLA Modules:
  0.0 96.1 jit_solution(12847804370644812260)
XLA Ops:
  0.0 1.5 %payload.1.refs_0_ = bf16[192,1536]{1,0:T(8,128)(2,1)S(1)} custom-call(s32[1,192]{1,0:T(1,128)} %segments.1, s32[1,192]{1,0:T(1,128)} %rows.1, s32[1,192]{1,0:T(1,128)} %columns.1, s32[1,192]{1,0:T(1,128)} %mask.1, bf16[1408]{0:T(1024)(128)(2,1)} %embed.1, bf16[1,192,1408]{2,1,0:T(8,128)(2,1)} %patches.1), custom_call_target="tpu_custom_call" | custom-call | flops 270336 | bytes 1081344 | tf_op jit(solution)/shard_map/payload/pallas_call | solution.py:203
  2.0 2.6 %collective-permute-start = (bf16[192,1536]{1,0:T(8,128)(2,1)S(1)}, bf16[192,1536]{1,0:T(8,128)(2,1)S(1)}, u32[]{:S(2)}, u32[]{:S(2)}) collective-permute-start(bf16[192,1536]{1,0:T(8,128)(2,1)S(1)} %payload.1.refs_0_), channel_id=1, source_target_pairs={{0,8},{4,12},{8,0},{12,4},{16,24},{20,28},{24,16},{28,20},{1,9},{5... | collective-permute-start | bytes 1769480 | tf_op jit(solution)/shard_map/ppermute | solution.py:601
  4.6 1.5 %collective-permute-start.1 = (bf16[192,1536]{1,0:T(8,128)(2,1)S(1)}, bf16[192,1536]{1,0:T(8,128)(2,1)S(1)}, u32[]{:S(2)}, u32[]{:S(2)}) collective-permute-start(bf16[192,1536]{1,0:T(8,128)(2,1)S(1)} %payload.1.refs_0_), channel_id=1, source_target_pairs={{0,16},{4,20},{8,24},{12,28},{16,0},{20,4},{24,8},{28,12},{1,17},{... | collective-permute-start | bytes 1769480 | tf_op jit(solution)/shard_map/ppermute | solution.py:601
  8.2 5.1 %prepare.1 = (f32[1,1408]{1,0:T(1,128)S(1)}, f32[1,1408]{1,0:T(1,128)S(1)}, f32[1,448]{1,0:T(1,128)S(1)}, bf16[1536,1408]{1,0:T(8,128)(2,1)S(1)}, bf16[448,5632]...) custom-call(s32[8]{0:T(128)S(1)} %stack.35.ids, bf16[1408,1408]{1,0:T(8,128)(2,1)} %out_weight.1, ...), custom_call_target="tpu_custom_call" | custom-call | flops 1141899264 | bytes 20996096 | tf_op jit(solution)/shard_map/prepare/pallas_call | solution.py:437
  13.3 2.0 %norm_qkv.4 = (bf16[1536,1408]{1,0:T(8,128)(2,1)S(1)}, bf16[1536,1024]{1,0:T(8,128)(2,1)S(1)}, bf16[1536,128]{1,0:T(8,128)(2,1)S(1)}) custom-call(bf16[192,1536]{1,0:T(8,128)(2,1)S(1)} %payload.1.refs_0_, bf16[192,1536]{1,0:T(8,128)(2,1)S(1)} %collective-permute-done.2.refs_1_, bf16[128,512]{1,0:T(8,128)(2,1)S(1)} %copy-done, ...), custom_call_target="tpu_custom_call" | custom-call | flops 2491416576 | bytes 6488064 | tf_op jit(solution)/shard_map/norm_qkv/pallas_call | solution.py:279
  15.3 3.1 %collective-permute-done.across_x.refs_0_ = bf16[192,1536]{1,0:T(8,128)(2,1)S(1)} collective-permute-done((bf16[192,1536]{1,0:T(8,128)(2,1)S(1)}, bf16[192,1536]{1,0:T(8,128)(2,1)S(1)}, u32[]{:S(2)}, u32[]{:S(2)}) %collective-permute-start) | collective-permute-done | bytes 589856 | tf_op jit(solution)/shard_map/ppermute | solution.py:601
  18.5 1.5 %collective-permute-done.1.across_y.refs_0_ = bf16[192,1536]{1,0:T(8,128)(2,1)S(1)} collective-permute-done((bf16[192,1536]{1,0:T(8,128)(2,1)S(1)}, bf16[192,1536]{1,0:T(8,128)(2,1)S(1)}, u32[]{:S(2)}, u32[]{:S(2)}) %collective-permute-start.1) | collective-permute-done | bytes 589856 | tf_op jit(solution)/shard_map/ppermute | solution.py:601
  20.5 1.6 %collective-permute-start.3 = (bf16[96,1536]{1,0:T(8,128)(2,1)S(1)}, bf16[96,1536]{1,0:T(8,128)(2,1)S(1)}, u32[]{:S(2)}, u32[]{:S(2)}) collective-permute-start(bf16[96,1536]{1,0:T(8,128)(2,1)S(1)} %get-tuple-element.51), channel_id=1, source_target_pairs={{0,16},{4,20},{8,24},{12,28},{16,0},{20,4},{24,8},{28,12},{1,17},{... | collective-permute-start | bytes 884744 | tf_op jit(solution)/shard_map/ppermute | solution.py:601
  22.6 2.0 %norm_qkv.5 = (bf16[1536,1408]{1,0:T(8,128)(2,1)S(1)}, bf16[1536,1024]{1,0:T(8,128)(2,1)S(1)}, bf16[1536,128]{1,0:T(8,128)(2,1)S(1)}) custom-call(bf16[192,1536]{1,0:T(8,128)(2,1)S(1)} %collective-permute-done.across_x.refs_0_, bf16[192,1536]{1,0:T(8,128)(2,1)S(1)} %collective-permute-done.6.refs_1_, ...), custom_call_target="tpu_custom_call", output_to_operand_aliasing={{0}: (5, {}), {1}: (6, {}), {2}: (7, {})} | custom-call | flops 2491416576 | bytes 6488064 | tf_op jit(solution)/shard_map/norm_qkv/pallas_call | solution.py:279
  24.6 2.0 %norm_qkv.6 = (bf16[1536,1408]{1,0:T(8,128)(2,1)S(1)}, bf16[1536,1024]{1,0:T(8,128)(2,1)S(1)}, bf16[1536,128]{1,0:T(8,128)(2,1)S(1)}) custom-call(bf16[192,1536]{1,0:T(8,128)(2,1)S(1)} %collective-permute-done.1.across_y.refs_0_, bf16[192,1536]{1,0:T(8,128)(2,1)S(1)} %collective-permute-done.5.refs_1_, ...), custom_call_target="tpu_custom_call", output_to_operand_aliasing={{0}: (5, {}), {1}: (6, {}), {2}: (7, {})} | custom-call | flops 2491416576 | bytes 6488064 | tf_op jit(solution)/shard_map/norm_qkv/pallas_call | solution.py:279
  26.6 2.9 %collective-permute-done.3.refs_0_ = bf16[96,1536]{1,0:T(8,128)(2,1)S(1)} collective-permute-done((bf16[96,1536]{1,0:T(8,128)(2,1)S(1)}, bf16[96,1536]{1,0:T(8,128)(2,1)S(1)}, u32[]{:S(2)}, u32[]{:S(2)}) %collective-permute-start.3) | collective-permute-done | bytes 294944 | tf_op jit(solution)/shard_map/ppermute | solution.py:601
  29.5 1.2 %collective-permute-done.4.refs_1_ = bf16[96,1536]{1,0:T(8,128)(2,1)S(1)} collective-permute-done((bf16[96,1536]{1,0:T(8,128)(2,1)S(1)}, bf16[96,1536]{1,0:T(8,128)(2,1)S(1)}, u32[]{:S(2)}, u32[]{:S(2)}) %collective-permute-start.4) | collective-permute-done | bytes 294944 | tf_op jit(solution)/shard_map/ppermute | solution.py:601
  31.2 1.1 %collective-permute-done.7.refs_2_ = bf16[96,1536]{1,0:T(8,128)(2,1)S(1)} collective-permute-done((bf16[96,1536]{1,0:T(8,128)(2,1)S(1)}, bf16[96,1536]{1,0:T(8,128)(2,1)S(1)}, u32[]{:S(2)}, u32[]{:S(2)}) %collective-permute-start.7) | collective-permute-done | bytes 294944 | tf_op jit(solution)/shard_map/ppermute | solution.py:601
  32.7 1.9 %norm_qkv.7 = (bf16[1536,1408]{1,0:T(8,128)(2,1)S(1)}, bf16[1536,1024]{1,0:T(8,128)(2,1)S(1)}, bf16[1536,128]{1,0:T(8,128)(2,1)S(1)}) custom-call(bf16[96,1536]{1,0:T(8,128)(2,1)S(1)} %collective-permute-done.3.refs_0_, bf16[96,1536]{1,0:T(8,128)(2,1)S(1)} %collective-permute-done.4.refs_1_, ...), custom_call_target="tpu_custom_call", output_to_operand_aliasing={{0}: (7, {}), {1}: (8, {}), {2}: (9, {})} | custom-call | flops 2491416576 | bytes 6488064 | tf_op jit(solution)/shard_map/norm_qkv/pallas_call | solution.py:279
  34.7 3.8 %attention.2.refs_5_ = bf16[1152,128]{1,0:T(8,128)(2,1)S(1)} custom-call(bf16[1536,128]{1,0:T(8,128)(2,1)S(1)} %get-tuple-element.69.labels, bf16[1536,1024]{1,0:T(8,128)(2,1)S(1)} %get-tuple-element.70.block), custom_call_target="tpu_custom_call" | custom-call | flops 3019898880 | bytes 3145728 | tf_op jit(solution)/shard_map/attention/pallas_call | solution.py:383
  39.4 4.5 %attention.3 = (bf16[1152,128]{1,0:T(8,128)(2,1)S(1)}, bf16[16,128]{1,0:T(8,128)(2,1)S(1)}) custom-call(bf16[1536,128]{1,0:T(8,128)(2,1)S(1)} %get-tuple-element.69.labels, bf16[1536,1024]{1,0:T(8,128)(2,1)S(1)} %get-tuple-element.70.block, s32[1,4]{1,0:T(1,128)S(1)} %copy-done.4), custom_call_target="tpu_custom_call" | custom-call | flops 3019898880 | bytes 3145728 | tf_op jit(solution)/shard_map/attention/pallas_call | solution.py:383
  43.9 3.6 %collective-permute-done.10.across_y.refs_9_ = bf16[1152,128]{1,0:T(8,128)(2,1)S(1)} collective-permute-done((bf16[1152,128]{1,0:T(8,128)(2,1)S(1)}, bf16[1152,128]{1,0:T(8,128)(2,1)S(1)}, u32[]{:S(2)}, u32[]{:S(2)}) %collective-permute-start.10) | collective-permute-done | bytes 294944 | tf_op jit(solution)/shard_map/ppermute | solution.py:601
  48.3 1.6 %collective-permute-start.16 = (bf16[576,128]{1,0:T(8,128)(2,1)S(1)}, bf16[576,128]{1,0:T(8,128)(2,1)S(1)}, u32[]{:S(2)}, u32[]{:S(2)}) collective-permute-start(bf16[576,128]{1,0:T(8,128)(2,1)S(1)} %get-tuple-element.74), channel_id=1, source_target_pairs={{0,16},{4,20},{8,24},{12,28},{16,0},{20,4},{24,8},{28,12},{1,17},{... | collective-permute-start | bytes 442376 | tf_op jit(solution)/shard_map/ppermute | solution.py:601
  50.4 1.4 %collective-permute-start.23 = (bf16[1152,128]{1,0:T(8,128)(2,1)S(1)}, bf16[1152,128]{1,0:T(8,128)(2,1)S(1)}, u32[]{:S(2)}, u32[]{:S(2)}) collective-permute-start(bf16[1152,128]{1,0:T(8,128)(2,1)S(1)} %get-tuple-element.76.refs_5_), channel_id=1, source_target_pairs={{0,24},{4,28},{8,16},{12,20},{16,8},{20,12},{24,0},{28,4},{1,25},{... | collective-permute-start | bytes 884744 | tf_op jit(solution)/shard_map/ppermute | solution.py:601
  51.9 2.4 %collective-permute-done.16.refs_11_ = bf16[576,128]{1,0:T(8,128)(2,1)S(1)} collective-permute-done((bf16[576,128]{1,0:T(8,128)(2,1)S(1)}, bf16[576,128]{1,0:T(8,128)(2,1)S(1)}, u32[]{:S(2)}, u32[]{:S(2)}) %collective-permute-start.16) | collective-permute-done | bytes 147488 | tf_op jit(solution)/shard_map/ppermute | solution.py:601
  54.2 1.5 %collective-permute-start.21 = (bf16[1152,128]{1,0:T(8,128)(2,1)S(1)}, bf16[1152,128]{1,0:T(8,128)(2,1)S(1)}, u32[]{:S(2)}, u32[]{:S(2)}) collective-permute-start(bf16[1152,128]{1,0:T(8,128)(2,1)S(1)} %get-tuple-element.76.refs_5_), channel_id=1, source_target_pairs={{0,16},{4,20},{8,24},{12,28},{16,0},{20,4},{24,8},{28,12},{1,17},{... | collective-permute-start | bytes 884744 | tf_op jit(solution)/shard_map/ppermute | solution.py:601
  55.7 0.9 collective-permute-done.17.refs_12_
  57.7 0.9 collective-permute-done.18.refs_13_
  58.8 6.4 %out_merge.2.refs_14_ = bf16[192,448]{1,0:T(8,128)(2,1)S(1)} custom-call(bf16[1536,1408]{1,0:T(8,128)(2,1)S(1)} %get-tuple-element.63.refs_0_, bf16[1536,1408]{1,0:T(8,128)(2,1)S(1)} %get-tuple-element.48.refs_1_, f32[1,1408]{1,0:T(1,128)S(1)} %get-tuple-element.64.refs_2_, bf16[448,5632]{1,0:T(8,128)(2,1)S(1)} %get-tuple-element.65.refs_3_, ...), custom_call_target="tpu_custom_call" | custom-call | bytes 1024 | tf_op jit(solution)/shard_map/out_merge/pallas_call | solution.py:544
  65.6 2.0 %collective-permute-done.21.refs_9_ = bf16[1152,128]{1,0:T(8,128)(2,1)S(1)} collective-permute-done((bf16[1152,128]{1,0:T(8,128)(2,1)S(1)}, bf16[1152,128]{1,0:T(8,128)(2,1)S(1)}, u32[]{:S(2)}, u32[]{:S(2)}) %collective-permute-start.21) | collective-permute-done | bytes 294944 | tf_op jit(solution)/shard_map/ppermute | solution.py:601
  68.1 1.1 %collective-permute-done.22.refs_10_ = bf16[1152,128]{1,0:T(8,128)(2,1)S(1)} collective-permute-done((bf16[1152,128]{1,0:T(8,128)(2,1)S(1)}, bf16[1152,128]{1,0:T(8,128)(2,1)S(1)}, u32[]{:S(2)}, u32[]{:S(2)}) %collective-permute-start.22) | collective-permute-done | bytes 294944 | tf_op jit(solution)/shard_map/ppermute | solution.py:601
  69.6 6.9 %out_merge.3 = (bf16[672,128]{1,0:T(8,128)(2,1)S(1)}, bf16[672,128]{1,0:T(8,128)(2,1)S(1)}, bf16[672,128]{1,0:T(8,128)(2,1)S(1)}, bf16[672,128]{1,0:T(8,128)(2,1)S(1)}) custom-call(bf16[1536,1408]{1,0:T(8,128)(2,1)S(1)} %get-tuple-element.63.refs_0_, bf16[1536,1408]{1,0:T(8,128)(2,1)S(1)} %get-tuple-element.48.refs_1_, ...), custom_call_target="tpu_custom_call" | custom-call | bytes 1024 | tf_op jit(solution)/shard_map/out_merge/pallas_call | solution.py:544
  76.6 5.0 %collective-permute-start.27 = (bf16[672,128]{1,0:T(8,128)(2,1)S(1)}, bf16[672,128]{1,0:T(8,128)(2,1)S(1)}, u32[]{:S(2)}, u32[]{:S(2)}) collective-permute-start(bf16[672,128]{1,0:T(8,128)(2,1)S(1)} %get-tuple-element.83), channel_id=1, source_target_pairs={{0,3},{1,2},{2,1},{3,0},{4,7},{5,6},{6,5},{7,4},{8,11},{9,10},{10,... | collective-permute-start | bytes 516104 | tf_op jit(solution)/shard_map/ppermute | solution.py:745
  83.0 3.8 %collective-permute-done.27.block = bf16[672,128]{1,0:T(8,128)(2,1)S(1)} collective-permute-done((bf16[672,128]{1,0:T(8,128)(2,1)S(1)}, bf16[672,128]{1,0:T(8,128)(2,1)S(1)}, u32[]{:S(2)}, u32[]{:S(2)}) %collective-permute-start.27) | collective-permute-done | bytes 172064 | tf_op jit(solution)/shard_map/ppermute | solution.py:745
  87.5 4.8 %collective-permute-done.26.block = bf16[672,128]{1,0:T(8,128)(2,1)S(1)} collective-permute-done((bf16[672,128]{1,0:T(8,128)(2,1)S(1)}, bf16[672,128]{1,0:T(8,128)(2,1)S(1)}, u32[]{:S(2)}, u32[]{:S(2)}) %collective-permute-start.26) | collective-permute-done | bytes 172064 | tf_op jit(solution)/shard_map/ppermute | solution.py:745
  93.1 2.1 %collective-permute-done.25.block = bf16[672,128]{1,0:T(8,128)(2,1)S(1)} collective-permute-done((bf16[672,128]{1,0:T(8,128)(2,1)S(1)}, bf16[672,128]{1,0:T(8,128)(2,1)S(1)}, u32[]{:S(2)}, u32[]{:S(2)}) %collective-permute-start.25) | collective-permute-done | bytes 172064 | tf_op jit(solution)/shard_map/ppermute | solution.py:745
  95.1 0.8 place_rows.7
  (51 shorter events, 12.5 us)
Async XLA Ops:
  1.5 11.9 %collective-permute-start.2 = (bf16[192,1536]{1,0:T(8,128)(2,1)S(1)}, bf16[192,1536]{1,0:T(8,128)(2,1)S(1)}, u32[]{:S(2)}, u32[]{:S(2)}) collective-permute-start(bf16[192,1536]{1,0:T(8,128)(2,1)S(1)} %payload.1.refs_0_), channel_id=1, source_target_pairs={{0,4},{4,0},{8,12},{12,8},{16,20},{20,16},{24,28},{28,24},{1,5},{5... | collective-permute-start | bytes 1769480 | tf_op jit(solution)/shard_map/ppermute | solution.py:601
  2.0 16.5 %collective-permute-start = (bf16[192,1536]{1,0:T(8,128)(2,1)S(1)}, bf16[192,1536]{1,0:T(8,128)(2,1)S(1)}, u32[]{:S(2)}, u32[]{:S(2)}) collective-permute-start(bf16[192,1536]{1,0:T(8,128)(2,1)S(1)} %payload.1.refs_0_), channel_id=1, source_target_pairs={{0,8},{4,12},{8,0},{12,4},{16,24},{20,28},{24,16},{28,20},{1,9},{5... | collective-permute-start | bytes 1769480 | tf_op jit(solution)/shard_map/ppermute | solution.py:601
  4.6 15.4 %collective-permute-start.1 = (bf16[192,1536]{1,0:T(8,128)(2,1)S(1)}, bf16[192,1536]{1,0:T(8,128)(2,1)S(1)}, u32[]{:S(2)}, u32[]{:S(2)}) collective-permute-start(bf16[192,1536]{1,0:T(8,128)(2,1)S(1)} %payload.1.refs_0_), channel_id=1, source_target_pairs={{0,16},{4,20},{8,24},{12,28},{16,0},{20,4},{24,8},{28,12},{1,17},{... | collective-permute-start | bytes 1769480 | tf_op jit(solution)/shard_map/ppermute | solution.py:601
  6.2 0.7 copy-start.1
  6.8 0.7 copy-start.2
  8.2 5.1 %copy-start = (bf16[128,512]{1,0:T(8,128)(2,1)S(1)}, bf16[128,512]{1,0:T(8,128)(2,1)}, u32[]{:S(2)}) copy-start(bf16[128,512]{1,0:T(8,128)(2,1)} %constant.24.clone.refs_2_.refs_4_) | copy-start | bytes 393220
  20.0 2.7 %collective-permute-start.6 = (bf16[192,1536]{1,0:T(8,128)(2,1)S(1)}, bf16[192,1536]{1,0:T(8,128)(2,1)S(1)}, u32[]{:S(2)}, u32[]{:S(2)}) collective-permute-start(bf16[192,1536]{1,0:T(8,128)(2,1)S(1)} %collective-permute-done.across_x.refs_0_), channel_id=1, source_target_pairs={{0,4},{4,0},{8,12},{12,8},{16,20},{20,16},{24,28},{28,24},{1,5},{5... | collective-permute-start | bytes 1769480 | tf_op jit(solution)/shard_map/ppermute | solution.py:601
  20.0 4.7 %collective-permute-start.5 = (bf16[192,1536]{1,0:T(8,128)(2,1)S(1)}, bf16[192,1536]{1,0:T(8,128)(2,1)S(1)}, u32[]{:S(2)}, u32[]{:S(2)}) collective-permute-start(bf16[192,1536]{1,0:T(8,128)(2,1)S(1)} %collective-permute-done.1.across_y.refs_0_), channel_id=1, source_target_pairs={{0,4},{4,0},{8,12},{12,8},{16,20},{20,16},{24,28},{28,24},{1,5},{5... | collective-permute-start | bytes 1769480 | tf_op jit(solution)/shard_map/ppermute | solution.py:601
  20.5 9.0 %collective-permute-start.3 = (bf16[96,1536]{1,0:T(8,128)(2,1)S(1)}, bf16[96,1536]{1,0:T(8,128)(2,1)S(1)}, u32[]{:S(2)}, u32[]{:S(2)}) collective-permute-start(bf16[96,1536]{1,0:T(8,128)(2,1)S(1)} %get-tuple-element.51), channel_id=1, source_target_pairs={{0,16},{4,20},{8,24},{12,28},{16,0},{20,4},{24,8},{28,12},{1,17},{... | collective-permute-start | bytes 884744 | tf_op jit(solution)/shard_map/ppermute | solution.py:601
  22.1 8.6 %collective-permute-start.4 = (bf16[96,1536]{1,0:T(8,128)(2,1)S(1)}, bf16[96,1536]{1,0:T(8,128)(2,1)S(1)}, u32[]{:S(2)}, u32[]{:S(2)}) collective-permute-start(bf16[96,1536]{1,0:T(8,128)(2,1)S(1)} %get-tuple-element.52), channel_id=1, source_target_pairs={{0,8},{4,12},{8,0},{12,4},{16,24},{20,28},{24,16},{28,20},{1,9},{5... | collective-permute-start | bytes 884744 | tf_op jit(solution)/shard_map/ppermute | solution.py:601
  30.7 1.6 %collective-permute-start.7 = (bf16[96,1536]{1,0:T(8,128)(2,1)S(1)}, bf16[96,1536]{1,0:T(8,128)(2,1)S(1)}, u32[]{:S(2)}, u32[]{:S(2)}) collective-permute-start(bf16[96,1536]{1,0:T(8,128)(2,1)S(1)} %collective-permute-done.3.refs_0_), channel_id=1, source_target_pairs={{0,4},{4,0},{8,12},{12,8},{16,20},{20,16},{24,28},{28,24},{1,5},{5... | collective-permute-start | bytes 884744 | tf_op jit(solution)/shard_map/ppermute | solution.py:601
  30.7 2.0 %collective-permute-start.8 = (bf16[96,1536]{1,0:T(8,128)(2,1)S(1)}, bf16[96,1536]{1,0:T(8,128)(2,1)S(1)}, u32[]{:S(2)}, u32[]{:S(2)}) collective-permute-start(bf16[96,1536]{1,0:T(8,128)(2,1)S(1)} %collective-permute-done.4.refs_1_), channel_id=1, source_target_pairs={{0,4},{4,0},{8,12},{12,8},{16,20},{20,16},{24,28},{28,24},{1,5},{5... | collective-permute-start | bytes 884744 | tf_op jit(solution)/shard_map/ppermute | solution.py:601
  34.7 4.7 %copy-start.4 = (s32[1,4]{1,0:T(1,128)S(1)}, s32[1,4]{1,0:T(1,128)}, u32[]{:S(2)}) copy-start(s32[1,4]{1,0:T(1,128)} %refs_0_.3) | copy-start | bytes 52
  38.4 9.1 %collective-permute-start.10 = (bf16[1152,128]{1,0:T(8,128)(2,1)S(1)}, bf16[1152,128]{1,0:T(8,128)(2,1)S(1)}, u32[]{:S(2)}, u32[]{:S(2)}) collective-permute-start(bf16[1152,128]{1,0:T(8,128)(2,1)S(1)} %attention.2.refs_5_), channel_id=1, source_target_pairs={{0,16},{4,20},{8,24},{12,28},{16,0},{20,4},{24,8},{28,12},{1,17},{... | collective-permute-start | bytes 884744 | tf_op jit(solution)/shard_map/ppermute | solution.py:601
  39.0 8.8 %collective-permute-start.9 = (bf16[1152,128]{1,0:T(8,128)(2,1)S(1)}, bf16[1152,128]{1,0:T(8,128)(2,1)S(1)}, u32[]{:S(2)}, u32[]{:S(2)}) collective-permute-start(bf16[1152,128]{1,0:T(8,128)(2,1)S(1)} %attention.2.refs_5_), channel_id=1, source_target_pairs={{0,8},{4,12},{8,0},{12,4},{16,24},{20,28},{24,16},{28,20},{1,9},{5... | collective-permute-start | bytes 884744 | tf_op jit(solution)/shard_map/ppermute | solution.py:601
  39.4 11.0 %collective-permute-start.13 = (bf16[1152,128]{1,0:T(8,128)(2,1)S(1)}, bf16[1152,128]{1,0:T(8,128)(2,1)S(1)}, u32[]{:S(2)}, u32[]{:S(2)}) collective-permute-start(bf16[1152,128]{1,0:T(8,128)(2,1)S(1)} %attention.2.refs_5_), channel_id=1, source_target_pairs={{0,4},{4,0},{8,12},{12,8},{16,20},{20,16},{24,28},{28,24},{1,5},{5... | collective-permute-start | bytes 884744 | tf_op jit(solution)/shard_map/ppermute | solution.py:601
  47.8 9.4 %collective-permute-start.14 = (bf16[1152,128]{1,0:T(8,128)(2,1)S(1)}, bf16[1152,128]{1,0:T(8,128)(2,1)S(1)}, u32[]{:S(2)}, u32[]{:S(2)}) collective-permute-start(bf16[1152,128]{1,0:T(8,128)(2,1)S(1)} %collective-permute-done.9.across_x.refs_7_), channel_id=1, source_target_pairs={{0,4},{4,0},{8,12},{12,8},{16,20},{20,16},{24,28},{28,24},{1,5},{5... | collective-permute-start | bytes 884744 | tf_op jit(solution)/shard_map/ppermute | solution.py:601
  47.8 9.4 %collective-permute-start.15 = (bf16[1152,128]{1,0:T(8,128)(2,1)S(1)}, bf16[1152,128]{1,0:T(8,128)(2,1)S(1)}, u32[]{:S(2)}, u32[]{:S(2)}) collective-permute-start(bf16[1152,128]{1,0:T(8,128)(2,1)S(1)} %collective-permute-done.10.across_y.refs_9_), channel_id=1, source_target_pairs={{0,4},{4,0},{8,12},{12,8},{16,20},{20,16},{24,28},{28,24},{1,5},{5... | collective-permute-start | bytes 884744 | tf_op jit(solution)/shard_map/ppermute | solution.py:601
  48.3 5.9 %collective-permute-start.16 = (bf16[576,128]{1,0:T(8,128)(2,1)S(1)}, bf16[576,128]{1,0:T(8,128)(2,1)S(1)}, u32[]{:S(2)}, u32[]{:S(2)}) collective-permute-start(bf16[576,128]{1,0:T(8,128)(2,1)S(1)} %get-tuple-element.74), channel_id=1, source_target_pairs={{0,16},{4,20},{8,24},{12,28},{16,0},{20,4},{24,8},{28,12},{1,17},{... | collective-permute-start | bytes 442376 | tf_op jit(solution)/shard_map/ppermute | solution.py:601
  49.9 6.8 %collective-permute-start.17 = (bf16[576,128]{1,0:T(8,128)(2,1)S(1)}, bf16[576,128]{1,0:T(8,128)(2,1)S(1)}, u32[]{:S(2)}, u32[]{:S(2)}) collective-permute-start(bf16[576,128]{1,0:T(8,128)(2,1)S(1)} %get-tuple-element.75), channel_id=1, source_target_pairs={{0,8},{4,12},{8,0},{12,4},{16,24},{20,28},{24,16},{28,20},{1,9},{5... | collective-permute-start | bytes 442376 | tf_op jit(solution)/shard_map/ppermute | solution.py:601
  50.4 14.8 %collective-permute-start.23 = (bf16[1152,128]{1,0:T(8,128)(2,1)S(1)}, bf16[1152,128]{1,0:T(8,128)(2,1)S(1)}, u32[]{:S(2)}, u32[]{:S(2)}) collective-permute-start(bf16[1152,128]{1,0:T(8,128)(2,1)S(1)} %get-tuple-element.76.refs_5_), channel_id=1, source_target_pairs={{0,24},{4,28},{8,16},{12,20},{16,8},{20,12},{24,0},{28,4},{1,25},{... | collective-permute-start | bytes 884744 | tf_op jit(solution)/shard_map/ppermute | solution.py:601
  54.2 13.4 %collective-permute-start.21 = (bf16[1152,128]{1,0:T(8,128)(2,1)S(1)}, bf16[1152,128]{1,0:T(8,128)(2,1)S(1)}, u32[]{:S(2)}, u32[]{:S(2)}) collective-permute-start(bf16[1152,128]{1,0:T(8,128)(2,1)S(1)} %get-tuple-element.76.refs_5_), channel_id=1, source_target_pairs={{0,16},{4,20},{8,24},{12,28},{16,0},{20,4},{24,8},{28,12},{1,17},{... | collective-permute-start | bytes 884744 | tf_op jit(solution)/shard_map/ppermute | solution.py:601
  56.6 11.4 %collective-permute-start.12 = (bf16[1152,128]{1,0:T(8,128)(2,1)S(1)}, bf16[1152,128]{1,0:T(8,128)(2,1)S(1)}, u32[]{:S(2)}, u32[]{:S(2)}) collective-permute-start(bf16[1152,128]{1,0:T(8,128)(2,1)S(1)} %get-tuple-element.76.refs_5_), channel_id=1, source_target_pairs={{0,8},{4,12},{8,0},{12,4},{16,24},{20,28},{24,16},{28,20},{1,9},{5... | collective-permute-start | bytes 884744 | tf_op jit(solution)/shard_map/ppermute | solution.py:601
  57.2 1.4 %collective-permute-start.18 = (bf16[576,128]{1,0:T(8,128)(2,1)S(1)}, bf16[576,128]{1,0:T(8,128)(2,1)S(1)}, u32[]{:S(2)}, u32[]{:S(2)}) collective-permute-start(bf16[576,128]{1,0:T(8,128)(2,1)S(1)} %collective-permute-done.16.refs_11_), channel_id=1, source_target_pairs={{0,4},{4,0},{8,12},{12,8},{16,20},{20,16},{24,28},{28,24},{1,5},{5... | collective-permute-start | bytes 442376 | tf_op jit(solution)/shard_map/ppermute | solution.py:601
  57.2 1.6 %collective-permute-start.19 = (bf16[576,128]{1,0:T(8,128)(2,1)S(1)}, bf16[576,128]{1,0:T(8,128)(2,1)S(1)}, u32[]{:S(2)}, u32[]{:S(2)}) collective-permute-start(bf16[576,128]{1,0:T(8,128)(2,1)S(1)} %collective-permute-done.17.refs_12_), channel_id=1, source_target_pairs={{0,4},{4,0},{8,12},{12,8},{16,20},{20,16},{24,28},{28,24},{1,5},{5... | collective-permute-start | bytes 442376 | tf_op jit(solution)/shard_map/ppermute | solution.py:601
  58.6 9.6 %collective-permute-start.11 = (bf16[1152,128]{1,0:T(8,128)(2,1)S(1)}, bf16[1152,128]{1,0:T(8,128)(2,1)S(1)}, u32[]{:S(2)}, u32[]{:S(2)}) collective-permute-start(bf16[1152,128]{1,0:T(8,128)(2,1)S(1)} %get-tuple-element.76.refs_5_), channel_id=1, source_target_pairs={{0,4},{4,0},{8,12},{12,8},{16,20},{20,16},{24,28},{28,24},{1,5},{5... | collective-permute-start | bytes 884744 | tf_op jit(solution)/shard_map/ppermute | solution.py:601
  65.2 2.9 %collective-permute-start.24 = (bf16[1152,128]{1,0:T(8,128)(2,1)S(1)}, bf16[1152,128]{1,0:T(8,128)(2,1)S(1)}, u32[]{:S(2)}, u32[]{:S(2)}) collective-permute-start(bf16[1152,128]{1,0:T(8,128)(2,1)S(1)} %collective-permute-done.23.refs_11_), channel_id=1, source_target_pairs={{0,4},{4,0},{8,12},{12,8},{16,20},{20,16},{24,28},{28,24},{1,5},{5... | collective-permute-start | bytes 884744 | tf_op jit(solution)/shard_map/ppermute | solution.py:601
  67.6 1.6 %collective-permute-start.22 = (bf16[1152,128]{1,0:T(8,128)(2,1)S(1)}, bf16[1152,128]{1,0:T(8,128)(2,1)S(1)}, u32[]{:S(2)}, u32[]{:S(2)}) collective-permute-start(bf16[1152,128]{1,0:T(8,128)(2,1)S(1)} %collective-permute-done.21.refs_9_), channel_id=1, source_target_pairs={{0,4},{4,0},{8,12},{12,8},{16,20},{20,16},{24,28},{28,24},{1,5},{5... | collective-permute-start | bytes 884744 | tf_op jit(solution)/shard_map/ppermute | solution.py:601
  68.1 1.6 %collective-permute-start.20 = (bf16[1152,128]{1,0:T(8,128)(2,1)S(1)}, bf16[1152,128]{1,0:T(8,128)(2,1)S(1)}, u32[]{:S(2)}, u32[]{:S(2)}) collective-permute-start(bf16[1152,128]{1,0:T(8,128)(2,1)S(1)} %collective-permute-done.12.refs_7_), channel_id=1, source_target_pairs={{0,4},{4,0},{8,12},{12,8},{16,20},{20,16},{24,28},{28,24},{1,5},{5... | collective-permute-start | bytes 884744 | tf_op jit(solution)/shard_map/ppermute | solution.py:601
  76.6 10.2 %collective-permute-start.27 = (bf16[672,128]{1,0:T(8,128)(2,1)S(1)}, bf16[672,128]{1,0:T(8,128)(2,1)S(1)}, u32[]{:S(2)}, u32[]{:S(2)}) collective-permute-start(bf16[672,128]{1,0:T(8,128)(2,1)S(1)} %get-tuple-element.83), channel_id=1, source_target_pairs={{0,3},{1,2},{2,1},{3,0},{4,7},{5,6},{6,5},{7,4},{8,11},{9,10},{10,... | collective-permute-start | bytes 516104 | tf_op jit(solution)/shard_map/ppermute | solution.py:745
  81.5 10.7 %collective-permute-start.26 = (bf16[672,128]{1,0:T(8,128)(2,1)S(1)}, bf16[672,128]{1,0:T(8,128)(2,1)S(1)}, u32[]{:S(2)}, u32[]{:S(2)}) collective-permute-start(bf16[672,128]{1,0:T(8,128)(2,1)S(1)} %get-tuple-element.82), channel_id=1, source_target_pairs={{0,1},{1,0},{2,3},{3,2},{4,5},{5,4},{6,7},{7,6},{8,9},{9,8},{10,11... | collective-permute-start | bytes 516104 | tf_op jit(solution)/shard_map/ppermute | solution.py:745
  81.5 13.6 %collective-permute-start.25 = (bf16[672,128]{1,0:T(8,128)(2,1)S(1)}, bf16[672,128]{1,0:T(8,128)(2,1)S(1)}, u32[]{:S(2)}, u32[]{:S(2)}) collective-permute-start(bf16[672,128]{1,0:T(8,128)(2,1)S(1)} %get-tuple-element.81), channel_id=1, source_target_pairs={{0,2},{1,3},{2,0},{3,1},{4,6},{5,7},{6,4},{7,5},{8,10},{9,11},{10,... | collective-permute-start | bytes 516104 | tf_op jit(solution)/shard_map/ppermute | solution.py:745
  (1 other events, 0.7 us)

commit v16 on v15

--- a/solution.py
+++ b/solution.py
@@ -152,7 +152,7 @@
 FAR_APART = -(2.0**100)
 IMAGE_LANE = 96
 NORM_ROWS = 16
-CHUNKS = (768, 768)
+CHUNKS = (896, 640)
 
 
 def norm_rows(values, gain_row):

time: 96.7 us -> 100 us (1.034)
  waiting for transfers between devices: 33 us -> 36.2 us
    ppermute x25, waiting for transfers between devices: 22.3 us -> 24.2 us  [send_seq(): return lax.ppermute(value, 'seq', [(i, i ^ flip) for i in range(size)])]
    ppermute x3, waiting for transfers between devices: 10.6 us -> 12 us  [fast_local(): lax.ppermute(made[flip], 'pack', [(z, z ^ flip) for z in range(packs)])]
  transfers between devices with their start and end apart: 28 -> 28, of which waited for: 19 -> 16; matrix products, arithmetic and copies ran while one was open for 0% -> 0% of each run, Pallas kernels for 25% -> 25%
where the time goes in v16:
time: 100 us; the launch traced here: 99.8 us
  Pallas kernels  39.4 us (39%)
  waiting for transfers between devices  36.2 us (36%)
  starting transfers between devices  21.8 us (22%)
  local copies, waits for them, and re-layouts  2.15 us (2%)
    ppermute x25, waiting for transfers between devices, send_seq(): return lax.ppermute(value, 'seq', [(i, i ^ flip) for i in range(size)])  24.2 us
    ppermute x25, starting transfers between devices, send_seq(): return lax.ppermute(value, 'seq', [(i, i ^ flip) for i in range(size)])  15.9 us
    pallas_call x2, Pallas kernels, merge_call(): pl.pallas_call(functools.partial(merge_kernel, start, [len(source) for so...  13.7 us
    ppermute x3, waiting for transfers between devices, fast_local(): lax.ppermute(made[flip], 'pack', [(z, z ^ flip) for z in range(packs)])  12 us
    pallas_call x2, Pallas kernels, attention_call(): pl.pallas_call(functools.partial(attention_kernel, start, owners[0].shape...  8.2 us
    pallas_call x4, Pallas kernels, qkv_call(): pl.pallas_call(functools.partial(qkv_kernel, len(first), flip), in_specs=...  7.85 us
    ppermute x3, starting transfers between devices, fast_local(): lax.ppermute(made[flip], 'pack', [(z, z ^ flip) for z in range(packs)])  5.87 us
    pallas_call x1, Pallas kernels, prepare_call(): pl.pallas_call(functools.partial(prepare_kernel, shards), in_specs=[pl.Bl...  5.1 us
  transfers between devices with their start and end apart: 28, of which 16 were waited for; matrix products, arithmetic and copies ran while one was open for 0% of the time, Pallas kernels for 25%

profile of v16, /device:TPU:0, one launch (start us, length us, event | category | flops | bytes accessed | tf_op | source)
XLA Modules:
  0.0 99.8 jit_solution(3397408629769110663)
XLA Ops:
  0.0 1.5 %payload.1.refs_0_ = bf16[192,1536]{1,0:T(8,128)(2,1)S(1)} custom-call(s32[1,192]{1,0:T(1,128)} %segments.1, s32[1,192]{1,0:T(1,128)} %rows.1, s32[1,192]{1,0:T(1,128)} %columns.1, s32[1,192]{1,0:T(1,128)} %mask.1, bf16[1408]{0:T(1024)(128)(2,1)} %embed.1, bf16[1,192,1408]{2,1,0:T(8,128)(2,1)} %patches.1), custom_call_target="tpu_custom_call" | custom-call | flops 270336 | bytes 1081344 | tf_op jit(solution)/shard_map/payload/pallas_call | solution.py:203
  2.0 2.6 %collective-permute-start = (bf16[192,1536]{1,0:T(8,128)(2,1)S(1)}, bf16[192,1536]{1,0:T(8,128)(2,1)S(1)}, u32[]{:S(2)}, u32[]{:S(2)}) collective-permute-start(bf16[192,1536]{1,0:T(8,128)(2,1)S(1)} %payload.1.refs_0_), channel_id=1, source_target_pairs={{0,8},{4,12},{8,0},{12,4},{16,24},{20,28},{24,16},{28,20},{1,9},{5... | collective-permute-start | bytes 1769480 | tf_op jit(solution)/shard_map/ppermute | solution.py:601
  4.6 1.5 %collective-permute-start.1 = (bf16[192,1536]{1,0:T(8,128)(2,1)S(1)}, bf16[192,1536]{1,0:T(8,128)(2,1)S(1)}, u32[]{:S(2)}, u32[]{:S(2)}) collective-permute-start(bf16[192,1536]{1,0:T(8,128)(2,1)S(1)} %payload.1.refs_0_), channel_id=1, source_target_pairs={{0,16},{4,20},{8,24},{12,28},{16,0},{20,4},{24,8},{28,12},{1,17},{... | collective-permute-start | bytes 1769480 | tf_op jit(solution)/shard_map/ppermute | solution.py:601
  8.2 5.1 %prepare.1 = (f32[1,1408]{1,0:T(1,128)S(1)}, f32[1,1408]{1,0:T(1,128)S(1)}, f32[1,448]{1,0:T(1,128)S(1)}, bf16[1536,1408]{1,0:T(8,128)(2,1)S(1)}, bf16[448,5632]...) custom-call(s32[8]{0:T(128)S(1)} %stack.35.ids, bf16[1408,1408]{1,0:T(8,128)(2,1)} %out_weight.1, ...), custom_call_target="tpu_custom_call" | custom-call | flops 1141899264 | bytes 20996096 | tf_op jit(solution)/shard_map/prepare/pallas_call | solution.py:437
  13.3 2.0 %norm_qkv.4 = (bf16[1536,1408]{1,0:T(8,128)(2,1)S(1)}, bf16[1536,1024]{1,0:T(8,128)(2,1)S(1)}, bf16[1536,128]{1,0:T(8,128)(2,1)S(1)}) custom-call(bf16[192,1536]{1,0:T(8,128)(2,1)S(1)} %payload.1.refs_0_, bf16[192,1536]{1,0:T(8,128)(2,1)S(1)} %collective-permute-done.2.refs_1_, bf16[128,512]{1,0:T(8,128)(2,1)S(1)} %copy-done, ...), custom_call_target="tpu_custom_call" | custom-call | flops 2491416576 | bytes 6488064 | tf_op jit(solution)/shard_map/norm_qkv/pallas_call | solution.py:279
  15.3 3.1 %collective-permute-done.across_x.refs_0_ = bf16[192,1536]{1,0:T(8,128)(2,1)S(1)} collective-permute-done((bf16[192,1536]{1,0:T(8,128)(2,1)S(1)}, bf16[192,1536]{1,0:T(8,128)(2,1)S(1)}, u32[]{:S(2)}, u32[]{:S(2)}) %collective-permute-start) | collective-permute-done | bytes 589856 | tf_op jit(solution)/shard_map/ppermute | solution.py:601
  18.5 1.5 %collective-permute-done.1.across_y.refs_0_ = bf16[192,1536]{1,0:T(8,128)(2,1)S(1)} collective-permute-done((bf16[192,1536]{1,0:T(8,128)(2,1)S(1)}, bf16[192,1536]{1,0:T(8,128)(2,1)S(1)}, u32[]{:S(2)}, u32[]{:S(2)}) %collective-permute-start.1) | collective-permute-done | bytes 589856 | tf_op jit(solution)/shard_map/ppermute | solution.py:601
  20.5 1.6 %collective-permute-start.3 = (bf16[96,1536]{1,0:T(8,128)(2,1)S(1)}, bf16[96,1536]{1,0:T(8,128)(2,1)S(1)}, u32[]{:S(2)}, u32[]{:S(2)}) collective-permute-start(bf16[96,1536]{1,0:T(8,128)(2,1)S(1)} %get-tuple-element.51), channel_id=1, source_target_pairs={{0,16},{4,20},{8,24},{12,28},{16,0},{20,4},{24,8},{28,12},{1,17},{... | collective-permute-start | bytes 884744 | tf_op jit(solution)/shard_map/ppermute | solution.py:601
  22.6 2.0 %norm_qkv.5 = (bf16[1536,1408]{1,0:T(8,128)(2,1)S(1)}, bf16[1536,1024]{1,0:T(8,128)(2,1)S(1)}, bf16[1536,128]{1,0:T(8,128)(2,1)S(1)}) custom-call(bf16[192,1536]{1,0:T(8,128)(2,1)S(1)} %collective-permute-done.across_x.refs_0_, bf16[192,1536]{1,0:T(8,128)(2,1)S(1)} %collective-permute-done.6.refs_1_, ...), custom_call_target="tpu_custom_call", output_to_operand_aliasing={{0}: (5, {}), {1}: (6, {}), {2}: (7, {})} | custom-call | flops 2491416576 | bytes 6488064 | tf_op jit(solution)/shard_map/norm_qkv/pallas_call | solution.py:279
  24.6 2.0 %norm_qkv.6 = (bf16[1536,1408]{1,0:T(8,128)(2,1)S(1)}, bf16[1536,1024]{1,0:T(8,128)(2,1)S(1)}, bf16[1536,128]{1,0:T(8,128)(2,1)S(1)}) custom-call(bf16[192,1536]{1,0:T(8,128)(2,1)S(1)} %collective-permute-done.1.across_y.refs_0_, bf16[192,1536]{1,0:T(8,128)(2,1)S(1)} %collective-permute-done.5.refs_1_, ...), custom_call_target="tpu_custom_call", output_to_operand_aliasing={{0}: (5, {}), {1}: (6, {}), {2}: (7, {})} | custom-call | flops 2491416576 | bytes 6488064 | tf_op jit(solution)/shard_map/norm_qkv/pallas_call | solution.py:279
  26.6 2.9 %collective-permute-done.3.refs_0_ = bf16[96,1536]{1,0:T(8,128)(2,1)S(1)} collective-permute-done((bf16[96,1536]{1,0:T(8,128)(2,1)S(1)}, bf16[96,1536]{1,0:T(8,128)(2,1)S(1)}, u32[]{:S(2)}, u32[]{:S(2)}) %collective-permute-start.3) | collective-permute-done | bytes 294944 | tf_op jit(solution)/shard_map/ppermute | solution.py:601
  29.5 1.2 %collective-permute-done.4.refs_1_ = bf16[96,1536]{1,0:T(8,128)(2,1)S(1)} collective-permute-done((bf16[96,1536]{1,0:T(8,128)(2,1)S(1)}, bf16[96,1536]{1,0:T(8,128)(2,1)S(1)}, u32[]{:S(2)}, u32[]{:S(2)}) %collective-permute-start.4) | collective-permute-done | bytes 294944 | tf_op jit(solution)/shard_map/ppermute | solution.py:601
  31.2 1.1 %collective-permute-done.7.refs_2_ = bf16[96,1536]{1,0:T(8,128)(2,1)S(1)} collective-permute-done((bf16[96,1536]{1,0:T(8,128)(2,1)S(1)}, bf16[96,1536]{1,0:T(8,128)(2,1)S(1)}, u32[]{:S(2)}, u32[]{:S(2)}) %collective-permute-start.7) | collective-permute-done | bytes 294944 | tf_op jit(solution)/shard_map/ppermute | solution.py:601
  32.7 1.9 %norm_qkv.7 = (bf16[1536,1408]{1,0:T(8,128)(2,1)S(1)}, bf16[1536,1024]{1,0:T(8,128)(2,1)S(1)}, bf16[1536,128]{1,0:T(8,128)(2,1)S(1)}) custom-call(bf16[96,1536]{1,0:T(8,128)(2,1)S(1)} %collective-permute-done.3.refs_0_, bf16[96,1536]{1,0:T(8,128)(2,1)S(1)} %collective-permute-done.4.refs_1_, ...), custom_call_target="tpu_custom_call", output_to_operand_aliasing={{0}: (7, {}), {1}: (8, {}), {2}: (9, {})} | custom-call | flops 2491416576 | bytes 6488064 | tf_op jit(solution)/shard_map/norm_qkv/pallas_call | solution.py:279
  34.7 4.1 %attention.2.refs_5_ = bf16[1344,128]{1,0:T(8,128)(2,1)S(1)} custom-call(bf16[1536,128]{1,0:T(8,128)(2,1)S(1)} %get-tuple-element.69.labels, bf16[1536,1024]{1,0:T(8,128)(2,1)S(1)} %get-tuple-element.70.block), custom_call_target="tpu_custom_call" | custom-call | flops 3523215360 | bytes 3145728 | tf_op jit(solution)/shard_map/attention/pallas_call | solution.py:383
  39.8 4.1 %attention.3 = (bf16[960,128]{1,0:T(8,128)(2,1)S(1)}, bf16[16,128]{1,0:T(8,128)(2,1)S(1)}) custom-call(bf16[1536,128]{1,0:T(8,128)(2,1)S(1)} %get-tuple-element.69.labels, bf16[1536,1024]{1,0:T(8,128)(2,1)S(1)} %get-tuple-element.70.block, s32[1,4]{1,0:T(1,128)S(1)} %copy-done.4), custom_call_target="tpu_custom_call" | custom-call | flops 2516582400 | bytes 3145728 | tf_op jit(solution)/shard_map/attention/pallas_call | solution.py:383
  43.9 5.1 %collective-permute-done.10.across_y.refs_9_ = bf16[1344,128]{1,0:T(8,128)(2,1)S(1)} collective-permute-done((bf16[1344,128]{1,0:T(8,128)(2,1)S(1)}, bf16[1344,128]{1,0:T(8,128)(2,1)S(1)}, u32[]{:S(2)}, u32[]{:S(2)}) %collective-permute-start.10) | collective-permute-done | bytes 344096 | tf_op jit(solution)/shard_map/ppermute | solution.py:601
  49.2 1.6 %collective-permute-start.16 = (bf16[672,128]{1,0:T(8,128)(2,1)S(1)}, bf16[672,128]{1,0:T(8,128)(2,1)S(1)}, u32[]{:S(2)}, u32[]{:S(2)}) collective-permute-start(bf16[672,128]{1,0:T(8,128)(2,1)S(1)} %get-tuple-element.74), channel_id=1, source_target_pairs={{0,16},{4,20},{8,24},{12,28},{16,0},{20,4},{24,8},{28,12},{1,17},{... | collective-permute-start | bytes 516104 | tf_op jit(solution)/shard_map/ppermute | solution.py:601
  51.4 3.4 %collective-permute-done.16.refs_11_ = bf16[672,128]{1,0:T(8,128)(2,1)S(1)} collective-permute-done((bf16[672,128]{1,0:T(8,128)(2,1)S(1)}, bf16[672,128]{1,0:T(8,128)(2,1)S(1)}, u32[]{:S(2)}, u32[]{:S(2)}) %collective-permute-start.16) | collective-permute-done | bytes 172064 | tf_op jit(solution)/shard_map/ppermute | solution.py:601
  54.7 1.5 %collective-permute-done.17.refs_12_ = bf16[672,128]{1,0:T(8,128)(2,1)S(1)} collective-permute-done((bf16[672,128]{1,0:T(8,128)(2,1)S(1)}, bf16[672,128]{1,0:T(8,128)(2,1)S(1)}, u32[]{:S(2)}, u32[]{:S(2)}) %collective-permute-start.17) | collective-permute-done | bytes 172064 | tf_op jit(solution)/shard_map/ppermute | solution.py:601
  57.2 1.5 %collective-permute-start.21 = (bf16[960,128]{1,0:T(8,128)(2,1)S(1)}, bf16[960,128]{1,0:T(8,128)(2,1)S(1)}, u32[]{:S(2)}, u32[]{:S(2)}) collective-permute-start(bf16[960,128]{1,0:T(8,128)(2,1)S(1)} %get-tuple-element.76.refs_5_), channel_id=1, source_target_pairs={{0,16},{4,20},{8,24},{12,28},{16,0},{20,4},{24,8},{28,12},{1,17},{... | collective-permute-start | bytes 737288 | tf_op jit(solution)/shard_map/ppermute | solution.py:601
  58.8 1.5 %collective-permute-start.12 = (bf16[960,128]{1,0:T(8,128)(2,1)S(1)}, bf16[960,128]{1,0:T(8,128)(2,1)S(1)}, u32[]{:S(2)}, u32[]{:S(2)}) collective-permute-start(bf16[960,128]{1,0:T(8,128)(2,1)S(1)} %get-tuple-element.76.refs_5_), channel_id=1, source_target_pairs={{0,8},{4,12},{8,0},{12,4},{16,24},{20,28},{24,16},{28,20},{1,9},{5... | collective-permute-start | bytes 737288 | tf_op jit(solution)/shard_map/ppermute | solution.py:601
  60.3 7.2 %out_merge.2.refs_14_ = bf16[224,448]{1,0:T(8,128)(2,1)S(1)} custom-call(bf16[1536,1408]{1,0:T(8,128)(2,1)S(1)} %get-tuple-element.63.refs_0_, bf16[1536,1408]{1,0:T(8,128)(2,1)S(1)} %get-tuple-element.48.refs_1_, f32[1,1408]{1,0:T(1,128)S(1)} %get-tuple-element.64.refs_2_, bf16[448,5632]{1,0:T(8,128)(2,1)S(1)} %get-tuple-element.65.refs_3_, ...), custom_call_target="tpu_custom_call" | custom-call | bytes 1024 | tf_op jit(solution)/shard_map/out_merge/pallas_call | solution.py:544
  68.1 2.4 %collective-permute-done.21.refs_9_ = bf16[960,128]{1,0:T(8,128)(2,1)S(1)} collective-permute-done((bf16[960,128]{1,0:T(8,128)(2,1)S(1)}, bf16[960,128]{1,0:T(8,128)(2,1)S(1)}, u32[]{:S(2)}, u32[]{:S(2)}) %collective-permute-start.21) | collective-permute-done | bytes 245792 | tf_op jit(solution)/shard_map/ppermute | solution.py:601
  71.0 1.0 collective-permute-done.22.refs_10_
  72.3 6.4 %out_merge.3 = (bf16[672,128]{1,0:T(8,128)(2,1)S(1)}, bf16[672,128]{1,0:T(8,128)(2,1)S(1)}, bf16[672,128]{1,0:T(8,128)(2,1)S(1)}, bf16[672,128]{1,0:T(8,128)(2,1)S(1)}) custom-call(bf16[1536,1408]{1,0:T(8,128)(2,1)S(1)} %get-tuple-element.63.refs_0_, bf16[1536,1408]{1,0:T(8,128)(2,1)S(1)} %get-tuple-element.48.refs_1_, ...), custom_call_target="tpu_custom_call" | custom-call | bytes 1024 | tf_op jit(solution)/shard_map/out_merge/pallas_call | solution.py:544
  78.8 5.2 %collective-permute-start.27 = (bf16[672,128]{1,0:T(8,128)(2,1)S(1)}, bf16[672,128]{1,0:T(8,128)(2,1)S(1)}, u32[]{:S(2)}, u32[]{:S(2)}) collective-permute-start(bf16[672,128]{1,0:T(8,128)(2,1)S(1)} %get-tuple-element.83), channel_id=1, source_target_pairs={{0,3},{1,2},{2,1},{3,0},{4,7},{5,6},{6,5},{7,4},{8,11},{9,10},{10,... | collective-permute-start | bytes 516104 | tf_op jit(solution)/shard_map/ppermute | solution.py:745
  85.4 3.8 %collective-permute-done.27.block = bf16[672,128]{1,0:T(8,128)(2,1)S(1)} collective-permute-done((bf16[672,128]{1,0:T(8,128)(2,1)S(1)}, bf16[672,128]{1,0:T(8,128)(2,1)S(1)}, u32[]{:S(2)}, u32[]{:S(2)}) %collective-permute-start.27) | collective-permute-done | bytes 172064 | tf_op jit(solution)/shard_map/ppermute | solution.py:745
  89.2 0.8 place_rows.5.refs_0_
  90.0 3.5 %collective-permute-done.26.block = bf16[672,128]{1,0:T(8,128)(2,1)S(1)} collective-permute-done((bf16[672,128]{1,0:T(8,128)(2,1)S(1)}, bf16[672,128]{1,0:T(8,128)(2,1)S(1)}, u32[]{:S(2)}, u32[]{:S(2)}) %collective-permute-start.26) | collective-permute-done | bytes 172064 | tf_op jit(solution)/shard_map/ppermute | solution.py:745
  93.5 0.8 place_rows.6.refs_0_
  94.2 4.6 %collective-permute-done.25.block = bf16[672,128]{1,0:T(8,128)(2,1)S(1)} collective-permute-done((bf16[672,128]{1,0:T(8,128)(2,1)S(1)}, bf16[672,128]{1,0:T(8,128)(2,1)S(1)}, u32[]{:S(2)}, u32[]{:S(2)}) %collective-permute-start.25) | collective-permute-done | bytes 172064 | tf_op jit(solution)/shard_map/ppermute | solution.py:745
  (51 shorter events, 11.1 us)
Async XLA Ops:
  1.5 11.9 %collective-permute-start.2 = (bf16[192,1536]{1,0:T(8,128)(2,1)S(1)}, bf16[192,1536]{1,0:T(8,128)(2,1)S(1)}, u32[]{:S(2)}, u32[]{:S(2)}) collective-permute-start(bf16[192,1536]{1,0:T(8,128)(2,1)S(1)} %payload.1.refs_0_), channel_id=1, source_target_pairs={{0,4},{4,0},{8,12},{12,8},{16,20},{20,16},{24,28},{28,24},{1,5},{5... | collective-permute-start | bytes 1769480 | tf_op jit(solution)/shard_map/ppermute | solution.py:601
  2.0 16.5 %collective-permute-start = (bf16[192,1536]{1,0:T(8,128)(2,1)S(1)}, bf16[192,1536]{1,0:T(8,128)(2,1)S(1)}, u32[]{:S(2)}, u32[]{:S(2)}) collective-permute-start(bf16[192,1536]{1,0:T(8,128)(2,1)S(1)} %payload.1.refs_0_), channel_id=1, source_target_pairs={{0,8},{4,12},{8,0},{12,4},{16,24},{20,28},{24,16},{28,20},{1,9},{5... | collective-permute-start | bytes 1769480 | tf_op jit(solution)/shard_map/ppermute | solution.py:601
  4.6 15.4 %collective-permute-start.1 = (bf16[192,1536]{1,0:T(8,128)(2,1)S(1)}, bf16[192,1536]{1,0:T(8,128)(2,1)S(1)}, u32[]{:S(2)}, u32[]{:S(2)}) collective-permute-start(bf16[192,1536]{1,0:T(8,128)(2,1)S(1)} %payload.1.refs_0_), channel_id=1, source_target_pairs={{0,16},{4,20},{8,24},{12,28},{16,0},{20,4},{24,8},{28,12},{1,17},{... | collective-permute-start | bytes 1769480 | tf_op jit(solution)/shard_map/ppermute | solution.py:601
  6.2 0.7 copy-start.1
  6.8 0.7 copy-start.2
  8.2 5.1 %copy-start = (bf16[128,512]{1,0:T(8,128)(2,1)S(1)}, bf16[128,512]{1,0:T(8,128)(2,1)}, u32[]{:S(2)}) copy-start(bf16[128,512]{1,0:T(8,128)(2,1)} %constant.24.clone.refs_2_.refs_4_) | copy-start | bytes 393220
  20.0 2.7 %collective-permute-start.6 = (bf16[192,1536]{1,0:T(8,128)(2,1)S(1)}, bf16[192,1536]{1,0:T(8,128)(2,1)S(1)}, u32[]{:S(2)}, u32[]{:S(2)}) collective-permute-start(bf16[192,1536]{1,0:T(8,128)(2,1)S(1)} %collective-permute-done.across_x.refs_0_), channel_id=1, source_target_pairs={{0,4},{4,0},{8,12},{12,8},{16,20},{20,16},{24,28},{28,24},{1,5},{5... | collective-permute-start | bytes 1769480 | tf_op jit(solution)/shard_map/ppermute | solution.py:601
  20.0 4.7 %collective-permute-start.5 = (bf16[192,1536]{1,0:T(8,128)(2,1)S(1)}, bf16[192,1536]{1,0:T(8,128)(2,1)S(1)}, u32[]{:S(2)}, u32[]{:S(2)}) collective-permute-start(bf16[192,1536]{1,0:T(8,128)(2,1)S(1)} %collective-permute-done.1.across_y.refs_0_), channel_id=1, source_target_pairs={{0,4},{4,0},{8,12},{12,8},{16,20},{20,16},{24,28},{28,24},{1,5},{5... | collective-permute-start | bytes 1769480 | tf_op jit(solution)/shard_map/ppermute | solution.py:601
  20.5 9.0 %collective-permute-start.3 = (bf16[96,1536]{1,0:T(8,128)(2,1)S(1)}, bf16[96,1536]{1,0:T(8,128)(2,1)S(1)}, u32[]{:S(2)}, u32[]{:S(2)}) collective-permute-start(bf16[96,1536]{1,0:T(8,128)(2,1)S(1)} %get-tuple-element.51), channel_id=1, source_target_pairs={{0,16},{4,20},{8,24},{12,28},{16,0},{20,4},{24,8},{28,12},{1,17},{... | collective-permute-start | bytes 884744 | tf_op jit(solution)/shard_map/ppermute | solution.py:601
  22.1 8.6 %collective-permute-start.4 = (bf16[96,1536]{1,0:T(8,128)(2,1)S(1)}, bf16[96,1536]{1,0:T(8,128)(2,1)S(1)}, u32[]{:S(2)}, u32[]{:S(2)}) collective-permute-start(bf16[96,1536]{1,0:T(8,128)(2,1)S(1)} %get-tuple-element.52), channel_id=1, source_target_pairs={{0,8},{4,12},{8,0},{12,4},{16,24},{20,28},{24,16},{28,20},{1,9},{5... | collective-permute-start | bytes 884744 | tf_op jit(solution)/shard_map/ppermute | solution.py:601
  30.7 1.6 %collective-permute-start.7 = (bf16[96,1536]{1,0:T(8,128)(2,1)S(1)}, bf16[96,1536]{1,0:T(8,128)(2,1)S(1)}, u32[]{:S(2)}, u32[]{:S(2)}) collective-permute-start(bf16[96,1536]{1,0:T(8,128)(2,1)S(1)} %collective-permute-done.3.refs_0_), channel_id=1, source_target_pairs={{0,4},{4,0},{8,12},{12,8},{16,20},{20,16},{24,28},{28,24},{1,5},{5... | collective-permute-start | bytes 884744 | tf_op jit(solution)/shard_map/ppermute | solution.py:601
  30.7 2.0 %collective-permute-start.8 = (bf16[96,1536]{1,0:T(8,128)(2,1)S(1)}, bf16[96,1536]{1,0:T(8,128)(2,1)S(1)}, u32[]{:S(2)}, u32[]{:S(2)}) collective-permute-start(bf16[96,1536]{1,0:T(8,128)(2,1)S(1)} %collective-permute-done.4.refs_1_), channel_id=1, source_target_pairs={{0,4},{4,0},{8,12},{12,8},{16,20},{20,16},{24,28},{28,24},{1,5},{5... | collective-permute-start | bytes 884744 | tf_op jit(solution)/shard_map/ppermute | solution.py:601
  34.7 5.1 %copy-start.4 = (s32[1,4]{1,0:T(1,128)S(1)}, s32[1,4]{1,0:T(1,128)}, u32[]{:S(2)}) copy-start(s32[1,4]{1,0:T(1,128)} %refs_0_.3) | copy-start | bytes 52
  38.8 10.2 %collective-permute-start.10 = (bf16[1344,128]{1,0:T(8,128)(2,1)S(1)}, bf16[1344,128]{1,0:T(8,128)(2,1)S(1)}, u32[]{:S(2)}, u32[]{:S(2)}) collective-permute-start(bf16[1344,128]{1,0:T(8,128)(2,1)S(1)} %attention.2.refs_5_), channel_id=1, source_target_pairs={{0,16},{4,20},{8,24},{12,28},{16,0},{20,4},{24,8},{28,12},{1,17},{... | collective-permute-start | bytes 1032200 | tf_op jit(solution)/shard_map/ppermute | solution.py:601
  39.4 9.8 %collective-permute-start.9 = (bf16[1344,128]{1,0:T(8,128)(2,1)S(1)}, bf16[1344,128]{1,0:T(8,128)(2,1)S(1)}, u32[]{:S(2)}, u32[]{:S(2)}) collective-permute-start(bf16[1344,128]{1,0:T(8,128)(2,1)S(1)} %attention.2.refs_5_), channel_id=1, source_target_pairs={{0,8},{4,12},{8,0},{12,4},{16,24},{20,28},{24,16},{28,20},{1,9},{5... | collective-permute-start | bytes 1032200 | tf_op jit(solution)/shard_map/ppermute | solution.py:601
  39.8 17.0 %collective-permute-start.13 = (bf16[1344,128]{1,0:T(8,128)(2,1)S(1)}, bf16[1344,128]{1,0:T(8,128)(2,1)S(1)}, u32[]{:S(2)}, u32[]{:S(2)}) collective-permute-start(bf16[1344,128]{1,0:T(8,128)(2,1)S(1)} %attention.2.refs_5_), channel_id=1, source_target_pairs={{0,4},{4,0},{8,12},{12,8},{16,20},{20,16},{24,28},{28,24},{1,5},{5... | collective-permute-start | bytes 1032200 | tf_op jit(solution)/shard_map/ppermute | solution.py:601
  49.2 5.5 %collective-permute-start.16 = (bf16[672,128]{1,0:T(8,128)(2,1)S(1)}, bf16[672,128]{1,0:T(8,128)(2,1)S(1)}, u32[]{:S(2)}, u32[]{:S(2)}) collective-permute-start(bf16[672,128]{1,0:T(8,128)(2,1)S(1)} %get-tuple-element.74), channel_id=1, source_target_pairs={{0,16},{4,20},{8,24},{12,28},{16,0},{20,4},{24,8},{28,12},{1,17},{... | collective-permute-start | bytes 516104 | tf_op jit(solution)/shard_map/ppermute | solution.py:601
  50.8 5.4 %collective-permute-start.17 = (bf16[672,128]{1,0:T(8,128)(2,1)S(1)}, bf16[672,128]{1,0:T(8,128)(2,1)S(1)}, u32[]{:S(2)}, u32[]{:S(2)}) collective-permute-start(bf16[672,128]{1,0:T(8,128)(2,1)S(1)} %get-tuple-element.75), channel_id=1, source_target_pairs={{0,8},{4,12},{8,0},{12,4},{16,24},{20,28},{24,16},{28,20},{1,9},{5... | collective-permute-start | bytes 516104 | tf_op jit(solution)/shard_map/ppermute | solution.py:601
  54.7 2.5 %collective-permute-start.18 = (bf16[672,128]{1,0:T(8,128)(2,1)S(1)}, bf16[672,128]{1,0:T(8,128)(2,1)S(1)}, u32[]{:S(2)}, u32[]{:S(2)}) collective-permute-start(bf16[672,128]{1,0:T(8,128)(2,1)S(1)} %collective-permute-done.16.refs_11_), channel_id=1, source_target_pairs={{0,4},{4,0},{8,12},{12,8},{16,20},{20,16},{24,28},{28,24},{1,5},{5... | collective-permute-start | bytes 516104 | tf_op jit(solution)/shard_map/ppermute | solution.py:601
  56.2 2.5 %collective-permute-start.19 = (bf16[672,128]{1,0:T(8,128)(2,1)S(1)}, bf16[672,128]{1,0:T(8,128)(2,1)S(1)}, u32[]{:S(2)}, u32[]{:S(2)}) collective-permute-start(bf16[672,128]{1,0:T(8,128)(2,1)S(1)} %collective-permute-done.17.refs_12_), channel_id=1, source_target_pairs={{0,4},{4,0},{8,12},{12,8},{16,20},{20,16},{24,28},{28,24},{1,5},{5... | collective-permute-start | bytes 516104 | tf_op jit(solution)/shard_map/ppermute | solution.py:601
  56.2 4.0 %collective-permute-start.14 = (bf16[1344,128]{1,0:T(8,128)(2,1)S(1)}, bf16[1344,128]{1,0:T(8,128)(2,1)S(1)}, u32[]{:S(2)}, u32[]{:S(2)}) collective-permute-start(bf16[1344,128]{1,0:T(8,128)(2,1)S(1)} %collective-permute-done.9.across_x.refs_7_), channel_id=1, source_target_pairs={{0,4},{4,0},{8,12},{12,8},{16,20},{20,16},{24,28},{28,24},{1,5},{5... | collective-permute-start | bytes 1032200 | tf_op jit(solution)/shard_map/ppermute | solution.py:601
  56.7 3.5 %collective-permute-start.15 = (bf16[1344,128]{1,0:T(8,128)(2,1)S(1)}, bf16[1344,128]{1,0:T(8,128)(2,1)S(1)}, u32[]{:S(2)}, u32[]{:S(2)}) collective-permute-start(bf16[1344,128]{1,0:T(8,128)(2,1)S(1)} %collective-permute-done.10.across_y.refs_9_), channel_id=1, source_target_pairs={{0,4},{4,0},{8,12},{12,8},{16,20},{20,16},{24,28},{28,24},{1,5},{5... | collective-permute-start | bytes 1032200 | tf_op jit(solution)/shard_map/ppermute | solution.py:601
  56.7 10.8 %collective-permute-start.23 = (bf16[960,128]{1,0:T(8,128)(2,1)S(1)}, bf16[960,128]{1,0:T(8,128)(2,1)S(1)}, u32[]{:S(2)}, u32[]{:S(2)}) collective-permute-start(bf16[960,128]{1,0:T(8,128)(2,1)S(1)} %get-tuple-element.76.refs_5_), channel_id=1, source_target_pairs={{0,24},{4,28},{8,16},{12,20},{16,8},{20,12},{24,0},{28,4},{1,25},{... | collective-permute-start | bytes 737288 | tf_op jit(solution)/shard_map/ppermute | solution.py:601
  57.2 13.2 %collective-permute-start.21 = (bf16[960,128]{1,0:T(8,128)(2,1)S(1)}, bf16[960,128]{1,0:T(8,128)(2,1)S(1)}, u32[]{:S(2)}, u32[]{:S(2)}) collective-permute-start(bf16[960,128]{1,0:T(8,128)(2,1)S(1)} %get-tuple-element.76.refs_5_), channel_id=1, source_target_pairs={{0,16},{4,20},{8,24},{12,28},{16,0},{20,4},{24,8},{28,12},{1,17},{... | collective-permute-start | bytes 737288 | tf_op jit(solution)/shard_map/ppermute | solution.py:601
  58.8 11.7 %collective-permute-start.12 = (bf16[960,128]{1,0:T(8,128)(2,1)S(1)}, bf16[960,128]{1,0:T(8,128)(2,1)S(1)}, u32[]{:S(2)}, u32[]{:S(2)}) collective-permute-start(bf16[960,128]{1,0:T(8,128)(2,1)S(1)} %get-tuple-element.76.refs_5_), channel_id=1, source_target_pairs={{0,8},{4,12},{8,0},{12,4},{16,24},{20,28},{24,16},{28,20},{1,9},{5... | collective-permute-start | bytes 737288 | tf_op jit(solution)/shard_map/ppermute | solution.py:601
  60.3 10.7 %collective-permute-start.11 = (bf16[960,128]{1,0:T(8,128)(2,1)S(1)}, bf16[960,128]{1,0:T(8,128)(2,1)S(1)}, u32[]{:S(2)}, u32[]{:S(2)}) collective-permute-start(bf16[960,128]{1,0:T(8,128)(2,1)S(1)} %get-tuple-element.76.refs_5_), channel_id=1, source_target_pairs={{0,4},{4,0},{8,12},{12,8},{16,20},{20,16},{24,28},{28,24},{1,5},{5... | collective-permute-start | bytes 737288 | tf_op jit(solution)/shard_map/ppermute | solution.py:601
  67.5 3.5 %collective-permute-start.24 = (bf16[960,128]{1,0:T(8,128)(2,1)S(1)}, bf16[960,128]{1,0:T(8,128)(2,1)S(1)}, u32[]{:S(2)}, u32[]{:S(2)}) collective-permute-start(bf16[960,128]{1,0:T(8,128)(2,1)S(1)} %collective-permute-done.23.refs_11_), channel_id=1, source_target_pairs={{0,4},{4,0},{8,12},{12,8},{16,20},{20,16},{24,28},{28,24},{1,5},{5... | collective-permute-start | bytes 737288 | tf_op jit(solution)/shard_map/ppermute | solution.py:601
  70.5 1.5 %collective-permute-start.22 = (bf16[960,128]{1,0:T(8,128)(2,1)S(1)}, bf16[960,128]{1,0:T(8,128)(2,1)S(1)}, u32[]{:S(2)}, u32[]{:S(2)}) collective-permute-start(bf16[960,128]{1,0:T(8,128)(2,1)S(1)} %collective-permute-done.21.refs_9_), channel_id=1, source_target_pairs={{0,4},{4,0},{8,12},{12,8},{16,20},{20,16},{24,28},{28,24},{1,5},{5... | collective-permute-start | bytes 737288 | tf_op jit(solution)/shard_map/ppermute | solution.py:601
  70.5 1.9 %collective-permute-start.20 = (bf16[960,128]{1,0:T(8,128)(2,1)S(1)}, bf16[960,128]{1,0:T(8,128)(2,1)S(1)}, u32[]{:S(2)}, u32[]{:S(2)}) collective-permute-start(bf16[960,128]{1,0:T(8,128)(2,1)S(1)} %collective-permute-done.12.refs_7_), channel_id=1, source_target_pairs={{0,4},{4,0},{8,12},{12,8},{16,20},{20,16},{24,28},{28,24},{1,5},{5... | collective-permute-start | bytes 737288 | tf_op jit(solution)/shard_map/ppermute | solution.py:601
  78.8 10.4 %collective-permute-start.27 = (bf16[672,128]{1,0:T(8,128)(2,1)S(1)}, bf16[672,128]{1,0:T(8,128)(2,1)S(1)}, u32[]{:S(2)}, u32[]{:S(2)}) collective-permute-start(bf16[672,128]{1,0:T(8,128)(2,1)S(1)} %get-tuple-element.83), channel_id=1, source_target_pairs={{0,3},{1,2},{2,1},{3,0},{4,7},{5,6},{6,5},{7,4},{8,11},{9,10},{10,... | collective-permute-start | bytes 516104 | tf_op jit(solution)/shard_map/ppermute | solution.py:745
  84.0 9.5 %collective-permute-start.26 = (bf16[672,128]{1,0:T(8,128)(2,1)S(1)}, bf16[672,128]{1,0:T(8,128)(2,1)S(1)}, u32[]{:S(2)}, u32[]{:S(2)}) collective-permute-start(bf16[672,128]{1,0:T(8,128)(2,1)S(1)} %get-tuple-element.82), channel_id=1, source_target_pairs={{0,1},{1,0},{2,3},{3,2},{4,5},{5,4},{6,7},{7,6},{8,9},{9,8},{10,11... | collective-permute-start | bytes 516104 | tf_op jit(solution)/shard_map/ppermute | solution.py:745
  84.0 14.9 %collective-permute-start.25 = (bf16[672,128]{1,0:T(8,128)(2,1)S(1)}, bf16[672,128]{1,0:T(8,128)(2,1)S(1)}, u32[]{:S(2)}, u32[]{:S(2)}) collective-permute-start(bf16[672,128]{1,0:T(8,128)(2,1)S(1)} %get-tuple-element.81), channel_id=1, source_target_pairs={{0,2},{1,3},{2,0},{3,1},{4,6},{5,7},{6,4},{7,5},{8,10},{9,11},{10,... | collective-permute-start | bytes 516104 | tf_op jit(solution)/shard_map/ppermute | solution.py:745
  (1 other events, 0.7 us)

commit v17 on v15

--- a/solution.py
+++ b/solution.py
@@ -151,6 +151,8 @@
 POSITIONS = 64
 FAR_APART = -(2.0**100)
 IMAGE_LANE = 96
+PAIR_ROWS = 3 * LANES
+PAIR_CHIPS = (0, 3, 1, 2)
 NORM_ROWS = 16
 CHUNKS = (768, 768)
 
@@ -405,12 +407,16 @@
         row_out[...] = row[...].astype(jnp.float32)[None, :]
     rest = 2 * HD - LANES
     copies = [(qkv_weight, qkv_buffer), (spread, spread_buffer)]
-    out[shards * LANES :] = jnp.zeros((shards // 2 * LANES, D), jnp.bfloat16)
+    for pair in range(shards // 2):
+        low = pair * PAIR_ROWS + 2 * LANES
+        out[low : low + LANES] = jnp.zeros((LANES, D), jnp.bfloat16)
     for place in range(shards):
         start = pl.multiple_of(ids[place] * (2 * HD), 16)
-        to = (shards + place // 2) * LANES + place % 2 * rest
+        base = place // 2 * PAIR_ROWS
+        wide = base + place % 2 * LANES
+        to = base + 2 * LANES + place % 2 * rest
         copies.append(
-            (out_weight.at[pl.ds(start, LANES), :], out.at[pl.ds(place * LANES, LANES), :])
+            (out_weight.at[pl.ds(start, LANES), :], out.at[pl.ds(wide, LANES), :])
         )
         copies.append((out_weight.at[pl.ds(start + LANES, rest), :], out.at[pl.ds(to, rest), :]))
     copies.append((merge_weight, merge))
@@ -457,34 +463,26 @@
     )(ids, *map(in_hbm, operands), *rows)
 
 
-def merge_kernel(start, counts, packs, last, *refs):
-    inputs, weight, gain, merge_weight, bias = refs[:5]
-    pieces = refs[5 : 5 + sum(counts)]
-    *refs, state, tokens = refs[5 + sum(counts) :]
-    rows = state.shape[1]
+def out_product(sources, rows, weight, first_pair):
     half = rows // 2
     rest = 2 * HD - LANES
-    sources, at = [], 0
-    for count in counts:
-        sources.append(stacked(pieces[at : at + count]))
-        at += count
-    shards = len(sources)
     lane = lax.broadcasted_iota(jnp.int32, (half, LANES), 1)
-    lined = [source[:rows, :] for source in sources]
-    for pair in range(shards // 2):
-        mine = sources[2 * pair][rows:, :].astype(jnp.float32)
-        other = sources[2 * pair + 1][rows:, :].astype(jnp.float32)
+    lined = []
+    for same, swapped in zip(sources[::2], sources[1::2]):
+        mine, other = same[rows:, :].astype(jnp.float32), swapped[rows:, :].astype(jnp.float32)
         upper = jnp.where(lane < rest, mine, pltpu.roll(other, rest, 1))
         lower = jnp.where(lane < rest, pltpu.roll(mine, LANES - rest, 1), other)
-        lined.append(jnp.concatenate([upper, lower], axis=0).astype(jnp.bfloat16))
-    mixed = jnp.dot(
-        jnp.concatenate(lined, axis=1), weight[...], preferred_element_type=jnp.float32
-    )
-    for column in range(D // LANES):
-        lanes = slice(column * LANES, (column + 1) * LANES)
-        before = inputs[start : start + rows, lanes]
-        state[column] = before.astype(jnp.float32) + mixed[:, lanes]
-    groups = rows // 4
+        tail = jnp.concatenate([upper, lower], axis=0).astype(jnp.bfloat16)
+        lined += [same[:rows, :], swapped[:rows, :], tail]
+    low = first_pair * PAIR_ROWS
+    high = low + len(sources) // 2 * PAIR_ROWS
+    return jnp.dot(
+        jnp.concatenate(lined, axis=1), weight[low:high, :], preferred_element_type=jnp.float32
+    )
+
+
+def merged_product(state, tokens, gain, merge_weight, bias):
+    groups = tokens.shape[0]
     for block in range(0, groups, NORM_ROWS):
         for quadrant in range(4):
             at = pl.ds(4 * block + quadrant, NORM_ROWS, stride=4)
@@ -497,10 +495,46 @@
     total = bias[...] + lax.dot_general(
         tokens[...], merge_weight[...], (((1,), (1,)), ((), ())), preferred_element_type=jnp.float32
     )
-    total = total.astype(jnp.bfloat16)
-    if not last:
-        refs[0][...] = total
-        return
+    return total.astype(jnp.bfloat16)
+
+
+def split(pieces, counts):
+    sources, at = [], 0
+    for count in counts:
+        sources.append(stacked(pieces[at : at + count]))
+        at += count
+    return sources
+
+
+def add_inputs(state, inputs, start, mixed):
+    for column in range(D // LANES):
+        lanes = slice(column * LANES, (column + 1) * LANES)
+        before = inputs[start : start + mixed.shape[0], lanes]
+        state[column] = before.astype(jnp.float32) + mixed[:, lanes]
+
+
+def merge_kernel(start, counts, inputs, weight, gain, merge_weight, bias, *refs):
+    *pieces, out, state, tokens = refs
+    mixed = out_product(split(pieces, counts), state.shape[1], weight, 0)
+    add_inputs(state, inputs, start, mixed)
+    out[...] = merged_product(state, tokens, gain, merge_weight, bias)
+
+
+def partial_kernel(start, counts, inputs, weight, *refs):
+    *pieces, state = refs
+    mixed = out_product(split(pieces, counts), state.shape[1], weight, 0)
+    add_inputs(state, inputs, start, mixed)
+
+
+def finish_kernel(
+    first_pair, packs, partial, weight, gain, merge_weight, bias, *refs
+):
+    *refs, state, tokens = refs
+    sources, refs = [one[...] for one in refs[:4]], refs[4:]
+    mixed = out_product(sources, state.shape[1], weight, first_pair)
+    for column in range(D // LANES):
+        state[column] = partial[column] + mixed[:, column * LANES : (column + 1) * LANES]
+    total = merged_product(state, tokens, gain, merge_weight, bias)
     note, *earlier = refs[:-packs]
     me = lax.axis_index("pack")
     outs = refs[-packs:]
@@ -528,38 +562,60 @@
         out[whole * most :, :] = jnp.concatenate([low, up], axis=1).astype(jnp.bfloat16)
 
 
-def merge_call(start, rows, sources, inputs, weight, gain, merge_weight, bias, packs, route):
-    groups = rows // 4
-    width = merge_weight.shape[0]
-    pieces = [piece for source in sources for piece in source]
+def vmem_call(kernel, name, operands, shapes, scratch):
     vmem = pl.BlockSpec(memory_space=pltpu.VMEM)
-    operands = [in_vmem(inputs), in_vmem(weight), gain, in_vmem(merge_weight), bias, *pieces]
-    specs = [vmem] * len(operands)
-    shapes = [jax.ShapeDtypeStruct((groups, width), jnp.bfloat16)]
-    if route:
-        most, *others = route
-        operands += others
-        specs += [vmem] * len(others)
-        shapes = [jax.ShapeDtypeStruct((most * width // LANES, LANES), jnp.bfloat16)] * packs
     return pl.pallas_call(
-        functools.partial(
-            merge_kernel, start, [len(source) for source in sources], packs, bool(route)
-        ),
-        in_specs=specs,
+        kernel,
+        in_specs=[vmem] * len(operands),
         out_specs=[vmem] * len(shapes),
-        scratch_shapes=[
-            pltpu.VMEM((D // LANES, rows, LANES), jnp.float32),
-            pltpu.VMEM((groups, 4 * D), jnp.bfloat16),
-        ],
+        scratch_shapes=scratch,
         out_shape=shapes,
         compiler_params=pltpu.CompilerParams(vmem_limit_bytes=20 << 20),
-        cost_estimate=pl.CostEstimate(
-            flops=0,
-            bytes_accessed=1024,
-            transcendentals=rows,
-        ),
-        name="out_merge",
+        cost_estimate=pl.CostEstimate(flops=0, bytes_accessed=1024, transcendentals=0),
+        name=name,
     )(*operands)
+
+
+def merge_scratch(rows):
+    return [
+        pltpu.VMEM((D // LANES, rows, LANES), jnp.float32),
+        pltpu.VMEM((rows // 4, 4 * D), jnp.bfloat16),
+    ]
+
+
+def merge_call(start, rows, sources, inputs, weight, gain, merge_weight, bias):
+    pieces = [piece for source in sources for piece in source]
+    return vmem_call(
+        functools.partial(merge_kernel, start, [len(source) for source in sources]),
+        "out_merge",
+        [in_vmem(inputs), in_vmem(weight), gain, in_vmem(merge_weight), bias, *pieces],
+        [jax.ShapeDtypeStruct((rows // 4, merge_weight.shape[0]), jnp.bfloat16)],
+        merge_scratch(rows),
+    )[0]
+
+
+def partial_call(start, rows, sources, inputs, weight):
+    return vmem_call(
+        functools.partial(partial_kernel, start, [1] * len(sources)),
+        "out_near",
+        [in_vmem(inputs), in_vmem(weight), *sources],
+        [pltpu.VMEM((D // LANES, rows, LANES), jnp.float32)],
+        [],
+    )[0]
+
+
+def finish_call(
+    rows, partial, sources, first_pair, weight, gain, merge_weight, bias, packs, most, note, earlier
+):
+    shape = (most * merge_weight.shape[0] // LANES, LANES)
+    return vmem_call(
+        functools.partial(finish_kernel, first_pair, packs),
+        "out_far_merge",
+        [in_vmem(partial), in_vmem(weight), gain, in_vmem(merge_weight), bias, *sources]
+        + [note, earlier],
+        [jax.ShapeDtypeStruct(shape, jnp.bfloat16)] * packs,
+        merge_scratch(rows),
+    )
 
 
 def place_kernel(place, block, *refs):
@@ -698,7 +754,7 @@
     order = weight_order(heads_here)
     spread = (order[:, None] == np.arange(qkv_weight.shape[1])[None, :]).astype(jnp.bfloat16)
     table = jnp.asarray(angle_table(heads_here))
-    ids = jnp.stack([me ^ place for place in range(shards)])
+    ids = jnp.stack([me ^ (2 * chip + core) for chip in PAIR_CHIPS for core in range(2)])
     gain, merge_gain_row, bias, ordered, merge_rows, weight = prepare_call(
         shards,
         ids,
@@ -733,14 +789,28 @@
     (late,) = after([late], *halves)
     late_shares = [late] + [send_seq(late, flip) for flip in (2, 4, 6)]
     near = [send_seq(one, 1) for one in (across_x, across_y)]
-    merge = lambda start, rows, sources, route: merge_call(
-        start, rows, sources, inputs, ordered, merge_gain_row, merge_rows, bias, packs, route
-    )
-    sources = [[own], [own_swap], [across_x], near[:1], [across_y], near[1:], far]
-    (projected,) = merge(0, first_rows, sources + [[send_seq(one, 1) for one in far]], ())
+    sources = [[own], [own_swap], far, [send_seq(one, 1) for one in far]]
+    sources += [[across_x], near[:1], [across_y], near[1:]]
+    projected = merge_call(
+        0, first_rows, sources, inputs, ordered, merge_gain_row, merge_rows, bias
+    )
     late_shares[1:] = [after([one], projected)[0] for one in late_shares[1:]]
-    sources = [[one] for share in late_shares for one in (share, send_seq(share, 1))]
-    made = merge(first_rows, last_rows, sources, (most, note, projected))
+    pairs = [[late_shares[chip], send_seq(late_shares[chip], 1)] for chip in PAIR_CHIPS]
+    partial = partial_call(first_rows, last_rows, pairs[0] + pairs[1], inputs, ordered)
+    made = finish_call(
+        last_rows,
+        partial,
+        pairs[2] + pairs[3],
+        2,
+        ordered,
+        merge_gain_row,
+        merge_rows,
+        bias,
+        packs,
+        most,
+        note,
+        projected,
+    )
     sent = {
         flip: lax.ppermute(made[flip], "pack", [(z, z ^ flip) for z in range(packs)])
         for flip in range(packs - 1, 0, -1)

time: 96.7 us -> 98.2 us (1.016)
  Pallas kernels: 39.1 us -> 42.2 us
  starting transfers between devices: 21.5 us -> 20.3 us
    pallas_call x2, Pallas kernels: 8.25 us -> 10.8 us  [attention_call(): pl.pallas_call(functools.partial(attention_kernel, start, owners[0].shape...]
    ppermute x25, waiting for transfers between devices: 22.3 us -> 20.8 us  [send_seq(): return lax.ppermute(value, 'seq', [(i, i ^ flip) for i in range(size)])]
    ppermute x3, waiting for transfers between devices: 10.6 us -> 12 us  [fast_local(): lax.ppermute(made[flip], 'pack', [(z, z ^ flip) for z in range(packs)])]
    ppermute x3, starting transfers between devices: 5.6 us -> 4.45 us  [fast_local(): lax.ppermute(made[flip], 'pack', [(z, z ^ flip) for z in range(packs)])]
    pallas_call x2 -> x3, Pallas kernels: 13.4 us -> 13.9 us  [vmem_call(): pl.pallas_call(kernel, in_specs=[vmem] * len(operands), out_specs=[vmem]...]
  transfers between devices with their start and end apart: 28 -> 28, of which waited for: 19 -> 16; matrix products, arithmetic and copies ran while one was open for 0% -> 0% of each run, Pallas kernels for 25% -> 28%
where the time goes in v17:
time: 98.2 us; the launch traced here: 97.9 us
  Pallas kernels  42.2 us (43%)
  waiting for transfers between devices  32.8 us (33%)
  starting transfers between devices  20.3 us (21%)
  local copies, waits for them, and re-layouts  2.15 us (2%)
    ppermute x25, waiting for transfers between devices, send_seq(): return lax.ppermute(value, 'seq', [(i, i ^ flip) for i in range(size)])  20.8 us
    ppermute x25, starting transfers between devices, send_seq(): return lax.ppermute(value, 'seq', [(i, i ^ flip) for i in range(size)])  15.8 us
    pallas_call x3, Pallas kernels, vmem_call(): pl.pallas_call(kernel, in_specs=[vmem] * len(operands), out_specs=[vmem]...  13.9 us
    ppermute x3, waiting for transfers between devices, fast_local(): lax.ppermute(made[flip], 'pack', [(z, z ^ flip) for z in range(packs)])  12 us
    pallas_call x2, Pallas kernels, attention_call(): pl.pallas_call(functools.partial(attention_kernel, start, owners[0].shape...  10.8 us
    pallas_call x4, Pallas kernels, qkv_call(): pl.pallas_call(functools.partial(qkv_kernel, len(first), flip), in_specs=...  7.85 us
    pallas_call x1, Pallas kernels, prepare_call(): pl.pallas_call(functools.partial(prepare_kernel, shards), in_specs=[pl.Bl...  5.1 us
    ppermute x3, starting transfers between devices, fast_local(): lax.ppermute(made[flip], 'pack', [(z, z ^ flip) for z in range(packs)])  4.45 us
  transfers between devices with their start and end apart: 28, of which 16 were waited for; matrix products, arithmetic and copies ran while one was open for 0% of the time, Pallas kernels for 28%

profile of v17, /device:TPU:0, one launch (start us, length us, event | category | flops | bytes accessed | tf_op | source)
XLA Modules:
  0.0 97.9 jit_solution(9528999538731138430)
XLA Ops:
  0.0 1.5 %payload.1.refs_0_ = bf16[192,1536]{1,0:T(8,128)(2,1)S(1)} custom-call(s32[1,192]{1,0:T(1,128)} %segments.1, s32[1,192]{1,0:T(1,128)} %rows.1, s32[1,192]{1,0:T(1,128)} %columns.1, s32[1,192]{1,0:T(1,128)} %mask.1, bf16[1408]{0:T(1024)(128)(2,1)} %embed.1, bf16[1,192,1408]{2,1,0:T(8,128)(2,1)} %patches.1), custom_call_target="tpu_custom_call" | custom-call | flops 270336 | bytes 1081344 | tf_op jit(solution)/shard_map/payload/pallas_call | solution.py:205
  2.0 2.6 %collective-permute-start = (bf16[192,1536]{1,0:T(8,128)(2,1)S(1)}, bf16[192,1536]{1,0:T(8,128)(2,1)S(1)}, u32[]{:S(2)}, u32[]{:S(2)}) collective-permute-start(bf16[192,1536]{1,0:T(8,128)(2,1)S(1)} %payload.1.refs_0_), channel_id=1, source_target_pairs={{0,8},{4,12},{8,0},{12,4},{16,24},{20,28},{24,16},{28,20},{1,9},{5... | collective-permute-start | bytes 1769480 | tf_op jit(solution)/shard_map/ppermute | solution.py:657
  4.6 1.5 %collective-permute-start.1 = (bf16[192,1536]{1,0:T(8,128)(2,1)S(1)}, bf16[192,1536]{1,0:T(8,128)(2,1)S(1)}, u32[]{:S(2)}, u32[]{:S(2)}) collective-permute-start(bf16[192,1536]{1,0:T(8,128)(2,1)S(1)} %payload.1.refs_0_), channel_id=1, source_target_pairs={{0,16},{4,20},{8,24},{12,28},{16,0},{20,4},{24,8},{28,12},{1,17},{... | collective-permute-start | bytes 1769480 | tf_op jit(solution)/shard_map/ppermute | solution.py:657
  8.2 5.1 %prepare.1 = (f32[1,1408]{1,0:T(1,128)S(1)}, f32[1,1408]{1,0:T(1,128)S(1)}, f32[1,448]{1,0:T(1,128)S(1)}, bf16[1536,1408]{1,0:T(8,128)(2,1)S(1)}, bf16[448,5632]...) custom-call(s32[8]{0:T(128)S(1)} %stack.35.ids, bf16[1408,1408]{1,0:T(8,128)(2,1)} %out_weight.1, ...), custom_call_target="tpu_custom_call" | custom-call | flops 1141899264 | bytes 20996096 | tf_op jit(solution)/shard_map/prepare/pallas_call | solution.py:443
  13.3 2.0 %norm_qkv.4 = (bf16[1536,1408]{1,0:T(8,128)(2,1)S(1)}, bf16[1536,1024]{1,0:T(8,128)(2,1)S(1)}, bf16[1536,128]{1,0:T(8,128)(2,1)S(1)}) custom-call(bf16[192,1536]{1,0:T(8,128)(2,1)S(1)} %payload.1.refs_0_, bf16[192,1536]{1,0:T(8,128)(2,1)S(1)} %collective-permute-done.2.refs_1_, bf16[128,512]{1,0:T(8,128)(2,1)S(1)} %copy-done, ...), custom_call_target="tpu_custom_call" | custom-call | flops 2491416576 | bytes 6488064 | tf_op jit(solution)/shard_map/norm_qkv/pallas_call | solution.py:281
  15.3 3.1 %collective-permute-done.across_x.refs_0_ = bf16[192,1536]{1,0:T(8,128)(2,1)S(1)} collective-permute-done((bf16[192,1536]{1,0:T(8,128)(2,1)S(1)}, bf16[192,1536]{1,0:T(8,128)(2,1)S(1)}, u32[]{:S(2)}, u32[]{:S(2)}) %collective-permute-start) | collective-permute-done | bytes 589856 | tf_op jit(solution)/shard_map/ppermute | solution.py:657
  18.5 1.5 %collective-permute-done.1.across_y.refs_0_ = bf16[192,1536]{1,0:T(8,128)(2,1)S(1)} collective-permute-done((bf16[192,1536]{1,0:T(8,128)(2,1)S(1)}, bf16[192,1536]{1,0:T(8,128)(2,1)S(1)}, u32[]{:S(2)}, u32[]{:S(2)}) %collective-permute-start.1) | collective-permute-done | bytes 589856 | tf_op jit(solution)/shard_map/ppermute | solution.py:657
  20.5 1.6 %collective-permute-start.3 = (bf16[96,1536]{1,0:T(8,128)(2,1)S(1)}, bf16[96,1536]{1,0:T(8,128)(2,1)S(1)}, u32[]{:S(2)}, u32[]{:S(2)}) collective-permute-start(bf16[96,1536]{1,0:T(8,128)(2,1)S(1)} %get-tuple-element.51), channel_id=1, source_target_pairs={{0,16},{4,20},{8,24},{12,28},{16,0},{20,4},{24,8},{28,12},{1,17},{... | collective-permute-start | bytes 884744 | tf_op jit(solution)/shard_map/ppermute | solution.py:657
  22.6 2.0 %norm_qkv.5 = (bf16[1536,1408]{1,0:T(8,128)(2,1)S(1)}, bf16[1536,1024]{1,0:T(8,128)(2,1)S(1)}, bf16[1536,128]{1,0:T(8,128)(2,1)S(1)}) custom-call(bf16[192,1536]{1,0:T(8,128)(2,1)S(1)} %collective-permute-done.across_x.refs_0_, bf16[192,1536]{1,0:T(8,128)(2,1)S(1)} %collective-permute-done.6.refs_1_, ...), custom_call_target="tpu_custom_call", output_to_operand_aliasing={{0}: (5, {}), {1}: (6, {}), {2}: (7, {})} | custom-call | flops 2491416576 | bytes 6488064 | tf_op jit(solution)/shard_map/norm_qkv/pallas_call | solution.py:281
  24.6 2.0 %norm_qkv.6 = (bf16[1536,1408]{1,0:T(8,128)(2,1)S(1)}, bf16[1536,1024]{1,0:T(8,128)(2,1)S(1)}, bf16[1536,128]{1,0:T(8,128)(2,1)S(1)}) custom-call(bf16[192,1536]{1,0:T(8,128)(2,1)S(1)} %collective-permute-done.1.across_y.refs_0_, bf16[192,1536]{1,0:T(8,128)(2,1)S(1)} %collective-permute-done.5.refs_1_, ...), custom_call_target="tpu_custom_call", output_to_operand_aliasing={{0}: (5, {}), {1}: (6, {}), {2}: (7, {})} | custom-call | flops 2491416576 | bytes 6488064 | tf_op jit(solution)/shard_map/norm_qkv/pallas_call | solution.py:281
  26.6 2.9 %collective-permute-done.3.refs_0_ = bf16[96,1536]{1,0:T(8,128)(2,1)S(1)} collective-permute-done((bf16[96,1536]{1,0:T(8,128)(2,1)S(1)}, bf16[96,1536]{1,0:T(8,128)(2,1)S(1)}, u32[]{:S(2)}, u32[]{:S(2)}) %collective-permute-start.3) | collective-permute-done | bytes 294944 | tf_op jit(solution)/shard_map/ppermute | solution.py:657
  29.5 1.2 %collective-permute-done.4.refs_1_ = bf16[96,1536]{1,0:T(8,128)(2,1)S(1)} collective-permute-done((bf16[96,1536]{1,0:T(8,128)(2,1)S(1)}, bf16[96,1536]{1,0:T(8,128)(2,1)S(1)}, u32[]{:S(2)}, u32[]{:S(2)}) %collective-permute-start.4) | collective-permute-done | bytes 294944 | tf_op jit(solution)/shard_map/ppermute | solution.py:657
  31.2 1.1 %collective-permute-done.7.refs_2_ = bf16[96,1536]{1,0:T(8,128)(2,1)S(1)} collective-permute-done((bf16[96,1536]{1,0:T(8,128)(2,1)S(1)}, bf16[96,1536]{1,0:T(8,128)(2,1)S(1)}, u32[]{:S(2)}, u32[]{:S(2)}) %collective-permute-start.7) | collective-permute-done | bytes 294944 | tf_op jit(solution)/shard_map/ppermute | solution.py:657
  32.7 1.9 %norm_qkv.7 = (bf16[1536,1408]{1,0:T(8,128)(2,1)S(1)}, bf16[1536,1024]{1,0:T(8,128)(2,1)S(1)}, bf16[1536,128]{1,0:T(8,128)(2,1)S(1)}) custom-call(bf16[96,1536]{1,0:T(8,128)(2,1)S(1)} %collective-permute-done.3.refs_0_, bf16[96,1536]{1,0:T(8,128)(2,1)S(1)} %collective-permute-done.4.refs_1_, ...), custom_call_target="tpu_custom_call", output_to_operand_aliasing={{0}: (7, {}), {1}: (8, {}), {2}: (9, {})} | custom-call | flops 2491416576 | bytes 6488064 | tf_op jit(solution)/shard_map/norm_qkv/pallas_call | solution.py:281
  34.7 5.0 %attention.2.refs_0_ = bf16[1152,128]{1,0:T(8,128)(2,1)S(1)} custom-call(bf16[1536,128]{1,0:T(8,128)(2,1)S(1)} %get-tuple-element.66.labels, bf16[1536,1024]{1,0:T(8,128)(2,1)S(1)} %get-tuple-element.67.block), custom_call_target="tpu_custom_call" | custom-call | flops 3019898880 | bytes 3145728 | tf_op jit(solution)/shard_map/attention/pallas_call | solution.py:385
  40.7 5.8 %attention.3 = (bf16[1152,128]{1,0:T(8,128)(2,1)S(1)}, bf16[16,128]{1,0:T(8,128)(2,1)S(1)}) custom-call(bf16[1536,128]{1,0:T(8,128)(2,1)S(1)} %get-tuple-element.66.labels, bf16[1536,1024]{1,0:T(8,128)(2,1)S(1)} %get-tuple-element.67.block, s32[1,4]{1,0:T(1,128)S(1)} %copy-done.4), custom_call_target="tpu_custom_call" | custom-call | flops 3019898880 | bytes 3145728 | tf_op jit(solution)/shard_map/attention/pallas_call | solution.py:385
  46.5 2.4 %collective-permute-done.10.across_y.refs_8_ = bf16[1152,128]{1,0:T(8,128)(2,1)S(1)} collective-permute-done((bf16[1152,128]{1,0:T(8,128)(2,1)S(1)}, bf16[1152,128]{1,0:T(8,128)(2,1)S(1)}, u32[]{:S(2)}, u32[]{:S(2)}) %collective-permute-start.10) | collective-permute-done | bytes 294944 | tf_op jit(solution)/shard_map/ppermute | solution.py:657
  49.6 1.6 %collective-permute-start.14 = (bf16[576,128]{1,0:T(8,128)(2,1)S(1)}, bf16[576,128]{1,0:T(8,128)(2,1)S(1)}, u32[]{:S(2)}, u32[]{:S(2)}) collective-permute-start(bf16[576,128]{1,0:T(8,128)(2,1)S(1)} %get-tuple-element.71), channel_id=1, source_target_pairs={{0,16},{4,20},{8,24},{12,28},{16,0},{20,4},{24,8},{28,12},{1,17},{... | collective-permute-start | bytes 442376 | tf_op jit(solution)/shard_map/ppermute | solution.py:657
  52.1 4.3 %collective-permute-done.14.refs_2_ = bf16[576,128]{1,0:T(8,128)(2,1)S(1)} collective-permute-done((bf16[576,128]{1,0:T(8,128)(2,1)S(1)}, bf16[576,128]{1,0:T(8,128)(2,1)S(1)}, u32[]{:S(2)}, u32[]{:S(2)}) %collective-permute-start.14) | collective-permute-done | bytes 147488 | tf_op jit(solution)/shard_map/ppermute | solution.py:657
  56.4 1.5 %collective-permute-start.12 = (bf16[1152,128]{1,0:T(8,128)(2,1)S(1)}, bf16[1152,128]{1,0:T(8,128)(2,1)S(1)}, u32[]{:S(2)}, u32[]{:S(2)}) collective-permute-start(bf16[1152,128]{1,0:T(8,128)(2,1)S(1)} %get-tuple-element.73.refs_0_), channel_id=1, source_target_pairs={{0,24},{4,28},{8,16},{12,20},{16,8},{20,12},{24,0},{28,4},{1,25},{... | collective-permute-start | bytes 884744 | tf_op jit(solution)/shard_map/ppermute | solution.py:657
  57.9 1.5 %collective-permute-start.21 = (bf16[1152,128]{1,0:T(8,128)(2,1)S(1)}, bf16[1152,128]{1,0:T(8,128)(2,1)S(1)}, u32[]{:S(2)}, u32[]{:S(2)}) collective-permute-start(bf16[1152,128]{1,0:T(8,128)(2,1)S(1)} %get-tuple-element.73.refs_0_), channel_id=1, source_target_pairs={{0,8},{4,12},{8,0},{12,4},{16,24},{20,28},{24,16},{28,20},{1,9},{5... | collective-permute-start | bytes 884744 | tf_op jit(solution)/shard_map/ppermute | solution.py:657
  59.9 0.9 collective-permute-done.16.refs_4_
  61.0 6.6 %out_merge.1.refs_5_ = bf16[192,448]{1,0:T(8,128)(2,1)S(1)} custom-call(bf16[1536,1408]{1,0:T(8,128)(2,1)S(1)} %get-tuple-element.63.inputs, bf16[1536,1408]{1,0:T(8,128)(2,1)S(1)} %get-tuple-element.48.weight, f32[1,1408]{1,0:T(1,128)S(1)} %get-tuple-element.74.gain, bf16[448,5632]{1,0:T(8,128)(2,1)S(1)} %get-tuple-element.75.merge_weight, ...), custom_call_target="tpu_custom_call" | custom-call | bytes 1024 | tf_op jit(solution)/shard_map/out_merge/pallas_call | solution.py:567
  68.6 2.2 %collective-permute-done.21.refs_0_ = bf16[1152,128]{1,0:T(8,128)(2,1)S(1)} collective-permute-done((bf16[1152,128]{1,0:T(8,128)(2,1)S(1)}, bf16[1152,128]{1,0:T(8,128)(2,1)S(1)}, u32[]{:S(2)}, u32[]{:S(2)}) %collective-permute-start.21) | collective-permute-done | bytes 294944 | tf_op jit(solution)/shard_map/ppermute | solution.py:657
  70.8 2.0 %out_near.1.partial = f32[11,768,128]{2,1,0:T(8,128)S(1)} custom-call(bf16[1536,1408]{1,0:T(8,128)(2,1)S(1)} %get-tuple-element.63.inputs, bf16[1536,1408]{1,0:T(8,128)(2,1)S(1)} %get-tuple-element.48.weight, bf16[1152,128]{1,0:T(8,128)(2,1)S(1)} %get-tuple-element.73.refs_0_, bf16[1152,128]{1,0:T(8,128)(2,1)S(1)} %collective-permute-done.11.refs_1_, ...), custom_call_target="tpu_custom_call" | custom-call | bytes 1024 | tf_op jit(solution)/shard_map/out_near/pallas_call | solution.py:567
  72.9 5.3 %out_far_merge.1 = (bf16[672,128]{1,0:T(8,128)(2,1)S(1)}, bf16[672,128]{1,0:T(8,128)(2,1)S(1)}, bf16[672,128]{1,0:T(8,128)(2,1)S(1)}, bf16[672,128]{1,0:T(8,128)(2,1)S(1)}) custom-call(f32[11,768,128]{2,1,0:T(8,128)S(1)} %out_near.1.partial, bf16[1536,1408]{1,0:T(8,128)(2,1)S(1)} %get-tuple-element.48.weight, f32[1,1408]{1,0:T(1,128)S(1)} %get-tuple-element.74.gain, ...), custom_call_target="tpu_custom_call" | custom-call | bytes 1024 | tf_op jit(solution)/shard_map/out_far_merge/pallas_call | solution.py:567
  78.2 2.4 %collective-permute-start.27 = (bf16[672,128]{1,0:T(8,128)(2,1)S(1)}, bf16[672,128]{1,0:T(8,128)(2,1)S(1)}, u32[]{:S(2)}, u32[]{:S(2)}) collective-permute-start(bf16[672,128]{1,0:T(8,128)(2,1)S(1)} %get-tuple-element.83), channel_id=1, source_target_pairs={{0,3},{1,2},{2,1},{3,0},{4,7},{5,6},{6,5},{7,4},{8,11},{9,10},{10,... | collective-permute-start | bytes 516104 | tf_op jit(solution)/shard_map/ppermute | solution.py:815
  80.6 0.8 collective-permute-start.26
  81.4 1.2 %collective-permute-start.25 = (bf16[672,128]{1,0:T(8,128)(2,1)S(1)}, bf16[672,128]{1,0:T(8,128)(2,1)S(1)}, u32[]{:S(2)}, u32[]{:S(2)}) collective-permute-start(bf16[672,128]{1,0:T(8,128)(2,1)S(1)} %get-tuple-element.81), channel_id=1, source_target_pairs={{0,2},{1,3},{2,0},{3,1},{4,6},{5,7},{6,4},{7,5},{8,10},{9,11},{10,... | collective-permute-start | bytes 516104 | tf_op jit(solution)/shard_map/ppermute | solution.py:815
  83.4 3.9 %collective-permute-done.27.block = bf16[672,128]{1,0:T(8,128)(2,1)S(1)} collective-permute-done((bf16[672,128]{1,0:T(8,128)(2,1)S(1)}, bf16[672,128]{1,0:T(8,128)(2,1)S(1)}, u32[]{:S(2)}, u32[]{:S(2)}) %collective-permute-start.27) | collective-permute-done | bytes 172064 | tf_op jit(solution)/shard_map/ppermute | solution.py:815
  88.1 3.7 %collective-permute-done.26.block = bf16[672,128]{1,0:T(8,128)(2,1)S(1)} collective-permute-done((bf16[672,128]{1,0:T(8,128)(2,1)S(1)}, bf16[672,128]{1,0:T(8,128)(2,1)S(1)}, u32[]{:S(2)}, u32[]{:S(2)}) %collective-permute-start.26) | collective-permute-done | bytes 172064 | tf_op jit(solution)/shard_map/ppermute | solution.py:815
  92.5 4.4 %collective-permute-done.25.block = bf16[672,128]{1,0:T(8,128)(2,1)S(1)} collective-permute-done((bf16[672,128]{1,0:T(8,128)(2,1)S(1)}, bf16[672,128]{1,0:T(8,128)(2,1)S(1)}, u32[]{:S(2)}, u32[]{:S(2)}) %collective-permute-start.25) | collective-permute-done | bytes 172064 | tf_op jit(solution)/shard_map/ppermute | solution.py:815
  (52 shorter events, 12.1 us)
Async XLA Ops:
  1.5 11.9 %collective-permute-start.2 = (bf16[192,1536]{1,0:T(8,128)(2,1)S(1)}, bf16[192,1536]{1,0:T(8,128)(2,1)S(1)}, u32[]{:S(2)}, u32[]{:S(2)}) collective-permute-start(bf16[192,1536]{1,0:T(8,128)(2,1)S(1)} %payload.1.refs_0_), channel_id=1, source_target_pairs={{0,4},{4,0},{8,12},{12,8},{16,20},{20,16},{24,28},{28,24},{1,5},{5... | collective-permute-start | bytes 1769480 | tf_op jit(solution)/shard_map/ppermute | solution.py:657
  2.0 16.5 %collective-permute-start = (bf16[192,1536]{1,0:T(8,128)(2,1)S(1)}, bf16[192,1536]{1,0:T(8,128)(2,1)S(1)}, u32[]{:S(2)}, u32[]{:S(2)}) collective-permute-start(bf16[192,1536]{1,0:T(8,128)(2,1)S(1)} %payload.1.refs_0_), channel_id=1, source_target_pairs={{0,8},{4,12},{8,0},{12,4},{16,24},{20,28},{24,16},{28,20},{1,9},{5... | collective-permute-start | bytes 1769480 | tf_op jit(solution)/shard_map/ppermute | solution.py:657
  4.6 15.4 %collective-permute-start.1 = (bf16[192,1536]{1,0:T(8,128)(2,1)S(1)}, bf16[192,1536]{1,0:T(8,128)(2,1)S(1)}, u32[]{:S(2)}, u32[]{:S(2)}) collective-permute-start(bf16[192,1536]{1,0:T(8,128)(2,1)S(1)} %payload.1.refs_0_), channel_id=1, source_target_pairs={{0,16},{4,20},{8,24},{12,28},{16,0},{20,4},{24,8},{28,12},{1,17},{... | collective-permute-start | bytes 1769480 | tf_op jit(solution)/shard_map/ppermute | solution.py:657
  6.2 0.7 copy-start.1
  6.8 0.7 copy-start.2
  8.2 5.1 %copy-start = (bf16[128,512]{1,0:T(8,128)(2,1)S(1)}, bf16[128,512]{1,0:T(8,128)(2,1)}, u32[]{:S(2)}) copy-start(bf16[128,512]{1,0:T(8,128)(2,1)} %constant.24.clone.refs_2_.refs_4_) | copy-start | bytes 393220
  20.0 2.7 %collective-permute-start.6 = (bf16[192,1536]{1,0:T(8,128)(2,1)S(1)}, bf16[192,1536]{1,0:T(8,128)(2,1)S(1)}, u32[]{:S(2)}, u32[]{:S(2)}) collective-permute-start(bf16[192,1536]{1,0:T(8,128)(2,1)S(1)} %collective-permute-done.across_x.refs_0_), channel_id=1, source_target_pairs={{0,4},{4,0},{8,12},{12,8},{16,20},{20,16},{24,28},{28,24},{1,5},{5... | collective-permute-start | bytes 1769480 | tf_op jit(solution)/shard_map/ppermute | solution.py:657
  20.0 4.7 %collective-permute-start.5 = (bf16[192,1536]{1,0:T(8,128)(2,1)S(1)}, bf16[192,1536]{1,0:T(8,128)(2,1)S(1)}, u32[]{:S(2)}, u32[]{:S(2)}) collective-permute-start(bf16[192,1536]{1,0:T(8,128)(2,1)S(1)} %collective-permute-done.1.across_y.refs_0_), channel_id=1, source_target_pairs={{0,4},{4,0},{8,12},{12,8},{16,20},{20,16},{24,28},{28,24},{1,5},{5... | collective-permute-start | bytes 1769480 | tf_op jit(solution)/shard_map/ppermute | solution.py:657
  20.5 9.0 %collective-permute-start.3 = (bf16[96,1536]{1,0:T(8,128)(2,1)S(1)}, bf16[96,1536]{1,0:T(8,128)(2,1)S(1)}, u32[]{:S(2)}, u32[]{:S(2)}) collective-permute-start(bf16[96,1536]{1,0:T(8,128)(2,1)S(1)} %get-tuple-element.51), channel_id=1, source_target_pairs={{0,16},{4,20},{8,24},{12,28},{16,0},{20,4},{24,8},{28,12},{1,17},{... | collective-permute-start | bytes 884744 | tf_op jit(solution)/shard_map/ppermute | solution.py:657
  22.1 8.6 %collective-permute-start.4 = (bf16[96,1536]{1,0:T(8,128)(2,1)S(1)}, bf16[96,1536]{1,0:T(8,128)(2,1)S(1)}, u32[]{:S(2)}, u32[]{:S(2)}) collective-permute-start(bf16[96,1536]{1,0:T(8,128)(2,1)S(1)} %get-tuple-element.52), channel_id=1, source_target_pairs={{0,8},{4,12},{8,0},{12,4},{16,24},{20,28},{24,16},{28,20},{1,9},{5... | collective-permute-start | bytes 884744 | tf_op jit(solution)/shard_map/ppermute | solution.py:657
  30.7 1.6 %collective-permute-start.7 = (bf16[96,1536]{1,0:T(8,128)(2,1)S(1)}, bf16[96,1536]{1,0:T(8,128)(2,1)S(1)}, u32[]{:S(2)}, u32[]{:S(2)}) collective-permute-start(bf16[96,1536]{1,0:T(8,128)(2,1)S(1)} %collective-permute-done.3.refs_0_), channel_id=1, source_target_pairs={{0,4},{4,0},{8,12},{12,8},{16,20},{20,16},{24,28},{28,24},{1,5},{5... | collective-permute-start | bytes 884744 | tf_op jit(solution)/shard_map/ppermute | solution.py:657
  30.7 2.0 %collective-permute-start.8 = (bf16[96,1536]{1,0:T(8,128)(2,1)S(1)}, bf16[96,1536]{1,0:T(8,128)(2,1)S(1)}, u32[]{:S(2)}, u32[]{:S(2)}) collective-permute-start(bf16[96,1536]{1,0:T(8,128)(2,1)S(1)} %collective-permute-done.4.refs_1_), channel_id=1, source_target_pairs={{0,4},{4,0},{8,12},{12,8},{16,20},{20,16},{24,28},{28,24},{1,5},{5... | collective-permute-start | bytes 884744 | tf_op jit(solution)/shard_map/ppermute | solution.py:657
  34.7 6.0 %copy-start.4 = (s32[1,4]{1,0:T(1,128)S(1)}, s32[1,4]{1,0:T(1,128)}, u32[]{:S(2)}) copy-start(s32[1,4]{1,0:T(1,128)} %refs_0_.3) | copy-start | bytes 52
  39.7 9.1 %collective-permute-start.10 = (bf16[1152,128]{1,0:T(8,128)(2,1)S(1)}, bf16[1152,128]{1,0:T(8,128)(2,1)S(1)}, u32[]{:S(2)}, u32[]{:S(2)}) collective-permute-start(bf16[1152,128]{1,0:T(8,128)(2,1)S(1)} %attention.2.refs_0_), channel_id=1, source_target_pairs={{0,16},{4,20},{8,24},{12,28},{16,0},{20,4},{24,8},{28,12},{1,17},{... | collective-permute-start | bytes 884744 | tf_op jit(solution)/shard_map/ppermute | solution.py:657
  40.3 8.8 %collective-permute-start.9 = (bf16[1152,128]{1,0:T(8,128)(2,1)S(1)}, bf16[1152,128]{1,0:T(8,128)(2,1)S(1)}, u32[]{:S(2)}, u32[]{:S(2)}) collective-permute-start(bf16[1152,128]{1,0:T(8,128)(2,1)S(1)} %attention.2.refs_0_), channel_id=1, source_target_pairs={{0,8},{4,12},{8,0},{12,4},{16,24},{20,28},{24,16},{28,20},{1,9},{5... | collective-permute-start | bytes 884744 | tf_op jit(solution)/shard_map/ppermute | solution.py:657
  40.7 11.0 %collective-permute-start.13 = (bf16[1152,128]{1,0:T(8,128)(2,1)S(1)}, bf16[1152,128]{1,0:T(8,128)(2,1)S(1)}, u32[]{:S(2)}, u32[]{:S(2)}) collective-permute-start(bf16[1152,128]{1,0:T(8,128)(2,1)S(1)} %attention.2.refs_0_), channel_id=1, source_target_pairs={{0,4},{4,0},{8,12},{12,8},{16,20},{20,16},{24,28},{28,24},{1,5},{5... | collective-permute-start | bytes 884744 | tf_op jit(solution)/shard_map/ppermute | solution.py:657
  49.1 10.3 %collective-permute-start.18 = (bf16[1152,128]{1,0:T(8,128)(2,1)S(1)}, bf16[1152,128]{1,0:T(8,128)(2,1)S(1)}, u32[]{:S(2)}, u32[]{:S(2)}) collective-permute-start(bf16[1152,128]{1,0:T(8,128)(2,1)S(1)} %collective-permute-done.9.across_x.refs_6_), channel_id=1, source_target_pairs={{0,4},{4,0},{8,12},{12,8},{16,20},{20,16},{24,28},{28,24},{1,5},{5... | collective-permute-start | bytes 884744 | tf_op jit(solution)/shard_map/ppermute | solution.py:657
  49.1 10.3 %collective-permute-start.19 = (bf16[1152,128]{1,0:T(8,128)(2,1)S(1)}, bf16[1152,128]{1,0:T(8,128)(2,1)S(1)}, u32[]{:S(2)}, u32[]{:S(2)}) collective-permute-start(bf16[1152,128]{1,0:T(8,128)(2,1)S(1)} %collective-permute-done.10.across_y.refs_8_), channel_id=1, source_target_pairs={{0,4},{4,0},{8,12},{12,8},{16,20},{20,16},{24,28},{28,24},{1,5},{5... | collective-permute-start | bytes 884744 | tf_op jit(solution)/shard_map/ppermute | solution.py:657
  49.6 6.8 %collective-permute-start.14 = (bf16[576,128]{1,0:T(8,128)(2,1)S(1)}, bf16[576,128]{1,0:T(8,128)(2,1)S(1)}, u32[]{:S(2)}, u32[]{:S(2)}) collective-permute-start(bf16[576,128]{1,0:T(8,128)(2,1)S(1)} %get-tuple-element.71), channel_id=1, source_target_pairs={{0,16},{4,20},{8,24},{12,28},{16,0},{20,4},{24,8},{28,12},{1,17},{... | collective-permute-start | bytes 442376 | tf_op jit(solution)/shard_map/ppermute | solution.py:657
  51.2 6.7 %collective-permute-start.15 = (bf16[576,128]{1,0:T(8,128)(2,1)S(1)}, bf16[576,128]{1,0:T(8,128)(2,1)S(1)}, u32[]{:S(2)}, u32[]{:S(2)}) collective-permute-start(bf16[576,128]{1,0:T(8,128)(2,1)S(1)} %get-tuple-element.72), channel_id=1, source_target_pairs={{0,8},{4,12},{8,0},{12,4},{16,24},{20,28},{24,16},{28,20},{1,9},{5... | collective-permute-start | bytes 442376 | tf_op jit(solution)/shard_map/ppermute | solution.py:657
  51.7 16.3 %collective-permute-start.23 = (bf16[1152,128]{1,0:T(8,128)(2,1)S(1)}, bf16[1152,128]{1,0:T(8,128)(2,1)S(1)}, u32[]{:S(2)}, u32[]{:S(2)}) collective-permute-start(bf16[1152,128]{1,0:T(8,128)(2,1)S(1)} %get-tuple-element.73.refs_0_), channel_id=1, source_target_pairs={{0,16},{4,20},{8,24},{12,28},{16,0},{20,4},{24,8},{28,12},{1,17},{... | collective-permute-start | bytes 884744 | tf_op jit(solution)/shard_map/ppermute | solution.py:657
  56.4 11.7 %collective-permute-start.12 = (bf16[1152,128]{1,0:T(8,128)(2,1)S(1)}, bf16[1152,128]{1,0:T(8,128)(2,1)S(1)}, u32[]{:S(2)}, u32[]{:S(2)}) collective-permute-start(bf16[1152,128]{1,0:T(8,128)(2,1)S(1)} %get-tuple-element.73.refs_0_), channel_id=1, source_target_pairs={{0,24},{4,28},{8,16},{12,20},{16,8},{20,12},{24,0},{28,4},{1,25},{... | collective-permute-start | bytes 884744 | tf_op jit(solution)/shard_map/ppermute | solution.py:657
  57.9 12.9 %collective-permute-start.21 = (bf16[1152,128]{1,0:T(8,128)(2,1)S(1)}, bf16[1152,128]{1,0:T(8,128)(2,1)S(1)}, u32[]{:S(2)}, u32[]{:S(2)}) collective-permute-start(bf16[1152,128]{1,0:T(8,128)(2,1)S(1)} %get-tuple-element.73.refs_0_), channel_id=1, source_target_pairs={{0,8},{4,12},{8,0},{12,4},{16,24},{20,28},{24,16},{28,20},{1,9},{5... | collective-permute-start | bytes 884744 | tf_op jit(solution)/shard_map/ppermute | solution.py:657
  59.4 1.4 %collective-permute-start.16 = (bf16[576,128]{1,0:T(8,128)(2,1)S(1)}, bf16[576,128]{1,0:T(8,128)(2,1)S(1)}, u32[]{:S(2)}, u32[]{:S(2)}) collective-permute-start(bf16[576,128]{1,0:T(8,128)(2,1)S(1)} %collective-permute-done.14.refs_2_), channel_id=1, source_target_pairs={{0,4},{4,0},{8,12},{12,8},{16,20},{20,16},{24,28},{28,24},{1,5},{5... | collective-permute-start | bytes 442376 | tf_op jit(solution)/shard_map/ppermute | solution.py:657
  59.4 1.6 %collective-permute-start.17 = (bf16[576,128]{1,0:T(8,128)(2,1)S(1)}, bf16[576,128]{1,0:T(8,128)(2,1)S(1)}, u32[]{:S(2)}, u32[]{:S(2)}) collective-permute-start(bf16[576,128]{1,0:T(8,128)(2,1)S(1)} %collective-permute-done.15.refs_3_), channel_id=1, source_target_pairs={{0,4},{4,0},{8,12},{12,8},{16,20},{20,16},{24,28},{28,24},{1,5},{5... | collective-permute-start | bytes 442376 | tf_op jit(solution)/shard_map/ppermute | solution.py:657
  60.7 10.1 %collective-permute-start.11 = (bf16[1152,128]{1,0:T(8,128)(2,1)S(1)}, bf16[1152,128]{1,0:T(8,128)(2,1)S(1)}, u32[]{:S(2)}, u32[]{:S(2)}) collective-permute-start(bf16[1152,128]{1,0:T(8,128)(2,1)S(1)} %get-tuple-element.73.refs_0_), channel_id=1, source_target_pairs={{0,4},{4,0},{8,12},{12,8},{16,20},{20,16},{24,28},{28,24},{1,5},{5... | collective-permute-start | bytes 884744 | tf_op jit(solution)/shard_map/ppermute | solution.py:657
  68.1 4.8 %collective-permute-start.24 = (bf16[1152,128]{1,0:T(8,128)(2,1)S(1)}, bf16[1152,128]{1,0:T(8,128)(2,1)S(1)}, u32[]{:S(2)}, u32[]{:S(2)}) collective-permute-start(bf16[1152,128]{1,0:T(8,128)(2,1)S(1)} %collective-permute-done.23.refs_2_), channel_id=1, source_target_pairs={{0,4},{4,0},{8,12},{12,8},{16,20},{20,16},{24,28},{28,24},{1,5},{5... | collective-permute-start | bytes 884744 | tf_op jit(solution)/shard_map/ppermute | solution.py:657
  68.1 2.7 %collective-permute-start.20 = (bf16[1152,128]{1,0:T(8,128)(2,1)S(1)}, bf16[1152,128]{1,0:T(8,128)(2,1)S(1)}, u32[]{:S(2)}, u32[]{:S(2)}) collective-permute-start(bf16[1152,128]{1,0:T(8,128)(2,1)S(1)} %collective-permute-done.12.refs_2_), channel_id=1, source_target_pairs={{0,4},{4,0},{8,12},{12,8},{16,20},{20,16},{24,28},{28,24},{1,5},{5... | collective-permute-start | bytes 884744 | tf_op jit(solution)/shard_map/ppermute | solution.py:657
  70.8 2.0 %collective-permute-start.22 = (bf16[1152,128]{1,0:T(8,128)(2,1)S(1)}, bf16[1152,128]{1,0:T(8,128)(2,1)S(1)}, u32[]{:S(2)}, u32[]{:S(2)}) collective-permute-start(bf16[1152,128]{1,0:T(8,128)(2,1)S(1)} %collective-permute-done.21.refs_0_), channel_id=1, source_target_pairs={{0,4},{4,0},{8,12},{12,8},{16,20},{20,16},{24,28},{28,24},{1,5},{5... | collective-permute-start | bytes 884744 | tf_op jit(solution)/shard_map/ppermute | solution.py:657
  78.2 9.1 %collective-permute-start.27 = (bf16[672,128]{1,0:T(8,128)(2,1)S(1)}, bf16[672,128]{1,0:T(8,128)(2,1)S(1)}, u32[]{:S(2)}, u32[]{:S(2)}) collective-permute-start(bf16[672,128]{1,0:T(8,128)(2,1)S(1)} %get-tuple-element.83), channel_id=1, source_target_pairs={{0,3},{1,2},{2,1},{3,0},{4,7},{5,6},{6,5},{7,4},{8,11},{9,10},{10,... | collective-permute-start | bytes 516104 | tf_op jit(solution)/shard_map/ppermute | solution.py:815
  80.6 11.2 %collective-permute-start.26 = (bf16[672,128]{1,0:T(8,128)(2,1)S(1)}, bf16[672,128]{1,0:T(8,128)(2,1)S(1)}, u32[]{:S(2)}, u32[]{:S(2)}) collective-permute-start(bf16[672,128]{1,0:T(8,128)(2,1)S(1)} %get-tuple-element.82), channel_id=1, source_target_pairs={{0,1},{1,0},{2,3},{3,2},{4,5},{5,4},{6,7},{7,6},{8,9},{9,8},{10,11... | collective-permute-start | bytes 516104 | tf_op jit(solution)/shard_map/ppermute | solution.py:815
  81.4 15.5 %collective-permute-start.25 = (bf16[672,128]{1,0:T(8,128)(2,1)S(1)}, bf16[672,128]{1,0:T(8,128)(2,1)S(1)}, u32[]{:S(2)}, u32[]{:S(2)}) collective-permute-start(bf16[672,128]{1,0:T(8,128)(2,1)S(1)} %get-tuple-element.81), channel_id=1, source_target_pairs={{0,2},{1,3},{2,0},{3,1},{4,6},{5,7},{6,4},{7,5},{8,10},{9,11},{10,... | collective-permute-start | bytes 516104 | tf_op jit(solution)/shard_map/ppermute | solution.py:815
  (1 other events, 0.7 us)

commit v18 on v15

--- a/solution.py
+++ b/solution.py
@@ -174,7 +174,7 @@
     return pltpu.with_memory_space_constraint(value, pltpu.HBM)
 
 
-def payload_kernel(segments, rows, columns, mask, embed, patches, out):
+def label_kernel(segments, rows, columns, mask, out):
     labels = [one[...].astype(jnp.float32) for one in (segments, rows, columns, mask)]
     labels.append(jnp.zeros((4, labels[0].shape[1]), jnp.float32))
     labels = jnp.concatenate(labels, axis=0).astype(jnp.bfloat16)
@@ -187,49 +187,62 @@
         (((0,), (0,)), ((), ())),
         preferred_element_type=jnp.float32,
     )
-    masked = turned[:, 3:4] > 0.5
-    tokens = jnp.where(
-        masked, embed[...].astype(jnp.float32)[None, :], patches[0].astype(jnp.float32)
-    )
-    out[:, :D] = tokens.astype(jnp.bfloat16)
-    out[:, D:] = turned.astype(jnp.bfloat16)
-
-
-def payload_call(segments, rows, columns, mask, embed, patches):
-    count = patches.shape[1]
-    operands = (segments, rows, columns, mask, embed, patches)
+    out[...] = turned.astype(jnp.bfloat16)
+
+
+def label_call(segments, rows, columns, mask):
+    operands = (segments, rows, columns, mask)
     fixed = lambda shape: pl.BlockSpec(shape, lambda i: (0,) * len(shape))
-    shape = (count, D + LANES)
+    shape = (segments.shape[1], LANES)
     return pl.pallas_call(
-        payload_kernel,
+        label_kernel,
         grid=(1,),
         in_specs=[fixed(one.shape) for one in operands],
         out_specs=fixed(shape),
         out_shape=jax.ShapeDtypeStruct(shape, jnp.bfloat16),
-        compiler_params=pltpu.CompilerParams(vmem_limit_bytes=8 << 20),
-        cost_estimate=pl.CostEstimate(
-            flops=count * D, bytes_accessed=4 * count * D, transcendentals=0
-        ),
-        name="payload",
+        compiler_params=pltpu.CompilerParams(vmem_limit_bytes=4 << 20),
+        cost_estimate=pl.CostEstimate(flops=0, bytes_accessed=1024, transcendentals=0),
+        name="labels",
     )(*map(in_hbm, operands))
+
+
+def join_kernel(flip, mine, other, out):
+    size = mine.shape[0]
+    up = (lax.axis_index("seq") // flip) % 2
+    out[pl.ds(pl.multiple_of(up * size, size), size), :] = mine[...]
+    out[pl.ds(pl.multiple_of((1 - up) * size, size), size), :] = other[...]
+
+
+def join_call(flip, mine, other):
+    vmem = pl.BlockSpec(memory_space=pltpu.VMEM)
+    shape = (2 * mine.shape[0], mine.shape[1])
+    return pl.pallas_call(
+        functools.partial(join_kernel, flip),
+        in_specs=[vmem] * 2,
+        out_specs=vmem,
+        out_shape=jax.ShapeDtypeStruct(shape, mine.dtype),
+        compiler_params=pltpu.CompilerParams(vmem_limit_bytes=4 << 20),
+        cost_estimate=pl.CostEstimate(flops=0, bytes_accessed=1024, transcendentals=0),
+        name="join",
+    )(mine, other)
 
 
 def qkv_kernel(count, flip, *refs):
     me = lax.axis_index("seq")
     first, second = refs[:count], refs[count : 2 * count]
-    table, gain, weight = refs[2 * count : 2 * count + 3]
-    inputs_out, qkv_out, label_out = refs[-3:]
+    all_labels, embed, table, gain, weight = refs[2 * count : 2 * count + 5]
+    inputs_out, qkv_out = refs[-2:]
     mine, other = stacked(first), stacked(second)
     leads = me % 2 == 0
     ahead = jnp.where(leads, mine, other)
     behind = jnp.where(leads, other, mine)
-    both = jnp.concatenate([ahead, behind], axis=0)
+    both = jnp.concatenate([ahead, behind], axis=0).astype(jnp.float32)
     rows = both.shape[0]
     at = pl.ds(pl.multiple_of((me // 2 ^ flip) * rows, rows), rows)
-    inputs_out[at, :] = both[:, :D]
-    label_out[at, :] = both[:, D:]
-    labels = both[:, D:].astype(jnp.float32)
-    normed = norm_rows(both[:, :D].astype(jnp.float32), gain[...]).astype(jnp.bfloat16)
+    labels = all_labels[at, :].astype(jnp.float32)
+    both = jnp.where(labels[:, 3:4] > 0.5, embed[...], both)
+    inputs_out[at, :] = both.astype(jnp.bfloat16)
+    normed = norm_rows(both, gain[...]).astype(jnp.bfloat16)
     columns = lax.dot_general(
         normed, weight[...], (((1,), (1,)), ((), ())), preferred_element_type=jnp.float32
     )
@@ -270,10 +283,10 @@
         qkv_out[at, number * LANES : (number + 1) * LANES] = part.astype(jnp.bfloat16)
 
 
-def qkv_call(flip, first, second, table, gain, weight, earlier, total):
+def qkv_call(flip, first, second, labels, embed, table, gain, weight, earlier, total):
     rows = 2 * sum(piece.shape[0] for piece in first)
-    widths = (D, 8 * LANES, LANES)
-    operands = [*first, *second, table, gain, in_vmem(weight)]
+    widths = (D, 8 * LANES)
+    operands = [*first, *second, labels, embed, table, gain, in_vmem(weight)]
     vmem = pl.BlockSpec(memory_space=pltpu.VMEM)
     held = [in_vmem(one) for one in earlier]
     return pl.pallas_call(
@@ -396,7 +409,7 @@
             transcendentals=rows * total,
         ),
         name="attention",
-    )(in_vmem(labels), in_vmem(block), *owners)
+    )(labels, in_vmem(block), *owners)
 
 
 def prepare_kernel(shards, ids, out_weight, merge_weight, qkv_weight, spread, *refs):
@@ -692,34 +705,37 @@
     total = local_rows * shards
     me = lax.axis_index("seq").astype(jnp.int32)
 
-    value = payload_call(segment_ids, patch_rows, patch_column, patch_mask, mask_embed, patches)
+    value = patches[0]
     own_swap, across_x, across_y = near_shards(value)
+    labels = label_call(segment_ids, patch_rows, patch_column, patch_mask)
+    for flip in (1, 2, 4):
+        labels = join_call(flip, labels, send_seq(labels, flip))
 
     order = weight_order(heads_here)
     spread = (order[:, None] == np.arange(qkv_weight.shape[1])[None, :]).astype(jnp.bfloat16)
     table = jnp.asarray(angle_table(heads_here))
     ids = jnp.stack([me ^ place for place in range(shards)])
-    gain, merge_gain_row, bias, ordered, merge_rows, weight = prepare_call(
+    gain, merge_gain_row, embed, bias, ordered, merge_rows, weight = prepare_call(
         shards,
         ids,
         out_weight,
         merge_weight.T,
         qkv_weight.T,
         jnp.asarray(spread),
-        (norm_gain, merge_gain, merge_bias),
+        (norm_gain, merge_gain, mask_embed, merge_bias),
     )
 
     project = lambda place, first, second, earlier: qkv_call(
-        place, first, second, table, gain, weight, earlier, total
+        place, first, second, labels, embed, table, gain, weight, earlier, total
     )
     buffers = project(0, [value], [own_swap], ())
-    across_x, across_y = after([across_x, across_y], buffers[2], ordered)
+    across_x, across_y = after([across_x, across_y], buffers[1], ordered)
     far = far_shards(across_x, across_y)
     buffers = project(1, [across_x], [send_seq(across_x, 1)], buffers)
     buffers = project(2, [across_y], [send_seq(across_y, 1)], buffers)
-    far = after(far, buffers[2])
+    far = after(far, buffers[1])
     buffers = project(3, far, [send_seq(one, 1) for one in far], buffers)
-    inputs, block, labels = buffers
+    inputs, block = buffers
 
     most = 2 * (total // 4) // images
     first_rows, last_rows = CHUNKS

time: 96.7 us -> 108 us (1.12)
  waiting for transfers between devices: 33 us -> 40.3 us
  starting transfers between devices: 21.5 us -> 25.6 us
    ppermute x25 -> x28, waiting for transfers between devices: 22.3 us -> 27.7 us  [send_seq(): return lax.ppermute(value, 'seq', [(i, i ^ flip) for i in range(size)])]
    ppermute x25 -> x28, starting transfers between devices: 15.9 us -> 21.1 us  [send_seq(): return lax.ppermute(value, 'seq', [(i, i ^ flip) for i in range(size)])]
    ppermute x3, waiting for transfers between devices: 10.6 us -> 12.6 us  [fast_local(): lax.ppermute(made[flip], 'pack', [(z, z ^ flip) for z in range(packs)])]
    unnamed x10 -> x14, local copies, waits for them, and re-layouts: 2.06 us -> 2.75 us
  transfers between devices with their start and end apart: 28 -> 31, of which waited for: 19 -> 18; matrix products, arithmetic and copies ran while one was open for 0% -> 0% of each run, Pallas kernels for 25% -> 23%
where the time goes in v18:
time: 108 us
  waiting for transfers between devices  40.3 us (37%)
  Pallas kernels  38.9 us (36%)
  starting transfers between devices  25.6 us (24%)
  local copies, waits for them, and re-layouts  2.84 us (3%)
    ppermute x28, waiting for transfers between devices, send_seq(): return lax.ppermute(value, 'seq', [(i, i ^ flip) for i in range(size)])  27.7 us
    ppermute x28, starting transfers between devices, send_seq(): return lax.ppermute(value, 'seq', [(i, i ^ flip) for i in range(size)])  21.1 us
    pallas_call x2, Pallas kernels, merge_call(): pl.pallas_call(functools.partial(merge_kernel, start, [len(source) for so...  13.3 us
    ppermute x3, waiting for transfers between devices, fast_local(): lax.ppermute(made[flip], 'pack', [(z, z ^ flip) for z in range(packs)])  12.6 us
    pallas_call x2, Pallas kernels, attention_call(): pl.pallas_call(functools.partial(attention_kernel, start, owners[0].shape...  8.19 us
    pallas_call x4, Pallas kernels, qkv_call(): pl.pallas_call(functools.partial(qkv_kernel, len(first), flip), in_specs=...  8.11 us
    pallas_call x1, Pallas kernels, prepare_call(): pl.pallas_call(functools.partial(prepare_kernel, shards), in_specs=[pl.Bl...  5.1 us
    ppermute x3, starting transfers between devices, fast_local(): lax.ppermute(made[flip], 'pack', [(z, z ^ flip) for z in range(packs)])  4.52 us
  transfers between devices with their start and end apart: 31, of which 18 were waited for; matrix products, arithmetic and copies ran while one was open for 0% of the time, Pallas kernels for 23%

profile of v18, /device:TPU:0, one launch (start us, length us, event | category | flops | bytes accessed | tf_op | source)
XLA Modules:
  0.0 108.0 jit_solution(11403002307103512355)
XLA Ops:
  0.5 0.9 labels.1.mine
  1.5 2.9 %collective-permute-start = (bf16[192,1408]{1,0:T(8,128)(2,1)}, bf16[192,1408]{1,0:T(8,128)(2,1)S(1)}, u32[]{:S(2)}, u32[]{:S(2)}) collective-permute-start(bf16[192,1408]{1,0:T(8,128)(2,1)} %bitcast.13), channel_id=1, source_target_pairs={{0,8},{4,12},{8,0},{12,4},{16,24},{20,28},{24,16},{28,20},{1,9},{5... | collective-permute-start | bytes 1622024 | tf_op jit(solution)/shard_map/ppermute | solution.py:614
  4.4 1.5 %collective-permute-start.1 = (bf16[192,1408]{1,0:T(8,128)(2,1)}, bf16[192,1408]{1,0:T(8,128)(2,1)S(1)}, u32[]{:S(2)}, u32[]{:S(2)}) collective-permute-start(bf16[192,1408]{1,0:T(8,128)(2,1)} %bitcast.14), channel_id=1, source_target_pairs={{0,16},{4,20},{8,24},{12,28},{16,0},{20,4},{24,8},{28,12},{1,17},{... | collective-permute-start | bytes 1622024 | tf_op jit(solution)/shard_map/ppermute | solution.py:614
  6.6 12.7 %collective-permute-done.4.other = bf16[384,128]{1,0:T(8,128)(2,1)S(1)} collective-permute-done((bf16[384,128]{1,0:T(8,128)(2,1)S(1)}, bf16[384,128]{1,0:T(8,128)(2,1)S(1)}, u32[]{:S(2)}, u32[]{:S(2)}) %collective-permute-start.4) | collective-permute-done | bytes 98336 | tf_op jit(solution)/shard_map/ppermute | solution.py:614
  19.3 1.8 %collective-permute-start.5 = (bf16[768,128]{1,0:T(8,128)(2,1)S(1)}, bf16[768,128]{1,0:T(8,128)(2,1)S(1)}, u32[]{:S(2)}, u32[]{:S(2)}) collective-permute-start(bf16[768,128]{1,0:T(8,128)(2,1)S(1)} %join.4.mine), channel_id=1, source_target_pairs={{0,16},{4,20},{8,24},{12,28},{16,0},{20,4},{24,8},{28,12},{1,17},{... | collective-permute-start | bytes 589832 | tf_op jit(solution)/shard_map/ppermute | solution.py:614
  24.0 5.1 %prepare.1 = (f32[1,1408]{1,0:T(1,128)S(1)}, f32[1,1408]{1,0:T(1,128)S(1)}, f32[1,1408]{1,0:T(1,128)S(1)}, f32[1,448]{1,0:T(1,128)S(1)}, bf16[1536,1408]{1,0:T(8...) custom-call(s32[8]{0:T(128)S(1)} %stack.35.ids, bf16[1408,1408]{1,0:T(8,128)(2,1)} %out_weight.1, ...), custom_call_target="tpu_custom_call" | custom-call | flops 1141899264 | bytes 20996096 | tf_op jit(solution)/shard_map/prepare/pallas_call | solution.py:450
  29.2 2.1 %norm_qkv.4 = (bf16[1536,1408]{1,0:T(8,128)(2,1)S(1)}, bf16[1536,1024]{1,0:T(8,128)(2,1)S(1)}) custom-call(bf16[192,1408]{1,0:T(8,128)(2,1)S(1)} %bitcast.15, bf16[192,1408]{1,0:T(8,128)(2,1)S(1)} %collective-permute-done.2.refs_1_, bf16[1536,128]{1,0:T(8,128)(2,1)S(1)} %join.5.refs_2_.refs_4_.labels, f32[1,1408]{1,0:T(1,128)S(1)} %get-tuple-element.42.refs_3_.refs_5_, ...), custom_call_target="tpu_custom_call" | custom-call | flops 2491416576 | bytes 6488064 | tf_op jit(solution)/shard_map/norm_qkv/pallas_call | solution.py:292
  32.2 1.7 %collective-permute-start.7 = (bf16[96,1408]{1,0:T(8,128)(2,1)S(1)}, bf16[96,1408]{1,0:T(8,128)(2,1)S(1)}, u32[]{:S(2)}, u32[]{:S(2)}) collective-permute-start(bf16[96,1408]{1,0:T(8,128)(2,1)S(1)} %get-tuple-element.50), channel_id=1, source_target_pairs={{0,8},{4,12},{8,0},{12,4},{16,24},{20,28},{24,16},{28,20},{1,9},{5... | collective-permute-start | bytes 811016 | tf_op jit(solution)/shard_map/ppermute | solution.py:614
  34.0 2.0 %norm_qkv.5 = (bf16[1536,1408]{1,0:T(8,128)(2,1)S(1)}, bf16[1536,1024]{1,0:T(8,128)(2,1)S(1)}) custom-call(bf16[192,1408]{1,0:T(8,128)(2,1)S(1)} %collective-permute-done.across_x.refs_0_, bf16[192,1408]{1,0:T(8,128)(2,1)S(1)} %collective-permute-done.9.refs_1_, ...), custom_call_target="tpu_custom_call", output_to_operand_aliasing={{0}: (7, {}), {1}: (8, {})} | custom-call | flops 2491416576 | bytes 6488064 | tf_op jit(solution)/shard_map/norm_qkv/pallas_call | solution.py:292
  36.0 2.0 %norm_qkv.6 = (bf16[1536,1408]{1,0:T(8,128)(2,1)S(1)}, bf16[1536,1024]{1,0:T(8,128)(2,1)S(1)}) custom-call(bf16[192,1408]{1,0:T(8,128)(2,1)S(1)} %collective-permute-done.1.across_y.refs_0_, bf16[192,1408]{1,0:T(8,128)(2,1)S(1)} %collective-permute-done.8.refs_1_, ...), custom_call_target="tpu_custom_call", output_to_operand_aliasing={{0}: (7, {}), {1}: (8, {})} | custom-call | flops 2491416576 | bytes 6488064 | tf_op jit(solution)/shard_map/norm_qkv/pallas_call | solution.py:292
  38.1 2.4 %collective-permute-done.6.refs_0_ = bf16[96,1408]{1,0:T(8,128)(2,1)S(1)} collective-permute-done((bf16[96,1408]{1,0:T(8,128)(2,1)S(1)}, bf16[96,1408]{1,0:T(8,128)(2,1)S(1)}, u32[]{:S(2)}, u32[]{:S(2)}) %collective-permute-start.6) | collective-permute-done | bytes 270368 | tf_op jit(solution)/shard_map/ppermute | solution.py:614
  41.0 1.0 collective-permute-done.10.refs_2_
  42.4 2.0 %norm_qkv.7 = (bf16[1536,1408]{1,0:T(8,128)(2,1)S(1)}, bf16[1536,1024]{1,0:T(8,128)(2,1)S(1)}) custom-call(bf16[96,1408]{1,0:T(8,128)(2,1)S(1)} %collective-permute-done.6.refs_0_, bf16[96,1408]{1,0:T(8,128)(2,1)S(1)} %collective-permute-done.7.refs_1_, ...), custom_call_target="tpu_custom_call", output_to_operand_aliasing={{0}: (9, {}), {1}: (10, {})} | custom-call | flops 2491416576 | bytes 6488064 | tf_op jit(solution)/shard_map/norm_qkv/pallas_call | solution.py:292
  44.5 3.9 %attention.2.refs_5_ = bf16[1152,128]{1,0:T(8,128)(2,1)S(1)} custom-call(bf16[1536,128]{1,0:T(8,128)(2,1)S(1)} %join.5.refs_2_.refs_4_.labels, bf16[1536,1024]{1,0:T(8,128)(2,1)S(1)} %get-tuple-element.64.block), custom_call_target="tpu_custom_call" | custom-call | flops 3019898880 | bytes 3145728 | tf_op jit(solution)/shard_map/attention/pallas_call | solution.py:396
  48.4 1.7 %collective-permute-start.12 = (bf16[1152,128]{1,0:T(8,128)(2,1)S(1)}, bf16[1152,128]{1,0:T(8,128)(2,1)S(1)}, u32[]{:S(2)}, u32[]{:S(2)}) collective-permute-start(bf16[1152,128]{1,0:T(8,128)(2,1)S(1)} %attention.2.refs_5_), channel_id=1, source_target_pairs={{0,8},{4,12},{8,0},{12,4},{16,24},{20,28},{24,16},{28,20},{1,9},{5... | collective-permute-start | bytes 884744 | tf_op jit(solution)/shard_map/ppermute | solution.py:614
  50.1 1.5 %collective-permute-start.13 = (bf16[1152,128]{1,0:T(8,128)(2,1)S(1)}, bf16[1152,128]{1,0:T(8,128)(2,1)S(1)}, u32[]{:S(2)}, u32[]{:S(2)}) collective-permute-start(bf16[1152,128]{1,0:T(8,128)(2,1)S(1)} %attention.2.refs_5_), channel_id=1, source_target_pairs={{0,16},{4,20},{8,24},{12,28},{16,0},{20,4},{24,8},{28,12},{1,17},{... | collective-permute-start | bytes 884744 | tf_op jit(solution)/shard_map/ppermute | solution.py:614
  51.6 4.3 %attention.3 = (bf16[1152,128]{1,0:T(8,128)(2,1)S(1)}, bf16[16,128]{1,0:T(8,128)(2,1)S(1)}) custom-call(bf16[1536,128]{1,0:T(8,128)(2,1)S(1)} %join.5.refs_2_.refs_4_.labels, bf16[1536,1024]{1,0:T(8,128)(2,1)S(1)} %get-tuple-element.64.block, s32[1,4]{1,0:T(1,128)S(1)} %copy-done.6), custom_call_target="tpu_custom_call" | custom-call | flops 3019898880 | bytes 3145728 | tf_op jit(solution)/shard_map/attention/pallas_call | solution.py:396
  55.9 1.6 %collective-permute-done.12.across_x.refs_7_ = bf16[1152,128]{1,0:T(8,128)(2,1)S(1)} collective-permute-done((bf16[1152,128]{1,0:T(8,128)(2,1)S(1)}, bf16[1152,128]{1,0:T(8,128)(2,1)S(1)}, u32[]{:S(2)}, u32[]{:S(2)}) %collective-permute-start.12) | collective-permute-done | bytes 294944 | tf_op jit(solution)/shard_map/ppermute | solution.py:614
  57.5 1.3 %collective-permute-done.13.across_y.refs_9_ = bf16[1152,128]{1,0:T(8,128)(2,1)S(1)} collective-permute-done((bf16[1152,128]{1,0:T(8,128)(2,1)S(1)}, bf16[1152,128]{1,0:T(8,128)(2,1)S(1)}, u32[]{:S(2)}, u32[]{:S(2)}) %collective-permute-start.13) | collective-permute-done | bytes 294944 | tf_op jit(solution)/shard_map/ppermute | solution.py:614
  59.4 1.6 %collective-permute-start.19 = (bf16[576,128]{1,0:T(8,128)(2,1)S(1)}, bf16[576,128]{1,0:T(8,128)(2,1)S(1)}, u32[]{:S(2)}, u32[]{:S(2)}) collective-permute-start(bf16[576,128]{1,0:T(8,128)(2,1)S(1)} %get-tuple-element.68), channel_id=1, source_target_pairs={{0,16},{4,20},{8,24},{12,28},{16,0},{20,4},{24,8},{28,12},{1,17},{... | collective-permute-start | bytes 442376 | tf_op jit(solution)/shard_map/ppermute | solution.py:614
  61.5 1.4 %collective-permute-start.26 = (bf16[1152,128]{1,0:T(8,128)(2,1)S(1)}, bf16[1152,128]{1,0:T(8,128)(2,1)S(1)}, u32[]{:S(2)}, u32[]{:S(2)}) collective-permute-start(bf16[1152,128]{1,0:T(8,128)(2,1)S(1)} %get-tuple-element.70.refs_5_), channel_id=1, source_target_pairs={{0,24},{4,28},{8,16},{12,20},{16,8},{20,12},{24,0},{28,4},{1,25},{... | collective-permute-start | bytes 884744 | tf_op jit(solution)/shard_map/ppermute | solution.py:614
  63.0 2.4 %collective-permute-done.19.refs_11_ = bf16[576,128]{1,0:T(8,128)(2,1)S(1)} collective-permute-done((bf16[576,128]{1,0:T(8,128)(2,1)S(1)}, bf16[576,128]{1,0:T(8,128)(2,1)S(1)}, u32[]{:S(2)}, u32[]{:S(2)}) %collective-permute-start.19) | collective-permute-done | bytes 147488 | tf_op jit(solution)/shard_map/ppermute | solution.py:614
  65.3 1.5 %collective-permute-start.24 = (bf16[1152,128]{1,0:T(8,128)(2,1)S(1)}, bf16[1152,128]{1,0:T(8,128)(2,1)S(1)}, u32[]{:S(2)}, u32[]{:S(2)}) collective-permute-start(bf16[1152,128]{1,0:T(8,128)(2,1)S(1)} %get-tuple-element.70.refs_5_), channel_id=1, source_target_pairs={{0,16},{4,20},{8,24},{12,28},{16,0},{20,4},{24,8},{28,12},{1,17},{... | collective-permute-start | bytes 884744 | tf_op jit(solution)/shard_map/ppermute | solution.py:614
  66.8 0.9 collective-permute-done.20.refs_12_
  69.8 6.4 %out_merge.2.refs_14_ = bf16[192,448]{1,0:T(8,128)(2,1)S(1)} custom-call(bf16[1536,1408]{1,0:T(8,128)(2,1)S(1)} %get-tuple-element.58.refs_0_, bf16[1536,1408]{1,0:T(8,128)(2,1)S(1)} %get-tuple-element.46.refs_1_, f32[1,1408]{1,0:T(1,128)S(1)} %get-tuple-element.59.refs_2_, bf16[448,5632]{1,0:T(8,128)(2,1)S(1)} %get-tuple-element.60.refs_3_, ...), custom_call_target="tpu_custom_call" | custom-call | bytes 1024 | tf_op jit(solution)/shard_map/out_merge/pallas_call | solution.py:557
  76.6 2.1 %collective-permute-done.24.refs_9_ = bf16[1152,128]{1,0:T(8,128)(2,1)S(1)} collective-permute-done((bf16[1152,128]{1,0:T(8,128)(2,1)S(1)}, bf16[1152,128]{1,0:T(8,128)(2,1)S(1)}, u32[]{:S(2)}, u32[]{:S(2)}) %collective-permute-start.24) | collective-permute-done | bytes 294944 | tf_op jit(solution)/shard_map/ppermute | solution.py:614
  79.2 1.1 collective-permute-done.25.refs_10_
  80.7 7.0 %out_merge.3 = (bf16[672,128]{1,0:T(8,128)(2,1)S(1)}, bf16[672,128]{1,0:T(8,128)(2,1)S(1)}, bf16[672,128]{1,0:T(8,128)(2,1)S(1)}, bf16[672,128]{1,0:T(8,128)(2,1)S(1)}) custom-call(bf16[1536,1408]{1,0:T(8,128)(2,1)S(1)} %get-tuple-element.58.refs_0_, bf16[1536,1408]{1,0:T(8,128)(2,1)S(1)} %get-tuple-element.46.refs_1_, ...), custom_call_target="tpu_custom_call" | custom-call | bytes 1024 | tf_op jit(solution)/shard_map/out_merge/pallas_call | solution.py:557
  87.7 3.7 %collective-permute-start.30 = (bf16[672,128]{1,0:T(8,128)(2,1)S(1)}, bf16[672,128]{1,0:T(8,128)(2,1)S(1)}, u32[]{:S(2)}, u32[]{:S(2)}) collective-permute-start(bf16[672,128]{1,0:T(8,128)(2,1)S(1)} %get-tuple-element.77), channel_id=1, source_target_pairs={{0,3},{1,2},{2,1},{3,0},{4,7},{5,6},{6,5},{7,4},{8,11},{9,10},{10,... | collective-permute-start | bytes 516104 | tf_op jit(solution)/shard_map/ppermute | solution.py:761
  93.0 3.8 %collective-permute-done.30.block = bf16[672,128]{1,0:T(8,128)(2,1)S(1)} collective-permute-done((bf16[672,128]{1,0:T(8,128)(2,1)S(1)}, bf16[672,128]{1,0:T(8,128)(2,1)S(1)}, u32[]{:S(2)}, u32[]{:S(2)}) %collective-permute-start.30) | collective-permute-done | bytes 172064 | tf_op jit(solution)/shard_map/ppermute | solution.py:761
  97.6 2.3 %collective-permute-done.29.block = bf16[672,128]{1,0:T(8,128)(2,1)S(1)} collective-permute-done((bf16[672,128]{1,0:T(8,128)(2,1)S(1)}, bf16[672,128]{1,0:T(8,128)(2,1)S(1)}, u32[]{:S(2)}, u32[]{:S(2)}) %collective-permute-start.29) | collective-permute-done | bytes 172064 | tf_op jit(solution)/shard_map/ppermute | solution.py:761
  100.6 6.5 %collective-permute-done.28.block = bf16[672,128]{1,0:T(8,128)(2,1)S(1)} collective-permute-done((bf16[672,128]{1,0:T(8,128)(2,1)S(1)}, bf16[672,128]{1,0:T(8,128)(2,1)S(1)}, u32[]{:S(2)}, u32[]{:S(2)}) %collective-permute-start.28) | collective-permute-done | bytes 172064 | tf_op jit(solution)/shard_map/ppermute | solution.py:761
  (64 shorter events, 14.5 us)
Async XLA Ops:
  0.0 29.2 %collective-permute-start.2 = (bf16[192,1408]{1,0:T(8,128)(2,1)}, bf16[192,1408]{1,0:T(8,128)(2,1)S(1)}, u32[]{:S(2)}, u32[]{:S(2)}) collective-permute-start(bf16[192,1408]{1,0:T(8,128)(2,1)} %bitcast.12), channel_id=1, source_target_pairs={{0,4},{4,0},{8,12},{12,8},{16,20},{20,16},{24,28},{28,24},{1,5},{5... | collective-permute-start | bytes 1622024 | tf_op jit(solution)/shard_map/ppermute | solution.py:614
  1.4 4.6 %collective-permute-start.3 = (bf16[192,128]{1,0:T(8,128)(2,1)S(1)}, bf16[192,128]{1,0:T(8,128)(2,1)S(1)}, u32[]{:S(2)}, u32[]{:S(2)}) collective-permute-start(bf16[192,128]{1,0:T(8,128)(2,1)S(1)} %labels.1.mine), channel_id=1, source_target_pairs={{0,4},{4,0},{8,12},{12,8},{16,20},{20,16},{24,28},{28,24},{1,5},{5... | collective-permute-start | bytes 147464 | tf_op jit(solution)/shard_map/ppermute | solution.py:614
  1.5 29.8 %collective-permute-start = (bf16[192,1408]{1,0:T(8,128)(2,1)}, bf16[192,1408]{1,0:T(8,128)(2,1)S(1)}, u32[]{:S(2)}, u32[]{:S(2)}) collective-permute-start(bf16[192,1408]{1,0:T(8,128)(2,1)} %bitcast.13), channel_id=1, source_target_pairs={{0,8},{4,12},{8,0},{12,4},{16,24},{20,28},{24,16},{28,20},{1,9},{5... | collective-permute-start | bytes 1622024 | tf_op jit(solution)/shard_map/ppermute | solution.py:614
  4.4 26.8 %collective-permute-start.1 = (bf16[192,1408]{1,0:T(8,128)(2,1)}, bf16[192,1408]{1,0:T(8,128)(2,1)S(1)}, u32[]{:S(2)}, u32[]{:S(2)}) collective-permute-start(bf16[192,1408]{1,0:T(8,128)(2,1)} %bitcast.14), channel_id=1, source_target_pairs={{0,16},{4,20},{8,24},{12,28},{16,0},{20,4},{24,8},{28,12},{1,17},{... | collective-permute-start | bytes 1622024 | tf_op jit(solution)/shard_map/ppermute | solution.py:614
  6.0 13.3 %collective-permute-start.4 = (bf16[384,128]{1,0:T(8,128)(2,1)S(1)}, bf16[384,128]{1,0:T(8,128)(2,1)S(1)}, u32[]{:S(2)}, u32[]{:S(2)}) collective-permute-start(bf16[384,128]{1,0:T(8,128)(2,1)S(1)} %join.3.mine), channel_id=1, source_target_pairs={{0,8},{4,12},{8,0},{12,4},{16,24},{20,28},{24,16},{28,20},{1,9},{5... | collective-permute-start | bytes 294920 | tf_op jit(solution)/shard_map/ppermute | solution.py:614
  19.3 9.8 %collective-permute-start.5 = (bf16[768,128]{1,0:T(8,128)(2,1)S(1)}, bf16[768,128]{1,0:T(8,128)(2,1)S(1)}, u32[]{:S(2)}, u32[]{:S(2)}) collective-permute-start(bf16[768,128]{1,0:T(8,128)(2,1)S(1)} %join.4.mine), channel_id=1, source_target_pairs={{0,16},{4,20},{8,24},{12,28},{16,0},{20,4},{24,8},{28,12},{1,17},{... | collective-permute-start | bytes 589832 | tf_op jit(solution)/shard_map/ppermute | solution.py:614
  31.3 2.7 %collective-permute-start.9 = (bf16[192,1408]{1,0:T(8,128)(2,1)S(1)}, bf16[192,1408]{1,0:T(8,128)(2,1)S(1)}, u32[]{:S(2)}, u32[]{:S(2)}) collective-permute-start(bf16[192,1408]{1,0:T(8,128)(2,1)S(1)} %collective-permute-done.across_x.refs_0_), channel_id=1, source_target_pairs={{0,4},{4,0},{8,12},{12,8},{16,20},{20,16},{24,28},{28,24},{1,5},{5... | collective-permute-start | bytes 1622024 | tf_op jit(solution)/shard_map/ppermute | solution.py:614
  31.4 4.6 %collective-permute-start.8 = (bf16[192,1408]{1,0:T(8,128)(2,1)S(1)}, bf16[192,1408]{1,0:T(8,128)(2,1)S(1)}, u32[]{:S(2)}, u32[]{:S(2)}) collective-permute-start(bf16[192,1408]{1,0:T(8,128)(2,1)S(1)} %collective-permute-done.1.across_y.refs_0_), channel_id=1, source_target_pairs={{0,4},{4,0},{8,12},{12,8},{16,20},{20,16},{24,28},{28,24},{1,5},{5... | collective-permute-start | bytes 1622024 | tf_op jit(solution)/shard_map/ppermute | solution.py:614
  31.9 8.5 %collective-permute-start.6 = (bf16[96,1408]{1,0:T(8,128)(2,1)S(1)}, bf16[96,1408]{1,0:T(8,128)(2,1)S(1)}, u32[]{:S(2)}, u32[]{:S(2)}) collective-permute-start(bf16[96,1408]{1,0:T(8,128)(2,1)S(1)} %get-tuple-element.49), channel_id=1, source_target_pairs={{0,16},{4,20},{8,24},{12,28},{16,0},{20,4},{24,8},{28,12},{1,17},{... | collective-permute-start | bytes 811016 | tf_op jit(solution)/shard_map/ppermute | solution.py:614
  32.2 8.3 %collective-permute-start.7 = (bf16[96,1408]{1,0:T(8,128)(2,1)S(1)}, bf16[96,1408]{1,0:T(8,128)(2,1)S(1)}, u32[]{:S(2)}, u32[]{:S(2)}) collective-permute-start(bf16[96,1408]{1,0:T(8,128)(2,1)S(1)} %get-tuple-element.50), channel_id=1, source_target_pairs={{0,8},{4,12},{8,0},{12,4},{16,24},{20,28},{24,16},{28,20},{1,9},{5... | collective-permute-start | bytes 811016 | tf_op jit(solution)/shard_map/ppermute | solution.py:614
  40.5 1.5 %collective-permute-start.10 = (bf16[96,1408]{1,0:T(8,128)(2,1)S(1)}, bf16[96,1408]{1,0:T(8,128)(2,1)S(1)}, u32[]{:S(2)}, u32[]{:S(2)}) collective-permute-start(bf16[96,1408]{1,0:T(8,128)(2,1)S(1)} %collective-permute-done.6.refs_0_), channel_id=1, source_target_pairs={{0,4},{4,0},{8,12},{12,8},{16,20},{20,16},{24,28},{28,24},{1,5},{5... | collective-permute-start | bytes 811016 | tf_op jit(solution)/shard_map/ppermute | solution.py:614
  40.5 1.9 %collective-permute-start.11 = (bf16[96,1408]{1,0:T(8,128)(2,1)S(1)}, bf16[96,1408]{1,0:T(8,128)(2,1)S(1)}, u32[]{:S(2)}, u32[]{:S(2)}) collective-permute-start(bf16[96,1408]{1,0:T(8,128)(2,1)S(1)} %collective-permute-done.7.refs_1_), channel_id=1, source_target_pairs={{0,4},{4,0},{8,12},{12,8},{16,20},{20,16},{24,28},{28,24},{1,5},{5... | collective-permute-start | bytes 811016 | tf_op jit(solution)/shard_map/ppermute | solution.py:614
  44.4 7.2 %copy-start.6 = (s32[1,4]{1,0:T(1,128)S(1)}, s32[1,4]{1,0:T(1,128)}, u32[]{:S(2)}) copy-start(s32[1,4]{1,0:T(1,128)} %refs_0_.3) | copy-start | bytes 52
  48.4 9.2 %collective-permute-start.12 = (bf16[1152,128]{1,0:T(8,128)(2,1)S(1)}, bf16[1152,128]{1,0:T(8,128)(2,1)S(1)}, u32[]{:S(2)}, u32[]{:S(2)}) collective-permute-start(bf16[1152,128]{1,0:T(8,128)(2,1)S(1)} %attention.2.refs_5_), channel_id=1, source_target_pairs={{0,8},{4,12},{8,0},{12,4},{16,24},{20,28},{24,16},{28,20},{1,9},{5... | collective-permute-start | bytes 884744 | tf_op jit(solution)/shard_map/ppermute | solution.py:614
  50.1 8.8 %collective-permute-start.13 = (bf16[1152,128]{1,0:T(8,128)(2,1)S(1)}, bf16[1152,128]{1,0:T(8,128)(2,1)S(1)}, u32[]{:S(2)}, u32[]{:S(2)}) collective-permute-start(bf16[1152,128]{1,0:T(8,128)(2,1)S(1)} %attention.2.refs_5_), channel_id=1, source_target_pairs={{0,16},{4,20},{8,24},{12,28},{16,0},{20,4},{24,8},{28,12},{1,17},{... | collective-permute-start | bytes 884744 | tf_op jit(solution)/shard_map/ppermute | solution.py:614
  51.6 9.9 %collective-permute-start.16 = (bf16[1152,128]{1,0:T(8,128)(2,1)S(1)}, bf16[1152,128]{1,0:T(8,128)(2,1)S(1)}, u32[]{:S(2)}, u32[]{:S(2)}) collective-permute-start(bf16[1152,128]{1,0:T(8,128)(2,1)S(1)} %attention.2.refs_5_), channel_id=1, source_target_pairs={{0,4},{4,0},{8,12},{12,8},{16,20},{20,16},{24,28},{28,24},{1,5},{5... | collective-permute-start | bytes 884744 | tf_op jit(solution)/shard_map/ppermute | solution.py:614
  58.9 9.4 %collective-permute-start.17 = (bf16[1152,128]{1,0:T(8,128)(2,1)S(1)}, bf16[1152,128]{1,0:T(8,128)(2,1)S(1)}, u32[]{:S(2)}, u32[]{:S(2)}) collective-permute-start(bf16[1152,128]{1,0:T(8,128)(2,1)S(1)} %collective-permute-done.12.across_x.refs_7_), channel_id=1, source_target_pairs={{0,4},{4,0},{8,12},{12,8},{16,20},{20,16},{24,28},{28,24},{1,5},{5... | collective-permute-start | bytes 884744 | tf_op jit(solution)/shard_map/ppermute | solution.py:614
  58.9 9.4 %collective-permute-start.18 = (bf16[1152,128]{1,0:T(8,128)(2,1)S(1)}, bf16[1152,128]{1,0:T(8,128)(2,1)S(1)}, u32[]{:S(2)}, u32[]{:S(2)}) collective-permute-start(bf16[1152,128]{1,0:T(8,128)(2,1)S(1)} %collective-permute-done.13.across_y.refs_9_), channel_id=1, source_target_pairs={{0,4},{4,0},{8,12},{12,8},{16,20},{20,16},{24,28},{28,24},{1,5},{5... | collective-permute-start | bytes 884744 | tf_op jit(solution)/shard_map/ppermute | solution.py:614
  59.4 5.9 %collective-permute-start.19 = (bf16[576,128]{1,0:T(8,128)(2,1)S(1)}, bf16[576,128]{1,0:T(8,128)(2,1)S(1)}, u32[]{:S(2)}, u32[]{:S(2)}) collective-permute-start(bf16[576,128]{1,0:T(8,128)(2,1)S(1)} %get-tuple-element.68), channel_id=1, source_target_pairs={{0,16},{4,20},{8,24},{12,28},{16,0},{20,4},{24,8},{28,12},{1,17},{... | collective-permute-start | bytes 442376 | tf_op jit(solution)/shard_map/ppermute | solution.py:614
  61.0 6.8 %collective-permute-start.20 = (bf16[576,128]{1,0:T(8,128)(2,1)S(1)}, bf16[576,128]{1,0:T(8,128)(2,1)S(1)}, u32[]{:S(2)}, u32[]{:S(2)}) collective-permute-start(bf16[576,128]{1,0:T(8,128)(2,1)S(1)} %get-tuple-element.69), channel_id=1, source_target_pairs={{0,8},{4,12},{8,0},{12,4},{16,24},{20,28},{24,16},{28,20},{1,9},{5... | collective-permute-start | bytes 442376 | tf_op jit(solution)/shard_map/ppermute | solution.py:614
  61.5 14.7 %collective-permute-start.26 = (bf16[1152,128]{1,0:T(8,128)(2,1)S(1)}, bf16[1152,128]{1,0:T(8,128)(2,1)S(1)}, u32[]{:S(2)}, u32[]{:S(2)}) collective-permute-start(bf16[1152,128]{1,0:T(8,128)(2,1)S(1)} %get-tuple-element.70.refs_5_), channel_id=1, source_target_pairs={{0,24},{4,28},{8,16},{12,20},{16,8},{20,12},{24,0},{28,4},{1,25},{... | collective-permute-start | bytes 884744 | tf_op jit(solution)/shard_map/ppermute | solution.py:614
  65.3 13.4 %collective-permute-start.24 = (bf16[1152,128]{1,0:T(8,128)(2,1)S(1)}, bf16[1152,128]{1,0:T(8,128)(2,1)S(1)}, u32[]{:S(2)}, u32[]{:S(2)}) collective-permute-start(bf16[1152,128]{1,0:T(8,128)(2,1)S(1)} %get-tuple-element.70.refs_5_), channel_id=1, source_target_pairs={{0,16},{4,20},{8,24},{12,28},{16,0},{20,4},{24,8},{28,12},{1,17},{... | collective-permute-start | bytes 884744 | tf_op jit(solution)/shard_map/ppermute | solution.py:614
  67.7 11.4 %collective-permute-start.15 = (bf16[1152,128]{1,0:T(8,128)(2,1)S(1)}, bf16[1152,128]{1,0:T(8,128)(2,1)S(1)}, u32[]{:S(2)}, u32[]{:S(2)}) collective-permute-start(bf16[1152,128]{1,0:T(8,128)(2,1)S(1)} %get-tuple-element.70.refs_5_), channel_id=1, source_target_pairs={{0,8},{4,12},{8,0},{12,4},{16,24},{20,28},{24,16},{28,20},{1,9},{5... | collective-permute-start | bytes 884744 | tf_op jit(solution)/shard_map/ppermute | solution.py:614
  68.3 1.4 %collective-permute-start.21 = (bf16[576,128]{1,0:T(8,128)(2,1)S(1)}, bf16[576,128]{1,0:T(8,128)(2,1)S(1)}, u32[]{:S(2)}, u32[]{:S(2)}) collective-permute-start(bf16[576,128]{1,0:T(8,128)(2,1)S(1)} %collective-permute-done.19.refs_11_), channel_id=1, source_target_pairs={{0,4},{4,0},{8,12},{12,8},{16,20},{20,16},{24,28},{28,24},{1,5},{5... | collective-permute-start | bytes 442376 | tf_op jit(solution)/shard_map/ppermute | solution.py:614
  68.3 1.6 %collective-permute-start.22 = (bf16[576,128]{1,0:T(8,128)(2,1)S(1)}, bf16[576,128]{1,0:T(8,128)(2,1)S(1)}, u32[]{:S(2)}, u32[]{:S(2)}) collective-permute-start(bf16[576,128]{1,0:T(8,128)(2,1)S(1)} %collective-permute-done.20.refs_12_), channel_id=1, source_target_pairs={{0,4},{4,0},{8,12},{12,8},{16,20},{20,16},{24,28},{28,24},{1,5},{5... | collective-permute-start | bytes 442376 | tf_op jit(solution)/shard_map/ppermute | solution.py:614
  69.6 9.6 %collective-permute-start.14 = (bf16[1152,128]{1,0:T(8,128)(2,1)S(1)}, bf16[1152,128]{1,0:T(8,128)(2,1)S(1)}, u32[]{:S(2)}, u32[]{:S(2)}) collective-permute-start(bf16[1152,128]{1,0:T(8,128)(2,1)S(1)} %get-tuple-element.70.refs_5_), channel_id=1, source_target_pairs={{0,4},{4,0},{8,12},{12,8},{16,20},{20,16},{24,28},{28,24},{1,5},{5... | collective-permute-start | bytes 884744 | tf_op jit(solution)/shard_map/ppermute | solution.py:614
  76.2 3.0 %collective-permute-start.27 = (bf16[1152,128]{1,0:T(8,128)(2,1)S(1)}, bf16[1152,128]{1,0:T(8,128)(2,1)S(1)}, u32[]{:S(2)}, u32[]{:S(2)}) collective-permute-start(bf16[1152,128]{1,0:T(8,128)(2,1)S(1)} %collective-permute-done.26.refs_11_), channel_id=1, source_target_pairs={{0,4},{4,0},{8,12},{12,8},{16,20},{20,16},{24,28},{28,24},{1,5},{5... | collective-permute-start | bytes 884744 | tf_op jit(solution)/shard_map/ppermute | solution.py:614
  78.7 1.6 %collective-permute-start.25 = (bf16[1152,128]{1,0:T(8,128)(2,1)S(1)}, bf16[1152,128]{1,0:T(8,128)(2,1)S(1)}, u32[]{:S(2)}, u32[]{:S(2)}) collective-permute-start(bf16[1152,128]{1,0:T(8,128)(2,1)S(1)} %collective-permute-done.24.refs_9_), channel_id=1, source_target_pairs={{0,4},{4,0},{8,12},{12,8},{16,20},{20,16},{24,28},{28,24},{1,5},{5... | collective-permute-start | bytes 884744 | tf_op jit(solution)/shard_map/ppermute | solution.py:614
  79.1 1.6 %collective-permute-start.23 = (bf16[1152,128]{1,0:T(8,128)(2,1)S(1)}, bf16[1152,128]{1,0:T(8,128)(2,1)S(1)}, u32[]{:S(2)}, u32[]{:S(2)}) collective-permute-start(bf16[1152,128]{1,0:T(8,128)(2,1)S(1)} %collective-permute-done.15.refs_7_), channel_id=1, source_target_pairs={{0,4},{4,0},{8,12},{12,8},{16,20},{20,16},{24,28},{28,24},{1,5},{5... | collective-permute-start | bytes 884744 | tf_op jit(solution)/shard_map/ppermute | solution.py:614
  87.7 9.1 %collective-permute-start.30 = (bf16[672,128]{1,0:T(8,128)(2,1)S(1)}, bf16[672,128]{1,0:T(8,128)(2,1)S(1)}, u32[]{:S(2)}, u32[]{:S(2)}) collective-permute-start(bf16[672,128]{1,0:T(8,128)(2,1)S(1)} %get-tuple-element.77), channel_id=1, source_target_pairs={{0,3},{1,2},{2,1},{3,0},{4,7},{5,6},{6,5},{7,4},{8,11},{9,10},{10,... | collective-permute-start | bytes 516104 | tf_op jit(solution)/shard_map/ppermute | solution.py:761
  91.3 8.5 %collective-permute-start.29 = (bf16[672,128]{1,0:T(8,128)(2,1)S(1)}, bf16[672,128]{1,0:T(8,128)(2,1)S(1)}, u32[]{:S(2)}, u32[]{:S(2)}) collective-permute-start(bf16[672,128]{1,0:T(8,128)(2,1)S(1)} %get-tuple-element.76), channel_id=1, source_target_pairs={{0,1},{1,0},{2,3},{3,2},{4,5},{5,4},{6,7},{7,6},{8,9},{9,8},{10,11... | collective-permute-start | bytes 516104 | tf_op jit(solution)/shard_map/ppermute | solution.py:761
  92.2 14.9 %collective-permute-start.28 = (bf16[672,128]{1,0:T(8,128)(2,1)S(1)}, bf16[672,128]{1,0:T(8,128)(2,1)S(1)}, u32[]{:S(2)}, u32[]{:S(2)}) collective-permute-start(bf16[672,128]{1,0:T(8,128)(2,1)S(1)} %get-tuple-element.75), channel_id=1, source_target_pairs={{0,2},{1,3},{2,0},{3,1},{4,6},{5,7},{6,4},{7,5},{8,10},{9,11},{10,... | collective-permute-start | bytes 516104 | tf_op jit(solution)/shard_map/ppermute | solution.py:761
  (6 other events, 13.1 us)

commit v19 on v15

--- a/solution.py
+++ b/solution.py
@@ -248,8 +248,7 @@
         b = columns[:, start + LANES : start + 2 * LANES]
         return a * cosine - b * sine, b * cosine + a * sine
 
-    factor = HD**-0.5 * float(np.log2(np.e))
-    query_a, query_b = (one * factor for one in turn(0))
+    query_a, query_b = turn(0)
     key_a, key_b = turn(2 * LANES)
     zero = jnp.zeros_like(key_a)
     image = numbers == labels[:, :1] + IMAGE_LANE
@@ -316,6 +315,7 @@
     begin = jnp.sum(jnp.where(one_row < lowest, 1, 0)) // BLOCK
     end = (jnp.sum(jnp.where(one_row <= largest, 1, 0)) + BLOCK - 1) // BLOCK
     queries = block[start : start + rows, : 2 * LANES]
+    factor = HD**-0.5 * float(np.log2(np.e))
     high[...] = jnp.full_like(high, 2 * FAR_APART)
 
     def score(step, carry):
@@ -337,7 +337,7 @@
         at = pl.ds(pl.multiple_of(step * BLOCK, BLOCK), BLOCK)
         sums = []
         for head in range(2):
-            weights = jnp.exp2(scores[head, step] - highest[head])
+            weights = jnp.exp2((scores[head, step] - highest[head]) * factor)
             values = block[at, (6 + head) * LANES : (7 + head) * LANES]
             sums.append(
                 carry[head]

time: 96.7 us -> 97.7 us (1.010)
  waiting for transfers between devices: 33 us -> 34.2 us
    ppermute x3, waiting for transfers between devices: 10.6 us -> 11.9 us  [fast_local(): lax.ppermute(made[flip], 'pack', [(z, z ^ flip) for z in range(packs)])]
where the time goes in v19:
time: 97.7 us; the launch traced here: 97.4 us
  Pallas kernels  39.2 us (40%)
  waiting for transfers between devices  34.2 us (35%)
  starting transfers between devices  21.5 us (22%)
  local copies, waits for them, and re-layouts  2.15 us (2%)
    ppermute x25, waiting for transfers between devices, send_seq(): return lax.ppermute(value, 'seq', [(i, i ^ flip) for i in range(size)])  22.3 us
    ppermute x25, starting transfers between devices, send_seq(): return lax.ppermute(value, 'seq', [(i, i ^ flip) for i in range(size)])  15.9 us
    pallas_call x2, Pallas kernels, merge_call(): pl.pallas_call(functools.partial(merge_kernel, start, [len(source) for so...  13.3 us
    ppermute x3, waiting for transfers between devices, fast_local(): lax.ppermute(made[flip], 'pack', [(z, z ^ flip) for z in range(packs)])  11.9 us
    pallas_call x2, Pallas kernels, attention_call(): pl.pallas_call(functools.partial(attention_kernel, start, owners[0].shape...  8.39 us
    pallas_call x4, Pallas kernels, qkv_call(): pl.pallas_call(functools.partial(qkv_kernel, len(first), flip), in_specs=...  7.8 us
    ppermute x3, starting transfers between devices, fast_local(): lax.ppermute(made[flip], 'pack', [(z, z ^ flip) for z in range(packs)])  5.64 us
    pallas_call x1, Pallas kernels, prepare_call(): pl.pallas_call(functools.partial(prepare_kernel, shards), in_specs=[pl.Bl...  5.1 us
  transfers between devices with their start and end apart: 28, of which 19 were waited for; matrix products, arithmetic and copies ran while one was open for 0% of the time, Pallas kernels for 25%

profile of v19, /device:TPU:0, one launch (start us, length us, event | category | flops | bytes accessed | tf_op | source)
XLA Modules:
  0.0 97.4 jit_solution(17005713373017506584)
XLA Ops:
  0.0 1.5 %payload.1.refs_0_ = bf16[192,1536]{1,0:T(8,128)(2,1)S(1)} custom-call(s32[1,192]{1,0:T(1,128)} %segments.1, s32[1,192]{1,0:T(1,128)} %rows.1, s32[1,192]{1,0:T(1,128)} %columns.1, s32[1,192]{1,0:T(1,128)} %mask.1, bf16[1408]{0:T(1024)(128)(2,1)} %embed.1, bf16[1,192,1408]{2,1,0:T(8,128)(2,1)} %patches.1), custom_call_target="tpu_custom_call" | custom-call | flops 270336 | bytes 1081344 | tf_op jit(solution)/shard_map/payload/pallas_call | solution.py:203
  2.0 2.6 %collective-permute-start = (bf16[192,1536]{1,0:T(8,128)(2,1)S(1)}, bf16[192,1536]{1,0:T(8,128)(2,1)S(1)}, u32[]{:S(2)}, u32[]{:S(2)}) collective-permute-start(bf16[192,1536]{1,0:T(8,128)(2,1)S(1)} %payload.1.refs_0_), channel_id=1, source_target_pairs={{0,8},{4,12},{8,0},{12,4},{16,24},{20,28},{24,16},{28,20},{1,9},{5... | collective-permute-start | bytes 1769480 | tf_op jit(solution)/shard_map/ppermute | solution.py:601
  4.6 1.5 %collective-permute-start.1 = (bf16[192,1536]{1,0:T(8,128)(2,1)S(1)}, bf16[192,1536]{1,0:T(8,128)(2,1)S(1)}, u32[]{:S(2)}, u32[]{:S(2)}) collective-permute-start(bf16[192,1536]{1,0:T(8,128)(2,1)S(1)} %payload.1.refs_0_), channel_id=1, source_target_pairs={{0,16},{4,20},{8,24},{12,28},{16,0},{20,4},{24,8},{28,12},{1,17},{... | collective-permute-start | bytes 1769480 | tf_op jit(solution)/shard_map/ppermute | solution.py:601
  8.2 5.1 %prepare.1 = (f32[1,1408]{1,0:T(1,128)S(1)}, f32[1,1408]{1,0:T(1,128)S(1)}, f32[1,448]{1,0:T(1,128)S(1)}, bf16[1536,1408]{1,0:T(8,128)(2,1)S(1)}, bf16[448,5632]...) custom-call(s32[8]{0:T(128)S(1)} %stack.35.ids, bf16[1408,1408]{1,0:T(8,128)(2,1)} %out_weight.1, ...), custom_call_target="tpu_custom_call" | custom-call | flops 1141899264 | bytes 20996096 | tf_op jit(solution)/shard_map/prepare/pallas_call | solution.py:437
  13.3 2.0 %norm_qkv.4 = (bf16[1536,1408]{1,0:T(8,128)(2,1)S(1)}, bf16[1536,1024]{1,0:T(8,128)(2,1)S(1)}, bf16[1536,128]{1,0:T(8,128)(2,1)S(1)}) custom-call(bf16[192,1536]{1,0:T(8,128)(2,1)S(1)} %payload.1.refs_0_, bf16[192,1536]{1,0:T(8,128)(2,1)S(1)} %collective-permute-done.2.refs_1_, bf16[128,512]{1,0:T(8,128)(2,1)S(1)} %copy-done, ...), custom_call_target="tpu_custom_call" | custom-call | flops 2491416576 | bytes 6488064 | tf_op jit(solution)/shard_map/norm_qkv/pallas_call | solution.py:278
  15.3 3.1 %collective-permute-done.across_x.refs_0_ = bf16[192,1536]{1,0:T(8,128)(2,1)S(1)} collective-permute-done((bf16[192,1536]{1,0:T(8,128)(2,1)S(1)}, bf16[192,1536]{1,0:T(8,128)(2,1)S(1)}, u32[]{:S(2)}, u32[]{:S(2)}) %collective-permute-start) | collective-permute-done | bytes 589856 | tf_op jit(solution)/shard_map/ppermute | solution.py:601
  18.5 1.5 %collective-permute-done.1.across_y.refs_0_ = bf16[192,1536]{1,0:T(8,128)(2,1)S(1)} collective-permute-done((bf16[192,1536]{1,0:T(8,128)(2,1)S(1)}, bf16[192,1536]{1,0:T(8,128)(2,1)S(1)}, u32[]{:S(2)}, u32[]{:S(2)}) %collective-permute-start.1) | collective-permute-done | bytes 589856 | tf_op jit(solution)/shard_map/ppermute | solution.py:601
  20.5 1.6 %collective-permute-start.3 = (bf16[96,1536]{1,0:T(8,128)(2,1)S(1)}, bf16[96,1536]{1,0:T(8,128)(2,1)S(1)}, u32[]{:S(2)}, u32[]{:S(2)}) collective-permute-start(bf16[96,1536]{1,0:T(8,128)(2,1)S(1)} %get-tuple-element.51), channel_id=1, source_target_pairs={{0,16},{4,20},{8,24},{12,28},{16,0},{20,4},{24,8},{28,12},{1,17},{... | collective-permute-start | bytes 884744 | tf_op jit(solution)/shard_map/ppermute | solution.py:601
  22.6 2.0 %norm_qkv.5 = (bf16[1536,1408]{1,0:T(8,128)(2,1)S(1)}, bf16[1536,1024]{1,0:T(8,128)(2,1)S(1)}, bf16[1536,128]{1,0:T(8,128)(2,1)S(1)}) custom-call(bf16[192,1536]{1,0:T(8,128)(2,1)S(1)} %collective-permute-done.across_x.refs_0_, bf16[192,1536]{1,0:T(8,128)(2,1)S(1)} %collective-permute-done.6.refs_1_, ...), custom_call_target="tpu_custom_call", output_to_operand_aliasing={{0}: (5, {}), {1}: (6, {}), {2}: (7, {})} | custom-call | flops 2491416576 | bytes 6488064 | tf_op jit(solution)/shard_map/norm_qkv/pallas_call | solution.py:278
  24.6 2.0 %norm_qkv.6 = (bf16[1536,1408]{1,0:T(8,128)(2,1)S(1)}, bf16[1536,1024]{1,0:T(8,128)(2,1)S(1)}, bf16[1536,128]{1,0:T(8,128)(2,1)S(1)}) custom-call(bf16[192,1536]{1,0:T(8,128)(2,1)S(1)} %collective-permute-done.1.across_y.refs_0_, bf16[192,1536]{1,0:T(8,128)(2,1)S(1)} %collective-permute-done.5.refs_1_, ...), custom_call_target="tpu_custom_call", output_to_operand_aliasing={{0}: (5, {}), {1}: (6, {}), {2}: (7, {})} | custom-call | flops 2491416576 | bytes 6488064 | tf_op jit(solution)/shard_map/norm_qkv/pallas_call | solution.py:278
  26.6 2.9 %collective-permute-done.3.refs_0_ = bf16[96,1536]{1,0:T(8,128)(2,1)S(1)} collective-permute-done((bf16[96,1536]{1,0:T(8,128)(2,1)S(1)}, bf16[96,1536]{1,0:T(8,128)(2,1)S(1)}, u32[]{:S(2)}, u32[]{:S(2)}) %collective-permute-start.3) | collective-permute-done | bytes 294944 | tf_op jit(solution)/shard_map/ppermute | solution.py:601
  29.5 1.2 %collective-permute-done.4.refs_1_ = bf16[96,1536]{1,0:T(8,128)(2,1)S(1)} collective-permute-done((bf16[96,1536]{1,0:T(8,128)(2,1)S(1)}, bf16[96,1536]{1,0:T(8,128)(2,1)S(1)}, u32[]{:S(2)}, u32[]{:S(2)}) %collective-permute-start.4) | collective-permute-done | bytes 294944 | tf_op jit(solution)/shard_map/ppermute | solution.py:601
  31.2 1.1 %collective-permute-done.7.refs_2_ = bf16[96,1536]{1,0:T(8,128)(2,1)S(1)} collective-permute-done((bf16[96,1536]{1,0:T(8,128)(2,1)S(1)}, bf16[96,1536]{1,0:T(8,128)(2,1)S(1)}, u32[]{:S(2)}, u32[]{:S(2)}) %collective-permute-start.7) | collective-permute-done | bytes 294944 | tf_op jit(solution)/shard_map/ppermute | solution.py:601
  32.7 1.9 %norm_qkv.7 = (bf16[1536,1408]{1,0:T(8,128)(2,1)S(1)}, bf16[1536,1024]{1,0:T(8,128)(2,1)S(1)}, bf16[1536,128]{1,0:T(8,128)(2,1)S(1)}) custom-call(bf16[96,1536]{1,0:T(8,128)(2,1)S(1)} %collective-permute-done.3.refs_0_, bf16[96,1536]{1,0:T(8,128)(2,1)S(1)} %collective-permute-done.4.refs_1_, ...), custom_call_target="tpu_custom_call", output_to_operand_aliasing={{0}: (7, {}), {1}: (8, {}), {2}: (9, {})} | custom-call | flops 2491416576 | bytes 6488064 | tf_op jit(solution)/shard_map/norm_qkv/pallas_call | solution.py:278
  34.7 3.8 %attention.2.refs_5_ = bf16[1152,128]{1,0:T(8,128)(2,1)S(1)} custom-call(bf16[1536,128]{1,0:T(8,128)(2,1)S(1)} %get-tuple-element.69.labels, bf16[1536,1024]{1,0:T(8,128)(2,1)S(1)} %get-tuple-element.70.block), custom_call_target="tpu_custom_call" | custom-call | flops 3019898880 | bytes 3145728 | tf_op jit(solution)/shard_map/attention/pallas_call | solution.py:383
  39.5 4.6 %attention.3 = (bf16[1152,128]{1,0:T(8,128)(2,1)S(1)}, bf16[16,128]{1,0:T(8,128)(2,1)S(1)}) custom-call(bf16[1536,128]{1,0:T(8,128)(2,1)S(1)} %get-tuple-element.69.labels, bf16[1536,1024]{1,0:T(8,128)(2,1)S(1)} %get-tuple-element.70.block, s32[1,4]{1,0:T(1,128)S(1)} %copy-done.4), custom_call_target="tpu_custom_call" | custom-call | flops 3019898880 | bytes 3145728 | tf_op jit(solution)/shard_map/attention/pallas_call | solution.py:383
  44.0 3.6 %collective-permute-done.10.across_y.refs_9_ = bf16[1152,128]{1,0:T(8,128)(2,1)S(1)} collective-permute-done((bf16[1152,128]{1,0:T(8,128)(2,1)S(1)}, bf16[1152,128]{1,0:T(8,128)(2,1)S(1)}, u32[]{:S(2)}, u32[]{:S(2)}) %collective-permute-start.10) | collective-permute-done | bytes 294944 | tf_op jit(solution)/shard_map/ppermute | solution.py:601
  48.4 1.6 %collective-permute-start.16 = (bf16[576,128]{1,0:T(8,128)(2,1)S(1)}, bf16[576,128]{1,0:T(8,128)(2,1)S(1)}, u32[]{:S(2)}, u32[]{:S(2)}) collective-permute-start(bf16[576,128]{1,0:T(8,128)(2,1)S(1)} %get-tuple-element.74), channel_id=1, source_target_pairs={{0,16},{4,20},{8,24},{12,28},{16,0},{20,4},{24,8},{28,12},{1,17},{... | collective-permute-start | bytes 442376 | tf_op jit(solution)/shard_map/ppermute | solution.py:601
  50.5 1.4 %collective-permute-start.23 = (bf16[1152,128]{1,0:T(8,128)(2,1)S(1)}, bf16[1152,128]{1,0:T(8,128)(2,1)S(1)}, u32[]{:S(2)}, u32[]{:S(2)}) collective-permute-start(bf16[1152,128]{1,0:T(8,128)(2,1)S(1)} %get-tuple-element.76.refs_5_), channel_id=1, source_target_pairs={{0,24},{4,28},{8,16},{12,20},{16,8},{20,12},{24,0},{28,4},{1,25},{... | collective-permute-start | bytes 884744 | tf_op jit(solution)/shard_map/ppermute | solution.py:601
  51.9 2.4 %collective-permute-done.16.refs_11_ = bf16[576,128]{1,0:T(8,128)(2,1)S(1)} collective-permute-done((bf16[576,128]{1,0:T(8,128)(2,1)S(1)}, bf16[576,128]{1,0:T(8,128)(2,1)S(1)}, u32[]{:S(2)}, u32[]{:S(2)}) %collective-permute-start.16) | collective-permute-done | bytes 147488 | tf_op jit(solution)/shard_map/ppermute | solution.py:601
  54.3 1.5 %collective-permute-start.21 = (bf16[1152,128]{1,0:T(8,128)(2,1)S(1)}, bf16[1152,128]{1,0:T(8,128)(2,1)S(1)}, u32[]{:S(2)}, u32[]{:S(2)}) collective-permute-start(bf16[1152,128]{1,0:T(8,128)(2,1)S(1)} %get-tuple-element.76.refs_5_), channel_id=1, source_target_pairs={{0,16},{4,20},{8,24},{12,28},{16,0},{20,4},{24,8},{28,12},{1,17},{... | collective-permute-start | bytes 884744 | tf_op jit(solution)/shard_map/ppermute | solution.py:601
  55.8 0.9 collective-permute-done.17.refs_12_
  57.8 0.9 collective-permute-done.18.refs_13_
  58.8 6.4 %out_merge.2.refs_14_ = bf16[192,448]{1,0:T(8,128)(2,1)S(1)} custom-call(bf16[1536,1408]{1,0:T(8,128)(2,1)S(1)} %get-tuple-element.63.refs_0_, bf16[1536,1408]{1,0:T(8,128)(2,1)S(1)} %get-tuple-element.48.refs_1_, f32[1,1408]{1,0:T(1,128)S(1)} %get-tuple-element.64.refs_2_, bf16[448,5632]{1,0:T(8,128)(2,1)S(1)} %get-tuple-element.65.refs_3_, ...), custom_call_target="tpu_custom_call" | custom-call | bytes 1024 | tf_op jit(solution)/shard_map/out_merge/pallas_call | solution.py:544
  65.6 2.0 %collective-permute-done.21.refs_9_ = bf16[1152,128]{1,0:T(8,128)(2,1)S(1)} collective-permute-done((bf16[1152,128]{1,0:T(8,128)(2,1)S(1)}, bf16[1152,128]{1,0:T(8,128)(2,1)S(1)}, u32[]{:S(2)}, u32[]{:S(2)}) %collective-permute-start.21) | collective-permute-done | bytes 294944 | tf_op jit(solution)/shard_map/ppermute | solution.py:601
  68.2 1.1 %collective-permute-done.22.refs_10_ = bf16[1152,128]{1,0:T(8,128)(2,1)S(1)} collective-permute-done((bf16[1152,128]{1,0:T(8,128)(2,1)S(1)}, bf16[1152,128]{1,0:T(8,128)(2,1)S(1)}, u32[]{:S(2)}, u32[]{:S(2)}) %collective-permute-start.22) | collective-permute-done | bytes 294944 | tf_op jit(solution)/shard_map/ppermute | solution.py:601
  69.7 6.9 %out_merge.3 = (bf16[672,128]{1,0:T(8,128)(2,1)S(1)}, bf16[672,128]{1,0:T(8,128)(2,1)S(1)}, bf16[672,128]{1,0:T(8,128)(2,1)S(1)}, bf16[672,128]{1,0:T(8,128)(2,1)S(1)}) custom-call(bf16[1536,1408]{1,0:T(8,128)(2,1)S(1)} %get-tuple-element.63.refs_0_, bf16[1536,1408]{1,0:T(8,128)(2,1)S(1)} %get-tuple-element.48.refs_1_, ...), custom_call_target="tpu_custom_call" | custom-call | bytes 1024 | tf_op jit(solution)/shard_map/out_merge/pallas_call | solution.py:544
  76.6 5.0 %collective-permute-start.27 = (bf16[672,128]{1,0:T(8,128)(2,1)S(1)}, bf16[672,128]{1,0:T(8,128)(2,1)S(1)}, u32[]{:S(2)}, u32[]{:S(2)}) collective-permute-start(bf16[672,128]{1,0:T(8,128)(2,1)S(1)} %get-tuple-element.83), channel_id=1, source_target_pairs={{0,3},{1,2},{2,1},{3,0},{4,7},{5,6},{6,5},{7,4},{8,11},{9,10},{10,... | collective-permute-start | bytes 516104 | tf_op jit(solution)/shard_map/ppermute | solution.py:745
  83.0 3.8 %collective-permute-done.27.block = bf16[672,128]{1,0:T(8,128)(2,1)S(1)} collective-permute-done((bf16[672,128]{1,0:T(8,128)(2,1)S(1)}, bf16[672,128]{1,0:T(8,128)(2,1)S(1)}, u32[]{:S(2)}, u32[]{:S(2)}) %collective-permute-start.27) | collective-permute-done | bytes 172064 | tf_op jit(solution)/shard_map/ppermute | solution.py:745
  86.8 0.8 place_rows.5.refs_0_
  87.6 3.5 %collective-permute-done.26.block = bf16[672,128]{1,0:T(8,128)(2,1)S(1)} collective-permute-done((bf16[672,128]{1,0:T(8,128)(2,1)S(1)}, bf16[672,128]{1,0:T(8,128)(2,1)S(1)}, u32[]{:S(2)}, u32[]{:S(2)}) %collective-permute-start.26) | collective-permute-done | bytes 172064 | tf_op jit(solution)/shard_map/ppermute | solution.py:745
  91.9 4.6 %collective-permute-done.25.block = bf16[672,128]{1,0:T(8,128)(2,1)S(1)} collective-permute-done((bf16[672,128]{1,0:T(8,128)(2,1)S(1)}, bf16[672,128]{1,0:T(8,128)(2,1)S(1)}, u32[]{:S(2)}, u32[]{:S(2)}) %collective-permute-start.25) | collective-permute-done | bytes 172064 | tf_op jit(solution)/shard_map/ppermute | solution.py:745
  (51 shorter events, 12.5 us)
Async XLA Ops:
  1.5 11.9 %collective-permute-start.2 = (bf16[192,1536]{1,0:T(8,128)(2,1)S(1)}, bf16[192,1536]{1,0:T(8,128)(2,1)S(1)}, u32[]{:S(2)}, u32[]{:S(2)}) collective-permute-start(bf16[192,1536]{1,0:T(8,128)(2,1)S(1)} %payload.1.refs_0_), channel_id=1, source_target_pairs={{0,4},{4,0},{8,12},{12,8},{16,20},{20,16},{24,28},{28,24},{1,5},{5... | collective-permute-start | bytes 1769480 | tf_op jit(solution)/shard_map/ppermute | solution.py:601
  2.0 16.5 %collective-permute-start = (bf16[192,1536]{1,0:T(8,128)(2,1)S(1)}, bf16[192,1536]{1,0:T(8,128)(2,1)S(1)}, u32[]{:S(2)}, u32[]{:S(2)}) collective-permute-start(bf16[192,1536]{1,0:T(8,128)(2,1)S(1)} %payload.1.refs_0_), channel_id=1, source_target_pairs={{0,8},{4,12},{8,0},{12,4},{16,24},{20,28},{24,16},{28,20},{1,9},{5... | collective-permute-start | bytes 1769480 | tf_op jit(solution)/shard_map/ppermute | solution.py:601
  4.6 15.4 %collective-permute-start.1 = (bf16[192,1536]{1,0:T(8,128)(2,1)S(1)}, bf16[192,1536]{1,0:T(8,128)(2,1)S(1)}, u32[]{:S(2)}, u32[]{:S(2)}) collective-permute-start(bf16[192,1536]{1,0:T(8,128)(2,1)S(1)} %payload.1.refs_0_), channel_id=1, source_target_pairs={{0,16},{4,20},{8,24},{12,28},{16,0},{20,4},{24,8},{28,12},{1,17},{... | collective-permute-start | bytes 1769480 | tf_op jit(solution)/shard_map/ppermute | solution.py:601
  6.2 0.7 copy-start.1
  6.8 0.7 copy-start.2
  8.2 5.1 %copy-start = (bf16[128,512]{1,0:T(8,128)(2,1)S(1)}, bf16[128,512]{1,0:T(8,128)(2,1)}, u32[]{:S(2)}) copy-start(bf16[128,512]{1,0:T(8,128)(2,1)} %constant.24.clone.refs_2_.refs_4_) | copy-start | bytes 393220
  20.0 2.7 %collective-permute-start.6 = (bf16[192,1536]{1,0:T(8,128)(2,1)S(1)}, bf16[192,1536]{1,0:T(8,128)(2,1)S(1)}, u32[]{:S(2)}, u32[]{:S(2)}) collective-permute-start(bf16[192,1536]{1,0:T(8,128)(2,1)S(1)} %collective-permute-done.across_x.refs_0_), channel_id=1, source_target_pairs={{0,4},{4,0},{8,12},{12,8},{16,20},{20,16},{24,28},{28,24},{1,5},{5... | collective-permute-start | bytes 1769480 | tf_op jit(solution)/shard_map/ppermute | solution.py:601
  20.0 4.6 %collective-permute-start.5 = (bf16[192,1536]{1,0:T(8,128)(2,1)S(1)}, bf16[192,1536]{1,0:T(8,128)(2,1)S(1)}, u32[]{:S(2)}, u32[]{:S(2)}) collective-permute-start(bf16[192,1536]{1,0:T(8,128)(2,1)S(1)} %collective-permute-done.1.across_y.refs_0_), channel_id=1, source_target_pairs={{0,4},{4,0},{8,12},{12,8},{16,20},{20,16},{24,28},{28,24},{1,5},{5... | collective-permute-start | bytes 1769480 | tf_op jit(solution)/shard_map/ppermute | solution.py:601
  20.5 9.0 %collective-permute-start.3 = (bf16[96,1536]{1,0:T(8,128)(2,1)S(1)}, bf16[96,1536]{1,0:T(8,128)(2,1)S(1)}, u32[]{:S(2)}, u32[]{:S(2)}) collective-permute-start(bf16[96,1536]{1,0:T(8,128)(2,1)S(1)} %get-tuple-element.51), channel_id=1, source_target_pairs={{0,16},{4,20},{8,24},{12,28},{16,0},{20,4},{24,8},{28,12},{1,17},{... | collective-permute-start | bytes 884744 | tf_op jit(solution)/shard_map/ppermute | solution.py:601
  22.1 8.6 %collective-permute-start.4 = (bf16[96,1536]{1,0:T(8,128)(2,1)S(1)}, bf16[96,1536]{1,0:T(8,128)(2,1)S(1)}, u32[]{:S(2)}, u32[]{:S(2)}) collective-permute-start(bf16[96,1536]{1,0:T(8,128)(2,1)S(1)} %get-tuple-element.52), channel_id=1, source_target_pairs={{0,8},{4,12},{8,0},{12,4},{16,24},{20,28},{24,16},{28,20},{1,9},{5... | collective-permute-start | bytes 884744 | tf_op jit(solution)/shard_map/ppermute | solution.py:601
  30.7 1.6 %collective-permute-start.7 = (bf16[96,1536]{1,0:T(8,128)(2,1)S(1)}, bf16[96,1536]{1,0:T(8,128)(2,1)S(1)}, u32[]{:S(2)}, u32[]{:S(2)}) collective-permute-start(bf16[96,1536]{1,0:T(8,128)(2,1)S(1)} %collective-permute-done.3.refs_0_), channel_id=1, source_target_pairs={{0,4},{4,0},{8,12},{12,8},{16,20},{20,16},{24,28},{28,24},{1,5},{5... | collective-permute-start | bytes 884744 | tf_op jit(solution)/shard_map/ppermute | solution.py:601
  30.7 2.0 %collective-permute-start.8 = (bf16[96,1536]{1,0:T(8,128)(2,1)S(1)}, bf16[96,1536]{1,0:T(8,128)(2,1)S(1)}, u32[]{:S(2)}, u32[]{:S(2)}) collective-permute-start(bf16[96,1536]{1,0:T(8,128)(2,1)S(1)} %collective-permute-done.4.refs_1_), channel_id=1, source_target_pairs={{0,4},{4,0},{8,12},{12,8},{16,20},{20,16},{24,28},{28,24},{1,5},{5... | collective-permute-start | bytes 884744 | tf_op jit(solution)/shard_map/ppermute | solution.py:601
  34.7 4.8 %copy-start.4 = (s32[1,4]{1,0:T(1,128)S(1)}, s32[1,4]{1,0:T(1,128)}, u32[]{:S(2)}) copy-start(s32[1,4]{1,0:T(1,128)} %refs_0_.3) | copy-start | bytes 52
  38.5 9.1 %collective-permute-start.10 = (bf16[1152,128]{1,0:T(8,128)(2,1)S(1)}, bf16[1152,128]{1,0:T(8,128)(2,1)S(1)}, u32[]{:S(2)}, u32[]{:S(2)}) collective-permute-start(bf16[1152,128]{1,0:T(8,128)(2,1)S(1)} %attention.2.refs_5_), channel_id=1, source_target_pairs={{0,16},{4,20},{8,24},{12,28},{16,0},{20,4},{24,8},{28,12},{1,17},{... | collective-permute-start | bytes 884744 | tf_op jit(solution)/shard_map/ppermute | solution.py:601
  39.1 8.8 %collective-permute-start.9 = (bf16[1152,128]{1,0:T(8,128)(2,1)S(1)}, bf16[1152,128]{1,0:T(8,128)(2,1)S(1)}, u32[]{:S(2)}, u32[]{:S(2)}) collective-permute-start(bf16[1152,128]{1,0:T(8,128)(2,1)S(1)} %attention.2.refs_5_), channel_id=1, source_target_pairs={{0,8},{4,12},{8,0},{12,4},{16,24},{20,28},{24,16},{28,20},{1,9},{5... | collective-permute-start | bytes 884744 | tf_op jit(solution)/shard_map/ppermute | solution.py:601
  39.4 11.0 %collective-permute-start.13 = (bf16[1152,128]{1,0:T(8,128)(2,1)S(1)}, bf16[1152,128]{1,0:T(8,128)(2,1)S(1)}, u32[]{:S(2)}, u32[]{:S(2)}) collective-permute-start(bf16[1152,128]{1,0:T(8,128)(2,1)S(1)} %attention.2.refs_5_), channel_id=1, source_target_pairs={{0,4},{4,0},{8,12},{12,8},{16,20},{20,16},{24,28},{28,24},{1,5},{5... | collective-permute-start | bytes 884744 | tf_op jit(solution)/shard_map/ppermute | solution.py:601
  47.8 9.4 %collective-permute-start.14 = (bf16[1152,128]{1,0:T(8,128)(2,1)S(1)}, bf16[1152,128]{1,0:T(8,128)(2,1)S(1)}, u32[]{:S(2)}, u32[]{:S(2)}) collective-permute-start(bf16[1152,128]{1,0:T(8,128)(2,1)S(1)} %collective-permute-done.9.across_x.refs_7_), channel_id=1, source_target_pairs={{0,4},{4,0},{8,12},{12,8},{16,20},{20,16},{24,28},{28,24},{1,5},{5... | collective-permute-start | bytes 884744 | tf_op jit(solution)/shard_map/ppermute | solution.py:601
  47.8 9.4 %collective-permute-start.15 = (bf16[1152,128]{1,0:T(8,128)(2,1)S(1)}, bf16[1152,128]{1,0:T(8,128)(2,1)S(1)}, u32[]{:S(2)}, u32[]{:S(2)}) collective-permute-start(bf16[1152,128]{1,0:T(8,128)(2,1)S(1)} %collective-permute-done.10.across_y.refs_9_), channel_id=1, source_target_pairs={{0,4},{4,0},{8,12},{12,8},{16,20},{20,16},{24,28},{28,24},{1,5},{5... | collective-permute-start | bytes 884744 | tf_op jit(solution)/shard_map/ppermute | solution.py:601
  48.4 5.9 %collective-permute-start.16 = (bf16[576,128]{1,0:T(8,128)(2,1)S(1)}, bf16[576,128]{1,0:T(8,128)(2,1)S(1)}, u32[]{:S(2)}, u32[]{:S(2)}) collective-permute-start(bf16[576,128]{1,0:T(8,128)(2,1)S(1)} %get-tuple-element.74), channel_id=1, source_target_pairs={{0,16},{4,20},{8,24},{12,28},{16,0},{20,4},{24,8},{28,12},{1,17},{... | collective-permute-start | bytes 442376 | tf_op jit(solution)/shard_map/ppermute | solution.py:601
  49.9 6.8 %collective-permute-start.17 = (bf16[576,128]{1,0:T(8,128)(2,1)S(1)}, bf16[576,128]{1,0:T(8,128)(2,1)S(1)}, u32[]{:S(2)}, u32[]{:S(2)}) collective-permute-start(bf16[576,128]{1,0:T(8,128)(2,1)S(1)} %get-tuple-element.75), channel_id=1, source_target_pairs={{0,8},{4,12},{8,0},{12,4},{16,24},{20,28},{24,16},{28,20},{1,9},{5... | collective-permute-start | bytes 442376 | tf_op jit(solution)/shard_map/ppermute | solution.py:601
  50.5 14.8 %collective-permute-start.23 = (bf16[1152,128]{1,0:T(8,128)(2,1)S(1)}, bf16[1152,128]{1,0:T(8,128)(2,1)S(1)}, u32[]{:S(2)}, u32[]{:S(2)}) collective-permute-start(bf16[1152,128]{1,0:T(8,128)(2,1)S(1)} %get-tuple-element.76.refs_5_), channel_id=1, source_target_pairs={{0,24},{4,28},{8,16},{12,20},{16,8},{20,12},{24,0},{28,4},{1,25},{... | collective-permute-start | bytes 884744 | tf_op jit(solution)/shard_map/ppermute | solution.py:601
  54.3 13.4 %collective-permute-start.21 = (bf16[1152,128]{1,0:T(8,128)(2,1)S(1)}, bf16[1152,128]{1,0:T(8,128)(2,1)S(1)}, u32[]{:S(2)}, u32[]{:S(2)}) collective-permute-start(bf16[1152,128]{1,0:T(8,128)(2,1)S(1)} %get-tuple-element.76.refs_5_), channel_id=1, source_target_pairs={{0,16},{4,20},{8,24},{12,28},{16,0},{20,4},{24,8},{28,12},{1,17},{... | collective-permute-start | bytes 884744 | tf_op jit(solution)/shard_map/ppermute | solution.py:601
  56.7 11.4 %collective-permute-start.12 = (bf16[1152,128]{1,0:T(8,128)(2,1)S(1)}, bf16[1152,128]{1,0:T(8,128)(2,1)S(1)}, u32[]{:S(2)}, u32[]{:S(2)}) collective-permute-start(bf16[1152,128]{1,0:T(8,128)(2,1)S(1)} %get-tuple-element.76.refs_5_), channel_id=1, source_target_pairs={{0,8},{4,12},{8,0},{12,4},{16,24},{20,28},{24,16},{28,20},{1,9},{5... | collective-permute-start | bytes 884744 | tf_op jit(solution)/shard_map/ppermute | solution.py:601
  57.2 1.4 %collective-permute-start.18 = (bf16[576,128]{1,0:T(8,128)(2,1)S(1)}, bf16[576,128]{1,0:T(8,128)(2,1)S(1)}, u32[]{:S(2)}, u32[]{:S(2)}) collective-permute-start(bf16[576,128]{1,0:T(8,128)(2,1)S(1)} %collective-permute-done.16.refs_11_), channel_id=1, source_target_pairs={{0,4},{4,0},{8,12},{12,8},{16,20},{20,16},{24,28},{28,24},{1,5},{5... | collective-permute-start | bytes 442376 | tf_op jit(solution)/shard_map/ppermute | solution.py:601
  57.3 1.6 %collective-permute-start.19 = (bf16[576,128]{1,0:T(8,128)(2,1)S(1)}, bf16[576,128]{1,0:T(8,128)(2,1)S(1)}, u32[]{:S(2)}, u32[]{:S(2)}) collective-permute-start(bf16[576,128]{1,0:T(8,128)(2,1)S(1)} %collective-permute-done.17.refs_12_), channel_id=1, source_target_pairs={{0,4},{4,0},{8,12},{12,8},{16,20},{20,16},{24,28},{28,24},{1,5},{5... | collective-permute-start | bytes 442376 | tf_op jit(solution)/shard_map/ppermute | solution.py:601
  58.6 9.6 %collective-permute-start.11 = (bf16[1152,128]{1,0:T(8,128)(2,1)S(1)}, bf16[1152,128]{1,0:T(8,128)(2,1)S(1)}, u32[]{:S(2)}, u32[]{:S(2)}) collective-permute-start(bf16[1152,128]{1,0:T(8,128)(2,1)S(1)} %get-tuple-element.76.refs_5_), channel_id=1, source_target_pairs={{0,4},{4,0},{8,12},{12,8},{16,20},{20,16},{24,28},{28,24},{1,5},{5... | collective-permute-start | bytes 884744 | tf_op jit(solution)/shard_map/ppermute | solution.py:601
  65.3 2.9 %collective-permute-start.24 = (bf16[1152,128]{1,0:T(8,128)(2,1)S(1)}, bf16[1152,128]{1,0:T(8,128)(2,1)S(1)}, u32[]{:S(2)}, u32[]{:S(2)}) collective-permute-start(bf16[1152,128]{1,0:T(8,128)(2,1)S(1)} %collective-permute-done.23.refs_11_), channel_id=1, source_target_pairs={{0,4},{4,0},{8,12},{12,8},{16,20},{20,16},{24,28},{28,24},{1,5},{5... | collective-permute-start | bytes 884744 | tf_op jit(solution)/shard_map/ppermute | solution.py:601
  67.6 1.6 %collective-permute-start.22 = (bf16[1152,128]{1,0:T(8,128)(2,1)S(1)}, bf16[1152,128]{1,0:T(8,128)(2,1)S(1)}, u32[]{:S(2)}, u32[]{:S(2)}) collective-permute-start(bf16[1152,128]{1,0:T(8,128)(2,1)S(1)} %collective-permute-done.21.refs_9_), channel_id=1, source_target_pairs={{0,4},{4,0},{8,12},{12,8},{16,20},{20,16},{24,28},{28,24},{1,5},{5... | collective-permute-start | bytes 884744 | tf_op jit(solution)/shard_map/ppermute | solution.py:601
  68.1 1.6 %collective-permute-start.20 = (bf16[1152,128]{1,0:T(8,128)(2,1)S(1)}, bf16[1152,128]{1,0:T(8,128)(2,1)S(1)}, u32[]{:S(2)}, u32[]{:S(2)}) collective-permute-start(bf16[1152,128]{1,0:T(8,128)(2,1)S(1)} %collective-permute-done.12.refs_7_), channel_id=1, source_target_pairs={{0,4},{4,0},{8,12},{12,8},{16,20},{20,16},{24,28},{28,24},{1,5},{5... | collective-permute-start | bytes 884744 | tf_op jit(solution)/shard_map/ppermute | solution.py:601
  76.6 10.2 %collective-permute-start.27 = (bf16[672,128]{1,0:T(8,128)(2,1)S(1)}, bf16[672,128]{1,0:T(8,128)(2,1)S(1)}, u32[]{:S(2)}, u32[]{:S(2)}) collective-permute-start(bf16[672,128]{1,0:T(8,128)(2,1)S(1)} %get-tuple-element.83), channel_id=1, source_target_pairs={{0,3},{1,2},{2,1},{3,0},{4,7},{5,6},{6,5},{7,4},{8,11},{9,10},{10,... | collective-permute-start | bytes 516104 | tf_op jit(solution)/shard_map/ppermute | solution.py:745
  81.6 9.5 %collective-permute-start.26 = (bf16[672,128]{1,0:T(8,128)(2,1)S(1)}, bf16[672,128]{1,0:T(8,128)(2,1)S(1)}, u32[]{:S(2)}, u32[]{:S(2)}) collective-permute-start(bf16[672,128]{1,0:T(8,128)(2,1)S(1)} %get-tuple-element.82), channel_id=1, source_target_pairs={{0,1},{1,0},{2,3},{3,2},{4,5},{5,4},{6,7},{7,6},{8,9},{9,8},{10,11... | collective-permute-start | bytes 516104 | tf_op jit(solution)/shard_map/ppermute | solution.py:745
  81.6 14.9 %collective-permute-start.25 = (bf16[672,128]{1,0:T(8,128)(2,1)S(1)}, bf16[672,128]{1,0:T(8,128)(2,1)S(1)}, u32[]{:S(2)}, u32[]{:S(2)}) collective-permute-start(bf16[672,128]{1,0:T(8,128)(2,1)S(1)} %get-tuple-element.81), channel_id=1, source_target_pairs={{0,2},{1,3},{2,0},{3,1},{4,6},{5,7},{6,4},{7,5},{8,10},{9,11},{10,... | collective-permute-start | bytes 516104 | tf_op jit(solution)/shard_map/ppermute | solution.py:745
  (1 other events, 0.7 us)
